TPU v7x, 256 devices: a whole 4x4x8 slice. The times are simulated.
256 devices in a mesh: tr: 64 (over z, x, core), fq: 4 (over y).
Axes of the slice: x: 4, y: 4, z: 8, core: 2. Of those that a mesh axis runs over, the one named last changes fastest.
Arguments:
- traces: bfloat16 [524288, 1024], P('tr', 'fq'), may hold values from -6 to 6
- shot_index: int32 [524288], P('tr'), may hold values from 0 to 8191, as said below
- receiver_index: int32 [524288], P('tr'), may hold values from 0 to 8191
- live_counts: int32 [64], P('tr'), may hold values from 1 to 8192, 393216 in all
- shot_terms: float32 [8192, 512], P('tr', 'fq'), may hold values from 1 to 2.2
- receiver_terms: float32 [8192, 512], P('tr', 'fq'), may hold values from 1 to 2.2
Outputs:
- shot_sums: float32 [8192, 512], P('tr', 'fq')
- receiver_sums: float32 [8192, 512], P('tr', 'fq')
Inputs may be any that keep to these rules, and one draw needn't show every extreme that they name: `shot_index`: A trace slot of block b (slots b * 8192 to (b + 1) * 8192 - 1) has a shot among (b - 1) * 128 to (b + 2) * 128 - 1.
All inputs are finite; a program needn't handle non-finite values. No bound on the sum of `live_counts` on one device may be relied on, other than what follows from the above.
Results may differ from a plain program's by a relative error of at most 0.0017.
Values may be sent and summed in bfloat16 or wider, within the bound.
No kernel may reach another device: no remote copies, remote signals or barrier semaphores. Data moves between devices by JAX's collectives and lax.ppermute only.
A program may use at most 128 MiB of HBM per device.

v0:
```python
import math

import jax
import jax.numpy as jnp
from jax import lax
from jax.sharding import PartitionSpec as P


def padded(value, sides, width):
    for axis, dim in sides:
        size, length = (lax.axis_size(axis), value.shape[dim])
        up = [(i, (i + 1) % size) for i in range(size - 1)]
        down = [(j, i) for i, j in up]
        last = lax.slice_in_dim(value, length - width, length, axis=dim)
        leading = lax.slice_in_dim(value, 0, width, axis=dim)
        before = lax.ppermute(last, axis, up)
        after = lax.ppermute(leading, axis, down)
        value = jnp.concatenate([before, value, after], axis=dim)
    return value


def from_behind(value, axis, by):
    size = lax.axis_size(axis)
    pairs = [(i, i + by) for i in range(size) if 0 <= i + by < size]
    return lax.ppermute(value, axis, pairs)


def make_table(samples, first, count):
    times = jnp.arange(samples, dtype=jnp.int32)[:, None]
    freqs = first + jnp.arange(count, dtype=jnp.int32)[None, :]
    phase = times * freqs % samples
    angle = phase.astype(jnp.float32) * (2.0 * math.pi / samples)
    return jnp.concatenate([jnp.cos(angle), -jnp.sin(angle)], axis=1).astype(jnp.bfloat16)


def per_device(traces, shot_index, receiver_index, live_counts, shot_terms, receiver_terms):
    row_count = traces.shape[0]
    band_width = shot_terms.shape[1]
    shot_block = shot_terms.shape[0]
    rec_block = receiver_terms.shape[0]
    samples = traces.shape[1] * lax.axis_size("fq")
    band_index = lax.axis_index("fq")
    owner_index = lax.axis_index("tr")
    table = make_table(samples, band_index * band_width, band_width)
    spectrum = jnp.dot(
        lax.all_gather(traces, "fq", axis=1, tiled=True), table, preferred_element_type=jnp.float32
    )
    real_part = spectrum[:, :band_width]
    imag_part = spectrum[:, band_width:]
    logamp = 0.5 * jnp.log(real_part * real_part + imag_part * imag_part + 1.0)
    live = (jnp.arange(row_count, dtype=jnp.int32) < live_counts[0]).astype(jnp.float32)[:, None]
    rec_table = lax.all_gather(receiver_terms, "tr", axis=0, tiled=True)
    rec_values = jnp.take(rec_table, receiver_index, axis=0)
    shot_table = padded(shot_terms, (("tr", 0),), shot_block)
    shot_local = shot_index - (owner_index - 1) * shot_block
    shot_values = jnp.take(shot_table, shot_local, axis=0)
    resid = live * (logamp - shot_values - rec_values)
    shot_part = jax.ops.segment_sum(resid, shot_local, num_segments=shot_table.shape[0])
    arrived_left = from_behind(shot_part[2 * shot_block :], "tr", 1)
    arrived_right = from_behind(shot_part[:shot_block], "tr", -1)
    shot_sums = shot_part[shot_block : 2 * shot_block] + arrived_left + arrived_right
    rec_part = jax.ops.segment_sum(
        resid, receiver_index, num_segments=rec_block * lax.axis_size("tr")
    )
    receiver_sums = lax.psum_scatter(rec_part, "tr", scatter_dimension=0, tiled=True)
    return (shot_sums, receiver_sums)


def solution(mesh):
    return jax.shard_map(
        per_device,
        mesh=mesh,
        in_specs=(P("tr", "fq"), P("tr"), P("tr"), P("tr"), P("tr", "fq"), P("tr", "fq")),
        out_specs=(P("tr", "fq"), P("tr", "fq")),
        check_vma=False,
    )
```

profile of v0, /device:TPU:8, one launch (start us, length us, event | category | flops | bytes accessed | tf_op | source)
XLA Modules:
  0.0 483.6 jit_solution(12278282994885745908)
XLA Ops:
  7.2 0.0 copy-start.1
  7.2 0.0 copy-start
  7.2 0.0 copy-start.2
  7.2 0.0 all-gather.5.cloned.1.call-start
  7.2 0.7 all-gather.5.cloned.1.call-update
  7.9 0.0 all-gather.3.cloned.1.call-start
  8.0 0.7 all-gather.3.cloned.1.call-update
  8.7 0.0 reduce-scatter.2.cloned.1.call-start
  8.7 0.0 copy-done.1
  8.7 1.7 collective-permute-start
  10.5 1.3 collective-permute-start.1
  12.4 0.0 copy-done
  12.5 0.0 copy-done.2
  12.5 2.2 cosine_convert_fusion
  14.8 0.0 collective-permute-done
  14.8 0.1 collective-permute-done.1
  14.9 27.7 %gather_fusion = f32[8192,128]{1,0:T(8,128)} fusion(f32[384,128]{1,0:T(8,128)S(1)} %pad_maximum_fusion, s32[8192]{0:T(1024)S(1)} %fusion.22), kind=kCustom, calls=%fused_computation | custom fusion | bytes 8421376 | tf_op jit(solution)/shard_map/jit(_take)/gather | solution.py:56
  42.6 5.7 %copy.10 = f32[8192,128]{0,1:T(8,128)} copy(f32[8192,128]{1,0:T(8,128)} %gather_fusion) | data formatting | bytes 8388608 | tf_op jit(solution)/shard_map/jit(_take)/gather | solution.py:56
  48.3 44.4 %all-gather.5.cloned.1.call-done = f32[8192,128]{1,0:T(8,128)} async-done(((f32[128,128]{1,0:T(8,128)}), f32[8192,128]{1,0:T(8,128)}) %all-gather.5.cloned.1.call-update) | async-done | bytes 4194320 | tf_op jit(solution)/shard_map/all_gather | solution.py:52
  92.7 29.9 %gather_fusion.1 = f32[8192,128]{1,0:T(8,128)} fusion(f32[8192,128]{1,0:T(8,128)} %all-gather.5.cloned.1.call-done, s32[8192]{0:T(1024)S(1)} %fusion.23), kind=kCustom, calls=%fused_computation.1 | custom fusion | bytes 8421376 | tf_op jit(solution)/shard_map/jit(_take)/gather | solution.py:53
  122.6 5.7 %copy.11 = f32[8192,128]{0,1:T(8,128)} copy(f32[8192,128]{1,0:T(8,128)} %gather_fusion.1) | data formatting | bytes 8388608 | tf_op jit(solution)/shard_map/jit(_take)/gather | solution.py:53
  128.3 122.4 %all-gather.3.cloned.1.call-done = bf16[8192,1024]{1,0:T(8,128)(2,1)} async-done(((bf16[8192,256]{1,0:T(8,128)(2,1)}), bf16[8192,1024]{1,0:T(8,128)(2,1)}) %all-gather.3.cloned.1.call-update) | async-done | bytes 16777232 | tf_op jit(solution)/shard_map/all_gather | solution.py:46
  250.6 19.1 %convolution_bitcast_fusion = f32[8192,256]{0,1:T(8,128)} fusion(bf16[8192,1024]{1,0:T(8,128)(2,1)} %all-gather.3.cloned.1.call-done, bf16[1024,128]{1,0:T(8,128)(2,1)S(1)} %get-tuple-element.7, bf16[1024,128]{1,0:T(8,128)(2,1)S(1)} %get-tuple-element.6), kind=kOutput, calls=%fused_computation.4 | convolution fusion | flops 4296015872 | bytes 25690112 | tf_op jit(solution)/shard_map/dot_general | solution.py:45
  269.7 8.8 %fusion.6 = f32[8192,128]{0,1:T(8,128)} fusion(f32[8192,256]{0,1:T(8,128)} %convolution_bitcast_fusion, f32[8192,128]{0,1:T(8,128)} %copy.11, f32[8192,128]{0,1:T(8,128)} %copy.10, f32[8192]{0:T(1024)S(1)} %get-tuple-element.8, pred[8192]{0:T(1024)(128)(4,1)S(1)} %get-tuple-element.9, pred[8192]{0:T(1024)(128)(4,1)S(1)} %get-tuple-element.2), kind=kLoop, calls=%fused_computation.12 | loop fusion | flops 10485760 | bytes 21020672 | tf_op jit(solution)/shard_map/mul | solution.py:57
  278.5 5.6 %copy.12 = f32[8192,128]{1,0:T(8,128)} copy(f32[8192,128]{0,1:T(8,128)} %fusion.6) | data formatting | bytes 8388608 | tf_op jit(solution)/shard_map/mul | solution.py:57
  284.1 46.5 %scatter_custom_fusion.1 = f32[8192,128]{1,0:T(8,128)} fusion(s32[8192]{0:T(1024)S(1)} %copy-done, f32[8192,128]{1,0:T(8,128)} %copy.12, f32[]{:T(128)} %constant.33.clone.1), kind=kCustom, calls=%fused_computation.14 | custom fusion | flops 1048576 | bytes 4194816 | tf_op jit(solution)/shard_map/scatter-add | solution.py:62
  330.6 0.0 reduce-scatter.2.cloned.1.call-update
  330.6 44.4 %scatter_custom_fusion = f32[384,128]{1,0:T(8,128)S(1)} fusion(s32[8192]{0:T(1024)S(1)} %get-tuple-element.3, f32[8192,128]{1,0:T(8,128)} %copy.12, f32[]{:T(128)} %constant.33.clone.1), kind=kCustom, calls=%fused_computation.31 | custom fusion | flops 1048576 | bytes 197120 | tf_op jit(solution)/shard_map/scatter-add | solution.py:58
  375.0 1.3 collective-permute-start.2
  376.3 1.3 collective-permute-start.3
  377.6 0.0 collective-permute-done.2
  377.6 4.7 collective-permute-done.3
  382.3 0.6 fusion.20
  382.9 94.2 %reduce-scatter.2.cloned.1.call-done = f32[128,128]{1,0:T(8,128)} async-done(((f32[8192,128]{1,0:T(8,128)}), f32[128,128]{1,0:T(8,128)}) %reduce-scatter.2.cloned.1.call-update) | async-done | bytes 65552 | tf_op jit(solution)/shard_map/reduce_scatter | solution.py:65
  (7 shorter events, 0.1 us)
Async XLA Ops:
  7.2 1.6 copy-start.1
  7.2 5.3 %copy-start = (s32[8192]{0:T(1024)S(1)}, s32[8192]{0:T(1024)}, u32[]{:S(2)}) copy-start(s32[8192]{0:T(1024)} %param.8) | copy-start | bytes 98308
  7.2 5.3 %copy-start.2 = (s32[8192]{0:T(1024)S(1)}, s32[8192]{0:T(1024)}, u32[]{:S(2)}) copy-start(s32[8192]{0:T(1024)} %param.7) | copy-start | bytes 98308
  7.2 85.5 %all-gather.5.cloned.1.call-start = ((), (), s32[]{:S(2)}) async-start(), calls=%async_computation.2 | async-start | bytes 4259840 | tf_op jit(solution)/shard_map/all_gather | solution.py:52
  7.9 242.7 %all-gather.3.cloned.1.call-start = ((), (), s32[]{:S(2)}) async-start(), calls=%async_computation.1 | async-start | bytes 20971520 | tf_op jit(solution)/shard_map/all_gather | solution.py:46
  8.7 468.4 %reduce-scatter.2.cloned.1.call-start = ((), (), s32[]{:S(2)}) async-start(), calls=%async_computation.3 | async-start | bytes 4259840 | tf_op jit(solution)/shard_map/reduce_scatter | solution.py:65
  8.7 6.1 %collective-permute-start = (f32[128,128]{1,0:T(8,128)S(1)}, f32[128,128]{1,0:T(8,128)S(1)}, u32[]{:S(2)}, u32[]{:S(2)}) collective-permute-start(f32[128,128]{1,0:T(8,128)S(1)} %copy-done.1), channel_id=1, source_target_pairs={{0,4},{4,8},{8,12},{12,16},{16,20},{20,24},{24,28},{28,32},{32,36}... | collective-permute-start | bytes 196616 | tf_op jit(solution)/shard_map/ppermute | solution.py:16
  10.5 4.4 collective-permute-start.1
  375.0 2.6 collective-permute-start.2
  376.3 6.0 %collective-permute-start.3 = (f32[128,128]{1,0:T(8,128)S(1)}, f32[128,128]{1,0:T(8,128)S(1)}, u32[]{:S(2)}, u32[]{:S(2)}) collective-permute-start(f32[128,128]{1,0:T(8,128)S(1)} %get-tuple-element.5), channel_id=1, source_target_pairs={{4,0},{8,4},{12,8},{16,12},{20,16},{24,20},{28,24},{32,28},{36,32}... | collective-permute-start | bytes 196616 | tf_op jit(solution)/shard_map/ppermute | solution.py:25
Sparse Core Ops, SparseCore 0:
  10.8 81.8 all-gather.4
  94.5 156.0 all-gather.2
  330.7 146.3 reduce-scatter.1
where the time goes:
time: 484 us
  waiting for transfers between devices  267 us (55%)
  other arithmetic  103 us (21%)
  local copies, waits for them, and re-layouts  74.6 us (15%)
  matrix products  19.1 us (4%)
  between operations  14.6 us (3%)
  starting transfers between devices  5.73 us (1%)
    all_gather x1, waiting for transfers between devices, per_device(): lax.all_gather(traces, 'fq', axis=1, tiled=True)  122 us
    reduce_scatter x1, waiting for transfers between devices, per_device(): lax.psum_scatter(rec_part, 'tr', scatter_dimension=0, tiled=True)  94.2 us
    scatter-add x1, other arithmetic, per_device(): jax.ops.segment_sum(resid, receiver_index, num_segments=rec_block * lax.a...  46.5 us
    all_gather x1, waiting for transfers between devices, per_device(): rec_table = lax.all_gather(receiver_terms, 'tr', axis=0, tiled=True)  44.4 us
    scatter-add x1, other arithmetic, per_device(): jax.ops.segment_sum(resid, shot_local, num_segments=shot_table.shape[0])  44.4 us
    gather x2, local copies, waits for them, and re-layouts, per_device(): rec_values = jnp.take(rec_table, receiver_index, axis=0)  35.6 us
    gather x2, local copies, waits for them, and re-layouts, per_device(): shot_values = jnp.take(shot_table, shot_local, axis=0)  33.4 us
    dot_general x1, matrix products, per_device(): jnp.dot(lax.all_gather(traces, 'fq', axis=1, tiled=True), table, preferre...  19.1 us
  transfers between devices with their start and end apart: 7, of which 5 were waited for; matrix products, arithmetic and copies ran while one was open for 24% of the time, Pallas kernels for 0%

commit v1 on v0

v1 whole, which is shorter than its diff:
```python
import math

import jax
import jax.numpy as jnp
from jax import lax
from jax.experimental import pallas as pl
from jax.experimental.pallas import tpu as pltpu
from jax.sharding import PartitionSpec as P

NZ, NX, NC, NY = 8, 4, 2, 4
LA_TOP = 9.1
LA_SCALE = 65535.0 / LA_TOP
REC_LOW, REC_HIGH = 1.0, 2.2
REC_SCALE = 65535.0 / (REC_HIGH - REC_LOW)
SUM_SCALE = 1.0 / 32.0
CHUNKS = 2
VMEM = pltpu.CompilerParams(vmem_limit_bytes=56 * 2**20)


def tr_of(z, x, c):
    return (z * NX + x) * NC + c


def sites():
    return [(z, x, c) for z in range(NZ) for x in range(NX) for c in range(NC)]


def send_x(value, k):
    return lax.ppermute(value, "tr", [(tr_of(z, x, c), tr_of(z, (x + k) % NX, c)) for z, x, c in sites()])


def send_z(value, k):
    return lax.ppermute(value, "tr", [(tr_of(z, x, c), tr_of((z + k) % NZ, x, c)) for z, x, c in sites()])


def swap_z(value):
    return lax.ppermute(value, "tr", [(tr_of(z, x, c), tr_of(z ^ 1, x, c)) for z, x, c in sites()])


def swap_core(value):
    return lax.ppermute(value, "tr", [(tr_of(z, x, c), tr_of(z, x, c ^ 1)) for z, x, c in sites()])


def send_y(value, k):
    return lax.ppermute(value, "fq", [(i, (i + k) % NY) for i in range(NY)])


def make_table(samples, y, width):
    part = samples // NY
    steps = jnp.arange(NY, dtype=jnp.int32)
    times = (((y - steps) % NY) * part)[:, None] + jnp.arange(part, dtype=jnp.int32)[None, :]
    times = times.reshape(samples, 1)
    freqs = (((y + steps) % NY) * width)[:, None] + jnp.arange(width, dtype=jnp.int32)[None, :]
    freqs = jnp.stack([freqs, freqs], axis=1).reshape(1, NY * 2 * width)
    imag = (jnp.arange(NY * 2 * width, dtype=jnp.int32) // width % 2 == 1)[None, :]
    phase = times * freqs % samples
    angle = phase.astype(jnp.float32) * (2.0 * math.pi / samples)
    return jnp.where(imag, -jnp.sin(angle), jnp.cos(angle)).astype(jnp.bfloat16)


def spectra(blocks, table, width):
    rows, part = blocks[0].shape
    tile = 512

    def body(b0, b1, b2, b3, t, o0, o1, o2, o3):
        for k, out in enumerate((o0, o1, o2, o3)):
            cols = pl.ds(k * 2 * width, 2 * width)
            acc = None
            for j, b in enumerate((b0, b1, b2, b3)):
                one = jnp.dot(b[...], t[pl.ds(j * part, part), cols], preferred_element_type=jnp.float32)
                acc = one if acc is None else acc + one
            re, im = acc[:, :width], acc[:, width:]
            logamp = 0.5 * jnp.log(re * re + im * im + 1.0)
            code = jnp.minimum(logamp * LA_SCALE + 0.5, 65535.0).astype(jnp.int32) - 32768
            out[...] = code.astype(jnp.int16)

    return pl.pallas_call(
        body,
        grid=(rows // tile,),
        in_specs=[pl.BlockSpec((tile, part), lambda i: (i, 0))] * 4
        + [pl.BlockSpec(table.shape, lambda i: (0, 0))],
        out_specs=[pl.BlockSpec((tile, width), lambda i: (i, 0))] * 4,
        out_shape=[jax.ShapeDtypeStruct((rows, width), jnp.int16)] * 4,
        compiler_params=VMEM,
        cost_estimate=pl.CostEstimate(flops=2 * rows * 1024 * 1024, bytes_accessed=rows * 3072 + 2**21, transcendentals=rows * 512),
        name="spectra",
    )(*blocks, table)


def gather_terms(own, other, shot_near, rec_at, shot_at):
    rows, width = rec_at.shape[0], own.shape[1]
    half = own.shape[0]

    def body(rec_at, shot_at, own, other, shot, out, rec):
        rec[pl.ds(0, half), :] = (own[...].astype(jnp.float32) + 32768.0) * (1.0 / REC_SCALE) + REC_LOW
        rec[pl.ds(half, half), :] = (other[...].astype(jnp.float32) + 32768.0) * (1.0 / REC_SCALE) + REC_LOW

        def step(b, _):
            for u in range(16):
                i = b * 16 + u
                out[pl.ds(i, 1), :] = rec[pl.ds(rec_at[i], 1), :] + shot[pl.ds(shot_at[i], 1), :]
            return 0

        lax.fori_loop(0, rows // 16, step, 0)

    vm, sm = pl.BlockSpec(memory_space=pltpu.VMEM), pl.BlockSpec(memory_space=pltpu.SMEM)
    return pl.pallas_call(
        body,
        in_specs=[sm, sm, vm, vm, vm],
        out_specs=vm,
        out_shape=jax.ShapeDtypeStruct((rows, width), jnp.float32),
        scratch_shapes=[pltpu.VMEM((2 * half, width), jnp.float32)],
        compiler_params=VMEM,
        cost_estimate=pl.CostEstimate(flops=rows * width, bytes_accessed=48 * 2**20, transcendentals=0),
        name="gather_terms",
    )(rec_at, shot_at, own, other, shot_near)


def residual(code, model, live):
    logamp = (code.astype(jnp.float32) + 32768.0) * (1.0 / LA_SCALE)
    alive = lax.broadcasted_iota(jnp.int32, code.shape, 0) < live
    return jnp.where(alive, logamp - model, 0.0)


def sum_receivers(codes, model, live, rec_at, count):
    rows, width = model.shape
    piece = codes[0].shape[0]
    parts = len(codes)
    banks, depth = 4, 2

    def body(*refs):
        rec_at, live, model = refs[:3]
        codes = refs[3 : 3 + parts]
        out, res = refs[3 + parts : 5 + parts]
        sums = (out,) + refs[5 + parts :]
        for s in sums:
            s[...] = jnp.zeros_like(s)
        for k, code in enumerate(codes):
            at = pl.ds(k * piece, piece)
            res[at, :] = residual(code[...], model[at, :], live[k])

        def step(b, _):
            group = banks * depth
            at = [rec_at[b * group + u] for u in range(group)]
            row = [res[pl.ds(b * group + u, 1), :] for u in range(group)]
            for u in range(banks):
                v = u + banks
                s = sums[u]
                first = s[pl.ds(at[u], 1), :]
                second = s[pl.ds(at[v], 1), :]
                again = (at[u] == at[v]).astype(jnp.float32)
                s[pl.ds(at[u], 1), :] = first + row[u]
                s[pl.ds(at[v], 1), :] = second + (row[v] + again * row[u])
            return 0

        lax.fori_loop(0, rows // (banks * depth), step, 0)
        out[...] = (sums[0][...] + sums[1][...]) + (sums[2][...] + sums[3][...])

    vm, sm = pl.BlockSpec(memory_space=pltpu.VMEM), pl.BlockSpec(memory_space=pltpu.SMEM)
    return pl.pallas_call(
        body,
        in_specs=[sm, sm] + [vm] * (1 + parts),
        out_specs=vm,
        out_shape=jax.ShapeDtypeStruct((count, width), jnp.float32),
        scratch_shapes=[pltpu.VMEM((rows, width), jnp.float32)] + [pltpu.VMEM((count, width), jnp.float32)] * (banks - 1),
        compiler_params=VMEM,
        cost_estimate=pl.CostEstimate(flops=rows * width, bytes_accessed=48 * 2**20, transcendentals=0),
        name="sum_receivers",
    )(rec_at, live, model, *codes)


def sum_shots(codes, model, live, shot_at, count):
    rows, width = model.shape
    piece = codes[0].shape[0]
    parts = len(codes)

    def body(*refs):
        shot_at, live, model = refs[:3]
        codes, out = refs[3 : 3 + parts], refs[3 + parts]
        acc = jnp.zeros((count, 2 * width), jnp.float32)
        for k, code in enumerate(codes):
            at = pl.ds(k * piece, piece)
            res = residual(code[...], model[at, :], live[k])
            high = res.astype(jnp.bfloat16)
            low = (res - high.astype(jnp.float32)).astype(jnp.bfloat16)
            both = jnp.concatenate([high, low], axis=1)
            hot = lax.broadcasted_iota(jnp.int32, (count, piece), 0) == shot_at[:, at]
            acc = acc + jnp.dot(hot.astype(jnp.bfloat16), both, preferred_element_type=jnp.float32)
        out[...] = acc[:, :width] + acc[:, width:]

    vm, sm = pl.BlockSpec(memory_space=pltpu.VMEM), pl.BlockSpec(memory_space=pltpu.SMEM)
    return pl.pallas_call(
        body,
        in_specs=[vm, sm] + [vm] * (1 + parts),
        out_specs=vm,
        out_shape=jax.ShapeDtypeStruct((count, width), jnp.float32),
        compiler_params=VMEM,
        cost_estimate=pl.CostEstimate(flops=4 * rows * width * count, bytes_accessed=12 * 2**20, transcendentals=0),
        name="sum_shots",
    )(shot_at[None, :], live, model, *codes)


def neighbour(value, by):
    size = NZ * NX * NC
    return lax.ppermute(value, "tr", [(i, i + by) for i in range(size) if 0 <= i + by < size])


def per_device(traces, shot_index, receiver_index, live_counts, shot_terms, receiver_terms):
    rows, part = traces.shape
    block, width = shot_terms.shape
    share, piece = rows // NY, rows // NY // CHUNKS
    owner, y = lax.axis_index("tr"), lax.axis_index("fq")
    z, x, c = owner // (NX * NC), owner // NC % NX, owner % NC

    parts = [lax.dynamic_slice_in_dim(traces, (y + k) % NY * share, share, 0) for k in range(NY)]
    got = [[None] * NY for _ in range(CHUNKS)]
    for h in range(CHUNKS):
        for k in (0, 1, 3, 2):
            mine = parts[k][h * piece : (h + 1) * piece]
            got[h][k] = send_y(mine, k) if k else mine

    code = jnp.clip(jnp.round((receiver_terms - REC_LOW) * REC_SCALE), 0.0, 65535.0).astype(jnp.int32) - 32768
    terms = code.astype(jnp.int16)
    terms = jnp.concatenate([terms] + [send_z(terms, -2 * k) for k in range(1, NZ // 2)])
    terms = jnp.concatenate([terms, swap_z(terms)])
    terms = jnp.concatenate([terms] + [send_x(terms, -k) for k in range(1, NX)])
    far_terms = swap_core(terms)

    def ordered(v):
        v = v.reshape(NY, CHUNKS, piece)
        v = jnp.stack([lax.dynamic_index_in_dim(v, (y - k) % NY, 0, keepdims=False) for k in range(NY)], axis=1)
        return v.reshape(rows)

    near = receiver_index // block
    rz, rx, rc = near // (NX * NC), near // NC % NX, near % NC
    odd = (rz ^ z) & 1
    place = (((rc ^ c) * NX + (rx - x) % NX) * 2 + odd) * (NZ // 2) + (rz - (z ^ odd)) % NZ // 2
    rec_at = ordered(place * block + receiver_index % block)
    shot_at = ordered(shot_index - (owner - 1) * block)
    live = live_counts[0] - jnp.stack([(y - k) % NY * share + h * piece for h in range(CHUNKS) for k in range(NY)])

    shot_near = jnp.concatenate([neighbour(shot_terms, 1), shot_terms, neighbour(shot_terms, -1)])

    table = make_table(part * NY, y, width)
    codes = []
    for h in range(CHUNKS):
        outs = spectra(got[h], table, width)
        codes += [send_y(outs[k], k) if k else outs[k] for k in range(NY)]
    model = gather_terms(terms, far_terms, shot_near, rec_at, shot_at)

    sums = sum_receivers(codes, model, live, rec_at, block * NZ * NX * NC)
    half = sums.shape[0] // 2
    sums = sums[:half] + swap_core(sums[half:])
    sums = sums.reshape(NX, NZ * block, width)
    sent = (sums * SUM_SCALE).astype(jnp.float16)
    come = [send_x(sent[k], k).astype(jnp.float32) for k in (1, 3, 2)]
    sums = sums[0] + (come[0] + come[1] + come[2]) * (1.0 / SUM_SCALE)
    half = sums.shape[0] // 2
    sent = (sums[half:] * SUM_SCALE).astype(jnp.float16)
    sums = sums[:half] + swap_z(sent).astype(jnp.float32) * (1.0 / SUM_SCALE)
    sums = sums.reshape(NZ // 2, block, width)
    sent = (sums * SUM_SCALE).astype(jnp.float16)
    come = [send_z(sent[k], 2 * k).astype(jnp.float32) for k in (1, 3, 2)]
    receiver_sums = sums[0] + (come[0] + come[1] + come[2]) * (1.0 / SUM_SCALE)

    shots = sum_shots(codes, model, live, shot_at, 3 * block)
    shot_sums = shots[block : 2 * block] + neighbour(shots[2 * block :], 1) + neighbour(shots[:block], -1)
    return (shot_sums, receiver_sums)


def solution(mesh):
    return jax.shard_map(
        per_device,
        mesh=mesh,
        in_specs=(P("tr", "fq"), P("tr"), P("tr"), P("tr"), P("tr", "fq"), P("tr", "fq")),
        out_specs=(P("tr", "fq"), P("tr", "fq")),
        check_vma=False,
    )
```

time: 484 us -> 202 us (0.42)
  waiting for transfers between devices: 267 us -> 36.5 us
  other arithmetic: 103 us -> 23.4 us
  local copies, waits for them, and re-layouts: 74.6 us -> 10.8 us
  Pallas kernels: 0 us -> 62.1 us
  starting transfers between devices: 5.73 us -> 67.2 us
  matrix products: 19.1 us -> 0 us
  between operations: 14.6 us -> 1.84 us
    all_gather x2 -> x0, waiting for transfers between devices: 167 us -> none  [the longest x1 122 us: per_device(): lax.all_gather(traces, 'fq', axis=1, tiled=True)]
    reduce_scatter x1 -> x0, waiting for transfers between devices: 94.2 us -> none  [per_device(): lax.psum_scatter(rec_part, 'tr', scatter_dimension=0, tiled=True)]
    scatter-add x2 -> x0, other arithmetic: 90.9 us -> none  [the longest x1 46.5 us: per_device(): jax.ops.segment_sum(resid, receiver_index, num_segments=rec_block * lax.a...]
    gather x4 -> x0, local copies, waits for them, and re-layouts: 68.9 us -> none  [the longest x2 35.6 us: per_device(): rec_values = jnp.take(rec_table, receiver_index, axis=0)]
    pallas_call x0 -> x5, Pallas kernels: none -> 62.1 us  [the longest x1 27 us: sum_receivers(): pl.pallas_call(body, in_specs=[sm, sm] + [vm] * (1 + parts), out_specs=vm...]
    ppermute x4 -> x32, starting transfers between devices: 5.62 us -> 67.2 us  [the longest x12 27.9 us: send_y(): return lax.ppermute(value, 'fq', [(i, (i + k) % NY) for i in range(NY)])]
    ppermute x4 -> x32, waiting for transfers between devices: 4.76 us -> 36.5 us  [the longest x12 21.2 us: send_y(): return lax.ppermute(value, 'fq', [(i, (i + k) % NY) for i in range(NY)])]
    dot_general x1 -> x0, matrix products: 19.1 us -> none  [per_device(): jnp.dot(lax.all_gather(traces, 'fq', axis=1, tiled=True), table, preferre...]
  transfers between devices with their start and end apart: 7 -> 32, of which waited for: 5 -> 9; matrix products, arithmetic and copies ran while one was open for 24% -> 14% of each run, Pallas kernels for 0% -> 17%
where the time goes in v1:
time: 202 us
  starting transfers between devices  67.2 us (33%)
  Pallas kernels  62.1 us (31%)
  waiting for transfers between devices  36.5 us (18%)
  other arithmetic  23.4 us (12%)
  local copies, waits for them, and re-layouts  10.8 us (5%)
    ppermute x12, starting transfers between devices, send_y(): return lax.ppermute(value, 'fq', [(i, (i + k) % NY) for i in range(NY)])  27.9 us
    pallas_call x1, Pallas kernels, sum_receivers(): pl.pallas_call(body, in_specs=[sm, sm] + [vm] * (1 + parts), out_specs=vm...  27 us
    ppermute x6, starting transfers between devices, send_z(): lax.ppermute(value, 'tr', [(tr_of(z, x, c), tr_of((z + k) % NZ, x, c)) fo...  22.5 us
    ppermute x12, waiting for transfers between devices, send_y(): return lax.ppermute(value, 'fq', [(i, (i + k) % NY) for i in range(NY)])  21.2 us
    convert_element_type x1, other arithmetic, make_table(): return jnp.where(imag, -jnp.sin(angle), jnp.cos(angle)).astype(jnp.bfloat16)  18.2 us
    pallas_call x1, Pallas kernels, gather_terms(): pl.pallas_call(body, in_specs=[sm, sm, vm, vm, vm], out_specs=vm, out_sha...  17.7 us
    pallas_call x2, Pallas kernels, spectra(): pl.pallas_call(body, grid=(rows // tile,), in_specs=[pl.BlockSpec((tile,...  11.5 us
    ppermute x6, starting transfers between devices, send_x(): lax.ppermute(value, 'tr', [(tr_of(z, x, c), tr_of(z, (x + k) % NX, c)) fo...  9 us
  transfers between devices with their start and end apart: 32, of which 9 were waited for; matrix products, arithmetic and copies ran while one was open for 14% of the time, Pallas kernels for 17%

profile of v1, /device:TPU:8, one launch (start us, length us, event | category | flops | bytes accessed | tf_op | source)
XLA Modules:
  0.0 201.8 jit_solution(1092998050293888194)
XLA Ops:
  0.6 0.9 constant_dynamic-update-slice_fusion.4
  1.5 3.3 %collective-permute-start.2 = (s16[128,128]{1,0:T(8,128)(2,1)S(1)}, s16[128,128]{1,0:T(8,128)(2,1)S(1)}, u32[]{:S(2)}, u32[]{:S(2)}) collective-permute-start(s16[128,128]{1,0:T(8,128)(2,1)S(1)} %get-tuple-element.23), channel_id=1, source_target_pairs={{0,64},{4,68},{8,72},{12,76},{16,80},{20,84},{24,88},{28,92},{32,9... | collective-permute-start | bytes 98312 | tf_op jit(solution)/shard_map/ppermute | solution.py:33
  4.8 5.4 %collective-permute-start.1 = (s16[128,128]{1,0:T(8,128)(2,1)S(1)}, s16[128,128]{1,0:T(8,128)(2,1)S(1)}, u32[]{:S(2)}, u32[]{:S(2)}) collective-permute-start(s16[128,128]{1,0:T(8,128)(2,1)S(1)} %get-tuple-element.23), channel_id=1, source_target_pairs={{0,128},{4,132},{8,136},{12,140},{16,144},{20,148},{24,152},{28,15... | collective-permute-start | bytes 98312 | tf_op jit(solution)/shard_map/ppermute | solution.py:33
  10.2 2.7 %collective-permute-start = (s16[128,128]{1,0:T(8,128)(2,1)S(1)}, s16[128,128]{1,0:T(8,128)(2,1)S(1)}, u32[]{:S(2)}, u32[]{:S(2)}) collective-permute-start(s16[128,128]{1,0:T(8,128)(2,1)S(1)} %get-tuple-element.23), channel_id=1, source_target_pairs={{0,192},{4,196},{8,200},{12,204},{16,208},{20,212},{24,216},{28,22... | collective-permute-start | bytes 98312 | tf_op jit(solution)/shard_map/ppermute | solution.py:33
  12.9 3.9 %constant_dynamic-slice_fusion.4 = (bf16[1024,256]{1,0:T(8,128)(2,1)}, bf16[1024,256]{1,0:T(8,128)(2,1)}, bf16[1024,256]{1,0:T(8,128)(2,1)}, bf16[1024,256]{1,0:...) fusion(bf16[8192,256]{1,0:T(8,128)(2,1)} %param.6, ...), kind=kLoop, calls=%fused_computation.104 | loop fusion | bytes 8388640 | tf_op jit(solution)/shard_map/slice | solution.py:219
  17.3 3.0 %collective-permute-start.12 = (bf16[1024,256]{1,0:T(8,128)(2,1)}, bf16[1024,256]{1,0:T(8,128)(2,1)}, u32[]{:S(2)}, u32[]{:S(2)}) collective-permute-start(bf16[1024,256]{1,0:T(8,128)(2,1)} %get-tuple-element.25), channel_id=1, source_target_pairs={{0,3},{1,0},{2,1},{3,2},{4,7},{5,4},{6,5},{7,6},{8,11},{9,8},{10,9... | collective-permute-start | bytes 1572872 | tf_op jit(solution)/shard_map/ppermute | solution.py:45
  20.5 1.1 collective-permute-start.3
  21.7 3.9 %collective-permute-done.3 = s16[512,128]{1,0:T(8,128)(2,1)S(1)} collective-permute-done((s16[512,128]{1,0:T(8,128)(2,1)S(1)}, s16[512,128]{1,0:T(8,128)(2,1)S(1)}, u32[]{:S(2)}, u32[]{:S(2)}) %collective-permute-start.3) | collective-permute-done | bytes 131104 | tf_op jit(solution)/shard_map/ppermute | solution.py:37
  25.6 1.6 collective-permute-start.6
  27.2 2.7 %collective-permute-start.5 = (s16[1024,128]{1,0:T(8,128)(2,1)S(1)}, s16[1024,128]{1,0:T(8,128)(2,1)S(1)}, u32[]{:S(2)}, u32[]{:S(2)}) collective-permute-start(s16[1024,128]{1,0:T(8,128)(2,1)S(1)} %get-tuple-element.40), channel_id=1, source_target_pairs={{0,16},{4,20},{8,24},{12,28},{16,0},{20,4},{24,8},{28,12},{32,48},... | collective-permute-start | bytes 786440 | tf_op jit(solution)/shard_map/ppermute | solution.py:29
  29.9 1.4 collective-permute-start.4
  31.4 18.2 %select_convert_fusion.t = bf16[1024,1024]{1,0:T(8,128)(2,1)} fusion(s32[1024]{0:T(1024)S(1)} %bitcast.23, s32[1024]{0:T(1024)S(1)} %bitcast.24, pred[1024]{0:T(1024)(128)(4,1)S(1)} %fusion.25), kind=kLoop, calls=%fused_computation.8 | loop fusion | flops 17825792 | bytes 2106368 | tf_op jit(solution)/shard_map/convert_element_type | solution.py:58
  49.7 2.3 %collective-permute-start.10 = (bf16[1024,256]{1,0:T(8,128)(2,1)}, bf16[1024,256]{1,0:T(8,128)(2,1)}, u32[]{:S(2)}, u32[]{:S(2)}) collective-permute-start(bf16[1024,256]{1,0:T(8,128)(2,1)} %get-tuple-element.27), channel_id=1, source_target_pairs={{0,1},{1,2},{2,3},{3,0},{4,5},{5,6},{6,7},{7,4},{8,9},{9,10},{10,1... | collective-permute-start | bytes 1572872 | tf_op jit(solution)/shard_map/ppermute | solution.py:45
  53.2 2.1 %collective-permute-start.16 = (bf16[1024,256]{1,0:T(8,128)(2,1)S(1)}, bf16[1024,256]{1,0:T(8,128)(2,1)}, u32[]{:S(2)}, u32[]{:S(2)}) collective-permute-start(bf16[1024,256]{1,0:T(8,128)(2,1)S(1)} %get-tuple-element.29), channel_id=1, source_target_pairs={{0,1},{1,2},{2,3},{3,0},{4,5},{5,6},{6,7},{7,4},{8,9},{9,10},{10,1... | collective-permute-start | bytes 1572872 | tf_op jit(solution)/shard_map/ppermute | solution.py:45
  55.3 6.8 %collective-permute-done.11.b2 = bf16[1024,256]{1,0:T(8,128)(2,1)} collective-permute-done((bf16[1024,256]{1,0:T(8,128)(2,1)}, bf16[1024,256]{1,0:T(8,128)(2,1)}, u32[]{:S(2)}, u32[]{:S(2)}) %collective-permute-start.11) | collective-permute-done | bytes 524320 | tf_op jit(solution)/shard_map/ppermute | solution.py:45
  63.2 11.9 %collective-permute-done.10.b1 = bf16[1024,256]{1,0:T(8,128)(2,1)} collective-permute-done((bf16[1024,256]{1,0:T(8,128)(2,1)}, bf16[1024,256]{1,0:T(8,128)(2,1)}, u32[]{:S(2)}, u32[]{:S(2)}) %collective-permute-start.10) | collective-permute-done | bytes 524320 | tf_op jit(solution)/shard_map/ppermute | solution.py:45
  75.1 5.8 %spectra.2 = (s16[1024,128]{1,0:T(8,128)(2,1)}, s16[1024,128]{1,0:T(8,128)(2,1)}, s16[1024,128]{1,0:T(8,128)(2,1)}, s16[1024,128]{1,0:T(8,128)(2,1)}) custom-call(bf16[1024,256]{1,0:T(8,128)(2,1)} %get-tuple-element.28.b0, bf16[1024,256]{1,0:T(8,128)(2,1)} %collective-permute-done.10.b1, bf16[1024,256]{1,0:T(8,128)(2,1)} %collective-permute-done.11.b2, ...), custom_call_target="tpu_custom_call" | custom-call | flops 2147483648 | bytes 5242880 | tf_op jit(solution)/shard_map/spectra/pallas_call | solution.py:77
  80.9 0.7 collective-permute-start.13
  82.4 1.4 collective-permute-start.8
  83.8 2.5 %collective-permute-done.16.b1 = bf16[1024,256]{1,0:T(8,128)(2,1)} collective-permute-done((bf16[1024,256]{1,0:T(8,128)(2,1)S(1)}, bf16[1024,256]{1,0:T(8,128)(2,1)}, u32[]{:S(2)}, u32[]{:S(2)}) %collective-permute-start.16) | collective-permute-done | bytes 524320 | tf_op jit(solution)/shard_map/ppermute | solution.py:45
  86.3 1.3 collective-permute-start.9
  87.6 2.7 %collective-permute-start.14 = (s16[1024,128]{1,0:T(8,128)(2,1)}, s16[1024,128]{1,0:T(8,128)(2,1)S(1)}, u32[]{:S(2)}, u32[]{:S(2)}) collective-permute-start(s16[1024,128]{1,0:T(8,128)(2,1)} %get-tuple-element.12), channel_id=1, source_target_pairs={{0,2},{1,3},{2,0},{3,1},{4,6},{5,7},{6,4},{7,5},{8,10},{9,11},{10,... | collective-permute-start | bytes 786440 | tf_op jit(solution)/shard_map/ppermute | solution.py:45
  90.3 5.8 %spectra.3 = (s16[1024,128]{1,0:T(8,128)(2,1)}, s16[1024,128]{1,0:T(8,128)(2,1)}, s16[1024,128]{1,0:T(8,128)(2,1)}, s16[1024,128]{1,0:T(8,128)(2,1)}) custom-call(bf16[1024,256]{1,0:T(8,128)(2,1)} %get-tuple-element.30.b0, bf16[1024,256]{1,0:T(8,128)(2,1)} %collective-permute-done.16.b1, bf16[1024,256]{1,0:T(8,128)(2,1)} %collective-permute-done.17.b2, ...), custom_call_target="tpu_custom_call" | custom-call | flops 2147483648 | bytes 5242880 | tf_op jit(solution)/shard_map/spectra/pallas_call | solution.py:77
  96.1 11.0 %collective-permute-start.15 = (s16[1024,128]{1,0:T(8,128)(2,1)S(1)}, s16[1024,128]{1,0:T(8,128)(2,1)S(1)}, u32[]{:S(2)}, u32[]{:S(2)}) collective-permute-start(s16[1024,128]{1,0:T(8,128)(2,1)S(1)} %copy-done.12), channel_id=1, source_target_pairs={{0,3},{1,0},{2,1},{3,2},{4,7},{5,4},{6,5},{7,6},{8,11},{9,8},{10,9... | collective-permute-start | bytes 786440 | tf_op jit(solution)/shard_map/ppermute | solution.py:45
  107.0 1.2 collective-permute-start.19
  108.3 1.5 collective-permute-start.20
  109.7 2.5 %collective-permute-start.21 = (s16[1024,128]{1,0:T(8,128)(2,1)}, s16[1024,128]{1,0:T(8,128)(2,1)S(1)}, u32[]{:S(2)}, u32[]{:S(2)}) collective-permute-start(s16[1024,128]{1,0:T(8,128)(2,1)} %get-tuple-element.17), channel_id=1, source_target_pairs={{0,3},{1,0},{2,1},{3,2},{4,7},{5,4},{6,5},{7,6},{8,11},{9,8},{10,9... | collective-permute-start | bytes 786440 | tf_op jit(solution)/shard_map/ppermute | solution.py:45
  112.8 0.7 pad_maximum_fusion.shot
  113.5 17.7 %gather_terms.1.refs_2_ = f32[8192,128]{1,0:T(8,128)} custom-call(s32[8192]{0:T(1024)} %bitcast.20, s32[8192]{0:T(1024)} %bitcast.22, s16[4096,128]{1,0:T(8,128)(2,1)} %copy-done.1, s16[4096,128]{1,0:T(8,128)(2,1)} %copy-done.2, f32[384,128]{1,0:T(8,128)} %pad_maximum_fusion.shot), custom_call_target="tpu_custom_call" | custom-call | flops 1048576 | bytes 50331648 | tf_op jit(solution)/shard_map/gather_terms/pallas_call | solution.py:107
  132.3 27.0 %sum_receivers.1 = f32[8192,128]{1,0:T(8,128)} custom-call(s32[8192]{0:T(1024)} %bitcast.21, s32[8]{0:T(128)} %broadcast_subtract_fusion.1.refs_1_, f32[8192,128]{1,0:T(8,128)} %gather_terms.1.refs_2_, s16[1024,128]{1,0:T(8,128)(2,1)} %get-tuple-element.10.refs_3_, s16[1024,128]{1,0:T(8,128)(2,1)} %copy-done.3, s16[1024,128]{1,0:T(8,128)(2,1)} %copy-done.4, ...), custom_call_target="tpu_custom_call" | custom-call | flops 1048576 | bytes 50331648 | tf_op jit(solution)/shard_map/sum_receivers/pallas_call | solution.py:160
  159.4 1.9 slice.104
  161.6 4.1 %collective-permute-done.24 = f32[4096,128]{1,0:T(8,128)S(1)} collective-permute-done((f32[4096,128]{1,0:T(8,128)S(1)}, f32[4096,128]{1,0:T(8,128)S(1)}, u32[]{:S(2)}, u32[]{:S(2)}) %collective-permute-start.24) | collective-permute-done | bytes 2097184 | tf_op jit(solution)/shard_map/ppermute | solution.py:41
  166.0 0.9 fusion.34
  167.5 0.9 collective-permute-start.27
  168.3 1.8 collective-permute-start.26
  170.2 0.7 broadcast_in_dim_reshape.3.refs_0_
  170.8 5.8 %sum_shots.1 = f32[384,128]{1,0:T(8,128)} custom-call(s32[1,8192]{1,0:T(1,128)} %broadcast_in_dim_reshape.3.refs_0_, s32[8]{0:T(128)} %broadcast_subtract_fusion.1.refs_1_, f32[8192,128]{1,0:T(8,128)} %gather_terms.1.refs_2_, s16[1024,128]{1,0:T(8,128)(2,1)} %get-tuple-element.10.refs_3_, s16[1024,128]{1,0:T(8,128)(2,1)} %copy-done.3, ...), custom_call_target="tpu_custom_call" | custom-call | flops 1610612736 | bytes 12582912 | tf_op jit(solution)/shard_map/sum_shots/pallas_call | solution.py:192
  176.6 5.6 %collective-permute-done.25 = f16[1024,128]{1,0:T(8,128)(2,1)S(1)} collective-permute-done((f16[1024,128]{1,0:T(8,128)(2,1)}, f16[1024,128]{1,0:T(8,128)(2,1)S(1)}, u32[]{:S(2)}, u32[]{:S(2)}) %collective-permute-start.25) | collective-permute-done | bytes 262176 | tf_op jit(solution)/shard_map/ppermute | solution.py:29
  182.8 1.1 collective-permute-start.28
  183.9 0.9 fusion.35
  184.8 1.3 collective-permute-start.22
  186.1 1.3 collective-permute-start.23
  188.0 5.0 %collective-permute-start.29 = (f16[128,128]{1,0:T(8,128)(2,1)S(1)}, f16[128,128]{1,0:T(8,128)(2,1)S(1)}, u32[]{:S(2)}, u32[]{:S(2)}) collective-permute-start(f16[128,128]{1,0:T(8,128)(2,1)S(1)} %get-tuple-element.37), channel_id=1, source_target_pairs={{0,64},{4,68},{8,72},{12,76},{16,80},{20,84},{24,88},{28,92},{32,9... | collective-permute-start | bytes 98312 | tf_op jit(solution)/shard_map/ppermute | solution.py:33
  193.0 2.1 %collective-permute-start.31 = (f16[128,128]{1,0:T(8,128)(2,1)S(1)}, f16[128,128]{1,0:T(8,128)(2,1)S(1)}, u32[]{:S(2)}, u32[]{:S(2)}) collective-permute-start(f16[128,128]{1,0:T(8,128)(2,1)S(1)} %get-tuple-element.38), channel_id=1, source_target_pairs={{0,128},{4,132},{8,136},{12,140},{16,144},{20,148},{24,152},{28,15... | collective-permute-start | bytes 98312 | tf_op jit(solution)/shard_map/ppermute | solution.py:33
  195.1 4.0 %collective-permute-start.30 = (f16[128,128]{1,0:T(8,128)(2,1)S(1)}, f16[128,128]{1,0:T(8,128)(2,1)S(1)}, u32[]{:S(2)}, u32[]{:S(2)}) collective-permute-start(f16[128,128]{1,0:T(8,128)(2,1)S(1)} %get-tuple-element.39), channel_id=1, source_target_pairs={{0,192},{4,196},{8,200},{12,204},{16,208},{20,212},{24,216},{28,22... | collective-permute-start | bytes 98312 | tf_op jit(solution)/shard_map/ppermute | solution.py:33
  199.1 1.5 fusion.4
  200.6 0.6 collective-permute-done.31
  201.2 0.6 slice_add_fusion.3
  (96 shorter events, 6.9 us)
Async XLA Ops:
  1.5 19.0 %collective-permute-start.2 = (s16[128,128]{1,0:T(8,128)(2,1)S(1)}, s16[128,128]{1,0:T(8,128)(2,1)S(1)}, u32[]{:S(2)}, u32[]{:S(2)}) collective-permute-start(s16[128,128]{1,0:T(8,128)(2,1)S(1)} %get-tuple-element.23), channel_id=1, source_target_pairs={{0,64},{4,68},{8,72},{12,76},{16,80},{20,84},{24,88},{28,92},{32,9... | collective-permute-start | bytes 98312 | tf_op jit(solution)/shard_map/ppermute | solution.py:33
  4.8 15.7 %collective-permute-start.1 = (s16[128,128]{1,0:T(8,128)(2,1)S(1)}, s16[128,128]{1,0:T(8,128)(2,1)S(1)}, u32[]{:S(2)}, u32[]{:S(2)}) collective-permute-start(s16[128,128]{1,0:T(8,128)(2,1)S(1)} %get-tuple-element.23), channel_id=1, source_target_pairs={{0,128},{4,132},{8,136},{12,140},{16,144},{20,148},{24,152},{28,15... | collective-permute-start | bytes 98312 | tf_op jit(solution)/shard_map/ppermute | solution.py:33
  10.2 10.3 %collective-permute-start = (s16[128,128]{1,0:T(8,128)(2,1)S(1)}, s16[128,128]{1,0:T(8,128)(2,1)S(1)}, u32[]{:S(2)}, u32[]{:S(2)}) collective-permute-start(s16[128,128]{1,0:T(8,128)(2,1)S(1)} %get-tuple-element.23), channel_id=1, source_target_pairs={{0,192},{4,196},{8,200},{12,204},{16,208},{20,212},{24,216},{28,22... | collective-permute-start | bytes 98312 | tf_op jit(solution)/shard_map/ppermute | solution.py:33
  16.7 35.4 %copy-start.10 = (s32[8192]{0:T(1024)S(1)}, s32[8192]{0:T(1024)}, u32[]{:S(2)}) copy-start(s32[8192]{0:T(1024)} %param.8) | copy-start | bytes 98308
  16.8 36.3 %copy-start.11 = (s32[8192]{0:T(1024)S(1)}, s32[8192]{0:T(1024)}, u32[]{:S(2)}) copy-start(s32[8192]{0:T(1024)} %param.7) | copy-start | bytes 98308
  16.8 65.6 %collective-permute-start.18 = (bf16[1024,256]{1,0:T(8,128)(2,1)}, bf16[1024,256]{1,0:T(8,128)(2,1)}, u32[]{:S(2)}, u32[]{:S(2)}) collective-permute-start(bf16[1024,256]{1,0:T(8,128)(2,1)} %get-tuple-element.24), channel_id=1, source_target_pairs={{0,3},{1,0},{2,1},{3,2},{4,7},{5,4},{6,5},{7,6},{8,11},{9,8},{10,9... | collective-permute-start | bytes 1572872 | tf_op jit(solution)/shard_map/ppermute | solution.py:45
  17.3 35.9 %collective-permute-start.12 = (bf16[1024,256]{1,0:T(8,128)(2,1)}, bf16[1024,256]{1,0:T(8,128)(2,1)}, u32[]{:S(2)}, u32[]{:S(2)}) collective-permute-start(bf16[1024,256]{1,0:T(8,128)(2,1)} %get-tuple-element.25), channel_id=1, source_target_pairs={{0,3},{1,0},{2,1},{3,2},{4,7},{5,4},{6,5},{7,6},{8,11},{9,8},{10,9... | collective-permute-start | bytes 1572872 | tf_op jit(solution)/shard_map/ppermute | solution.py:45
  20.5 5.1 %collective-permute-start.3 = (s16[512,128]{1,0:T(8,128)(2,1)S(1)}, s16[512,128]{1,0:T(8,128)(2,1)S(1)}, u32[]{:S(2)}, u32[]{:S(2)}) collective-permute-start(s16[512,128]{1,0:T(8,128)(2,1)S(1)} %pad_add_fusion), channel_id=1, source_target_pairs={{0,32},{4,36},{8,40},{12,44},{16,48},{20,52},{24,56},{28,60},{32,0... | collective-permute-start | bytes 393224 | tf_op jit(solution)/shard_map/ppermute | solution.py:37
  25.6 26.3 %collective-permute-start.6 = (s16[1024,128]{1,0:T(8,128)(2,1)S(1)}, s16[1024,128]{1,0:T(8,128)(2,1)S(1)}, u32[]{:S(2)}, u32[]{:S(2)}) collective-permute-start(s16[1024,128]{1,0:T(8,128)(2,1)S(1)} %get-tuple-element.40), channel_id=1, source_target_pairs={{0,8},{4,12},{8,16},{12,20},{16,24},{20,28},{24,0},{28,4},{32,40},... | collective-permute-start | bytes 786440 | tf_op jit(solution)/shard_map/ppermute | solution.py:29
  27.2 22.5 %collective-permute-start.5 = (s16[1024,128]{1,0:T(8,128)(2,1)S(1)}, s16[1024,128]{1,0:T(8,128)(2,1)S(1)}, u32[]{:S(2)}, u32[]{:S(2)}) collective-permute-start(s16[1024,128]{1,0:T(8,128)(2,1)S(1)} %get-tuple-element.40), channel_id=1, source_target_pairs={{0,16},{4,20},{8,24},{12,28},{16,0},{20,4},{24,8},{28,12},{32,48},... | collective-permute-start | bytes 786440 | tf_op jit(solution)/shard_map/ppermute | solution.py:29
  29.9 19.7 %collective-permute-start.4 = (s16[1024,128]{1,0:T(8,128)(2,1)S(1)}, s16[1024,128]{1,0:T(8,128)(2,1)S(1)}, u32[]{:S(2)}, u32[]{:S(2)}) collective-permute-start(s16[1024,128]{1,0:T(8,128)(2,1)S(1)} %get-tuple-element.40), channel_id=1, source_target_pairs={{0,24},{4,28},{8,0},{12,4},{16,8},{20,12},{24,16},{28,20},{32,56},... | collective-permute-start | bytes 786440 | tf_op jit(solution)/shard_map/ppermute | solution.py:29
  49.6 12.5 %collective-permute-start.11 = (bf16[1024,256]{1,0:T(8,128)(2,1)}, bf16[1024,256]{1,0:T(8,128)(2,1)}, u32[]{:S(2)}, u32[]{:S(2)}) collective-permute-start(bf16[1024,256]{1,0:T(8,128)(2,1)} %get-tuple-element.26), channel_id=1, source_target_pairs={{0,2},{1,3},{2,0},{3,1},{4,6},{5,7},{6,4},{7,5},{8,10},{9,11},{10,... | collective-permute-start | bytes 1572872 | tf_op jit(solution)/shard_map/ppermute | solution.py:45
  49.7 25.4 %collective-permute-start.10 = (bf16[1024,256]{1,0:T(8,128)(2,1)}, bf16[1024,256]{1,0:T(8,128)(2,1)}, u32[]{:S(2)}, u32[]{:S(2)}) collective-permute-start(bf16[1024,256]{1,0:T(8,128)(2,1)} %get-tuple-element.27), channel_id=1, source_target_pairs={{0,1},{1,2},{2,3},{3,0},{4,5},{5,6},{6,7},{7,4},{8,9},{9,10},{10,1... | collective-permute-start | bytes 1572872 | tf_op jit(solution)/shard_map/ppermute | solution.py:45
  52.0 28.8 %copy-start.1 = (s16[4096,128]{1,0:T(8,128)(2,1)}, s16[4096,128]{1,0:T(8,128)(2,1)S(1)}, u32[]{:S(2)}) copy-start(s16[4096,128]{1,0:T(8,128)(2,1)S(1)} %constant_dynamic-update-slice_fusion.5.own) | copy-start | bytes 3145732
  52.0 57.7 %collective-permute-start.7 = (s16[4096,128]{1,0:T(8,128)(2,1)S(1)}, s16[4096,128]{1,0:T(8,128)(2,1)S(1)}, u32[]{:S(2)}, u32[]{:S(2)}) collective-permute-start(s16[4096,128]{1,0:T(8,128)(2,1)S(1)} %constant_dynamic-update-slice_fusion.5.own), channel_id=1, source_target_pairs={{0,4},{4,0},{8,12},{12,8},{16,20},{20,16},{24,28},{28,24},{32,36},... | collective-permute-start | bytes 3145736 | tf_op jit(solution)/shard_map/ppermute | solution.py:41
  53.2 33.1 %collective-permute-start.16 = (bf16[1024,256]{1,0:T(8,128)(2,1)S(1)}, bf16[1024,256]{1,0:T(8,128)(2,1)}, u32[]{:S(2)}, u32[]{:S(2)}) collective-permute-start(bf16[1024,256]{1,0:T(8,128)(2,1)S(1)} %get-tuple-element.29), channel_id=1, source_target_pairs={{0,1},{1,2},{2,3},{3,0},{4,5},{5,6},{6,7},{7,4},{8,9},{9,10},{10,1... | collective-permute-start | bytes 1572872 | tf_op jit(solution)/shard_map/ppermute | solution.py:45
  62.1 25.5 %collective-permute-start.17 = (bf16[1024,256]{1,0:T(8,128)(2,1)S(1)}, bf16[1024,256]{1,0:T(8,128)(2,1)}, u32[]{:S(2)}, u32[]{:S(2)}) collective-permute-start(bf16[1024,256]{1,0:T(8,128)(2,1)S(1)} %get-tuple-element.31), channel_id=1, source_target_pairs={{0,2},{1,3},{2,0},{3,1},{4,6},{5,7},{6,4},{7,5},{8,10},{9,11},{10,... | collective-permute-start | bytes 1572872 | tf_op jit(solution)/shard_map/ppermute | solution.py:45
  62.4 20.0 %copy-start.9 = (f32[128,128]{1,0:T(8,128)S(1)}, f32[128,128]{1,0:T(8,128)}, u32[]{:S(2)}) copy-start(f32[128,128]{1,0:T(8,128)} %param.10) | copy-start | bytes 196612
  80.9 27.4 %collective-permute-start.13 = (s16[1024,128]{1,0:T(8,128)(2,1)}, s16[1024,128]{1,0:T(8,128)(2,1)S(1)}, u32[]{:S(2)}, u32[]{:S(2)}) collective-permute-start(s16[1024,128]{1,0:T(8,128)(2,1)} %get-tuple-element.11), channel_id=1, source_target_pairs={{0,1},{1,2},{2,3},{3,0},{4,5},{5,6},{6,7},{7,4},{8,9},{9,10},{10,1... | collective-permute-start | bytes 786440 | tf_op jit(solution)/shard_map/ppermute | solution.py:45
  82.3 13.7 %copy-start.12 = (s16[1024,128]{1,0:T(8,128)(2,1)S(1)}, s16[1024,128]{1,0:T(8,128)(2,1)}, u32[]{:S(2)}) copy-start(s16[1024,128]{1,0:T(8,128)(2,1)} %get-tuple-element.13) | copy-start | bytes 786436
  82.4 13.7 %collective-permute-start.8 = (f32[128,128]{1,0:T(8,128)S(1)}, f32[128,128]{1,0:T(8,128)S(1)}, u32[]{:S(2)}, u32[]{:S(2)}) collective-permute-start(f32[128,128]{1,0:T(8,128)S(1)} %copy-done.9), channel_id=1, source_target_pairs={{0,4},{4,8},{8,12},{12,16},{16,20},{20,24},{24,28},{28,32},{32,36}... | collective-permute-start | bytes 196616 | tf_op jit(solution)/shard_map/ppermute | solution.py:205
  86.3 20.7 %collective-permute-start.9 = (f32[128,128]{1,0:T(8,128)S(1)}, f32[128,128]{1,0:T(8,128)S(1)}, u32[]{:S(2)}, u32[]{:S(2)}) collective-permute-start(f32[128,128]{1,0:T(8,128)S(1)} %copy-done.9), channel_id=1, source_target_pairs={{4,0},{8,4},{12,8},{16,12},{20,16},{24,20},{28,24},{32,28},{36,32}... | collective-permute-start | bytes 196616 | tf_op jit(solution)/shard_map/ppermute | solution.py:205
  87.6 43.7 %collective-permute-start.14 = (s16[1024,128]{1,0:T(8,128)(2,1)}, s16[1024,128]{1,0:T(8,128)(2,1)S(1)}, u32[]{:S(2)}, u32[]{:S(2)}) collective-permute-start(s16[1024,128]{1,0:T(8,128)(2,1)} %get-tuple-element.12), channel_id=1, source_target_pairs={{0,2},{1,3},{2,0},{3,1},{4,6},{5,7},{6,4},{7,5},{8,10},{9,11},{10,... | collective-permute-start | bytes 786440 | tf_op jit(solution)/shard_map/ppermute | solution.py:45
  96.1 35.2 %collective-permute-start.15 = (s16[1024,128]{1,0:T(8,128)(2,1)S(1)}, s16[1024,128]{1,0:T(8,128)(2,1)S(1)}, u32[]{:S(2)}, u32[]{:S(2)}) collective-permute-start(s16[1024,128]{1,0:T(8,128)(2,1)S(1)} %copy-done.12), channel_id=1, source_target_pairs={{0,3},{1,0},{2,1},{3,2},{4,7},{5,4},{6,5},{7,6},{8,11},{9,8},{10,9... | collective-permute-start | bytes 786440 | tf_op jit(solution)/shard_map/ppermute | solution.py:45
  107.0 24.3 %collective-permute-start.19 = (s16[1024,128]{1,0:T(8,128)(2,1)}, s16[1024,128]{1,0:T(8,128)(2,1)S(1)}, u32[]{:S(2)}, u32[]{:S(2)}) collective-permute-start(s16[1024,128]{1,0:T(8,128)(2,1)} %get-tuple-element.15), channel_id=1, source_target_pairs={{0,1},{1,2},{2,3},{3,0},{4,5},{5,6},{6,7},{7,4},{8,9},{9,10},{10,1... | collective-permute-start | bytes 786440 | tf_op jit(solution)/shard_map/ppermute | solution.py:45
  108.3 23.1 %copy-start.3 = (s16[1024,128]{1,0:T(8,128)(2,1)}, s16[1024,128]{1,0:T(8,128)(2,1)S(1)}, u32[]{:S(2)}) copy-start(s16[1024,128]{1,0:T(8,128)(2,1)S(1)} %collective-permute-done.13.refs_4_) | copy-start | bytes 786436
  108.3 23.1 %collective-permute-start.20 = (s16[1024,128]{1,0:T(8,128)(2,1)}, s16[1024,128]{1,0:T(8,128)(2,1)S(1)}, u32[]{:S(2)}, u32[]{:S(2)}) collective-permute-start(s16[1024,128]{1,0:T(8,128)(2,1)} %get-tuple-element.16), channel_id=1, source_target_pairs={{0,2},{1,3},{2,0},{3,1},{4,6},{5,7},{6,4},{7,5},{8,10},{9,11},{10,... | collective-permute-start | bytes 786440 | tf_op jit(solution)/shard_map/ppermute | solution.py:45
  109.7 3.8 %copy-start.2 = (s16[4096,128]{1,0:T(8,128)(2,1)}, s16[4096,128]{1,0:T(8,128)(2,1)S(1)}, u32[]{:S(2)}) copy-start(s16[4096,128]{1,0:T(8,128)(2,1)S(1)} %collective-permute-done.7.other) | copy-start | bytes 3145732
  109.7 21.6 %collective-permute-start.21 = (s16[1024,128]{1,0:T(8,128)(2,1)}, s16[1024,128]{1,0:T(8,128)(2,1)S(1)}, u32[]{:S(2)}, u32[]{:S(2)}) collective-permute-start(s16[1024,128]{1,0:T(8,128)(2,1)} %get-tuple-element.17), channel_id=1, source_target_pairs={{0,3},{1,0},{2,1},{3,2},{4,7},{5,4},{6,5},{7,6},{8,11},{9,8},{10,9... | collective-permute-start | bytes 786440 | tf_op jit(solution)/shard_map/ppermute | solution.py:45
  131.3 0.7 copy-start.4
  131.3 0.8 copy-start.5
  131.3 0.9 copy-start.6
  131.3 0.9 copy-start.7
  131.4 1.0 copy-start.8
  159.4 6.4 %copy-start = (f32[8192,128]{1,0:T(8,128)S(1)}, f32[8192,128]{1,0:T(8,128)}, u32[]{:S(2)}) copy-start(f32[8192,128]{1,0:T(8,128)} %sum_receivers.1) | copy-start | bytes 12582916
  161.3 4.5 %collective-permute-start.24 = (f32[4096,128]{1,0:T(8,128)S(1)}, f32[4096,128]{1,0:T(8,128)S(1)}, u32[]{:S(2)}, u32[]{:S(2)}) collective-permute-start(f32[4096,128]{1,0:T(8,128)S(1)} %slice.104), channel_id=1, source_target_pairs={{0,4},{4,0},{8,12},{12,8},{16,20},{20,16},{24,28},{28,24},{32,36},... | collective-permute-start | bytes 6291464 | tf_op jit(solution)/shard_map/ppermute | solution.py:41
  166.9 15.4 %collective-permute-start.25 = (f16[1024,128]{1,0:T(8,128)(2,1)}, f16[1024,128]{1,0:T(8,128)(2,1)S(1)}, u32[]{:S(2)}, u32[]{:S(2)}) collective-permute-start(f16[1024,128]{1,0:T(8,128)(2,1)} %get-tuple-element.32), channel_id=1, source_target_pairs={{0,8},{4,12},{8,16},{12,20},{16,24},{20,28},{24,0},{28,4},{32,40},... | collective-permute-start | bytes 786440 | tf_op jit(solution)/shard_map/ppermute | solution.py:29
  167.5 14.8 %collective-permute-start.27 = (f16[1024,128]{1,0:T(8,128)(2,1)S(1)}, f16[1024,128]{1,0:T(8,128)(2,1)S(1)}, u32[]{:S(2)}, u32[]{:S(2)}) collective-permute-start(f16[1024,128]{1,0:T(8,128)(2,1)S(1)} %get-tuple-element.33), channel_id=1, source_target_pairs={{0,16},{4,20},{8,24},{12,28},{16,0},{20,4},{24,8},{28,12},{32,48},... | collective-permute-start | bytes 786440 | tf_op jit(solution)/shard_map/ppermute | solution.py:29
  168.3 14.3 %collective-permute-start.26 = (f16[1024,128]{1,0:T(8,128)(2,1)S(1)}, f16[1024,128]{1,0:T(8,128)(2,1)S(1)}, u32[]{:S(2)}, u32[]{:S(2)}) collective-permute-start(f16[1024,128]{1,0:T(8,128)(2,1)S(1)} %get-tuple-element.34), channel_id=1, source_target_pairs={{0,24},{4,28},{8,0},{12,4},{16,8},{20,12},{24,16},{28,20},{32,56},... | collective-permute-start | bytes 786440 | tf_op jit(solution)/shard_map/ppermute | solution.py:29
  182.8 5.1 %collective-permute-start.28 = (f16[512,128]{1,0:T(8,128)(2,1)S(1)}, f16[512,128]{1,0:T(8,128)(2,1)S(1)}, u32[]{:S(2)}, u32[]{:S(2)}) collective-permute-start(f16[512,128]{1,0:T(8,128)(2,1)S(1)} %fusion.3), channel_id=1, source_target_pairs={{0,32},{4,36},{8,40},{12,44},{16,48},{20,52},{24,56},{28,60},{32,0... | collective-permute-start | bytes 393224 | tf_op jit(solution)/shard_map/ppermute | solution.py:37
  184.8 14.2 %collective-permute-start.22 = (f32[128,128]{1,0:T(8,128)S(1)}, f32[128,128]{1,0:T(8,128)S(1)}, u32[]{:S(2)}, u32[]{:S(2)}) collective-permute-start(f32[128,128]{1,0:T(8,128)S(1)} %get-tuple-element.35), channel_id=1, source_target_pairs={{0,4},{4,8},{8,12},{12,16},{16,20},{20,24},{24,28},{28,32},{32,36}... | collective-permute-start | bytes 196616 | tf_op jit(solution)/shard_map/ppermute | solution.py:205
  186.1 12.9 %collective-permute-start.23 = (f32[128,128]{1,0:T(8,128)S(1)}, f32[128,128]{1,0:T(8,128)S(1)}, u32[]{:S(2)}, u32[]{:S(2)}) collective-permute-start(f32[128,128]{1,0:T(8,128)S(1)} %get-tuple-element.36), channel_id=1, source_target_pairs={{4,0},{8,4},{12,8},{16,12},{20,16},{24,20},{28,24},{32,28},{36,32}... | collective-permute-start | bytes 196616 | tf_op jit(solution)/shard_map/ppermute | solution.py:205
  188.0 12.6 %collective-permute-start.29 = (f16[128,128]{1,0:T(8,128)(2,1)S(1)}, f16[128,128]{1,0:T(8,128)(2,1)S(1)}, u32[]{:S(2)}, u32[]{:S(2)}) collective-permute-start(f16[128,128]{1,0:T(8,128)(2,1)S(1)} %get-tuple-element.37), channel_id=1, source_target_pairs={{0,64},{4,68},{8,72},{12,76},{16,80},{20,84},{24,88},{28,92},{32,9... | collective-permute-start | bytes 98312 | tf_op jit(solution)/shard_map/ppermute | solution.py:33
  193.0 8.2 %collective-permute-start.31 = (f16[128,128]{1,0:T(8,128)(2,1)S(1)}, f16[128,128]{1,0:T(8,128)(2,1)S(1)}, u32[]{:S(2)}, u32[]{:S(2)}) collective-permute-start(f16[128,128]{1,0:T(8,128)(2,1)S(1)} %get-tuple-element.38), channel_id=1, source_target_pairs={{0,128},{4,132},{8,136},{12,140},{16,144},{20,148},{24,152},{28,15... | collective-permute-start | bytes 98312 | tf_op jit(solution)/shard_map/ppermute | solution.py:33
  195.1 6.1 %collective-permute-start.30 = (f16[128,128]{1,0:T(8,128)(2,1)S(1)}, f16[128,128]{1,0:T(8,128)(2,1)S(1)}, u32[]{:S(2)}, u32[]{:S(2)}) collective-permute-start(f16[128,128]{1,0:T(8,128)(2,1)S(1)} %get-tuple-element.39), channel_id=1, source_target_pairs={{0,192},{4,196},{8,200},{12,204},{16,208},{20,212},{24,216},{28,22... | collective-permute-start | bytes 98312 | tf_op jit(solution)/shard_map/ppermute | solution.py:33

commit v2 on v1

--- a/solution.py
+++ b/solution.py
@@ -14,6 +14,8 @@
 REC_SCALE = 65535.0 / (REC_HIGH - REC_LOW)
 SUM_SCALE = 1.0 / 32.0
 CHUNKS = 2
+SMALL = pltpu.CompilerParams(vmem_limit_bytes=12 * 2**20)
+COST = pl.CostEstimate(flops=1000, bytes_accessed=1000, transcendentals=0)
 VMEM = pltpu.CompilerParams(vmem_limit_bytes=56 * 2**20)
 
 
@@ -46,23 +48,112 @@
 
 
 def make_table(samples, y, width):
-    part = samples // NY
-    steps = jnp.arange(NY, dtype=jnp.int32)
-    times = (((y - steps) % NY) * part)[:, None] + jnp.arange(part, dtype=jnp.int32)[None, :]
-    times = times.reshape(samples, 1)
-    freqs = (((y + steps) % NY) * width)[:, None] + jnp.arange(width, dtype=jnp.int32)[None, :]
-    freqs = jnp.stack([freqs, freqs], axis=1).reshape(1, NY * 2 * width)
-    imag = (jnp.arange(NY * 2 * width, dtype=jnp.int32) // width % 2 == 1)[None, :]
-    phase = times * freqs % samples
-    angle = phase.astype(jnp.float32) * (2.0 * math.pi / samples)
-    return jnp.where(imag, -jnp.sin(angle), jnp.cos(angle)).astype(jnp.bfloat16)
-
-
-def spectra(blocks, table, width):
+    part, cols = samples // NY, NY * 2 * width
+    tile = 128
+    quarter = samples // 4
+
+    def body(y_ref, out):
+        y = y_ref[0]
+        row = pl.program_id(0) * tile
+        time = (y - row // part) % NY * part + row % part + lax.broadcasted_iota(jnp.int32, (tile, 1), 0)
+        for k in range(NY):
+            first = (y + k) % NY * width
+            for half in range(2):
+                freq = first + lax.broadcasted_iota(jnp.int32, (1, width), 1)
+                phase = (time * freq + half * quarter) % samples
+                turn = (phase + quarter // 2) // quarter
+                rest = (phase - turn * quarter).astype(jnp.float32) * (2.0 * math.pi / samples)
+                sq = rest * rest
+                cos = 1.0 + sq * (-0.5 + sq * (1 / 24 + sq * (-1 / 720 + sq * (1 / 40320 - sq * (1 / 3628800)))))
+                sin = rest * (1.0 + sq * (-1 / 6 + sq * (1 / 120 + sq * (-1 / 5040 + sq * (1 / 362880)))))
+                value = jnp.where(turn % 2 == 1, sin, cos)
+                value = jnp.where((turn % 4 == 1) | (turn % 4 == 2), -value, value)
+                out[:, pl.ds((2 * k + half) * width, width)] = value.astype(jnp.bfloat16)
+
+    return pl.pallas_call(
+        body,
+        grid=(samples // tile,),
+        in_specs=[pl.BlockSpec(memory_space=pltpu.SMEM)],
+        out_specs=pl.BlockSpec((tile, cols), lambda i: (i, 0)),
+        out_shape=jax.ShapeDtypeStruct((samples, cols), jnp.bfloat16),
+        compiler_params=SMALL,
+        cost_estimate=COST,
+        name="make_table",
+    )(y[None])
+
+
+def join(parts, after=()):
+    size = parts[0].shape[0]
+
+    def body(*refs):
+        out = refs[-1]
+        for k in range(len(parts)):
+            out[pl.ds(k * size, size), :] = refs[k][...]
+
+    vm = pl.BlockSpec(memory_space=pltpu.VMEM)
+    return pl.pallas_call(
+        body,
+        in_specs=[vm] * len(parts) + [pl.BlockSpec(memory_space=pl.ANY)] * len(after),
+        out_specs=vm,
+        out_shape=jax.ShapeDtypeStruct((size * len(parts),) + parts[0].shape[1:], parts[0].dtype),
+        compiler_params=SMALL,
+        cost_estimate=COST,
+        name="join",
+    )(*parts, *after)
+
+
+def take_rows(traces, y, chunk, after=()):
+    rows, part = traces.shape
+    piece = rows // NY // CHUNKS
+    tile = min(piece, 256)
+    steps = piece // tile
+
+    def body(y_ref, *refs):
+        for a, b in zip(refs[:3], refs[3 + len(after) :]):
+            b[...] = a[...]
+
+    def spot(k):
+        return pl.BlockSpec((tile, part), lambda i, y: (((y[0] + k) % NY * CHUNKS + chunk) * steps + i, 0))
+
+    return pl.pallas_call(
+        body,
+        grid_spec=pltpu.PrefetchScalarGridSpec(
+            num_scalar_prefetch=1,
+            grid=(steps,),
+            in_specs=[spot(k) for k in range(1, NY)] + [pl.BlockSpec(memory_space=pl.ANY)] * len(after),
+            out_specs=[pl.BlockSpec((tile, part), lambda i, y: (i, 0))] * 3,
+        ),
+        out_shape=[jax.ShapeDtypeStruct((piece, part), traces.dtype)] * 3,
+        compiler_params=SMALL,
+        cost_estimate=COST,
+        name="take_rows",
+    )(y[None], traces, traces, traces, *after)
+
+
+def encode_terms(terms, after):
+    def body(a, *refs):
+        b = refs[-1]
+        code = jnp.clip((a[...] - REC_LOW) * REC_SCALE + 0.5, 0.0, 65535.0).astype(jnp.int32) - 32768
+        b[...] = code.astype(jnp.int16)
+
+    vm = pl.BlockSpec(memory_space=pltpu.VMEM)
+    return pl.pallas_call(
+        body,
+        in_specs=[vm] + [pl.BlockSpec(memory_space=pl.ANY)] * len(after),
+        out_specs=vm,
+        out_shape=jax.ShapeDtypeStruct(terms.shape, jnp.int16),
+        compiler_params=SMALL,
+        cost_estimate=COST,
+        name="encode_terms",
+    )(terms, *after)
+
+
+def spectra(traces, y, chunk, blocks, table, width):
     rows, part = blocks[0].shape
-    tile = 512
-
-    def body(b0, b1, b2, b3, t, o0, o1, o2, o3):
+    tile = min(rows, 512)
+    steps = rows // tile
+
+    def body(y_ref, b0, b1, b2, b3, t, o0, o1, o2, o3):
         for k, out in enumerate((o0, o1, o2, o3)):
             cols = pl.ds(k * 2 * width, 2 * width)
             acc = None
@@ -76,15 +167,19 @@
 
     return pl.pallas_call(
         body,
-        grid=(rows // tile,),
-        in_specs=[pl.BlockSpec((tile, part), lambda i: (i, 0))] * 4
-        + [pl.BlockSpec(table.shape, lambda i: (0, 0))],
-        out_specs=[pl.BlockSpec((tile, width), lambda i: (i, 0))] * 4,
+        grid_spec=pltpu.PrefetchScalarGridSpec(
+            num_scalar_prefetch=1,
+            grid=(steps,),
+            in_specs=[pl.BlockSpec((tile, part), lambda i, y: ((y[0] * CHUNKS + chunk) * steps + i, 0))]
+            + [pl.BlockSpec((tile, part), lambda i, y: (i, 0))] * 3
+            + [pl.BlockSpec(table.shape, lambda i, y: (0, 0))],
+            out_specs=[pl.BlockSpec((tile, width), lambda i, y: (i, 0))] * 4,
+        ),
         out_shape=[jax.ShapeDtypeStruct((rows, width), jnp.int16)] * 4,
         compiler_params=VMEM,
-        cost_estimate=pl.CostEstimate(flops=2 * rows * 1024 * 1024, bytes_accessed=rows * 3072 + 2**21, transcendentals=rows * 512),
+        cost_estimate=COST,
         name="spectra",
-    )(*blocks, table)
+    )(y[None], traces, *blocks, table)
 
 
 def gather_terms(own, other, shot_near, rec_at, shot_at):
@@ -96,12 +191,13 @@
         rec[pl.ds(half, half), :] = (other[...].astype(jnp.float32) + 32768.0) * (1.0 / REC_SCALE) + REC_LOW
 
         def step(b, _):
-            for u in range(16):
-                i = b * 16 + u
-                out[pl.ds(i, 1), :] = rec[pl.ds(rec_at[i], 1), :] + shot[pl.ds(shot_at[i], 1), :]
+            at = [b * 32 + u for u in range(32)]
+            row = [rec[pl.ds(rec_at[i], 1), :] + shot[pl.ds(shot_at[i], 1), :] for i in at]
+            for i, value in zip(at, row):
+                out[pl.ds(i, 1), :] = value
             return 0
 
-        lax.fori_loop(0, rows // 16, step, 0)
+        lax.fori_loop(0, rows // 32, step, 0)
 
     vm, sm = pl.BlockSpec(memory_space=pltpu.VMEM), pl.BlockSpec(memory_space=pltpu.SMEM)
     return pl.pallas_call(
@@ -111,7 +207,7 @@
         out_shape=jax.ShapeDtypeStruct((rows, width), jnp.float32),
         scratch_shapes=[pltpu.VMEM((2 * half, width), jnp.float32)],
         compiler_params=VMEM,
-        cost_estimate=pl.CostEstimate(flops=rows * width, bytes_accessed=48 * 2**20, transcendentals=0),
+        cost_estimate=COST,
         name="gather_terms",
     )(rec_at, shot_at, own, other, shot_near)
 
@@ -126,7 +222,7 @@
     rows, width = model.shape
     piece = codes[0].shape[0]
     parts = len(codes)
-    banks, depth = 4, 2
+    banks, group = 8, 32
 
     def body(*refs):
         rec_at, live, model = refs[:3]
@@ -140,21 +236,15 @@
             res[at, :] = residual(code[...], model[at, :], live[k])
 
         def step(b, _):
-            group = banks * depth
-            at = [rec_at[b * group + u] for u in range(group)]
-            row = [res[pl.ds(b * group + u, 1), :] for u in range(group)]
-            for u in range(banks):
-                v = u + banks
-                s = sums[u]
-                first = s[pl.ds(at[u], 1), :]
-                second = s[pl.ds(at[v], 1), :]
-                again = (at[u] == at[v]).astype(jnp.float32)
-                s[pl.ds(at[u], 1), :] = first + row[u]
-                s[pl.ds(at[v], 1), :] = second + (row[v] + again * row[u])
+            for u in range(group):
+                s, at = sums[u % banks], pl.ds(rec_at[b * group + u], 1)
+                s[at, :] = s[at, :] + res[pl.ds(b * group + u, 1), :]
             return 0
 
-        lax.fori_loop(0, rows // (banks * depth), step, 0)
-        out[...] = (sums[0][...] + sums[1][...]) + (sums[2][...] + sums[3][...])
+        lax.fori_loop(0, rows // group, step, 0)
+        out[...] = ((sums[0][...] + sums[1][...]) + (sums[2][...] + sums[3][...])) + (
+            (sums[4][...] + sums[5][...]) + (sums[6][...] + sums[7][...])
+        )
 
     vm, sm = pl.BlockSpec(memory_space=pltpu.VMEM), pl.BlockSpec(memory_space=pltpu.SMEM)
     return pl.pallas_call(
@@ -164,7 +254,7 @@
         out_shape=jax.ShapeDtypeStruct((count, width), jnp.float32),
         scratch_shapes=[pltpu.VMEM((rows, width), jnp.float32)] + [pltpu.VMEM((count, width), jnp.float32)] * (banks - 1),
         compiler_params=VMEM,
-        cost_estimate=pl.CostEstimate(flops=rows * width, bytes_accessed=48 * 2**20, transcendentals=0),
+        cost_estimate=COST,
         name="sum_receivers",
     )(rec_at, live, model, *codes)
 
@@ -195,7 +285,7 @@
         out_specs=vm,
         out_shape=jax.ShapeDtypeStruct((count, width), jnp.float32),
         compiler_params=VMEM,
-        cost_estimate=pl.CostEstimate(flops=4 * rows * width * count, bytes_accessed=12 * 2**20, transcendentals=0),
+        cost_estimate=COST,
         name="sum_shots",
     )(shot_at[None, :], live, model, *codes)
 
@@ -212,18 +302,20 @@
     owner, y = lax.axis_index("tr"), lax.axis_index("fq")
     z, x, c = owner // (NX * NC), owner // NC % NX, owner % NC
 
-    parts = [lax.dynamic_slice_in_dim(traces, (y + k) % NY * share, share, 0) for k in range(NY)]
-    got = [[None] * NY for _ in range(CHUNKS)]
+    got, after = [], ()
     for h in range(CHUNKS):
-        for k in (0, 1, 3, 2):
-            mine = parts[k][h * piece : (h + 1) * piece]
-            got[h][k] = send_y(mine, k) if k else mine
-
-    code = jnp.clip(jnp.round((receiver_terms - REC_LOW) * REC_SCALE), 0.0, 65535.0).astype(jnp.int32) - 32768
-    terms = code.astype(jnp.int16)
-    terms = jnp.concatenate([terms] + [send_z(terms, -2 * k) for k in range(1, NZ // 2)])
-    terms = jnp.concatenate([terms, swap_z(terms)])
-    terms = jnp.concatenate([terms] + [send_x(terms, -k) for k in range(1, NX)])
+        mine = take_rows(traces, y, h, after)
+        come = {k: send_y(mine[k - 1], k) for k in (1, 3, 2)}
+        got.append([come[k] for k in range(1, NY)])
+        after = (come[1], come[3])
+    table = make_table(part * NY, y, width)
+    coded = [spectra(traces, y, h, got[h], table, width) for h in range(CHUNKS)]
+    codes = [send_y(outs[k], k) if k else outs[k] for outs in coded for k in range(NY)]
+
+    terms = encode_terms(receiver_terms, (got[0][0], got[0][2], table))
+    terms = join([terms] + [send_z(terms, -2 * k) for k in range(1, NZ // 2)], (got[0][1],))
+    terms = join([terms, swap_z(terms)], (got[1][0], got[1][2], coded[0][0]))
+    terms = join([terms] + [send_x(terms, -k) for k in range(1, NX)], (codes[1], codes[3], coded[1][0]))
     far_terms = swap_core(terms)
 
     def ordered(v):
@@ -241,11 +333,6 @@
 
     shot_near = jnp.concatenate([neighbour(shot_terms, 1), shot_terms, neighbour(shot_terms, -1)])
 
-    table = make_table(part * NY, y, width)
-    codes = []
-    for h in range(CHUNKS):
-        outs = spectra(got[h], table, width)
-        codes += [send_y(outs[k], k) if k else outs[k] for k in range(NY)]
     model = gather_terms(terms, far_terms, shot_near, rec_at, shot_at)
 
     sums = sum_receivers(codes, model, live, rec_at, block * NZ * NX * NC)

time: 202 us -> 180 us (0.89); the launches traced: 202 us -> 178 us
  other arithmetic: 23.4 us -> 4.09 us
  waiting for transfers between devices: 36.5 us -> 29.8 us
  local copies, waits for them, and re-layouts: 10.8 us -> 14.2 us
  starting transfers between devices: 67.2 us -> 65.1 us
    convert_element_type x1 -> x0, other arithmetic: 18.2 us -> none  [make_table(): return jnp.where(imag, -jnp.sin(angle), jnp.cos(angle)).astype(jnp.bfloat16)]
    pallas_call x2 -> x9, Pallas kernels: 11.5 us -> 23.2 us  [the longest x2 11.5 us: spectra(): pl.pallas_call(body, grid_spec=pltpu.PrefetchScalarGridSpec(num_scalar_pr...]
    pallas_call x1, Pallas kernels: 27 us -> 17.2 us  [sum_receivers(): pl.pallas_call(body, in_specs=[sm, sm] + [vm] * (1 + parts), out_specs=vm...]
    ppermute x12, waiting for transfers between devices: 21.2 us -> 11.4 us  [send_y(): return lax.ppermute(value, 'fq', [(i, (i + k) % NY) for i in range(NY)])]
    ppermute x6, waiting for transfers between devices: 0.66 us -> 9.09 us  [send_z(): lax.ppermute(value, 'tr', [(tr_of(z, x, c), tr_of((z + k) % NZ, x, c)) fo...]
    unnamed x35 -> x54, local copies, waits for them, and re-layouts: 2.37 us -> 10.5 us
    ppermute x6, starting transfers between devices: 22.5 us -> 17.4 us  [send_z(): lax.ppermute(value, 'tr', [(tr_of(z, x, c), tr_of((z + k) % NZ, x, c)) fo...]
    ppermute x2, waiting for transfers between devices: 4.37 us -> 0.01 us  [swap_z(): lax.ppermute(value, 'tr', [(tr_of(z, x, c), tr_of(z ^ 1, x, c)) for z, x,...]
  transfers between devices with their start and end apart: 32 -> 32, of which waited for: 9 -> 12; matrix products, arithmetic and copies ran while one was open for 14% -> 3% of each run, Pallas kernels for 17% -> 26%
where the time goes in v2:
time: 180 us; the launch traced here: 178 us
  starting transfers between devices  65.1 us (36%)
  Pallas kernels  62.8 us (35%)
  waiting for transfers between devices  29.8 us (17%)
  local copies, waits for them, and re-layouts  14.2 us (8%)
  other arithmetic  4.09 us (2%)
  between operations  1.8 us (1%)
    ppermute x12, starting transfers between devices, send_y(): return lax.ppermute(value, 'fq', [(i, (i + k) % NY) for i in range(NY)])  26.4 us
    ppermute x6, starting transfers between devices, send_z(): lax.ppermute(value, 'tr', [(tr_of(z, x, c), tr_of((z + k) % NZ, x, c)) fo...  17.4 us
    pallas_call x1, Pallas kernels, sum_receivers(): pl.pallas_call(body, in_specs=[sm, sm] + [vm] * (1 + parts), out_specs=vm...  17.2 us
    pallas_call x1, Pallas kernels, gather_terms(): pl.pallas_call(body, in_specs=[sm, sm, vm, vm, vm], out_specs=vm, out_sha...  16.5 us
    pallas_call x2, Pallas kernels, spectra(): pl.pallas_call(body, grid_spec=pltpu.PrefetchScalarGridSpec(num_scalar_pr...  11.5 us
    ppermute x12, waiting for transfers between devices, send_y(): return lax.ppermute(value, 'fq', [(i, (i + k) % NY) for i in range(NY)])  11.4 us
    pallas_call x1, Pallas kernels, make_table(): pl.pallas_call(body, grid=(samples // tile,), in_specs=[pl.BlockSpec(memo...  11.2 us
    unnamed x54, local copies, waits for them, and re-layouts  10.5 us
  transfers between devices with their start and end apart: 32, of which 12 were waited for; matrix products, arithmetic and copies ran while one was open for 3% of the time, Pallas kernels for 26%

profile of v2, /device:TPU:8, one launch (start us, length us, event | category | flops | bytes accessed | tf_op | source)
XLA Modules:
  0.0 177.8 jit_solution(9384601956503143897)
XLA Ops:
  0.6 2.2 %copy-done = bf16[8192,256]{1,0:T(8,128)(2,1)S(1)} copy-done((bf16[8192,256]{1,0:T(8,128)(2,1)S(1)}, bf16[8192,256]{1,0:T(8,128)(2,1)}, u32[]{:S(2)}) %copy-start) | copy-done | bytes 4194328
  3.0 1.7 collective-permute-start
  5.4 2.0 %collective-permute-start.5 = (bf16[1024,256]{1,0:T(8,128)(2,1)S(1)}, bf16[1024,256]{1,0:T(8,128)(2,1)S(1)}, u32[]{:S(2)}, u32[]{:S(2)}) collective-permute-start(bf16[1024,256]{1,0:T(8,128)(2,1)S(1)} %get-tuple-element.18), channel_id=1, source_target_pairs={{0,2},{1,3},{2,0},{3,1},{4,6},{5,7},{6,4},{7,5},{8,10},{9,11},{10,... | collective-permute-start | bytes 1572872 | tf_op jit(solution)/shard_map/ppermute | solution.py:47
  7.4 10.7 %collective-permute-done.refs_0_.refs_3_.b1 = bf16[1024,256]{1,0:T(8,128)(2,1)S(1)} collective-permute-done((bf16[1024,256]{1,0:T(8,128)(2,1)S(1)}, bf16[1024,256]{1,0:T(8,128)(2,1)S(1)}, u32[]{:S(2)}, u32[]{:S(2)}) %collective-permute-start) | collective-permute-done | bytes 524320 | tf_op jit(solution)/shard_map/ppermute | solution.py:47
  19.0 9.6 %collective-permute-start.7 = (bf16[1024,256]{1,0:T(8,128)(2,1)S(1)}, bf16[1024,256]{1,0:T(8,128)(2,1)S(1)}, u32[]{:S(2)}, u32[]{:S(2)}) collective-permute-start(bf16[1024,256]{1,0:T(8,128)(2,1)S(1)} %get-tuple-element.19), channel_id=1, source_target_pairs={{0,1},{1,2},{2,3},{3,0},{4,5},{5,6},{6,7},{7,4},{8,9},{9,10},{10,1... | collective-permute-start | bytes 1572872 | tf_op jit(solution)/shard_map/ppermute | solution.py:47
  28.6 4.2 %collective-permute-start.14 = (bf16[1024,256]{1,0:T(8,128)(2,1)S(1)}, bf16[1024,256]{1,0:T(8,128)(2,1)S(1)}, u32[]{:S(2)}, u32[]{:S(2)}) collective-permute-start(bf16[1024,256]{1,0:T(8,128)(2,1)S(1)} %get-tuple-element.24), channel_id=1, source_target_pairs={{0,2},{1,3},{2,0},{3,1},{4,6},{5,7},{6,4},{7,5},{8,10},{9,11},{10,... | collective-permute-start | bytes 1572872 | tf_op jit(solution)/shard_map/ppermute | solution.py:47
  32.8 11.2 %make_table.1.refs_2_.t = bf16[1024,1024]{1,0:T(8,128)(2,1)S(1)} custom-call(s32[1]{0:T(128)} %bitcast.9.y_ref), custom_call_target="tpu_custom_call" | custom-call | flops 1000 | bytes 1000 | tf_op jit(solution)/shard_map/make_table/pallas_call | solution.py:73
  44.1 6.6 %collective-permute-start.2 = (s16[128,128]{1,0:T(8,128)(2,1)S(1)}, s16[128,128]{1,0:T(8,128)(2,1)S(1)}, u32[]{:S(2)}, u32[]{:S(2)}) collective-permute-start(s16[128,128]{1,0:T(8,128)(2,1)S(1)} %encode_terms.1.refs_0_), channel_id=1, source_target_pairs={{0,192},{4,196},{8,200},{12,204},{16,208},{20,212},{24,216},{28,22... | collective-permute-start | bytes 98312 | tf_op jit(solution)/shard_map/ppermute | solution.py:35
  50.7 1.0 collective-permute-start.3
  52.3 2.2 %collective-permute-start.4 = (s16[128,128]{1,0:T(8,128)(2,1)S(1)}, s16[128,128]{1,0:T(8,128)(2,1)S(1)}, u32[]{:S(2)}, u32[]{:S(2)}) collective-permute-start(s16[128,128]{1,0:T(8,128)(2,1)S(1)} %encode_terms.1.refs_0_), channel_id=1, source_target_pairs={{0,64},{4,68},{8,72},{12,76},{16,80},{20,84},{24,88},{28,92},{32,9... | collective-permute-start | bytes 98312 | tf_op jit(solution)/shard_map/ppermute | solution.py:35
  54.6 4.0 %collective-permute-done.3.refs_2_ = s16[128,128]{1,0:T(8,128)(2,1)S(1)} collective-permute-done((s16[128,128]{1,0:T(8,128)(2,1)S(1)}, s16[128,128]{1,0:T(8,128)(2,1)S(1)}, u32[]{:S(2)}, u32[]{:S(2)}) %collective-permute-start.3) | collective-permute-done | bytes 32800 | tf_op jit(solution)/shard_map/ppermute | solution.py:35
  58.9 0.8 collective-permute-start.6
  59.8 5.8 %spectra.2 = (s16[1024,128]{1,0:T(8,128)(2,1)}, s16[1024,128]{1,0:T(8,128)(2,1)}, s16[1024,128]{1,0:T(8,128)(2,1)}, s16[1024,128]{1,0:T(8,128)(2,1)}) custom-call(s32[1]{0:T(128)} %bitcast.9.y_ref, bf16[8192,256]{1,0:T(8,128)(2,1)} %b0.3, bf16[1024,256]{1,0:T(8,128)(2,1)} %copy-done.2, bf16[1024,256]{1,0:T(8,128)(2,1)} %copy-done.11, ...), custom_call_target="tpu_custom_call" | custom-call | flops 1000 | bytes 1000 | tf_op jit(solution)/shard_map/spectra/pallas_call | solution.py:168
  66.2 1.3 collective-permute-start.13
  67.6 1.1 copy-done.5
  68.7 2.8 %collective-permute-start.9 = (s16[1024,128]{1,0:T(8,128)(2,1)S(1)}, s16[1024,128]{1,0:T(8,128)(2,1)S(1)}, u32[]{:S(2)}, u32[]{:S(2)}) collective-permute-start(s16[1024,128]{1,0:T(8,128)(2,1)S(1)} %join.4.refs_0_), channel_id=1, source_target_pairs={{0,24},{4,28},{8,0},{12,4},{16,8},{20,12},{24,16},{28,20},{32,56},... | collective-permute-start | bytes 786440 | tf_op jit(solution)/shard_map/ppermute | solution.py:31
  71.6 0.8 collective-permute-start.10
  72.4 0.8 copy-done.22
  73.2 0.9 collective-permute-start.11
  74.1 5.8 %spectra.3 = (s16[1024,128]{1,0:T(8,128)(2,1)}, s16[1024,128]{1,0:T(8,128)(2,1)}, s16[1024,128]{1,0:T(8,128)(2,1)}, s16[1024,128]{1,0:T(8,128)(2,1)}) custom-call(s32[1]{0:T(128)} %bitcast.9.y_ref, bf16[8192,256]{1,0:T(8,128)(2,1)} %b0.3, bf16[1024,256]{1,0:T(8,128)(2,1)} %copy-done.9, bf16[1024,256]{1,0:T(8,128)(2,1)} %copy-done.22, ...), custom_call_target="tpu_custom_call" | custom-call | flops 1000 | bytes 1000 | tf_op jit(solution)/shard_map/spectra/pallas_call | solution.py:168
  79.9 1.3 collective-permute-start.17
  81.2 3.7 %collective-permute-start.16 = (f32[128,128]{1,0:T(8,128)S(1)}, f32[128,128]{1,0:T(8,128)}, u32[]{:S(2)}, u32[]{:S(2)}) collective-permute-start(f32[128,128]{1,0:T(8,128)S(1)} %copy-done.23), channel_id=1, source_target_pairs={{0,4},{4,8},{8,12},{12,16},{16,20},{20,24},{24,28},{28,32},{32,36}... | collective-permute-start | bytes 196616 | tf_op jit(solution)/shard_map/ppermute | solution.py:295
  85.6 0.9 copy-done.8
  86.6 0.9 copy-done.13
  87.6 0.9 collective-permute-start.15
  91.7 2.6 %collective-permute-start.19 = (s16[1024,128]{1,0:T(8,128)(2,1)}, s16[1024,128]{1,0:T(8,128)(2,1)S(1)}, u32[]{:S(2)}, u32[]{:S(2)}) collective-permute-start(s16[1024,128]{1,0:T(8,128)(2,1)} %get-tuple-element.27), channel_id=1, source_target_pairs={{0,1},{1,2},{2,3},{3,0},{4,5},{5,6},{6,7},{7,4},{8,9},{9,10},{10,1... | collective-permute-start | bytes 786440 | tf_op jit(solution)/shard_map/ppermute | solution.py:47
  94.3 1.5 collective-permute-start.20
  95.8 1.3 collective-permute-start.21
  97.7 1.6 pad_maximum_fusion.shot
  99.3 1.0 copy-done.16
  100.2 16.5 %gather_terms.1.refs_2_ = f32[8192,128]{1,0:T(8,128)} custom-call(s32[8192]{0:T(1024)} %bitcast.17, s32[8192]{0:T(1024)} %bitcast.19, s16[4096,128]{1,0:T(8,128)(2,1)} %copy-done.4, s16[4096,128]{1,0:T(8,128)(2,1)} %copy-done.16, f32[384,128]{1,0:T(8,128)} %pad_maximum_fusion.shot), custom_call_target="tpu_custom_call" | custom-call | flops 1000 | bytes 1000 | tf_op jit(solution)/shard_map/gather_terms/pallas_call | solution.py:203
  118.4 17.2 %sum_receivers.1 = f32[8192,128]{1,0:T(8,128)} custom-call(s32[8192]{0:T(1024)} %bitcast.18, s32[8]{0:T(128)} %broadcast_subtract_fusion.1.refs_1_, f32[8192,128]{1,0:T(8,128)} %gather_terms.1.refs_2_, s16[1024,128]{1,0:T(8,128)(2,1)} %get-tuple-element.21.refs_4_.refs_3_, s16[1024,128]{1,0:T(8,128)(2,1)} %copy-done.6, s16[1024,128]{1,0:T(8,128)(2,1)} %copy-done.17, ...), custom_call_target="tpu_custom_call" | custom-call | flops 1000 | bytes 1000 | tf_op jit(solution)/shard_map/sum_receivers/pallas_call | solution.py:250
  135.6 1.9 %slice.72 = f32[4096,128]{1,0:T(8,128)S(1)} slice(f32[8192,128]{1,0:T(8,128)} %sum_receivers.1), slice={[4096:8192], [0:128]} | slice | bytes 4194304 | tf_op jit(solution)/shard_map/slice | solution.py:340
  137.6 4.1 %collective-permute-done.24 = f32[4096,128]{1,0:T(8,128)S(1)} collective-permute-done((f32[4096,128]{1,0:T(8,128)S(1)}, f32[4096,128]{1,0:T(8,128)S(1)}, u32[]{:S(2)}, u32[]{:S(2)}) %collective-permute-start.24) | collective-permute-done | bytes 2097184 | tf_op jit(solution)/shard_map/ppermute | solution.py:43
  142.0 0.8 fusion.22
  142.8 2.0 %collective-permute-start.27 = (f16[1024,128]{1,0:T(8,128)(2,1)}, f16[1024,128]{1,0:T(8,128)(2,1)S(1)}, u32[]{:S(2)}, u32[]{:S(2)}) collective-permute-start(f16[1024,128]{1,0:T(8,128)(2,1)} %get-tuple-element.35), channel_id=1, source_target_pairs={{0,16},{4,20},{8,24},{12,28},{16,0},{20,4},{24,8},{28,12},{32,48},... | collective-permute-start | bytes 786440 | tf_op jit(solution)/shard_map/ppermute | solution.py:31
  144.9 1.1 collective-permute-start.26
  145.9 1.0 collective-permute-start.25
  147.6 5.8 %sum_shots.1 = f32[384,128]{1,0:T(8,128)} custom-call(s32[1,8192]{1,0:T(1,128)} %broadcast_in_dim_reshape.3.refs_0_, s32[8]{0:T(128)} %broadcast_subtract_fusion.1.refs_1_, f32[8192,128]{1,0:T(8,128)} %gather_terms.1.refs_2_, s16[1024,128]{1,0:T(8,128)(2,1)} %get-tuple-element.21.refs_4_.refs_3_, s16[1024,128]{1,0:T(8,128)(2,1)} %copy-done.6, ...), custom_call_target="tpu_custom_call" | custom-call | flops 1000 | bytes 1000 | tf_op jit(solution)/shard_map/sum_shots/pallas_call | solution.py:282
  153.8 4.3 %collective-permute-done.26 = f16[1024,128]{1,0:T(8,128)(2,1)S(1)} collective-permute-done((f16[1024,128]{1,0:T(8,128)(2,1)S(1)}, f16[1024,128]{1,0:T(8,128)(2,1)S(1)}, u32[]{:S(2)}, u32[]{:S(2)}) %collective-permute-start.26) | collective-permute-done | bytes 262176 | tf_op jit(solution)/shard_map/ppermute | solution.py:31
  158.7 1.6 collective-permute-start.28
  160.3 1.3 collective-permute-start.23
  161.6 3.0 %collective-permute-start.22 = (f32[128,128]{1,0:T(8,128)S(1)}, f32[128,128]{1,0:T(8,128)S(1)}, u32[]{:S(2)}, u32[]{:S(2)}) collective-permute-start(f32[128,128]{1,0:T(8,128)S(1)} %get-tuple-element.37), channel_id=1, source_target_pairs={{0,4},{4,8},{8,12},{12,16},{16,20},{20,24},{24,28},{28,32},{32,36}... | collective-permute-start | bytes 196616 | tf_op jit(solution)/shard_map/ppermute | solution.py:295
  164.8 4.6 %collective-permute-start.31 = (f16[128,128]{1,0:T(8,128)(2,1)S(1)}, f16[128,128]{1,0:T(8,128)(2,1)S(1)}, u32[]{:S(2)}, u32[]{:S(2)}) collective-permute-start(f16[128,128]{1,0:T(8,128)(2,1)S(1)} %get-tuple-element.40), channel_id=1, source_target_pairs={{0,128},{4,132},{8,136},{12,140},{16,144},{20,148},{24,152},{28,15... | collective-permute-start | bytes 98312 | tf_op jit(solution)/shard_map/ppermute | solution.py:35
  169.4 1.7 collective-permute-start.30
  171.1 1.2 collective-permute-start.29
  173.1 1.8 %collective-permute-done.30 = f16[128,128]{1,0:T(8,128)(2,1)S(1)} collective-permute-done((f16[128,128]{1,0:T(8,128)(2,1)S(1)}, f16[128,128]{1,0:T(8,128)(2,1)S(1)}, u32[]{:S(2)}, u32[]{:S(2)}) %collective-permute-start.30) | collective-permute-done | bytes 32800 | tf_op jit(solution)/shard_map/ppermute | solution.py:35
  174.9 2.2 %collective-permute-done.29 = f16[128,128]{1,0:T(8,128)(2,1)S(1)} collective-permute-done((f16[128,128]{1,0:T(8,128)(2,1)S(1)}, f16[128,128]{1,0:T(8,128)(2,1)S(1)}, u32[]{:S(2)}, u32[]{:S(2)}) %collective-permute-start.29) | collective-permute-done | bytes 32800 | tf_op jit(solution)/shard_map/ppermute | solution.py:35
  (111 shorter events, 12.3 us)
Async XLA Ops:
  0.6 2.2 %copy-start = (bf16[8192,256]{1,0:T(8,128)(2,1)S(1)}, bf16[8192,256]{1,0:T(8,128)(2,1)}, u32[]{:S(2)}) copy-start(bf16[8192,256]{1,0:T(8,128)(2,1)} %b0.3) | copy-start | bytes 12582916
  3.0 15.1 %collective-permute-start = (bf16[1024,256]{1,0:T(8,128)(2,1)S(1)}, bf16[1024,256]{1,0:T(8,128)(2,1)S(1)}, u32[]{:S(2)}, u32[]{:S(2)}) collective-permute-start(bf16[1024,256]{1,0:T(8,128)(2,1)S(1)} %get-tuple-element.16), channel_id=1, source_target_pairs={{0,1},{1,2},{2,3},{3,0},{4,5},{5,6},{6,7},{7,4},{8,9},{9,10},{10,1... | collective-permute-start | bytes 1572872 | tf_op jit(solution)/shard_map/ppermute | solution.py:47
  4.7 14.1 %collective-permute-start.1 = (bf16[1024,256]{1,0:T(8,128)(2,1)S(1)}, bf16[1024,256]{1,0:T(8,128)(2,1)S(1)}, u32[]{:S(2)}, u32[]{:S(2)}) collective-permute-start(bf16[1024,256]{1,0:T(8,128)(2,1)S(1)} %get-tuple-element.17), channel_id=1, source_target_pairs={{0,3},{1,0},{2,1},{3,2},{4,7},{5,4},{6,5},{7,6},{8,11},{9,8},{10,9... | collective-permute-start | bytes 1572872 | tf_op jit(solution)/shard_map/ppermute | solution.py:47
  5.4 45.4 %collective-permute-start.5 = (bf16[1024,256]{1,0:T(8,128)(2,1)S(1)}, bf16[1024,256]{1,0:T(8,128)(2,1)S(1)}, u32[]{:S(2)}, u32[]{:S(2)}) collective-permute-start(bf16[1024,256]{1,0:T(8,128)(2,1)S(1)} %get-tuple-element.18), channel_id=1, source_target_pairs={{0,2},{1,3},{2,0},{3,1},{4,6},{5,7},{6,4},{7,5},{8,10},{9,11},{10,... | collective-permute-start | bytes 1572872 | tf_op jit(solution)/shard_map/ppermute | solution.py:47
  18.1 25.9 %copy-start.2 = (bf16[1024,256]{1,0:T(8,128)(2,1)}, bf16[1024,256]{1,0:T(8,128)(2,1)S(1)}, u32[]{:S(2)}) copy-start(bf16[1024,256]{1,0:T(8,128)(2,1)S(1)} %collective-permute-done.refs_0_.refs_3_.b1) | copy-start | bytes 1572868
  18.8 25.3 %copy-start.3 = (bf16[1024,256]{1,0:T(8,128)(2,1)}, bf16[1024,256]{1,0:T(8,128)(2,1)S(1)}, u32[]{:S(2)}) copy-start(bf16[1024,256]{1,0:T(8,128)(2,1)S(1)} %collective-permute-done.1.refs_1_.refs_4_.b3) | copy-start | bytes 1572868
  19.0 25.1 %copy-start.14 = (f32[128,128]{1,0:T(8,128)S(1)}, f32[128,128]{1,0:T(8,128)}, u32[]{:S(2)}) copy-start(f32[128,128]{1,0:T(8,128)} %a.1) | copy-start | bytes 196612
  19.0 48.6 %collective-permute-start.7 = (bf16[1024,256]{1,0:T(8,128)(2,1)S(1)}, bf16[1024,256]{1,0:T(8,128)(2,1)S(1)}, u32[]{:S(2)}, u32[]{:S(2)}) collective-permute-start(bf16[1024,256]{1,0:T(8,128)(2,1)S(1)} %get-tuple-element.19), channel_id=1, source_target_pairs={{0,1},{1,2},{2,3},{3,0},{4,5},{5,6},{6,7},{7,4},{8,9},{9,10},{10,1... | collective-permute-start | bytes 1572872 | tf_op jit(solution)/shard_map/ppermute | solution.py:47
  28.6 39.0 %collective-permute-start.8 = (bf16[1024,256]{1,0:T(8,128)(2,1)S(1)}, bf16[1024,256]{1,0:T(8,128)(2,1)S(1)}, u32[]{:S(2)}, u32[]{:S(2)}) collective-permute-start(bf16[1024,256]{1,0:T(8,128)(2,1)S(1)} %get-tuple-element.20), channel_id=1, source_target_pairs={{0,3},{1,0},{2,1},{3,2},{4,7},{5,4},{6,5},{7,6},{8,11},{9,8},{10,9... | collective-permute-start | bytes 1572872 | tf_op jit(solution)/shard_map/ppermute | solution.py:47
  28.6 43.8 %collective-permute-start.14 = (bf16[1024,256]{1,0:T(8,128)(2,1)S(1)}, bf16[1024,256]{1,0:T(8,128)(2,1)S(1)}, u32[]{:S(2)}, u32[]{:S(2)}) collective-permute-start(bf16[1024,256]{1,0:T(8,128)(2,1)S(1)} %get-tuple-element.24), channel_id=1, source_target_pairs={{0,2},{1,3},{2,0},{3,1},{4,6},{5,7},{6,4},{7,5},{8,10},{9,11},{10,... | collective-permute-start | bytes 1572872 | tf_op jit(solution)/shard_map/ppermute | solution.py:47
  44.1 15.7 %copy-start.1 = (bf16[1024,1024]{1,0:T(8,128)(2,1)}, bf16[1024,1024]{1,0:T(8,128)(2,1)S(1)}, u32[]{:S(2)}) copy-start(bf16[1024,1024]{1,0:T(8,128)(2,1)S(1)} %make_table.1.refs_2_.t) | copy-start | bytes 6291460
  44.1 8.2 %collective-permute-start.2 = (s16[128,128]{1,0:T(8,128)(2,1)S(1)}, s16[128,128]{1,0:T(8,128)(2,1)S(1)}, u32[]{:S(2)}, u32[]{:S(2)}) collective-permute-start(s16[128,128]{1,0:T(8,128)(2,1)S(1)} %encode_terms.1.refs_0_), channel_id=1, source_target_pairs={{0,192},{4,196},{8,200},{12,204},{16,208},{20,212},{24,216},{28,22... | collective-permute-start | bytes 98312 | tf_op jit(solution)/shard_map/ppermute | solution.py:35
  50.7 9.0 %copy-start.11 = (bf16[1024,256]{1,0:T(8,128)(2,1)}, bf16[1024,256]{1,0:T(8,128)(2,1)S(1)}, u32[]{:S(2)}) copy-start(bf16[1024,256]{1,0:T(8,128)(2,1)S(1)} %collective-permute-done.5.refs_4_.b2) | copy-start | bytes 1572868
  50.7 7.8 %collective-permute-start.3 = (s16[128,128]{1,0:T(8,128)(2,1)S(1)}, s16[128,128]{1,0:T(8,128)(2,1)S(1)}, u32[]{:S(2)}, u32[]{:S(2)}) collective-permute-start(s16[128,128]{1,0:T(8,128)(2,1)S(1)} %encode_terms.1.refs_0_), channel_id=1, source_target_pairs={{0,128},{4,132},{8,136},{12,140},{16,144},{20,148},{24,152},{28,15... | collective-permute-start | bytes 98312 | tf_op jit(solution)/shard_map/ppermute | solution.py:35
  52.3 6.6 %collective-permute-start.4 = (s16[128,128]{1,0:T(8,128)(2,1)S(1)}, s16[128,128]{1,0:T(8,128)(2,1)S(1)}, u32[]{:S(2)}, u32[]{:S(2)}) collective-permute-start(s16[128,128]{1,0:T(8,128)(2,1)S(1)} %encode_terms.1.refs_0_), channel_id=1, source_target_pairs={{0,64},{4,68},{8,72},{12,76},{16,80},{20,84},{24,88},{28,92},{32,9... | collective-permute-start | bytes 98312 | tf_op jit(solution)/shard_map/ppermute | solution.py:35
  58.9 7.3 %collective-permute-start.6 = (s16[512,128]{1,0:T(8,128)(2,1)S(1)}, s16[512,128]{1,0:T(8,128)(2,1)S(1)}, u32[]{:S(2)}, u32[]{:S(2)}) collective-permute-start(s16[512,128]{1,0:T(8,128)(2,1)S(1)} %join.3.refs_0_), channel_id=1, source_target_pairs={{0,32},{4,36},{8,40},{12,44},{16,48},{20,52},{24,56},{28,60},{32,0... | collective-permute-start | bytes 393224 | tf_op jit(solution)/shard_map/ppermute | solution.py:39
  65.5 14.4 %collective-permute-start.12 = (s16[1024,128]{1,0:T(8,128)(2,1)}, s16[1024,128]{1,0:T(8,128)(2,1)S(1)}, u32[]{:S(2)}, u32[]{:S(2)}) collective-permute-start(s16[1024,128]{1,0:T(8,128)(2,1)} %get-tuple-element.22), channel_id=1, source_target_pairs={{0,1},{1,2},{2,3},{3,0},{4,5},{5,6},{6,7},{7,4},{8,9},{9,10},{10,1... | collective-permute-start | bytes 786440 | tf_op jit(solution)/shard_map/ppermute | solution.py:47
  66.2 15.0 %collective-permute-start.13 = (s16[1024,128]{1,0:T(8,128)(2,1)}, s16[1024,128]{1,0:T(8,128)(2,1)S(1)}, u32[]{:S(2)}, u32[]{:S(2)}) collective-permute-start(s16[1024,128]{1,0:T(8,128)(2,1)} %get-tuple-element.23), channel_id=1, source_target_pairs={{0,3},{1,0},{2,1},{3,2},{4,7},{5,4},{6,5},{7,6},{8,11},{9,8},{10,9... | collective-permute-start | bytes 786440 | tf_op jit(solution)/shard_map/ppermute | solution.py:47
  67.6 6.5 %copy-start.9 = (bf16[1024,256]{1,0:T(8,128)(2,1)}, bf16[1024,256]{1,0:T(8,128)(2,1)S(1)}, u32[]{:S(2)}) copy-start(bf16[1024,256]{1,0:T(8,128)(2,1)S(1)} %collective-permute-done.7.refs_2_.b1) | copy-start | bytes 1572868
  67.6 6.5 %copy-start.10 = (bf16[1024,256]{1,0:T(8,128)(2,1)}, bf16[1024,256]{1,0:T(8,128)(2,1)S(1)}, u32[]{:S(2)}) copy-start(bf16[1024,256]{1,0:T(8,128)(2,1)S(1)} %collective-permute-done.8.refs_3_.b3) | copy-start | bytes 1572868
  68.7 16.2 %collective-permute-start.9 = (s16[1024,128]{1,0:T(8,128)(2,1)S(1)}, s16[1024,128]{1,0:T(8,128)(2,1)S(1)}, u32[]{:S(2)}, u32[]{:S(2)}) collective-permute-start(s16[1024,128]{1,0:T(8,128)(2,1)S(1)} %join.4.refs_0_), channel_id=1, source_target_pairs={{0,24},{4,28},{8,0},{12,4},{16,8},{20,12},{24,16},{28,20},{32,56},... | collective-permute-start | bytes 786440 | tf_op jit(solution)/shard_map/ppermute | solution.py:31
  71.6 13.3 %collective-permute-start.10 = (s16[1024,128]{1,0:T(8,128)(2,1)S(1)}, s16[1024,128]{1,0:T(8,128)(2,1)S(1)}, u32[]{:S(2)}, u32[]{:S(2)}) collective-permute-start(s16[1024,128]{1,0:T(8,128)(2,1)S(1)} %join.4.refs_0_), channel_id=1, source_target_pairs={{0,16},{4,20},{8,24},{12,28},{16,0},{20,4},{24,8},{28,12},{32,48},... | collective-permute-start | bytes 786440 | tf_op jit(solution)/shard_map/ppermute | solution.py:31
  73.2 11.7 %collective-permute-start.11 = (s16[1024,128]{1,0:T(8,128)(2,1)S(1)}, s16[1024,128]{1,0:T(8,128)(2,1)S(1)}, u32[]{:S(2)}, u32[]{:S(2)}) collective-permute-start(s16[1024,128]{1,0:T(8,128)(2,1)S(1)} %join.4.refs_0_), channel_id=1, source_target_pairs={{0,8},{4,12},{8,16},{12,20},{16,24},{20,28},{24,0},{28,4},{32,40},... | collective-permute-start | bytes 786440 | tf_op jit(solution)/shard_map/ppermute | solution.py:31
  74.1 5.8 %copy-start.23 = (f32[128,128]{1,0:T(8,128)S(1)}, f32[128,128]{1,0:T(8,128)}, u32[]{:S(2)}) copy-start(f32[128,128]{1,0:T(8,128)} %param.10) | copy-start | bytes 196612
  74.1 14.4 %copy-start.24 = (s32[8192]{0:T(1024)S(1)}, s32[8192]{0:T(1024)}, u32[]{:S(2)}) copy-start(s32[8192]{0:T(1024)} %param.8) | copy-start | bytes 98308
  74.1 14.6 %copy-start.25 = (s32[8192]{0:T(1024)S(1)}, s32[8192]{0:T(1024)}, u32[]{:S(2)}) copy-start(s32[8192]{0:T(1024)} %param.7) | copy-start | bytes 98308
  79.9 36.9 %copy-start.6 = (s16[1024,128]{1,0:T(8,128)(2,1)}, s16[1024,128]{1,0:T(8,128)(2,1)S(1)}, u32[]{:S(2)}) copy-start(s16[1024,128]{1,0:T(8,128)(2,1)S(1)} %collective-permute-done.12.refs_4_) | copy-start | bytes 786436
  79.9 14.4 %collective-permute-start.17 = (f32[128,128]{1,0:T(8,128)S(1)}, f32[128,128]{1,0:T(8,128)}, u32[]{:S(2)}, u32[]{:S(2)}) collective-permute-start(f32[128,128]{1,0:T(8,128)S(1)} %copy-done.23), channel_id=1, source_target_pairs={{4,0},{8,4},{12,8},{16,12},{20,16},{24,20},{28,24},{32,28},{36,32}... | collective-permute-start | bytes 196616 | tf_op jit(solution)/shard_map/ppermute | solution.py:295
  81.2 35.6 %copy-start.7 = (s16[1024,128]{1,0:T(8,128)(2,1)}, s16[1024,128]{1,0:T(8,128)(2,1)S(1)}, u32[]{:S(2)}) copy-start(s16[1024,128]{1,0:T(8,128)(2,1)S(1)} %collective-permute-done.13.refs_5_.refs_6_) | copy-start | bytes 786436
  81.2 14.6 %collective-permute-start.16 = (f32[128,128]{1,0:T(8,128)S(1)}, f32[128,128]{1,0:T(8,128)}, u32[]{:S(2)}, u32[]{:S(2)}) collective-permute-start(f32[128,128]{1,0:T(8,128)S(1)} %copy-done.23), channel_id=1, source_target_pairs={{0,4},{4,8},{8,12},{12,16},{16,20},{20,24},{24,28},{28,32},{32,36}... | collective-permute-start | bytes 196616 | tf_op jit(solution)/shard_map/ppermute | solution.py:295
  87.6 11.7 %copy-start.4 = (s16[4096,128]{1,0:T(8,128)(2,1)}, s16[4096,128]{1,0:T(8,128)(2,1)S(1)}, u32[]{:S(2)}) copy-start(s16[4096,128]{1,0:T(8,128)(2,1)S(1)} %join.5.own) | copy-start | bytes 3145732
  87.6 11.6 %collective-permute-start.15 = (s16[4096,128]{1,0:T(8,128)(2,1)S(1)}, s16[4096,128]{1,0:T(8,128)(2,1)S(1)}, u32[]{:S(2)}, u32[]{:S(2)}) collective-permute-start(s16[4096,128]{1,0:T(8,128)(2,1)S(1)} %join.5.own), channel_id=1, source_target_pairs={{0,4},{4,0},{8,12},{12,8},{16,20},{20,16},{24,28},{28,24},{32,36},... | collective-permute-start | bytes 3145736 | tf_op jit(solution)/shard_map/ppermute | solution.py:43
  91.0 25.8 %collective-permute-start.18 = (s16[1024,128]{1,0:T(8,128)(2,1)}, s16[1024,128]{1,0:T(8,128)(2,1)S(1)}, u32[]{:S(2)}, u32[]{:S(2)}) collective-permute-start(s16[1024,128]{1,0:T(8,128)(2,1)} %get-tuple-element.26), channel_id=1, source_target_pairs={{0,2},{1,3},{2,0},{3,1},{4,6},{5,7},{6,4},{7,5},{8,10},{9,11},{10,... | collective-permute-start | bytes 786440 | tf_op jit(solution)/shard_map/ppermute | solution.py:47
  91.7 25.1 %collective-permute-start.19 = (s16[1024,128]{1,0:T(8,128)(2,1)}, s16[1024,128]{1,0:T(8,128)(2,1)S(1)}, u32[]{:S(2)}, u32[]{:S(2)}) collective-permute-start(s16[1024,128]{1,0:T(8,128)(2,1)} %get-tuple-element.27), channel_id=1, source_target_pairs={{0,1},{1,2},{2,3},{3,0},{4,5},{5,6},{6,7},{7,4},{8,9},{9,10},{10,1... | collective-permute-start | bytes 786440 | tf_op jit(solution)/shard_map/ppermute | solution.py:47
  94.3 22.5 %collective-permute-start.20 = (s16[1024,128]{1,0:T(8,128)(2,1)}, s16[1024,128]{1,0:T(8,128)(2,1)S(1)}, u32[]{:S(2)}, u32[]{:S(2)}) collective-permute-start(s16[1024,128]{1,0:T(8,128)(2,1)} %get-tuple-element.28), channel_id=1, source_target_pairs={{0,2},{1,3},{2,0},{3,1},{4,6},{5,7},{6,4},{7,5},{8,10},{9,11},{10,... | collective-permute-start | bytes 786440 | tf_op jit(solution)/shard_map/ppermute | solution.py:47
  95.8 21.0 %collective-permute-start.21 = (s16[1024,128]{1,0:T(8,128)(2,1)}, s16[1024,128]{1,0:T(8,128)(2,1)S(1)}, u32[]{:S(2)}, u32[]{:S(2)}) collective-permute-start(s16[1024,128]{1,0:T(8,128)(2,1)} %get-tuple-element.29), channel_id=1, source_target_pairs={{0,3},{1,0},{2,1},{3,2},{4,7},{5,4},{6,5},{7,6},{8,11},{9,8},{10,9... | collective-permute-start | bytes 786440 | tf_op jit(solution)/shard_map/ppermute | solution.py:47
  135.6 6.1 %copy-start.15 = (f32[8192,128]{1,0:T(8,128)S(1)}, f32[8192,128]{1,0:T(8,128)}, u32[]{:S(2)}) copy-start(f32[8192,128]{1,0:T(8,128)} %sum_receivers.1) | copy-start | bytes 12582916
  137.5 4.2 %collective-permute-start.24 = (f32[4096,128]{1,0:T(8,128)S(1)}, f32[4096,128]{1,0:T(8,128)S(1)}, u32[]{:S(2)}, u32[]{:S(2)}) collective-permute-start(f32[4096,128]{1,0:T(8,128)S(1)} %slice.72), channel_id=1, source_target_pairs={{0,4},{4,0},{8,12},{12,8},{16,20},{20,16},{24,28},{28,24},{32,36},... | collective-permute-start | bytes 6291464 | tf_op jit(solution)/shard_map/ppermute | solution.py:43
  142.8 10.9 %collective-permute-start.27 = (f16[1024,128]{1,0:T(8,128)(2,1)}, f16[1024,128]{1,0:T(8,128)(2,1)S(1)}, u32[]{:S(2)}, u32[]{:S(2)}) collective-permute-start(f16[1024,128]{1,0:T(8,128)(2,1)} %get-tuple-element.35), channel_id=1, source_target_pairs={{0,16},{4,20},{8,24},{12,28},{16,0},{20,4},{24,8},{28,12},{32,48},... | collective-permute-start | bytes 786440 | tf_op jit(solution)/shard_map/ppermute | solution.py:31
  144.9 13.2 %collective-permute-start.26 = (f16[1024,128]{1,0:T(8,128)(2,1)S(1)}, f16[1024,128]{1,0:T(8,128)(2,1)S(1)}, u32[]{:S(2)}, u32[]{:S(2)}) collective-permute-start(f16[1024,128]{1,0:T(8,128)(2,1)S(1)} %get-tuple-element.36), channel_id=1, source_target_pairs={{0,24},{4,28},{8,0},{12,4},{16,8},{20,12},{24,16},{28,20},{32,56},... | collective-permute-start | bytes 786440 | tf_op jit(solution)/shard_map/ppermute | solution.py:31
  145.9 12.6 %collective-permute-start.25 = (f16[1024,128]{1,0:T(8,128)(2,1)S(1)}, f16[1024,128]{1,0:T(8,128)(2,1)S(1)}, u32[]{:S(2)}, u32[]{:S(2)}) collective-permute-start(f16[1024,128]{1,0:T(8,128)(2,1)S(1)} %get-tuple-element.34), channel_id=1, source_target_pairs={{0,8},{4,12},{8,16},{12,20},{16,24},{20,28},{24,0},{28,4},{32,40},... | collective-permute-start | bytes 786440 | tf_op jit(solution)/shard_map/ppermute | solution.py:31
  153.4 7.0 %copy-start.21 = (f32[384,128]{1,0:T(8,128)S(1)}, f32[384,128]{1,0:T(8,128)}, u32[]{:S(2)}) copy-start(f32[384,128]{1,0:T(8,128)} %sum_shots.1) | copy-start | bytes 589828
  158.7 6.0 %collective-permute-start.28 = (f16[512,128]{1,0:T(8,128)(2,1)S(1)}, f16[512,128]{1,0:T(8,128)(2,1)S(1)}, u32[]{:S(2)}, u32[]{:S(2)}) collective-permute-start(f16[512,128]{1,0:T(8,128)(2,1)S(1)} %fusion), channel_id=1, source_target_pairs={{0,32},{4,36},{8,40},{12,44},{16,48},{20,52},{24,56},{28,60},{32,0... | collective-permute-start | bytes 393224 | tf_op jit(solution)/shard_map/ppermute | solution.py:39
  160.3 12.0 %collective-permute-start.23 = (f32[128,128]{1,0:T(8,128)S(1)}, f32[128,128]{1,0:T(8,128)S(1)}, u32[]{:S(2)}, u32[]{:S(2)}) collective-permute-start(f32[128,128]{1,0:T(8,128)S(1)} %get-tuple-element.38), channel_id=1, source_target_pairs={{4,0},{8,4},{12,8},{16,12},{20,16},{24,20},{28,24},{32,28},{36,32}... | collective-permute-start | bytes 196616 | tf_op jit(solution)/shard_map/ppermute | solution.py:295
  161.6 10.7 %collective-permute-start.22 = (f32[128,128]{1,0:T(8,128)S(1)}, f32[128,128]{1,0:T(8,128)S(1)}, u32[]{:S(2)}, u32[]{:S(2)}) collective-permute-start(f32[128,128]{1,0:T(8,128)S(1)} %get-tuple-element.37), channel_id=1, source_target_pairs={{0,4},{4,8},{8,12},{12,16},{16,20},{20,24},{24,28},{28,32},{32,36}... | collective-permute-start | bytes 196616 | tf_op jit(solution)/shard_map/ppermute | solution.py:295
  164.8 8.3 %collective-permute-start.31 = (f16[128,128]{1,0:T(8,128)(2,1)S(1)}, f16[128,128]{1,0:T(8,128)(2,1)S(1)}, u32[]{:S(2)}, u32[]{:S(2)}) collective-permute-start(f16[128,128]{1,0:T(8,128)(2,1)S(1)} %get-tuple-element.40), channel_id=1, source_target_pairs={{0,128},{4,132},{8,136},{12,140},{16,144},{20,148},{24,152},{28,15... | collective-permute-start | bytes 98312 | tf_op jit(solution)/shard_map/ppermute | solution.py:35
  169.4 5.6 %collective-permute-start.30 = (f16[128,128]{1,0:T(8,128)(2,1)S(1)}, f16[128,128]{1,0:T(8,128)(2,1)S(1)}, u32[]{:S(2)}, u32[]{:S(2)}) collective-permute-start(f16[128,128]{1,0:T(8,128)(2,1)S(1)} %get-tuple-element.41), channel_id=1, source_target_pairs={{0,192},{4,196},{8,200},{12,204},{16,208},{20,212},{24,216},{28,22... | collective-permute-start | bytes 98312 | tf_op jit(solution)/shard_map/ppermute | solution.py:35
  171.1 6.1 %collective-permute-start.29 = (f16[128,128]{1,0:T(8,128)(2,1)S(1)}, f16[128,128]{1,0:T(8,128)(2,1)S(1)}, u32[]{:S(2)}, u32[]{:S(2)}) collective-permute-start(f16[128,128]{1,0:T(8,128)(2,1)S(1)} %get-tuple-element.39), channel_id=1, source_target_pairs={{0,64},{4,68},{8,72},{12,76},{16,80},{20,84},{24,88},{28,92},{32,9... | collective-permute-start | bytes 98312 | tf_op jit(solution)/shard_map/ppermute | solution.py:35
  (10 other events, 8.6 us)

commit v3 on v2

--- a/solution.py
+++ b/solution.py
@@ -13,7 +13,8 @@
 REC_LOW, REC_HIGH = 1.0, 2.2
 REC_SCALE = 65535.0 / (REC_HIGH - REC_LOW)
 SUM_SCALE = 1.0 / 32.0
-CHUNKS = 2
+SENT = (1024, 1024)
+BACK = ((0, 0, 1024), (1, 0, 1024))
 SMALL = pltpu.CompilerParams(vmem_limit_bytes=12 * 2**20)
 COST = pl.CostEstimate(flops=1000, bytes_accessed=1000, transcendentals=0)
 VMEM = pltpu.CompilerParams(vmem_limit_bytes=56 * 2**20)
@@ -27,20 +28,8 @@
     return [(z, x, c) for z in range(NZ) for x in range(NX) for c in range(NC)]
 
 
-def send_x(value, k):
-    return lax.ppermute(value, "tr", [(tr_of(z, x, c), tr_of(z, (x + k) % NX, c)) for z, x, c in sites()])
-
-
-def send_z(value, k):
-    return lax.ppermute(value, "tr", [(tr_of(z, x, c), tr_of((z + k) % NZ, x, c)) for z, x, c in sites()])
-
-
-def swap_z(value):
-    return lax.ppermute(value, "tr", [(tr_of(z, x, c), tr_of(z ^ 1, x, c)) for z, x, c in sites()])
-
-
-def swap_core(value):
-    return lax.ppermute(value, "tr", [(tr_of(z, x, c), tr_of(z, x, c ^ 1)) for z, x, c in sites()])
+def swap(value, dz, dx, dc):
+    return lax.ppermute(value, "tr", [(tr_of(z, x, c), tr_of(z ^ dz, x ^ dx, c ^ dc)) for z, x, c in sites()])
 
 
 def send_y(value, k):
@@ -51,6 +40,7 @@
     part, cols = samples // NY, NY * 2 * width
     tile = 128
     quarter = samples // 4
+    shift = quarter.bit_length() - 1
 
     def body(y_ref, out):
         y = y_ref[0]
@@ -60,14 +50,14 @@
             first = (y + k) % NY * width
             for half in range(2):
                 freq = first + lax.broadcasted_iota(jnp.int32, (1, width), 1)
-                phase = (time * freq + half * quarter) % samples
-                turn = (phase + quarter // 2) // quarter
+                phase = (time * freq + half * quarter) & (samples - 1)
+                turn = lax.shift_right_logical(phase + quarter // 2, shift)
                 rest = (phase - turn * quarter).astype(jnp.float32) * (2.0 * math.pi / samples)
                 sq = rest * rest
                 cos = 1.0 + sq * (-0.5 + sq * (1 / 24 + sq * (-1 / 720 + sq * (1 / 40320 - sq * (1 / 3628800)))))
                 sin = rest * (1.0 + sq * (-1 / 6 + sq * (1 / 120 + sq * (-1 / 5040 + sq * (1 / 362880)))))
-                value = jnp.where(turn % 2 == 1, sin, cos)
-                value = jnp.where((turn % 4 == 1) | (turn % 4 == 2), -value, value)
+                value = jnp.where((turn & 1) == 1, sin, cos)
+                value = jnp.where(((turn + 1) & 2) == 2, -value, value)
                 out[:, pl.ds((2 * k + half) * width, width)] = value.astype(jnp.bfloat16)
 
     return pl.pallas_call(
@@ -77,7 +67,7 @@
         out_specs=pl.BlockSpec((tile, cols), lambda i: (i, 0)),
         out_shape=jax.ShapeDtypeStruct((samples, cols), jnp.bfloat16),
         compiler_params=SMALL,
-        cost_estimate=COST,
+        cost_estimate=pl.CostEstimate(flops=2**30, bytes_accessed=2**25, transcendentals=0),
         name="make_table",
     )(y[None])
 
@@ -102,18 +92,17 @@
     )(*parts, *after)
 
 
-def take_rows(traces, y, chunk, after=()):
+def take_rows(traces, y, first, piece, after=()):
     rows, part = traces.shape
-    piece = rows // NY // CHUNKS
-    tile = min(piece, 256)
-    steps = piece // tile
+    tile = 256
+    share, start, steps = rows // NY // tile, first // tile, piece // tile
 
     def body(y_ref, *refs):
         for a, b in zip(refs[:3], refs[3 + len(after) :]):
             b[...] = a[...]
 
     def spot(k):
-        return pl.BlockSpec((tile, part), lambda i, y: (((y[0] + k) % NY * CHUNKS + chunk) * steps + i, 0))
+        return pl.BlockSpec((tile, part), lambda i, y: ((y[0] + k) % NY * share + start + i, 0))
 
     return pl.pallas_call(
         body,
@@ -148,13 +137,12 @@
     )(terms, *after)
 
 
-def spectra(traces, y, chunk, blocks, table, width):
-    rows, part = blocks[0].shape
-    tile = min(rows, 512)
-    steps = rows // tile
-
-    def body(y_ref, b0, b1, b2, b3, t, o0, o1, o2, o3):
-        for k, out in enumerate((o0, o1, o2, o3)):
+def spectra(traces, y, first, inner, rows, blocks, table, width, after=()):
+    part, tile = traces.shape[1], 256
+    share, start, steps = traces.shape[0] // NY // tile, first // tile, rows // tile
+
+    def body(y_ref, b0, b1, b2, b3, t, *refs):
+        for k, out in enumerate(refs[len(after) :]):
             cols = pl.ds(k * 2 * width, 2 * width)
             acc = None
             for j, b in enumerate((b0, b1, b2, b3)):
@@ -170,25 +158,28 @@
         grid_spec=pltpu.PrefetchScalarGridSpec(
             num_scalar_prefetch=1,
             grid=(steps,),
-            in_specs=[pl.BlockSpec((tile, part), lambda i, y: ((y[0] * CHUNKS + chunk) * steps + i, 0))]
-            + [pl.BlockSpec((tile, part), lambda i, y: (i, 0))] * 3
-            + [pl.BlockSpec(table.shape, lambda i, y: (0, 0))],
+            in_specs=[pl.BlockSpec((tile, part), lambda i, y: (y[0] * share + start + i, 0))]
+            + [pl.BlockSpec((tile, part), lambda i, y: (inner // tile + i, 0))] * 3
+            + [pl.BlockSpec(table.shape, lambda i, y: (0, 0))]
+            + [pl.BlockSpec(memory_space=pl.ANY)] * len(after),
             out_specs=[pl.BlockSpec((tile, width), lambda i, y: (i, 0))] * 4,
         ),
         out_shape=[jax.ShapeDtypeStruct((rows, width), jnp.int16)] * 4,
         compiler_params=VMEM,
         cost_estimate=COST,
         name="spectra",
-    )(y[None], traces, *blocks, table)
-
-
-def gather_terms(own, other, shot_near, rec_at, shot_at):
-    rows, width = rec_at.shape[0], own.shape[1]
-    half = own.shape[0]
-
-    def body(rec_at, shot_at, own, other, shot, out, rec):
-        rec[pl.ds(0, half), :] = (own[...].astype(jnp.float32) + 32768.0) * (1.0 / REC_SCALE) + REC_LOW
-        rec[pl.ds(half, half), :] = (other[...].astype(jnp.float32) + 32768.0) * (1.0 / REC_SCALE) + REC_LOW
+    )(y[None], traces, *blocks, table, *after)
+
+
+def gather_terms(coded, shot_near, rec_at, shot_at):
+    rows, width = rec_at.shape[0], shot_near.shape[1]
+    parts = len(coded)
+    spans = spans_of(coded)
+
+    def body(rec_at, shot_at, shot, *refs):
+        out, rec = refs[parts:]
+        for code, at in zip(refs, spans):
+            rec[at, :] = (code[...].astype(jnp.float32) + 32768.0) * (1.0 / REC_SCALE) + REC_LOW
 
         def step(b, _):
             at = [b * 32 + u for u in range(32)]
@@ -202,14 +193,14 @@
     vm, sm = pl.BlockSpec(memory_space=pltpu.VMEM), pl.BlockSpec(memory_space=pltpu.SMEM)
     return pl.pallas_call(
         body,
-        in_specs=[sm, sm, vm, vm, vm],
+        in_specs=[sm, sm, vm] + [vm] * parts,
         out_specs=vm,
         out_shape=jax.ShapeDtypeStruct((rows, width), jnp.float32),
-        scratch_shapes=[pltpu.VMEM((2 * half, width), jnp.float32)],
+        scratch_shapes=[pltpu.VMEM((sum(code.shape[0] for code in coded), width), jnp.float32)],
         compiler_params=VMEM,
         cost_estimate=COST,
         name="gather_terms",
-    )(rec_at, shot_at, own, other, shot_near)
+    )(rec_at, shot_at, shot_near, *coded)
 
 
 def residual(code, model, live):
@@ -218,10 +209,15 @@
     return jnp.where(alive, logamp - model, 0.0)
 
 
+def spans_of(codes):
+    sizes = [code.shape[0] for code in codes]
+    return [pl.ds(sum(sizes[:k]), size) for k, size in enumerate(sizes)]
+
+
 def sum_receivers(codes, model, live, rec_at, count):
     rows, width = model.shape
-    piece = codes[0].shape[0]
     parts = len(codes)
+    spans = spans_of(codes)
     banks, group = 8, 32
 
     def body(*refs):
@@ -231,8 +227,7 @@
         sums = (out,) + refs[5 + parts :]
         for s in sums:
             s[...] = jnp.zeros_like(s)
-        for k, code in enumerate(codes):
-            at = pl.ds(k * piece, piece)
+        for k, (code, at) in enumerate(zip(codes, spans)):
             res[at, :] = residual(code[...], model[at, :], live[k])
 
         def step(b, _):
@@ -261,20 +256,19 @@
 
 def sum_shots(codes, model, live, shot_at, count):
     rows, width = model.shape
-    piece = codes[0].shape[0]
     parts = len(codes)
+    spans = spans_of(codes)
 
     def body(*refs):
         shot_at, live, model = refs[:3]
         codes, out = refs[3 : 3 + parts], refs[3 + parts]
         acc = jnp.zeros((count, 2 * width), jnp.float32)
-        for k, code in enumerate(codes):
-            at = pl.ds(k * piece, piece)
+        for k, (code, at) in enumerate(zip(codes, spans)):
             res = residual(code[...], model[at, :], live[k])
             high = res.astype(jnp.bfloat16)
             low = (res - high.astype(jnp.float32)).astype(jnp.bfloat16)
             both = jnp.concatenate([high, low], axis=1)
-            hot = lax.broadcasted_iota(jnp.int32, (count, piece), 0) == shot_at[:, at]
+            hot = lax.broadcasted_iota(jnp.int32, (count, at.size), 0) == shot_at[:, at]
             acc = acc + jnp.dot(hot.astype(jnp.bfloat16), both, preferred_element_type=jnp.float32)
         out[...] = acc[:, :width] + acc[:, width:]
 
@@ -298,60 +292,68 @@
 def per_device(traces, shot_index, receiver_index, live_counts, shot_terms, receiver_terms):
     rows, part = traces.shape
     block, width = shot_terms.shape
-    share, piece = rows // NY, rows // NY // CHUNKS
+    share = rows // NY
+    starts = [sum(SENT[:t]) for t in range(len(SENT))]
+    first = [starts[t] + inner for t, inner, _ in BACK]
     owner, y = lax.axis_index("tr"), lax.axis_index("fq")
     z, x, c = owner // (NX * NC), owner // NC % NX, owner % NC
 
     got, after = [], ()
-    for h in range(CHUNKS):
-        mine = take_rows(traces, y, h, after)
+    for start, size in zip(starts, SENT):
+        mine = take_rows(traces, y, start, size, after)
         come = {k: send_y(mine[k - 1], k) for k in (1, 3, 2)}
         got.append([come[k] for k in range(1, NY)])
-        after = (come[1], come[3])
+        after = got[-1]
+        if start == 0:
+            mine_first = mine[0]
     table = make_table(part * NY, y, width)
-    coded = [spectra(traces, y, h, got[h], table, width) for h in range(CHUNKS)]
-    codes = [send_y(outs[k], k) if k else outs[k] for outs in coded for k in range(NY)]
-
-    terms = encode_terms(receiver_terms, (got[0][0], got[0][2], table))
-    terms = join([terms] + [send_z(terms, -2 * k) for k in range(1, NZ // 2)], (got[0][1],))
-    terms = join([terms, swap_z(terms)], (got[1][0], got[1][2], coded[0][0]))
-    terms = join([terms] + [send_x(terms, -k) for k in range(1, NX)], (codes[1], codes[3], coded[1][0]))
-    far_terms = swap_core(terms)
+    terms = encode_terms(receiver_terms, (mine_first,))
+    terms = join([terms, swap(terms, 1, 0, 0)])
+    terms = join([terms, swap(terms, 2, 0, 0)])
+    terms = join([terms, swap(terms, 4, 0, 0)], (table,))
+    terms = join([terms, swap(terms, 0, 1, 0)])
+    terms = join([terms, swap(terms, 0, 2, 0)])
+    far_terms = [swap(terms, 0, 0, 1)]
 
     def ordered(v):
-        v = v.reshape(NY, CHUNKS, piece)
-        v = jnp.stack([lax.dynamic_index_in_dim(v, (y - k) % NY, 0, keepdims=False) for k in range(NY)], axis=1)
-        return v.reshape(rows)
+        v = v.reshape(NY, share)
+        v = jnp.stack([lax.dynamic_index_in_dim(v, (y - k) % NY, 0, keepdims=False) for k in range(NY)])
+        return jnp.concatenate([v[:, at : at + size].reshape(NY * size) for at, (_, _, size) in zip(first, BACK)])
 
     near = receiver_index // block
     rz, rx, rc = near // (NX * NC), near // NC % NX, near % NC
-    odd = (rz ^ z) & 1
-    place = (((rc ^ c) * NX + (rx - x) % NX) * 2 + odd) * (NZ // 2) + (rz - (z ^ odd)) % NZ // 2
+    place = ((rc ^ c) * NX + (rx ^ x)) * NZ + (rz ^ z)
     rec_at = ordered(place * block + receiver_index % block)
     shot_at = ordered(shot_index - (owner - 1) * block)
-    live = live_counts[0] - jnp.stack([(y - k) % NY * share + h * piece for h in range(CHUNKS) for k in range(NY)])
-
+    live = live_counts[0] - jnp.stack([(y - k) % NY * share + at for at in first for k in range(NY)])
+
+    shot_terms = join([shot_terms], got[0])
     shot_near = jnp.concatenate([neighbour(shot_terms, 1), shot_terms, neighbour(shot_terms, -1)])
 
-    model = gather_terms(terms, far_terms, shot_near, rec_at, shot_at)
+    model = gather_terms([terms] + far_terms, shot_near, rec_at, shot_at)
+
+    codes = []
+    for t, inner, size in BACK:
+        after = (model,) if t else ()
+        outs = spectra(traces, y, starts[t] + inner, inner, size, got[t], table, width, after)
+        codes += [send_y(outs[k], k) if k else outs[k] for k in range(NY)]
 
     sums = sum_receivers(codes, model, live, rec_at, block * NZ * NX * NC)
     half = sums.shape[0] // 2
-    sums = sums[:half] + swap_core(sums[half:])
+    sums = sums[:half] + swap(sums[half:], 0, 0, 1)
     sums = sums.reshape(NX, NZ * block, width)
     sent = (sums * SUM_SCALE).astype(jnp.float16)
-    come = [send_x(sent[k], k).astype(jnp.float32) for k in (1, 3, 2)]
-    sums = sums[0] + (come[0] + come[1] + come[2]) * (1.0 / SUM_SCALE)
-    half = sums.shape[0] // 2
-    sent = (sums[half:] * SUM_SCALE).astype(jnp.float16)
-    sums = sums[:half] + swap_z(sent).astype(jnp.float32) * (1.0 / SUM_SCALE)
+    come = [swap(sent[k], 0, k, 0).astype(jnp.float32) for k in (1, 3, 2)]
+    shots = sum_shots(codes, model, live, shot_at, 3 * block)
+    shot_sums = shots[block : 2 * block] + neighbour(shots[2 * block :], 1) + neighbour(shots[:block], -1)
+    sums = join([sums[0]], (shot_sums,)) + (come[0] + come[1] + come[2]) * (1.0 / SUM_SCALE)
+    sums = sums.reshape(2, NZ // 2 * block, width)
+    sent = (sums[1] * SUM_SCALE).astype(jnp.float16)
+    sums = sums[0] + swap(sent, 4, 0, 0).astype(jnp.float32) * (1.0 / SUM_SCALE)
     sums = sums.reshape(NZ // 2, block, width)
     sent = (sums * SUM_SCALE).astype(jnp.float16)
-    come = [send_z(sent[k], 2 * k).astype(jnp.float32) for k in (1, 3, 2)]
+    come = [swap(sent[k], k, 0, 0).astype(jnp.float32) for k in (1, 3, 2)]
     receiver_sums = sums[0] + (come[0] + come[1] + come[2]) * (1.0 / SUM_SCALE)
-
-    shots = sum_shots(codes, model, live, shot_at, 3 * block)
-    shot_sums = shots[block : 2 * block] + neighbour(shots[2 * block :], 1) + neighbour(shots[:block], -1)
     return (shot_sums, receiver_sums)
 
 

time: 180 us -> 186 us (1.033)
  waiting for transfers between devices: 29.8 us -> 48.1 us
  starting transfers between devices: 65.1 us -> 56.5 us
  local copies, waits for them, and re-layouts: 14.2 us -> 11.3 us
    ppermute x16 -> x14, waiting for transfers between devices: 18.4 us -> 36.4 us  [swap(): lax.ppermute(value, 'tr', [(tr_of(z, x, c), tr_of(z ^ dz, x ^ dx, c ^ dc)...]
    ppermute x12, starting transfers between devices: 26.4 us -> 17.5 us  [send_y(): return lax.ppermute(value, 'fq', [(i, (i + k) % NY) for i in range(NY)])]
    pallas_call x1, Pallas kernels: 11.2 us -> 5.3 us  [make_table(): pl.pallas_call(body, grid=(samples // tile,), in_specs=[pl.BlockSpec(memo...]
    unnamed x54 -> x56, local copies, waits for them, and re-layouts: 10.5 us -> 6.24 us
    pallas_call x2, Pallas kernels: 0.35 us -> 3.17 us  [take_rows(): pl.pallas_call(body, grid_spec=pltpu.PrefetchScalarGridSpec(num_scalar_pr...]
    ppermute x16 -> x14, starting transfers between devices: 29.4 us -> 30.3 us  [swap(): lax.ppermute(value, 'tr', [(tr_of(z, x, c), tr_of(z ^ dz, x ^ dx, c ^ dc)...]
  transfers between devices with their start and end apart: 32 -> 30, of which waited for: 12 -> 11; matrix products, arithmetic and copies ran while one was open for 3% -> 3% of each run, Pallas kernels for 26% -> 23%
where the time goes in v3:
time: 186 us; the launch traced here: 184 us
  Pallas kernels  62.1 us (33%)
  starting transfers between devices  56.5 us (30%)
  waiting for transfers between devices  48.1 us (26%)
  local copies, waits for them, and re-layouts  11.3 us (6%)
  other arithmetic  4.03 us (2%)
  between operations  1.89 us (1%)
    ppermute x14, waiting for transfers between devices, swap(): lax.ppermute(value, 'tr', [(tr_of(z, x, c), tr_of(z ^ dz, x ^ dx, c ^ dc)...  36.4 us
    ppermute x14, starting transfers between devices, swap(): lax.ppermute(value, 'tr', [(tr_of(z, x, c), tr_of(z ^ dz, x ^ dx, c ^ dc)...  30.3 us
    ppermute x12, starting transfers between devices, send_y(): return lax.ppermute(value, 'fq', [(i, (i + k) % NY) for i in range(NY)])  17.5 us
    pallas_call x1, Pallas kernels, sum_receivers(): pl.pallas_call(body, in_specs=[sm, sm] + [vm] * (1 + parts), out_specs=vm...  17.2 us
    pallas_call x1, Pallas kernels, gather_terms(): pl.pallas_call(body, in_specs=[sm, sm, vm] + [vm] * parts, out_specs=vm,...  16.5 us
    pallas_call x2, Pallas kernels, spectra(): pl.pallas_call(body, grid_spec=pltpu.PrefetchScalarGridSpec(num_scalar_pr...  12.6 us
    ppermute x12, waiting for transfers between devices, send_y(): return lax.ppermute(value, 'fq', [(i, (i + k) % NY) for i in range(NY)])  11.7 us
    ppermute x4, starting transfers between devices, neighbour(): lax.ppermute(value, 'tr', [(i, i + by) for i in range(size) if 0 <= i + b...  8.65 us
  transfers between devices with their start and end apart: 30, of which 11 were waited for; matrix products, arithmetic and copies ran while one was open for 3% of the time, Pallas kernels for 23%

profile of v3, /device:TPU:8, one launch (start us, length us, event | category | flops | bytes accessed | tf_op | source)
XLA Modules:
  0.0 183.9 jit_solution(11009851286747813559)
XLA Ops:
  0.6 2.2 %copy-done = bf16[8192,256]{1,0:T(8,128)(2,1)S(1)} copy-done((bf16[8192,256]{1,0:T(8,128)(2,1)S(1)}, bf16[8192,256]{1,0:T(8,128)(2,1)}, u32[]{:S(2)}) %copy-start) | copy-done | bytes 4194328
  2.8 1.7 take_rows.2
  4.6 2.0 %collective-permute-start.5 = (s16[128,128]{1,0:T(8,128)(2,1)S(1)}, s16[128,128]{1,0:T(8,128)(2,1)S(1)}, u32[]{:S(2)}, u32[]{:S(2)}) collective-permute-start(s16[128,128]{1,0:T(8,128)(2,1)S(1)} %encode_terms.1.refs_0_), channel_id=1, source_target_pairs={{0,32},{4,36},{8,40},{12,44},{16,48},{20,52},{24,56},{28,60},{32,0... | collective-permute-start | bytes 98312 | tf_op jit(solution)/shard_map/ppermute | solution.py:32
  6.6 2.0 %collective-permute-done.5.refs_1_ = s16[128,128]{1,0:T(8,128)(2,1)S(1)} collective-permute-done((s16[128,128]{1,0:T(8,128)(2,1)S(1)}, s16[128,128]{1,0:T(8,128)(2,1)S(1)}, u32[]{:S(2)}, u32[]{:S(2)}) %collective-permute-start.5) | collective-permute-done | bytes 32800 | tf_op jit(solution)/shard_map/ppermute | solution.py:32
  8.6 3.3 %collective-permute-start.6 = (s16[256,128]{1,0:T(8,128)(2,1)S(1)}, s16[256,128]{1,0:T(8,128)(2,1)S(1)}, u32[]{:S(2)}, u32[]{:S(2)}) collective-permute-start(s16[256,128]{1,0:T(8,128)(2,1)S(1)} %join.8.refs_0_), channel_id=1, source_target_pairs={{0,64},{4,68},{8,72},{12,76},{16,80},{20,84},{24,88},{28,92},{32,9... | collective-permute-start | bytes 196616 | tf_op jit(solution)/shard_map/ppermute | solution.py:32
  11.9 1.6 collective-permute-start
  13.4 0.9 collective-permute-start.1
  14.4 2.4 %collective-permute-start.2 = (bf16[1024,256]{1,0:T(8,128)(2,1)}, bf16[1024,256]{1,0:T(8,128)(2,1)}, u32[]{:S(2)}, u32[]{:S(2)}) collective-permute-start(bf16[1024,256]{1,0:T(8,128)(2,1)} %get-tuple-element.18), channel_id=1, source_target_pairs={{0,3},{1,0},{2,1},{3,2},{4,7},{5,4},{6,5},{7,6},{8,11},{9,8},{10,9... | collective-permute-start | bytes 1572872 | tf_op jit(solution)/shard_map/ppermute | solution.py:36
  16.8 5.5 %collective-permute-start.7 = (s16[512,128]{1,0:T(8,128)(2,1)S(1)}, s16[512,128]{1,0:T(8,128)(2,1)S(1)}, u32[]{:S(2)}, u32[]{:S(2)}) collective-permute-start(s16[512,128]{1,0:T(8,128)(2,1)S(1)} %join.9.refs_0_), channel_id=1, source_target_pairs={{0,128},{4,132},{8,136},{12,140},{16,144},{20,148},{24,152},{28,15... | collective-permute-start | bytes 393224 | tf_op jit(solution)/shard_map/ppermute | solution.py:32
  22.9 5.3 %make_table.1.refs_2_.t = bf16[1024,1024]{1,0:T(8,128)(2,1)S(1)} custom-call(s32[1]{0:T(128)} %bitcast.10.y_ref), custom_call_target="tpu_custom_call" | custom-call | flops 1073741824 | bytes 33554432 | tf_op jit(solution)/shard_map/make_table/pallas_call | solution.py:63
  29.0 0.9 copy-done.8
  29.9 1.6 collective-permute-start.8
  32.6 3.9 %collective-permute-done.8.refs_1_ = s16[1024,128]{1,0:T(8,128)(2,1)} collective-permute-done((s16[1024,128]{1,0:T(8,128)(2,1)S(1)}, s16[1024,128]{1,0:T(8,128)(2,1)}, u32[]{:S(2)}, u32[]{:S(2)}) %collective-permute-start.8) | collective-permute-done | bytes 262176 | tf_op jit(solution)/shard_map/ppermute | solution.py:32
  36.5 1.1 join.11.refs_0_
  37.6 3.1 %collective-permute-start.9 = (s16[2048,128]{1,0:T(8,128)(2,1)S(1)}, s16[2048,128]{1,0:T(8,128)(2,1)S(1)}, u32[]{:S(2)}, u32[]{:S(2)}) collective-permute-start(s16[2048,128]{1,0:T(8,128)(2,1)S(1)} %join.11.refs_0_), channel_id=1, source_target_pairs={{0,16},{4,20},{8,24},{12,28},{16,0},{20,4},{24,8},{28,12},{32,48},... | collective-permute-start | bytes 1572872 | tf_op jit(solution)/shard_map/ppermute | solution.py:32
  40.8 9.0 %collective-permute-done.9.refs_1_ = s16[2048,128]{1,0:T(8,128)(2,1)S(1)} collective-permute-done((s16[2048,128]{1,0:T(8,128)(2,1)S(1)}, s16[2048,128]{1,0:T(8,128)(2,1)S(1)}, u32[]{:S(2)}, u32[]{:S(2)}) %collective-permute-start.9) | collective-permute-done | bytes 524320 | tf_op jit(solution)/shard_map/ppermute | solution.py:32
  50.1 1.3 collective-permute-start.4
  51.4 3.0 %collective-permute-start.3 = (f32[128,128]{1,0:T(8,128)S(1)}, f32[128,128]{1,0:T(8,128)S(1)}, u32[]{:S(2)}, u32[]{:S(2)}) collective-permute-start(f32[128,128]{1,0:T(8,128)S(1)} %join.7), channel_id=1, source_target_pairs={{0,4},{4,8},{8,12},{12,16},{16,20},{20,24},{24,28},{28,32},{32,36}... | collective-permute-start | bytes 196616 | tf_op jit(solution)/shard_map/ppermute | solution.py:289
  54.5 1.4 take_rows.3
  55.9 1.2 collective-permute-start.14
  57.2 2.3 %collective-permute-start.15 = (bf16[1024,256]{1,0:T(8,128)(2,1)S(1)}, bf16[1024,256]{1,0:T(8,128)(2,1)S(1)}, u32[]{:S(2)}, u32[]{:S(2)}) collective-permute-start(bf16[1024,256]{1,0:T(8,128)(2,1)S(1)} %get-tuple-element.24), channel_id=1, source_target_pairs={{0,2},{1,3},{2,0},{3,1},{4,6},{5,7},{6,4},{7,5},{8,10},{9,11},{10,... | collective-permute-start | bytes 1572872 | tf_op jit(solution)/shard_map/ppermute | solution.py:36
  59.4 1.1 collective-permute-start.16
  60.5 6.3 %spectra.2 = (s16[1024,128]{1,0:T(8,128)(2,1)}, s16[1024,128]{1,0:T(8,128)(2,1)}, s16[1024,128]{1,0:T(8,128)(2,1)}, s16[1024,128]{1,0:T(8,128)(2,1)}) custom-call(s32[1]{0:T(128)} %bitcast.10.y_ref, bf16[8192,256]{1,0:T(8,128)(2,1)} %b0.3, bf16[1024,256]{1,0:T(8,128)(2,1)} %copy-done.3, bf16[1024,256]{1,0:T(8,128)(2,1)} %copy-done.4, ...), custom_call_target="tpu_custom_call" | custom-call | flops 1000 | bytes 1000 | tf_op jit(solution)/shard_map/spectra/pallas_call | solution.py:156
  66.9 1.0 collective-permute-start.11
  68.6 2.5 %collective-permute-start.12 = (s16[1024,128]{1,0:T(8,128)(2,1)}, s16[1024,128]{1,0:T(8,128)(2,1)S(1)}, u32[]{:S(2)}, u32[]{:S(2)}) collective-permute-start(s16[1024,128]{1,0:T(8,128)(2,1)} %get-tuple-element.21), channel_id=1, source_target_pairs={{0,2},{1,3},{2,0},{3,1},{4,6},{5,7},{6,4},{7,5},{8,10},{9,11},{10,... | collective-permute-start | bytes 786440 | tf_op jit(solution)/shard_map/ppermute | solution.py:36
  71.1 16.5 %gather_terms.1.refs_0_.refs_2_ = f32[8192,128]{1,0:T(8,128)} custom-call(s32[8192]{0:T(1024)} %copy-done.22, s32[8192]{0:T(1024)} %copy-done.21, f32[384,128]{1,0:T(8,128)} %pad_maximum_fusion.shot, s16[4096,128]{1,0:T(8,128)(2,1)} %copy-done.5, s16[4096,128]{1,0:T(8,128)(2,1)} %collective-permute-done.10.refs_1_), custom_call_target="tpu_custom_call" | custom-call | flops 1000 | bytes 1000 | tf_op jit(solution)/shard_map/gather_terms/pallas_call | solution.py:194
  89.5 6.3 %spectra.3 = (s16[1024,128]{1,0:T(8,128)(2,1)}, s16[1024,128]{1,0:T(8,128)(2,1)}, s16[1024,128]{1,0:T(8,128)(2,1)}, s16[1024,128]{1,0:T(8,128)(2,1)}) custom-call(s32[1]{0:T(128)} %bitcast.10.y_ref, bf16[8192,256]{1,0:T(8,128)(2,1)} %b0.3, bf16[1024,256]{1,0:T(8,128)(2,1)} %copy-done.18, bf16[1024,256]{1,0:T(8,128)(2,1)} %copy-done.19, ...), custom_call_target="tpu_custom_call" | custom-call | flops 1000 | bytes 1000 | tf_op jit(solution)/shard_map/spectra/pallas_call | solution.py:156
  95.9 2.0 %collective-permute-start.17 = (s16[1024,128]{1,0:T(8,128)(2,1)}, s16[1024,128]{1,0:T(8,128)(2,1)S(1)}, u32[]{:S(2)}, u32[]{:S(2)}) collective-permute-start(s16[1024,128]{1,0:T(8,128)(2,1)} %get-tuple-element.27), channel_id=1, source_target_pairs={{0,1},{1,2},{2,3},{3,0},{4,5},{5,6},{6,7},{7,4},{8,9},{9,10},{10,1... | collective-permute-start | bytes 786440 | tf_op jit(solution)/shard_map/ppermute | solution.py:36
  97.8 2.3 %collective-permute-start.18 = (s16[1024,128]{1,0:T(8,128)(2,1)}, s16[1024,128]{1,0:T(8,128)(2,1)S(1)}, u32[]{:S(2)}, u32[]{:S(2)}) collective-permute-start(s16[1024,128]{1,0:T(8,128)(2,1)} %get-tuple-element.28), channel_id=1, source_target_pairs={{0,2},{1,3},{2,0},{3,1},{4,6},{5,7},{6,4},{7,5},{8,10},{9,11},{10,... | collective-permute-start | bytes 786440 | tf_op jit(solution)/shard_map/ppermute | solution.py:36
  101.5 3.9 %collective-permute-done.17.refs_8_ = s16[1024,128]{1,0:T(8,128)(2,1)S(1)} collective-permute-done((s16[1024,128]{1,0:T(8,128)(2,1)}, s16[1024,128]{1,0:T(8,128)(2,1)S(1)}, u32[]{:S(2)}, u32[]{:S(2)}) %collective-permute-start.17) | collective-permute-done | bytes 262176 | tf_op jit(solution)/shard_map/ppermute | solution.py:36
  105.4 3.4 %collective-permute-done.18.refs_9_ = s16[1024,128]{1,0:T(8,128)(2,1)S(1)} collective-permute-done((s16[1024,128]{1,0:T(8,128)(2,1)}, s16[1024,128]{1,0:T(8,128)(2,1)S(1)}, u32[]{:S(2)}, u32[]{:S(2)}) %collective-permute-start.18) | collective-permute-done | bytes 262176 | tf_op jit(solution)/shard_map/ppermute | solution.py:36
  108.8 4.4 %collective-permute-done.19.refs_10_ = s16[1024,128]{1,0:T(8,128)(2,1)S(1)} collective-permute-done((s16[1024,128]{1,0:T(8,128)(2,1)}, s16[1024,128]{1,0:T(8,128)(2,1)S(1)}, u32[]{:S(2)}, u32[]{:S(2)}) %collective-permute-start.19) | collective-permute-done | bytes 262176 | tf_op jit(solution)/shard_map/ppermute | solution.py:36
  113.9 17.2 %sum_receivers.1 = f32[8192,128]{1,0:T(8,128)} custom-call(s32[8192]{0:T(1024)} %copy-done.22, s32[8]{0:T(128)} %broadcast_subtract_fusion.1.refs_1_, f32[8192,128]{1,0:T(8,128)} %gather_terms.1.refs_0_.refs_2_, s16[1024,128]{1,0:T(8,128)(2,1)} %get-tuple-element.19.refs_3_, s16[1024,128]{1,0:T(8,128)(2,1)} %copy-done.12, s16[1024,128]{1,0:T(8,128)(2,1)} %copy-done.13, ...), custom_call_target="tpu_custom_call" | custom-call | flops 1000 | bytes 1000 | tf_op jit(solution)/shard_map/sum_receivers/pallas_call | solution.py:245
  131.1 3.0 %slice.94 = f32[4096,128]{1,0:T(8,128)} slice(f32[8192,128]{1,0:T(8,128)} %sum_receivers.1), slice={[4096:8192], [0:128]} | slice | bytes 4194304 | tf_op jit(solution)/shard_map/slice | solution.py:343
  134.1 6.0 %sum_shots.1 = f32[384,128]{1,0:T(8,128)} custom-call(s32[1,8192]{1,0:T(1,128)} %bitcast.28, s32[8]{0:T(128)} %broadcast_subtract_fusion.1.refs_1_, f32[8192,128]{1,0:T(8,128)} %gather_terms.1.refs_0_.refs_2_, s16[1024,128]{1,0:T(8,128)(2,1)} %get-tuple-element.19.refs_3_, s16[1024,128]{1,0:T(8,128)(2,1)} %copy-done.12, s16[1024,128]{1,0:T(8,128)(2,1)} %copy-done.13, ...), custom_call_target="tpu_custom_call" | custom-call | flops 1000 | bytes 1000 | tf_op jit(solution)/shard_map/sum_shots/pallas_call | solution.py:276
  140.1 0.9 fusion.19
  141.0 1.3 collective-permute-start.21
  142.3 3.0 %collective-permute-start.20 = (f32[128,128]{1,0:T(8,128)S(1)}, f32[128,128]{1,0:T(8,128)S(1)}, u32[]{:S(2)}, u32[]{:S(2)}) collective-permute-start(f32[128,128]{1,0:T(8,128)S(1)} %get-tuple-element.37), channel_id=1, source_target_pairs={{0,4},{4,8},{8,12},{12,16},{16,20},{20,24},{24,28},{28,32},{32,36}... | collective-permute-start | bytes 196616 | tf_op jit(solution)/shard_map/ppermute | solution.py:289
  145.8 3.0 %collective-permute-start.25 = (f16[1024,128]{1,0:T(8,128)(2,1)S(1)}, f16[1024,128]{1,0:T(8,128)(2,1)S(1)}, u32[]{:S(2)}, u32[]{:S(2)}) collective-permute-start(f16[1024,128]{1,0:T(8,128)(2,1)S(1)} %get-tuple-element.35), channel_id=1, source_target_pairs={{0,16},{4,20},{8,24},{12,28},{16,0},{20,4},{24,8},{28,12},{32,48},... | collective-permute-start | bytes 786440 | tf_op jit(solution)/shard_map/ppermute | solution.py:32
  148.8 1.6 collective-permute-start.24
  151.0 0.9 fusion.1.refs_1_
  152.0 4.9 %collective-permute-done.25 = f16[1024,128]{1,0:T(8,128)(2,1)S(1)} collective-permute-done((f16[1024,128]{1,0:T(8,128)(2,1)S(1)}, f16[1024,128]{1,0:T(8,128)(2,1)S(1)}, u32[]{:S(2)}, u32[]{:S(2)}) %collective-permute-start.25) | collective-permute-done | bytes 262176 | tf_op jit(solution)/shard_map/ppermute | solution.py:32
  156.8 6.2 %collective-permute-done.24 = f16[1024,128]{1,0:T(8,128)(2,1)S(1)} collective-permute-done((f16[1024,128]{1,0:T(8,128)(2,1)S(1)}, f16[1024,128]{1,0:T(8,128)(2,1)S(1)}, u32[]{:S(2)}, u32[]{:S(2)}) %collective-permute-start.24) | collective-permute-done | bytes 262176 | tf_op jit(solution)/shard_map/ppermute | solution.py:32
  163.2 3.9 %collective-permute-start.26 = (f16[512,128]{1,0:T(8,128)(2,1)S(1)}, f16[512,128]{1,0:T(8,128)(2,1)S(1)}, u32[]{:S(2)}, u32[]{:S(2)}) collective-permute-start(f16[512,128]{1,0:T(8,128)(2,1)S(1)} %fusion), channel_id=1, source_target_pairs={{0,128},{4,132},{8,136},{12,140},{16,144},{20,148},{24,152},{28,15... | collective-permute-start | bytes 393224 | tf_op jit(solution)/shard_map/ppermute | solution.py:32
  167.1 6.2 %collective-permute-done.26 = f16[512,128]{1,0:T(8,128)(2,1)S(1)} collective-permute-done((f16[512,128]{1,0:T(8,128)(2,1)S(1)}, f16[512,128]{1,0:T(8,128)(2,1)S(1)}, u32[]{:S(2)}, u32[]{:S(2)}) %collective-permute-start.26) | collective-permute-done | bytes 131104 | tf_op jit(solution)/shard_map/ppermute | solution.py:32
  173.4 4.1 %collective-permute-start.29 = (f16[128,128]{1,0:T(8,128)(2,1)S(1)}, f16[128,128]{1,0:T(8,128)(2,1)S(1)}, u32[]{:S(2)}, u32[]{:S(2)}) collective-permute-start(f16[128,128]{1,0:T(8,128)(2,1)S(1)} %get-tuple-element.40), channel_id=1, source_target_pairs={{0,64},{4,68},{8,72},{12,76},{16,80},{20,84},{24,88},{28,92},{32,9... | collective-permute-start | bytes 98312 | tf_op jit(solution)/shard_map/ppermute | solution.py:32
  177.5 1.0 collective-permute-start.28
  179.4 3.8 %collective-permute-done.28 = f16[128,128]{1,0:T(8,128)(2,1)S(1)} collective-permute-done((f16[128,128]{1,0:T(8,128)(2,1)S(1)}, f16[128,128]{1,0:T(8,128)(2,1)S(1)}, u32[]{:S(2)}, u32[]{:S(2)}) %collective-permute-start.28) | collective-permute-done | bytes 32800 | tf_op jit(solution)/shard_map/ppermute | solution.py:32
  (107 shorter events, 9.5 us)
Async XLA Ops:
  0.6 2.2 %copy-start = (bf16[8192,256]{1,0:T(8,128)(2,1)S(1)}, bf16[8192,256]{1,0:T(8,128)(2,1)}, u32[]{:S(2)}) copy-start(bf16[8192,256]{1,0:T(8,128)(2,1)} %b0.3) | copy-start | bytes 12582916
  2.8 19.5 %copy-start.23 = (s32[8192]{0:T(1024)S(1)}, s32[8192]{0:T(1024)}, u32[]{:S(2)}) copy-start(s32[8192]{0:T(1024)} %param.7) | copy-start | bytes 98308
  4.6 4.0 %collective-permute-start.5 = (s16[128,128]{1,0:T(8,128)(2,1)S(1)}, s16[128,128]{1,0:T(8,128)(2,1)S(1)}, u32[]{:S(2)}, u32[]{:S(2)}) collective-permute-start(s16[128,128]{1,0:T(8,128)(2,1)S(1)} %encode_terms.1.refs_0_), channel_id=1, source_target_pairs={{0,32},{4,36},{8,40},{12,44},{16,48},{20,52},{24,56},{28,60},{32,0... | collective-permute-start | bytes 98312 | tf_op jit(solution)/shard_map/ppermute | solution.py:32
  8.6 8.2 %collective-permute-start.6 = (s16[256,128]{1,0:T(8,128)(2,1)S(1)}, s16[256,128]{1,0:T(8,128)(2,1)S(1)}, u32[]{:S(2)}, u32[]{:S(2)}) collective-permute-start(s16[256,128]{1,0:T(8,128)(2,1)S(1)} %join.8.refs_0_), channel_id=1, source_target_pairs={{0,64},{4,68},{8,72},{12,76},{16,80},{20,84},{24,88},{28,92},{32,9... | collective-permute-start | bytes 196616 | tf_op jit(solution)/shard_map/ppermute | solution.py:32
  11.9 38.2 %collective-permute-start = (bf16[1024,256]{1,0:T(8,128)(2,1)}, bf16[1024,256]{1,0:T(8,128)(2,1)S(1)}, u32[]{:S(2)}, u32[]{:S(2)}) collective-permute-start(bf16[1024,256]{1,0:T(8,128)(2,1)} %get-tuple-element.16.refs_0_), channel_id=1, source_target_pairs={{0,1},{1,2},{2,3},{3,0},{4,5},{5,6},{6,7},{7,4},{8,9},{9,10},{10,1... | collective-permute-start | bytes 1572872 | tf_op jit(solution)/shard_map/ppermute | solution.py:36
  13.4 36.6 %collective-permute-start.1 = (bf16[1024,256]{1,0:T(8,128)(2,1)}, bf16[1024,256]{1,0:T(8,128)(2,1)S(1)}, u32[]{:S(2)}, u32[]{:S(2)}) collective-permute-start(bf16[1024,256]{1,0:T(8,128)(2,1)} %get-tuple-element.17), channel_id=1, source_target_pairs={{0,2},{1,3},{2,0},{3,1},{4,6},{5,7},{6,4},{7,5},{8,10},{9,11},{10,... | collective-permute-start | bytes 1572872 | tf_op jit(solution)/shard_map/ppermute | solution.py:36
  14.4 35.7 %collective-permute-start.2 = (bf16[1024,256]{1,0:T(8,128)(2,1)}, bf16[1024,256]{1,0:T(8,128)(2,1)}, u32[]{:S(2)}, u32[]{:S(2)}) collective-permute-start(bf16[1024,256]{1,0:T(8,128)(2,1)} %get-tuple-element.18), channel_id=1, source_target_pairs={{0,3},{1,0},{2,1},{3,2},{4,7},{5,4},{6,5},{7,6},{8,11},{9,8},{10,9... | collective-permute-start | bytes 1572872 | tf_op jit(solution)/shard_map/ppermute | solution.py:36
  16.8 11.4 %collective-permute-start.7 = (s16[512,128]{1,0:T(8,128)(2,1)S(1)}, s16[512,128]{1,0:T(8,128)(2,1)S(1)}, u32[]{:S(2)}, u32[]{:S(2)}) collective-permute-start(s16[512,128]{1,0:T(8,128)(2,1)S(1)} %join.9.refs_0_), channel_id=1, source_target_pairs={{0,128},{4,132},{8,136},{12,140},{16,144},{20,148},{24,152},{28,15... | collective-permute-start | bytes 393224 | tf_op jit(solution)/shard_map/ppermute | solution.py:32
  28.2 12.6 %copy-start.2 = (bf16[1024,1024]{1,0:T(8,128)(2,1)}, bf16[1024,1024]{1,0:T(8,128)(2,1)S(1)}, u32[]{:S(2)}) copy-start(bf16[1024,1024]{1,0:T(8,128)(2,1)S(1)} %make_table.1.refs_2_.t) | copy-start | bytes 6291460
  29.9 20.2 %copy-start.10 = (f32[128,128]{1,0:T(8,128)S(1)}, f32[128,128]{1,0:T(8,128)}, u32[]{:S(2)}) copy-start(f32[128,128]{1,0:T(8,128)} %refs_0_.4) | copy-start | bytes 196612
  29.9 6.6 %collective-permute-start.8 = (s16[1024,128]{1,0:T(8,128)(2,1)S(1)}, s16[1024,128]{1,0:T(8,128)(2,1)}, u32[]{:S(2)}, u32[]{:S(2)}) collective-permute-start(s16[1024,128]{1,0:T(8,128)(2,1)S(1)} %join.10.refs_0_), channel_id=1, source_target_pairs={{0,8},{4,12},{8,0},{12,4},{16,24},{20,28},{24,16},{28,20},{32,40},... | collective-permute-start | bytes 786440 | tf_op jit(solution)/shard_map/ppermute | solution.py:32
  36.5 18.0 %copy-start.1 = (bf16[8192,256]{1,0:T(8,128)(2,1)S(1)}, bf16[8192,256]{1,0:T(8,128)(2,1)}, u32[]{:S(2)}) copy-start(bf16[8192,256]{1,0:T(8,128)(2,1)} %b0.3) | copy-start | bytes 12582916
  37.6 12.2 %collective-permute-start.9 = (s16[2048,128]{1,0:T(8,128)(2,1)S(1)}, s16[2048,128]{1,0:T(8,128)(2,1)S(1)}, u32[]{:S(2)}, u32[]{:S(2)}) collective-permute-start(s16[2048,128]{1,0:T(8,128)(2,1)S(1)} %join.11.refs_0_), channel_id=1, source_target_pairs={{0,16},{4,20},{8,24},{12,28},{16,0},{20,4},{24,8},{28,12},{32,48},... | collective-permute-start | bytes 1572872 | tf_op jit(solution)/shard_map/ppermute | solution.py:32
  49.9 6.1 %copy-start.5 = (s16[4096,128]{1,0:T(8,128)(2,1)}, s16[4096,128]{1,0:T(8,128)(2,1)S(1)}, u32[]{:S(2)}) copy-start(s16[4096,128]{1,0:T(8,128)(2,1)S(1)} %join.12.refs_0_) | copy-start | bytes 3145732
  49.9 18.7 %collective-permute-start.10 = (s16[4096,128]{1,0:T(8,128)(2,1)S(1)}, s16[4096,128]{1,0:T(8,128)(2,1)}, u32[]{:S(2)}, u32[]{:S(2)}) collective-permute-start(s16[4096,128]{1,0:T(8,128)(2,1)S(1)} %join.12.refs_0_), channel_id=1, source_target_pairs={{0,4},{4,0},{8,12},{12,8},{16,20},{20,16},{24,28},{28,24},{32,36},... | collective-permute-start | bytes 3145736 | tf_op jit(solution)/shard_map/ppermute | solution.py:32
  50.1 5.9 %copy-start.3 = (bf16[1024,256]{1,0:T(8,128)(2,1)}, bf16[1024,256]{1,0:T(8,128)(2,1)S(1)}, u32[]{:S(2)}) copy-start(bf16[1024,256]{1,0:T(8,128)(2,1)S(1)} %collective-permute-done.refs_1_.b1.refs_3_) | copy-start | bytes 1572868
  50.1 5.9 %copy-start.4 = (bf16[1024,256]{1,0:T(8,128)(2,1)}, bf16[1024,256]{1,0:T(8,128)(2,1)S(1)}, u32[]{:S(2)}) copy-start(bf16[1024,256]{1,0:T(8,128)(2,1)S(1)} %collective-permute-done.1.refs_2_.b2.refs_4_) | copy-start | bytes 1572868
  50.1 9.3 %collective-permute-start.4 = (f32[128,128]{1,0:T(8,128)S(1)}, f32[128,128]{1,0:T(8,128)S(1)}, u32[]{:S(2)}, u32[]{:S(2)}) collective-permute-start(f32[128,128]{1,0:T(8,128)S(1)} %join.7), channel_id=1, source_target_pairs={{4,0},{8,4},{12,8},{16,12},{20,16},{24,20},{28,24},{32,28},{36,32}... | collective-permute-start | bytes 196616 | tf_op jit(solution)/shard_map/ppermute | solution.py:289
  51.4 15.4 %collective-permute-start.3 = (f32[128,128]{1,0:T(8,128)S(1)}, f32[128,128]{1,0:T(8,128)S(1)}, u32[]{:S(2)}, u32[]{:S(2)}) collective-permute-start(f32[128,128]{1,0:T(8,128)S(1)} %join.7), channel_id=1, source_target_pairs={{0,4},{4,8},{8,12},{12,16},{16,20},{20,24},{24,28},{28,32},{32,36}... | collective-permute-start | bytes 196616 | tf_op jit(solution)/shard_map/ppermute | solution.py:289
  55.9 31.6 %collective-permute-start.14 = (bf16[1024,256]{1,0:T(8,128)(2,1)}, bf16[1024,256]{1,0:T(8,128)(2,1)S(1)}, u32[]{:S(2)}, u32[]{:S(2)}) collective-permute-start(bf16[1024,256]{1,0:T(8,128)(2,1)} %get-tuple-element.23), channel_id=1, source_target_pairs={{0,1},{1,2},{2,3},{3,0},{4,5},{5,6},{6,7},{7,4},{8,9},{9,10},{10,1... | collective-permute-start | bytes 1572872 | tf_op jit(solution)/shard_map/ppermute | solution.py:36
  57.2 30.7 %collective-permute-start.15 = (bf16[1024,256]{1,0:T(8,128)(2,1)S(1)}, bf16[1024,256]{1,0:T(8,128)(2,1)S(1)}, u32[]{:S(2)}, u32[]{:S(2)}) collective-permute-start(bf16[1024,256]{1,0:T(8,128)(2,1)S(1)} %get-tuple-element.24), channel_id=1, source_target_pairs={{0,2},{1,3},{2,0},{3,1},{4,6},{5,7},{6,4},{7,5},{8,10},{9,11},{10,... | collective-permute-start | bytes 1572872 | tf_op jit(solution)/shard_map/ppermute | solution.py:36
  59.4 28.4 %collective-permute-start.16 = (bf16[1024,256]{1,0:T(8,128)(2,1)S(1)}, bf16[1024,256]{1,0:T(8,128)(2,1)S(1)}, u32[]{:S(2)}, u32[]{:S(2)}) collective-permute-start(bf16[1024,256]{1,0:T(8,128)(2,1)S(1)} %get-tuple-element.25), channel_id=1, source_target_pairs={{0,3},{1,0},{2,1},{3,2},{4,7},{5,4},{6,5},{7,6},{8,11},{9,8},{10,9... | collective-permute-start | bytes 1572872 | tf_op jit(solution)/shard_map/ppermute | solution.py:36
  60.5 6.3 %copy-start.21 = (s32[8192]{0:T(1024)}, s32[8192]{0:T(1024)S(1)}, u32[]{:S(2)}) copy-start(s32[8192]{0:T(1024)S(1)} %bitcast_dynamic-update-slice_fusion.2.shot_at) | copy-start | bytes 98308
  66.9 33.3 %collective-permute-start.11 = (s16[1024,128]{1,0:T(8,128)(2,1)}, s16[1024,128]{1,0:T(8,128)(2,1)S(1)}, u32[]{:S(2)}, u32[]{:S(2)}) collective-permute-start(s16[1024,128]{1,0:T(8,128)(2,1)} %get-tuple-element.20), channel_id=1, source_target_pairs={{0,1},{1,2},{2,3},{3,0},{4,5},{5,6},{6,7},{7,4},{8,9},{9,10},{10,1... | collective-permute-start | bytes 786440 | tf_op jit(solution)/shard_map/ppermute | solution.py:36
  67.9 3.2 %copy-start.22 = (s32[8192]{0:T(1024)}, s32[8192]{0:T(1024)S(1)}, u32[]{:S(2)}) copy-start(s32[8192]{0:T(1024)S(1)} %bitcast_dynamic-update-slice_fusion.rec_at.refs_0_) | copy-start | bytes 98308
  68.6 19.0 %copy-start.25 = (s16[1024,128]{1,0:T(8,128)(2,1)S(1)}, s16[1024,128]{1,0:T(8,128)(2,1)}, u32[]{:S(2)}) copy-start(s16[1024,128]{1,0:T(8,128)(2,1)} %get-tuple-element.22) | copy-start | bytes 786436
  68.6 32.9 %collective-permute-start.12 = (s16[1024,128]{1,0:T(8,128)(2,1)}, s16[1024,128]{1,0:T(8,128)(2,1)S(1)}, u32[]{:S(2)}, u32[]{:S(2)}) collective-permute-start(s16[1024,128]{1,0:T(8,128)(2,1)} %get-tuple-element.21), channel_id=1, source_target_pairs={{0,2},{1,3},{2,0},{3,1},{4,6},{5,7},{6,4},{7,5},{8,10},{9,11},{10,... | collective-permute-start | bytes 786440 | tf_op jit(solution)/shard_map/ppermute | solution.py:36
  87.6 13.9 %collective-permute-start.13 = (s16[1024,128]{1,0:T(8,128)(2,1)S(1)}, s16[1024,128]{1,0:T(8,128)(2,1)S(1)}, u32[]{:S(2)}, u32[]{:S(2)}) collective-permute-start(s16[1024,128]{1,0:T(8,128)(2,1)S(1)} %copy-done.25), channel_id=1, source_target_pairs={{0,3},{1,0},{2,1},{3,2},{4,7},{5,4},{6,5},{7,6},{8,11},{9,8},{10,9... | collective-permute-start | bytes 786440 | tf_op jit(solution)/shard_map/ppermute | solution.py:36
  95.9 9.5 %collective-permute-start.17 = (s16[1024,128]{1,0:T(8,128)(2,1)}, s16[1024,128]{1,0:T(8,128)(2,1)S(1)}, u32[]{:S(2)}, u32[]{:S(2)}) collective-permute-start(s16[1024,128]{1,0:T(8,128)(2,1)} %get-tuple-element.27), channel_id=1, source_target_pairs={{0,1},{1,2},{2,3},{3,0},{4,5},{5,6},{6,7},{7,4},{8,9},{9,10},{10,1... | collective-permute-start | bytes 786440 | tf_op jit(solution)/shard_map/ppermute | solution.py:36
  97.8 11.0 %collective-permute-start.18 = (s16[1024,128]{1,0:T(8,128)(2,1)}, s16[1024,128]{1,0:T(8,128)(2,1)S(1)}, u32[]{:S(2)}, u32[]{:S(2)}) collective-permute-start(s16[1024,128]{1,0:T(8,128)(2,1)} %get-tuple-element.28), channel_id=1, source_target_pairs={{0,2},{1,3},{2,0},{3,1},{4,6},{5,7},{6,4},{7,5},{8,10},{9,11},{10,... | collective-permute-start | bytes 786440 | tf_op jit(solution)/shard_map/ppermute | solution.py:36
  100.1 13.0 %copy-start.12 = (s16[1024,128]{1,0:T(8,128)(2,1)}, s16[1024,128]{1,0:T(8,128)(2,1)S(1)}, u32[]{:S(2)}) copy-start(s16[1024,128]{1,0:T(8,128)(2,1)S(1)} %collective-permute-done.11.refs_4_) | copy-start | bytes 786436
  100.1 13.0 %collective-permute-start.19 = (s16[1024,128]{1,0:T(8,128)(2,1)}, s16[1024,128]{1,0:T(8,128)(2,1)S(1)}, u32[]{:S(2)}, u32[]{:S(2)}) collective-permute-start(s16[1024,128]{1,0:T(8,128)(2,1)} %get-tuple-element.29), channel_id=1, source_target_pairs={{0,3},{1,0},{2,1},{3,2},{4,7},{5,4},{6,5},{7,6},{8,11},{9,8},{10,9... | collective-permute-start | bytes 786440 | tf_op jit(solution)/shard_map/ppermute | solution.py:36
  101.5 11.7 %copy-start.13 = (s16[1024,128]{1,0:T(8,128)(2,1)}, s16[1024,128]{1,0:T(8,128)(2,1)S(1)}, u32[]{:S(2)}) copy-start(s16[1024,128]{1,0:T(8,128)(2,1)S(1)} %collective-permute-done.12.refs_5_) | copy-start | bytes 786436
  101.5 11.7 %copy-start.14 = (s16[1024,128]{1,0:T(8,128)(2,1)}, s16[1024,128]{1,0:T(8,128)(2,1)S(1)}, u32[]{:S(2)}) copy-start(s16[1024,128]{1,0:T(8,128)(2,1)S(1)} %collective-permute-done.13.refs_6_) | copy-start | bytes 786436
  105.4 7.8 %copy-start.15 = (s16[1024,128]{1,0:T(8,128)(2,1)}, s16[1024,128]{1,0:T(8,128)(2,1)S(1)}, u32[]{:S(2)}) copy-start(s16[1024,128]{1,0:T(8,128)(2,1)S(1)} %collective-permute-done.17.refs_8_) | copy-start | bytes 786436
  108.8 4.4 %copy-start.16 = (s16[1024,128]{1,0:T(8,128)(2,1)}, s16[1024,128]{1,0:T(8,128)(2,1)S(1)}, u32[]{:S(2)}) copy-start(s16[1024,128]{1,0:T(8,128)(2,1)S(1)} %collective-permute-done.18.refs_9_) | copy-start | bytes 786436
  134.1 11.2 %collective-permute-start.22 = (f32[4096,128]{1,0:T(8,128)}, f32[4096,128]{1,0:T(8,128)S(1)}, u32[]{:S(2)}, u32[]{:S(2)}) collective-permute-start(f32[4096,128]{1,0:T(8,128)} %slice.94), channel_id=1, source_target_pairs={{0,4},{4,0},{8,12},{12,8},{16,20},{20,16},{24,28},{28,24},{32,36},... | collective-permute-start | bytes 6291464 | tf_op jit(solution)/shard_map/ppermute | solution.py:32
  134.1 11.2 %copy-start.11 = (f32[8192,128]{1,0:T(8,128)S(1)}, f32[8192,128]{1,0:T(8,128)}, u32[]{:S(2)}) copy-start(f32[8192,128]{1,0:T(8,128)} %sum_receivers.1) | copy-start | bytes 12582916
  141.0 10.0 %collective-permute-start.21 = (f32[128,128]{1,0:T(8,128)S(1)}, f32[128,128]{1,0:T(8,128)S(1)}, u32[]{:S(2)}, u32[]{:S(2)}) collective-permute-start(f32[128,128]{1,0:T(8,128)S(1)} %get-tuple-element.38), channel_id=1, source_target_pairs={{4,0},{8,4},{12,8},{16,12},{20,16},{24,20},{28,24},{32,28},{36,32}... | collective-permute-start | bytes 196616 | tf_op jit(solution)/shard_map/ppermute | solution.py:289
  142.3 8.7 %collective-permute-start.20 = (f32[128,128]{1,0:T(8,128)S(1)}, f32[128,128]{1,0:T(8,128)S(1)}, u32[]{:S(2)}, u32[]{:S(2)}) collective-permute-start(f32[128,128]{1,0:T(8,128)S(1)} %get-tuple-element.37), channel_id=1, source_target_pairs={{0,4},{4,8},{8,12},{12,16},{16,20},{20,24},{24,28},{28,32},{32,36}... | collective-permute-start | bytes 196616 | tf_op jit(solution)/shard_map/ppermute | solution.py:289
  145.8 11.0 %collective-permute-start.25 = (f16[1024,128]{1,0:T(8,128)(2,1)S(1)}, f16[1024,128]{1,0:T(8,128)(2,1)S(1)}, u32[]{:S(2)}, u32[]{:S(2)}) collective-permute-start(f16[1024,128]{1,0:T(8,128)(2,1)S(1)} %get-tuple-element.35), channel_id=1, source_target_pairs={{0,16},{4,20},{8,24},{12,28},{16,0},{20,4},{24,8},{28,12},{32,48},... | collective-permute-start | bytes 786440 | tf_op jit(solution)/shard_map/ppermute | solution.py:32
  148.8 14.2 %collective-permute-start.24 = (f16[1024,128]{1,0:T(8,128)(2,1)S(1)}, f16[1024,128]{1,0:T(8,128)(2,1)S(1)}, u32[]{:S(2)}, u32[]{:S(2)}) collective-permute-start(f16[1024,128]{1,0:T(8,128)(2,1)S(1)} %get-tuple-element.36), channel_id=1, source_target_pairs={{0,24},{4,28},{8,16},{12,20},{16,8},{20,12},{24,0},{28,4},{32,56},... | collective-permute-start | bytes 786440 | tf_op jit(solution)/shard_map/ppermute | solution.py:32
  150.4 12.6 %collective-permute-start.23 = (f16[1024,128]{1,0:T(8,128)(2,1)S(1)}, f16[1024,128]{1,0:T(8,128)(2,1)S(1)}, u32[]{:S(2)}, u32[]{:S(2)}) collective-permute-start(f16[1024,128]{1,0:T(8,128)(2,1)S(1)} %get-tuple-element.34), channel_id=1, source_target_pairs={{0,8},{4,12},{8,0},{12,4},{16,24},{20,28},{24,16},{28,20},{32,40},... | collective-permute-start | bytes 786440 | tf_op jit(solution)/shard_map/ppermute | solution.py:32
  151.9 11.3 %copy-start.6 = (f32[128,128]{1,0:T(8,128)}, f32[128,128]{1,0:T(8,128)S(1)}, u32[]{:S(2)}) copy-start(f32[128,128]{1,0:T(8,128)S(1)} %fusion.1.refs_1_) | copy-start | bytes 196612
  163.2 10.1 %collective-permute-start.26 = (f16[512,128]{1,0:T(8,128)(2,1)S(1)}, f16[512,128]{1,0:T(8,128)(2,1)S(1)}, u32[]{:S(2)}, u32[]{:S(2)}) collective-permute-start(f16[512,128]{1,0:T(8,128)(2,1)S(1)} %fusion), channel_id=1, source_target_pairs={{0,128},{4,132},{8,136},{12,140},{16,144},{20,148},{24,152},{28,15... | collective-permute-start | bytes 393224 | tf_op jit(solution)/shard_map/ppermute | solution.py:32
  173.4 6.1 %collective-permute-start.29 = (f16[128,128]{1,0:T(8,128)(2,1)S(1)}, f16[128,128]{1,0:T(8,128)(2,1)S(1)}, u32[]{:S(2)}, u32[]{:S(2)}) collective-permute-start(f16[128,128]{1,0:T(8,128)(2,1)S(1)} %get-tuple-element.40), channel_id=1, source_target_pairs={{0,64},{4,68},{8,72},{12,76},{16,80},{20,84},{24,88},{28,92},{32,9... | collective-permute-start | bytes 98312 | tf_op jit(solution)/shard_map/ppermute | solution.py:32
  177.5 5.7 %collective-permute-start.28 = (f16[128,128]{1,0:T(8,128)(2,1)S(1)}, f16[128,128]{1,0:T(8,128)(2,1)S(1)}, u32[]{:S(2)}, u32[]{:S(2)}) collective-permute-start(f16[128,128]{1,0:T(8,128)(2,1)S(1)} %get-tuple-element.41), channel_id=1, source_target_pairs={{0,96},{4,100},{8,104},{12,108},{16,112},{20,116},{24,120},{28,124... | collective-permute-start | bytes 98312 | tf_op jit(solution)/shard_map/ppermute | solution.py:32
  178.6 4.7 %collective-permute-start.27 = (f16[128,128]{1,0:T(8,128)(2,1)S(1)}, f16[128,128]{1,0:T(8,128)(2,1)S(1)}, u32[]{:S(2)}, u32[]{:S(2)}) collective-permute-start(f16[128,128]{1,0:T(8,128)(2,1)S(1)} %get-tuple-element.39), channel_id=1, source_target_pairs={{0,32},{4,36},{8,40},{12,44},{16,48},{20,52},{24,56},{28,60},{32,0... | collective-permute-start | bytes 98312 | tf_op jit(solution)/shard_map/ppermute | solution.py:32
  (8 other events, 8.2 us)

commit v4 on v3

--- a/solution.py
+++ b/solution.py
@@ -13,8 +13,8 @@
 REC_LOW, REC_HIGH = 1.0, 2.2
 REC_SCALE = 65535.0 / (REC_HIGH - REC_LOW)
 SUM_SCALE = 1.0 / 32.0
-SENT = (1024, 1024)
-BACK = ((0, 0, 1024), (1, 0, 1024))
+SENT = (2048,)
+BACK = ((0, 0, 768), (0, 768, 1280))
 SMALL = pltpu.CompilerParams(vmem_limit_bytes=12 * 2**20)
 COST = pl.CostEstimate(flops=1000, bytes_accessed=1000, transcendentals=0)
 VMEM = pltpu.CompilerParams(vmem_limit_bytes=56 * 2**20)
@@ -137,12 +137,12 @@
     )(terms, *after)
 
 
-def spectra(traces, y, first, inner, rows, blocks, table, width, after=()):
+def spectra(traces, y, first, inner, rows, blocks, table, width):
     part, tile = traces.shape[1], 256
     share, start, steps = traces.shape[0] // NY // tile, first // tile, rows // tile
 
-    def body(y_ref, b0, b1, b2, b3, t, *refs):
-        for k, out in enumerate(refs[len(after) :]):
+    def body(y_ref, b0, b1, b2, b3, t, *outs):
+        for k, out in enumerate(outs):
             cols = pl.ds(k * 2 * width, 2 * width)
             acc = None
             for j, b in enumerate((b0, b1, b2, b3)):
@@ -160,24 +160,23 @@
             grid=(steps,),
             in_specs=[pl.BlockSpec((tile, part), lambda i, y: (y[0] * share + start + i, 0))]
             + [pl.BlockSpec((tile, part), lambda i, y: (inner // tile + i, 0))] * 3
-            + [pl.BlockSpec(table.shape, lambda i, y: (0, 0))]
-            + [pl.BlockSpec(memory_space=pl.ANY)] * len(after),
+            + [pl.BlockSpec(table.shape, lambda i, y: (0, 0))],
             out_specs=[pl.BlockSpec((tile, width), lambda i, y: (i, 0))] * 4,
         ),
         out_shape=[jax.ShapeDtypeStruct((rows, width), jnp.int16)] * 4,
         compiler_params=VMEM,
         cost_estimate=COST,
         name="spectra",
-    )(y[None], traces, *blocks, table, *after)
-
-
-def gather_terms(coded, shot_near, rec_at, shot_at):
+    )(y[None], traces, *blocks, table)
+
+
+def gather_terms(coded, shot_near, rec_at, shot_at, after):
     rows, width = rec_at.shape[0], shot_near.shape[1]
     parts = len(coded)
     spans = spans_of(coded)
 
     def body(rec_at, shot_at, shot, *refs):
-        out, rec = refs[parts:]
+        out, rec = refs[parts + len(after) :]
         for code, at in zip(refs, spans):
             rec[at, :] = (code[...].astype(jnp.float32) + 32768.0) * (1.0 / REC_SCALE) + REC_LOW
 
@@ -193,14 +192,14 @@
     vm, sm = pl.BlockSpec(memory_space=pltpu.VMEM), pl.BlockSpec(memory_space=pltpu.SMEM)
     return pl.pallas_call(
         body,
-        in_specs=[sm, sm, vm] + [vm] * parts,
+        in_specs=[sm, sm, vm] + [vm] * parts + [pl.BlockSpec(memory_space=pl.ANY)] * len(after),
         out_specs=vm,
         out_shape=jax.ShapeDtypeStruct((rows, width), jnp.float32),
         scratch_shapes=[pltpu.VMEM((sum(code.shape[0] for code in coded), width), jnp.float32)],
         compiler_params=VMEM,
         cost_estimate=COST,
         name="gather_terms",
-    )(rec_at, shot_at, shot_near, *coded)
+    )(rec_at, shot_at, shot_near, *coded, *after)
 
 
 def residual(code, model, live):
@@ -223,8 +222,8 @@
     def body(*refs):
         rec_at, live, model = refs[:3]
         codes = refs[3 : 3 + parts]
-        out, res = refs[3 + parts : 5 + parts]
-        sums = (out,) + refs[5 + parts :]
+        near, far, res = refs[3 + parts : 6 + parts]
+        sums = refs[6 + parts :]
         for s in sums:
             s[...] = jnp.zeros_like(s)
         for k, (code, at) in enumerate(zip(codes, spans)):
@@ -237,17 +236,18 @@
             return 0
 
         lax.fori_loop(0, rows // group, step, 0)
-        out[...] = ((sums[0][...] + sums[1][...]) + (sums[2][...] + sums[3][...])) + (
-            (sums[4][...] + sums[5][...]) + (sums[6][...] + sums[7][...])
-        )
+        for out, at in ((near, pl.ds(0, count // 2)), (far, pl.ds(count // 2, count // 2))):
+            out[...] = ((sums[0][at, :] + sums[1][at, :]) + (sums[2][at, :] + sums[3][at, :])) + (
+                (sums[4][at, :] + sums[5][at, :]) + (sums[6][at, :] + sums[7][at, :])
+            )
 
     vm, sm = pl.BlockSpec(memory_space=pltpu.VMEM), pl.BlockSpec(memory_space=pltpu.SMEM)
     return pl.pallas_call(
         body,
         in_specs=[sm, sm] + [vm] * (1 + parts),
-        out_specs=vm,
-        out_shape=jax.ShapeDtypeStruct((count, width), jnp.float32),
-        scratch_shapes=[pltpu.VMEM((rows, width), jnp.float32)] + [pltpu.VMEM((count, width), jnp.float32)] * (banks - 1),
+        out_specs=[vm, vm],
+        out_shape=[jax.ShapeDtypeStruct((count // 2, width), jnp.float32)] * 2,
+        scratch_shapes=[pltpu.VMEM((rows, width), jnp.float32)] + [pltpu.VMEM((count, width), jnp.float32)] * banks,
         compiler_params=VMEM,
         cost_estimate=COST,
         name="sum_receivers",
@@ -307,13 +307,10 @@
         if start == 0:
             mine_first = mine[0]
     table = make_table(part * NY, y, width)
-    terms = encode_terms(receiver_terms, (mine_first,))
-    terms = join([terms, swap(terms, 1, 0, 0)])
-    terms = join([terms, swap(terms, 2, 0, 0)])
-    terms = join([terms, swap(terms, 4, 0, 0)], (table,))
-    terms = join([terms, swap(terms, 0, 1, 0)])
-    terms = join([terms, swap(terms, 0, 2, 0)])
-    far_terms = [swap(terms, 0, 0, 1)]
+    codes, coded = [], []
+    for t, inner, size in BACK:
+        coded.append(spectra(traces, y, starts[t] + inner, inner, size, got[t], table, width))
+        codes += [send_y(coded[-1][k], k) if k else coded[-1][k] for k in range(NY)]
 
     def ordered(v):
         v = v.reshape(NY, share)
@@ -322,37 +319,35 @@
 
     near = receiver_index // block
     rz, rx, rc = near // (NX * NC), near // NC % NX, near % NC
-    place = ((rc ^ c) * NX + (rx ^ x)) * NZ + (rz ^ z)
+    turn = rz ^ z
+    place = (((rc ^ c) * NX + (rx ^ x)) * 2 + (turn & 1)) * (NZ // 2) + turn // 2
     rec_at = ordered(place * block + receiver_index % block)
     shot_at = ordered(shot_index - (owner - 1) * block)
     live = live_counts[0] - jnp.stack([(y - k) % NY * share + at for at in first for k in range(NY)])
 
-    shot_terms = join([shot_terms], got[0])
+    terms = encode_terms(receiver_terms, (mine_first,))
+    terms = join([terms, swap(terms, 2, 0, 0)])
+    terms = join([terms, swap(terms, 4, 0, 0)])
+    terms = join([terms, swap(terms, 1, 0, 0)], (table,))
+    shot_terms = join([shot_terms], (terms,))
     shot_near = jnp.concatenate([neighbour(shot_terms, 1), shot_terms, neighbour(shot_terms, -1)])
-
-    model = gather_terms([terms] + far_terms, shot_near, rec_at, shot_at)
-
-    codes = []
-    for t, inner, size in BACK:
-        after = (model,) if t else ()
-        outs = spectra(traces, y, starts[t] + inner, inner, size, got[t], table, width, after)
-        codes += [send_y(outs[k], k) if k else outs[k] for k in range(NY)]
-
-    sums = sum_receivers(codes, model, live, rec_at, block * NZ * NX * NC)
-    half = sums.shape[0] // 2
-    sums = sums[:half] + swap(sums[half:], 0, 0, 1)
-    sums = sums.reshape(NX, NZ * block, width)
+    terms = join([terms, swap(terms, 0, 1, 0)], got[0] + [shot_near, rec_at, shot_at])
+    terms = join([terms, swap(terms, 0, 2, 0)], [coded[1][0]] + codes[1:NY])
+    far_terms = [swap(terms, 0, 0, 1)]
+
+    model = gather_terms([terms] + far_terms, shot_near, rec_at, shot_at, (coded[-1][0],))
+    sums, far_sums = sum_receivers(codes, model, live, rec_at, block * NZ * NX * NC)
+    sums = (sums + swap(far_sums, 0, 0, 1)).reshape(NX, 2, NZ // 2, block, width)
+    shots = sum_shots(codes, model, live, shot_at, 3 * block)
     sent = (sums * SUM_SCALE).astype(jnp.float16)
     come = [swap(sent[k], 0, k, 0).astype(jnp.float32) for k in (1, 3, 2)]
-    shots = sum_shots(codes, model, live, shot_at, 3 * block)
+    sums = sums[0] + (come[0] + come[1] + come[2]) * (1.0 / SUM_SCALE)
+    shots = join([shots], (sums,))
     shot_sums = shots[block : 2 * block] + neighbour(shots[2 * block :], 1) + neighbour(shots[:block], -1)
-    sums = join([sums[0]], (shot_sums,)) + (come[0] + come[1] + come[2]) * (1.0 / SUM_SCALE)
-    sums = sums.reshape(2, NZ // 2 * block, width)
     sent = (sums[1] * SUM_SCALE).astype(jnp.float16)
-    sums = sums[0] + swap(sent, 4, 0, 0).astype(jnp.float32) * (1.0 / SUM_SCALE)
-    sums = sums.reshape(NZ // 2, block, width)
+    sums = sums[0] + swap(sent, 1, 0, 0).astype(jnp.float32) * (1.0 / SUM_SCALE)
     sent = (sums * SUM_SCALE).astype(jnp.float16)
-    come = [swap(sent[k], k, 0, 0).astype(jnp.float32) for k in (1, 3, 2)]
+    come = [swap(sent[k], 2 * k, 0, 0).astype(jnp.float32) for k in (1, 3, 2)]
     receiver_sums = sums[0] + (come[0] + come[1] + come[2]) * (1.0 / SUM_SCALE)
     return (shot_sums, receiver_sums)
 

time: 186 us -> 169 us (0.909)
  waiting for transfers between devices: 48.1 us -> 34.4 us
  local copies, waits for them, and re-layouts: 11.3 us -> 9.43 us
    ppermute x14, waiting for transfers between devices: 36.4 us -> 18.3 us  [swap(): lax.ppermute(value, 'tr', [(tr_of(z, x, c), tr_of(z ^ dz, x ^ dx, c ^ dc)...]
    ppermute x12 -> x9, starting transfers between devices: 17.5 us -> 14.3 us  [send_y(): return lax.ppermute(value, 'fq', [(i, (i + k) % NY) for i in range(NY)])]
    slice x3 -> x1, local copies, waits for them, and re-layouts: 3.09 us -> 0.03 us  [per_device(): sums = sums[0] + (come[0] + come[1] + come[2]) * (1.0 / SUM_SCALE)]
    ppermute x14, starting transfers between devices: 30.3 us -> 32.8 us  [swap(): lax.ppermute(value, 'tr', [(tr_of(z, x, c), tr_of(z ^ dz, x ^ dx, c ^ dc)...]
    ppermute x12 -> x9, waiting for transfers between devices: 11.7 us -> 14 us  [send_y(): return lax.ppermute(value, 'fq', [(i, (i + k) % NY) for i in range(NY)])]
    ppermute x4, waiting for transfers between devices: 0.01 us -> 2.09 us  [neighbour(): lax.ppermute(value, 'tr', [(i, i + by) for i in range(size) if 0 <= i + b...]
    unnamed x56 -> x50, local copies, waits for them, and re-layouts: 6.24 us -> 8.23 us
  transfers between devices with their start and end apart: 30 -> 27, of which waited for: 11 -> 12; matrix products, arithmetic and copies ran while one was open for 3% -> 2% of each run, Pallas kernels for 23% -> 24%
where the time goes in v4:
time: 169 us; the launch traced here: 168 us
  Pallas kernels  62 us (37%)
  starting transfers between devices  54.9 us (32%)
  waiting for transfers between devices  34.4 us (20%)
  local copies, waits for them, and re-layouts  9.43 us (6%)
  other arithmetic  5.78 us (3%)
  between operations  1.76 us (1%)
    ppermute x14, starting transfers between devices, swap(): lax.ppermute(value, 'tr', [(tr_of(z, x, c), tr_of(z ^ dz, x ^ dx, c ^ dc)...  32.8 us
    ppermute x14, waiting for transfers between devices, swap(): lax.ppermute(value, 'tr', [(tr_of(z, x, c), tr_of(z ^ dz, x ^ dx, c ^ dc)...  18.3 us
    pallas_call x1, Pallas kernels, sum_receivers(): pl.pallas_call(body, in_specs=[sm, sm] + [vm] * (1 + parts), out_specs=[v...  16.6 us
    pallas_call x1, Pallas kernels, gather_terms(): pl.pallas_call(body, in_specs=[sm, sm, vm] + [vm] * parts + [pl.BlockSpec...  16.5 us
    ppermute x9, starting transfers between devices, send_y(): return lax.ppermute(value, 'fq', [(i, (i + k) % NY) for i in range(NY)])  14.3 us
    ppermute x9, waiting for transfers between devices, send_y(): return lax.ppermute(value, 'fq', [(i, (i + k) % NY) for i in range(NY)])  14 us
    pallas_call x2, Pallas kernels, spectra(): pl.pallas_call(body, grid_spec=pltpu.PrefetchScalarGridSpec(num_scalar_pr...  12.9 us
    unnamed x50, local copies, waits for them, and re-layouts  8.23 us
  transfers between devices with their start and end apart: 27, of which 12 were waited for; matrix products, arithmetic and copies ran while one was open for 2% of the time, Pallas kernels for 24%

profile of v4, /device:TPU:8, one launch (start us, length us, event | category | flops | bytes accessed | tf_op | source)
XLA Modules:
  0.0 168.2 jit_solution(17809944056840524845)
XLA Ops:
  0.6 2.2 %copy-done = bf16[8192,256]{1,0:T(8,128)(2,1)S(1)} copy-done((bf16[8192,256]{1,0:T(8,128)(2,1)S(1)}, bf16[8192,256]{1,0:T(8,128)(2,1)}, u32[]{:S(2)}) %copy-start) | copy-done | bytes 4194328
  2.8 3.4 %take_rows.1 = (bf16[2048,256]{1,0:T(8,128)(2,1)}, bf16[2048,256]{1,0:T(8,128)(2,1)}, bf16[2048,256]{1,0:T(8,128)(2,1)}) custom-call(s32[1]{0:T(128)} %bitcast.10.y_ref, bf16[8192,256]{1,0:T(8,128)(2,1)S(1)} %copy-done, bf16[8192,256]{1,0:T(8,128)(2,1)S(1)} %copy-done, bf16[8192,256]{1,0:T(8,128)(2,1)S(1)} %copy-done), custom_call_target="tpu_custom_call" | custom-call | flops 1000 | bytes 1000 | tf_op jit(solution)/shard_map/take_rows/pallas_call | solution.py:107
  6.2 1.6 collective-permute-start.6
  7.8 3.4 %collective-permute-start = (s16[128,128]{1,0:T(8,128)(2,1)S(1)}, s16[128,128]{1,0:T(8,128)(2,1)S(1)}, u32[]{:S(2)}, u32[]{:S(2)}) collective-permute-start(s16[128,128]{1,0:T(8,128)(2,1)S(1)} %encode_terms.1.refs_0_), channel_id=1, source_target_pairs={{0,64},{4,68},{8,72},{12,76},{16,80},{20,84},{24,88},{28,92},{32,9... | collective-permute-start | bytes 98312 | tf_op jit(solution)/shard_map/ppermute | solution.py:32
  11.2 0.9 collective-permute-start.7
  12.1 2.4 %collective-permute-start.8 = (bf16[2048,256]{1,0:T(8,128)(2,1)}, bf16[2048,256]{1,0:T(8,128)(2,1)}, u32[]{:S(2)}, u32[]{:S(2)}) collective-permute-start(bf16[2048,256]{1,0:T(8,128)(2,1)} %get-tuple-element.17), channel_id=1, source_target_pairs={{0,3},{1,0},{2,1},{3,2},{4,7},{5,4},{6,5},{7,6},{8,11},{9,8},{10,9... | collective-permute-start | bytes 3145736 | tf_op jit(solution)/shard_map/ppermute | solution.py:36
  15.6 5.5 %collective-permute-start.1 = (s16[256,128]{1,0:T(8,128)(2,1)S(1)}, s16[256,128]{1,0:T(8,128)(2,1)S(1)}, u32[]{:S(2)}, u32[]{:S(2)}) collective-permute-start(s16[256,128]{1,0:T(8,128)(2,1)S(1)} %join.7.refs_0_), channel_id=1, source_target_pairs={{0,128},{4,132},{8,136},{12,140},{16,144},{20,148},{24,152},{28,15... | collective-permute-start | bytes 196616 | tf_op jit(solution)/shard_map/ppermute | solution.py:32
  21.1 2.8 %collective-permute-done.1.refs_1_ = s16[256,128]{1,0:T(8,128)(2,1)S(1)} collective-permute-done((s16[256,128]{1,0:T(8,128)(2,1)S(1)}, s16[256,128]{1,0:T(8,128)(2,1)S(1)}, u32[]{:S(2)}, u32[]{:S(2)}) %collective-permute-start.1) | collective-permute-done | bytes 65568 | tf_op jit(solution)/shard_map/ppermute | solution.py:32
  23.9 2.6 %collective-permute-start.2 = (s16[512,128]{1,0:T(8,128)(2,1)S(1)}, s16[512,128]{1,0:T(8,128)(2,1)S(1)}, u32[]{:S(2)}, u32[]{:S(2)}) collective-permute-start(s16[512,128]{1,0:T(8,128)(2,1)S(1)} %join.8.refs_0_), channel_id=1, source_target_pairs={{0,32},{4,36},{8,40},{12,44},{16,48},{20,52},{24,56},{28,60},{32,0... | collective-permute-start | bytes 393224 | tf_op jit(solution)/shard_map/ppermute | solution.py:32
  26.5 5.3 %make_table.1.refs_2_.t = bf16[1024,1024]{1,0:T(8,128)(2,1)S(1)} custom-call(s32[1]{0:T(128)} %bitcast.10.y_ref), custom_call_target="tpu_custom_call" | custom-call | flops 1073741824 | bytes 33554432 | tf_op jit(solution)/shard_map/make_table/pallas_call | solution.py:63
  33.2 0.9 copy-done.14
  34.1 1.6 collective-permute-start.5
  35.7 0.8 copy-done.16
  36.6 1.3 collective-permute-start.4
  37.9 0.7 reshape.42
  38.6 1.2 collective-permute-done.4
  39.8 3.6 %collective-permute-start.3 = (f32[128,128]{1,0:T(8,128)S(1)}, f32[128,128]{1,0:T(8,128)S(1)}, u32[]{:S(2)}, u32[]{:S(2)}) collective-permute-start(f32[128,128]{1,0:T(8,128)S(1)} %join.10), channel_id=1, source_target_pairs={{0,4},{4,8},{8,12},{12,16},{16,20},{20,24},{24,28},{28,32},{32,36}... | collective-permute-start | bytes 196616 | tf_op jit(solution)/shard_map/ppermute | solution.py:289
  43.5 0.9 collective-permute-done.3
  44.3 0.9 pad_maximum_fusion.refs_5_.shot
  45.2 13.9 %collective-permute-done.8.refs_4_.b3 = bf16[2048,256]{1,0:T(8,128)(2,1)} collective-permute-done((bf16[2048,256]{1,0:T(8,128)(2,1)}, bf16[2048,256]{1,0:T(8,128)(2,1)}, u32[]{:S(2)}, u32[]{:S(2)}) %collective-permute-start.8) | collective-permute-done | bytes 1048608 | tf_op jit(solution)/shard_map/ppermute | solution.py:36
  59.1 0.8 copy-done.11
  59.8 1.1 join.11.refs_0_
  61.0 3.1 %collective-permute-start.9 = (s16[2048,128]{1,0:T(8,128)(2,1)S(1)}, s16[2048,128]{1,0:T(8,128)(2,1)S(1)}, u32[]{:S(2)}, u32[]{:S(2)}) collective-permute-start(s16[2048,128]{1,0:T(8,128)(2,1)S(1)} %join.11.refs_0_), channel_id=1, source_target_pairs={{0,16},{4,20},{8,24},{12,28},{16,0},{20,4},{24,8},{28,12},{32,48},... | collective-permute-start | bytes 1572872 | tf_op jit(solution)/shard_map/ppermute | solution.py:32
  64.1 5.5 %spectra.3 = (s16[768,128]{1,0:T(8,128)(2,1)}, s16[768,128]{1,0:T(8,128)(2,1)}, s16[768,128]{1,0:T(8,128)(2,1)}, s16[768,128]{1,0:T(8,128)(2,1)}) custom-call(s32[1]{0:T(128)} %bitcast.10.y_ref, bf16[8192,256]{1,0:T(8,128)(2,1)} %b0.3, bf16[2048,256]{1,0:T(8,128)(2,1)} %copy-done.2, bf16[2048,256]{1,0:T(8,128)(2,1)} %collective-permute-done.7.refs_3_.b2, ...), custom_call_target="tpu_custom_call" | custom-call | flops 1000 | bytes 1000 | tf_op jit(solution)/shard_map/spectra/pallas_call | solution.py:156
  69.6 1.4 collective-permute-start.10
  71.0 1.0 collective-permute-start.11
  72.0 2.0 %collective-permute-start.12 = (s16[768,128]{1,0:T(8,128)(2,1)}, s16[768,128]{1,0:T(8,128)(2,1)S(1)}, u32[]{:S(2)}, u32[]{:S(2)}) collective-permute-start(s16[768,128]{1,0:T(8,128)(2,1)} %get-tuple-element.21), channel_id=1, source_target_pairs={{0,3},{1,0},{2,1},{3,2},{4,7},{5,4},{6,5},{7,6},{8,11},{9,8},{10,9... | collective-permute-start | bytes 589832 | tf_op jit(solution)/shard_map/ppermute | solution.py:36
  74.0 7.4 %spectra.2 = (s16[1280,128]{1,0:T(8,128)(2,1)}, s16[1280,128]{1,0:T(8,128)(2,1)}, s16[1280,128]{1,0:T(8,128)(2,1)}, s16[1280,128]{1,0:T(8,128)(2,1)}) custom-call(s32[1]{0:T(128)} %bitcast.10.y_ref, bf16[8192,256]{1,0:T(8,128)(2,1)} %b0.3, bf16[2048,256]{1,0:T(8,128)(2,1)} %copy-done.2, bf16[2048,256]{1,0:T(8,128)(2,1)} %collective-permute-done.7.refs_3_.b2, ...), custom_call_target="tpu_custom_call" | custom-call | flops 1000 | bytes 1000 | tf_op jit(solution)/shard_map/spectra/pallas_call | solution.py:156
  81.5 1.1 copy-done.3
  83.6 3.1 %collective-permute-start.15 = (s16[1280,128]{1,0:T(8,128)(2,1)S(1)}, s16[1280,128]{1,0:T(8,128)(2,1)S(1)}, u32[]{:S(2)}, u32[]{:S(2)}) collective-permute-start(s16[1280,128]{1,0:T(8,128)(2,1)S(1)} %copy-done.23), channel_id=1, source_target_pairs={{0,2},{1,3},{2,0},{3,1},{4,6},{5,7},{6,4},{7,5},{8,10},{9,11},{10,... | collective-permute-start | bytes 983048 | tf_op jit(solution)/shard_map/ppermute | solution.py:36
  86.7 1.2 collective-permute-start.16
  89.2 16.5 %gather_terms.1.refs_2_ = f32[8192,128]{1,0:T(8,128)} custom-call(s32[8192]{0:T(1024)} %copy-done.12, s32[8192]{0:T(1024)} %copy-done.10, f32[384,128]{1,0:T(8,128)} %copy-done.8, s16[4096,128]{1,0:T(8,128)(2,1)} %copy-done.4, s16[4096,128]{1,0:T(8,128)(2,1)} %collective-permute-done.13.refs_1_, s16[1280,128]{1,0:T(8,128)(2,1)} %get-tuple-element.18.refs_2_.refs_7_), custom_call_target="tpu_custom_call" | custom-call | flops 1000 | bytes 1000 | tf_op jit(solution)/shard_map/gather_terms/pallas_call | solution.py:193
  106.7 16.6 %sum_receivers.1 = (f32[4096,128]{1,0:T(8,128)}, f32[4096,128]{1,0:T(8,128)}) custom-call(s32[8192]{0:T(1024)} %copy-done.12, s32[8]{0:T(128)} %broadcast_subtract_fusion.1.refs_1_, f32[8192,128]{1,0:T(8,128)} %gather_terms.1.refs_2_, s16[768,128]{1,0:T(8,128)(2,1)} %get-tuple-element.22.refs_3_, s16[768,128]{1,0:T(8,128)(2,1)} %copy-done.5, ...), custom_call_target="tpu_custom_call" | custom-call | flops 1000 | bytes 1000 | tf_op jit(solution)/shard_map/sum_receivers/pallas_call | solution.py:245
  123.4 4.4 %collective-permute-done.17 = f32[4096,128]{1,0:T(8,128)S(1)} collective-permute-done((f32[4096,128]{1,0:T(8,128)}, f32[4096,128]{1,0:T(8,128)S(1)}, u32[]{:S(2)}, u32[]{:S(2)}) %collective-permute-start.17) | collective-permute-done | bytes 2097184 | tf_op jit(solution)/shard_map/ppermute | solution.py:32
  127.7 2.0 %multiply_convert_fusion = (f16[4096,128]{1,0:T(8,128)(2,1)S(1)}, f32[4096,128]{1,0:T(8,128)S(1)}) fusion(f32[4096,128]{1,0:T(8,128)} %get-tuple-element.26, f32[4096,128]{1,0:T(8,128)S(1)} %collective-permute-done.17), kind=kLoop, calls=%fused_computation | loop fusion | flops 1572864 | bytes 7340032 | tf_op jit(solution)/shard_map/convert_element_type | solution.py:342
  130.5 1.5 collective-permute-start.18
  132.0 2.1 %collective-permute-start.19 = (f16[2,4,128,128]{3,2,1,0:T(8,128)(2,1)S(1)}, f16[2,4,128,128]{3,2,1,0:T(8,128)(2,1)S(1)}, u32[]{:S(2)}, u32[]{:S(2)}) collective-permute-start(f16[2,4,128,128]{3,2,1,0:T(8,128)(2,1)S(1)} %bitcast.35), channel_id=1, source_target_pairs={{0,24},{4,28},{8,16},{12,20},{16,8},{20,12},{24,0},{28,4},{32,56},... | collective-permute-start | bytes 786440 | tf_op jit(solution)/shard_map/ppermute | solution.py:32
  134.1 5.9 %sum_shots.1.refs_0_ = f32[384,128]{1,0:T(8,128)} custom-call(s32[1,8192]{1,0:T(1,128)} %bitcast.33, s32[8]{0:T(128)} %broadcast_subtract_fusion.1.refs_1_, f32[8192,128]{1,0:T(8,128)} %gather_terms.1.refs_2_, s16[768,128]{1,0:T(8,128)(2,1)} %get-tuple-element.22.refs_3_, s16[768,128]{1,0:T(8,128)(2,1)} %copy-done.5, s16[768,128]{1,0:T(8,128)(2,1)} %copy-done.6, ...), custom_call_target="tpu_custom_call" | custom-call | flops 1000 | bytes 1000 | tf_op jit(solution)/shard_map/sum_shots/pallas_call | solution.py:276
  140.7 3.3 %collective-permute-done.18 = f16[2,4,128,128]{3,2,1,0:T(8,128)(2,1)S(1)} collective-permute-done((f16[2,4,128,128]{3,2,1,0:T(8,128)(2,1)S(1)}, f16[2,4,128,128]{3,2,1,0:T(8,128)(2,1)S(1)}, u32[]{:S(2)}, u32[]{:S(2)}) %collective-permute-start.18) | collective-permute-done | bytes 262176 | tf_op jit(solution)/shard_map/ppermute | solution.py:32
  144.0 1.5 collective-permute-done.19
  145.7 2.0 %collective-permute-start.23 = (f16[4,128,128]{2,1,0:T(8,128)(2,1)S(1)}, f16[4,128,128]{2,1,0:T(8,128)(2,1)S(1)}, u32[]{:S(2)}, u32[]{:S(2)}) collective-permute-start(f16[4,128,128]{2,1,0:T(8,128)(2,1)S(1)} %fusion.2), channel_id=1, source_target_pairs={{0,32},{4,36},{8,40},{12,44},{16,48},{20,52},{24,56},{28,60},{32,0... | collective-permute-start | bytes 393224 | tf_op jit(solution)/shard_map/ppermute | solution.py:32
  147.7 1.6 collective-permute-start.21
  149.3 1.3 collective-permute-start.22
  150.6 0.7 collective-permute-done.23
  151.4 4.5 %collective-permute-start.24 = (f16[128,128]{1,0:T(8,128)(2,1)S(1)}, f16[128,128]{1,0:T(8,128)(2,1)S(1)}, u32[]{:S(2)}, u32[]{:S(2)}) collective-permute-start(f16[128,128]{1,0:T(8,128)(2,1)S(1)} %get-tuple-element.37), channel_id=1, source_target_pairs={{0,64},{4,68},{8,72},{12,76},{16,80},{20,84},{24,88},{28,92},{32,9... | collective-permute-start | bytes 98312 | tf_op jit(solution)/shard_map/ppermute | solution.py:32
  155.9 5.6 %collective-permute-start.26 = (f16[128,128]{1,0:T(8,128)(2,1)S(1)}, f16[128,128]{1,0:T(8,128)(2,1)S(1)}, u32[]{:S(2)}, u32[]{:S(2)}) collective-permute-start(f16[128,128]{1,0:T(8,128)(2,1)S(1)} %get-tuple-element.38), channel_id=1, source_target_pairs={{0,128},{4,132},{8,136},{12,140},{16,144},{20,148},{24,152},{28,15... | collective-permute-start | bytes 98312 | tf_op jit(solution)/shard_map/ppermute | solution.py:32
  162.5 1.6 collective-permute-done.26
  164.1 3.4 %collective-permute-done.25 = f16[128,128]{1,0:T(8,128)(2,1)S(1)} collective-permute-done((f16[128,128]{1,0:T(8,128)(2,1)S(1)}, f16[128,128]{1,0:T(8,128)(2,1)S(1)}, u32[]{:S(2)}, u32[]{:S(2)}) %collective-permute-start.25) | collective-permute-done | bytes 32800 | tf_op jit(solution)/shard_map/ppermute | solution.py:32
  (99 shorter events, 8.5 us)
Async XLA Ops:
  0.6 2.2 %copy-start = (bf16[8192,256]{1,0:T(8,128)(2,1)S(1)}, bf16[8192,256]{1,0:T(8,128)(2,1)}, u32[]{:S(2)}) copy-start(bf16[8192,256]{1,0:T(8,128)(2,1)} %b0.3) | copy-start | bytes 12582916
  2.8 5.0 %copy-start.15 = (f32[128,128]{1,0:T(8,128)S(1)}, f32[128,128]{1,0:T(8,128)}, u32[]{:S(2)}) copy-start(f32[128,128]{1,0:T(8,128)} %a.1) | copy-start | bytes 196612
  2.8 11.7 %copy-start.20 = (s32[8192]{0:T(1024)S(1)}, s32[8192]{0:T(1024)}, u32[]{:S(2)}) copy-start(s32[8192]{0:T(1024)} %param.8) | copy-start | bytes 98308
  2.8 11.9 %copy-start.21 = (s32[8192]{0:T(1024)S(1)}, s32[8192]{0:T(1024)}, u32[]{:S(2)}) copy-start(s32[8192]{0:T(1024)} %param.7) | copy-start | bytes 98308
  6.2 52.8 %collective-permute-start.6 = (bf16[2048,256]{1,0:T(8,128)(2,1)}, bf16[2048,256]{1,0:T(8,128)(2,1)S(1)}, u32[]{:S(2)}, u32[]{:S(2)}) collective-permute-start(bf16[2048,256]{1,0:T(8,128)(2,1)} %get-tuple-element.15.refs_0_), channel_id=1, source_target_pairs={{0,1},{1,2},{2,3},{3,0},{4,5},{5,6},{6,7},{7,4},{8,9},{9,10},{10,1... | collective-permute-start | bytes 3145736 | tf_op jit(solution)/shard_map/ppermute | solution.py:36
  7.8 7.7 %collective-permute-start = (s16[128,128]{1,0:T(8,128)(2,1)S(1)}, s16[128,128]{1,0:T(8,128)(2,1)S(1)}, u32[]{:S(2)}, u32[]{:S(2)}) collective-permute-start(s16[128,128]{1,0:T(8,128)(2,1)S(1)} %encode_terms.1.refs_0_), channel_id=1, source_target_pairs={{0,64},{4,68},{8,72},{12,76},{16,80},{20,84},{24,88},{28,92},{32,9... | collective-permute-start | bytes 98312 | tf_op jit(solution)/shard_map/ppermute | solution.py:32
  11.2 34.0 %collective-permute-start.7 = (bf16[2048,256]{1,0:T(8,128)(2,1)}, bf16[2048,256]{1,0:T(8,128)(2,1)}, u32[]{:S(2)}, u32[]{:S(2)}) collective-permute-start(bf16[2048,256]{1,0:T(8,128)(2,1)} %get-tuple-element.16), channel_id=1, source_target_pairs={{0,2},{1,3},{2,0},{3,1},{4,6},{5,7},{6,4},{7,5},{8,10},{9,11},{10,... | collective-permute-start | bytes 3145736 | tf_op jit(solution)/shard_map/ppermute | solution.py:36
  12.1 46.9 %collective-permute-start.8 = (bf16[2048,256]{1,0:T(8,128)(2,1)}, bf16[2048,256]{1,0:T(8,128)(2,1)}, u32[]{:S(2)}, u32[]{:S(2)}) collective-permute-start(bf16[2048,256]{1,0:T(8,128)(2,1)} %get-tuple-element.17), channel_id=1, source_target_pairs={{0,3},{1,0},{2,1},{3,2},{4,7},{5,4},{6,5},{7,6},{8,11},{9,8},{10,9... | collective-permute-start | bytes 3145736 | tf_op jit(solution)/shard_map/ppermute | solution.py:36
  15.6 8.3 %collective-permute-start.1 = (s16[256,128]{1,0:T(8,128)(2,1)S(1)}, s16[256,128]{1,0:T(8,128)(2,1)S(1)}, u32[]{:S(2)}, u32[]{:S(2)}) collective-permute-start(s16[256,128]{1,0:T(8,128)(2,1)S(1)} %join.7.refs_0_), channel_id=1, source_target_pairs={{0,128},{4,132},{8,136},{12,140},{16,144},{20,148},{24,152},{28,15... | collective-permute-start | bytes 196616 | tf_op jit(solution)/shard_map/ppermute | solution.py:32
  23.9 8.7 %collective-permute-start.2 = (s16[512,128]{1,0:T(8,128)(2,1)S(1)}, s16[512,128]{1,0:T(8,128)(2,1)S(1)}, u32[]{:S(2)}, u32[]{:S(2)}) collective-permute-start(s16[512,128]{1,0:T(8,128)(2,1)S(1)} %join.8.refs_0_), channel_id=1, source_target_pairs={{0,32},{4,36},{8,40},{12,44},{16,48},{20,52},{24,56},{28,60},{32,0... | collective-permute-start | bytes 393224 | tf_op jit(solution)/shard_map/ppermute | solution.py:32
  31.8 29.2 %copy-start.1 = (bf16[1024,1024]{1,0:T(8,128)(2,1)}, bf16[1024,1024]{1,0:T(8,128)(2,1)S(1)}, u32[]{:S(2)}) copy-start(bf16[1024,1024]{1,0:T(8,128)(2,1)S(1)} %make_table.1.refs_2_.t) | copy-start | bytes 6291460
  33.2 0.9 copy-start.14
  34.1 11.0 %collective-permute-start.5 = (s16[1024,128]{1,0:T(8,128)(2,1)S(1)}, s16[1024,128]{1,0:T(8,128)(2,1)}, u32[]{:S(2)}, u32[]{:S(2)}) collective-permute-start(s16[1024,128]{1,0:T(8,128)(2,1)S(1)} %join.9.refs_1_.refs_0_), channel_id=1, source_target_pairs={{0,8},{4,12},{8,0},{12,4},{16,24},{20,28},{24,16},{28,20},{32,40},... | collective-permute-start | bytes 786440 | tf_op jit(solution)/shard_map/ppermute | solution.py:32
  35.7 0.8 copy-start.16
  36.6 3.3 %collective-permute-start.4 = (f32[128,128]{1,0:T(8,128)S(1)}, f32[128,128]{1,0:T(8,128)}, u32[]{:S(2)}, u32[]{:S(2)}) collective-permute-start(f32[128,128]{1,0:T(8,128)S(1)} %join.10), channel_id=1, source_target_pairs={{4,0},{8,4},{12,8},{16,12},{20,16},{24,20},{28,24},{32,28},{36,32}... | collective-permute-start | bytes 196616 | tf_op jit(solution)/shard_map/ppermute | solution.py:289
  39.8 4.5 %collective-permute-start.3 = (f32[128,128]{1,0:T(8,128)S(1)}, f32[128,128]{1,0:T(8,128)S(1)}, u32[]{:S(2)}, u32[]{:S(2)}) collective-permute-start(f32[128,128]{1,0:T(8,128)S(1)} %join.10), channel_id=1, source_target_pairs={{0,4},{4,8},{8,12},{12,16},{16,20},{20,24},{24,28},{28,32},{32,36}... | collective-permute-start | bytes 196616 | tf_op jit(solution)/shard_map/ppermute | solution.py:289
  43.4 17.5 %copy-start.12 = (s32[8192]{0:T(1024)}, s32[8192]{0:T(1024)S(1)}, u32[]{:S(2)}) copy-start(s32[8192]{0:T(1024)S(1)} %constant_dynamic-update-slice_fusion.1.refs_6_.rec_at.refs_0_) | copy-start | bytes 98308
  45.2 15.8 %copy-start.8 = (f32[384,128]{1,0:T(8,128)}, f32[384,128]{1,0:T(8,128)S(1)}, u32[]{:S(2)}) copy-start(f32[384,128]{1,0:T(8,128)S(1)} %pad_maximum_fusion.refs_5_.shot) | copy-start | bytes 589828
  59.1 0.8 copy-start.11
  59.8 1.2 copy-start.2
  61.0 20.5 %collective-permute-start.9 = (s16[2048,128]{1,0:T(8,128)(2,1)S(1)}, s16[2048,128]{1,0:T(8,128)(2,1)S(1)}, u32[]{:S(2)}, u32[]{:S(2)}) collective-permute-start(s16[2048,128]{1,0:T(8,128)(2,1)S(1)} %join.11.refs_0_), channel_id=1, source_target_pairs={{0,16},{4,20},{8,24},{12,28},{16,0},{20,4},{24,8},{28,12},{32,48},... | collective-permute-start | bytes 1572872 | tf_op jit(solution)/shard_map/ppermute | solution.py:32
  69.6 11.8 %collective-permute-start.10 = (s16[768,128]{1,0:T(8,128)(2,1)}, s16[768,128]{1,0:T(8,128)(2,1)S(1)}, u32[]{:S(2)}, u32[]{:S(2)}) collective-permute-start(s16[768,128]{1,0:T(8,128)(2,1)} %get-tuple-element.19), channel_id=1, source_target_pairs={{0,1},{1,2},{2,3},{3,0},{4,5},{5,6},{6,7},{7,4},{8,9},{9,10},{10,1... | collective-permute-start | bytes 589832 | tf_op jit(solution)/shard_map/ppermute | solution.py:36
  71.0 10.5 %collective-permute-start.11 = (s16[768,128]{1,0:T(8,128)(2,1)}, s16[768,128]{1,0:T(8,128)(2,1)S(1)}, u32[]{:S(2)}, u32[]{:S(2)}) collective-permute-start(s16[768,128]{1,0:T(8,128)(2,1)} %get-tuple-element.20), channel_id=1, source_target_pairs={{0,2},{1,3},{2,0},{3,1},{4,6},{5,7},{6,4},{7,5},{8,10},{9,11},{10,... | collective-permute-start | bytes 589832 | tf_op jit(solution)/shard_map/ppermute | solution.py:36
  72.0 9.6 %collective-permute-start.12 = (s16[768,128]{1,0:T(8,128)(2,1)}, s16[768,128]{1,0:T(8,128)(2,1)S(1)}, u32[]{:S(2)}, u32[]{:S(2)}) collective-permute-start(s16[768,128]{1,0:T(8,128)(2,1)} %get-tuple-element.21), channel_id=1, source_target_pairs={{0,3},{1,0},{2,1},{3,2},{4,7},{5,4},{6,5},{7,6},{8,11},{9,8},{10,9... | collective-permute-start | bytes 589832 | tf_op jit(solution)/shard_map/ppermute | solution.py:36
  81.4 24.3 %copy-start.5 = (s16[768,128]{1,0:T(8,128)(2,1)}, s16[768,128]{1,0:T(8,128)(2,1)S(1)}, u32[]{:S(2)}) copy-start(s16[768,128]{1,0:T(8,128)(2,1)S(1)} %collective-permute-done.10.refs_3_.refs_4_) | copy-start | bytes 589828
  81.4 24.3 %copy-start.6 = (s16[768,128]{1,0:T(8,128)(2,1)}, s16[768,128]{1,0:T(8,128)(2,1)S(1)}, u32[]{:S(2)}) copy-start(s16[768,128]{1,0:T(8,128)(2,1)S(1)} %collective-permute-done.11.refs_4_.refs_5_) | copy-start | bytes 589828
  81.5 24.2 %copy-start.7 = (s16[768,128]{1,0:T(8,128)(2,1)}, s16[768,128]{1,0:T(8,128)(2,1)S(1)}, u32[]{:S(2)}) copy-start(s16[768,128]{1,0:T(8,128)(2,1)S(1)} %collective-permute-done.12.refs_5_.refs_6_) | copy-start | bytes 589828
  81.5 1.1 copy-start.3
  82.6 1.0 copy-start.23
  82.6 4.0 %copy-start.22 = (s16[1280,128]{1,0:T(8,128)(2,1)S(1)}, s16[1280,128]{1,0:T(8,128)(2,1)}, u32[]{:S(2)}) copy-start(s16[1280,128]{1,0:T(8,128)(2,1)} %get-tuple-element.25) | copy-start | bytes 983044
  82.7 6.5 %copy-start.4 = (s16[4096,128]{1,0:T(8,128)(2,1)}, s16[4096,128]{1,0:T(8,128)(2,1)S(1)}, u32[]{:S(2)}) copy-start(s16[4096,128]{1,0:T(8,128)(2,1)S(1)} %join.12.refs_0_) | copy-start | bytes 3145732
  82.7 6.5 %collective-permute-start.13 = (s16[4096,128]{1,0:T(8,128)(2,1)S(1)}, s16[4096,128]{1,0:T(8,128)(2,1)}, u32[]{:S(2)}, u32[]{:S(2)}) collective-permute-start(s16[4096,128]{1,0:T(8,128)(2,1)S(1)} %join.12.refs_0_), channel_id=1, source_target_pairs={{0,4},{4,0},{8,12},{12,8},{16,20},{20,16},{24,28},{28,24},{32,36},... | collective-permute-start | bytes 3145736 | tf_op jit(solution)/shard_map/ppermute | solution.py:32
  82.8 23.0 %collective-permute-start.14 = (s16[1280,128]{1,0:T(8,128)(2,1)}, s16[1280,128]{1,0:T(8,128)(2,1)S(1)}, u32[]{:S(2)}, u32[]{:S(2)}) collective-permute-start(s16[1280,128]{1,0:T(8,128)(2,1)} %get-tuple-element.23), channel_id=1, source_target_pairs={{0,1},{1,2},{2,3},{3,0},{4,5},{5,6},{6,7},{7,4},{8,9},{9,10},{10,1... | collective-permute-start | bytes 983048 | tf_op jit(solution)/shard_map/ppermute | solution.py:36
  83.6 22.2 %collective-permute-start.15 = (s16[1280,128]{1,0:T(8,128)(2,1)S(1)}, s16[1280,128]{1,0:T(8,128)(2,1)S(1)}, u32[]{:S(2)}, u32[]{:S(2)}) collective-permute-start(s16[1280,128]{1,0:T(8,128)(2,1)S(1)} %copy-done.23), channel_id=1, source_target_pairs={{0,2},{1,3},{2,0},{3,1},{4,6},{5,7},{6,4},{7,5},{8,10},{9,11},{10,... | collective-permute-start | bytes 983048 | tf_op jit(solution)/shard_map/ppermute | solution.py:36
  86.7 19.2 %collective-permute-start.16 = (s16[1280,128]{1,0:T(8,128)(2,1)S(1)}, s16[1280,128]{1,0:T(8,128)(2,1)S(1)}, u32[]{:S(2)}, u32[]{:S(2)}) collective-permute-start(s16[1280,128]{1,0:T(8,128)(2,1)S(1)} %copy-done.22), channel_id=1, source_target_pairs={{0,3},{1,0},{2,1},{3,2},{4,7},{5,4},{6,5},{7,6},{8,11},{9,8},{10,9... | collective-permute-start | bytes 983048 | tf_op jit(solution)/shard_map/ppermute | solution.py:36
  105.8 0.8 copy-start.18
  105.8 0.9 copy-start.19
  123.4 4.4 %collective-permute-start.17 = (f32[4096,128]{1,0:T(8,128)}, f32[4096,128]{1,0:T(8,128)S(1)}, u32[]{:S(2)}, u32[]{:S(2)}) collective-permute-start(f32[4096,128]{1,0:T(8,128)} %get-tuple-element.27), channel_id=1, source_target_pairs={{0,4},{4,0},{8,12},{12,8},{16,20},{20,16},{24,28},{28,24},{32,36},... | collective-permute-start | bytes 6291464 | tf_op jit(solution)/shard_map/ppermute | solution.py:32
  129.9 10.8 %collective-permute-start.20 = (f16[2,4,128,128]{3,2,1,0:T(8,128)(2,1)S(1)}, f16[2,4,128,128]{3,2,1,0:T(8,128)(2,1)S(1)}, u32[]{:S(2)}, u32[]{:S(2)}) collective-permute-start(f16[2,4,128,128]{3,2,1,0:T(8,128)(2,1)S(1)} %bitcast.37), channel_id=1, source_target_pairs={{0,16},{4,20},{8,24},{12,28},{16,0},{20,4},{24,8},{28,12},{32,48},... | collective-permute-start | bytes 786440 | tf_op jit(solution)/shard_map/ppermute | solution.py:32
  130.5 13.5 %collective-permute-start.18 = (f16[2,4,128,128]{3,2,1,0:T(8,128)(2,1)S(1)}, f16[2,4,128,128]{3,2,1,0:T(8,128)(2,1)S(1)}, u32[]{:S(2)}, u32[]{:S(2)}) collective-permute-start(f16[2,4,128,128]{3,2,1,0:T(8,128)(2,1)S(1)} %bitcast.36), channel_id=1, source_target_pairs={{0,8},{4,12},{8,0},{12,4},{16,24},{20,28},{24,16},{28,20},{32,40},... | collective-permute-start | bytes 786440 | tf_op jit(solution)/shard_map/ppermute | solution.py:32
  132.0 13.5 %collective-permute-start.19 = (f16[2,4,128,128]{3,2,1,0:T(8,128)(2,1)S(1)}, f16[2,4,128,128]{3,2,1,0:T(8,128)(2,1)S(1)}, u32[]{:S(2)}, u32[]{:S(2)}) collective-permute-start(f16[2,4,128,128]{3,2,1,0:T(8,128)(2,1)S(1)} %bitcast.35), channel_id=1, source_target_pairs={{0,24},{4,28},{8,16},{12,20},{16,8},{20,12},{24,0},{28,4},{32,56},... | collective-permute-start | bytes 786440 | tf_op jit(solution)/shard_map/ppermute | solution.py:32
  140.0 5.7 %copy-start.9 = (f32[384,128]{1,0:T(8,128)S(1)}, f32[384,128]{1,0:T(8,128)}, u32[]{:S(2)}) copy-start(f32[384,128]{1,0:T(8,128)} %sum_shots.1.refs_0_) | copy-start | bytes 589828
  145.7 5.7 %collective-permute-start.23 = (f16[4,128,128]{2,1,0:T(8,128)(2,1)S(1)}, f16[4,128,128]{2,1,0:T(8,128)(2,1)S(1)}, u32[]{:S(2)}, u32[]{:S(2)}) collective-permute-start(f16[4,128,128]{2,1,0:T(8,128)(2,1)S(1)} %fusion.2), channel_id=1, source_target_pairs={{0,32},{4,36},{8,40},{12,44},{16,48},{20,52},{24,56},{28,60},{32,0... | collective-permute-start | bytes 393224 | tf_op jit(solution)/shard_map/ppermute | solution.py:32
  147.7 14.2 %collective-permute-start.21 = (f32[128,128]{1,0:T(8,128)S(1)}, f32[128,128]{1,0:T(8,128)S(1)}, u32[]{:S(2)}, u32[]{:S(2)}) collective-permute-start(f32[128,128]{1,0:T(8,128)S(1)} %get-tuple-element.35), channel_id=1, source_target_pairs={{0,4},{4,8},{8,12},{12,16},{16,20},{20,24},{24,28},{28,32},{32,36}... | collective-permute-start | bytes 196616 | tf_op jit(solution)/shard_map/ppermute | solution.py:289
  149.3 12.5 %collective-permute-start.22 = (f32[128,128]{1,0:T(8,128)S(1)}, f32[128,128]{1,0:T(8,128)S(1)}, u32[]{:S(2)}, u32[]{:S(2)}) collective-permute-start(f32[128,128]{1,0:T(8,128)S(1)} %get-tuple-element.36), channel_id=1, source_target_pairs={{4,0},{8,4},{12,8},{16,12},{20,16},{24,20},{28,24},{32,28},{36,32}... | collective-permute-start | bytes 196616 | tf_op jit(solution)/shard_map/ppermute | solution.py:289
  151.4 11.0 %collective-permute-start.24 = (f16[128,128]{1,0:T(8,128)(2,1)S(1)}, f16[128,128]{1,0:T(8,128)(2,1)S(1)}, u32[]{:S(2)}, u32[]{:S(2)}) collective-permute-start(f16[128,128]{1,0:T(8,128)(2,1)S(1)} %get-tuple-element.37), channel_id=1, source_target_pairs={{0,64},{4,68},{8,72},{12,76},{16,80},{20,84},{24,88},{28,92},{32,9... | collective-permute-start | bytes 98312 | tf_op jit(solution)/shard_map/ppermute | solution.py:32
  155.9 8.2 %collective-permute-start.26 = (f16[128,128]{1,0:T(8,128)(2,1)S(1)}, f16[128,128]{1,0:T(8,128)(2,1)S(1)}, u32[]{:S(2)}, u32[]{:S(2)}) collective-permute-start(f16[128,128]{1,0:T(8,128)(2,1)S(1)} %get-tuple-element.38), channel_id=1, source_target_pairs={{0,128},{4,132},{8,136},{12,140},{16,144},{20,148},{24,152},{28,15... | collective-permute-start | bytes 98312 | tf_op jit(solution)/shard_map/ppermute | solution.py:32
  161.5 6.0 %collective-permute-start.25 = (f16[128,128]{1,0:T(8,128)(2,1)S(1)}, f16[128,128]{1,0:T(8,128)(2,1)S(1)}, u32[]{:S(2)}, u32[]{:S(2)}) collective-permute-start(f16[128,128]{1,0:T(8,128)(2,1)S(1)} %get-tuple-element.39), channel_id=1, source_target_pairs={{0,192},{4,196},{8,200},{12,204},{16,208},{20,212},{24,216},{28,22... | collective-permute-start | bytes 98312 | tf_op jit(solution)/shard_map/ppermute | solution.py:32
  (3 other events, 2.1 us)

commit v5 on v4

--- a/solution.py
+++ b/solution.py
@@ -14,7 +14,8 @@
 REC_SCALE = 65535.0 / (REC_HIGH - REC_LOW)
 SUM_SCALE = 1.0 / 32.0
 SENT = (2048,)
-BACK = ((0, 0, 768), (0, 768, 1280))
+BACK = ((0, 0, 1024), (0, 1024, 1024))
+LARGE = pltpu.CompilerParams(vmem_limit_bytes=60 * 2**20)
 SMALL = pltpu.CompilerParams(vmem_limit_bytes=12 * 2**20)
 COST = pl.CostEstimate(flops=1000, bytes_accessed=1000, transcendentals=0)
 VMEM = pltpu.CompilerParams(vmem_limit_bytes=56 * 2**20)
@@ -94,7 +95,7 @@
 
 def take_rows(traces, y, first, piece, after=()):
     rows, part = traces.shape
-    tile = 256
+    tile = 512
     share, start, steps = rows // NY // tile, first // tile, piece // tile
 
     def body(y_ref, *refs):
@@ -113,7 +114,7 @@
             out_specs=[pl.BlockSpec((tile, part), lambda i, y: (i, 0))] * 3,
         ),
         out_shape=[jax.ShapeDtypeStruct((piece, part), traces.dtype)] * 3,
-        compiler_params=SMALL,
+        compiler_params=LARGE,
         cost_estimate=COST,
         name="take_rows",
     )(y[None], traces, traces, traces, *after)
@@ -170,118 +171,113 @@
     )(y[None], traces, *blocks, table)
 
 
-def gather_terms(coded, shot_near, rec_at, shot_at, after):
-    rows, width = rec_at.shape[0], shot_near.shape[1]
-    parts = len(coded)
-    spans = spans_of(coded)
-
-    def body(rec_at, shot_at, shot, *refs):
-        out, rec = refs[parts + len(after) :]
-        for code, at in zip(refs, spans):
+def gather_shots(shot_near, shot_at, sizes):
+    width = shot_near.shape[1]
+    unroll = 64
+
+    def body(shot_at, shot, *outs):
+        for k, out in enumerate(outs):
+
+            def step(b, _, out=out, first=sum(sizes[:k])):
+                at = [b * unroll + u for u in range(unroll)]
+                row = [shot[pl.ds(shot_at[first + i], 1), :] for i in at]
+                for i, value in zip(at, row):
+                    out[pl.ds(i, 1), :] = value
+                return 0
+
+            lax.fori_loop(0, sizes[k] // unroll, step, 0)
+
+    vm, sm = pl.BlockSpec(memory_space=pltpu.VMEM), pl.BlockSpec(memory_space=pltpu.SMEM)
+    return pl.pallas_call(
+        body,
+        in_specs=[sm, vm],
+        out_specs=[vm] * len(sizes),
+        out_shape=[jax.ShapeDtypeStruct((size, width), jnp.float32) for size in sizes],
+        compiler_params=VMEM,
+        cost_estimate=COST,
+        name="gather_shots",
+    )(shot_at, shot_near)
+
+
+def sum_receivers(codes, shots, coded, live, rec_at, before):
+    rows, width = shots.shape
+    size, half = codes[0].shape[0], coded[0].shape[0]
+    banks, unroll = 4, 32
+    parts, held = len(codes), len(before)
+
+    def body(*refs):
+        rec_at, live, shots, own, other = refs[:5]
+        codes, before = refs[5 : 5 + parts], refs[5 + parts : 5 + parts + held]
+        near, far, res, rec = refs[5 + parts + held : 9 + parts + held]
+        sums = refs[9 + parts + held :]
+        halves = (pl.ds(0, half), pl.ds(half, half))
+        for code, at in zip((own, other), halves):
             rec[at, :] = (code[...].astype(jnp.float32) + 32768.0) * (1.0 / REC_SCALE) + REC_LOW
+        rec[pl.ds(2 * half, 8), :] = jnp.zeros((8, width), jnp.float32)
+        for k, s in enumerate(sums):
+            if k or not held:
+                s[...] = jnp.zeros_like(s)
+        for s, at in zip(before, halves):
+            sums[0][at, :] = s[...]
+        for k, code in enumerate(codes):
+            at = pl.ds(k * size, size)
+            logamp = (code[...].astype(jnp.float32) + 32768.0) * (1.0 / LA_SCALE)
+            alive = lax.broadcasted_iota(jnp.int32, code.shape, 0) < live[k]
+            res[at, :] = jnp.where(alive, logamp - shots[at, :], 0.0)
 
         def step(b, _):
-            at = [b * 32 + u for u in range(32)]
-            row = [rec[pl.ds(rec_at[i], 1), :] + shot[pl.ds(shot_at[i], 1), :] for i in at]
-            for i, value in zip(at, row):
-                out[pl.ds(i, 1), :] = value
+            for u in range(unroll):
+                s, row, at = sums[u % banks], pl.ds(b * unroll + u, 1), pl.ds(rec_at[b * unroll + u], 1)
+                value = res[row, :] - rec[at, :]
+                s[at, :] = s[at, :] + value
+                res[row, :] = value
             return 0
 
-        lax.fori_loop(0, rows // 32, step, 0)
+        lax.fori_loop(0, rows // unroll, step, 0)
+        for out, at in zip((near, far), halves):
+            out[...] = (sums[0][at, :] + sums[1][at, :]) + (sums[2][at, :] + sums[3][at, :])
 
     vm, sm = pl.BlockSpec(memory_space=pltpu.VMEM), pl.BlockSpec(memory_space=pltpu.SMEM)
-    return pl.pallas_call(
-        body,
-        in_specs=[sm, sm, vm] + [vm] * parts + [pl.BlockSpec(memory_space=pl.ANY)] * len(after),
-        out_specs=vm,
-        out_shape=jax.ShapeDtypeStruct((rows, width), jnp.float32),
-        scratch_shapes=[pltpu.VMEM((sum(code.shape[0] for code in coded), width), jnp.float32)],
+    sums = pltpu.VMEM((2 * half + 8, width), jnp.float32)
+    return pl.pallas_call(
+        body,
+        in_specs=[sm, sm] + [vm] * (3 + parts + held),
+        out_specs=[vm] * 3,
+        out_shape=[jax.ShapeDtypeStruct((n, width), jnp.float32) for n in (half, half, rows)],
+        scratch_shapes=[sums] * (1 + banks),
         compiler_params=VMEM,
         cost_estimate=COST,
-        name="gather_terms",
-    )(rec_at, shot_at, shot_near, *coded, *after)
-
-
-def residual(code, model, live):
-    logamp = (code.astype(jnp.float32) + 32768.0) * (1.0 / LA_SCALE)
-    alive = lax.broadcasted_iota(jnp.int32, code.shape, 0) < live
-    return jnp.where(alive, logamp - model, 0.0)
-
-
-def spans_of(codes):
-    sizes = [code.shape[0] for code in codes]
-    return [pl.ds(sum(sizes[:k]), size) for k, size in enumerate(sizes)]
-
-
-def sum_receivers(codes, model, live, rec_at, count):
-    rows, width = model.shape
-    parts = len(codes)
-    spans = spans_of(codes)
-    banks, group = 8, 32
-
-    def body(*refs):
-        rec_at, live, model = refs[:3]
-        codes = refs[3 : 3 + parts]
-        near, far, res = refs[3 + parts : 6 + parts]
-        sums = refs[6 + parts :]
-        for s in sums:
-            s[...] = jnp.zeros_like(s)
-        for k, (code, at) in enumerate(zip(codes, spans)):
-            res[at, :] = residual(code[...], model[at, :], live[k])
-
-        def step(b, _):
-            for u in range(group):
-                s, at = sums[u % banks], pl.ds(rec_at[b * group + u], 1)
-                s[at, :] = s[at, :] + res[pl.ds(b * group + u, 1), :]
-            return 0
-
-        lax.fori_loop(0, rows // group, step, 0)
-        for out, at in ((near, pl.ds(0, count // 2)), (far, pl.ds(count // 2, count // 2))):
-            out[...] = ((sums[0][at, :] + sums[1][at, :]) + (sums[2][at, :] + sums[3][at, :])) + (
-                (sums[4][at, :] + sums[5][at, :]) + (sums[6][at, :] + sums[7][at, :])
-            )
-
-    vm, sm = pl.BlockSpec(memory_space=pltpu.VMEM), pl.BlockSpec(memory_space=pltpu.SMEM)
-    return pl.pallas_call(
-        body,
-        in_specs=[sm, sm] + [vm] * (1 + parts),
-        out_specs=[vm, vm],
-        out_shape=[jax.ShapeDtypeStruct((count // 2, width), jnp.float32)] * 2,
-        scratch_shapes=[pltpu.VMEM((rows, width), jnp.float32)] + [pltpu.VMEM((count, width), jnp.float32)] * banks,
-        compiler_params=VMEM,
-        cost_estimate=COST,
         name="sum_receivers",
-    )(rec_at, live, model, *codes)
-
-
-def sum_shots(codes, model, live, shot_at, count):
-    rows, width = model.shape
-    parts = len(codes)
-    spans = spans_of(codes)
-
-    def body(*refs):
-        shot_at, live, model = refs[:3]
-        codes, out = refs[3 : 3 + parts], refs[3 + parts]
-        acc = jnp.zeros((count, 2 * width), jnp.float32)
-        for k, (code, at) in enumerate(zip(codes, spans)):
-            res = residual(code[...], model[at, :], live[k])
-            high = res.astype(jnp.bfloat16)
-            low = (res - high.astype(jnp.float32)).astype(jnp.bfloat16)
-            both = jnp.concatenate([high, low], axis=1)
-            hot = lax.broadcasted_iota(jnp.int32, (count, at.size), 0) == shot_at[:, at]
-            acc = acc + jnp.dot(hot.astype(jnp.bfloat16), both, preferred_element_type=jnp.float32)
-        out[...] = acc[:, :width] + acc[:, width:]
-
-    vm, sm = pl.BlockSpec(memory_space=pltpu.VMEM), pl.BlockSpec(memory_space=pltpu.SMEM)
-    return pl.pallas_call(
-        body,
-        in_specs=[vm, sm] + [vm] * (1 + parts),
+    )(rec_at, live, shots, *coded, *codes, *before)
+
+
+def sum_shots(residuals, shot_at, count):
+    width = residuals[0].shape[1]
+    tile = 1024
+
+    def body(shot_at, *refs):
+        acc, first = jnp.zeros((count, 2 * width), jnp.float32), 0
+        for res in refs[:-1]:
+            for k in range(0, res.shape[0], tile):
+                value = res[pl.ds(k, tile), :]
+                high = value.astype(jnp.bfloat16)
+                low = (value - high.astype(jnp.float32)).astype(jnp.bfloat16)
+                both = jnp.concatenate([high, low], axis=1)
+                hot = lax.broadcasted_iota(jnp.int32, (count, tile), 0) == shot_at[:, pl.ds(first + k, tile)]
+                acc = acc + jnp.dot(hot.astype(jnp.bfloat16), both, preferred_element_type=jnp.float32)
+            first += res.shape[0]
+        refs[-1][...] = acc[:, :width] + acc[:, width:]
+
+    vm = pl.BlockSpec(memory_space=pltpu.VMEM)
+    return pl.pallas_call(
+        body,
+        in_specs=[vm] * (1 + len(residuals)),
         out_specs=vm,
         out_shape=jax.ShapeDtypeStruct((count, width), jnp.float32),
         compiler_params=VMEM,
         cost_estimate=COST,
         name="sum_shots",
-    )(shot_at[None, :], live, model, *codes)
+    )(shot_at[None, :], *residuals)
 
 
 def neighbour(value, by):
@@ -321,7 +317,9 @@
     rz, rx, rc = near // (NX * NC), near // NC % NX, near % NC
     turn = rz ^ z
     place = (((rc ^ c) * NX + (rx ^ x)) * 2 + (turn & 1)) * (NZ // 2) + turn // 2
-    rec_at = ordered(place * block + receiver_index % block)
+    place = place * block + receiver_index % block
+    spare = block * NZ * NX * NC
+    rec_at = ordered(jnp.where(jnp.arange(rows, dtype=jnp.int32) < live_counts[0], place, spare))
     shot_at = ordered(shot_index - (owner - 1) * block)
     live = live_counts[0] - jnp.stack([(y - k) % NY * share + at for at in first for k in range(NY)])
 
@@ -331,24 +329,34 @@
     terms = join([terms, swap(terms, 1, 0, 0)], (table,))
     shot_terms = join([shot_terms], (terms,))
     shot_near = jnp.concatenate([neighbour(shot_terms, 1), shot_terms, neighbour(shot_terms, -1)])
-    terms = join([terms, swap(terms, 0, 1, 0)], got[0] + [shot_near, rec_at, shot_at])
+    shots = gather_shots(shot_near, shot_at, [size * NY for _, _, size in BACK])
+    terms = join([terms, swap(terms, 0, 1, 0)], got[0] + [shots[0], rec_at, coded[0][0]])
     terms = join([terms, swap(terms, 0, 2, 0)], [coded[1][0]] + codes[1:NY])
-    far_terms = [swap(terms, 0, 0, 1)]
-
-    model = gather_terms([terms] + far_terms, shot_near, rec_at, shot_at, (coded[-1][0],))
-    sums, far_sums = sum_receivers(codes, model, live, rec_at, block * NZ * NX * NC)
+    far_terms = swap(terms, 0, 0, 1)
+
+    sums, residuals, done = (), [], 0
+    for h, part_shots in enumerate(shots):
+        some = slice(h * NY, (h + 1) * NY)
+        at = rec_at[done : done + part_shots.shape[0]]
+        done += part_shots.shape[0]
+        *sums, resid = sum_receivers(codes[some], part_shots, [terms, far_terms], live[some], at, sums)
+        residuals.append(resid)
+    sums, far_sums = sums
     sums = (sums + swap(far_sums, 0, 0, 1)).reshape(NX, 2, NZ // 2, block, width)
-    shots = sum_shots(codes, model, live, shot_at, 3 * block)
+    shots = sum_shots(residuals, shot_at, 3 * block)
     sent = (sums * SUM_SCALE).astype(jnp.float16)
     come = [swap(sent[k], 0, k, 0).astype(jnp.float32) for k in (1, 3, 2)]
-    sums = sums[0] + (come[0] + come[1] + come[2]) * (1.0 / SUM_SCALE)
+    mine = join([sums[0].reshape(-1, width)], (shots,)).reshape(sums.shape[1:])
+    sums = mine + (come[0] + come[1] + come[2]) * (1.0 / SUM_SCALE)
     shots = join([shots], (sums,))
     shot_sums = shots[block : 2 * block] + neighbour(shots[2 * block :], 1) + neighbour(shots[:block], -1)
     sent = (sums[1] * SUM_SCALE).astype(jnp.float16)
     sums = sums[0] + swap(sent, 1, 0, 0).astype(jnp.float32) * (1.0 / SUM_SCALE)
-    sent = (sums * SUM_SCALE).astype(jnp.float16)
-    come = [swap(sent[k], 2 * k, 0, 0).astype(jnp.float32) for k in (1, 3, 2)]
-    receiver_sums = sums[0] + (come[0] + come[1] + come[2]) * (1.0 / SUM_SCALE)
+    sums = sums.reshape(2, 2, block, width)
+    sent = (sums[:, 1] * SUM_SCALE).astype(jnp.float16)
+    sums = sums[:, 0] + swap(sent, 2, 0, 0).astype(jnp.float32) * (1.0 / SUM_SCALE)
+    sent = (sums[1] * SUM_SCALE).astype(jnp.float16)
+    receiver_sums = sums[0] + swap(sent, 4, 0, 0).astype(jnp.float32) * (1.0 / SUM_SCALE)
     return (shot_sums, receiver_sums)
 
 

time: 169 us -> 176 us (1.041)
  Pallas kernels: 62 us -> 67.2 us
  local copies, waits for them, and re-layouts: 9.43 us -> 13.7 us
    pallas_call x3 -> x4, Pallas kernels: 39.1 us -> 44.8 us  [the longest x2 29.9 us: sum_receivers(): pl.pallas_call(body, in_specs=[sm, sm] + [vm] * (3 + parts + held), out_s...]
    unnamed x50 -> x71, local copies, waits for them, and re-layouts: 8.23 us -> 12.7 us
    ppermute x4, waiting for transfers between devices: 2.09 us -> 0.01 us  [neighbour(): lax.ppermute(value, 'tr', [(i, i + by) for i in range(size) if 0 <= i + b...]
    ppermute x14 -> x13, waiting for transfers between devices: 18.3 us -> 19.9 us  [swap(): lax.ppermute(value, 'tr', [(tr_of(z, x, c), tr_of(z ^ dz, x ^ dx, c ^ dc)...]
    ppermute x14 -> x13, starting transfers between devices: 32.8 us -> 33.6 us  [swap(): lax.ppermute(value, 'tr', [(tr_of(z, x, c), tr_of(z ^ dz, x ^ dx, c ^ dc)...]
  transfers between devices with their start and end apart: 27 -> 26, of which waited for: 12 -> 11; matrix products, arithmetic and copies ran while one was open for 2% -> 1% of each run, Pallas kernels for 24% -> 27%
where the time goes in v5:
time: 176 us; the launch traced here: 175 us
  Pallas kernels  67.2 us (38%)
  starting transfers between devices  54.9 us (31%)
  waiting for transfers between devices  33 us (19%)
  local copies, waits for them, and re-layouts  13.7 us (8%)
  other arithmetic  4.43 us (3%)
  between operations  1.81 us (1%)
    ppermute x13, starting transfers between devices, swap(): lax.ppermute(value, 'tr', [(tr_of(z, x, c), tr_of(z ^ dz, x ^ dx, c ^ dc)...  33.6 us
    pallas_call x2, Pallas kernels, sum_receivers(): pl.pallas_call(body, in_specs=[sm, sm] + [vm] * (3 + parts + held), out_s...  29.9 us
    ppermute x13, waiting for transfers between devices, swap(): lax.ppermute(value, 'tr', [(tr_of(z, x, c), tr_of(z ^ dz, x ^ dx, c ^ dc)...  19.9 us
    ppermute x9, starting transfers between devices, send_y(): return lax.ppermute(value, 'fq', [(i, (i + k) % NY) for i in range(NY)])  14.3 us
    ppermute x9, waiting for transfers between devices, send_y(): return lax.ppermute(value, 'fq', [(i, (i + k) % NY) for i in range(NY)])  13.1 us
    unnamed x71, local copies, waits for them, and re-layouts  12.7 us
    pallas_call x2, Pallas kernels, spectra(): pl.pallas_call(body, grid_spec=pltpu.PrefetchScalarGridSpec(num_scalar_pr...  12.6 us
    pallas_call x1, Pallas kernels, gather_shots(): pl.pallas_call(body, in_specs=[sm, vm], out_specs=[vm] * len(sizes), out_...  10.3 us
  transfers between devices with their start and end apart: 26, of which 11 were waited for; matrix products, arithmetic and copies ran while one was open for 1% of the time, Pallas kernels for 27%

profile of v5, /device:TPU:8, one launch (start us, length us, event | category | flops | bytes accessed | tf_op | source)
XLA Modules:
  0.0 175.0 jit_solution(753586969122325569)
XLA Ops:
  0.7 4.2 %take_rows.1 = (bf16[2048,256]{1,0:T(8,128)(2,1)}, bf16[2048,256]{1,0:T(8,128)(2,1)}, bf16[2048,256]{1,0:T(8,128)(2,1)}) custom-call(s32[1]{0:T(128)} %bitcast.10.y_ref, bf16[8192,256]{1,0:T(8,128)(2,1)} %b0.3, bf16[8192,256]{1,0:T(8,128)(2,1)} %b0.3, bf16[8192,256]{1,0:T(8,128)(2,1)} %b0.3), custom_call_target="tpu_custom_call" | custom-call | flops 1000 | bytes 1000 | tf_op jit(solution)/shard_map/take_rows/pallas_call | solution.py:108
  4.9 1.6 collective-permute-start.6
  6.5 1.3 copy-done.12
  7.8 3.4 %collective-permute-start = (s16[128,128]{1,0:T(8,128)(2,1)S(1)}, s16[128,128]{1,0:T(8,128)(2,1)S(1)}, u32[]{:S(2)}, u32[]{:S(2)}) collective-permute-start(s16[128,128]{1,0:T(8,128)(2,1)S(1)} %encode_terms.1.refs_0_), channel_id=1, source_target_pairs={{0,64},{4,68},{8,72},{12,76},{16,80},{20,84},{24,88},{28,92},{32,9... | collective-permute-start | bytes 98312 | tf_op jit(solution)/shard_map/ppermute | solution.py:33
  12.1 2.4 %collective-permute-start.8 = (bf16[2048,256]{1,0:T(8,128)(2,1)}, bf16[2048,256]{1,0:T(8,128)(2,1)S(1)}, u32[]{:S(2)}, u32[]{:S(2)}) collective-permute-start(bf16[2048,256]{1,0:T(8,128)(2,1)} %get-tuple-element.24), channel_id=1, source_target_pairs={{0,3},{1,0},{2,1},{3,2},{4,7},{5,4},{6,5},{7,6},{8,11},{9,8},{10,9... | collective-permute-start | bytes 3145736 | tf_op jit(solution)/shard_map/ppermute | solution.py:37
  15.5 5.5 %collective-permute-start.1 = (s16[256,128]{1,0:T(8,128)(2,1)S(1)}, s16[256,128]{1,0:T(8,128)(2,1)S(1)}, u32[]{:S(2)}, u32[]{:S(2)}) collective-permute-start(s16[256,128]{1,0:T(8,128)(2,1)S(1)} %join.8.refs_0_), channel_id=1, source_target_pairs={{0,128},{4,132},{8,136},{12,140},{16,144},{20,148},{24,152},{28,15... | collective-permute-start | bytes 196616 | tf_op jit(solution)/shard_map/ppermute | solution.py:33
  21.0 2.7 %collective-permute-done.1.refs_1_ = s16[256,128]{1,0:T(8,128)(2,1)S(1)} collective-permute-done((s16[256,128]{1,0:T(8,128)(2,1)S(1)}, s16[256,128]{1,0:T(8,128)(2,1)S(1)}, u32[]{:S(2)}, u32[]{:S(2)}) %collective-permute-start.1) | collective-permute-done | bytes 65568 | tf_op jit(solution)/shard_map/ppermute | solution.py:33
  23.8 2.6 %collective-permute-start.2 = (s16[512,128]{1,0:T(8,128)(2,1)S(1)}, s16[512,128]{1,0:T(8,128)(2,1)S(1)}, u32[]{:S(2)}, u32[]{:S(2)}) collective-permute-start(s16[512,128]{1,0:T(8,128)(2,1)S(1)} %join.9.refs_0_), channel_id=1, source_target_pairs={{0,32},{4,36},{8,40},{12,44},{16,48},{20,52},{24,56},{28,60},{32,0... | collective-permute-start | bytes 393224 | tf_op jit(solution)/shard_map/ppermute | solution.py:33
  26.4 5.3 %make_table.1.refs_2_.t = bf16[1024,1024]{1,0:T(8,128)(2,1)S(1)} custom-call(s32[1]{0:T(128)} %bitcast.10.y_ref), custom_call_target="tpu_custom_call" | custom-call | flops 1073741824 | bytes 33554432 | tf_op jit(solution)/shard_map/make_table/pallas_call | solution.py:64
  32.6 1.3 collective-permute-start.4
  33.9 3.0 %collective-permute-start.3 = (f32[128,128]{1,0:T(8,128)S(1)}, f32[128,128]{1,0:T(8,128)S(1)}, u32[]{:S(2)}, u32[]{:S(2)}) collective-permute-start(f32[128,128]{1,0:T(8,128)S(1)} %join.11), channel_id=1, source_target_pairs={{0,4},{4,8},{8,12},{12,16},{16,20},{20,24},{24,28},{28,32},{32,36}... | collective-permute-start | bytes 196616 | tf_op jit(solution)/shard_map/ppermute | solution.py:285
  37.0 1.6 collective-permute-start.5
  39.3 10.3 %gather_shots.1 = (f32[4096,128]{1,0:T(8,128)}, f32[4096,128]{1,0:T(8,128)}) custom-call(s32[8192]{0:T(1024)} %copy-done.23, f32[384,128]{1,0:T(8,128)} %pad_maximum_fusion.shot), custom_call_target="tpu_custom_call" | custom-call | flops 1000 | bytes 1000 | tf_op jit(solution)/shard_map/gather_shots/pallas_call | solution.py:191
  49.6 9.3 %collective-permute-done.8.b3.refs_4_ = bf16[2048,256]{1,0:T(8,128)(2,1)S(1)} collective-permute-done((bf16[2048,256]{1,0:T(8,128)(2,1)}, bf16[2048,256]{1,0:T(8,128)(2,1)S(1)}, u32[]{:S(2)}, u32[]{:S(2)}) %collective-permute-start.8) | collective-permute-done | bytes 1048608 | tf_op jit(solution)/shard_map/ppermute | solution.py:37
  58.9 1.0 copy-done.5
  59.9 1.0 copy-done.1
  60.9 6.3 %spectra.2 = (s16[1024,128]{1,0:T(8,128)(2,1)}, s16[1024,128]{1,0:T(8,128)(2,1)}, s16[1024,128]{1,0:T(8,128)(2,1)}, s16[1024,128]{1,0:T(8,128)(2,1)}) custom-call(s32[1]{0:T(128)} %bitcast.10.y_ref, bf16[8192,256]{1,0:T(8,128)(2,1)} %b0.3, bf16[2048,256]{1,0:T(8,128)(2,1)} %copy-done.1, bf16[2048,256]{1,0:T(8,128)(2,1)} %copy-done.3, ...), custom_call_target="tpu_custom_call" | custom-call | flops 1000 | bytes 1000 | tf_op jit(solution)/shard_map/spectra/pallas_call | solution.py:157
  67.2 1.2 copy-done.2
  68.4 1.2 copy-done.4
  69.7 1.2 copy-done.6
  70.9 0.9 copy-done.13
  71.9 3.1 %collective-permute-start.9 = (s16[2048,128]{1,0:T(8,128)(2,1)S(1)}, s16[2048,128]{1,0:T(8,128)(2,1)S(1)}, u32[]{:S(2)}, u32[]{:S(2)}) collective-permute-start(s16[2048,128]{1,0:T(8,128)(2,1)S(1)} %join.12.refs_0_), channel_id=1, source_target_pairs={{0,16},{4,20},{8,24},{12,28},{16,0},{20,4},{24,8},{28,12},{32,48},... | collective-permute-start | bytes 1572872 | tf_op jit(solution)/shard_map/ppermute | solution.py:33
  75.0 1.4 collective-permute-start.10
  76.4 1.0 collective-permute-start.11
  77.4 2.0 %collective-permute-start.12 = (s16[1024,128]{1,0:T(8,128)(2,1)S(1)}, s16[1024,128]{1,0:T(8,128)(2,1)S(1)}, u32[]{:S(2)}, u32[]{:S(2)}) collective-permute-start(s16[1024,128]{1,0:T(8,128)(2,1)S(1)} %copy-done.30), channel_id=1, source_target_pairs={{0,3},{1,0},{2,1},{3,2},{4,7},{5,4},{6,5},{7,6},{8,11},{9,8},{10,9... | collective-permute-start | bytes 786440 | tf_op jit(solution)/shard_map/ppermute | solution.py:37
  79.4 6.3 %spectra.3 = (s16[1024,128]{1,0:T(8,128)(2,1)}, s16[1024,128]{1,0:T(8,128)(2,1)}, s16[1024,128]{1,0:T(8,128)(2,1)}, s16[1024,128]{1,0:T(8,128)(2,1)}) custom-call(s32[1]{0:T(128)} %bitcast.10.y_ref, bf16[8192,256]{1,0:T(8,128)(2,1)} %b0.3, bf16[2048,256]{1,0:T(8,128)(2,1)} %copy-done.1, bf16[2048,256]{1,0:T(8,128)(2,1)} %copy-done.3, ...), custom_call_target="tpu_custom_call" | custom-call | flops 1000 | bytes 1000 | tf_op jit(solution)/shard_map/spectra/pallas_call | solution.py:157
  85.7 1.1 collective-permute-done.11.refs_4_.refs_7_
  86.8 2.7 %collective-permute-done.12.refs_5_.refs_8_ = s16[1024,128]{1,0:T(8,128)(2,1)S(1)} collective-permute-done((s16[1024,128]{1,0:T(8,128)(2,1)S(1)}, s16[1024,128]{1,0:T(8,128)(2,1)S(1)}, u32[]{:S(2)}, u32[]{:S(2)}) %collective-permute-start.12) | collective-permute-done | bytes 262176 | tf_op jit(solution)/shard_map/ppermute | solution.py:37
  89.6 1.0 copy-done.11
  91.6 2.9 %collective-permute-start.15 = (s16[1024,128]{1,0:T(8,128)(2,1)S(1)}, s16[1024,128]{1,0:T(8,128)(2,1)S(1)}, u32[]{:S(2)}, u32[]{:S(2)}) collective-permute-start(s16[1024,128]{1,0:T(8,128)(2,1)S(1)} %copy-done.29), channel_id=1, source_target_pairs={{0,2},{1,3},{2,0},{3,1},{4,6},{5,7},{6,4},{7,5},{8,10},{9,11},{10,... | collective-permute-start | bytes 786440 | tf_op jit(solution)/shard_map/ppermute | solution.py:37
  94.5 1.5 collective-permute-start.16
  97.5 14.3 %sum_receivers.2 = (f32[4096,128]{1,0:T(8,128)}, f32[4096,128]{1,0:T(8,128)}, f32[4096,128]{1,0:T(8,128)}) custom-call(s32[4096]{0:T(1024)} %bitcast.74, s32[4]{0:T(128)} %get-tuple-element.60.refs_1_, f32[4096,128]{1,0:T(8,128)} %get-tuple-element.22.refs_5_.refs_2_, s16[4096,128]{1,0:T(8,128)(2,1)} %copy-done.7, s16[4096,128]{1,0:T(8,128)(2,1)} %copy-done.19, ...), custom_call_target="tpu_custom_call" | custom-call | flops 1000 | bytes 1000 | tf_op jit(solution)/shard_map/sum_receivers/pallas_call | solution.py:242
  112.7 15.6 %sum_receivers.3 = (f32[4096,128]{1,0:T(8,128)}, f32[4096,128]{1,0:T(8,128)}, f32[4096,128]{1,0:T(8,128)}) custom-call(s32[4096]{0:T(1024)} %bitcast.72, s32[4]{0:T(128)} %get-tuple-element.59.refs_1_, f32[4096,128]{1,0:T(8,128)} %get-tuple-element.31.refs_2_, s16[4096,128]{1,0:T(8,128)(2,1)} %copy-done.7, s16[4096,128]{1,0:T(8,128)(2,1)} %copy-done.19, ...), custom_call_target="tpu_custom_call" | custom-call | flops 1000 | bytes 1000 | tf_op jit(solution)/shard_map/sum_receivers/pallas_call | solution.py:242
  128.3 4.4 %collective-permute-done.17 = f32[4096,128]{1,0:T(8,128)S(1)} collective-permute-done((f32[4096,128]{1,0:T(8,128)}, f32[4096,128]{1,0:T(8,128)S(1)}, u32[]{:S(2)}, u32[]{:S(2)}) %collective-permute-start.17) | collective-permute-done | bytes 2097184 | tf_op jit(solution)/shard_map/ppermute | solution.py:33
  132.7 2.0 %multiply_convert_fusion = (f16[4096,128]{1,0:T(8,128)(2,1)S(1)}, f32[4096,128]{1,0:T(8,128)S(1)}) fusion(f32[4096,128]{1,0:T(8,128)} %get-tuple-element.38, f32[4096,128]{1,0:T(8,128)S(1)} %collective-permute-done.17), kind=kLoop, calls=%fused_computation | loop fusion | flops 1572864 | bytes 7340032 | tf_op jit(solution)/shard_map/convert_element_type | solution.py:347
  135.3 1.9 %collective-permute-start.18 = (f16[2,4,128,128]{3,2,1,0:T(8,128)(2,1)S(1)}, f16[2,4,128,128]{3,2,1,0:T(8,128)(2,1)S(1)}, u32[]{:S(2)}, u32[]{:S(2)}) collective-permute-start(f16[2,4,128,128]{3,2,1,0:T(8,128)(2,1)S(1)} %bitcast.68), channel_id=1, source_target_pairs={{0,8},{4,12},{8,0},{12,4},{16,24},{20,28},{24,16},{28,20},{32,40},... | collective-permute-start | bytes 786440 | tf_op jit(solution)/shard_map/ppermute | solution.py:33
  137.2 1.8 %collective-permute-start.19 = (f16[2,4,128,128]{3,2,1,0:T(8,128)(2,1)S(1)}, f16[2,4,128,128]{3,2,1,0:T(8,128)(2,1)S(1)}, u32[]{:S(2)}, u32[]{:S(2)}) collective-permute-start(f16[2,4,128,128]{3,2,1,0:T(8,128)(2,1)S(1)} %bitcast.67), channel_id=1, source_target_pairs={{0,24},{4,28},{8,16},{12,20},{16,8},{20,12},{24,0},{28,4},{32,56},... | collective-permute-start | bytes 786440 | tf_op jit(solution)/shard_map/ppermute | solution.py:33
  139.0 4.7 %sum_shots.1.refs_1_.refs_0_ = f32[384,128]{1,0:T(8,128)} custom-call(s32[1,8192]{1,0:T(1,128)} %bitcast.70, f32[4096,128]{1,0:T(8,128)} %get-tuple-element.30.refs_0_, f32[4096,128]{1,0:T(8,128)} %get-tuple-element.37.refs_1_), custom_call_target="tpu_custom_call" | custom-call | flops 1000 | bytes 1000 | tf_op jit(solution)/shard_map/sum_shots/pallas_call | solution.py:272
  143.8 1.0 copy-done.9
  145.6 3.6 %collective-permute-done.18 = f16[2,4,128,128]{3,2,1,0:T(8,128)(2,1)S(1)} collective-permute-done((f16[2,4,128,128]{3,2,1,0:T(8,128)(2,1)S(1)}, f16[2,4,128,128]{3,2,1,0:T(8,128)(2,1)S(1)}, u32[]{:S(2)}, u32[]{:S(2)}) %collective-permute-start.18) | collective-permute-done | bytes 262176 | tf_op jit(solution)/shard_map/ppermute | solution.py:33
  149.2 1.2 collective-permute-done.19
  150.5 2.2 %collective-permute-start.23 = (f16[4,128,128]{2,1,0:T(8,128)(2,1)S(1)}, f16[4,128,128]{2,1,0:T(8,128)(2,1)S(1)}, u32[]{:S(2)}, u32[]{:S(2)}) collective-permute-start(f16[4,128,128]{2,1,0:T(8,128)(2,1)S(1)} %fusion.2), channel_id=1, source_target_pairs={{0,32},{4,36},{8,40},{12,44},{16,48},{20,52},{24,56},{28,60},{32,0... | collective-permute-start | bytes 393224 | tf_op jit(solution)/shard_map/ppermute | solution.py:33
  152.8 3.7 %collective-permute-done.23 = f16[4,128,128]{2,1,0:T(8,128)(2,1)S(1)} collective-permute-done((f16[4,128,128]{2,1,0:T(8,128)(2,1)S(1)}, f16[4,128,128]{2,1,0:T(8,128)(2,1)S(1)}, u32[]{:S(2)}, u32[]{:S(2)}) %collective-permute-start.23) | collective-permute-done | bytes 131104 | tf_op jit(solution)/shard_map/ppermute | solution.py:33
  157.0 1.3 collective-permute-start.21
  158.3 1.3 collective-permute-start.22
  159.6 2.3 %collective-permute-done.24 = f16[2,128,128]{2,1,0:T(8,128)(2,1)S(1)} collective-permute-done((f16[2,128,128]{2,1,0:T(8,128)(2,1)S(1)}, f16[2,128,128]{2,1,0:T(8,128)(2,1)S(1)}, u32[]{:S(2)}, u32[]{:S(2)}) %collective-permute-start.24) | collective-permute-done | bytes 65568 | tf_op jit(solution)/shard_map/ppermute | solution.py:33
  161.9 10.6 %collective-permute-start.25 = (f16[128,128]{1,0:T(8,128)(2,1)S(1)}, f16[128,128]{1,0:T(8,128)(2,1)S(1)}, u32[]{:S(2)}, u32[]{:S(2)}) collective-permute-start(f16[128,128]{1,0:T(8,128)(2,1)S(1)} %fusion.25), channel_id=1, source_target_pairs={{0,128},{4,132},{8,136},{12,140},{16,144},{20,148},{24,152},{28,15... | collective-permute-start | bytes 98312 | tf_op jit(solution)/shard_map/ppermute | solution.py:33
  173.1 1.2 collective-permute-done.25
  (117 shorter events, 10.0 us)
Async XLA Ops:
  0.6 5.8 %copy-start.17 = (f32[128,128]{1,0:T(8,128)S(1)}, f32[128,128]{1,0:T(8,128)}, u32[]{:S(2)}) copy-start(f32[128,128]{1,0:T(8,128)} %a.1) | copy-start | bytes 196612
  0.6 14.5 %copy-start.26 = (s32[8192]{0:T(1024)S(1)}, s32[8192]{0:T(1024)}, u32[]{:S(2)}) copy-start(s32[8192]{0:T(1024)} %param.8) | copy-start | bytes 98308
  0.7 14.6 %copy-start.27 = (s32[8192]{0:T(1024)S(1)}, s32[8192]{0:T(1024)}, u32[]{:S(2)}) copy-start(s32[8192]{0:T(1024)} %param.7) | copy-start | bytes 98308
  4.9 54.0 %collective-permute-start.6 = (bf16[2048,256]{1,0:T(8,128)(2,1)}, bf16[2048,256]{1,0:T(8,128)(2,1)S(1)}, u32[]{:S(2)}, u32[]{:S(2)}) collective-permute-start(bf16[2048,256]{1,0:T(8,128)(2,1)} %get-tuple-element.21.refs_0_), channel_id=1, source_target_pairs={{0,1},{1,2},{2,3},{3,0},{4,5},{5,6},{6,7},{7,4},{8,9},{9,10},{10,1... | collective-permute-start | bytes 3145736 | tf_op jit(solution)/shard_map/ppermute | solution.py:37
  6.5 1.3 copy-start.12
  7.8 7.7 %collective-permute-start = (s16[128,128]{1,0:T(8,128)(2,1)S(1)}, s16[128,128]{1,0:T(8,128)(2,1)S(1)}, u32[]{:S(2)}, u32[]{:S(2)}) collective-permute-start(s16[128,128]{1,0:T(8,128)(2,1)S(1)} %encode_terms.1.refs_0_), channel_id=1, source_target_pairs={{0,64},{4,68},{8,72},{12,76},{16,80},{20,84},{24,88},{28,92},{32,9... | collective-permute-start | bytes 98312 | tf_op jit(solution)/shard_map/ppermute | solution.py:33
  11.1 38.5 %collective-permute-start.7 = (bf16[2048,256]{1,0:T(8,128)(2,1)}, bf16[2048,256]{1,0:T(8,128)(2,1)S(1)}, u32[]{:S(2)}, u32[]{:S(2)}) collective-permute-start(bf16[2048,256]{1,0:T(8,128)(2,1)} %get-tuple-element.23), channel_id=1, source_target_pairs={{0,2},{1,3},{2,0},{3,1},{4,6},{5,7},{6,4},{7,5},{8,10},{9,11},{10,... | collective-permute-start | bytes 3145736 | tf_op jit(solution)/shard_map/ppermute | solution.py:37
  12.1 46.8 %collective-permute-start.8 = (bf16[2048,256]{1,0:T(8,128)(2,1)}, bf16[2048,256]{1,0:T(8,128)(2,1)S(1)}, u32[]{:S(2)}, u32[]{:S(2)}) collective-permute-start(bf16[2048,256]{1,0:T(8,128)(2,1)} %get-tuple-element.24), channel_id=1, source_target_pairs={{0,3},{1,0},{2,1},{3,2},{4,7},{5,4},{6,5},{7,6},{8,11},{9,8},{10,9... | collective-permute-start | bytes 3145736 | tf_op jit(solution)/shard_map/ppermute | solution.py:37
  15.5 8.3 %collective-permute-start.1 = (s16[256,128]{1,0:T(8,128)(2,1)S(1)}, s16[256,128]{1,0:T(8,128)(2,1)S(1)}, u32[]{:S(2)}, u32[]{:S(2)}) collective-permute-start(s16[256,128]{1,0:T(8,128)(2,1)S(1)} %join.8.refs_0_), channel_id=1, source_target_pairs={{0,128},{4,132},{8,136},{12,140},{16,144},{20,148},{24,152},{28,15... | collective-permute-start | bytes 196616 | tf_op jit(solution)/shard_map/ppermute | solution.py:33
  23.8 7.9 %collective-permute-start.2 = (s16[512,128]{1,0:T(8,128)(2,1)S(1)}, s16[512,128]{1,0:T(8,128)(2,1)S(1)}, u32[]{:S(2)}, u32[]{:S(2)}) collective-permute-start(s16[512,128]{1,0:T(8,128)(2,1)S(1)} %join.9.refs_0_), channel_id=1, source_target_pairs={{0,32},{4,36},{8,40},{12,44},{16,48},{20,52},{24,56},{28,60},{32,0... | collective-permute-start | bytes 393224 | tf_op jit(solution)/shard_map/ppermute | solution.py:33
  31.7 27.2 %copy-start = (bf16[1024,1024]{1,0:T(8,128)(2,1)}, bf16[1024,1024]{1,0:T(8,128)(2,1)S(1)}, u32[]{:S(2)}) copy-start(bf16[1024,1024]{1,0:T(8,128)(2,1)S(1)} %make_table.1.refs_2_.t) | copy-start | bytes 6291460
  32.6 4.3 %collective-permute-start.4 = (f32[128,128]{1,0:T(8,128)S(1)}, f32[128,128]{1,0:T(8,128)S(1)}, u32[]{:S(2)}, u32[]{:S(2)}) collective-permute-start(f32[128,128]{1,0:T(8,128)S(1)} %join.11), channel_id=1, source_target_pairs={{4,0},{8,4},{12,8},{16,12},{20,16},{24,20},{28,24},{32,28},{36,32}... | collective-permute-start | bytes 196616 | tf_op jit(solution)/shard_map/ppermute | solution.py:285
  33.9 4.7 %collective-permute-start.3 = (f32[128,128]{1,0:T(8,128)S(1)}, f32[128,128]{1,0:T(8,128)S(1)}, u32[]{:S(2)}, u32[]{:S(2)}) collective-permute-start(f32[128,128]{1,0:T(8,128)S(1)} %join.11), channel_id=1, source_target_pairs={{0,4},{4,8},{8,12},{12,16},{16,20},{20,24},{24,28},{28,32},{32,36}... | collective-permute-start | bytes 196616 | tf_op jit(solution)/shard_map/ppermute | solution.py:285
  37.0 30.2 %collective-permute-start.5 = (s16[1024,128]{1,0:T(8,128)(2,1)S(1)}, s16[1024,128]{1,0:T(8,128)(2,1)S(1)}, u32[]{:S(2)}, u32[]{:S(2)}) collective-permute-start(s16[1024,128]{1,0:T(8,128)(2,1)S(1)} %join.10.refs_1_.refs_0_), channel_id=1, source_target_pairs={{0,8},{4,12},{8,0},{12,4},{16,24},{20,28},{24,16},{28,20},{32,40},... | collective-permute-start | bytes 786440 | tf_op jit(solution)/shard_map/ppermute | solution.py:33
  38.5 28.6 %copy-start.24 = (s32[1,8,4,128]{3,1,2,0:T(8,128)}, s32[1,8,4,128]{3,1,2,0:T(8,128)S(1)}, u32[]{:S(2)}) copy-start(s32[1,8,4,128]{3,1,2,0:T(8,128)S(1)} %copy.20) | copy-start | bytes 49156
  38.6 28.6 %copy-start.25 = (s32[1,8,4,128]{3,1,2,0:T(8,128)}, s32[1,8,4,128]{3,1,2,0:T(8,128)S(1)}, u32[]{:S(2)}) copy-start(s32[1,8,4,128]{3,1,2,0:T(8,128)S(1)} %copy.21) | copy-start | bytes 49156
  49.6 17.6 %copy-start.8 = (f32[4096,128]{1,0:T(8,128)S(1)}, f32[4096,128]{1,0:T(8,128)}, u32[]{:S(2)}) copy-start(f32[4096,128]{1,0:T(8,128)} %get-tuple-element.22.refs_5_.refs_2_) | copy-start | bytes 6291460
  49.6 9.3 %copy-start.3 = (bf16[2048,256]{1,0:T(8,128)(2,1)}, bf16[2048,256]{1,0:T(8,128)(2,1)S(1)}, u32[]{:S(2)}) copy-start(bf16[2048,256]{1,0:T(8,128)(2,1)S(1)} %collective-permute-done.7.b2.refs_3_) | copy-start | bytes 3145732
  58.9 1.0 copy-start.5
  67.2 1.2 copy-start.2
  68.4 1.2 copy-start.4
  69.6 1.2 copy-start.6
  71.8 3.2 %copy-start.32 = (s16[1024,128]{1,0:T(8,128)(2,1)S(1)}, s16[1024,128]{1,0:T(8,128)(2,1)}, u32[]{:S(2)}) copy-start(s16[1024,128]{1,0:T(8,128)(2,1)} %get-tuple-element.27) | copy-start | bytes 786436
  71.8 4.6 %copy-start.31 = (s16[1024,128]{1,0:T(8,128)(2,1)S(1)}, s16[1024,128]{1,0:T(8,128)(2,1)}, u32[]{:S(2)}) copy-start(s16[1024,128]{1,0:T(8,128)(2,1)} %get-tuple-element.28) | copy-start | bytes 786436
  71.8 5.6 %copy-start.30 = (s16[1024,128]{1,0:T(8,128)(2,1)S(1)}, s16[1024,128]{1,0:T(8,128)(2,1)}, u32[]{:S(2)}) copy-start(s16[1024,128]{1,0:T(8,128)(2,1)} %get-tuple-element.29) | copy-start | bytes 786436
  71.9 17.7 %collective-permute-start.9 = (s16[2048,128]{1,0:T(8,128)(2,1)S(1)}, s16[2048,128]{1,0:T(8,128)(2,1)S(1)}, u32[]{:S(2)}, u32[]{:S(2)}) collective-permute-start(s16[2048,128]{1,0:T(8,128)(2,1)S(1)} %join.12.refs_0_), channel_id=1, source_target_pairs={{0,16},{4,20},{8,24},{12,28},{16,0},{20,4},{24,8},{28,12},{32,48},... | collective-permute-start | bytes 1572872 | tf_op jit(solution)/shard_map/ppermute | solution.py:33
  75.0 10.7 %collective-permute-start.10 = (s16[1024,128]{1,0:T(8,128)(2,1)S(1)}, s16[1024,128]{1,0:T(8,128)(2,1)S(1)}, u32[]{:S(2)}, u32[]{:S(2)}) collective-permute-start(s16[1024,128]{1,0:T(8,128)(2,1)S(1)} %copy-done.32), channel_id=1, source_target_pairs={{0,1},{1,2},{2,3},{3,0},{4,5},{5,6},{6,7},{7,4},{8,9},{9,10},{10,1... | collective-permute-start | bytes 786440 | tf_op jit(solution)/shard_map/ppermute | solution.py:37
  76.4 10.4 %collective-permute-start.11 = (s16[1024,128]{1,0:T(8,128)(2,1)S(1)}, s16[1024,128]{1,0:T(8,128)(2,1)S(1)}, u32[]{:S(2)}, u32[]{:S(2)}) collective-permute-start(s16[1024,128]{1,0:T(8,128)(2,1)S(1)} %copy-done.31), channel_id=1, source_target_pairs={{0,2},{1,3},{2,0},{3,1},{4,6},{5,7},{6,4},{7,5},{8,10},{9,11},{10,... | collective-permute-start | bytes 786440 | tf_op jit(solution)/shard_map/ppermute | solution.py:37
  77.4 12.2 %collective-permute-start.12 = (s16[1024,128]{1,0:T(8,128)(2,1)S(1)}, s16[1024,128]{1,0:T(8,128)(2,1)S(1)}, u32[]{:S(2)}, u32[]{:S(2)}) collective-permute-start(s16[1024,128]{1,0:T(8,128)(2,1)S(1)} %copy-done.30), channel_id=1, source_target_pairs={{0,3},{1,0},{2,1},{3,2},{4,7},{5,4},{6,5},{7,6},{8,11},{9,8},{10,9... | collective-permute-start | bytes 786440 | tf_op jit(solution)/shard_map/ppermute | solution.py:37
  85.7 10.8 %copy-start.14 = (s16[1024,128]{1,0:T(8,128)(2,1)}, s16[1024,128]{1,0:T(8,128)(2,1)S(1)}, u32[]{:S(2)}) copy-start(s16[1024,128]{1,0:T(8,128)(2,1)S(1)} %collective-permute-done.10.refs_3_.refs_6_) | copy-start | bytes 786436
  86.8 9.7 %copy-start.15 = (s16[1024,128]{1,0:T(8,128)(2,1)}, s16[1024,128]{1,0:T(8,128)(2,1)S(1)}, u32[]{:S(2)}) copy-start(s16[1024,128]{1,0:T(8,128)(2,1)S(1)} %collective-permute-done.11.refs_4_.refs_7_) | copy-start | bytes 786436
  89.6 7.0 %copy-start.16 = (s16[1024,128]{1,0:T(8,128)(2,1)}, s16[1024,128]{1,0:T(8,128)(2,1)S(1)}, u32[]{:S(2)}) copy-start(s16[1024,128]{1,0:T(8,128)(2,1)S(1)} %collective-permute-done.12.refs_5_.refs_8_) | copy-start | bytes 786436
  90.6 3.9 %copy-start.28 = (s16[1024,128]{1,0:T(8,128)(2,1)S(1)}, s16[1024,128]{1,0:T(8,128)(2,1)}, u32[]{:S(2)}) copy-start(s16[1024,128]{1,0:T(8,128)(2,1)} %get-tuple-element.34) | copy-start | bytes 786436
  90.7 5.9 %copy-start.7 = (s16[4096,128]{1,0:T(8,128)(2,1)}, s16[4096,128]{1,0:T(8,128)(2,1)S(1)}, u32[]{:S(2)}) copy-start(s16[4096,128]{1,0:T(8,128)(2,1)S(1)} %join.13.refs_3_) | copy-start | bytes 3145732
  90.7 5.9 %collective-permute-start.13 = (s16[4096,128]{1,0:T(8,128)(2,1)S(1)}, s16[4096,128]{1,0:T(8,128)(2,1)S(1)}, u32[]{:S(2)}, u32[]{:S(2)}) collective-permute-start(s16[4096,128]{1,0:T(8,128)(2,1)S(1)} %join.13.refs_3_), channel_id=1, source_target_pairs={{0,4},{4,0},{8,12},{12,8},{16,20},{20,16},{24,28},{28,24},{32,36},... | collective-permute-start | bytes 3145736 | tf_op jit(solution)/shard_map/ppermute | solution.py:33
  90.9 20.9 %collective-permute-start.14 = (s16[1024,128]{1,0:T(8,128)(2,1)}, s16[1024,128]{1,0:T(8,128)(2,1)S(1)}, u32[]{:S(2)}, u32[]{:S(2)}) collective-permute-start(s16[1024,128]{1,0:T(8,128)(2,1)} %get-tuple-element.32), channel_id=1, source_target_pairs={{0,1},{1,2},{2,3},{3,0},{4,5},{5,6},{6,7},{7,4},{8,9},{9,10},{10,1... | collective-permute-start | bytes 786440 | tf_op jit(solution)/shard_map/ppermute | solution.py:37
  91.6 20.2 %collective-permute-start.15 = (s16[1024,128]{1,0:T(8,128)(2,1)S(1)}, s16[1024,128]{1,0:T(8,128)(2,1)S(1)}, u32[]{:S(2)}, u32[]{:S(2)}) collective-permute-start(s16[1024,128]{1,0:T(8,128)(2,1)S(1)} %copy-done.29), channel_id=1, source_target_pairs={{0,2},{1,3},{2,0},{3,1},{4,6},{5,7},{6,4},{7,5},{8,10},{9,11},{10,... | collective-permute-start | bytes 786440 | tf_op jit(solution)/shard_map/ppermute | solution.py:37
  94.5 17.3 %collective-permute-start.16 = (s16[1024,128]{1,0:T(8,128)(2,1)S(1)}, s16[1024,128]{1,0:T(8,128)(2,1)S(1)}, u32[]{:S(2)}, u32[]{:S(2)}) collective-permute-start(s16[1024,128]{1,0:T(8,128)(2,1)S(1)} %copy-done.28), channel_id=1, source_target_pairs={{0,3},{1,0},{2,1},{3,2},{4,7},{5,4},{6,5},{7,6},{8,11},{9,8},{10,9... | collective-permute-start | bytes 786440 | tf_op jit(solution)/shard_map/ppermute | solution.py:37
  128.3 4.4 %collective-permute-start.17 = (f32[4096,128]{1,0:T(8,128)}, f32[4096,128]{1,0:T(8,128)S(1)}, u32[]{:S(2)}, u32[]{:S(2)}) collective-permute-start(f32[4096,128]{1,0:T(8,128)} %get-tuple-element.39), channel_id=1, source_target_pairs={{0,4},{4,0},{8,12},{12,8},{16,20},{20,16},{24,28},{28,24},{32,36},... | collective-permute-start | bytes 6291464 | tf_op jit(solution)/shard_map/ppermute | solution.py:33
  134.8 10.8 %collective-permute-start.20 = (f16[2,4,128,128]{3,2,1,0:T(8,128)(2,1)S(1)}, f16[2,4,128,128]{3,2,1,0:T(8,128)(2,1)S(1)}, u32[]{:S(2)}, u32[]{:S(2)}) collective-permute-start(f16[2,4,128,128]{3,2,1,0:T(8,128)(2,1)S(1)} %bitcast.69), channel_id=1, source_target_pairs={{0,16},{4,20},{8,24},{12,28},{16,0},{20,4},{24,8},{28,12},{32,48},... | collective-permute-start | bytes 786440 | tf_op jit(solution)/shard_map/ppermute | solution.py:33
  135.3 13.8 %collective-permute-start.18 = (f16[2,4,128,128]{3,2,1,0:T(8,128)(2,1)S(1)}, f16[2,4,128,128]{3,2,1,0:T(8,128)(2,1)S(1)}, u32[]{:S(2)}, u32[]{:S(2)}) collective-permute-start(f16[2,4,128,128]{3,2,1,0:T(8,128)(2,1)S(1)} %bitcast.68), channel_id=1, source_target_pairs={{0,8},{4,12},{8,0},{12,4},{16,24},{20,28},{24,16},{28,20},{32,40},... | collective-permute-start | bytes 786440 | tf_op jit(solution)/shard_map/ppermute | solution.py:33
  137.2 13.2 %collective-permute-start.19 = (f16[2,4,128,128]{3,2,1,0:T(8,128)(2,1)S(1)}, f16[2,4,128,128]{3,2,1,0:T(8,128)(2,1)S(1)}, u32[]{:S(2)}, u32[]{:S(2)}) collective-permute-start(f16[2,4,128,128]{3,2,1,0:T(8,128)(2,1)S(1)} %bitcast.67), channel_id=1, source_target_pairs={{0,24},{4,28},{8,16},{12,20},{16,8},{20,12},{24,0},{28,4},{32,56},... | collective-permute-start | bytes 786440 | tf_op jit(solution)/shard_map/ppermute | solution.py:33
  143.7 9.0 %copy-start.10 = (f32[384,128]{1,0:T(8,128)S(1)}, f32[384,128]{1,0:T(8,128)}, u32[]{:S(2)}) copy-start(f32[384,128]{1,0:T(8,128)} %sum_shots.1.refs_1_.refs_0_) | copy-start | bytes 589828
  150.5 5.9 %collective-permute-start.23 = (f16[4,128,128]{2,1,0:T(8,128)(2,1)S(1)}, f16[4,128,128]{2,1,0:T(8,128)(2,1)S(1)}, u32[]{:S(2)}, u32[]{:S(2)}) collective-permute-start(f16[4,128,128]{2,1,0:T(8,128)(2,1)S(1)} %fusion.2), channel_id=1, source_target_pairs={{0,32},{4,36},{8,40},{12,44},{16,48},{20,52},{24,56},{28,60},{32,0... | collective-permute-start | bytes 393224 | tf_op jit(solution)/shard_map/ppermute | solution.py:33
  156.5 5.3 %collective-permute-start.24 = (f16[2,128,128]{2,1,0:T(8,128)(2,1)S(1)}, f16[2,128,128]{2,1,0:T(8,128)(2,1)S(1)}, u32[]{:S(2)}, u32[]{:S(2)}) collective-permute-start(f16[2,128,128]{2,1,0:T(8,128)(2,1)S(1)} %fusion.6), channel_id=1, source_target_pairs={{0,64},{4,68},{8,72},{12,76},{16,80},{20,84},{24,88},{28,92},{32,9... | collective-permute-start | bytes 196616 | tf_op jit(solution)/shard_map/ppermute | solution.py:33
  157.0 15.5 %collective-permute-start.21 = (f32[128,128]{1,0:T(8,128)S(1)}, f32[128,128]{1,0:T(8,128)S(1)}, u32[]{:S(2)}, u32[]{:S(2)}) collective-permute-start(f32[128,128]{1,0:T(8,128)S(1)} %get-tuple-element.45), channel_id=1, source_target_pairs={{0,4},{4,8},{8,12},{12,16},{16,20},{20,24},{24,28},{28,32},{32,36}... | collective-permute-start | bytes 196616 | tf_op jit(solution)/shard_map/ppermute | solution.py:285
  158.3 14.2 %collective-permute-start.22 = (f32[128,128]{1,0:T(8,128)S(1)}, f32[128,128]{1,0:T(8,128)S(1)}, u32[]{:S(2)}, u32[]{:S(2)}) collective-permute-start(f32[128,128]{1,0:T(8,128)S(1)} %get-tuple-element.46), channel_id=1, source_target_pairs={{4,0},{8,4},{12,8},{16,12},{20,16},{24,20},{28,24},{32,28},{36,32}... | collective-permute-start | bytes 196616 | tf_op jit(solution)/shard_map/ppermute | solution.py:285
  161.9 12.5 %collective-permute-start.25 = (f16[128,128]{1,0:T(8,128)(2,1)S(1)}, f16[128,128]{1,0:T(8,128)(2,1)S(1)}, u32[]{:S(2)}, u32[]{:S(2)}) collective-permute-start(f16[128,128]{1,0:T(8,128)(2,1)S(1)} %fusion.25), channel_id=1, source_target_pairs={{0,128},{4,132},{8,136},{12,140},{16,144},{20,148},{24,152},{28,15... | collective-permute-start | bytes 98312 | tf_op jit(solution)/shard_map/ppermute | solution.py:33
  (11 other events, 9.9 us)

commit v6 on v5

--- a/solution.py
+++ b/solution.py
@@ -13,12 +13,12 @@
 REC_LOW, REC_HIGH = 1.0, 2.2
 REC_SCALE = 65535.0 / (REC_HIGH - REC_LOW)
 SUM_SCALE = 1.0 / 32.0
-SENT = (2048,)
-BACK = ((0, 0, 1024), (0, 1024, 1024))
+BACK = (768, 1280)
 LARGE = pltpu.CompilerParams(vmem_limit_bytes=60 * 2**20)
+SUMS = pltpu.CompilerParams(vmem_limit_bytes=44 * 2**20)
 SMALL = pltpu.CompilerParams(vmem_limit_bytes=12 * 2**20)
 COST = pl.CostEstimate(flops=1000, bytes_accessed=1000, transcendentals=0)
-VMEM = pltpu.CompilerParams(vmem_limit_bytes=56 * 2**20)
+MEDIUM = pltpu.CompilerParams(vmem_limit_bytes=18 * 2**20)
 
 
 def tr_of(z, x, c):
@@ -93,31 +93,27 @@
     )(*parts, *after)
 
 
-def take_rows(traces, y, first, piece, after=()):
+def take_rows(traces, y, k):
     rows, part = traces.shape
     tile = 512
-    share, start, steps = rows // NY // tile, first // tile, piece // tile
-
-    def body(y_ref, *refs):
-        for a, b in zip(refs[:3], refs[3 + len(after) :]):
-            b[...] = a[...]
-
-    def spot(k):
-        return pl.BlockSpec((tile, part), lambda i, y: ((y[0] + k) % NY * share + start + i, 0))
+    steps = rows // NY // tile
+
+    def body(y_ref, a, b):
+        b[...] = a[...]
 
     return pl.pallas_call(
         body,
         grid_spec=pltpu.PrefetchScalarGridSpec(
             num_scalar_prefetch=1,
             grid=(steps,),
-            in_specs=[spot(k) for k in range(1, NY)] + [pl.BlockSpec(memory_space=pl.ANY)] * len(after),
-            out_specs=[pl.BlockSpec((tile, part), lambda i, y: (i, 0))] * 3,
+            in_specs=[pl.BlockSpec((tile, part), lambda i, y: ((y[0] + k) % NY * steps + i, 0))],
+            out_specs=pl.BlockSpec((tile, part), lambda i, y: (i, 0)),
         ),
-        out_shape=[jax.ShapeDtypeStruct((piece, part), traces.dtype)] * 3,
+        out_shape=jax.ShapeDtypeStruct((rows // NY, part), traces.dtype),
         compiler_params=LARGE,
         cost_estimate=COST,
         name="take_rows",
-    )(y[None], traces, traces, traces, *after)
+    )(y[None], traces)
 
 
 def encode_terms(terms, after):
@@ -138,7 +134,7 @@
     )(terms, *after)
 
 
-def spectra(traces, y, first, inner, rows, blocks, table, width):
+def spectra(traces, y, first, rows, blocks, table, width):
     part, tile = traces.shape[1], 256
     share, start, steps = traces.shape[0] // NY // tile, first // tile, rows // tile
 
@@ -160,12 +156,12 @@
             num_scalar_prefetch=1,
             grid=(steps,),
             in_specs=[pl.BlockSpec((tile, part), lambda i, y: (y[0] * share + start + i, 0))]
-            + [pl.BlockSpec((tile, part), lambda i, y: (inner // tile + i, 0))] * 3
+            + [pl.BlockSpec((tile, part), lambda i, y: (start + i, 0))] * 3
             + [pl.BlockSpec(table.shape, lambda i, y: (0, 0))],
             out_specs=[pl.BlockSpec((tile, width), lambda i, y: (i, 0))] * 4,
         ),
         out_shape=[jax.ShapeDtypeStruct((rows, width), jnp.int16)] * 4,
-        compiler_params=VMEM,
+        compiler_params=MEDIUM,
         cost_estimate=COST,
         name="spectra",
     )(y[None], traces, *blocks, table)
@@ -193,7 +189,7 @@
         in_specs=[sm, vm],
         out_specs=[vm] * len(sizes),
         out_shape=[jax.ShapeDtypeStruct((size, width), jnp.float32) for size in sizes],
-        compiler_params=VMEM,
+        compiler_params=MEDIUM,
         cost_estimate=COST,
         name="gather_shots",
     )(shot_at, shot_near)
@@ -245,7 +241,7 @@
         out_specs=[vm] * 3,
         out_shape=[jax.ShapeDtypeStruct((n, width), jnp.float32) for n in (half, half, rows)],
         scratch_shapes=[sums] * (1 + banks),
-        compiler_params=VMEM,
+        compiler_params=SUMS,
         cost_estimate=COST,
         name="sum_receivers",
     )(rec_at, live, shots, *coded, *codes, *before)
@@ -274,7 +270,7 @@
         in_specs=[vm] * (1 + len(residuals)),
         out_specs=vm,
         out_shape=jax.ShapeDtypeStruct((count, width), jnp.float32),
-        compiler_params=VMEM,
+        compiler_params=MEDIUM,
         cost_estimate=COST,
         name="sum_shots",
     )(shot_at[None, :], *residuals)
@@ -289,29 +285,22 @@
     rows, part = traces.shape
     block, width = shot_terms.shape
     share = rows // NY
-    starts = [sum(SENT[:t]) for t in range(len(SENT))]
-    first = [starts[t] + inner for t, inner, _ in BACK]
+    first = [sum(BACK[:h]) for h in range(len(BACK))]
     owner, y = lax.axis_index("tr"), lax.axis_index("fq")
     z, x, c = owner // (NX * NC), owner // NC % NX, owner % NC
 
-    got, after = [], ()
-    for start, size in zip(starts, SENT):
-        mine = take_rows(traces, y, start, size, after)
-        come = {k: send_y(mine[k - 1], k) for k in (1, 3, 2)}
-        got.append([come[k] for k in range(1, NY)])
-        after = got[-1]
-        if start == 0:
-            mine_first = mine[0]
+    come = {k: send_y(take_rows(traces, y, k), k) for k in (1, 3, 2)}
+    got = [come[k] for k in range(1, NY)]
     table = make_table(part * NY, y, width)
     codes, coded = [], []
-    for t, inner, size in BACK:
-        coded.append(spectra(traces, y, starts[t] + inner, inner, size, got[t], table, width))
+    for at, size in zip(first, BACK):
+        coded.append(spectra(traces, y, at, size, got, table, width))
         codes += [send_y(coded[-1][k], k) if k else coded[-1][k] for k in range(NY)]
 
     def ordered(v):
         v = v.reshape(NY, share)
         v = jnp.stack([lax.dynamic_index_in_dim(v, (y - k) % NY, 0, keepdims=False) for k in range(NY)])
-        return jnp.concatenate([v[:, at : at + size].reshape(NY * size) for at, (_, _, size) in zip(first, BACK)])
+        return jnp.concatenate([v[:, at : at + size].reshape(NY * size) for at, size in zip(first, BACK)])
 
     near = receiver_index // block
     rz, rx, rc = near // (NX * NC), near // NC % NX, near % NC
@@ -323,14 +312,14 @@
     shot_at = ordered(shot_index - (owner - 1) * block)
     live = live_counts[0] - jnp.stack([(y - k) % NY * share + at for at in first for k in range(NY)])
 
-    terms = encode_terms(receiver_terms, (mine_first,))
+    terms = encode_terms(receiver_terms, (table,))
     terms = join([terms, swap(terms, 2, 0, 0)])
     terms = join([terms, swap(terms, 4, 0, 0)])
-    terms = join([terms, swap(terms, 1, 0, 0)], (table,))
+    terms = join([terms, swap(terms, 1, 0, 0)])
     shot_terms = join([shot_terms], (terms,))
     shot_near = jnp.concatenate([neighbour(shot_terms, 1), shot_terms, neighbour(shot_terms, -1)])
-    shots = gather_shots(shot_near, shot_at, [size * NY for _, _, size in BACK])
-    terms = join([terms, swap(terms, 0, 1, 0)], got[0] + [shots[0], rec_at, coded[0][0]])
+    shots = gather_shots(shot_near, shot_at, [size * NY for size in BACK])
+    terms = join([terms, swap(terms, 0, 1, 0)], got + [shots[0], rec_at, coded[0][0]])
     terms = join([terms, swap(terms, 0, 2, 0)], [coded[1][0]] + codes[1:NY])
     far_terms = swap(terms, 0, 0, 1)
 
@@ -348,10 +337,10 @@
     come = [swap(sent[k], 0, k, 0).astype(jnp.float32) for k in (1, 3, 2)]
     mine = join([sums[0].reshape(-1, width)], (shots,)).reshape(sums.shape[1:])
     sums = mine + (come[0] + come[1] + come[2]) * (1.0 / SUM_SCALE)
-    shots = join([shots], (sums,))
     shot_sums = shots[block : 2 * block] + neighbour(shots[2 * block :], 1) + neighbour(shots[:block], -1)
     sent = (sums[1] * SUM_SCALE).astype(jnp.float16)
-    sums = sums[0] + swap(sent, 1, 0, 0).astype(jnp.float32) * (1.0 / SUM_SCALE)
+    mine = join([sums[0].reshape(-1, width)], (shot_sums,)).reshape(sums.shape[1:])
+    sums = mine + swap(sent, 1, 0, 0).astype(jnp.float32) * (1.0 / SUM_SCALE)
     sums = sums.reshape(2, 2, block, width)
     sent = (sums[:, 1] * SUM_SCALE).astype(jnp.float16)
     sums = sums[:, 0] + swap(sent, 2, 0, 0).astype(jnp.float32) * (1.0 / SUM_SCALE)

time: 176 us -> 167 us (0.949)
  Pallas kernels: 67.2 us -> 59.6 us
  starting transfers between devices: 54.9 us -> 52.5 us
  local copies, waits for them, and re-layouts: 13.7 us -> 15.5 us
  waiting for transfers between devices: 33 us -> 31.2 us
    ppermute x9, waiting for transfers between devices: 13.1 us -> 4.37 us  [send_y(): return lax.ppermute(value, 'fq', [(i, (i + k) % NY) for i in range(NY)])]
    ppermute x13, waiting for transfers between devices: 19.9 us -> 26.8 us  [swap(): lax.ppermute(value, 'tr', [(tr_of(z, x, c), tr_of(z ^ dz, x ^ dx, c ^ dc)...]
    pallas_call x2, Pallas kernels: 29.9 us -> 23.9 us  [sum_receivers(): pl.pallas_call(body, in_specs=[sm, sm] + [vm] * (3 + parts + held), out_s...]
    pallas_call x1 -> x3, Pallas kernels: 4.22 us -> 10.1 us  [take_rows(): pl.pallas_call(body, grid_spec=pltpu.PrefetchScalarGridSpec(num_scalar_pr...]
    pallas_call x2, Pallas kernels: 12.6 us -> 9.13 us  [spectra(): pl.pallas_call(body, grid_spec=pltpu.PrefetchScalarGridSpec(num_scalar_pr...]
    pallas_call x1, Pallas kernels: 4.72 us -> 1.82 us  [sum_shots(): pl.pallas_call(body, in_specs=[vm] * (1 + len(residuals)), out_specs=vm,...]
    ppermute x13, starting transfers between devices: 33.6 us -> 31.1 us  [swap(): lax.ppermute(value, 'tr', [(tr_of(z, x, c), tr_of(z ^ dz, x ^ dx, c ^ dc)...]
    pallas_call x1, Pallas kernels: 10.3 us -> 8.1 us  [gather_shots(): pl.pallas_call(body, in_specs=[sm, vm], out_specs=[vm] * len(sizes), out_...]
  transfers between devices with their start and end apart: 26 -> 26, of which waited for: 11 -> 14; matrix products, arithmetic and copies ran while one was open for 1% -> 4% of each run, Pallas kernels for 27% -> 24%
where the time goes in v6:
time: 167 us; the launch traced here: 165 us
  Pallas kernels  59.6 us (36%)
  starting transfers between devices  52.5 us (31%)
  waiting for transfers between devices  31.2 us (19%)
  local copies, waits for them, and re-layouts  15.5 us (9%)
  other arithmetic  4.19 us (3%)
  between operations  1.85 us (1%)
    ppermute x13, starting transfers between devices, swap(): lax.ppermute(value, 'tr', [(tr_of(z, x, c), tr_of(z ^ dz, x ^ dx, c ^ dc)...  31.1 us
    ppermute x13, waiting for transfers between devices, swap(): lax.ppermute(value, 'tr', [(tr_of(z, x, c), tr_of(z ^ dz, x ^ dx, c ^ dc)...  26.8 us
    pallas_call x2, Pallas kernels, sum_receivers(): pl.pallas_call(body, in_specs=[sm, sm] + [vm] * (3 + parts + held), out_s...  23.9 us
    ppermute x9, starting transfers between devices, send_y(): return lax.ppermute(value, 'fq', [(i, (i + k) % NY) for i in range(NY)])  13.9 us
    unnamed x61, local copies, waits for them, and re-layouts  12.3 us
    pallas_call x3, Pallas kernels, take_rows(): pl.pallas_call(body, grid_spec=pltpu.PrefetchScalarGridSpec(num_scalar_pr...  10.1 us
    pallas_call x2, Pallas kernels, spectra(): pl.pallas_call(body, grid_spec=pltpu.PrefetchScalarGridSpec(num_scalar_pr...  9.13 us
    pallas_call x1, Pallas kernels, gather_shots(): pl.pallas_call(body, in_specs=[sm, vm], out_specs=[vm] * len(sizes), out_...  8.1 us
  transfers between devices with their start and end apart: 26, of which 14 were waited for; matrix products, arithmetic and copies ran while one was open for 4% of the time, Pallas kernels for 24%

profile of v6, /device:TPU:8, one launch (start us, length us, event | category | flops | bytes accessed | tf_op | source)
XLA Modules:
  0.0 164.9 jit_solution(2228886692601336110)
XLA Ops:
  0.6 3.4 %take_rows.3 = bf16[2048,256]{1,0:T(8,128)(2,1)} custom-call(s32[1]{0:T(128)} %bitcast.10.y_ref, bf16[8192,256]{1,0:T(8,128)(2,1)} %b0.3), custom_call_target="tpu_custom_call" | custom-call | flops 1000 | bytes 1000 | tf_op jit(solution)/shard_map/take_rows/pallas_call | solution.py:104
  4.0 1.6 collective-permute-start.6
  5.6 3.4 %take_rows.4 = bf16[2048,256]{1,0:T(8,128)(2,1)} custom-call(s32[1]{0:T(128)} %bitcast.10.y_ref, bf16[8192,256]{1,0:T(8,128)(2,1)} %b0.3), custom_call_target="tpu_custom_call" | custom-call | flops 1000 | bytes 1000 | tf_op jit(solution)/shard_map/take_rows/pallas_call | solution.py:104
  9.0 2.7 %collective-permute-start.7 = (bf16[2048,256]{1,0:T(8,128)(2,1)}, bf16[2048,256]{1,0:T(8,128)(2,1)}, u32[]{:S(2)}, u32[]{:S(2)}) collective-permute-start(bf16[2048,256]{1,0:T(8,128)(2,1)} %take_rows.4), channel_id=1, source_target_pairs={{0,2},{1,3},{2,0},{3,1},{4,6},{5,7},{6,4},{7,5},{8,10},{9,11},{10,... | collective-permute-start | bytes 3145736 | tf_op jit(solution)/shard_map/ppermute | solution.py:37
  11.7 3.3 %take_rows.5 = bf16[2048,256]{1,0:T(8,128)(2,1)} custom-call(s32[1]{0:T(128)} %bitcast.10.y_ref, bf16[8192,256]{1,0:T(8,128)(2,1)} %b0.3), custom_call_target="tpu_custom_call" | custom-call | flops 1000 | bytes 1000 | tf_op jit(solution)/shard_map/take_rows/pallas_call | solution.py:104
  15.7 5.3 %make_table.1.refs_0_.t = bf16[1024,1024]{1,0:T(8,128)(2,1)S(1)} custom-call(s32[1]{0:T(128)} %bitcast.10.y_ref), custom_call_target="tpu_custom_call" | custom-call | flops 1073741824 | bytes 33554432 | tf_op jit(solution)/shard_map/make_table/pallas_call | solution.py:64
  21.1 3.4 %collective-permute-start = (s16[128,128]{1,0:T(8,128)(2,1)S(1)}, s16[128,128]{1,0:T(8,128)(2,1)S(1)}, u32[]{:S(2)}, u32[]{:S(2)}) collective-permute-start(s16[128,128]{1,0:T(8,128)(2,1)S(1)} %encode_terms.1.refs_0_), channel_id=1, source_target_pairs={{0,64},{4,68},{8,72},{12,76},{16,80},{20,84},{24,88},{28,92},{32,9... | collective-permute-start | bytes 98312 | tf_op jit(solution)/shard_map/ppermute | solution.py:33
  26.4 6.8 %collective-permute-start.1 = (s16[256,128]{1,0:T(8,128)(2,1)S(1)}, s16[256,128]{1,0:T(8,128)(2,1)S(1)}, u32[]{:S(2)}, u32[]{:S(2)}) collective-permute-start(s16[256,128]{1,0:T(8,128)(2,1)S(1)} %join.8.refs_0_), channel_id=1, source_target_pairs={{0,128},{4,132},{8,136},{12,140},{16,144},{20,148},{24,152},{28,15... | collective-permute-start | bytes 196616 | tf_op jit(solution)/shard_map/ppermute | solution.py:33
  33.2 2.7 %collective-permute-done.1.refs_1_ = s16[256,128]{1,0:T(8,128)(2,1)S(1)} collective-permute-done((s16[256,128]{1,0:T(8,128)(2,1)S(1)}, s16[256,128]{1,0:T(8,128)(2,1)S(1)}, u32[]{:S(2)}, u32[]{:S(2)}) %collective-permute-start.1) | collective-permute-done | bytes 65568 | tf_op jit(solution)/shard_map/ppermute | solution.py:33
  35.9 1.1 collective-permute-start.2
  37.7 3.3 %collective-permute-done.2.refs_1_ = s16[512,128]{1,0:T(8,128)(2,1)S(1)} collective-permute-done((s16[512,128]{1,0:T(8,128)(2,1)S(1)}, s16[512,128]{1,0:T(8,128)(2,1)S(1)}, u32[]{:S(2)}, u32[]{:S(2)}) %collective-permute-start.2) | collective-permute-done | bytes 131104 | tf_op jit(solution)/shard_map/ppermute | solution.py:33
  41.6 0.9 copy-done.19
  43.4 1.3 collective-permute-start.4
  46.0 3.6 %collective-permute-start.3 = (f32[128,128]{1,0:T(8,128)S(1)}, f32[128,128]{1,0:T(8,128)}, u32[]{:S(2)}, u32[]{:S(2)}) collective-permute-start(f32[128,128]{1,0:T(8,128)S(1)} %join.11), channel_id=1, source_target_pairs={{0,4},{4,8},{8,12},{12,16},{16,20},{20,24},{24,28},{28,32},{32,36}... | collective-permute-start | bytes 196616 | tf_op jit(solution)/shard_map/ppermute | solution.py:281
  49.7 1.0 collective-permute-start.5
  50.7 1.3 pad_add_fusion.7
  53.4 0.9 pad_maximum_fusion.shot
  55.1 8.1 %gather_shots.1 = (f32[3072,128]{1,0:T(8,128)S(1)}, f32[5120,128]{1,0:T(8,128)S(1)}) custom-call(s32[8192]{0:T(1024)S(1)} %copy-done.16, f32[384,128]{1,0:T(8,128)S(1)} %pad_maximum_fusion.shot), custom_call_target="tpu_custom_call" | custom-call | flops 1000 | bytes 1000 | tf_op jit(solution)/shard_map/gather_shots/pallas_call | solution.py:187
  63.2 1.5 copy-done.4
  64.7 2.7 %copy-done = bf16[8192,256]{1,0:T(8,128)(2,1)S(1)} copy-done((bf16[8192,256]{1,0:T(8,128)(2,1)S(1)}, bf16[8192,256]{1,0:T(8,128)(2,1)}, u32[]{:S(2)}) %copy-start) | copy-done | bytes 4194328
  67.5 3.7 %spectra.2 = (s16[768,128]{1,0:T(8,128)(2,1)S(1)}, s16[768,128]{1,0:T(8,128)(2,1)S(1)}, s16[768,128]{1,0:T(8,128)(2,1)S(1)}, s16[768,128]{1,0:T(8,128)(2,1)S(1)}) custom-call(s32[1]{0:T(128)} %bitcast.10.y_ref, bf16[8192,256]{1,0:T(8,128)(2,1)S(1)} %copy-done, bf16[2048,256]{1,0:T(8,128)(2,1)S(1)} %collective-permute-done.6.b1.refs_2_, ...), custom_call_target="tpu_custom_call" | custom-call | flops 1000 | bytes 1000 | tf_op jit(solution)/shard_map/spectra/pallas_call | solution.py:153
  71.1 1.0 join.12.refs_0_
  72.2 2.8 %collective-permute-start.9 = (s16[2048,128]{1,0:T(8,128)(2,1)S(1)}, s16[2048,128]{1,0:T(8,128)(2,1)S(1)}, u32[]{:S(2)}, u32[]{:S(2)}) collective-permute-start(s16[2048,128]{1,0:T(8,128)(2,1)S(1)} %join.12.refs_0_), channel_id=1, source_target_pairs={{0,16},{4,20},{8,24},{12,28},{16,0},{20,4},{24,8},{28,12},{32,48},... | collective-permute-start | bytes 1572872 | tf_op jit(solution)/shard_map/ppermute | solution.py:33
  75.0 3.4 %collective-permute-start.11 = (s16[768,128]{1,0:T(8,128)(2,1)S(1)}, s16[768,128]{1,0:T(8,128)(2,1)S(1)}, u32[]{:S(2)}, u32[]{:S(2)}) collective-permute-start(s16[768,128]{1,0:T(8,128)(2,1)S(1)} %get-tuple-element.22), channel_id=1, source_target_pairs={{0,2},{1,3},{2,0},{3,1},{4,6},{5,7},{6,4},{7,5},{8,10},{9,11},{10,... | collective-permute-start | bytes 589832 | tf_op jit(solution)/shard_map/ppermute | solution.py:37
  78.5 5.5 %spectra.3 = (s16[1280,128]{1,0:T(8,128)(2,1)S(1)}, s16[1280,128]{1,0:T(8,128)(2,1)S(1)}, s16[1280,128]{1,0:T(8,128)(2,1)S(1)}, s16[1280,128]{1,0:T(8,128)(2,1)S(1)}) custom-call(s32[1]{0:T(128)} %bitcast.10.y_ref, bf16[8192,256]{1,0:T(8,128)(2,1)S(1)} %copy-done, bf16[2048,256]{1,0:T(8,128)(2,1)S(1)} %collective-permute-done.6.b1.refs_2_, ...), custom_call_target="tpu_custom_call" | custom-call | flops 1000 | bytes 1000 | tf_op jit(solution)/shard_map/spectra/pallas_call | solution.py:153
  84.3 3.7 %collective-permute-done.12.refs_5_.refs_8_ = s16[768,128]{1,0:T(8,128)(2,1)S(1)} collective-permute-done((s16[768,128]{1,0:T(8,128)(2,1)S(1)}, s16[768,128]{1,0:T(8,128)(2,1)S(1)}, u32[]{:S(2)}, u32[]{:S(2)}) %collective-permute-start.12) | collective-permute-done | bytes 196640 | tf_op jit(solution)/shard_map/ppermute | solution.py:37
  89.4 3.0 %collective-permute-start.15 = (s16[1280,128]{1,0:T(8,128)(2,1)}, s16[1280,128]{1,0:T(8,128)(2,1)S(1)}, u32[]{:S(2)}, u32[]{:S(2)}) collective-permute-start(s16[1280,128]{1,0:T(8,128)(2,1)} %copy-done.23), channel_id=1, source_target_pairs={{0,2},{1,3},{2,0},{3,1},{4,6},{5,7},{6,4},{7,5},{8,10},{9,11},{10,... | collective-permute-start | bytes 983048 | tf_op jit(solution)/shard_map/ppermute | solution.py:37
  92.4 2.0 %collective-permute-start.16 = (s16[1280,128]{1,0:T(8,128)(2,1)}, s16[1280,128]{1,0:T(8,128)(2,1)S(1)}, u32[]{:S(2)}, u32[]{:S(2)}) collective-permute-start(s16[1280,128]{1,0:T(8,128)(2,1)} %copy-done.22), channel_id=1, source_target_pairs={{0,3},{1,0},{2,1},{3,2},{4,7},{5,4},{6,5},{7,6},{8,11},{9,8},{10,9... | collective-permute-start | bytes 983048 | tf_op jit(solution)/shard_map/ppermute | solution.py:37
  94.5 0.9 copy-done.9
  95.4 0.9 copy-done.11
  96.3 0.9 copy-done.13
  97.2 9.0 %sum_receivers.2 = (f32[4096,128]{1,0:T(8,128)S(1)}, f32[4096,128]{1,0:T(8,128)S(1)}, f32[3072,128]{1,0:T(8,128)S(1)}) custom-call(s32[3072]{0:T(1024)S(1)} %reshape.56.refs_0_, s32[4]{0:T(128)S(1)} %get-tuple-element.52.refs_1_, f32[3072,128]{1,0:T(8,128)S(1)} %copy-done.2, s16[4096,128]{1,0:T(8,128)(2,1)S(1)} %join.13.refs_3_, ...), custom_call_target="tpu_custom_call" | custom-call | flops 1000 | bytes 1000 | tf_op jit(solution)/shard_map/sum_receivers/pallas_call | solution.py:238
  106.2 1.3 copy-done.5
  108.0 14.9 %sum_receivers.3 = (f32[4096,128]{1,0:T(8,128)S(1)}, f32[4096,128]{1,0:T(8,128)S(1)}, f32[5120,128]{1,0:T(8,128)}) custom-call(s32[5120]{0:T(1024)S(1)} %reshape.57.refs_0_, s32[4]{0:T(128)S(1)} %get-tuple-element.51.refs_1_, f32[5120,128]{1,0:T(8,128)} %copy-done.4, s16[4096,128]{1,0:T(8,128)(2,1)S(1)} %join.13.refs_3_, ...), custom_call_target="tpu_custom_call" | custom-call | flops 1000 | bytes 1000 | tf_op jit(solution)/shard_map/sum_receivers/pallas_call | solution.py:238
  122.9 4.2 %collective-permute-done.19 = f32[4096,128]{1,0:T(8,128)S(1)} collective-permute-done((f32[4096,128]{1,0:T(8,128)S(1)}, f32[4096,128]{1,0:T(8,128)S(1)}, u32[]{:S(2)}, u32[]{:S(2)}) %collective-permute-start.19) | collective-permute-done | bytes 2097184 | tf_op jit(solution)/shard_map/ppermute | solution.py:33
  127.5 2.5 %collective-permute-start.22 = (f16[2,4,128,128]{3,2,1,0:T(8,128)(2,1)S(1)}, f16[2,4,128,128]{3,2,1,0:T(8,128)(2,1)S(1)}, u32[]{:S(2)}, u32[]{:S(2)}) collective-permute-start(f16[2,4,128,128]{3,2,1,0:T(8,128)(2,1)S(1)} %bitcast.44), channel_id=1, source_target_pairs={{0,16},{4,20},{8,24},{12,28},{16,0},{20,4},{24,8},{28,12},{32,48},... | collective-permute-start | bytes 786440 | tf_op jit(solution)/shard_map/ppermute | solution.py:33
  130.5 1.2 collective-permute-start.21
  131.7 1.8 %sum_shots.1.refs_1_ = f32[384,128]{1,0:T(8,128)S(1)} custom-call(s32[1,8192]{1,0:T(1,128)S(1)} %bitcast.39, f32[3072,128]{1,0:T(8,128)S(1)} %get-tuple-element.24.refs_0_, f32[5120,128]{1,0:T(8,128)S(1)} %copy-done.3), custom_call_target="tpu_custom_call" | custom-call | flops 1000 | bytes 1000 | tf_op jit(solution)/shard_map/sum_shots/pallas_call | solution.py:268
  133.6 1.3 collective-permute-start.17
  134.9 1.3 collective-permute-start.18
  136.2 2.1 %collective-permute-done.22 = f16[2,4,128,128]{3,2,1,0:T(8,128)(2,1)S(1)} collective-permute-done((f16[2,4,128,128]{3,2,1,0:T(8,128)(2,1)S(1)}, f16[2,4,128,128]{3,2,1,0:T(8,128)(2,1)S(1)}, u32[]{:S(2)}, u32[]{:S(2)}) %collective-permute-start.22) | collective-permute-done | bytes 262176 | tf_op jit(solution)/shard_map/ppermute | solution.py:33
  138.3 4.2 %collective-permute-done.20 = f16[2,4,128,128]{3,2,1,0:T(8,128)(2,1)S(1)} collective-permute-done((f16[2,4,128,128]{3,2,1,0:T(8,128)(2,1)S(1)}, f16[2,4,128,128]{3,2,1,0:T(8,128)(2,1)S(1)}, u32[]{:S(2)}, u32[]{:S(2)}) %collective-permute-start.20) | collective-permute-done | bytes 262176 | tf_op jit(solution)/shard_map/ppermute | solution.py:33
  143.3 2.5 %collective-permute-start.23 = (f16[4,128,128]{2,1,0:T(8,128)(2,1)S(1)}, f16[4,128,128]{2,1,0:T(8,128)(2,1)S(1)}, u32[]{:S(2)}, u32[]{:S(2)}) collective-permute-start(f16[4,128,128]{2,1,0:T(8,128)(2,1)S(1)} %get-tuple-element.39), channel_id=1, source_target_pairs={{0,32},{4,36},{8,40},{12,44},{16,48},{20,52},{24,56},{28,60},{32,0... | collective-permute-start | bytes 393224 | tf_op jit(solution)/shard_map/ppermute | solution.py:33
  145.8 3.6 %collective-permute-done.23 = f16[4,128,128]{2,1,0:T(8,128)(2,1)S(1)} collective-permute-done((f16[4,128,128]{2,1,0:T(8,128)(2,1)S(1)}, f16[4,128,128]{2,1,0:T(8,128)(2,1)S(1)}, u32[]{:S(2)}, u32[]{:S(2)}) %collective-permute-start.23) | collective-permute-done | bytes 131104 | tf_op jit(solution)/shard_map/ppermute | solution.py:33
  149.5 3.8 %collective-permute-start.24 = (f16[2,128,128]{2,1,0:T(8,128)(2,1)S(1)}, f16[2,128,128]{2,1,0:T(8,128)(2,1)S(1)}, u32[]{:S(2)}, u32[]{:S(2)}) collective-permute-start(f16[2,128,128]{2,1,0:T(8,128)(2,1)S(1)} %fusion.4), channel_id=1, source_target_pairs={{0,64},{4,68},{8,72},{12,76},{16,80},{20,84},{24,88},{28,92},{32,9... | collective-permute-start | bytes 196616 | tf_op jit(solution)/shard_map/ppermute | solution.py:33
  153.3 2.6 %collective-permute-done.24 = f16[2,128,128]{2,1,0:T(8,128)(2,1)S(1)} collective-permute-done((f16[2,128,128]{2,1,0:T(8,128)(2,1)S(1)}, f16[2,128,128]{2,1,0:T(8,128)(2,1)S(1)}, u32[]{:S(2)}, u32[]{:S(2)}) %collective-permute-start.24) | collective-permute-done | bytes 65568 | tf_op jit(solution)/shard_map/ppermute | solution.py:33
  155.9 5.5 %collective-permute-start.25 = (f16[128,128]{1,0:T(8,128)(2,1)S(1)}, f16[128,128]{1,0:T(8,128)(2,1)S(1)}, u32[]{:S(2)}, u32[]{:S(2)}) collective-permute-start(f16[128,128]{1,0:T(8,128)(2,1)S(1)} %fusion.23), channel_id=1, source_target_pairs={{0,128},{4,132},{8,136},{12,140},{16,144},{20,148},{24,152},{28,15... | collective-permute-start | bytes 98312 | tf_op jit(solution)/shard_map/ppermute | solution.py:33
  161.4 2.8 %collective-permute-done.25 = f16[128,128]{1,0:T(8,128)(2,1)S(1)} collective-permute-done((f16[128,128]{1,0:T(8,128)(2,1)S(1)}, f16[128,128]{1,0:T(8,128)(2,1)S(1)}, u32[]{:S(2)}, u32[]{:S(2)}) %collective-permute-start.25) | collective-permute-done | bytes 32800 | tf_op jit(solution)/shard_map/ppermute | solution.py:33
  (115 shorter events, 12.3 us)
Async XLA Ops:
  4.0 60.6 %collective-permute-start.6 = (bf16[2048,256]{1,0:T(8,128)(2,1)}, bf16[2048,256]{1,0:T(8,128)(2,1)S(1)}, u32[]{:S(2)}, u32[]{:S(2)}) collective-permute-start(bf16[2048,256]{1,0:T(8,128)(2,1)} %take_rows.3), channel_id=1, source_target_pairs={{0,1},{1,2},{2,3},{3,0},{4,5},{5,6},{6,7},{7,4},{8,9},{9,10},{10,1... | collective-permute-start | bytes 3145736 | tf_op jit(solution)/shard_map/ppermute | solution.py:37
  9.0 55.7 %collective-permute-start.7 = (bf16[2048,256]{1,0:T(8,128)(2,1)}, bf16[2048,256]{1,0:T(8,128)(2,1)}, u32[]{:S(2)}, u32[]{:S(2)}) collective-permute-start(bf16[2048,256]{1,0:T(8,128)(2,1)} %take_rows.4), channel_id=1, source_target_pairs={{0,2},{1,3},{2,0},{3,1},{4,6},{5,7},{6,4},{7,5},{8,10},{9,11},{10,... | collective-permute-start | bytes 3145736 | tf_op jit(solution)/shard_map/ppermute | solution.py:37
  15.0 6.0 %copy-start.20 = (f32[128,128]{1,0:T(8,128)S(1)}, f32[128,128]{1,0:T(8,128)}, u32[]{:S(2)}) copy-start(f32[128,128]{1,0:T(8,128)} %a.4) | copy-start | bytes 196612
  15.0 49.7 %collective-permute-start.8 = (bf16[2048,256]{1,0:T(8,128)(2,1)}, bf16[2048,256]{1,0:T(8,128)(2,1)}, u32[]{:S(2)}, u32[]{:S(2)}) collective-permute-start(bf16[2048,256]{1,0:T(8,128)(2,1)} %take_rows.5), channel_id=1, source_target_pairs={{0,3},{1,0},{2,1},{3,2},{4,7},{5,4},{6,5},{7,6},{8,11},{9,8},{10,9... | collective-permute-start | bytes 3145736 | tf_op jit(solution)/shard_map/ppermute | solution.py:37
  21.0 4.1 %copy-start.28 = (s32[8192]{0:T(1024)S(1)}, s32[8192]{0:T(1024)}, u32[]{:S(2)}) copy-start(s32[8192]{0:T(1024)} %param.8) | copy-start | bytes 98308
  21.0 4.2 %copy-start.29 = (s32[8192]{0:T(1024)S(1)}, s32[8192]{0:T(1024)}, u32[]{:S(2)}) copy-start(s32[8192]{0:T(1024)} %param.7) | copy-start | bytes 98308
  21.1 5.3 %collective-permute-start = (s16[128,128]{1,0:T(8,128)(2,1)S(1)}, s16[128,128]{1,0:T(8,128)(2,1)S(1)}, u32[]{:S(2)}, u32[]{:S(2)}) collective-permute-start(s16[128,128]{1,0:T(8,128)(2,1)S(1)} %encode_terms.1.refs_0_), channel_id=1, source_target_pairs={{0,64},{4,68},{8,72},{12,76},{16,80},{20,84},{24,88},{28,92},{32,9... | collective-permute-start | bytes 98312 | tf_op jit(solution)/shard_map/ppermute | solution.py:33
  26.4 9.6 %collective-permute-start.1 = (s16[256,128]{1,0:T(8,128)(2,1)S(1)}, s16[256,128]{1,0:T(8,128)(2,1)S(1)}, u32[]{:S(2)}, u32[]{:S(2)}) collective-permute-start(s16[256,128]{1,0:T(8,128)(2,1)S(1)} %join.8.refs_0_), channel_id=1, source_target_pairs={{0,128},{4,132},{8,136},{12,140},{16,144},{20,148},{24,152},{28,15... | collective-permute-start | bytes 196616 | tf_op jit(solution)/shard_map/ppermute | solution.py:33
  35.9 5.1 %collective-permute-start.2 = (s16[512,128]{1,0:T(8,128)(2,1)S(1)}, s16[512,128]{1,0:T(8,128)(2,1)S(1)}, u32[]{:S(2)}, u32[]{:S(2)}) collective-permute-start(s16[512,128]{1,0:T(8,128)(2,1)S(1)} %join.9.refs_0_), channel_id=1, source_target_pairs={{0,32},{4,36},{8,40},{12,44},{16,48},{20,52},{24,56},{28,60},{32,0... | collective-permute-start | bytes 393224 | tf_op jit(solution)/shard_map/ppermute | solution.py:33
  43.4 6.3 %collective-permute-start.4 = (f32[128,128]{1,0:T(8,128)S(1)}, f32[128,128]{1,0:T(8,128)S(1)}, u32[]{:S(2)}, u32[]{:S(2)}) collective-permute-start(f32[128,128]{1,0:T(8,128)S(1)} %join.11), channel_id=1, source_target_pairs={{4,0},{8,4},{12,8},{16,12},{20,16},{24,20},{28,24},{32,28},{36,32}... | collective-permute-start | bytes 196616 | tf_op jit(solution)/shard_map/ppermute | solution.py:281
  46.0 7.4 %collective-permute-start.3 = (f32[128,128]{1,0:T(8,128)S(1)}, f32[128,128]{1,0:T(8,128)}, u32[]{:S(2)}, u32[]{:S(2)}) collective-permute-start(f32[128,128]{1,0:T(8,128)S(1)} %join.11), channel_id=1, source_target_pairs={{0,4},{4,8},{8,12},{12,16},{16,20},{20,24},{24,28},{28,32},{32,36}... | collective-permute-start | bytes 196616 | tf_op jit(solution)/shard_map/ppermute | solution.py:281
  49.7 1.0 copy-start.27
  49.7 21.4 %collective-permute-start.5 = (s16[1024,128]{1,0:T(8,128)(2,1)S(1)}, s16[1024,128]{1,0:T(8,128)(2,1)}, u32[]{:S(2)}, u32[]{:S(2)}) collective-permute-start(s16[1024,128]{1,0:T(8,128)(2,1)S(1)} %join.10.refs_1_.refs_0_), channel_id=1, source_target_pairs={{0,8},{4,12},{8,0},{12,4},{16,24},{20,28},{24,16},{28,20},{32,40},... | collective-permute-start | bytes 786440 | tf_op jit(solution)/shard_map/ppermute | solution.py:33
  63.2 1.5 copy-start.4
  64.7 6.5 %copy-start.1 = (f32[3072,128]{1,0:T(8,128)}, f32[3072,128]{1,0:T(8,128)S(1)}, u32[]{:S(2)}) copy-start(f32[3072,128]{1,0:T(8,128)S(1)} %get-tuple-element.18.refs_5_.refs_2_) | copy-start | bytes 4718596
  64.7 2.8 %copy-start = (bf16[8192,256]{1,0:T(8,128)(2,1)S(1)}, bf16[8192,256]{1,0:T(8,128)(2,1)}, u32[]{:S(2)}) copy-start(bf16[8192,256]{1,0:T(8,128)(2,1)} %b0.3) | copy-start | bytes 12582916
  71.1 1.1 copy-start.6
  72.2 16.3 %collective-permute-start.9 = (s16[2048,128]{1,0:T(8,128)(2,1)S(1)}, s16[2048,128]{1,0:T(8,128)(2,1)S(1)}, u32[]{:S(2)}, u32[]{:S(2)}) collective-permute-start(s16[2048,128]{1,0:T(8,128)(2,1)S(1)} %join.12.refs_0_), channel_id=1, source_target_pairs={{0,16},{4,20},{8,24},{12,28},{16,0},{20,4},{24,8},{28,12},{32,48},... | collective-permute-start | bytes 1572872 | tf_op jit(solution)/shard_map/ppermute | solution.py:33
  75.0 9.0 %collective-permute-start.10 = (s16[768,128]{1,0:T(8,128)(2,1)S(1)}, s16[768,128]{1,0:T(8,128)(2,1)S(1)}, u32[]{:S(2)}, u32[]{:S(2)}) collective-permute-start(s16[768,128]{1,0:T(8,128)(2,1)S(1)} %get-tuple-element.21), channel_id=1, source_target_pairs={{0,1},{1,2},{2,3},{3,0},{4,5},{5,6},{6,7},{7,4},{8,9},{9,10},{10,1... | collective-permute-start | bytes 589832 | tf_op jit(solution)/shard_map/ppermute | solution.py:37
  75.0 9.3 %collective-permute-start.11 = (s16[768,128]{1,0:T(8,128)(2,1)S(1)}, s16[768,128]{1,0:T(8,128)(2,1)S(1)}, u32[]{:S(2)}, u32[]{:S(2)}) collective-permute-start(s16[768,128]{1,0:T(8,128)(2,1)S(1)} %get-tuple-element.22), channel_id=1, source_target_pairs={{0,2},{1,3},{2,0},{3,1},{4,6},{5,7},{6,4},{7,5},{8,10},{9,11},{10,... | collective-permute-start | bytes 589832 | tf_op jit(solution)/shard_map/ppermute | solution.py:37
  78.4 9.5 %collective-permute-start.12 = (s16[768,128]{1,0:T(8,128)(2,1)S(1)}, s16[768,128]{1,0:T(8,128)(2,1)S(1)}, u32[]{:S(2)}, u32[]{:S(2)}) collective-permute-start(s16[768,128]{1,0:T(8,128)(2,1)S(1)} %get-tuple-element.23), channel_id=1, source_target_pairs={{0,3},{1,0},{2,1},{3,2},{4,7},{5,4},{6,5},{7,6},{8,11},{9,8},{10,9... | collective-permute-start | bytes 589832 | tf_op jit(solution)/shard_map/ppermute | solution.py:37
  83.9 4.6 %copy-start.22 = (s16[1280,128]{1,0:T(8,128)(2,1)}, s16[1280,128]{1,0:T(8,128)(2,1)S(1)}, u32[]{:S(2)}) copy-start(s16[1280,128]{1,0:T(8,128)(2,1)S(1)} %get-tuple-element.28) | copy-start | bytes 983044
  83.9 4.6 %copy-start.23 = (s16[1280,128]{1,0:T(8,128)(2,1)}, s16[1280,128]{1,0:T(8,128)(2,1)S(1)}, u32[]{:S(2)}) copy-start(s16[1280,128]{1,0:T(8,128)(2,1)S(1)} %get-tuple-element.27) | copy-start | bytes 983044
  84.0 4.6 %copy-start.24 = (s16[1280,128]{1,0:T(8,128)(2,1)}, s16[1280,128]{1,0:T(8,128)(2,1)S(1)}, u32[]{:S(2)}) copy-start(s16[1280,128]{1,0:T(8,128)(2,1)S(1)} %get-tuple-element.26) | copy-start | bytes 983044
  84.0 10.5 %copy-start.2 = (f32[3072,128]{1,0:T(8,128)S(1)}, f32[3072,128]{1,0:T(8,128)}, u32[]{:S(2)}) copy-start(f32[3072,128]{1,0:T(8,128)} %copy-done.1) | copy-start | bytes 4718596
  84.0 10.5 %copy-start.7 = (s16[768,128]{1,0:T(8,128)(2,1)S(1)}, s16[768,128]{1,0:T(8,128)(2,1)}, u32[]{:S(2)}) copy-start(s16[768,128]{1,0:T(8,128)(2,1)} %copy-done.6) | copy-start | bytes 589828
  84.0 4.6 %copy-start.8 = (s16[768,128]{1,0:T(8,128)(2,1)}, s16[768,128]{1,0:T(8,128)(2,1)S(1)}, u32[]{:S(2)}) copy-start(s16[768,128]{1,0:T(8,128)(2,1)S(1)} %collective-permute-done.10.refs_3_.refs_6_) | copy-start | bytes 589828
  84.3 4.3 %copy-start.10 = (s16[768,128]{1,0:T(8,128)(2,1)}, s16[768,128]{1,0:T(8,128)(2,1)S(1)}, u32[]{:S(2)}) copy-start(s16[768,128]{1,0:T(8,128)(2,1)S(1)} %collective-permute-done.11.refs_4_.refs_7_) | copy-start | bytes 589828
  88.7 5.8 %collective-permute-start.13 = (s16[4096,128]{1,0:T(8,128)(2,1)S(1)}, s16[4096,128]{1,0:T(8,128)(2,1)}, u32[]{:S(2)}, u32[]{:S(2)}) collective-permute-start(s16[4096,128]{1,0:T(8,128)(2,1)S(1)} %join.13.refs_3_), channel_id=1, source_target_pairs={{0,4},{4,0},{8,12},{12,8},{16,20},{20,16},{24,28},{28,24},{32,36},... | collective-permute-start | bytes 3145736 | tf_op jit(solution)/shard_map/ppermute | solution.py:33
  88.8 18.8 %collective-permute-start.14 = (s16[1280,128]{1,0:T(8,128)(2,1)}, s16[1280,128]{1,0:T(8,128)(2,1)S(1)}, u32[]{:S(2)}, u32[]{:S(2)}) collective-permute-start(s16[1280,128]{1,0:T(8,128)(2,1)} %copy-done.24), channel_id=1, source_target_pairs={{0,1},{1,2},{2,3},{3,0},{4,5},{5,6},{6,7},{7,4},{8,9},{9,10},{10,1... | collective-permute-start | bytes 983048 | tf_op jit(solution)/shard_map/ppermute | solution.py:37
  89.4 18.2 %collective-permute-start.15 = (s16[1280,128]{1,0:T(8,128)(2,1)}, s16[1280,128]{1,0:T(8,128)(2,1)S(1)}, u32[]{:S(2)}, u32[]{:S(2)}) collective-permute-start(s16[1280,128]{1,0:T(8,128)(2,1)} %copy-done.23), channel_id=1, source_target_pairs={{0,2},{1,3},{2,0},{3,1},{4,6},{5,7},{6,4},{7,5},{8,10},{9,11},{10,... | collective-permute-start | bytes 983048 | tf_op jit(solution)/shard_map/ppermute | solution.py:37
  92.4 15.6 %collective-permute-start.16 = (s16[1280,128]{1,0:T(8,128)(2,1)}, s16[1280,128]{1,0:T(8,128)(2,1)S(1)}, u32[]{:S(2)}, u32[]{:S(2)}) collective-permute-start(s16[1280,128]{1,0:T(8,128)(2,1)} %copy-done.22), channel_id=1, source_target_pairs={{0,3},{1,0},{2,1},{3,2},{4,7},{5,4},{6,5},{7,6},{8,11},{9,8},{10,9... | collective-permute-start | bytes 983048 | tf_op jit(solution)/shard_map/ppermute | solution.py:37
  94.5 0.9 copy-start.9
  95.4 0.9 copy-start.11
  96.3 0.9 copy-start.13
  106.2 1.3 copy-start.5
  122.9 4.2 %collective-permute-start.19 = (f32[4096,128]{1,0:T(8,128)S(1)}, f32[4096,128]{1,0:T(8,128)S(1)}, u32[]{:S(2)}, u32[]{:S(2)}) collective-permute-start(f32[4096,128]{1,0:T(8,128)S(1)} %get-tuple-element.33), channel_id=1, source_target_pairs={{0,4},{4,0},{8,12},{12,8},{16,20},{20,16},{24,28},{28,24},{32,36},... | collective-permute-start | bytes 6291464 | tf_op jit(solution)/shard_map/ppermute | solution.py:33
  127.1 4.7 %copy-start.3 = (f32[5120,128]{1,0:T(8,128)S(1)}, f32[5120,128]{1,0:T(8,128)}, u32[]{:S(2)}) copy-start(f32[5120,128]{1,0:T(8,128)} %get-tuple-element.31.refs_1_) | copy-start | bytes 7864324
  127.1 4.7 %copy-start.17 = (s32[8192]{0:T(1024)S(1)}, s32[8192]{0:T(1024)}, u32[]{:S(2)}) copy-start(s32[8192]{0:T(1024)} %copy-done.15) | copy-start | bytes 98308
  127.5 10.8 %collective-permute-start.22 = (f16[2,4,128,128]{3,2,1,0:T(8,128)(2,1)S(1)}, f16[2,4,128,128]{3,2,1,0:T(8,128)(2,1)S(1)}, u32[]{:S(2)}, u32[]{:S(2)}) collective-permute-start(f16[2,4,128,128]{3,2,1,0:T(8,128)(2,1)S(1)} %bitcast.44), channel_id=1, source_target_pairs={{0,16},{4,20},{8,24},{12,28},{16,0},{20,4},{24,8},{28,12},{32,48},... | collective-permute-start | bytes 786440 | tf_op jit(solution)/shard_map/ppermute | solution.py:33
  130.0 12.5 %collective-permute-start.20 = (f16[2,4,128,128]{3,2,1,0:T(8,128)(2,1)S(1)}, f16[2,4,128,128]{3,2,1,0:T(8,128)(2,1)S(1)}, u32[]{:S(2)}, u32[]{:S(2)}) collective-permute-start(f16[2,4,128,128]{3,2,1,0:T(8,128)(2,1)S(1)} %bitcast.43), channel_id=1, source_target_pairs={{0,8},{4,12},{8,0},{12,4},{16,24},{20,28},{24,16},{28,20},{32,40},... | collective-permute-start | bytes 786440 | tf_op jit(solution)/shard_map/ppermute | solution.py:33
  130.5 12.5 %collective-permute-start.21 = (f16[2,4,128,128]{3,2,1,0:T(8,128)(2,1)S(1)}, f16[2,4,128,128]{3,2,1,0:T(8,128)(2,1)S(1)}, u32[]{:S(2)}, u32[]{:S(2)}) collective-permute-start(f16[2,4,128,128]{3,2,1,0:T(8,128)(2,1)S(1)} %bitcast.42), channel_id=1, source_target_pairs={{0,24},{4,28},{8,16},{12,20},{16,8},{20,12},{24,0},{28,4},{32,56},... | collective-permute-start | bytes 786440 | tf_op jit(solution)/shard_map/ppermute | solution.py:33
  133.6 12.2 %collective-permute-start.17 = (f32[128,128]{1,0:T(8,128)S(1)}, f32[128,128]{1,0:T(8,128)S(1)}, u32[]{:S(2)}, u32[]{:S(2)}) collective-permute-start(f32[128,128]{1,0:T(8,128)S(1)} %get-tuple-element.41), channel_id=1, source_target_pairs={{0,4},{4,8},{8,12},{12,16},{16,20},{20,24},{24,28},{28,32},{32,36}... | collective-permute-start | bytes 196616 | tf_op jit(solution)/shard_map/ppermute | solution.py:281
  134.9 10.8 %collective-permute-start.18 = (f32[128,128]{1,0:T(8,128)S(1)}, f32[128,128]{1,0:T(8,128)S(1)}, u32[]{:S(2)}, u32[]{:S(2)}) collective-permute-start(f32[128,128]{1,0:T(8,128)S(1)} %get-tuple-element.42), channel_id=1, source_target_pairs={{4,0},{8,4},{12,8},{16,12},{20,16},{24,20},{28,24},{32,28},{36,32}... | collective-permute-start | bytes 196616 | tf_op jit(solution)/shard_map/ppermute | solution.py:281
  143.3 6.1 %collective-permute-start.23 = (f16[4,128,128]{2,1,0:T(8,128)(2,1)S(1)}, f16[4,128,128]{2,1,0:T(8,128)(2,1)S(1)}, u32[]{:S(2)}, u32[]{:S(2)}) collective-permute-start(f16[4,128,128]{2,1,0:T(8,128)(2,1)S(1)} %get-tuple-element.39), channel_id=1, source_target_pairs={{0,32},{4,36},{8,40},{12,44},{16,48},{20,52},{24,56},{28,60},{32,0... | collective-permute-start | bytes 393224 | tf_op jit(solution)/shard_map/ppermute | solution.py:33
  145.7 19.1 %copy-start.14 = (f32[128,128]{1,0:T(8,128)}, f32[128,128]{1,0:T(8,128)S(1)}, u32[]{:S(2)}) copy-start(f32[128,128]{1,0:T(8,128)S(1)} %fusion.7.refs_1_) | copy-start | bytes 196612
  149.5 6.4 %collective-permute-start.24 = (f16[2,128,128]{2,1,0:T(8,128)(2,1)S(1)}, f16[2,128,128]{2,1,0:T(8,128)(2,1)S(1)}, u32[]{:S(2)}, u32[]{:S(2)}) collective-permute-start(f16[2,128,128]{2,1,0:T(8,128)(2,1)S(1)} %fusion.4), channel_id=1, source_target_pairs={{0,64},{4,68},{8,72},{12,76},{16,80},{20,84},{24,88},{28,92},{32,9... | collective-permute-start | bytes 196616 | tf_op jit(solution)/shard_map/ppermute | solution.py:33
  155.9 8.3 %collective-permute-start.25 = (f16[128,128]{1,0:T(8,128)(2,1)S(1)}, f16[128,128]{1,0:T(8,128)(2,1)S(1)}, u32[]{:S(2)}, u32[]{:S(2)}) collective-permute-start(f16[128,128]{1,0:T(8,128)(2,1)S(1)} %fusion.23), channel_id=1, source_target_pairs={{0,128},{4,132},{8,136},{12,140},{16,144},{20,148},{24,152},{28,15... | collective-permute-start | bytes 98312 | tf_op jit(solution)/shard_map/ppermute | solution.py:33
  (8 other events, 5.8 us)

commit v7 on v6

--- a/solution.py
+++ b/solution.py
@@ -13,7 +13,7 @@
 REC_LOW, REC_HIGH = 1.0, 2.2
 REC_SCALE = 65535.0 / (REC_HIGH - REC_LOW)
 SUM_SCALE = 1.0 / 32.0
-BACK = (768, 1280)
+PIECES = (1024, 1024)
 LARGE = pltpu.CompilerParams(vmem_limit_bytes=60 * 2**20)
 SUMS = pltpu.CompilerParams(vmem_limit_bytes=44 * 2**20)
 SMALL = pltpu.CompilerParams(vmem_limit_bytes=12 * 2**20)
@@ -37,14 +37,14 @@
     return lax.ppermute(value, "fq", [(i, (i + k) % NY) for i in range(NY)])
 
 
-def make_table(samples, y, width):
+def make_table(samples, y, width, after):
     part, cols = samples // NY, NY * 2 * width
     tile = 128
     quarter = samples // 4
     shift = quarter.bit_length() - 1
 
-    def body(y_ref, out):
-        y = y_ref[0]
+    def body(y_ref, *refs):
+        y, out = y_ref[0], refs[-1]
         row = pl.program_id(0) * tile
         time = (y - row // part) % NY * part + row % part + lax.broadcasted_iota(jnp.int32, (tile, 1), 0)
         for k in range(NY):
@@ -64,13 +64,13 @@
     return pl.pallas_call(
         body,
         grid=(samples // tile,),
-        in_specs=[pl.BlockSpec(memory_space=pltpu.SMEM)],
+        in_specs=[pl.BlockSpec(memory_space=pltpu.SMEM)] + [pl.BlockSpec(memory_space=pl.ANY)] * len(after),
         out_specs=pl.BlockSpec((tile, cols), lambda i: (i, 0)),
         out_shape=jax.ShapeDtypeStruct((samples, cols), jnp.bfloat16),
         compiler_params=SMALL,
         cost_estimate=pl.CostEstimate(flops=2**30, bytes_accessed=2**25, transcendentals=0),
         name="make_table",
-    )(y[None])
+    )(y[None], *after)
 
 
 def join(parts, after=()):
@@ -93,27 +93,31 @@
     )(*parts, *after)
 
 
-def take_rows(traces, y, k):
+def take_rows(traces, y, first, size, after=()):
     rows, part = traces.shape
-    tile = 512
-    steps = rows // NY // tile
-
-    def body(y_ref, a, b):
-        b[...] = a[...]
-
-    return pl.pallas_call(
-        body,
-        grid_spec=pltpu.PrefetchScalarGridSpec(
-            num_scalar_prefetch=1,
-            grid=(steps,),
-            in_specs=[pl.BlockSpec((tile, part), lambda i, y: ((y[0] + k) % NY * steps + i, 0))],
-            out_specs=pl.BlockSpec((tile, part), lambda i, y: (i, 0)),
-        ),
-        out_shape=jax.ShapeDtypeStruct((rows // NY, part), traces.dtype),
+
+    def body(y_ref, traces, *refs):
+        outs, sems = refs[len(after) : len(after) + NY], refs[len(after) + NY :]
+        copies = []
+        for k in range(NY):
+            at = pl.multiple_of((y_ref[0] + k) % NY * (rows // NY) + first, 16)
+            copies.append(pltpu.make_async_copy(traces.at[pl.ds(at, size), :], outs[k], sems[k]))
+        for copy in copies:
+            copy.start()
+        for copy in copies:
+            copy.wait()
+
+    hbm = pl.BlockSpec(memory_space=pl.ANY)
+    return pl.pallas_call(
+        body,
+        in_specs=[pl.BlockSpec(memory_space=pltpu.SMEM), hbm] + [hbm] * len(after),
+        out_specs=[hbm] * NY,
+        out_shape=[jax.ShapeDtypeStruct((size, part), traces.dtype)] * NY,
+        scratch_shapes=[pltpu.SemaphoreType.DMA] * NY,
         compiler_params=LARGE,
         cost_estimate=COST,
         name="take_rows",
-    )(y[None], traces)
+    )(y[None], traces, *after)
 
 
 def encode_terms(terms, after):
@@ -134,11 +138,11 @@
     )(terms, *after)
 
 
-def spectra(traces, y, first, rows, blocks, table, width):
-    part, tile = traces.shape[1], 256
-    share, start, steps = traces.shape[0] // NY // tile, first // tile, rows // tile
-
-    def body(y_ref, b0, b1, b2, b3, t, *outs):
+def spectra(blocks, table, width):
+    rows, part = blocks[0].shape
+    tile = 512
+
+    def body(b0, b1, b2, b3, t, *outs):
         for k, out in enumerate(outs):
             cols = pl.ds(k * 2 * width, 2 * width)
             acc = None
@@ -152,19 +156,14 @@
 
     return pl.pallas_call(
         body,
-        grid_spec=pltpu.PrefetchScalarGridSpec(
-            num_scalar_prefetch=1,
-            grid=(steps,),
-            in_specs=[pl.BlockSpec((tile, part), lambda i, y: (y[0] * share + start + i, 0))]
-            + [pl.BlockSpec((tile, part), lambda i, y: (start + i, 0))] * 3
-            + [pl.BlockSpec(table.shape, lambda i, y: (0, 0))],
-            out_specs=[pl.BlockSpec((tile, width), lambda i, y: (i, 0))] * 4,
-        ),
-        out_shape=[jax.ShapeDtypeStruct((rows, width), jnp.int16)] * 4,
+        grid=(rows // tile,),
+        in_specs=[pl.BlockSpec((tile, part), lambda i: (i, 0))] * NY + [pl.BlockSpec(table.shape, lambda i: (0, 0))],
+        out_specs=[pl.BlockSpec((tile, width), lambda i: (i, 0))] * NY,
+        out_shape=[jax.ShapeDtypeStruct((rows, width), jnp.int16)] * NY,
         compiler_params=MEDIUM,
         cost_estimate=COST,
         name="spectra",
-    )(y[None], traces, *blocks, table)
+    )(*blocks, table)
 
 
 def gather_shots(shot_near, shot_at, sizes):
@@ -285,22 +284,26 @@
     rows, part = traces.shape
     block, width = shot_terms.shape
     share = rows // NY
-    first = [sum(BACK[:h]) for h in range(len(BACK))]
+    first = [sum(PIECES[:h]) for h in range(len(PIECES))]
     owner, y = lax.axis_index("tr"), lax.axis_index("fq")
     z, x, c = owner // (NX * NC), owner // NC % NX, owner % NC
 
-    come = {k: send_y(take_rows(traces, y, k), k) for k in (1, 3, 2)}
-    got = [come[k] for k in range(1, NY)]
-    table = make_table(part * NY, y, width)
+    got, after = [], ()
+    for at, size in zip(first, PIECES):
+        mine = take_rows(traces, y, at, size, after)
+        come = {k: send_y(mine[k], k) for k in (1, 3, 2)}
+        after = [come[k] for k in range(1, NY)]
+        got.append([mine[0]] + after)
+    table = make_table(part * NY, y, width, got[0][:1])
     codes, coded = [], []
-    for at, size in zip(first, BACK):
-        coded.append(spectra(traces, y, at, size, got, table, width))
+    for blocks in got:
+        coded.append(spectra(blocks, table, width))
         codes += [send_y(coded[-1][k], k) if k else coded[-1][k] for k in range(NY)]
 
     def ordered(v):
         v = v.reshape(NY, share)
         v = jnp.stack([lax.dynamic_index_in_dim(v, (y - k) % NY, 0, keepdims=False) for k in range(NY)])
-        return jnp.concatenate([v[:, at : at + size].reshape(NY * size) for at, size in zip(first, BACK)])
+        return jnp.concatenate([v[:, at : at + size].reshape(NY * size) for at, size in zip(first, PIECES)])
 
     near = receiver_index // block
     rz, rx, rc = near // (NX * NC), near // NC % NX, near % NC
@@ -314,13 +317,13 @@
 
     terms = encode_terms(receiver_terms, (table,))
     terms = join([terms, swap(terms, 2, 0, 0)])
-    terms = join([terms, swap(terms, 4, 0, 0)])
-    terms = join([terms, swap(terms, 1, 0, 0)])
+    terms = join([terms, swap(terms, 4, 0, 0)], got[0][1:])
+    terms = join([terms, swap(terms, 1, 0, 0)], got[1][:1])
     shot_terms = join([shot_terms], (terms,))
     shot_near = jnp.concatenate([neighbour(shot_terms, 1), shot_terms, neighbour(shot_terms, -1)])
-    shots = gather_shots(shot_near, shot_at, [size * NY for size in BACK])
-    terms = join([terms, swap(terms, 0, 1, 0)], got + [shots[0], rec_at, coded[0][0]])
-    terms = join([terms, swap(terms, 0, 2, 0)], [coded[1][0]] + codes[1:NY])
+    shots = gather_shots(shot_near, shot_at, [size * NY for size in PIECES])
+    terms = join([terms, swap(terms, 0, 1, 0)], [coded[0][0]])
+    terms = join([terms, swap(terms, 0, 2, 0)], [shots[0], rec_at] + got[1][1:])
     far_terms = swap(terms, 0, 0, 1)
 
     sums, residuals, done = (), [], 0

time: 167 us -> 291 us (1.74)
  Pallas kernels: 59.6 us -> 177 us
  starting transfers between devices: 52.5 us -> 68.5 us
  waiting for transfers between devices: 31.2 us -> 27.7 us
    pallas_call x5 -> x4, Pallas kernels: 19.3 us -> 137 us  [the longest x2 129 us: take_rows(): pl.pallas_call(body, in_specs=[pl.BlockSpec(memory_space=pltpu.SMEM), hbm...]
    ppermute x13, starting transfers between devices: 31.1 us -> 42.2 us  [swap(): lax.ppermute(value, 'tr', [(tr_of(z, x, c), tr_of(z ^ dz, x ^ dx, c ^ dc)...]
    ppermute x9 -> x12, starting transfers between devices: 13.9 us -> 20.1 us  [send_y(): return lax.ppermute(value, 'fq', [(i, (i + k) % NY) for i in range(NY)])]
    unnamed x61 -> x53, local copies, waits for them, and re-layouts: 12.3 us -> 12.9 us
  transfers between devices with their start and end apart: 26 -> 29, of which waited for: 14 -> 11; matrix products, arithmetic and copies ran while one was open for 4% -> 0% of each run, Pallas kernels for 24% -> 34%
where the time goes in v7:
time: 291 us; the launch traced here: 290 us
  Pallas kernels  177 us (61%)
  starting transfers between devices  68.5 us (24%)
  waiting for transfers between devices  27.7 us (10%)
  local copies, waits for them, and re-layouts  13.3 us (5%)
    pallas_call x2, Pallas kernels, take_rows(): pl.pallas_call(body, in_specs=[pl.BlockSpec(memory_space=pltpu.SMEM), hbm...  129 us
    ppermute x13, starting transfers between devices, swap(): lax.ppermute(value, 'tr', [(tr_of(z, x, c), tr_of(z ^ dz, x ^ dx, c ^ dc)...  42.2 us
    ppermute x13, waiting for transfers between devices, swap(): lax.ppermute(value, 'tr', [(tr_of(z, x, c), tr_of(z ^ dz, x ^ dx, c ^ dc)...  25.3 us
    pallas_call x2, Pallas kernels, sum_receivers(): pl.pallas_call(body, in_specs=[sm, sm] + [vm] * (3 + parts + held), out_s...  24.7 us
    ppermute x12, starting transfers between devices, send_y(): return lax.ppermute(value, 'fq', [(i, (i + k) % NY) for i in range(NY)])  20.1 us
    unnamed x53, local copies, waits for them, and re-layouts  12.9 us
    pallas_call x1, Pallas kernels, gather_shots(): pl.pallas_call(body, in_specs=[sm, vm], out_specs=[vm] * len(sizes), out_...  8.11 us
    pallas_call x2, Pallas kernels, spectra(): pl.pallas_call(body, grid=(rows // tile,), in_specs=[pl.BlockSpec((tile,...  7.66 us
  transfers between devices with their start and end apart: 29, of which 11 were waited for; matrix products, arithmetic and copies ran while one was open for 0% of the time, Pallas kernels for 34%

profile of v7, /device:TPU:8, one launch (start us, length us, event | category | flops | bytes accessed | tf_op | source)
XLA Modules:
  0.0 290.0 jit_solution(3855769299662999320)
XLA Ops:
  0.6 64.7 %take_rows.2 = (bf16[1024,256]{1,0:T(8,128)(2,1)}, bf16[1024,256]{1,0:T(8,128)(2,1)}, bf16[1024,256]{1,0:T(8,128)(2,1)}, bf16[1024,256]{1,0:T(8,128)(2,1)}) custom-call(s32[1]{0:T(128)} %bitcast.10.y_ref, bf16[8192,256]{1,0:T(8,128)(2,1)} %traces.3), custom_call_target="tpu_custom_call" | custom-call | flops 1000 | bytes 1000 | tf_op jit(solution)/shard_map/take_rows/pallas_call | solution.py:111
  65.3 1.7 collective-permute-start.2
  67.0 2.7 collective-permute-start.3
  70.3 1.0 copy-done.16
  71.4 5.3 %make_table.1.refs_0_.t = bf16[1024,1024]{1,0:T(8,128)(2,1)S(1)} custom-call(s32[1]{0:T(128)} %bitcast.10.y_ref, bf16[1024,256]{1,0:T(8,128)(2,1)S(1)} %copy-done.16), custom_call_target="tpu_custom_call" | custom-call | flops 1073741824 | bytes 33554432 | tf_op jit(solution)/shard_map/make_table/pallas_call | solution.py:64
  76.8 3.4 %collective-permute-start = (s16[128,128]{1,0:T(8,128)(2,1)S(1)}, s16[128,128]{1,0:T(8,128)(2,1)S(1)}, u32[]{:S(2)}, u32[]{:S(2)}) collective-permute-start(s16[128,128]{1,0:T(8,128)(2,1)S(1)} %encode_terms.1.refs_0_), channel_id=1, source_target_pairs={{0,64},{4,68},{8,72},{12,76},{16,80},{20,84},{24,88},{28,92},{32,9... | collective-permute-start | bytes 98312 | tf_op jit(solution)/shard_map/ppermute | solution.py:33
  82.0 6.8 %collective-permute-start.1 = (s16[256,128]{1,0:T(8,128)(2,1)S(1)}, s16[256,128]{1,0:T(8,128)(2,1)S(1)}, u32[]{:S(2)}, u32[]{:S(2)}) collective-permute-start(s16[256,128]{1,0:T(8,128)(2,1)S(1)} %join.8.refs_0_), channel_id=1, source_target_pairs={{0,128},{4,132},{8,136},{12,140},{16,144},{20,148},{24,152},{28,15... | collective-permute-start | bytes 196616 | tf_op jit(solution)/shard_map/ppermute | solution.py:33
  88.9 2.3 collective-permute-done.1.refs_1_
  91.2 1.5 collective-permute-done.4.refs_4_.refs_2_.b3
  92.7 2.0 collective-permute-start.5
  94.8 64.7 %take_rows.3 = (bf16[1024,256]{1,0:T(8,128)(2,1)}, bf16[1024,256]{1,0:T(8,128)(2,1)}, bf16[1024,256]{1,0:T(8,128)(2,1)}, bf16[1024,256]{1,0:T(8,128)(2,1)}) custom-call(s32[1]{0:T(128)} %bitcast.10.y_ref, bf16[8192,256]{1,0:T(8,128)(2,1)} %traces.3, bf16[1024,256]{1,0:T(8,128)(2,1)} %copy-done.1, bf16[1024,256]{1,0:T(8,128)(2,1)} %copy-done.3, ...), custom_call_target="tpu_custom_call" | custom-call | flops 1000 | bytes 1000 | tf_op jit(solution)/shard_map/take_rows/pallas_call | solution.py:111
  160.5 1.6 collective-permute-start.8
  162.2 1.4 collective-permute-start.10
  163.5 1.5 collective-permute-start.11
  165.0 1.7 collective-permute-start.12
  167.7 1.0 copy-done.4
  168.7 1.0 copy-done.17
  169.8 4.7 %spectra.2 = (s16[1024,128]{1,0:T(8,128)(2,1)S(1)}, s16[1024,128]{1,0:T(8,128)(2,1)}, s16[1024,128]{1,0:T(8,128)(2,1)}, s16[1024,128]{1,0:T(8,128)(2,1)S(1)}) custom-call(bf16[1024,256]{1,0:T(8,128)(2,1)S(1)} %copy-done.17, bf16[1024,256]{1,0:T(8,128)(2,1)S(1)} %copy-done.2, bf16[1024,256]{1,0:T(8,128)(2,1)S(1)} %copy-done.4, ...), custom_call_target="tpu_custom_call" | custom-call | flops 1000 | bytes 1000 | tf_op jit(solution)/shard_map/spectra/pallas_call | solution.py:157
  174.4 1.3 collective-permute-start.7
  175.8 3.4 %collective-permute-start.9 = (s16[2048,128]{1,0:T(8,128)(2,1)S(1)}, s16[2048,128]{1,0:T(8,128)(2,1)S(1)}, u32[]{:S(2)}, u32[]{:S(2)}) collective-permute-start(s16[2048,128]{1,0:T(8,128)(2,1)S(1)} %join.12.refs_0_), channel_id=1, source_target_pairs={{0,16},{4,20},{8,24},{12,28},{16,0},{20,4},{24,8},{28,12},{32,48},... | collective-permute-start | bytes 1572872 | tf_op jit(solution)/shard_map/ppermute | solution.py:33
  179.2 2.1 collective-permute-start.6
  182.3 8.1 %gather_shots.1 = (f32[4096,128]{1,0:T(8,128)S(1)}, f32[4096,128]{1,0:T(8,128)S(1)}) custom-call(s32[8192]{0:T(1024)S(1)} %bitcast_dynamic-update-slice_fusion.shot_at, f32[384,128]{1,0:T(8,128)S(1)} %pad_maximum_fusion.shot), custom_call_target="tpu_custom_call" | custom-call | flops 1000 | bytes 1000 | tf_op jit(solution)/shard_map/gather_shots/pallas_call | solution.py:186
  190.5 1.5 collective-permute-done.9.refs_1_
  192.8 9.7 %collective-permute-start.13 = (s16[4096,128]{1,0:T(8,128)(2,1)S(1)}, s16[4096,128]{1,0:T(8,128)(2,1)}, u32[]{:S(2)}, u32[]{:S(2)}) collective-permute-start(s16[4096,128]{1,0:T(8,128)(2,1)S(1)} %join.13.refs_3_), channel_id=1, source_target_pairs={{0,4},{4,0},{8,12},{12,8},{16,20},{20,16},{24,28},{28,24},{32,36},... | collective-permute-start | bytes 3145736 | tf_op jit(solution)/shard_map/ppermute | solution.py:33
  202.9 3.3 %collective-permute-start.15 = (s16[1024,128]{1,0:T(8,128)(2,1)}, s16[1024,128]{1,0:T(8,128)(2,1)}, u32[]{:S(2)}, u32[]{:S(2)}) collective-permute-start(s16[1024,128]{1,0:T(8,128)(2,1)} %get-tuple-element.37), channel_id=1, source_target_pairs={{0,2},{1,3},{2,0},{3,1},{4,6},{5,7},{6,4},{7,5},{8,10},{9,11},{10,... | collective-permute-start | bytes 786440 | tf_op jit(solution)/shard_map/ppermute | solution.py:37
  207.5 1.0 copy-done.11
  208.6 1.0 copy-done.13
  210.6 3.0 %spectra.3 = (s16[1024,128]{1,0:T(8,128)(2,1)S(1)}, s16[1024,128]{1,0:T(8,128)(2,1)S(1)}, s16[1024,128]{1,0:T(8,128)(2,1)S(1)}, s16[1024,128]{1,0:T(8,128)(2,1)S(1)}) custom-call(bf16[1024,256]{1,0:T(8,128)(2,1)S(1)} %copy-done.9, bf16[1024,256]{1,0:T(8,128)(2,1)S(1)} %copy-done.11, bf16[1024,256]{1,0:T(8,128)(2,1)S(1)} %copy-done.13, ...), custom_call_target="tpu_custom_call" | custom-call | flops 1000 | bytes 1000 | tf_op jit(solution)/shard_map/spectra/pallas_call | solution.py:157
  213.7 2.1 collective-permute-start.17
  215.8 3.1 %collective-permute-start.18 = (s16[1024,128]{1,0:T(8,128)(2,1)S(1)}, s16[1024,128]{1,0:T(8,128)(2,1)S(1)}, u32[]{:S(2)}, u32[]{:S(2)}) collective-permute-start(s16[1024,128]{1,0:T(8,128)(2,1)S(1)} %get-tuple-element.43), channel_id=1, source_target_pairs={{0,2},{1,3},{2,0},{3,1},{4,6},{5,7},{6,4},{7,5},{8,10},{9,11},{10,... | collective-permute-start | bytes 786440 | tf_op jit(solution)/shard_map/ppermute | solution.py:37
  218.8 1.6 collective-permute-start.19
  220.5 11.7 %sum_receivers.2 = (f32[4096,128]{1,0:T(8,128)S(1)}, f32[4096,128]{1,0:T(8,128)S(1)}, f32[4096,128]{1,0:T(8,128)S(1)}) custom-call(s32[4096]{0:T(1024)S(1)} %bitcast.61, s32[4]{0:T(128)S(1)} %get-tuple-element.72.refs_1_, f32[4096,128]{1,0:T(8,128)} %copy-done, s16[4096,128]{1,0:T(8,128)(2,1)S(1)} %join.13.refs_3_, ...), custom_call_target="tpu_custom_call" | custom-call | flops 1000 | bytes 1000 | tf_op jit(solution)/shard_map/sum_receivers/pallas_call | solution.py:237
  232.2 1.3 copy-done.6
  233.6 1.4 copy-done.7
  234.9 13.0 %sum_receivers.3 = (f32[4096,128]{1,0:T(8,128)S(1)}, f32[4096,128]{1,0:T(8,128)S(1)}, f32[4096,128]{1,0:T(8,128)S(1)}) custom-call(s32[4096]{0:T(1024)S(1)} %bitcast.59, s32[4]{0:T(128)S(1)} %get-tuple-element.71.refs_1_, f32[4096,128]{1,0:T(8,128)} %copy-done.5, s16[4096,128]{1,0:T(8,128)(2,1)S(1)} %join.13.refs_3_, ...), custom_call_target="tpu_custom_call" | custom-call | flops 1000 | bytes 1000 | tf_op jit(solution)/shard_map/sum_receivers/pallas_call | solution.py:237
  248.1 4.1 %collective-permute-done.22 = f32[4096,128]{1,0:T(8,128)S(1)} collective-permute-done((f32[4096,128]{1,0:T(8,128)S(1)}, f32[4096,128]{1,0:T(8,128)S(1)}, u32[]{:S(2)}, u32[]{:S(2)}) %collective-permute-start.22) | collective-permute-done | bytes 2097184 | tf_op jit(solution)/shard_map/ppermute | solution.py:33
  252.7 3.8 %collective-permute-start.25 = (f16[2,4,128,128]{3,2,1,0:T(8,128)(2,1)S(1)}, f16[2,4,128,128]{3,2,1,0:T(8,128)(2,1)S(1)}, u32[]{:S(2)}, u32[]{:S(2)}) collective-permute-start(f16[2,4,128,128]{3,2,1,0:T(8,128)(2,1)S(1)} %bitcast.66), channel_id=1, source_target_pairs={{0,16},{4,20},{8,24},{12,28},{16,0},{20,4},{24,8},{28,12},{32,48},... | collective-permute-start | bytes 786440 | tf_op jit(solution)/shard_map/ppermute | solution.py:33
  256.5 1.2 collective-permute-start.24
  257.7 1.8 sum_shots.1.refs_1_
  259.5 1.5 collective-permute-start.20
  261.0 1.3 collective-permute-start.21
  262.4 1.2 collective-permute-done.25
  263.6 5.1 %collective-permute-done.23 = f16[2,4,128,128]{3,2,1,0:T(8,128)(2,1)S(1)} collective-permute-done((f16[2,4,128,128]{3,2,1,0:T(8,128)(2,1)S(1)}, f16[2,4,128,128]{3,2,1,0:T(8,128)(2,1)S(1)}, u32[]{:S(2)}, u32[]{:S(2)}) %collective-permute-start.23) | collective-permute-done | bytes 262176 | tf_op jit(solution)/shard_map/ppermute | solution.py:33
  269.2 5.2 %collective-permute-done.26 = f16[4,128,128]{2,1,0:T(8,128)(2,1)S(1)} collective-permute-done((f16[4,128,128]{2,1,0:T(8,128)(2,1)S(1)}, f16[4,128,128]{2,1,0:T(8,128)(2,1)S(1)}, u32[]{:S(2)}, u32[]{:S(2)}) %collective-permute-start.26) | collective-permute-done | bytes 131104 | tf_op jit(solution)/shard_map/ppermute | solution.py:33
  274.4 3.4 %collective-permute-start.27 = (f16[2,128,128]{2,1,0:T(8,128)(2,1)S(1)}, f16[2,128,128]{2,1,0:T(8,128)(2,1)S(1)}, u32[]{:S(2)}, u32[]{:S(2)}) collective-permute-start(f16[2,128,128]{2,1,0:T(8,128)(2,1)S(1)} %fusion.4), channel_id=1, source_target_pairs={{0,64},{4,68},{8,72},{12,76},{16,80},{20,84},{24,88},{28,92},{32,9... | collective-permute-start | bytes 196616 | tf_op jit(solution)/shard_map/ppermute | solution.py:33
  277.8 2.9 %collective-permute-done.27 = f16[2,128,128]{2,1,0:T(8,128)(2,1)S(1)} collective-permute-done((f16[2,128,128]{2,1,0:T(8,128)(2,1)S(1)}, f16[2,128,128]{2,1,0:T(8,128)(2,1)S(1)}, u32[]{:S(2)}, u32[]{:S(2)}) %collective-permute-start.27) | collective-permute-done | bytes 65568 | tf_op jit(solution)/shard_map/ppermute | solution.py:33
  280.8 6.6 %collective-permute-start.28 = (f16[128,128]{1,0:T(8,128)(2,1)S(1)}, f16[128,128]{1,0:T(8,128)(2,1)S(1)}, u32[]{:S(2)}, u32[]{:S(2)}) collective-permute-start(f16[128,128]{1,0:T(8,128)(2,1)S(1)} %fusion.23), channel_id=1, source_target_pairs={{0,128},{4,132},{8,136},{12,140},{16,144},{20,148},{24,152},{28,15... | collective-permute-start | bytes 98312 | tf_op jit(solution)/shard_map/ppermute | solution.py:33
  287.4 1.9 collective-permute-done.28
  (106 shorter events, 10.4 us)
Async XLA Ops:
  0.6 76.1 %copy-start.19 = (f32[128,128]{1,0:T(8,128)S(1)}, f32[128,128]{1,0:T(8,128)}, u32[]{:S(2)}) copy-start(f32[128,128]{1,0:T(8,128)} %a.1) | copy-start | bytes 196612
  65.3 25.9 %collective-permute-start.2 = (bf16[1024,256]{1,0:T(8,128)(2,1)}, bf16[1024,256]{1,0:T(8,128)(2,1)S(1)}, u32[]{:S(2)}, u32[]{:S(2)}) collective-permute-start(bf16[1024,256]{1,0:T(8,128)(2,1)} %get-tuple-element.27), channel_id=1, source_target_pairs={{0,1},{1,2},{2,3},{3,0},{4,5},{5,6},{6,7},{7,4},{8,9},{9,10},{10,1... | collective-permute-start | bytes 1572872 | tf_op jit(solution)/shard_map/ppermute | solution.py:37
  67.0 24.2 %collective-permute-start.3 = (bf16[1024,256]{1,0:T(8,128)(2,1)}, bf16[1024,256]{1,0:T(8,128)(2,1)S(1)}, u32[]{:S(2)}, u32[]{:S(2)}) collective-permute-start(bf16[1024,256]{1,0:T(8,128)(2,1)} %get-tuple-element.28), channel_id=1, source_target_pairs={{0,2},{1,3},{2,0},{3,1},{4,6},{5,7},{6,4},{7,5},{8,10},{9,11},{10,... | collective-permute-start | bytes 1572872 | tf_op jit(solution)/shard_map/ppermute | solution.py:37
  69.7 23.1 %collective-permute-start.4 = (bf16[1024,256]{1,0:T(8,128)(2,1)}, bf16[1024,256]{1,0:T(8,128)(2,1)}, u32[]{:S(2)}, u32[]{:S(2)}) collective-permute-start(bf16[1024,256]{1,0:T(8,128)(2,1)} %get-tuple-element.29), channel_id=1, source_target_pairs={{0,3},{1,0},{2,1},{3,2},{4,7},{5,4},{6,5},{7,6},{8,11},{9,8},{10,9... | collective-permute-start | bytes 1572872 | tf_op jit(solution)/shard_map/ppermute | solution.py:37
  70.3 1.0 copy-start.16
  76.7 4.1 %copy-start.22 = (s32[8192]{0:T(1024)S(1)}, s32[8192]{0:T(1024)}, u32[]{:S(2)}) copy-start(s32[8192]{0:T(1024)} %param.7) | copy-start | bytes 98308
  76.7 4.1 %copy-start.23 = (s32[8192]{0:T(1024)S(1)}, s32[8192]{0:T(1024)}, u32[]{:S(2)}) copy-start(s32[8192]{0:T(1024)} %param.8) | copy-start | bytes 98308
  76.8 5.3 %collective-permute-start = (s16[128,128]{1,0:T(8,128)(2,1)S(1)}, s16[128,128]{1,0:T(8,128)(2,1)S(1)}, u32[]{:S(2)}, u32[]{:S(2)}) collective-permute-start(s16[128,128]{1,0:T(8,128)(2,1)S(1)} %encode_terms.1.refs_0_), channel_id=1, source_target_pairs={{0,64},{4,68},{8,72},{12,76},{16,80},{20,84},{24,88},{28,92},{32,9... | collective-permute-start | bytes 98312 | tf_op jit(solution)/shard_map/ppermute | solution.py:33
  82.0 9.2 %collective-permute-start.1 = (s16[256,128]{1,0:T(8,128)(2,1)S(1)}, s16[256,128]{1,0:T(8,128)(2,1)S(1)}, u32[]{:S(2)}, u32[]{:S(2)}) collective-permute-start(s16[256,128]{1,0:T(8,128)(2,1)S(1)} %join.8.refs_0_), channel_id=1, source_target_pairs={{0,128},{4,132},{8,136},{12,140},{16,144},{20,148},{24,152},{28,15... | collective-permute-start | bytes 196616 | tf_op jit(solution)/shard_map/ppermute | solution.py:33
  91.2 3.6 %copy-start.1 = (bf16[1024,256]{1,0:T(8,128)(2,1)}, bf16[1024,256]{1,0:T(8,128)(2,1)S(1)}, u32[]{:S(2)}) copy-start(bf16[1024,256]{1,0:T(8,128)(2,1)S(1)} %collective-permute-done.2.refs_2_.refs_0_.b1) | copy-start | bytes 1572868
  91.2 3.6 %copy-start.3 = (bf16[1024,256]{1,0:T(8,128)(2,1)}, bf16[1024,256]{1,0:T(8,128)(2,1)S(1)}, u32[]{:S(2)}) copy-start(bf16[1024,256]{1,0:T(8,128)(2,1)S(1)} %collective-permute-done.3.refs_3_.refs_1_.b2) | copy-start | bytes 1572868
  92.7 66.7 %collective-permute-start.5 = (s16[512,128]{1,0:T(8,128)(2,1)S(1)}, s16[512,128]{1,0:T(8,128)(2,1)S(1)}, u32[]{:S(2)}, u32[]{:S(2)}) collective-permute-start(s16[512,128]{1,0:T(8,128)(2,1)S(1)} %join.9.refs_0_), channel_id=1, source_target_pairs={{0,32},{4,36},{8,40},{12,44},{16,48},{20,52},{24,56},{28,60},{32,0... | collective-permute-start | bytes 393224 | tf_op jit(solution)/shard_map/ppermute | solution.py:33
  159.5 1.0 copy-start.8
  160.5 15.2 %collective-permute-start.8 = (s16[1024,128]{1,0:T(8,128)(2,1)S(1)}, s16[1024,128]{1,0:T(8,128)(2,1)S(1)}, u32[]{:S(2)}, u32[]{:S(2)}) collective-permute-start(s16[1024,128]{1,0:T(8,128)(2,1)S(1)} %join.10.refs_1_.refs_0_), channel_id=1, source_target_pairs={{0,8},{4,12},{8,0},{12,4},{16,24},{20,28},{24,16},{28,20},{32,40},... | collective-permute-start | bytes 786440 | tf_op jit(solution)/shard_map/ppermute | solution.py:33
  162.2 28.3 %collective-permute-start.10 = (bf16[1024,256]{1,0:T(8,128)(2,1)}, bf16[1024,256]{1,0:T(8,128)(2,1)S(1)}, u32[]{:S(2)}, u32[]{:S(2)}) collective-permute-start(bf16[1024,256]{1,0:T(8,128)(2,1)} %get-tuple-element.33), channel_id=1, source_target_pairs={{0,1},{1,2},{2,3},{3,0},{4,5},{5,6},{6,7},{7,4},{8,9},{9,10},{10,1... | collective-permute-start | bytes 1572872 | tf_op jit(solution)/shard_map/ppermute | solution.py:37
  163.5 26.9 %collective-permute-start.11 = (bf16[1024,256]{1,0:T(8,128)(2,1)}, bf16[1024,256]{1,0:T(8,128)(2,1)S(1)}, u32[]{:S(2)}, u32[]{:S(2)}) collective-permute-start(bf16[1024,256]{1,0:T(8,128)(2,1)} %get-tuple-element.34), channel_id=1, source_target_pairs={{0,2},{1,3},{2,0},{3,1},{4,6},{5,7},{6,4},{7,5},{8,10},{9,11},{10,... | collective-permute-start | bytes 1572872 | tf_op jit(solution)/shard_map/ppermute | solution.py:37
  165.0 25.5 %collective-permute-start.12 = (bf16[1024,256]{1,0:T(8,128)(2,1)}, bf16[1024,256]{1,0:T(8,128)(2,1)S(1)}, u32[]{:S(2)}, u32[]{:S(2)}) collective-permute-start(bf16[1024,256]{1,0:T(8,128)(2,1)} %get-tuple-element.35), channel_id=1, source_target_pairs={{0,3},{1,0},{2,1},{3,2},{4,7},{5,4},{6,5},{7,6},{8,11},{9,8},{10,9... | collective-permute-start | bytes 1572872 | tf_op jit(solution)/shard_map/ppermute | solution.py:37
  166.6 1.0 copy-start.2
  169.8 4.7 %copy-start.20 = (f32[128,128]{1,0:T(8,128)S(1)}, f32[128,128]{1,0:T(8,128)}, u32[]{:S(2)}) copy-start(f32[128,128]{1,0:T(8,128)} %refs_0_.1) | copy-start | bytes 196612
  174.4 7.8 %copy-start.21 = (s16[1024,128]{1,0:T(8,128)(2,1)}, s16[1024,128]{1,0:T(8,128)(2,1)S(1)}, u32[]{:S(2)}) copy-start(s16[1024,128]{1,0:T(8,128)(2,1)S(1)} %get-tuple-element.38) | copy-start | bytes 786436
  174.4 4.8 %collective-permute-start.7 = (f32[128,128]{1,0:T(8,128)S(1)}, f32[128,128]{1,0:T(8,128)S(1)}, u32[]{:S(2)}, u32[]{:S(2)}) collective-permute-start(f32[128,128]{1,0:T(8,128)S(1)} %join.11), channel_id=1, source_target_pairs={{4,0},{8,4},{12,8},{16,12},{20,16},{24,20},{28,24},{32,28},{36,32}... | collective-permute-start | bytes 196616 | tf_op jit(solution)/shard_map/ppermute | solution.py:280
  175.8 16.2 %collective-permute-start.9 = (s16[2048,128]{1,0:T(8,128)(2,1)S(1)}, s16[2048,128]{1,0:T(8,128)(2,1)S(1)}, u32[]{:S(2)}, u32[]{:S(2)}) collective-permute-start(s16[2048,128]{1,0:T(8,128)(2,1)S(1)} %join.12.refs_0_), channel_id=1, source_target_pairs={{0,16},{4,20},{8,24},{12,28},{16,0},{20,4},{24,8},{28,12},{32,48},... | collective-permute-start | bytes 1572872 | tf_op jit(solution)/shard_map/ppermute | solution.py:33
  179.2 3.0 %collective-permute-start.6 = (f32[128,128]{1,0:T(8,128)S(1)}, f32[128,128]{1,0:T(8,128)S(1)}, u32[]{:S(2)}, u32[]{:S(2)}) collective-permute-start(f32[128,128]{1,0:T(8,128)S(1)} %join.11), channel_id=1, source_target_pairs={{0,4},{4,8},{8,12},{12,16},{16,20},{20,24},{24,28},{28,32},{32,36}... | collective-permute-start | bytes 196616 | tf_op jit(solution)/shard_map/ppermute | solution.py:280
  190.4 1.7 copy-start
  190.4 2.0 copy-start.5
  190.4 2.1 copy-start.10
  190.5 2.3 copy-start.12
  190.5 2.4 copy-start.14
  192.8 27.7 %collective-permute-start.13 = (s16[4096,128]{1,0:T(8,128)(2,1)S(1)}, s16[4096,128]{1,0:T(8,128)(2,1)}, u32[]{:S(2)}, u32[]{:S(2)}) collective-permute-start(s16[4096,128]{1,0:T(8,128)(2,1)S(1)} %join.13.refs_3_), channel_id=1, source_target_pairs={{0,4},{4,0},{8,12},{12,8},{16,20},{20,16},{24,28},{28,24},{32,36},... | collective-permute-start | bytes 3145736 | tf_op jit(solution)/shard_map/ppermute | solution.py:33
  202.5 13.2 %collective-permute-start.14 = (s16[1024,128]{1,0:T(8,128)(2,1)}, s16[1024,128]{1,0:T(8,128)(2,1)}, u32[]{:S(2)}, u32[]{:S(2)}) collective-permute-start(s16[1024,128]{1,0:T(8,128)(2,1)} %get-tuple-element.36), channel_id=1, source_target_pairs={{0,1},{1,2},{2,3},{3,0},{4,5},{5,6},{6,7},{7,4},{8,9},{9,10},{10,1... | collective-permute-start | bytes 786440 | tf_op jit(solution)/shard_map/ppermute | solution.py:37
  202.9 15.9 %collective-permute-start.15 = (s16[1024,128]{1,0:T(8,128)(2,1)}, s16[1024,128]{1,0:T(8,128)(2,1)}, u32[]{:S(2)}, u32[]{:S(2)}) collective-permute-start(s16[1024,128]{1,0:T(8,128)(2,1)} %get-tuple-element.37), channel_id=1, source_target_pairs={{0,2},{1,3},{2,0},{3,1},{4,6},{5,7},{6,4},{7,5},{8,10},{9,11},{10,... | collective-permute-start | bytes 786440 | tf_op jit(solution)/shard_map/ppermute | solution.py:37
  206.3 14.3 %collective-permute-start.16 = (s16[1024,128]{1,0:T(8,128)(2,1)}, s16[1024,128]{1,0:T(8,128)(2,1)S(1)}, u32[]{:S(2)}, u32[]{:S(2)}) collective-permute-start(s16[1024,128]{1,0:T(8,128)(2,1)} %copy-done.21), channel_id=1, source_target_pairs={{0,3},{1,0},{2,1},{3,2},{4,7},{5,4},{6,5},{7,6},{8,11},{9,8},{10,9... | collective-permute-start | bytes 786440 | tf_op jit(solution)/shard_map/ppermute | solution.py:37
  206.5 1.0 copy-start.9
  213.7 21.3 %collective-permute-start.17 = (s16[1024,128]{1,0:T(8,128)(2,1)S(1)}, s16[1024,128]{1,0:T(8,128)(2,1)S(1)}, u32[]{:S(2)}, u32[]{:S(2)}) collective-permute-start(s16[1024,128]{1,0:T(8,128)(2,1)S(1)} %get-tuple-element.42), channel_id=1, source_target_pairs={{0,1},{1,2},{2,3},{3,0},{4,5},{5,6},{6,7},{7,4},{8,9},{9,10},{10,1... | collective-permute-start | bytes 786440 | tf_op jit(solution)/shard_map/ppermute | solution.py:37
  215.8 19.2 %collective-permute-start.18 = (s16[1024,128]{1,0:T(8,128)(2,1)S(1)}, s16[1024,128]{1,0:T(8,128)(2,1)S(1)}, u32[]{:S(2)}, u32[]{:S(2)}) collective-permute-start(s16[1024,128]{1,0:T(8,128)(2,1)S(1)} %get-tuple-element.43), channel_id=1, source_target_pairs={{0,2},{1,3},{2,0},{3,1},{4,6},{5,7},{6,4},{7,5},{8,10},{9,11},{10,... | collective-permute-start | bytes 786440 | tf_op jit(solution)/shard_map/ppermute | solution.py:37
  218.8 16.1 %collective-permute-start.19 = (s16[1024,128]{1,0:T(8,128)(2,1)S(1)}, s16[1024,128]{1,0:T(8,128)(2,1)S(1)}, u32[]{:S(2)}, u32[]{:S(2)}) collective-permute-start(s16[1024,128]{1,0:T(8,128)(2,1)S(1)} %get-tuple-element.44), channel_id=1, source_target_pairs={{0,3},{1,0},{2,1},{3,2},{4,7},{5,4},{6,5},{7,6},{8,11},{9,8},{10,9... | collective-permute-start | bytes 786440 | tf_op jit(solution)/shard_map/ppermute | solution.py:37
  232.2 1.4 copy-start.6
  233.6 1.4 copy-start.7
  248.0 4.2 %collective-permute-start.22 = (f32[4096,128]{1,0:T(8,128)S(1)}, f32[4096,128]{1,0:T(8,128)S(1)}, u32[]{:S(2)}, u32[]{:S(2)}) collective-permute-start(f32[4096,128]{1,0:T(8,128)S(1)} %get-tuple-element.49), channel_id=1, source_target_pairs={{0,4},{4,0},{8,12},{12,8},{16,20},{20,16},{24,28},{28,24},{32,36},... | collective-permute-start | bytes 6291464 | tf_op jit(solution)/shard_map/ppermute | solution.py:33
  252.7 10.9 %collective-permute-start.25 = (f16[2,4,128,128]{3,2,1,0:T(8,128)(2,1)S(1)}, f16[2,4,128,128]{3,2,1,0:T(8,128)(2,1)S(1)}, u32[]{:S(2)}, u32[]{:S(2)}) collective-permute-start(f16[2,4,128,128]{3,2,1,0:T(8,128)(2,1)S(1)} %bitcast.66), channel_id=1, source_target_pairs={{0,16},{4,20},{8,24},{12,28},{16,0},{20,4},{24,8},{28,12},{32,48},... | collective-permute-start | bytes 786440 | tf_op jit(solution)/shard_map/ppermute | solution.py:33
  256.5 12.2 %collective-permute-start.23 = (f16[2,4,128,128]{3,2,1,0:T(8,128)(2,1)S(1)}, f16[2,4,128,128]{3,2,1,0:T(8,128)(2,1)S(1)}, u32[]{:S(2)}, u32[]{:S(2)}) collective-permute-start(f16[2,4,128,128]{3,2,1,0:T(8,128)(2,1)S(1)} %bitcast.65), channel_id=1, source_target_pairs={{0,8},{4,12},{8,0},{12,4},{16,24},{20,28},{24,16},{28,20},{32,40},... | collective-permute-start | bytes 786440 | tf_op jit(solution)/shard_map/ppermute | solution.py:33
  256.5 12.2 %collective-permute-start.24 = (f16[2,4,128,128]{3,2,1,0:T(8,128)(2,1)S(1)}, f16[2,4,128,128]{3,2,1,0:T(8,128)(2,1)S(1)}, u32[]{:S(2)}, u32[]{:S(2)}) collective-permute-start(f16[2,4,128,128]{3,2,1,0:T(8,128)(2,1)S(1)} %bitcast.64), channel_id=1, source_target_pairs={{0,24},{4,28},{8,16},{12,20},{16,8},{20,12},{24,0},{28,4},{32,56},... | collective-permute-start | bytes 786440 | tf_op jit(solution)/shard_map/ppermute | solution.py:33
  259.5 9.6 %collective-permute-start.20 = (f32[128,128]{1,0:T(8,128)S(1)}, f32[128,128]{1,0:T(8,128)S(1)}, u32[]{:S(2)}, u32[]{:S(2)}) collective-permute-start(f32[128,128]{1,0:T(8,128)S(1)} %get-tuple-element.57), channel_id=1, source_target_pairs={{0,4},{4,8},{8,12},{12,16},{16,20},{20,24},{24,28},{28,32},{32,36}... | collective-permute-start | bytes 196616 | tf_op jit(solution)/shard_map/ppermute | solution.py:280
  261.0 8.1 %collective-permute-start.21 = (f32[128,128]{1,0:T(8,128)S(1)}, f32[128,128]{1,0:T(8,128)S(1)}, u32[]{:S(2)}, u32[]{:S(2)}) collective-permute-start(f32[128,128]{1,0:T(8,128)S(1)} %get-tuple-element.58), channel_id=1, source_target_pairs={{4,0},{8,4},{12,8},{16,12},{20,16},{24,20},{28,24},{32,28},{36,32}... | collective-permute-start | bytes 196616 | tf_op jit(solution)/shard_map/ppermute | solution.py:280
  268.9 5.5 %collective-permute-start.26 = (f16[4,128,128]{2,1,0:T(8,128)(2,1)S(1)}, f16[4,128,128]{2,1,0:T(8,128)(2,1)S(1)}, u32[]{:S(2)}, u32[]{:S(2)}) collective-permute-start(f16[4,128,128]{2,1,0:T(8,128)(2,1)S(1)} %get-tuple-element.55), channel_id=1, source_target_pairs={{0,32},{4,36},{8,40},{12,44},{16,48},{20,52},{24,56},{28,60},{32,0... | collective-permute-start | bytes 393224 | tf_op jit(solution)/shard_map/ppermute | solution.py:33
  269.1 20.8 %copy-start.18 = (f32[128,128]{1,0:T(8,128)}, f32[128,128]{1,0:T(8,128)S(1)}, u32[]{:S(2)}) copy-start(f32[128,128]{1,0:T(8,128)S(1)} %fusion.7.refs_1_) | copy-start | bytes 196612
  274.4 6.3 %collective-permute-start.27 = (f16[2,128,128]{2,1,0:T(8,128)(2,1)S(1)}, f16[2,128,128]{2,1,0:T(8,128)(2,1)S(1)}, u32[]{:S(2)}, u32[]{:S(2)}) collective-permute-start(f16[2,128,128]{2,1,0:T(8,128)(2,1)S(1)} %fusion.4), channel_id=1, source_target_pairs={{0,64},{4,68},{8,72},{12,76},{16,80},{20,84},{24,88},{28,92},{32,9... | collective-permute-start | bytes 196616 | tf_op jit(solution)/shard_map/ppermute | solution.py:33
  280.8 8.5 %collective-permute-start.28 = (f16[128,128]{1,0:T(8,128)(2,1)S(1)}, f16[128,128]{1,0:T(8,128)(2,1)S(1)}, u32[]{:S(2)}, u32[]{:S(2)}) collective-permute-start(f16[128,128]{1,0:T(8,128)(2,1)S(1)} %fusion.23), channel_id=1, source_target_pairs={{0,128},{4,132},{8,136},{12,140},{16,144},{20,148},{24,152},{28,15... | collective-permute-start | bytes 98312 | tf_op jit(solution)/shard_map/ppermute | solution.py:33
  (5 other events, 5.2 us)

commit v8 on v7

--- a/solution.py
+++ b/solution.py
@@ -15,7 +15,7 @@
 SUM_SCALE = 1.0 / 32.0
 PIECES = (1024, 1024)
 LARGE = pltpu.CompilerParams(vmem_limit_bytes=60 * 2**20)
-SUMS = pltpu.CompilerParams(vmem_limit_bytes=44 * 2**20)
+SUMS = pltpu.CompilerParams(vmem_limit_bytes=32 * 2**20)
 SMALL = pltpu.CompilerParams(vmem_limit_bytes=12 * 2**20)
 COST = pl.CostEstimate(flops=1000, bytes_accessed=1000, transcendentals=0)
 MEDIUM = pltpu.CompilerParams(vmem_limit_bytes=18 * 2**20)
@@ -107,14 +107,14 @@
         for copy in copies:
             copy.wait()
 
-    hbm = pl.BlockSpec(memory_space=pl.ANY)
+    hbm, vm = pl.BlockSpec(memory_space=pl.ANY), pl.BlockSpec(memory_space=pltpu.VMEM)
     return pl.pallas_call(
         body,
         in_specs=[pl.BlockSpec(memory_space=pltpu.SMEM), hbm] + [hbm] * len(after),
-        out_specs=[hbm] * NY,
+        out_specs=[vm] * NY,
         out_shape=[jax.ShapeDtypeStruct((size, part), traces.dtype)] * NY,
         scratch_shapes=[pltpu.SemaphoreType.DMA] * NY,
-        compiler_params=LARGE,
+        compiler_params=SMALL,
         cost_estimate=COST,
         name="take_rows",
     )(y[None], traces, *after)
@@ -290,7 +290,10 @@
 
     got, after = [], ()
     for at, size in zip(first, PIECES):
-        mine = take_rows(traces, y, at, size, after)
+        if after:
+            mine = take_rows(traces, y, at, size, after)
+        else:
+            mine = [lax.dynamic_slice_in_dim(traces, (y + k) % NY * share + at, size, 0) for k in range(NY)]
         come = {k: send_y(mine[k], k) for k in (1, 3, 2)}
         after = [come[k] for k in range(1, NY)]
         got.append([mine[0]] + after)
@@ -315,12 +318,12 @@
     shot_at = ordered(shot_index - (owner - 1) * block)
     live = live_counts[0] - jnp.stack([(y - k) % NY * share + at for at in first for k in range(NY)])
 
+    shot_terms = join([shot_terms], (table,))
+    shot_near = jnp.concatenate([neighbour(shot_terms, 1), shot_terms, neighbour(shot_terms, -1)])
     terms = encode_terms(receiver_terms, (table,))
     terms = join([terms, swap(terms, 2, 0, 0)])
-    terms = join([terms, swap(terms, 4, 0, 0)], got[0][1:])
+    terms = join([terms, swap(terms, 4, 0, 0)], got[0][1:] + [shot_near])
     terms = join([terms, swap(terms, 1, 0, 0)], got[1][:1])
-    shot_terms = join([shot_terms], (terms,))
-    shot_near = jnp.concatenate([neighbour(shot_terms, 1), shot_terms, neighbour(shot_terms, -1)])
     shots = gather_shots(shot_near, shot_at, [size * NY for size in PIECES])
     terms = join([terms, swap(terms, 0, 1, 0)], [coded[0][0]])
     terms = join([terms, swap(terms, 0, 2, 0)], [shots[0], rec_at] + got[1][1:])

time: 291 us -> 150 us (0.52)
  Pallas kernels: 177 us -> 44.4 us
  starting transfers between devices: 68.5 us -> 59 us
  waiting for transfers between devices: 27.7 us -> 31.5 us
    pallas_call x2 -> x1, Pallas kernels: 129 us -> 0.18 us  [take_rows(): pl.pallas_call(body, in_specs=[pl.BlockSpec(memory_space=pltpu.SMEM), hbm...]
    ppermute x13, starting transfers between devices: 42.2 us -> 32.8 us  [swap(): lax.ppermute(value, 'tr', [(tr_of(z, x, c), tr_of(z ^ dz, x ^ dx, c ^ dc)...]
    ppermute x12, waiting for transfers between devices: 1.55 us -> 7.29 us  [send_y(): return lax.ppermute(value, 'fq', [(i, (i + k) % NY) for i in range(NY)])]
    unnamed x53 -> x47, local copies, waits for them, and re-layouts: 12.9 us -> 7.93 us
    pallas_call x2, Pallas kernels: 24.7 us -> 21.1 us  [sum_receivers(): pl.pallas_call(body, in_specs=[sm, sm] + [vm] * (3 + parts + held), out_s...]
  transfers between devices with their start and end apart: 29 -> 29, of which waited for: 11 -> 9; matrix products, arithmetic and copies ran while one was open for 0% -> 0% of each run, Pallas kernels for 34% -> 23%
where the time goes in v8:
time: 150 us; the launch traced here: 149 us
  starting transfers between devices  59 us (39%)
  Pallas kernels  44.4 us (30%)
  waiting for transfers between devices  31.5 us (21%)
  local copies, waits for them, and re-layouts  11.1 us (7%)
  between operations  2.02 us (1%)
    ppermute x13, starting transfers between devices, swap(): lax.ppermute(value, 'tr', [(tr_of(z, x, c), tr_of(z ^ dz, x ^ dx, c ^ dc)...  32.8 us
    ppermute x13, waiting for transfers between devices, swap(): lax.ppermute(value, 'tr', [(tr_of(z, x, c), tr_of(z ^ dz, x ^ dx, c ^ dc)...  24.2 us
    pallas_call x2, Pallas kernels, sum_receivers(): pl.pallas_call(body, in_specs=[sm, sm] + [vm] * (3 + parts + held), out_s...  21.1 us
    ppermute x12, starting transfers between devices, send_y(): return lax.ppermute(value, 'fq', [(i, (i + k) % NY) for i in range(NY)])  19 us
    pallas_call x1, Pallas kernels, gather_shots(): pl.pallas_call(body, in_specs=[sm, vm], out_specs=[vm] * len(sizes), out_...  8.11 us
    unnamed x47, local copies, waits for them, and re-layouts  7.93 us
    pallas_call x2, Pallas kernels, spectra(): pl.pallas_call(body, grid=(rows // tile,), in_specs=[pl.BlockSpec((tile,...  7.63 us
    ppermute x12, waiting for transfers between devices, send_y(): return lax.ppermute(value, 'fq', [(i, (i + k) % NY) for i in range(NY)])  7.29 us
  transfers between devices with their start and end apart: 29, of which 9 were waited for; matrix products, arithmetic and copies ran while one was open for 0% of the time, Pallas kernels for 23%

profile of v8, /device:TPU:8, one launch (start us, length us, event | category | flops | bytes accessed | tf_op | source)
XLA Modules:
  0.0 149.5 jit_solution(15793805518147802790)
XLA Ops:
  0.7 2.7 %constant_dynamic-slice_fusion = (bf16[1024,256]{1,0:T(8,128)(2,1)}, bf16[1024,256]{1,0:T(8,128)(2,1)}, bf16[1024,256]{1,0:T(8,128)(2,1)}, bf16[1024,256]{1,0:T(8,128)(2,1)S(1)}) fusion(bf16[8192,256]{1,0:T(8,128)(2,1)} %traces.1, s32[]{:T(128)S(6)} %select_n.159, s32[]{:T(128)S(6)} %select_n.157, s32[]{:T(128)S(6)} %select_n.155, s32[]{:T(128)S(6)} %select_n.153), kind=kLoop, calls=%fused_computation.74 | loop fusion | bytes 4194320 | tf_op jit(solution)/shard_map/dynamic_slice | solution.py:296
  3.4 2.2 %collective-permute-start.6 = (bf16[1024,256]{1,0:T(8,128)(2,1)}, bf16[1024,256]{1,0:T(8,128)(2,1)S(1)}, u32[]{:S(2)}, u32[]{:S(2)}) collective-permute-start(bf16[1024,256]{1,0:T(8,128)(2,1)} %get-tuple-element.44), channel_id=1, source_target_pairs={{0,3},{1,0},{2,1},{3,2},{4,7},{5,4},{6,5},{7,6},{8,11},{9,8},{10,9... | collective-permute-start | bytes 1572872 | tf_op jit(solution)/shard_map/ppermute | solution.py:37
  5.6 0.9 collective-permute-start.5
  6.5 1.9 %collective-permute-start.4 = (bf16[1024,256]{1,0:T(8,128)(2,1)}, bf16[1024,256]{1,0:T(8,128)(2,1)}, u32[]{:S(2)}, u32[]{:S(2)}) collective-permute-start(bf16[1024,256]{1,0:T(8,128)(2,1)} %get-tuple-element.46), channel_id=1, source_target_pairs={{0,1},{1,2},{2,3},{3,0},{4,5},{5,6},{6,7},{7,4},{8,9},{9,10},{10,1... | collective-permute-start | bytes 1572872 | tf_op jit(solution)/shard_map/ppermute | solution.py:37
  8.4 5.3 %make_table.1.refs_1_.refs_0_.t = bf16[1024,1024]{1,0:T(8,128)(2,1)S(1)} custom-call(s32[1]{0:T(128)} %bitcast.10.y_ref, bf16[1024,256]{1,0:T(8,128)(2,1)S(1)} %get-tuple-element.47.refs_0_.b0), custom_call_target="tpu_custom_call" | custom-call | flops 1073741824 | bytes 33554432 | tf_op jit(solution)/shard_map/make_table/pallas_call | solution.py:64
  13.7 3.4 %collective-permute-start.2 = (s16[128,128]{1,0:T(8,128)(2,1)S(1)}, s16[128,128]{1,0:T(8,128)(2,1)S(1)}, u32[]{:S(2)}, u32[]{:S(2)}) collective-permute-start(s16[128,128]{1,0:T(8,128)(2,1)S(1)} %encode_terms.1.refs_0_), channel_id=1, source_target_pairs={{0,64},{4,68},{8,72},{12,76},{16,80},{20,84},{24,88},{28,92},{32,9... | collective-permute-start | bytes 98312 | tf_op jit(solution)/shard_map/ppermute | solution.py:33
  17.1 1.3 collective-permute-start.1
  19.5 3.0 %collective-permute-start = (f32[128,128]{1,0:T(8,128)S(1)}, f32[128,128]{1,0:T(8,128)S(1)}, u32[]{:S(2)}, u32[]{:S(2)}) collective-permute-start(f32[128,128]{1,0:T(8,128)S(1)} %join.8), channel_id=1, source_target_pairs={{0,4},{4,8},{8,12},{12,16},{16,20},{20,24},{24,28},{28,32},{32,36}... | collective-permute-start | bytes 196616 | tf_op jit(solution)/shard_map/ppermute | solution.py:280
  22.6 5.5 %collective-permute-start.3 = (s16[256,128]{1,0:T(8,128)(2,1)S(1)}, s16[256,128]{1,0:T(8,128)(2,1)S(1)}, u32[]{:S(2)}, u32[]{:S(2)}) collective-permute-start(s16[256,128]{1,0:T(8,128)(2,1)S(1)} %join.9.refs_0_), channel_id=1, source_target_pairs={{0,128},{4,132},{8,136},{12,140},{16,144},{20,148},{24,152},{28,15... | collective-permute-start | bytes 196616 | tf_op jit(solution)/shard_map/ppermute | solution.py:33
  28.1 3.4 %collective-permute-done.3.refs_1_ = s16[256,128]{1,0:T(8,128)(2,1)S(1)} collective-permute-done((s16[256,128]{1,0:T(8,128)(2,1)S(1)}, s16[256,128]{1,0:T(8,128)(2,1)S(1)}, u32[]{:S(2)}, u32[]{:S(2)}) %collective-permute-start.3) | collective-permute-done | bytes 65568 | tf_op jit(solution)/shard_map/ppermute | solution.py:33
  31.5 3.7 %collective-permute-start.7 = (s16[512,128]{1,0:T(8,128)(2,1)S(1)}, s16[512,128]{1,0:T(8,128)(2,1)S(1)}, u32[]{:S(2)}, u32[]{:S(2)}) collective-permute-start(s16[512,128]{1,0:T(8,128)(2,1)S(1)} %join.10.refs_0_), channel_id=1, source_target_pairs={{0,32},{4,36},{8,40},{12,44},{16,48},{20,52},{24,56},{28,60},{32,0... | collective-permute-start | bytes 393224 | tf_op jit(solution)/shard_map/ppermute | solution.py:33
  35.2 2.2 %copy-done = bf16[8192,256]{1,0:T(8,128)(2,1)S(1)} copy-done((bf16[8192,256]{1,0:T(8,128)(2,1)S(1)}, bf16[8192,256]{1,0:T(8,128)(2,1)}, u32[]{:S(2)}) %copy-start) | copy-done | bytes 4194328
  37.5 1.3 collective-permute-done.7.refs_1_
  38.9 0.8 copy-done.5
  39.7 1.2 collective-permute-start.8
  41.1 2.4 %collective-permute-start.11 = (bf16[1024,256]{1,0:T(8,128)(2,1)S(1)}, bf16[1024,256]{1,0:T(8,128)(2,1)S(1)}, u32[]{:S(2)}, u32[]{:S(2)}) collective-permute-start(bf16[1024,256]{1,0:T(8,128)(2,1)S(1)} %get-tuple-element.26), channel_id=1, source_target_pairs={{0,2},{1,3},{2,0},{3,1},{4,6},{5,7},{6,4},{7,5},{8,10},{9,11},{10,... | collective-permute-start | bytes 1572872 | tf_op jit(solution)/shard_map/ppermute | solution.py:37
  43.6 1.4 collective-permute-start.12
  45.0 4.6 %spectra.2 = (s16[1024,128]{1,0:T(8,128)(2,1)S(1)}, s16[1024,128]{1,0:T(8,128)(2,1)}, s16[1024,128]{1,0:T(8,128)(2,1)}, s16[1024,128]{1,0:T(8,128)(2,1)S(1)}) custom-call(bf16[1024,256]{1,0:T(8,128)(2,1)S(1)} %copy-done.8, bf16[1024,256]{1,0:T(8,128)(2,1)} %collective-permute-done.4.refs_2_.refs_0_.b1, ...), custom_call_target="tpu_custom_call" | custom-call | flops 1000 | bytes 1000 | tf_op jit(solution)/shard_map/spectra/pallas_call | solution.py:157
  49.6 2.0 %collective-permute-start.9 = (s16[2048,128]{1,0:T(8,128)(2,1)S(1)}, s16[2048,128]{1,0:T(8,128)(2,1)S(1)}, u32[]{:S(2)}, u32[]{:S(2)}) collective-permute-start(s16[2048,128]{1,0:T(8,128)(2,1)S(1)} %join.12.refs_0_), channel_id=1, source_target_pairs={{0,16},{4,20},{8,24},{12,28},{16,0},{20,4},{24,8},{28,12},{32,48},... | collective-permute-start | bytes 1572872 | tf_op jit(solution)/shard_map/ppermute | solution.py:33
  51.7 8.1 %gather_shots.1 = (f32[4096,128]{1,0:T(8,128)S(1)}, f32[4096,128]{1,0:T(8,128)S(1)}) custom-call(s32[8192]{0:T(1024)S(1)} %bitcast_dynamic-update-slice_fusion.shot_at, f32[384,128]{1,0:T(8,128)S(1)} %pad_maximum_fusion.shot.refs_5_), custom_call_target="tpu_custom_call" | custom-call | flops 1000 | bytes 1000 | tf_op jit(solution)/shard_map/gather_shots/pallas_call | solution.py:186
  59.8 7.3 %collective-permute-done.12.refs_6_.b3 = bf16[1024,256]{1,0:T(8,128)(2,1)S(1)} collective-permute-done((bf16[1024,256]{1,0:T(8,128)(2,1)S(1)}, bf16[1024,256]{1,0:T(8,128)(2,1)S(1)}, u32[]{:S(2)}, u32[]{:S(2)}) %collective-permute-start.12) | collective-permute-done | bytes 524320 | tf_op jit(solution)/shard_map/ppermute | solution.py:37
  67.2 0.7 copy-done.13
  68.5 1.9 %collective-permute-start.15 = (s16[1024,128]{1,0:T(8,128)(2,1)}, s16[1024,128]{1,0:T(8,128)(2,1)}, u32[]{:S(2)}, u32[]{:S(2)}) collective-permute-start(s16[1024,128]{1,0:T(8,128)(2,1)} %get-tuple-element.29), channel_id=1, source_target_pairs={{0,2},{1,3},{2,0},{3,1},{4,6},{5,7},{6,4},{7,5},{8,10},{9,11},{10,... | collective-permute-start | bytes 786440 | tf_op jit(solution)/shard_map/ppermute | solution.py:37
  70.5 2.3 %collective-permute-start.16 = (s16[1024,128]{1,0:T(8,128)(2,1)}, s16[1024,128]{1,0:T(8,128)(2,1)S(1)}, u32[]{:S(2)}, u32[]{:S(2)}) collective-permute-start(s16[1024,128]{1,0:T(8,128)(2,1)} %copy-done.18), channel_id=1, source_target_pairs={{0,3},{1,0},{2,1},{3,2},{4,7},{5,4},{6,5},{7,6},{8,11},{9,8},{10,9... | collective-permute-start | bytes 786440 | tf_op jit(solution)/shard_map/ppermute | solution.py:37
  72.7 1.0 copy-done.6
  73.8 1.0 copy-done.10
  74.8 1.0 copy-done.12
  75.9 1.0 copy-done.14
  76.9 3.0 %spectra.3 = (s16[1024,128]{1,0:T(8,128)(2,1)S(1)}, s16[1024,128]{1,0:T(8,128)(2,1)S(1)}, s16[1024,128]{1,0:T(8,128)(2,1)S(1)}, s16[1024,128]{1,0:T(8,128)(2,1)S(1)}) custom-call(bf16[1024,256]{1,0:T(8,128)(2,1)S(1)} %copy-done.6, bf16[1024,256]{1,0:T(8,128)(2,1)S(1)} %copy-done.10, bf16[1024,256]{1,0:T(8,128)(2,1)S(1)} %copy-done.12, ...), custom_call_target="tpu_custom_call" | custom-call | flops 1000 | bytes 1000 | tf_op jit(solution)/shard_map/spectra/pallas_call | solution.py:157
  80.0 2.9 %collective-permute-start.18 = (s16[1024,128]{1,0:T(8,128)(2,1)S(1)}, s16[1024,128]{1,0:T(8,128)(2,1)S(1)}, u32[]{:S(2)}, u32[]{:S(2)}) collective-permute-start(s16[1024,128]{1,0:T(8,128)(2,1)S(1)} %get-tuple-element.35), channel_id=1, source_target_pairs={{0,2},{1,3},{2,0},{3,1},{4,6},{5,7},{6,4},{7,5},{8,10},{9,11},{10,... | collective-permute-start | bytes 786440 | tf_op jit(solution)/shard_map/ppermute | solution.py:37
  82.9 2.5 %collective-permute-start.19 = (s16[1024,128]{1,0:T(8,128)(2,1)S(1)}, s16[1024,128]{1,0:T(8,128)(2,1)S(1)}, u32[]{:S(2)}, u32[]{:S(2)}) collective-permute-start(s16[1024,128]{1,0:T(8,128)(2,1)S(1)} %get-tuple-element.36), channel_id=1, source_target_pairs={{0,3},{1,0},{2,1},{3,2},{4,7},{5,4},{6,5},{7,6},{8,11},{9,8},{10,9... | collective-permute-start | bytes 786440 | tf_op jit(solution)/shard_map/ppermute | solution.py:37
  85.5 10.7 %sum_receivers.2 = (f32[4096,128]{1,0:T(8,128)S(1)}, f32[4096,128]{1,0:T(8,128)S(1)}, f32[4096,128]{1,0:T(8,128)S(1)}) custom-call(s32[4096]{0:T(1024)S(1)} %bitcast.61, s32[4]{0:T(128)S(1)} %get-tuple-element.68.refs_1_, f32[4096,128]{1,0:T(8,128)S(1)} %copy-done.2, s16[4096,128]{1,0:T(8,128)(2,1)S(1)} %join.13.refs_3_, ...), custom_call_target="tpu_custom_call" | custom-call | flops 1000 | bytes 1000 | tf_op jit(solution)/shard_map/sum_receivers/pallas_call | solution.py:237
  96.3 10.4 %sum_receivers.3 = (f32[4096,128]{1,0:T(8,128)S(1)}, f32[4096,128]{1,0:T(8,128)S(1)}, f32[4096,128]{1,0:T(8,128)S(1)}) custom-call(s32[4096]{0:T(1024)S(1)} %bitcast.59, s32[4]{0:T(128)S(1)} %get-tuple-element.67.refs_1_, f32[4096,128]{1,0:T(8,128)S(1)} %copy-done.4, s16[4096,128]{1,0:T(8,128)(2,1)S(1)} %join.13.refs_3_, ...), custom_call_target="tpu_custom_call" | custom-call | flops 1000 | bytes 1000 | tf_op jit(solution)/shard_map/sum_receivers/pallas_call | solution.py:237
  106.8 4.1 %collective-permute-done.22 = f32[4096,128]{1,0:T(8,128)S(1)} collective-permute-done((f32[4096,128]{1,0:T(8,128)S(1)}, f32[4096,128]{1,0:T(8,128)S(1)}, u32[]{:S(2)}, u32[]{:S(2)}) %collective-permute-start.22) | collective-permute-done | bytes 2097184 | tf_op jit(solution)/shard_map/ppermute | solution.py:33
  111.4 2.9 %collective-permute-start.25 = (f16[2,4,128,128]{3,2,1,0:T(8,128)(2,1)S(1)}, f16[2,4,128,128]{3,2,1,0:T(8,128)(2,1)S(1)}, u32[]{:S(2)}, u32[]{:S(2)}) collective-permute-start(f16[2,4,128,128]{3,2,1,0:T(8,128)(2,1)S(1)} %bitcast.66), channel_id=1, source_target_pairs={{0,16},{4,20},{8,24},{12,28},{16,0},{20,4},{24,8},{28,12},{32,48},... | collective-permute-start | bytes 786440 | tf_op jit(solution)/shard_map/ppermute | solution.py:33
  114.3 1.2 collective-permute-start.23
  115.6 1.8 %sum_shots.1.refs_1_ = f32[384,128]{1,0:T(8,128)S(1)} custom-call(s32[1,8192]{1,0:T(1,128)S(1)} %bitcast.57, f32[4096,128]{1,0:T(8,128)S(1)} %get-tuple-element.31.refs_0_, f32[4096,128]{1,0:T(8,128)S(1)} %get-tuple-element.39.refs_1_), custom_call_target="tpu_custom_call" | custom-call | flops 1000 | bytes 1000 | tf_op jit(solution)/shard_map/sum_shots/pallas_call | solution.py:267
  117.4 1.5 collective-permute-start.20
  118.9 1.3 collective-permute-start.21
  120.3 1.9 %collective-permute-done.25 = f16[2,4,128,128]{3,2,1,0:T(8,128)(2,1)S(1)} collective-permute-done((f16[2,4,128,128]{3,2,1,0:T(8,128)(2,1)S(1)}, f16[2,4,128,128]{3,2,1,0:T(8,128)(2,1)S(1)}, u32[]{:S(2)}, u32[]{:S(2)}) %collective-permute-start.25) | collective-permute-done | bytes 262176 | tf_op jit(solution)/shard_map/ppermute | solution.py:33
  122.1 5.4 %collective-permute-done.23 = f16[2,4,128,128]{3,2,1,0:T(8,128)(2,1)S(1)} collective-permute-done((f16[2,4,128,128]{3,2,1,0:T(8,128)(2,1)S(1)}, f16[2,4,128,128]{3,2,1,0:T(8,128)(2,1)S(1)}, u32[]{:S(2)}, u32[]{:S(2)}) %collective-permute-start.23) | collective-permute-done | bytes 262176 | tf_op jit(solution)/shard_map/ppermute | solution.py:33
  127.7 2.4 %collective-permute-start.26 = (f16[4,128,128]{2,1,0:T(8,128)(2,1)S(1)}, f16[4,128,128]{2,1,0:T(8,128)(2,1)S(1)}, u32[]{:S(2)}, u32[]{:S(2)}) collective-permute-start(f16[4,128,128]{2,1,0:T(8,128)(2,1)S(1)} %get-tuple-element.51), channel_id=1, source_target_pairs={{0,32},{4,36},{8,40},{12,44},{16,48},{20,52},{24,56},{28,60},{32,0... | collective-permute-start | bytes 393224 | tf_op jit(solution)/shard_map/ppermute | solution.py:33
  130.2 3.6 %collective-permute-done.26 = f16[4,128,128]{2,1,0:T(8,128)(2,1)S(1)} collective-permute-done((f16[4,128,128]{2,1,0:T(8,128)(2,1)S(1)}, f16[4,128,128]{2,1,0:T(8,128)(2,1)S(1)}, u32[]{:S(2)}, u32[]{:S(2)}) %collective-permute-start.26) | collective-permute-done | bytes 131104 | tf_op jit(solution)/shard_map/ppermute | solution.py:33
  133.9 3.3 %collective-permute-start.27 = (f16[2,128,128]{2,1,0:T(8,128)(2,1)S(1)}, f16[2,128,128]{2,1,0:T(8,128)(2,1)S(1)}, u32[]{:S(2)}, u32[]{:S(2)}) collective-permute-start(f16[2,128,128]{2,1,0:T(8,128)(2,1)S(1)} %fusion.4), channel_id=1, source_target_pairs={{0,64},{4,68},{8,72},{12,76},{16,80},{20,84},{24,88},{28,92},{32,9... | collective-permute-start | bytes 196616 | tf_op jit(solution)/shard_map/ppermute | solution.py:33
  137.2 2.6 %collective-permute-done.27 = f16[2,128,128]{2,1,0:T(8,128)(2,1)S(1)} collective-permute-done((f16[2,128,128]{2,1,0:T(8,128)(2,1)S(1)}, f16[2,128,128]{2,1,0:T(8,128)(2,1)S(1)}, u32[]{:S(2)}, u32[]{:S(2)}) %collective-permute-start.27) | collective-permute-done | bytes 65568 | tf_op jit(solution)/shard_map/ppermute | solution.py:33
  139.8 7.1 %collective-permute-start.28 = (f16[128,128]{1,0:T(8,128)(2,1)S(1)}, f16[128,128]{1,0:T(8,128)(2,1)S(1)}, u32[]{:S(2)}, u32[]{:S(2)}) collective-permute-start(f16[128,128]{1,0:T(8,128)(2,1)S(1)} %fusion.23), channel_id=1, source_target_pairs={{0,128},{4,132},{8,136},{12,140},{16,144},{20,148},{24,152},{28,15... | collective-permute-start | bytes 98312 | tf_op jit(solution)/shard_map/ppermute | solution.py:33
  146.9 1.9 %collective-permute-done.28 = f16[128,128]{1,0:T(8,128)(2,1)S(1)} collective-permute-done((f16[128,128]{1,0:T(8,128)(2,1)S(1)}, f16[128,128]{1,0:T(8,128)(2,1)S(1)}, u32[]{:S(2)}, u32[]{:S(2)}) %collective-permute-start.28) | collective-permute-done | bytes 32800 | tf_op jit(solution)/shard_map/ppermute | solution.py:33
  148.8 0.6 fusion.6
  (100 shorter events, 2.7 us)
Async XLA Ops:
  3.4 10.3 %copy-start.7 = (bf16[1024,256]{1,0:T(8,128)(2,1)}, bf16[1024,256]{1,0:T(8,128)(2,1)S(1)}, u32[]{:S(2)}) copy-start(bf16[1024,256]{1,0:T(8,128)(2,1)S(1)} %get-tuple-element.47.refs_0_.b0) | copy-start | bytes 1572868
  3.4 10.2 %copy-start.16 = (f32[128,128]{1,0:T(8,128)S(1)}, f32[128,128]{1,0:T(8,128)}, u32[]{:S(2)}) copy-start(f32[128,128]{1,0:T(8,128)} %a.1) | copy-start | bytes 196612
  3.4 28.0 %collective-permute-start.6 = (bf16[1024,256]{1,0:T(8,128)(2,1)}, bf16[1024,256]{1,0:T(8,128)(2,1)S(1)}, u32[]{:S(2)}, u32[]{:S(2)}) collective-permute-start(bf16[1024,256]{1,0:T(8,128)(2,1)} %get-tuple-element.44), channel_id=1, source_target_pairs={{0,3},{1,0},{2,1},{3,2},{4,7},{5,4},{6,5},{7,6},{8,11},{9,8},{10,9... | collective-permute-start | bytes 1572872 | tf_op jit(solution)/shard_map/ppermute | solution.py:37
  5.6 25.9 %collective-permute-start.5 = (bf16[1024,256]{1,0:T(8,128)(2,1)}, bf16[1024,256]{1,0:T(8,128)(2,1)S(1)}, u32[]{:S(2)}, u32[]{:S(2)}) collective-permute-start(bf16[1024,256]{1,0:T(8,128)(2,1)} %get-tuple-element.45), channel_id=1, source_target_pairs={{0,2},{1,3},{2,0},{3,1},{4,6},{5,7},{6,4},{7,5},{8,10},{9,11},{10,... | collective-permute-start | bytes 1572872 | tf_op jit(solution)/shard_map/ppermute | solution.py:37
  6.5 25.0 %collective-permute-start.4 = (bf16[1024,256]{1,0:T(8,128)(2,1)}, bf16[1024,256]{1,0:T(8,128)(2,1)}, u32[]{:S(2)}, u32[]{:S(2)}) collective-permute-start(bf16[1024,256]{1,0:T(8,128)(2,1)} %get-tuple-element.46), channel_id=1, source_target_pairs={{0,1},{1,2},{2,3},{3,0},{4,5},{5,6},{6,7},{7,4},{8,9},{9,10},{10,1... | collective-permute-start | bytes 1572872 | tf_op jit(solution)/shard_map/ppermute | solution.py:37
  8.4 8.8 %copy-start.17 = (f32[128,128]{1,0:T(8,128)S(1)}, f32[128,128]{1,0:T(8,128)}, u32[]{:S(2)}) copy-start(f32[128,128]{1,0:T(8,128)} %refs_0_.1) | copy-start | bytes 196612
  13.7 5.5 %copy-start.19 = (s32[8192]{0:T(1024)S(1)}, s32[8192]{0:T(1024)}, u32[]{:S(2)}) copy-start(s32[8192]{0:T(1024)} %param.8) | copy-start | bytes 98308
  13.7 5.7 %copy-start.20 = (s32[8192]{0:T(1024)S(1)}, s32[8192]{0:T(1024)}, u32[]{:S(2)}) copy-start(s32[8192]{0:T(1024)} %param.7) | copy-start | bytes 98308
  13.7 5.7 %collective-permute-start.2 = (s16[128,128]{1,0:T(8,128)(2,1)S(1)}, s16[128,128]{1,0:T(8,128)(2,1)S(1)}, u32[]{:S(2)}, u32[]{:S(2)}) collective-permute-start(s16[128,128]{1,0:T(8,128)(2,1)S(1)} %encode_terms.1.refs_0_), channel_id=1, source_target_pairs={{0,64},{4,68},{8,72},{12,76},{16,80},{20,84},{24,88},{28,92},{32,9... | collective-permute-start | bytes 98312 | tf_op jit(solution)/shard_map/ppermute | solution.py:33
  17.1 5.5 %collective-permute-start.1 = (f32[128,128]{1,0:T(8,128)S(1)}, f32[128,128]{1,0:T(8,128)S(1)}, u32[]{:S(2)}, u32[]{:S(2)}) collective-permute-start(f32[128,128]{1,0:T(8,128)S(1)} %join.8), channel_id=1, source_target_pairs={{4,0},{8,4},{12,8},{16,12},{20,16},{24,20},{28,24},{32,28},{36,32}... | collective-permute-start | bytes 196616 | tf_op jit(solution)/shard_map/ppermute | solution.py:280
  19.5 8.6 %collective-permute-start = (f32[128,128]{1,0:T(8,128)S(1)}, f32[128,128]{1,0:T(8,128)S(1)}, u32[]{:S(2)}, u32[]{:S(2)}) collective-permute-start(f32[128,128]{1,0:T(8,128)S(1)} %join.8), channel_id=1, source_target_pairs={{0,4},{4,8},{8,12},{12,16},{16,20},{20,24},{24,28},{28,32},{32,36}... | collective-permute-start | bytes 196616 | tf_op jit(solution)/shard_map/ppermute | solution.py:280
  22.6 8.9 %collective-permute-start.3 = (s16[256,128]{1,0:T(8,128)(2,1)S(1)}, s16[256,128]{1,0:T(8,128)(2,1)S(1)}, u32[]{:S(2)}, u32[]{:S(2)}) collective-permute-start(s16[256,128]{1,0:T(8,128)(2,1)S(1)} %join.9.refs_0_), channel_id=1, source_target_pairs={{0,128},{4,132},{8,136},{12,140},{16,144},{20,148},{24,152},{28,15... | collective-permute-start | bytes 196616 | tf_op jit(solution)/shard_map/ppermute | solution.py:33
  31.5 7.4 %collective-permute-start.7 = (s16[512,128]{1,0:T(8,128)(2,1)S(1)}, s16[512,128]{1,0:T(8,128)(2,1)S(1)}, u32[]{:S(2)}, u32[]{:S(2)}) collective-permute-start(s16[512,128]{1,0:T(8,128)(2,1)S(1)} %join.10.refs_0_), channel_id=1, source_target_pairs={{0,32},{4,36},{8,40},{12,44},{16,48},{20,52},{24,56},{28,60},{32,0... | collective-permute-start | bytes 393224 | tf_op jit(solution)/shard_map/ppermute | solution.py:33
  35.2 2.2 %copy-start = (bf16[8192,256]{1,0:T(8,128)(2,1)S(1)}, bf16[8192,256]{1,0:T(8,128)(2,1)}, u32[]{:S(2)}) copy-start(bf16[8192,256]{1,0:T(8,128)(2,1)} %traces.1) | copy-start | bytes 12582916
  37.4 7.6 %copy-start.8 = (bf16[1024,256]{1,0:T(8,128)(2,1)S(1)}, bf16[1024,256]{1,0:T(8,128)(2,1)}, u32[]{:S(2)}) copy-start(bf16[1024,256]{1,0:T(8,128)(2,1)} %copy-done.7) | copy-start | bytes 1572868
  39.7 9.9 %collective-permute-start.8 = (s16[1024,128]{1,0:T(8,128)(2,1)S(1)}, s16[1024,128]{1,0:T(8,128)(2,1)S(1)}, u32[]{:S(2)}, u32[]{:S(2)}) collective-permute-start(s16[1024,128]{1,0:T(8,128)(2,1)S(1)} %join.11.refs_0_), channel_id=1, source_target_pairs={{0,8},{4,12},{8,0},{12,4},{16,24},{20,28},{24,16},{28,20},{32,40},... | collective-permute-start | bytes 786440 | tf_op jit(solution)/shard_map/ppermute | solution.py:33
  41.0 18.8 %collective-permute-start.10 = (bf16[1024,256]{1,0:T(8,128)(2,1)S(1)}, bf16[1024,256]{1,0:T(8,128)(2,1)S(1)}, u32[]{:S(2)}, u32[]{:S(2)}) collective-permute-start(bf16[1024,256]{1,0:T(8,128)(2,1)S(1)} %get-tuple-element.25), channel_id=1, source_target_pairs={{0,1},{1,2},{2,3},{3,0},{4,5},{5,6},{6,7},{7,4},{8,9},{9,10},{10,1... | collective-permute-start | bytes 1572872 | tf_op jit(solution)/shard_map/ppermute | solution.py:37
  41.1 18.7 %collective-permute-start.11 = (bf16[1024,256]{1,0:T(8,128)(2,1)S(1)}, bf16[1024,256]{1,0:T(8,128)(2,1)S(1)}, u32[]{:S(2)}, u32[]{:S(2)}) collective-permute-start(bf16[1024,256]{1,0:T(8,128)(2,1)S(1)} %get-tuple-element.26), channel_id=1, source_target_pairs={{0,2},{1,3},{2,0},{3,1},{4,6},{5,7},{6,4},{7,5},{8,10},{9,11},{10,... | collective-permute-start | bytes 1572872 | tf_op jit(solution)/shard_map/ppermute | solution.py:37
  43.6 23.5 %collective-permute-start.12 = (bf16[1024,256]{1,0:T(8,128)(2,1)S(1)}, bf16[1024,256]{1,0:T(8,128)(2,1)S(1)}, u32[]{:S(2)}, u32[]{:S(2)}) collective-permute-start(bf16[1024,256]{1,0:T(8,128)(2,1)S(1)} %get-tuple-element.27), channel_id=1, source_target_pairs={{0,3},{1,0},{2,1},{3,2},{4,7},{5,4},{6,5},{7,6},{8,11},{9,8},{10,9... | collective-permute-start | bytes 1572872 | tf_op jit(solution)/shard_map/ppermute | solution.py:37
  49.6 2.0 %copy-start.18 = (s16[1024,128]{1,0:T(8,128)(2,1)}, s16[1024,128]{1,0:T(8,128)(2,1)S(1)}, u32[]{:S(2)}) copy-start(s16[1024,128]{1,0:T(8,128)(2,1)S(1)} %get-tuple-element.30) | copy-start | bytes 786436
  49.6 17.5 %collective-permute-start.9 = (s16[2048,128]{1,0:T(8,128)(2,1)S(1)}, s16[2048,128]{1,0:T(8,128)(2,1)S(1)}, u32[]{:S(2)}, u32[]{:S(2)}) collective-permute-start(s16[2048,128]{1,0:T(8,128)(2,1)S(1)} %join.12.refs_0_), channel_id=1, source_target_pairs={{0,16},{4,20},{8,24},{12,28},{16,0},{20,4},{24,8},{28,12},{32,48},... | collective-permute-start | bytes 1572872 | tf_op jit(solution)/shard_map/ppermute | solution.py:33
  59.8 7.4 %copy-start.1 = (f32[4096,128]{1,0:T(8,128)}, f32[4096,128]{1,0:T(8,128)S(1)}, u32[]{:S(2)}) copy-start(f32[4096,128]{1,0:T(8,128)S(1)} %get-tuple-element.22.refs_2_) | copy-start | bytes 6291460
  59.8 7.4 %copy-start.3 = (f32[4096,128]{1,0:T(8,128)}, f32[4096,128]{1,0:T(8,128)S(1)}, u32[]{:S(2)}) copy-start(f32[4096,128]{1,0:T(8,128)S(1)} %get-tuple-element.32.refs_2_) | copy-start | bytes 6291460
  59.8 7.4 %copy-start.9 = (bf16[1024,256]{1,0:T(8,128)(2,1)}, bf16[1024,256]{1,0:T(8,128)(2,1)S(1)}, u32[]{:S(2)}) copy-start(bf16[1024,256]{1,0:T(8,128)(2,1)S(1)} %collective-permute-done.10.refs_4_.b1) | copy-start | bytes 1572868
  59.8 7.4 %copy-start.11 = (bf16[1024,256]{1,0:T(8,128)(2,1)}, bf16[1024,256]{1,0:T(8,128)(2,1)S(1)}, u32[]{:S(2)}) copy-start(bf16[1024,256]{1,0:T(8,128)(2,1)S(1)} %collective-permute-done.11.refs_5_.b2) | copy-start | bytes 1572868
  67.9 17.6 %collective-permute-start.13 = (s16[4096,128]{1,0:T(8,128)(2,1)S(1)}, s16[4096,128]{1,0:T(8,128)(2,1)}, u32[]{:S(2)}, u32[]{:S(2)}) collective-permute-start(s16[4096,128]{1,0:T(8,128)(2,1)S(1)} %join.13.refs_3_), channel_id=1, source_target_pairs={{0,4},{4,0},{8,12},{12,8},{16,20},{20,16},{24,28},{28,24},{32,36},... | collective-permute-start | bytes 3145736 | tf_op jit(solution)/shard_map/ppermute | solution.py:33
  67.9 12.1 %collective-permute-start.14 = (s16[1024,128]{1,0:T(8,128)(2,1)}, s16[1024,128]{1,0:T(8,128)(2,1)}, u32[]{:S(2)}, u32[]{:S(2)}) collective-permute-start(s16[1024,128]{1,0:T(8,128)(2,1)} %get-tuple-element.28), channel_id=1, source_target_pairs={{0,1},{1,2},{2,3},{3,0},{4,5},{5,6},{6,7},{7,4},{8,9},{9,10},{10,1... | collective-permute-start | bytes 786440 | tf_op jit(solution)/shard_map/ppermute | solution.py:37
  68.5 14.4 %collective-permute-start.15 = (s16[1024,128]{1,0:T(8,128)(2,1)}, s16[1024,128]{1,0:T(8,128)(2,1)}, u32[]{:S(2)}, u32[]{:S(2)}) collective-permute-start(s16[1024,128]{1,0:T(8,128)(2,1)} %get-tuple-element.29), channel_id=1, source_target_pairs={{0,2},{1,3},{2,0},{3,1},{4,6},{5,7},{6,4},{7,5},{8,10},{9,11},{10,... | collective-permute-start | bytes 786440 | tf_op jit(solution)/shard_map/ppermute | solution.py:37
  70.5 15.0 %copy-start.2 = (f32[4096,128]{1,0:T(8,128)S(1)}, f32[4096,128]{1,0:T(8,128)}, u32[]{:S(2)}) copy-start(f32[4096,128]{1,0:T(8,128)} %copy-done.1) | copy-start | bytes 6291460
  70.5 15.0 %collective-permute-start.16 = (s16[1024,128]{1,0:T(8,128)(2,1)}, s16[1024,128]{1,0:T(8,128)(2,1)S(1)}, u32[]{:S(2)}, u32[]{:S(2)}) collective-permute-start(s16[1024,128]{1,0:T(8,128)(2,1)} %copy-done.18), channel_id=1, source_target_pairs={{0,3},{1,0},{2,1},{3,2},{4,7},{5,4},{6,5},{7,6},{8,11},{9,8},{10,9... | collective-permute-start | bytes 786440 | tf_op jit(solution)/shard_map/ppermute | solution.py:37
  72.7 1.0 copy-start.6
  73.8 1.0 copy-start.10
  74.8 1.0 copy-start.12
  75.9 1.0 copy-start.14
  79.9 16.3 %collective-permute-start.17 = (s16[1024,128]{1,0:T(8,128)(2,1)S(1)}, s16[1024,128]{1,0:T(8,128)(2,1)S(1)}, u32[]{:S(2)}, u32[]{:S(2)}) collective-permute-start(s16[1024,128]{1,0:T(8,128)(2,1)S(1)} %get-tuple-element.34), channel_id=1, source_target_pairs={{0,1},{1,2},{2,3},{3,0},{4,5},{5,6},{6,7},{7,4},{8,9},{9,10},{10,1... | collective-permute-start | bytes 786440 | tf_op jit(solution)/shard_map/ppermute | solution.py:37
  80.0 16.2 %collective-permute-start.18 = (s16[1024,128]{1,0:T(8,128)(2,1)S(1)}, s16[1024,128]{1,0:T(8,128)(2,1)S(1)}, u32[]{:S(2)}, u32[]{:S(2)}) collective-permute-start(s16[1024,128]{1,0:T(8,128)(2,1)S(1)} %get-tuple-element.35), channel_id=1, source_target_pairs={{0,2},{1,3},{2,0},{3,1},{4,6},{5,7},{6,4},{7,5},{8,10},{9,11},{10,... | collective-permute-start | bytes 786440 | tf_op jit(solution)/shard_map/ppermute | solution.py:37
  82.9 13.4 %collective-permute-start.19 = (s16[1024,128]{1,0:T(8,128)(2,1)S(1)}, s16[1024,128]{1,0:T(8,128)(2,1)S(1)}, u32[]{:S(2)}, u32[]{:S(2)}) collective-permute-start(s16[1024,128]{1,0:T(8,128)(2,1)S(1)} %get-tuple-element.36), channel_id=1, source_target_pairs={{0,3},{1,0},{2,1},{3,2},{4,7},{5,4},{6,5},{7,6},{8,11},{9,8},{10,9... | collective-permute-start | bytes 786440 | tf_op jit(solution)/shard_map/ppermute | solution.py:37
  85.5 10.8 %copy-start.4 = (f32[4096,128]{1,0:T(8,128)S(1)}, f32[4096,128]{1,0:T(8,128)}, u32[]{:S(2)}) copy-start(f32[4096,128]{1,0:T(8,128)} %copy-done.3) | copy-start | bytes 6291460
  106.7 4.2 %collective-permute-start.22 = (f32[4096,128]{1,0:T(8,128)S(1)}, f32[4096,128]{1,0:T(8,128)S(1)}, u32[]{:S(2)}, u32[]{:S(2)}) collective-permute-start(f32[4096,128]{1,0:T(8,128)S(1)} %get-tuple-element.41), channel_id=1, source_target_pairs={{0,4},{4,0},{8,12},{12,8},{16,20},{20,16},{24,28},{28,24},{32,36},... | collective-permute-start | bytes 6291464 | tf_op jit(solution)/shard_map/ppermute | solution.py:33
  111.4 10.8 %collective-permute-start.25 = (f16[2,4,128,128]{3,2,1,0:T(8,128)(2,1)S(1)}, f16[2,4,128,128]{3,2,1,0:T(8,128)(2,1)S(1)}, u32[]{:S(2)}, u32[]{:S(2)}) collective-permute-start(f16[2,4,128,128]{3,2,1,0:T(8,128)(2,1)S(1)} %bitcast.66), channel_id=1, source_target_pairs={{0,16},{4,20},{8,24},{12,28},{16,0},{20,4},{24,8},{28,12},{32,48},... | collective-permute-start | bytes 786440 | tf_op jit(solution)/shard_map/ppermute | solution.py:33
  114.3 13.2 %collective-permute-start.23 = (f16[2,4,128,128]{3,2,1,0:T(8,128)(2,1)S(1)}, f16[2,4,128,128]{3,2,1,0:T(8,128)(2,1)S(1)}, u32[]{:S(2)}, u32[]{:S(2)}) collective-permute-start(f16[2,4,128,128]{3,2,1,0:T(8,128)(2,1)S(1)} %bitcast.65), channel_id=1, source_target_pairs={{0,8},{4,12},{8,0},{12,4},{16,24},{20,28},{24,16},{28,20},{32,40},... | collective-permute-start | bytes 786440 | tf_op jit(solution)/shard_map/ppermute | solution.py:33
  115.6 12.0 %collective-permute-start.24 = (f16[2,4,128,128]{3,2,1,0:T(8,128)(2,1)S(1)}, f16[2,4,128,128]{3,2,1,0:T(8,128)(2,1)S(1)}, u32[]{:S(2)}, u32[]{:S(2)}) collective-permute-start(f16[2,4,128,128]{3,2,1,0:T(8,128)(2,1)S(1)} %bitcast.64), channel_id=1, source_target_pairs={{0,24},{4,28},{8,16},{12,20},{16,8},{20,12},{24,0},{28,4},{32,56},... | collective-permute-start | bytes 786440 | tf_op jit(solution)/shard_map/ppermute | solution.py:33
  117.4 12.7 %collective-permute-start.20 = (f32[128,128]{1,0:T(8,128)S(1)}, f32[128,128]{1,0:T(8,128)S(1)}, u32[]{:S(2)}, u32[]{:S(2)}) collective-permute-start(f32[128,128]{1,0:T(8,128)S(1)} %get-tuple-element.53), channel_id=1, source_target_pairs={{0,4},{4,8},{8,12},{12,16},{16,20},{20,24},{24,28},{28,32},{32,36}... | collective-permute-start | bytes 196616 | tf_op jit(solution)/shard_map/ppermute | solution.py:280
  118.9 11.2 %collective-permute-start.21 = (f32[128,128]{1,0:T(8,128)S(1)}, f32[128,128]{1,0:T(8,128)S(1)}, u32[]{:S(2)}, u32[]{:S(2)}) collective-permute-start(f32[128,128]{1,0:T(8,128)S(1)} %get-tuple-element.54), channel_id=1, source_target_pairs={{4,0},{8,4},{12,8},{16,12},{20,16},{24,20},{28,24},{32,28},{36,32}... | collective-permute-start | bytes 196616 | tf_op jit(solution)/shard_map/ppermute | solution.py:280
  127.7 6.1 %collective-permute-start.26 = (f16[4,128,128]{2,1,0:T(8,128)(2,1)S(1)}, f16[4,128,128]{2,1,0:T(8,128)(2,1)S(1)}, u32[]{:S(2)}, u32[]{:S(2)}) collective-permute-start(f16[4,128,128]{2,1,0:T(8,128)(2,1)S(1)} %get-tuple-element.51), channel_id=1, source_target_pairs={{0,32},{4,36},{8,40},{12,44},{16,48},{20,52},{24,56},{28,60},{32,0... | collective-permute-start | bytes 393224 | tf_op jit(solution)/shard_map/ppermute | solution.py:33
  130.1 19.3 %copy-start.15 = (f32[128,128]{1,0:T(8,128)}, f32[128,128]{1,0:T(8,128)S(1)}, u32[]{:S(2)}) copy-start(f32[128,128]{1,0:T(8,128)S(1)} %fusion.7.refs_1_) | copy-start | bytes 196612
  133.9 5.9 %collective-permute-start.27 = (f16[2,128,128]{2,1,0:T(8,128)(2,1)S(1)}, f16[2,128,128]{2,1,0:T(8,128)(2,1)S(1)}, u32[]{:S(2)}, u32[]{:S(2)}) collective-permute-start(f16[2,128,128]{2,1,0:T(8,128)(2,1)S(1)} %fusion.4), channel_id=1, source_target_pairs={{0,64},{4,68},{8,72},{12,76},{16,80},{20,84},{24,88},{28,92},{32,9... | collective-permute-start | bytes 196616 | tf_op jit(solution)/shard_map/ppermute | solution.py:33
  139.8 9.0 %collective-permute-start.28 = (f16[128,128]{1,0:T(8,128)(2,1)S(1)}, f16[128,128]{1,0:T(8,128)(2,1)S(1)}, u32[]{:S(2)}, u32[]{:S(2)}) collective-permute-start(f16[128,128]{1,0:T(8,128)(2,1)S(1)} %fusion.23), channel_id=1, source_target_pairs={{0,128},{4,132},{8,136},{12,140},{16,144},{20,148},{24,152},{28,15... | collective-permute-start | bytes 98312 | tf_op jit(solution)/shard_map/ppermute | solution.py:33
  (2 other events, 1.6 us)

commit v9 on v8

--- a/solution.py
+++ b/solution.py
@@ -14,11 +14,9 @@
 REC_SCALE = 65535.0 / (REC_HIGH - REC_LOW)
 SUM_SCALE = 1.0 / 32.0
 PIECES = (1024, 1024)
-LARGE = pltpu.CompilerParams(vmem_limit_bytes=60 * 2**20)
 SUMS = pltpu.CompilerParams(vmem_limit_bytes=32 * 2**20)
 SMALL = pltpu.CompilerParams(vmem_limit_bytes=12 * 2**20)
 COST = pl.CostEstimate(flops=1000, bytes_accessed=1000, transcendentals=0)
-MEDIUM = pltpu.CompilerParams(vmem_limit_bytes=18 * 2**20)
 
 
 def tr_of(z, x, c):
@@ -93,33 +91,6 @@
     )(*parts, *after)
 
 
-def take_rows(traces, y, first, size, after=()):
-    rows, part = traces.shape
-
-    def body(y_ref, traces, *refs):
-        outs, sems = refs[len(after) : len(after) + NY], refs[len(after) + NY :]
-        copies = []
-        for k in range(NY):
-            at = pl.multiple_of((y_ref[0] + k) % NY * (rows // NY) + first, 16)
-            copies.append(pltpu.make_async_copy(traces.at[pl.ds(at, size), :], outs[k], sems[k]))
-        for copy in copies:
-            copy.start()
-        for copy in copies:
-            copy.wait()
-
-    hbm, vm = pl.BlockSpec(memory_space=pl.ANY), pl.BlockSpec(memory_space=pltpu.VMEM)
-    return pl.pallas_call(
-        body,
-        in_specs=[pl.BlockSpec(memory_space=pltpu.SMEM), hbm] + [hbm] * len(after),
-        out_specs=[vm] * NY,
-        out_shape=[jax.ShapeDtypeStruct((size, part), traces.dtype)] * NY,
-        scratch_shapes=[pltpu.SemaphoreType.DMA] * NY,
-        compiler_params=SMALL,
-        cost_estimate=COST,
-        name="take_rows",
-    )(y[None], traces, *after)
-
-
 def encode_terms(terms, after):
     def body(a, *refs):
         b = refs[-1]
@@ -160,7 +131,7 @@
         in_specs=[pl.BlockSpec((tile, part), lambda i: (i, 0))] * NY + [pl.BlockSpec(table.shape, lambda i: (0, 0))],
         out_specs=[pl.BlockSpec((tile, width), lambda i: (i, 0))] * NY,
         out_shape=[jax.ShapeDtypeStruct((rows, width), jnp.int16)] * NY,
-        compiler_params=MEDIUM,
+        compiler_params=SMALL,
         cost_estimate=COST,
         name="spectra",
     )(*blocks, table)
@@ -188,7 +159,7 @@
         in_specs=[sm, vm],
         out_specs=[vm] * len(sizes),
         out_shape=[jax.ShapeDtypeStruct((size, width), jnp.float32) for size in sizes],
-        compiler_params=MEDIUM,
+        compiler_params=SMALL,
         cost_estimate=COST,
         name="gather_shots",
     )(shot_at, shot_near)
@@ -269,7 +240,7 @@
         in_specs=[vm] * (1 + len(residuals)),
         out_specs=vm,
         out_shape=jax.ShapeDtypeStruct((count, width), jnp.float32),
-        compiler_params=MEDIUM,
+        compiler_params=SMALL,
         cost_estimate=COST,
         name="sum_shots",
     )(shot_at[None, :], *residuals)
@@ -288,15 +259,11 @@
     owner, y = lax.axis_index("tr"), lax.axis_index("fq")
     z, x, c = owner // (NX * NC), owner // NC % NX, owner % NC
 
-    got, after = [], ()
+    got = []
     for at, size in zip(first, PIECES):
-        if after:
-            mine = take_rows(traces, y, at, size, after)
-        else:
-            mine = [lax.dynamic_slice_in_dim(traces, (y + k) % NY * share + at, size, 0) for k in range(NY)]
+        mine = [lax.dynamic_slice_in_dim(traces, (y + k) % NY * share + at, size, 0) for k in range(NY)]
         come = {k: send_y(mine[k], k) for k in (1, 3, 2)}
-        after = [come[k] for k in range(1, NY)]
-        got.append([mine[0]] + after)
+        got.append([mine[0]] + [come[k] for k in range(1, NY)])
     table = make_table(part * NY, y, width, got[0][:1])
     codes, coded = [], []
     for blocks in got:
@@ -323,7 +290,7 @@
     terms = encode_terms(receiver_terms, (table,))
     terms = join([terms, swap(terms, 2, 0, 0)])
     terms = join([terms, swap(terms, 4, 0, 0)], got[0][1:] + [shot_near])
-    terms = join([terms, swap(terms, 1, 0, 0)], got[1][:1])
+    terms = join([terms, swap(terms, 1, 0, 0)])
     shots = gather_shots(shot_near, shot_at, [size * NY for size in PIECES])
     terms = join([terms, swap(terms, 0, 1, 0)], [coded[0][0]])
     terms = join([terms, swap(terms, 0, 2, 0)], [shots[0], rec_at] + got[1][1:])

time: 150 us -> 154 us (1.027); the launches traced: 149 us -> 152 us
  starting transfers between devices: 59 us -> 66.1 us
  waiting for transfers between devices: 31.5 us -> 26.4 us
    ppermute x12, waiting for transfers between devices: 7.29 us -> 0.03 us  [send_y(): return lax.ppermute(value, 'fq', [(i, (i + k) % NY) for i in range(NY)])]
    ppermute x13, starting transfers between devices: 32.8 us -> 36.8 us  [swap(): lax.ppermute(value, 'tr', [(tr_of(z, x, c), tr_of(z ^ dz, x ^ dx, c ^ dc)...]
    ppermute x12, starting transfers between devices: 19 us -> 22.2 us  [send_y(): return lax.ppermute(value, 'fq', [(i, (i + k) % NY) for i in range(NY)])]
    ppermute x13, waiting for transfers between devices: 24.2 us -> 26.3 us  [swap(): lax.ppermute(value, 'tr', [(tr_of(z, x, c), tr_of(z ^ dz, x ^ dx, c ^ dc)...]
    unnamed x47 -> x43, local copies, waits for them, and re-layouts: 7.93 us -> 6.93 us
  transfers between devices with their start and end apart: 29 -> 29, of which waited for: 9 -> 11; matrix products, arithmetic and copies ran while one was open for 0% -> 0% of each run, Pallas kernels for 23% -> 22%
where the time goes in v9:
time: 154 us; the launch traced here: 152 us
  starting transfers between devices  66.1 us (43%)
  Pallas kernels  44.5 us (29%)
  waiting for transfers between devices  26.4 us (17%)
  local copies, waits for them, and re-layouts  11.4 us (7%)
  between operations  1.99 us (1%)
    ppermute x13, starting transfers between devices, swap(): lax.ppermute(value, 'tr', [(tr_of(z, x, c), tr_of(z ^ dz, x ^ dx, c ^ dc)...  36.8 us
    ppermute x13, waiting for transfers between devices, swap(): lax.ppermute(value, 'tr', [(tr_of(z, x, c), tr_of(z ^ dz, x ^ dx, c ^ dc)...  26.3 us
    ppermute x12, starting transfers between devices, send_y(): return lax.ppermute(value, 'fq', [(i, (i + k) % NY) for i in range(NY)])  22.2 us
    pallas_call x2, Pallas kernels, sum_receivers(): pl.pallas_call(body, in_specs=[sm, sm] + [vm] * (3 + parts + held), out_s...  21.5 us
    pallas_call x1, Pallas kernels, gather_shots(): pl.pallas_call(body, in_specs=[sm, vm], out_specs=[vm] * len(sizes), out_...  8.11 us
    pallas_call x2, Pallas kernels, spectra(): pl.pallas_call(body, grid=(rows // tile,), in_specs=[pl.BlockSpec((tile,...  7.62 us
    ppermute x4, starting transfers between devices, neighbour(): lax.ppermute(value, 'tr', [(i, i + by) for i in range(size) if 0 <= i + b...  7.04 us
    unnamed x43, local copies, waits for them, and re-layouts  6.93 us
  transfers between devices with their start and end apart: 29, of which 11 were waited for; matrix products, arithmetic and copies ran while one was open for 0% of the time, Pallas kernels for 22%

profile of v9, /device:TPU:8, one launch (start us, length us, event | category | flops | bytes accessed | tf_op | source)
XLA Modules:
  0.0 151.8 jit_solution(7207300144173291365)
XLA Ops:
  0.7 4.0 %constant_dynamic-slice_fusion = (bf16[1024,256]{1,0:T(8,128)(2,1)}, bf16[1024,256]{1,0:T(8,128)(2,1)}, bf16[1024,256]{1,0:T(8,128)(2,1)}, bf16[1024,256]{1,0:T(...) fusion(bf16[8192,256]{1,0:T(8,128)(2,1)} %param.6, ...), kind=kLoop, calls=%fused_computation.74 | loop fusion | bytes 8388640 | tf_op jit(solution)/shard_map/dynamic_slice | solution.py:264
  4.7 2.3 %collective-permute-start.6 = (bf16[1024,256]{1,0:T(8,128)(2,1)}, bf16[1024,256]{1,0:T(8,128)(2,1)S(1)}, u32[]{:S(2)}, u32[]{:S(2)}) collective-permute-start(bf16[1024,256]{1,0:T(8,128)(2,1)} %get-tuple-element.39), channel_id=1, source_target_pairs={{0,3},{1,0},{2,1},{3,2},{4,7},{5,4},{6,5},{7,6},{8,11},{9,8},{10,9... | collective-permute-start | bytes 1572872 | tf_op jit(solution)/shard_map/ppermute | solution.py:35
  7.0 0.9 collective-permute-start.5
  7.8 1.9 %collective-permute-start.4 = (bf16[1024,256]{1,0:T(8,128)(2,1)}, bf16[1024,256]{1,0:T(8,128)(2,1)}, u32[]{:S(2)}, u32[]{:S(2)}) collective-permute-start(bf16[1024,256]{1,0:T(8,128)(2,1)} %get-tuple-element.41), channel_id=1, source_target_pairs={{0,1},{1,2},{2,3},{3,0},{4,5},{5,6},{6,7},{7,4},{8,9},{9,10},{10,1... | collective-permute-start | bytes 1572872 | tf_op jit(solution)/shard_map/ppermute | solution.py:35
  9.7 5.3 %make_table.1.refs_1_.refs_0_.t = bf16[1024,1024]{1,0:T(8,128)(2,1)S(1)} custom-call(s32[1]{0:T(128)} %bitcast.10.y_ref, bf16[1024,256]{1,0:T(8,128)(2,1)S(1)} %get-tuple-element.42.refs_0_.b0), custom_call_target="tpu_custom_call" | custom-call | flops 1073741824 | bytes 33554432 | tf_op jit(solution)/shard_map/make_table/pallas_call | solution.py:62
  15.1 3.4 %collective-permute-start.2 = (s16[128,128]{1,0:T(8,128)(2,1)S(1)}, s16[128,128]{1,0:T(8,128)(2,1)S(1)}, u32[]{:S(2)}, u32[]{:S(2)}) collective-permute-start(s16[128,128]{1,0:T(8,128)(2,1)S(1)} %encode_terms.1.refs_0_), channel_id=1, source_target_pairs={{0,64},{4,68},{8,72},{12,76},{16,80},{20,84},{24,88},{28,92},{32,9... | collective-permute-start | bytes 98312 | tf_op jit(solution)/shard_map/ppermute | solution.py:31
  18.5 1.3 collective-permute-start.1
  20.9 3.2 %collective-permute-start = (f32[128,128]{1,0:T(8,128)S(1)}, f32[128,128]{1,0:T(8,128)S(1)}, u32[]{:S(2)}, u32[]{:S(2)}) collective-permute-start(f32[128,128]{1,0:T(8,128)S(1)} %join.8), channel_id=1, source_target_pairs={{0,4},{4,8},{8,12},{12,16},{16,20},{20,24},{24,28},{28,32},{32,36}... | collective-permute-start | bytes 196616 | tf_op jit(solution)/shard_map/ppermute | solution.py:251
  24.1 1.3 collective-permute-start.11
  25.4 10.7 %collective-permute-start.3 = (s16[256,128]{1,0:T(8,128)(2,1)S(1)}, s16[256,128]{1,0:T(8,128)(2,1)S(1)}, u32[]{:S(2)}, u32[]{:S(2)}) collective-permute-start(s16[256,128]{1,0:T(8,128)(2,1)S(1)} %join.9.refs_0_), channel_id=1, source_target_pairs={{0,128},{4,132},{8,136},{12,140},{16,144},{20,148},{24,152},{28,15... | collective-permute-start | bytes 196616 | tf_op jit(solution)/shard_map/ppermute | solution.py:31
  36.1 2.5 %collective-permute-done.3.refs_1_ = s16[256,128]{1,0:T(8,128)(2,1)S(1)} collective-permute-done((s16[256,128]{1,0:T(8,128)(2,1)S(1)}, s16[256,128]{1,0:T(8,128)(2,1)S(1)}, u32[]{:S(2)}, u32[]{:S(2)}) %collective-permute-start.3) | collective-permute-done | bytes 65568 | tf_op jit(solution)/shard_map/ppermute | solution.py:31
  38.6 3.6 %collective-permute-start.12 = (bf16[1024,256]{1,0:T(8,128)(2,1)}, bf16[1024,256]{1,0:T(8,128)(2,1)S(1)}, u32[]{:S(2)}, u32[]{:S(2)}) collective-permute-start(bf16[1024,256]{1,0:T(8,128)(2,1)} %get-tuple-element.43), channel_id=1, source_target_pairs={{0,3},{1,0},{2,1},{3,2},{4,7},{5,4},{6,5},{7,6},{8,11},{9,8},{10,9... | collective-permute-start | bytes 1572872 | tf_op jit(solution)/shard_map/ppermute | solution.py:35
  42.2 2.0 %collective-permute-start.7 = (s16[512,128]{1,0:T(8,128)(2,1)S(1)}, s16[512,128]{1,0:T(8,128)(2,1)S(1)}, u32[]{:S(2)}, u32[]{:S(2)}) collective-permute-start(s16[512,128]{1,0:T(8,128)(2,1)S(1)} %join.10.refs_0_), channel_id=1, source_target_pairs={{0,32},{4,36},{8,40},{12,44},{16,48},{20,52},{24,56},{28,60},{32,0... | collective-permute-start | bytes 393224 | tf_op jit(solution)/shard_map/ppermute | solution.py:31
  44.3 3.0 %collective-permute-done.7.refs_1_ = s16[512,128]{1,0:T(8,128)(2,1)S(1)} collective-permute-done((s16[512,128]{1,0:T(8,128)(2,1)S(1)}, s16[512,128]{1,0:T(8,128)(2,1)S(1)}, u32[]{:S(2)}, u32[]{:S(2)}) %collective-permute-start.7) | collective-permute-done | bytes 131104 | tf_op jit(solution)/shard_map/ppermute | solution.py:31
  47.3 1.6 %collective-permute-start.8 = (s16[1024,128]{1,0:T(8,128)(2,1)S(1)}, s16[1024,128]{1,0:T(8,128)(2,1)S(1)}, u32[]{:S(2)}, u32[]{:S(2)}) collective-permute-start(s16[1024,128]{1,0:T(8,128)(2,1)S(1)} %join.11.refs_0_), channel_id=1, source_target_pairs={{0,8},{4,12},{8,0},{12,4},{16,24},{20,28},{24,16},{28,20},{32,40},... | collective-permute-start | bytes 786440 | tf_op jit(solution)/shard_map/ppermute | solution.py:31
  49.0 4.6 %spectra.2 = (s16[1024,128]{1,0:T(8,128)(2,1)S(1)}, s16[1024,128]{1,0:T(8,128)(2,1)}, s16[1024,128]{1,0:T(8,128)(2,1)}, s16[1024,128]{1,0:T(8,128)(2,1)S(1)}) custom-call(bf16[1024,256]{1,0:T(8,128)(2,1)S(1)} %copy-done.12, bf16[1024,256]{1,0:T(8,128)(2,1)} %collective-permute-done.4.refs_2_.b1, bf16[1024,256]{1,0:T(8,128)(2,1)S(1)} %collective-permute-done.5.refs_3_.b2, ...), custom_call_target="tpu_custom_call" | custom-call | flops 1000 | bytes 1000 | tf_op jit(solution)/shard_map/spectra/pallas_call | solution.py:128
  53.6 1.3 collective-permute-done.8.refs_1_
  55.0 2.3 %collective-permute-start.9 = (s16[2048,128]{1,0:T(8,128)(2,1)S(1)}, s16[2048,128]{1,0:T(8,128)(2,1)S(1)}, u32[]{:S(2)}, u32[]{:S(2)}) collective-permute-start(s16[2048,128]{1,0:T(8,128)(2,1)S(1)} %join.12.refs_0_), channel_id=1, source_target_pairs={{0,16},{4,20},{8,24},{12,28},{16,0},{20,4},{24,8},{28,12},{32,48},... | collective-permute-start | bytes 1572872 | tf_op jit(solution)/shard_map/ppermute | solution.py:31
  57.3 8.1 %gather_shots.1 = (f32[4096,128]{1,0:T(8,128)S(1)}, f32[4096,128]{1,0:T(8,128)S(1)}) custom-call(s32[8192]{0:T(1024)S(1)} %bitcast_dynamic-update-slice_fusion.shot_at, f32[384,128]{1,0:T(8,128)S(1)} %pad_maximum_fusion.shot.refs_5_), custom_call_target="tpu_custom_call" | custom-call | flops 1000 | bytes 1000 | tf_op jit(solution)/shard_map/gather_shots/pallas_call | solution.py:157
  65.5 1.4 copy-done.2
  67.3 0.9 copy-done
  68.6 5.4 %collective-permute-start.15 = (s16[1024,128]{1,0:T(8,128)(2,1)}, s16[1024,128]{1,0:T(8,128)(2,1)}, u32[]{:S(2)}, u32[]{:S(2)}) collective-permute-start(s16[1024,128]{1,0:T(8,128)(2,1)} %get-tuple-element.21), channel_id=1, source_target_pairs={{0,2},{1,3},{2,0},{3,1},{4,6},{5,7},{6,4},{7,5},{8,10},{9,11},{10,... | collective-permute-start | bytes 786440 | tf_op jit(solution)/shard_map/ppermute | solution.py:35
  74.1 1.0 copy-done.5
  75.2 1.0 copy-done.7
  76.2 1.0 copy-done.9
  77.2 1.0 copy-done.10
  78.3 3.0 %spectra.3 = (s16[1024,128]{1,0:T(8,128)(2,1)S(1)}, s16[1024,128]{1,0:T(8,128)(2,1)S(1)}, s16[1024,128]{1,0:T(8,128)(2,1)S(1)}, s16[1024,128]{1,0:T(8,128)(2,1)S(1)}) custom-call(bf16[1024,256]{1,0:T(8,128)(2,1)S(1)} %copy-done.10, bf16[1024,256]{1,0:T(8,128)(2,1)S(1)} %copy-done.7, bf16[1024,256]{1,0:T(8,128)(2,1)S(1)} %copy-done.5, ...), custom_call_target="tpu_custom_call" | custom-call | flops 1000 | bytes 1000 | tf_op jit(solution)/shard_map/spectra/pallas_call | solution.py:128
  81.3 2.1 %collective-permute-start.17 = (s16[1024,128]{1,0:T(8,128)(2,1)S(1)}, s16[1024,128]{1,0:T(8,128)(2,1)S(1)}, u32[]{:S(2)}, u32[]{:S(2)}) collective-permute-start(s16[1024,128]{1,0:T(8,128)(2,1)S(1)} %get-tuple-element.26), channel_id=1, source_target_pairs={{0,1},{1,2},{2,3},{3,0},{4,5},{5,6},{6,7},{7,4},{8,9},{9,10},{10,1... | collective-permute-start | bytes 786440 | tf_op jit(solution)/shard_map/ppermute | solution.py:35
  83.4 3.2 %collective-permute-start.18 = (s16[1024,128]{1,0:T(8,128)(2,1)S(1)}, s16[1024,128]{1,0:T(8,128)(2,1)S(1)}, u32[]{:S(2)}, u32[]{:S(2)}) collective-permute-start(s16[1024,128]{1,0:T(8,128)(2,1)S(1)} %get-tuple-element.27), channel_id=1, source_target_pairs={{0,2},{1,3},{2,0},{3,1},{4,6},{5,7},{6,4},{7,5},{8,10},{9,11},{10,... | collective-permute-start | bytes 786440 | tf_op jit(solution)/shard_map/ppermute | solution.py:35
  86.6 1.6 %collective-permute-start.19 = (s16[1024,128]{1,0:T(8,128)(2,1)S(1)}, s16[1024,128]{1,0:T(8,128)(2,1)S(1)}, u32[]{:S(2)}, u32[]{:S(2)}) collective-permute-start(s16[1024,128]{1,0:T(8,128)(2,1)S(1)} %get-tuple-element.28), channel_id=1, source_target_pairs={{0,3},{1,0},{2,1},{3,2},{4,7},{5,4},{6,5},{7,6},{8,11},{9,8},{10,9... | collective-permute-start | bytes 786440 | tf_op jit(solution)/shard_map/ppermute | solution.py:35
  88.3 10.7 %sum_receivers.2 = (f32[4096,128]{1,0:T(8,128)S(1)}, f32[4096,128]{1,0:T(8,128)S(1)}, f32[4096,128]{1,0:T(8,128)S(1)}) custom-call(s32[4096]{0:T(1024)S(1)} %bitcast.61, s32[4]{0:T(128)S(1)} %get-tuple-element.64.refs_1_, f32[4096,128]{1,0:T(8,128)S(1)} %copy-done.1, s16[4096,128]{1,0:T(8,128)(2,1)S(1)} %join.13.refs_3_, ...), custom_call_target="tpu_custom_call" | custom-call | flops 1000 | bytes 1000 | tf_op jit(solution)/shard_map/sum_receivers/pallas_call | solution.py:208
  99.1 10.7 %sum_receivers.3 = (f32[4096,128]{1,0:T(8,128)S(1)}, f32[4096,128]{1,0:T(8,128)S(1)}, f32[4096,128]{1,0:T(8,128)S(1)}) custom-call(s32[4096]{0:T(1024)S(1)} %bitcast.59, s32[4]{0:T(128)S(1)} %get-tuple-element.63.refs_1_, f32[4096,128]{1,0:T(8,128)S(1)} %copy-done.3, s16[4096,128]{1,0:T(8,128)(2,1)S(1)} %join.13.refs_3_, ...), custom_call_target="tpu_custom_call" | custom-call | flops 1000 | bytes 1000 | tf_op jit(solution)/shard_map/sum_receivers/pallas_call | solution.py:208
  109.9 4.1 %collective-permute-done.22 = f32[4096,128]{1,0:T(8,128)S(1)} collective-permute-done((f32[4096,128]{1,0:T(8,128)S(1)}, f32[4096,128]{1,0:T(8,128)S(1)}, u32[]{:S(2)}, u32[]{:S(2)}) %collective-permute-start.22) | collective-permute-done | bytes 2097184 | tf_op jit(solution)/shard_map/ppermute | solution.py:31
  114.5 2.3 %collective-permute-start.25 = (f16[2,4,128,128]{3,2,1,0:T(8,128)(2,1)S(1)}, f16[2,4,128,128]{3,2,1,0:T(8,128)(2,1)S(1)}, u32[]{:S(2)}, u32[]{:S(2)}) collective-permute-start(f16[2,4,128,128]{3,2,1,0:T(8,128)(2,1)S(1)} %bitcast.66), channel_id=1, source_target_pairs={{0,16},{4,20},{8,24},{12,28},{16,0},{20,4},{24,8},{28,12},{32,48},... | collective-permute-start | bytes 786440 | tf_op jit(solution)/shard_map/ppermute | solution.py:31
  117.3 1.4 collective-permute-start.24
  118.7 1.8 %sum_shots.1.refs_1_ = f32[384,128]{1,0:T(8,128)S(1)} custom-call(s32[1,8192]{1,0:T(1,128)S(1)} %bitcast.57, f32[4096,128]{1,0:T(8,128)S(1)} %get-tuple-element.23.refs_0_, f32[4096,128]{1,0:T(8,128)S(1)} %get-tuple-element.31.refs_1_), custom_call_target="tpu_custom_call" | custom-call | flops 1000 | bytes 1000 | tf_op jit(solution)/shard_map/sum_shots/pallas_call | solution.py:238
  120.5 1.3 collective-permute-start.20
  121.9 1.3 collective-permute-start.21
  123.2 2.1 %collective-permute-done.25 = f16[2,4,128,128]{3,2,1,0:T(8,128)(2,1)S(1)} collective-permute-done((f16[2,4,128,128]{3,2,1,0:T(8,128)(2,1)S(1)}, f16[2,4,128,128]{3,2,1,0:T(8,128)(2,1)S(1)}, u32[]{:S(2)}, u32[]{:S(2)}) %collective-permute-start.25) | collective-permute-done | bytes 262176 | tf_op jit(solution)/shard_map/ppermute | solution.py:31
  125.3 4.0 %collective-permute-done.23 = f16[2,4,128,128]{3,2,1,0:T(8,128)(2,1)S(1)} collective-permute-done((f16[2,4,128,128]{3,2,1,0:T(8,128)(2,1)S(1)}, f16[2,4,128,128]{3,2,1,0:T(8,128)(2,1)S(1)}, u32[]{:S(2)}, u32[]{:S(2)}) %collective-permute-start.23) | collective-permute-done | bytes 262176 | tf_op jit(solution)/shard_map/ppermute | solution.py:31
  129.2 0.8 collective-permute-done.24
  130.3 2.8 %collective-permute-start.26 = (f16[4,128,128]{2,1,0:T(8,128)(2,1)S(1)}, f16[4,128,128]{2,1,0:T(8,128)(2,1)S(1)}, u32[]{:S(2)}, u32[]{:S(2)}) collective-permute-start(f16[4,128,128]{2,1,0:T(8,128)(2,1)S(1)} %get-tuple-element.47), channel_id=1, source_target_pairs={{0,32},{4,36},{8,40},{12,44},{16,48},{20,52},{24,56},{28,60},{32,0... | collective-permute-start | bytes 393224 | tf_op jit(solution)/shard_map/ppermute | solution.py:31
  133.2 3.6 %collective-permute-done.26 = f16[4,128,128]{2,1,0:T(8,128)(2,1)S(1)} collective-permute-done((f16[4,128,128]{2,1,0:T(8,128)(2,1)S(1)}, f16[4,128,128]{2,1,0:T(8,128)(2,1)S(1)}, u32[]{:S(2)}, u32[]{:S(2)}) %collective-permute-start.26) | collective-permute-done | bytes 131104 | tf_op jit(solution)/shard_map/ppermute | solution.py:31
  136.8 3.4 %collective-permute-start.27 = (f16[2,128,128]{2,1,0:T(8,128)(2,1)S(1)}, f16[2,128,128]{2,1,0:T(8,128)(2,1)S(1)}, u32[]{:S(2)}, u32[]{:S(2)}) collective-permute-start(f16[2,128,128]{2,1,0:T(8,128)(2,1)S(1)} %fusion.4), channel_id=1, source_target_pairs={{0,64},{4,68},{8,72},{12,76},{16,80},{20,84},{24,88},{28,92},{32,9... | collective-permute-start | bytes 196616 | tf_op jit(solution)/shard_map/ppermute | solution.py:31
  140.2 2.5 %collective-permute-done.27 = f16[2,128,128]{2,1,0:T(8,128)(2,1)S(1)} collective-permute-done((f16[2,128,128]{2,1,0:T(8,128)(2,1)S(1)}, f16[2,128,128]{2,1,0:T(8,128)(2,1)S(1)}, u32[]{:S(2)}, u32[]{:S(2)}) %collective-permute-start.27) | collective-permute-done | bytes 65568 | tf_op jit(solution)/shard_map/ppermute | solution.py:31
  142.8 6.4 %collective-permute-start.28 = (f16[128,128]{1,0:T(8,128)(2,1)S(1)}, f16[128,128]{1,0:T(8,128)(2,1)S(1)}, u32[]{:S(2)}, u32[]{:S(2)}) collective-permute-start(f16[128,128]{1,0:T(8,128)(2,1)S(1)} %fusion.23), channel_id=1, source_target_pairs={{0,128},{4,132},{8,136},{12,140},{16,144},{20,148},{24,152},{28,15... | collective-permute-start | bytes 98312 | tf_op jit(solution)/shard_map/ppermute | solution.py:31
  149.1 2.0 %collective-permute-done.28 = f16[128,128]{1,0:T(8,128)(2,1)S(1)} collective-permute-done((f16[128,128]{1,0:T(8,128)(2,1)S(1)}, f16[128,128]{1,0:T(8,128)(2,1)S(1)}, u32[]{:S(2)}, u32[]{:S(2)}) %collective-permute-start.28) | collective-permute-done | bytes 32800 | tf_op jit(solution)/shard_map/ppermute | solution.py:31
  151.1 0.6 fusion.6
  (95 shorter events, 3.0 us)
Async XLA Ops:
  4.7 10.4 %copy-start.11 = (bf16[1024,256]{1,0:T(8,128)(2,1)}, bf16[1024,256]{1,0:T(8,128)(2,1)S(1)}, u32[]{:S(2)}) copy-start(bf16[1024,256]{1,0:T(8,128)(2,1)S(1)} %get-tuple-element.42.refs_0_.b0) | copy-start | bytes 1572868
  4.7 10.3 %copy-start.14 = (f32[128,128]{1,0:T(8,128)S(1)}, f32[128,128]{1,0:T(8,128)}, u32[]{:S(2)}) copy-start(f32[128,128]{1,0:T(8,128)} %a.1) | copy-start | bytes 196612
  4.7 33.9 %collective-permute-start.6 = (bf16[1024,256]{1,0:T(8,128)(2,1)}, bf16[1024,256]{1,0:T(8,128)(2,1)S(1)}, u32[]{:S(2)}, u32[]{:S(2)}) collective-permute-start(bf16[1024,256]{1,0:T(8,128)(2,1)} %get-tuple-element.39), channel_id=1, source_target_pairs={{0,3},{1,0},{2,1},{3,2},{4,7},{5,4},{6,5},{7,6},{8,11},{9,8},{10,9... | collective-permute-start | bytes 1572872 | tf_op jit(solution)/shard_map/ppermute | solution.py:35
  7.0 35.3 %collective-permute-start.5 = (bf16[1024,256]{1,0:T(8,128)(2,1)}, bf16[1024,256]{1,0:T(8,128)(2,1)S(1)}, u32[]{:S(2)}, u32[]{:S(2)}) collective-permute-start(bf16[1024,256]{1,0:T(8,128)(2,1)} %get-tuple-element.40), channel_id=1, source_target_pairs={{0,2},{1,3},{2,0},{3,1},{4,6},{5,7},{6,4},{7,5},{8,10},{9,11},{10,... | collective-permute-start | bytes 1572872 | tf_op jit(solution)/shard_map/ppermute | solution.py:35
  7.8 34.4 %collective-permute-start.4 = (bf16[1024,256]{1,0:T(8,128)(2,1)}, bf16[1024,256]{1,0:T(8,128)(2,1)}, u32[]{:S(2)}, u32[]{:S(2)}) collective-permute-start(bf16[1024,256]{1,0:T(8,128)(2,1)} %get-tuple-element.41), channel_id=1, source_target_pairs={{0,1},{1,2},{2,3},{3,0},{4,5},{5,6},{6,7},{7,4},{8,9},{9,10},{10,1... | collective-permute-start | bytes 1572872 | tf_op jit(solution)/shard_map/ppermute | solution.py:35
  9.7 8.7 %copy-start.15 = (f32[128,128]{1,0:T(8,128)S(1)}, f32[128,128]{1,0:T(8,128)}, u32[]{:S(2)}) copy-start(f32[128,128]{1,0:T(8,128)} %refs_0_.1) | copy-start | bytes 196612
  15.0 5.5 %copy-start.17 = (s32[8192]{0:T(1024)S(1)}, s32[8192]{0:T(1024)}, u32[]{:S(2)}) copy-start(s32[8192]{0:T(1024)} %param.8) | copy-start | bytes 98308
  15.0 5.7 %copy-start.18 = (s32[8192]{0:T(1024)S(1)}, s32[8192]{0:T(1024)}, u32[]{:S(2)}) copy-start(s32[8192]{0:T(1024)} %param.7) | copy-start | bytes 98308
  15.1 5.8 %collective-permute-start.2 = (s16[128,128]{1,0:T(8,128)(2,1)S(1)}, s16[128,128]{1,0:T(8,128)(2,1)S(1)}, u32[]{:S(2)}, u32[]{:S(2)}) collective-permute-start(s16[128,128]{1,0:T(8,128)(2,1)S(1)} %encode_terms.1.refs_0_), channel_id=1, source_target_pairs={{0,64},{4,68},{8,72},{12,76},{16,80},{20,84},{24,88},{28,92},{32,9... | collective-permute-start | bytes 98312 | tf_op jit(solution)/shard_map/ppermute | solution.py:31
  18.5 5.6 %collective-permute-start.1 = (f32[128,128]{1,0:T(8,128)S(1)}, f32[128,128]{1,0:T(8,128)S(1)}, u32[]{:S(2)}, u32[]{:S(2)}) collective-permute-start(f32[128,128]{1,0:T(8,128)S(1)} %join.8), channel_id=1, source_target_pairs={{4,0},{8,4},{12,8},{16,12},{20,16},{24,20},{28,24},{32,28},{36,32}... | collective-permute-start | bytes 196616 | tf_op jit(solution)/shard_map/ppermute | solution.py:251
  20.8 28.2 %copy-start.12 = (bf16[1024,256]{1,0:T(8,128)(2,1)S(1)}, bf16[1024,256]{1,0:T(8,128)(2,1)}, u32[]{:S(2)}) copy-start(bf16[1024,256]{1,0:T(8,128)(2,1)} %copy-done.11) | copy-start | bytes 1572868
  20.9 4.6 %collective-permute-start = (f32[128,128]{1,0:T(8,128)S(1)}, f32[128,128]{1,0:T(8,128)S(1)}, u32[]{:S(2)}, u32[]{:S(2)}) collective-permute-start(f32[128,128]{1,0:T(8,128)S(1)} %join.8), channel_id=1, source_target_pairs={{0,4},{4,8},{8,12},{12,16},{16,20},{20,24},{24,28},{28,32},{32,36}... | collective-permute-start | bytes 196616 | tf_op jit(solution)/shard_map/ppermute | solution.py:251
  24.1 42.7 %collective-permute-start.11 = (bf16[1024,256]{1,0:T(8,128)(2,1)}, bf16[1024,256]{1,0:T(8,128)(2,1)S(1)}, u32[]{:S(2)}, u32[]{:S(2)}) collective-permute-start(bf16[1024,256]{1,0:T(8,128)(2,1)} %get-tuple-element.37), channel_id=1, source_target_pairs={{0,2},{1,3},{2,0},{3,1},{4,6},{5,7},{6,4},{7,5},{8,10},{9,11},{10,... | collective-permute-start | bytes 1572872 | tf_op jit(solution)/shard_map/ppermute | solution.py:35
  25.4 13.2 %collective-permute-start.3 = (s16[256,128]{1,0:T(8,128)(2,1)S(1)}, s16[256,128]{1,0:T(8,128)(2,1)S(1)}, u32[]{:S(2)}, u32[]{:S(2)}) collective-permute-start(s16[256,128]{1,0:T(8,128)(2,1)S(1)} %join.9.refs_0_), channel_id=1, source_target_pairs={{0,128},{4,132},{8,136},{12,140},{16,144},{20,148},{24,152},{28,15... | collective-permute-start | bytes 196616 | tf_op jit(solution)/shard_map/ppermute | solution.py:31
  38.6 28.2 %collective-permute-start.10 = (bf16[1024,256]{1,0:T(8,128)(2,1)}, bf16[1024,256]{1,0:T(8,128)(2,1)S(1)}, u32[]{:S(2)}, u32[]{:S(2)}) collective-permute-start(bf16[1024,256]{1,0:T(8,128)(2,1)} %get-tuple-element.38), channel_id=1, source_target_pairs={{0,1},{1,2},{2,3},{3,0},{4,5},{5,6},{6,7},{7,4},{8,9},{9,10},{10,1... | collective-permute-start | bytes 1572872 | tf_op jit(solution)/shard_map/ppermute | solution.py:35
  38.6 28.2 %collective-permute-start.12 = (bf16[1024,256]{1,0:T(8,128)(2,1)}, bf16[1024,256]{1,0:T(8,128)(2,1)S(1)}, u32[]{:S(2)}, u32[]{:S(2)}) collective-permute-start(bf16[1024,256]{1,0:T(8,128)(2,1)} %get-tuple-element.43), channel_id=1, source_target_pairs={{0,3},{1,0},{2,1},{3,2},{4,7},{5,4},{6,5},{7,6},{8,11},{9,8},{10,9... | collective-permute-start | bytes 1572872 | tf_op jit(solution)/shard_map/ppermute | solution.py:35
  42.2 5.1 %collective-permute-start.7 = (s16[512,128]{1,0:T(8,128)(2,1)S(1)}, s16[512,128]{1,0:T(8,128)(2,1)S(1)}, u32[]{:S(2)}, u32[]{:S(2)}) collective-permute-start(s16[512,128]{1,0:T(8,128)(2,1)S(1)} %join.10.refs_0_), channel_id=1, source_target_pairs={{0,32},{4,36},{8,40},{12,44},{16,48},{20,52},{24,56},{28,60},{32,0... | collective-permute-start | bytes 393224 | tf_op jit(solution)/shard_map/ppermute | solution.py:31
  47.3 7.6 %collective-permute-start.8 = (s16[1024,128]{1,0:T(8,128)(2,1)S(1)}, s16[1024,128]{1,0:T(8,128)(2,1)S(1)}, u32[]{:S(2)}, u32[]{:S(2)}) collective-permute-start(s16[1024,128]{1,0:T(8,128)(2,1)S(1)} %join.11.refs_0_), channel_id=1, source_target_pairs={{0,8},{4,12},{8,0},{12,4},{16,24},{20,28},{24,16},{28,20},{32,40},... | collective-permute-start | bytes 786440 | tf_op jit(solution)/shard_map/ppermute | solution.py:31
  53.6 3.7 %copy-start.16 = (s16[1024,128]{1,0:T(8,128)(2,1)}, s16[1024,128]{1,0:T(8,128)(2,1)S(1)}, u32[]{:S(2)}) copy-start(s16[1024,128]{1,0:T(8,128)(2,1)S(1)} %get-tuple-element.22) | copy-start | bytes 786436
  55.0 12.2 %collective-permute-start.9 = (s16[2048,128]{1,0:T(8,128)(2,1)S(1)}, s16[2048,128]{1,0:T(8,128)(2,1)S(1)}, u32[]{:S(2)}, u32[]{:S(2)}) collective-permute-start(s16[2048,128]{1,0:T(8,128)(2,1)S(1)} %join.12.refs_0_), channel_id=1, source_target_pairs={{0,16},{4,20},{8,24},{12,28},{16,0},{20,4},{24,8},{28,12},{32,48},... | collective-permute-start | bytes 1572872 | tf_op jit(solution)/shard_map/ppermute | solution.py:31
  65.5 1.4 copy-start.2
  66.8 1.4 copy-start
  66.8 1.5 %copy-start.4 = (bf16[1024,256]{1,0:T(8,128)(2,1)}, bf16[1024,256]{1,0:T(8,128)(2,1)S(1)}, u32[]{:S(2)}) copy-start(bf16[1024,256]{1,0:T(8,128)(2,1)S(1)} %collective-permute-done.11.refs_5_.b2) | copy-start | bytes 1572868
  66.8 1.7 %copy-start.6 = (bf16[1024,256]{1,0:T(8,128)(2,1)}, bf16[1024,256]{1,0:T(8,128)(2,1)S(1)}, u32[]{:S(2)}) copy-start(bf16[1024,256]{1,0:T(8,128)(2,1)S(1)} %collective-permute-done.10.refs_4_.b1) | copy-start | bytes 1572868
  66.9 1.8 %copy-start.8 = (bf16[1024,256]{1,0:T(8,128)(2,1)}, bf16[1024,256]{1,0:T(8,128)(2,1)S(1)}, u32[]{:S(2)}) copy-start(bf16[1024,256]{1,0:T(8,128)(2,1)S(1)} %collective-permute-done.12.refs_6_.b3) | copy-start | bytes 1572868
  68.6 19.6 %collective-permute-start.13 = (s16[4096,128]{1,0:T(8,128)(2,1)S(1)}, s16[4096,128]{1,0:T(8,128)(2,1)}, u32[]{:S(2)}, u32[]{:S(2)}) collective-permute-start(s16[4096,128]{1,0:T(8,128)(2,1)S(1)} %join.13.refs_3_), channel_id=1, source_target_pairs={{0,4},{4,0},{8,12},{12,8},{16,20},{20,16},{24,28},{28,24},{32,36},... | collective-permute-start | bytes 3145736 | tf_op jit(solution)/shard_map/ppermute | solution.py:31
  68.6 14.8 %collective-permute-start.14 = (s16[1024,128]{1,0:T(8,128)(2,1)}, s16[1024,128]{1,0:T(8,128)(2,1)}, u32[]{:S(2)}, u32[]{:S(2)}) collective-permute-start(s16[1024,128]{1,0:T(8,128)(2,1)} %get-tuple-element.20), channel_id=1, source_target_pairs={{0,1},{1,2},{2,3},{3,0},{4,5},{5,6},{6,7},{7,4},{8,9},{9,10},{10,1... | collective-permute-start | bytes 786440 | tf_op jit(solution)/shard_map/ppermute | solution.py:35
  68.6 17.9 %collective-permute-start.15 = (s16[1024,128]{1,0:T(8,128)(2,1)}, s16[1024,128]{1,0:T(8,128)(2,1)}, u32[]{:S(2)}, u32[]{:S(2)}) collective-permute-start(s16[1024,128]{1,0:T(8,128)(2,1)} %get-tuple-element.21), channel_id=1, source_target_pairs={{0,2},{1,3},{2,0},{3,1},{4,6},{5,7},{6,4},{7,5},{8,10},{9,11},{10,... | collective-permute-start | bytes 786440 | tf_op jit(solution)/shard_map/ppermute | solution.py:35
  74.1 14.2 %collective-permute-start.16 = (s16[1024,128]{1,0:T(8,128)(2,1)}, s16[1024,128]{1,0:T(8,128)(2,1)S(1)}, u32[]{:S(2)}, u32[]{:S(2)}) collective-permute-start(s16[1024,128]{1,0:T(8,128)(2,1)} %copy-done.16), channel_id=1, source_target_pairs={{0,3},{1,0},{2,1},{3,2},{4,7},{5,4},{6,5},{7,6},{8,11},{9,8},{10,9... | collective-permute-start | bytes 786440 | tf_op jit(solution)/shard_map/ppermute | solution.py:35
  74.1 1.0 copy-start.5
  75.2 1.0 copy-start.7
  76.2 1.0 copy-start.9
  77.2 1.0 copy-start.10
  78.3 10.0 %copy-start.1 = (f32[4096,128]{1,0:T(8,128)S(1)}, f32[4096,128]{1,0:T(8,128)}, u32[]{:S(2)}) copy-start(f32[4096,128]{1,0:T(8,128)} %copy-done) | copy-start | bytes 6291460
  81.3 17.7 %collective-permute-start.17 = (s16[1024,128]{1,0:T(8,128)(2,1)S(1)}, s16[1024,128]{1,0:T(8,128)(2,1)S(1)}, u32[]{:S(2)}, u32[]{:S(2)}) collective-permute-start(s16[1024,128]{1,0:T(8,128)(2,1)S(1)} %get-tuple-element.26), channel_id=1, source_target_pairs={{0,1},{1,2},{2,3},{3,0},{4,5},{5,6},{6,7},{7,4},{8,9},{9,10},{10,1... | collective-permute-start | bytes 786440 | tf_op jit(solution)/shard_map/ppermute | solution.py:35
  83.4 15.6 %collective-permute-start.18 = (s16[1024,128]{1,0:T(8,128)(2,1)S(1)}, s16[1024,128]{1,0:T(8,128)(2,1)S(1)}, u32[]{:S(2)}, u32[]{:S(2)}) collective-permute-start(s16[1024,128]{1,0:T(8,128)(2,1)S(1)} %get-tuple-element.27), channel_id=1, source_target_pairs={{0,2},{1,3},{2,0},{3,1},{4,6},{5,7},{6,4},{7,5},{8,10},{9,11},{10,... | collective-permute-start | bytes 786440 | tf_op jit(solution)/shard_map/ppermute | solution.py:35
  86.6 12.5 %collective-permute-start.19 = (s16[1024,128]{1,0:T(8,128)(2,1)S(1)}, s16[1024,128]{1,0:T(8,128)(2,1)S(1)}, u32[]{:S(2)}, u32[]{:S(2)}) collective-permute-start(s16[1024,128]{1,0:T(8,128)(2,1)S(1)} %get-tuple-element.28), channel_id=1, source_target_pairs={{0,3},{1,0},{2,1},{3,2},{4,7},{5,4},{6,5},{7,6},{8,11},{9,8},{10,9... | collective-permute-start | bytes 786440 | tf_op jit(solution)/shard_map/ppermute | solution.py:35
  88.3 10.8 %copy-start.3 = (f32[4096,128]{1,0:T(8,128)S(1)}, f32[4096,128]{1,0:T(8,128)}, u32[]{:S(2)}) copy-start(f32[4096,128]{1,0:T(8,128)} %copy-done.2) | copy-start | bytes 6291460
  109.8 4.2 %collective-permute-start.22 = (f32[4096,128]{1,0:T(8,128)S(1)}, f32[4096,128]{1,0:T(8,128)S(1)}, u32[]{:S(2)}, u32[]{:S(2)}) collective-permute-start(f32[4096,128]{1,0:T(8,128)S(1)} %get-tuple-element.33), channel_id=1, source_target_pairs={{0,4},{4,0},{8,12},{12,8},{16,20},{20,16},{24,28},{28,24},{32,36},... | collective-permute-start | bytes 6291464 | tf_op jit(solution)/shard_map/ppermute | solution.py:31
  114.5 10.8 %collective-permute-start.25 = (f16[2,4,128,128]{3,2,1,0:T(8,128)(2,1)S(1)}, f16[2,4,128,128]{3,2,1,0:T(8,128)(2,1)S(1)}, u32[]{:S(2)}, u32[]{:S(2)}) collective-permute-start(f16[2,4,128,128]{3,2,1,0:T(8,128)(2,1)S(1)} %bitcast.66), channel_id=1, source_target_pairs={{0,16},{4,20},{8,24},{12,28},{16,0},{20,4},{24,8},{28,12},{32,48},... | collective-permute-start | bytes 786440 | tf_op jit(solution)/shard_map/ppermute | solution.py:31
  116.8 12.5 %collective-permute-start.23 = (f16[2,4,128,128]{3,2,1,0:T(8,128)(2,1)S(1)}, f16[2,4,128,128]{3,2,1,0:T(8,128)(2,1)S(1)}, u32[]{:S(2)}, u32[]{:S(2)}) collective-permute-start(f16[2,4,128,128]{3,2,1,0:T(8,128)(2,1)S(1)} %bitcast.65), channel_id=1, source_target_pairs={{0,8},{4,12},{8,0},{12,4},{16,24},{20,28},{24,16},{28,20},{32,40},... | collective-permute-start | bytes 786440 | tf_op jit(solution)/shard_map/ppermute | solution.py:31
  117.3 12.8 %collective-permute-start.24 = (f16[2,4,128,128]{3,2,1,0:T(8,128)(2,1)S(1)}, f16[2,4,128,128]{3,2,1,0:T(8,128)(2,1)S(1)}, u32[]{:S(2)}, u32[]{:S(2)}) collective-permute-start(f16[2,4,128,128]{3,2,1,0:T(8,128)(2,1)S(1)} %bitcast.64), channel_id=1, source_target_pairs={{0,24},{4,28},{8,16},{12,20},{16,8},{20,12},{24,0},{28,4},{32,56},... | collective-permute-start | bytes 786440 | tf_op jit(solution)/shard_map/ppermute | solution.py:31
  120.5 12.6 %collective-permute-start.20 = (f32[128,128]{1,0:T(8,128)S(1)}, f32[128,128]{1,0:T(8,128)S(1)}, u32[]{:S(2)}, u32[]{:S(2)}) collective-permute-start(f32[128,128]{1,0:T(8,128)S(1)} %get-tuple-element.49), channel_id=1, source_target_pairs={{0,4},{4,8},{8,12},{12,16},{16,20},{20,24},{24,28},{28,32},{32,36}... | collective-permute-start | bytes 196616 | tf_op jit(solution)/shard_map/ppermute | solution.py:251
  121.9 11.2 %collective-permute-start.21 = (f32[128,128]{1,0:T(8,128)S(1)}, f32[128,128]{1,0:T(8,128)S(1)}, u32[]{:S(2)}, u32[]{:S(2)}) collective-permute-start(f32[128,128]{1,0:T(8,128)S(1)} %get-tuple-element.50), channel_id=1, source_target_pairs={{4,0},{8,4},{12,8},{16,12},{20,16},{24,20},{28,24},{32,28},{36,32}... | collective-permute-start | bytes 196616 | tf_op jit(solution)/shard_map/ppermute | solution.py:251
  130.3 6.5 %collective-permute-start.26 = (f16[4,128,128]{2,1,0:T(8,128)(2,1)S(1)}, f16[4,128,128]{2,1,0:T(8,128)(2,1)S(1)}, u32[]{:S(2)}, u32[]{:S(2)}) collective-permute-start(f16[4,128,128]{2,1,0:T(8,128)(2,1)S(1)} %get-tuple-element.47), channel_id=1, source_target_pairs={{0,32},{4,36},{8,40},{12,44},{16,48},{20,52},{24,56},{28,60},{32,0... | collective-permute-start | bytes 393224 | tf_op jit(solution)/shard_map/ppermute | solution.py:31
  133.1 18.6 %copy-start.13 = (f32[128,128]{1,0:T(8,128)}, f32[128,128]{1,0:T(8,128)S(1)}, u32[]{:S(2)}) copy-start(f32[128,128]{1,0:T(8,128)S(1)} %fusion.7.refs_1_) | copy-start | bytes 196612
  136.8 5.9 %collective-permute-start.27 = (f16[2,128,128]{2,1,0:T(8,128)(2,1)S(1)}, f16[2,128,128]{2,1,0:T(8,128)(2,1)S(1)}, u32[]{:S(2)}, u32[]{:S(2)}) collective-permute-start(f16[2,128,128]{2,1,0:T(8,128)(2,1)S(1)} %fusion.4), channel_id=1, source_target_pairs={{0,64},{4,68},{8,72},{12,76},{16,80},{20,84},{24,88},{28,92},{32,9... | collective-permute-start | bytes 196616 | tf_op jit(solution)/shard_map/ppermute | solution.py:31
  142.8 8.4 %collective-permute-start.28 = (f16[128,128]{1,0:T(8,128)(2,1)S(1)}, f16[128,128]{1,0:T(8,128)(2,1)S(1)}, u32[]{:S(2)}, u32[]{:S(2)}) collective-permute-start(f16[128,128]{1,0:T(8,128)(2,1)S(1)} %fusion.23), channel_id=1, source_target_pairs={{0,128},{4,132},{8,136},{12,140},{16,144},{20,148},{24,152},{28,15... | collective-permute-start | bytes 98312 | tf_op jit(solution)/shard_map/ppermute | solution.py:31

commit v10 on v9

--- a/solution.py
+++ b/solution.py
@@ -89,6 +89,20 @@
         cost_estimate=COST,
         name="join",
     )(*parts, *after)
+
+
+def tie(values, after):
+    hbm = pl.BlockSpec(memory_space=pl.ANY)
+    return pl.pallas_call(
+        lambda *refs: None,
+        in_specs=[hbm] * (len(values) + len(after)),
+        out_specs=[hbm] * len(values),
+        out_shape=[jax.ShapeDtypeStruct(value.shape, value.dtype) for value in values],
+        input_output_aliases={k: k for k in range(len(values))},
+        compiler_params=SMALL,
+        cost_estimate=COST,
+        name="tie",
+    )(*values, *after)
 
 
 def encode_terms(terms, after):
@@ -262,6 +276,8 @@
     got = []
     for at, size in zip(first, PIECES):
         mine = [lax.dynamic_slice_in_dim(traces, (y + k) % NY * share + at, size, 0) for k in range(NY)]
+        if got:
+            mine[1:] = tie(mine[1:], got[0][1:])
         come = {k: send_y(mine[k], k) for k in (1, 3, 2)}
         got.append([mine[0]] + [come[k] for k in range(1, NY)])
     table = make_table(part * NY, y, width, got[0][:1])
@@ -292,8 +308,8 @@
     terms = join([terms, swap(terms, 4, 0, 0)], got[0][1:] + [shot_near])
     terms = join([terms, swap(terms, 1, 0, 0)])
     shots = gather_shots(shot_near, shot_at, [size * NY for size in PIECES])
-    terms = join([terms, swap(terms, 0, 1, 0)], [coded[0][0]])
-    terms = join([terms, swap(terms, 0, 2, 0)], [shots[0], rec_at] + got[1][1:])
+    terms = join([terms, swap(terms, 0, 1, 0)], [coded[0][0], shots[0], rec_at] + got[1][1:])
+    terms = join([terms, swap(terms, 0, 2, 0)], [coded[1][0]] + codes[1:NY])
     far_terms = swap(terms, 0, 0, 1)
 
     sums, residuals, done = (), [], 0

time: 154 us -> 153 us (level)
  waiting for transfers between devices: 26.4 us -> 33.9 us
  starting transfers between devices: 66.1 us -> 59.7 us
    ppermute x12, waiting for transfers between devices: 0.03 us -> 10.9 us  [send_y(): return lax.ppermute(value, 'fq', [(i, (i + k) % NY) for i in range(NY)])]
    ppermute x13, starting transfers between devices: 36.8 us -> 32 us  [swap(): lax.ppermute(value, 'tr', [(tr_of(z, x, c), tr_of(z ^ dz, x ^ dx, c ^ dc)...]
    ppermute x13, waiting for transfers between devices: 26.3 us -> 23 us  [swap(): lax.ppermute(value, 'tr', [(tr_of(z, x, c), tr_of(z ^ dz, x ^ dx, c ^ dc)...]
    unnamed x43 -> x51, local copies, waits for them, and re-layouts: 6.93 us -> 6.5 us
  transfers between devices with their start and end apart: 29 -> 29, of which waited for: 11 -> 13; matrix products, arithmetic and copies ran while one was open for 0% -> 0% of each run, Pallas kernels for 22% -> 22%
where the time goes in v10:
time: 153 us; the launch traced here: 152 us
  starting transfers between devices  59.7 us (39%)
  Pallas kernels  44.3 us (29%)
  waiting for transfers between devices  33.9 us (22%)
  local copies, waits for them, and re-layouts  11 us (7%)
  between operations  2.03 us (1%)
    ppermute x13, starting transfers between devices, swap(): lax.ppermute(value, 'tr', [(tr_of(z, x, c), tr_of(z ^ dz, x ^ dx, c ^ dc)...  32 us
    ppermute x13, waiting for transfers between devices, swap(): lax.ppermute(value, 'tr', [(tr_of(z, x, c), tr_of(z ^ dz, x ^ dx, c ^ dc)...  23 us
    pallas_call x2, Pallas kernels, sum_receivers(): pl.pallas_call(body, in_specs=[sm, sm] + [vm] * (3 + parts + held), out_s...  21.7 us
    ppermute x12, starting transfers between devices, send_y(): return lax.ppermute(value, 'fq', [(i, (i + k) % NY) for i in range(NY)])  20.8 us
    ppermute x12, waiting for transfers between devices, send_y(): return lax.ppermute(value, 'fq', [(i, (i + k) % NY) for i in range(NY)])  10.9 us
    pallas_call x1, Pallas kernels, gather_shots(): pl.pallas_call(body, in_specs=[sm, vm], out_specs=[vm] * len(sizes), out_...  8.11 us
    pallas_call x2, Pallas kernels, spectra(): pl.pallas_call(body, grid=(rows // tile,), in_specs=[pl.BlockSpec((tile,...  7.14 us
    ppermute x4, starting transfers between devices, neighbour(): lax.ppermute(value, 'tr', [(i, i + by) for i in range(size) if 0 <= i + b...  6.91 us
  transfers between devices with their start and end apart: 29, of which 13 were waited for; matrix products, arithmetic and copies ran while one was open for 0% of the time, Pallas kernels for 22%

profile of v10, /device:TPU:8, one launch (start us, length us, event | category | flops | bytes accessed | tf_op | source)
XLA Modules:
  0.0 152.3 jit_solution(6351900004514204905)
XLA Ops:
  0.7 4.0 %constant_dynamic-slice_fusion = (bf16[1024,256]{1,0:T(8,128)(2,1)}, bf16[1024,256]{1,0:T(8,128)(2,1)}, bf16[1024,256]{1,0:T(8,128)(2,1)}, bf16[1024,256]{1,0:T(...) fusion(bf16[8192,256]{1,0:T(8,128)(2,1)} %param.6, ...), kind=kLoop, calls=%fused_computation.74 | loop fusion | bytes 8388640 | tf_op jit(solution)/shard_map/dynamic_slice | solution.py:278
  4.7 2.3 %collective-permute-start.6 = (bf16[1024,256]{1,0:T(8,128)(2,1)}, bf16[1024,256]{1,0:T(8,128)(2,1)S(1)}, u32[]{:S(2)}, u32[]{:S(2)}) collective-permute-start(bf16[1024,256]{1,0:T(8,128)(2,1)} %get-tuple-element.45), channel_id=1, source_target_pairs={{0,3},{1,0},{2,1},{3,2},{4,7},{5,4},{6,5},{7,6},{8,11},{9,8},{10,9... | collective-permute-start | bytes 1572872 | tf_op jit(solution)/shard_map/ppermute | solution.py:35
  7.8 1.9 %collective-permute-start.4 = (bf16[1024,256]{1,0:T(8,128)(2,1)}, bf16[1024,256]{1,0:T(8,128)(2,1)}, u32[]{:S(2)}, u32[]{:S(2)}) collective-permute-start(bf16[1024,256]{1,0:T(8,128)(2,1)} %get-tuple-element.47), channel_id=1, source_target_pairs={{0,1},{1,2},{2,3},{3,0},{4,5},{5,6},{6,7},{7,4},{8,9},{9,10},{10,1... | collective-permute-start | bytes 1572872 | tf_op jit(solution)/shard_map/ppermute | solution.py:35
  9.7 5.3 %make_table.1.refs_1_.refs_0_.t = bf16[1024,1024]{1,0:T(8,128)(2,1)S(1)} custom-call(s32[1]{0:T(128)} %bitcast.10.y_ref, bf16[1024,256]{1,0:T(8,128)(2,1)S(1)} %get-tuple-element.48.refs_0_.b0), custom_call_target="tpu_custom_call" | custom-call | flops 1073741824 | bytes 33554432 | tf_op jit(solution)/shard_map/make_table/pallas_call | solution.py:62
  15.1 3.4 %collective-permute-start.2 = (s16[128,128]{1,0:T(8,128)(2,1)S(1)}, s16[128,128]{1,0:T(8,128)(2,1)S(1)}, u32[]{:S(2)}, u32[]{:S(2)}) collective-permute-start(s16[128,128]{1,0:T(8,128)(2,1)S(1)} %encode_terms.1.refs_0_), channel_id=1, source_target_pairs={{0,64},{4,68},{8,72},{12,76},{16,80},{20,84},{24,88},{28,92},{32,9... | collective-permute-start | bytes 98312 | tf_op jit(solution)/shard_map/ppermute | solution.py:31
  18.5 1.3 collective-permute-start.1
  21.0 3.0 %collective-permute-start = (f32[128,128]{1,0:T(8,128)S(1)}, f32[128,128]{1,0:T(8,128)S(1)}, u32[]{:S(2)}, u32[]{:S(2)}) collective-permute-start(f32[128,128]{1,0:T(8,128)S(1)} %join.8), channel_id=1, source_target_pairs={{0,4},{4,8},{8,12},{12,16},{16,20},{20,24},{24,28},{28,32},{32,36}... | collective-permute-start | bytes 196616 | tf_op jit(solution)/shard_map/ppermute | solution.py:265
  24.1 5.5 %collective-permute-start.3 = (s16[256,128]{1,0:T(8,128)(2,1)S(1)}, s16[256,128]{1,0:T(8,128)(2,1)S(1)}, u32[]{:S(2)}, u32[]{:S(2)}) collective-permute-start(s16[256,128]{1,0:T(8,128)(2,1)S(1)} %join.9.refs_0_), channel_id=1, source_target_pairs={{0,128},{4,132},{8,136},{12,140},{16,144},{20,148},{24,152},{28,15... | collective-permute-start | bytes 196616 | tf_op jit(solution)/shard_map/ppermute | solution.py:31
  29.6 1.3 collective-permute-done.5.refs_3_.b2.refs_4_
  30.9 0.9 collective-permute-done.4.refs_2_.b1.refs_3_
  31.8 1.4 collective-permute-start.9
  33.3 3.5 %collective-permute-start.10 = (bf16[1024,256]{1,0:T(8,128)(2,1)}, bf16[1024,256]{1,0:T(8,128)(2,1)S(1)}, u32[]{:S(2)}, u32[]{:S(2)}) collective-permute-start(bf16[1024,256]{1,0:T(8,128)(2,1)} %get-tuple-element.24), channel_id=1, source_target_pairs={{0,2},{1,3},{2,0},{3,1},{4,6},{5,7},{6,4},{7,5},{8,10},{9,11},{10,... | collective-permute-start | bytes 1572872 | tf_op jit(solution)/shard_map/ppermute | solution.py:35
  36.8 2.0 %collective-permute-start.7 = (s16[512,128]{1,0:T(8,128)(2,1)S(1)}, s16[512,128]{1,0:T(8,128)(2,1)S(1)}, u32[]{:S(2)}, u32[]{:S(2)}) collective-permute-start(s16[512,128]{1,0:T(8,128)(2,1)S(1)} %join.10.refs_0_), channel_id=1, source_target_pairs={{0,32},{4,36},{8,40},{12,44},{16,48},{20,52},{24,56},{28,60},{32,0... | collective-permute-start | bytes 393224 | tf_op jit(solution)/shard_map/ppermute | solution.py:31
  38.8 3.1 %collective-permute-done.7.refs_1_ = s16[512,128]{1,0:T(8,128)(2,1)S(1)} collective-permute-done((s16[512,128]{1,0:T(8,128)(2,1)S(1)}, s16[512,128]{1,0:T(8,128)(2,1)S(1)}, u32[]{:S(2)}, u32[]{:S(2)}) %collective-permute-start.7) | collective-permute-done | bytes 131104 | tf_op jit(solution)/shard_map/ppermute | solution.py:31
  41.9 1.6 %collective-permute-start.8 = (s16[1024,128]{1,0:T(8,128)(2,1)S(1)}, s16[1024,128]{1,0:T(8,128)(2,1)S(1)}, u32[]{:S(2)}, u32[]{:S(2)}) collective-permute-start(s16[1024,128]{1,0:T(8,128)(2,1)S(1)} %join.11.refs_0_), channel_id=1, source_target_pairs={{0,8},{4,12},{8,0},{12,4},{16,24},{20,28},{24,16},{28,20},{32,40},... | collective-permute-start | bytes 786440 | tf_op jit(solution)/shard_map/ppermute | solution.py:31
  43.5 8.1 %gather_shots.1 = (f32[4096,128]{1,0:T(8,128)S(1)}, f32[4096,128]{1,0:T(8,128)S(1)}) custom-call(s32[8192]{0:T(1024)S(1)} %bitcast_dynamic-update-slice_fusion.shot_at, f32[384,128]{1,0:T(8,128)S(1)} %pad_maximum_fusion.shot.refs_5_), custom_call_target="tpu_custom_call" | custom-call | flops 1000 | bytes 1000 | tf_op jit(solution)/shard_map/gather_shots/pallas_call | solution.py:171
  51.6 1.3 copy-done.2
  53.0 4.1 %spectra.2 = (s16[1024,128]{1,0:T(8,128)(2,1)S(1)}, s16[1024,128]{1,0:T(8,128)(2,1)S(1)}, s16[1024,128]{1,0:T(8,128)(2,1)S(1)}, s16[1024,128]{1,0:T(8,128)(2,1)S(1)}) custom-call(bf16[1024,256]{1,0:T(8,128)(2,1)S(1)} %copy-done.6, bf16[1024,256]{1,0:T(8,128)(2,1)} %collective-permute-done.4.refs_2_.b1.refs_3_, ...), custom_call_target="tpu_custom_call" | custom-call | flops 1000 | bytes 1000 | tf_op jit(solution)/shard_map/spectra/pallas_call | solution.py:142
  57.2 2.9 %collective-permute-done.11.refs_7_.b3 = bf16[1024,256]{1,0:T(8,128)(2,1)S(1)} collective-permute-done((bf16[1024,256]{1,0:T(8,128)(2,1)}, bf16[1024,256]{1,0:T(8,128)(2,1)S(1)}, u32[]{:S(2)}, u32[]{:S(2)}) %collective-permute-start.11) | collective-permute-done | bytes 524320 | tf_op jit(solution)/shard_map/ppermute | solution.py:35
  60.1 3.1 %collective-permute-start.12 = (s16[2048,128]{1,0:T(8,128)(2,1)S(1)}, s16[2048,128]{1,0:T(8,128)(2,1)S(1)}, u32[]{:S(2)}, u32[]{:S(2)}) collective-permute-start(s16[2048,128]{1,0:T(8,128)(2,1)S(1)} %join.12.refs_0_), channel_id=1, source_target_pairs={{0,16},{4,20},{8,24},{12,28},{16,0},{20,4},{24,8},{28,12},{32,48},... | collective-permute-start | bytes 1572872 | tf_op jit(solution)/shard_map/ppermute | solution.py:31
  63.8 3.2 %collective-permute-start.14 = (s16[1024,128]{1,0:T(8,128)(2,1)S(1)}, s16[1024,128]{1,0:T(8,128)(2,1)S(1)}, u32[]{:S(2)}, u32[]{:S(2)}) collective-permute-start(s16[1024,128]{1,0:T(8,128)(2,1)S(1)} %get-tuple-element.28), channel_id=1, source_target_pairs={{0,2},{1,3},{2,0},{3,1},{4,6},{5,7},{6,4},{7,5},{8,10},{9,11},{10,... | collective-permute-start | bytes 786440 | tf_op jit(solution)/shard_map/ppermute | solution.py:35
  67.1 1.7 %collective-permute-start.15 = (s16[1024,128]{1,0:T(8,128)(2,1)S(1)}, s16[1024,128]{1,0:T(8,128)(2,1)S(1)}, u32[]{:S(2)}, u32[]{:S(2)}) collective-permute-start(s16[1024,128]{1,0:T(8,128)(2,1)S(1)} %get-tuple-element.29), channel_id=1, source_target_pairs={{0,3},{1,0},{2,1},{3,2},{4,7},{5,4},{6,5},{7,6},{8,11},{9,8},{10,9... | collective-permute-start | bytes 786440 | tf_op jit(solution)/shard_map/ppermute | solution.py:35
  68.8 3.0 %spectra.3 = (s16[1024,128]{1,0:T(8,128)(2,1)S(1)}, s16[1024,128]{1,0:T(8,128)(2,1)S(1)}, s16[1024,128]{1,0:T(8,128)(2,1)S(1)}, s16[1024,128]{1,0:T(8,128)(2,1)S(1)}) custom-call(bf16[1024,256]{1,0:T(8,128)(2,1)S(1)} %copy-done.4, bf16[1024,256]{1,0:T(8,128)(2,1)S(1)} %collective-permute-done.9.refs_5_.b1, ...), custom_call_target="tpu_custom_call" | custom-call | flops 1000 | bytes 1000 | tf_op jit(solution)/shard_map/spectra/pallas_call | solution.py:142
  72.5 2.1 %collective-permute-done.14.refs_4_.refs_7_ = s16[1024,128]{1,0:T(8,128)(2,1)S(1)} collective-permute-done((s16[1024,128]{1,0:T(8,128)(2,1)S(1)}, s16[1024,128]{1,0:T(8,128)(2,1)S(1)}, u32[]{:S(2)}, u32[]{:S(2)}) %collective-permute-start.14) | collective-permute-done | bytes 262176 | tf_op jit(solution)/shard_map/ppermute | solution.py:35
  74.6 3.7 %collective-permute-done.15.refs_5_.refs_8_ = s16[1024,128]{1,0:T(8,128)(2,1)S(1)} collective-permute-done((s16[1024,128]{1,0:T(8,128)(2,1)S(1)}, s16[1024,128]{1,0:T(8,128)(2,1)S(1)}, u32[]{:S(2)}, u32[]{:S(2)}) %collective-permute-start.15) | collective-permute-done | bytes 262176 | tf_op jit(solution)/shard_map/ppermute | solution.py:35
  79.7 3.3 %collective-permute-start.18 = (s16[1024,128]{1,0:T(8,128)(2,1)}, s16[1024,128]{1,0:T(8,128)(2,1)S(1)}, u32[]{:S(2)}, u32[]{:S(2)}) collective-permute-start(s16[1024,128]{1,0:T(8,128)(2,1)} %copy-done.19), channel_id=1, source_target_pairs={{0,2},{1,3},{2,0},{3,1},{4,6},{5,7},{6,4},{7,5},{8,10},{9,11},{10,... | collective-permute-start | bytes 786440 | tf_op jit(solution)/shard_map/ppermute | solution.py:35
  83.0 1.4 collective-permute-start.19
  84.4 0.9 copy-done.8
  85.4 0.9 copy-done.10
  86.3 0.9 copy-done.12
  87.3 0.9 copy-done.14
  88.2 10.9 %sum_receivers.2 = (f32[4096,128]{1,0:T(8,128)S(1)}, f32[4096,128]{1,0:T(8,128)S(1)}, f32[4096,128]{1,0:T(8,128)S(1)}) custom-call(s32[4096]{0:T(1024)S(1)} %bitcast.61, s32[4]{0:T(128)S(1)} %get-tuple-element.70.refs_1_, f32[4096,128]{1,0:T(8,128)S(1)} %copy-done.1, s16[4096,128]{1,0:T(8,128)(2,1)S(1)} %join.13.refs_3_, ...), custom_call_target="tpu_custom_call" | custom-call | flops 1000 | bytes 1000 | tf_op jit(solution)/shard_map/sum_receivers/pallas_call | solution.py:222
  99.2 10.8 %sum_receivers.3 = (f32[4096,128]{1,0:T(8,128)S(1)}, f32[4096,128]{1,0:T(8,128)S(1)}, f32[4096,128]{1,0:T(8,128)S(1)}) custom-call(s32[4096]{0:T(1024)S(1)} %bitcast.59, s32[4]{0:T(128)S(1)} %get-tuple-element.69.refs_1_, f32[4096,128]{1,0:T(8,128)S(1)} %copy-done.3, s16[4096,128]{1,0:T(8,128)(2,1)S(1)} %join.13.refs_3_, ...), custom_call_target="tpu_custom_call" | custom-call | flops 1000 | bytes 1000 | tf_op jit(solution)/shard_map/sum_receivers/pallas_call | solution.py:222
  110.1 4.1 %collective-permute-done.22 = f32[4096,128]{1,0:T(8,128)S(1)} collective-permute-done((f32[4096,128]{1,0:T(8,128)S(1)}, f32[4096,128]{1,0:T(8,128)S(1)}, u32[]{:S(2)}, u32[]{:S(2)}) %collective-permute-start.22) | collective-permute-done | bytes 2097184 | tf_op jit(solution)/shard_map/ppermute | solution.py:31
  115.1 1.8 %collective-permute-start.23 = (f16[2,4,128,128]{3,2,1,0:T(8,128)(2,1)S(1)}, f16[2,4,128,128]{3,2,1,0:T(8,128)(2,1)S(1)}, u32[]{:S(2)}, u32[]{:S(2)}) collective-permute-start(f16[2,4,128,128]{3,2,1,0:T(8,128)(2,1)S(1)} %bitcast.65), channel_id=1, source_target_pairs={{0,8},{4,12},{8,0},{12,4},{16,24},{20,28},{24,16},{28,20},{32,40},... | collective-permute-start | bytes 786440 | tf_op jit(solution)/shard_map/ppermute | solution.py:31
  116.9 2.0 %collective-permute-start.24 = (f16[2,4,128,128]{3,2,1,0:T(8,128)(2,1)S(1)}, f16[2,4,128,128]{3,2,1,0:T(8,128)(2,1)S(1)}, u32[]{:S(2)}, u32[]{:S(2)}) collective-permute-start(f16[2,4,128,128]{3,2,1,0:T(8,128)(2,1)S(1)} %bitcast.64), channel_id=1, source_target_pairs={{0,24},{4,28},{8,16},{12,20},{16,8},{20,12},{24,0},{28,4},{32,56},... | collective-permute-start | bytes 786440 | tf_op jit(solution)/shard_map/ppermute | solution.py:31
  118.9 1.8 %sum_shots.1.refs_1_ = f32[384,128]{1,0:T(8,128)S(1)} custom-call(s32[1,8192]{1,0:T(1,128)S(1)} %bitcast.57, f32[4096,128]{1,0:T(8,128)S(1)} %get-tuple-element.30.refs_0_, f32[4096,128]{1,0:T(8,128)S(1)} %get-tuple-element.37.refs_1_), custom_call_target="tpu_custom_call" | custom-call | flops 1000 | bytes 1000 | tf_op jit(solution)/shard_map/sum_shots/pallas_call | solution.py:252
  120.7 1.3 collective-permute-start.20
  122.1 1.3 collective-permute-start.21
  123.4 2.1 %collective-permute-done.25 = f16[2,4,128,128]{3,2,1,0:T(8,128)(2,1)S(1)} collective-permute-done((f16[2,4,128,128]{3,2,1,0:T(8,128)(2,1)S(1)}, f16[2,4,128,128]{3,2,1,0:T(8,128)(2,1)S(1)}, u32[]{:S(2)}, u32[]{:S(2)}) %collective-permute-start.25) | collective-permute-done | bytes 262176 | tf_op jit(solution)/shard_map/ppermute | solution.py:31
  125.5 3.3 %collective-permute-done.23 = f16[2,4,128,128]{3,2,1,0:T(8,128)(2,1)S(1)} collective-permute-done((f16[2,4,128,128]{3,2,1,0:T(8,128)(2,1)S(1)}, f16[2,4,128,128]{3,2,1,0:T(8,128)(2,1)S(1)}, u32[]{:S(2)}, u32[]{:S(2)}) %collective-permute-start.23) | collective-permute-done | bytes 262176 | tf_op jit(solution)/shard_map/ppermute | solution.py:31
  128.8 1.4 collective-permute-done.24
  130.5 2.7 %collective-permute-start.26 = (f16[4,128,128]{2,1,0:T(8,128)(2,1)S(1)}, f16[4,128,128]{2,1,0:T(8,128)(2,1)S(1)}, u32[]{:S(2)}, u32[]{:S(2)}) collective-permute-start(f16[4,128,128]{2,1,0:T(8,128)(2,1)S(1)} %get-tuple-element.53), channel_id=1, source_target_pairs={{0,32},{4,36},{8,40},{12,44},{16,48},{20,52},{24,56},{28,60},{32,0... | collective-permute-start | bytes 393224 | tf_op jit(solution)/shard_map/ppermute | solution.py:31
  133.2 3.6 %collective-permute-done.26 = f16[4,128,128]{2,1,0:T(8,128)(2,1)S(1)} collective-permute-done((f16[4,128,128]{2,1,0:T(8,128)(2,1)S(1)}, f16[4,128,128]{2,1,0:T(8,128)(2,1)S(1)}, u32[]{:S(2)}, u32[]{:S(2)}) %collective-permute-start.26) | collective-permute-done | bytes 131104 | tf_op jit(solution)/shard_map/ppermute | solution.py:31
  136.9 3.7 %collective-permute-start.27 = (f16[2,128,128]{2,1,0:T(8,128)(2,1)S(1)}, f16[2,128,128]{2,1,0:T(8,128)(2,1)S(1)}, u32[]{:S(2)}, u32[]{:S(2)}) collective-permute-start(f16[2,128,128]{2,1,0:T(8,128)(2,1)S(1)} %fusion.4), channel_id=1, source_target_pairs={{0,64},{4,68},{8,72},{12,76},{16,80},{20,84},{24,88},{28,92},{32,9... | collective-permute-start | bytes 196616 | tf_op jit(solution)/shard_map/ppermute | solution.py:31
  140.6 2.9 %collective-permute-done.27 = f16[2,128,128]{2,1,0:T(8,128)(2,1)S(1)} collective-permute-done((f16[2,128,128]{2,1,0:T(8,128)(2,1)S(1)}, f16[2,128,128]{2,1,0:T(8,128)(2,1)S(1)}, u32[]{:S(2)}, u32[]{:S(2)}) %collective-permute-start.27) | collective-permute-done | bytes 65568 | tf_op jit(solution)/shard_map/ppermute | solution.py:31
  143.6 5.7 %collective-permute-start.28 = (f16[128,128]{1,0:T(8,128)(2,1)S(1)}, f16[128,128]{1,0:T(8,128)(2,1)S(1)}, u32[]{:S(2)}, u32[]{:S(2)}) collective-permute-start(f16[128,128]{1,0:T(8,128)(2,1)S(1)} %fusion.23), channel_id=1, source_target_pairs={{0,128},{4,132},{8,136},{12,140},{16,144},{20,148},{24,152},{28,15... | collective-permute-start | bytes 98312 | tf_op jit(solution)/shard_map/ppermute | solution.py:31
  149.3 2.3 %collective-permute-done.28 = f16[128,128]{1,0:T(8,128)(2,1)S(1)} collective-permute-done((f16[128,128]{1,0:T(8,128)(2,1)S(1)}, f16[128,128]{1,0:T(8,128)(2,1)S(1)}, u32[]{:S(2)}, u32[]{:S(2)}) %collective-permute-start.28) | collective-permute-done | bytes 32800 | tf_op jit(solution)/shard_map/ppermute | solution.py:31
  (104 shorter events, 6.1 us)
Async XLA Ops:
  4.7 10.4 %copy-start.5 = (bf16[1024,256]{1,0:T(8,128)(2,1)}, bf16[1024,256]{1,0:T(8,128)(2,1)S(1)}, u32[]{:S(2)}) copy-start(bf16[1024,256]{1,0:T(8,128)(2,1)S(1)} %get-tuple-element.48.refs_0_.b0) | copy-start | bytes 1572868
  4.7 10.3 %copy-start.16 = (f32[128,128]{1,0:T(8,128)S(1)}, f32[128,128]{1,0:T(8,128)}, u32[]{:S(2)}) copy-start(f32[128,128]{1,0:T(8,128)} %a.1) | copy-start | bytes 196612
  4.7 24.8 %collective-permute-start.6 = (bf16[1024,256]{1,0:T(8,128)(2,1)}, bf16[1024,256]{1,0:T(8,128)(2,1)S(1)}, u32[]{:S(2)}, u32[]{:S(2)}) collective-permute-start(bf16[1024,256]{1,0:T(8,128)(2,1)} %get-tuple-element.45), channel_id=1, source_target_pairs={{0,3},{1,0},{2,1},{3,2},{4,7},{5,4},{6,5},{7,6},{8,11},{9,8},{10,9... | collective-permute-start | bytes 1572872 | tf_op jit(solution)/shard_map/ppermute | solution.py:35
  7.0 23.9 %collective-permute-start.5 = (bf16[1024,256]{1,0:T(8,128)(2,1)}, bf16[1024,256]{1,0:T(8,128)(2,1)S(1)}, u32[]{:S(2)}, u32[]{:S(2)}) collective-permute-start(bf16[1024,256]{1,0:T(8,128)(2,1)} %get-tuple-element.46), channel_id=1, source_target_pairs={{0,2},{1,3},{2,0},{3,1},{4,6},{5,7},{6,4},{7,5},{8,10},{9,11},{10,... | collective-permute-start | bytes 1572872 | tf_op jit(solution)/shard_map/ppermute | solution.py:35
  7.8 24.0 %collective-permute-start.4 = (bf16[1024,256]{1,0:T(8,128)(2,1)}, bf16[1024,256]{1,0:T(8,128)(2,1)}, u32[]{:S(2)}, u32[]{:S(2)}) collective-permute-start(bf16[1024,256]{1,0:T(8,128)(2,1)} %get-tuple-element.47), channel_id=1, source_target_pairs={{0,1},{1,2},{2,3},{3,0},{4,5},{5,6},{6,7},{7,4},{8,9},{9,10},{10,1... | collective-permute-start | bytes 1572872 | tf_op jit(solution)/shard_map/ppermute | solution.py:35
  9.7 8.7 %copy-start.17 = (f32[128,128]{1,0:T(8,128)S(1)}, f32[128,128]{1,0:T(8,128)}, u32[]{:S(2)}) copy-start(f32[128,128]{1,0:T(8,128)} %refs_0_.1) | copy-start | bytes 196612
  15.0 5.5 %copy-start.21 = (s32[8192]{0:T(1024)S(1)}, s32[8192]{0:T(1024)}, u32[]{:S(2)}) copy-start(s32[8192]{0:T(1024)} %param.8) | copy-start | bytes 98308
  15.1 5.7 %copy-start.22 = (s32[8192]{0:T(1024)S(1)}, s32[8192]{0:T(1024)}, u32[]{:S(2)}) copy-start(s32[8192]{0:T(1024)} %param.7) | copy-start | bytes 98308
  15.1 5.8 %collective-permute-start.2 = (s16[128,128]{1,0:T(8,128)(2,1)S(1)}, s16[128,128]{1,0:T(8,128)(2,1)S(1)}, u32[]{:S(2)}, u32[]{:S(2)}) collective-permute-start(s16[128,128]{1,0:T(8,128)(2,1)S(1)} %encode_terms.1.refs_0_), channel_id=1, source_target_pairs={{0,64},{4,68},{8,72},{12,76},{16,80},{20,84},{24,88},{28,92},{32,9... | collective-permute-start | bytes 98312 | tf_op jit(solution)/shard_map/ppermute | solution.py:31
  18.5 5.6 %collective-permute-start.1 = (f32[128,128]{1,0:T(8,128)S(1)}, f32[128,128]{1,0:T(8,128)S(1)}, u32[]{:S(2)}, u32[]{:S(2)}) collective-permute-start(f32[128,128]{1,0:T(8,128)S(1)} %join.8), channel_id=1, source_target_pairs={{4,0},{8,4},{12,8},{16,12},{20,16},{24,20},{28,24},{32,28},{36,32}... | collective-permute-start | bytes 196616 | tf_op jit(solution)/shard_map/ppermute | solution.py:265
  21.0 8.6 %collective-permute-start = (f32[128,128]{1,0:T(8,128)S(1)}, f32[128,128]{1,0:T(8,128)S(1)}, u32[]{:S(2)}, u32[]{:S(2)}) collective-permute-start(f32[128,128]{1,0:T(8,128)S(1)} %join.8), channel_id=1, source_target_pairs={{0,4},{4,8},{8,12},{12,16},{16,20},{20,24},{24,28},{28,32},{32,36}... | collective-permute-start | bytes 196616 | tf_op jit(solution)/shard_map/ppermute | solution.py:265
  24.1 12.7 %collective-permute-start.3 = (s16[256,128]{1,0:T(8,128)(2,1)S(1)}, s16[256,128]{1,0:T(8,128)(2,1)S(1)}, u32[]{:S(2)}, u32[]{:S(2)}) collective-permute-start(s16[256,128]{1,0:T(8,128)(2,1)S(1)} %join.9.refs_0_), channel_id=1, source_target_pairs={{0,128},{4,132},{8,136},{12,140},{16,144},{20,148},{24,152},{28,15... | collective-permute-start | bytes 196616 | tf_op jit(solution)/shard_map/ppermute | solution.py:31
  31.8 21.1 %copy-start.6 = (bf16[1024,256]{1,0:T(8,128)(2,1)S(1)}, bf16[1024,256]{1,0:T(8,128)(2,1)}, u32[]{:S(2)}) copy-start(bf16[1024,256]{1,0:T(8,128)(2,1)} %copy-done.5) | copy-start | bytes 1572868
  31.8 25.3 %collective-permute-start.9 = (bf16[1024,256]{1,0:T(8,128)(2,1)}, bf16[1024,256]{1,0:T(8,128)(2,1)S(1)}, u32[]{:S(2)}, u32[]{:S(2)}) collective-permute-start(bf16[1024,256]{1,0:T(8,128)(2,1)} %get-tuple-element.23), channel_id=1, source_target_pairs={{0,1},{1,2},{2,3},{3,0},{4,5},{5,6},{6,7},{7,4},{8,9},{9,10},{10,1... | collective-permute-start | bytes 1572872 | tf_op jit(solution)/shard_map/ppermute | solution.py:35
  33.3 23.9 %collective-permute-start.10 = (bf16[1024,256]{1,0:T(8,128)(2,1)}, bf16[1024,256]{1,0:T(8,128)(2,1)S(1)}, u32[]{:S(2)}, u32[]{:S(2)}) collective-permute-start(bf16[1024,256]{1,0:T(8,128)(2,1)} %get-tuple-element.24), channel_id=1, source_target_pairs={{0,2},{1,3},{2,0},{3,1},{4,6},{5,7},{6,4},{7,5},{8,10},{9,11},{10,... | collective-permute-start | bytes 1572872 | tf_op jit(solution)/shard_map/ppermute | solution.py:35
  36.8 23.3 %collective-permute-start.11 = (bf16[1024,256]{1,0:T(8,128)(2,1)}, bf16[1024,256]{1,0:T(8,128)(2,1)S(1)}, u32[]{:S(2)}, u32[]{:S(2)}) collective-permute-start(bf16[1024,256]{1,0:T(8,128)(2,1)} %get-tuple-element.25), channel_id=1, source_target_pairs={{0,3},{1,0},{2,1},{3,2},{4,7},{5,4},{6,5},{7,6},{8,11},{9,8},{10,9... | collective-permute-start | bytes 1572872 | tf_op jit(solution)/shard_map/ppermute | solution.py:35
  36.8 5.1 %collective-permute-start.7 = (s16[512,128]{1,0:T(8,128)(2,1)S(1)}, s16[512,128]{1,0:T(8,128)(2,1)S(1)}, u32[]{:S(2)}, u32[]{:S(2)}) collective-permute-start(s16[512,128]{1,0:T(8,128)(2,1)S(1)} %join.10.refs_0_), channel_id=1, source_target_pairs={{0,32},{4,36},{8,40},{12,44},{16,48},{20,52},{24,56},{28,60},{32,0... | collective-permute-start | bytes 393224 | tf_op jit(solution)/shard_map/ppermute | solution.py:31
  41.9 15.2 %collective-permute-start.8 = (s16[1024,128]{1,0:T(8,128)(2,1)S(1)}, s16[1024,128]{1,0:T(8,128)(2,1)S(1)}, u32[]{:S(2)}, u32[]{:S(2)}) collective-permute-start(s16[1024,128]{1,0:T(8,128)(2,1)S(1)} %join.11.refs_0_), channel_id=1, source_target_pairs={{0,8},{4,12},{8,0},{12,4},{16,24},{20,28},{24,16},{28,20},{32,40},... | collective-permute-start | bytes 786440 | tf_op jit(solution)/shard_map/ppermute | solution.py:31
  51.6 1.3 copy-start.2
  53.0 7.1 %copy-start = (f32[4096,128]{1,0:T(8,128)}, f32[4096,128]{1,0:T(8,128)S(1)}, u32[]{:S(2)}) copy-start(f32[4096,128]{1,0:T(8,128)S(1)} %get-tuple-element.21.refs_3_.refs_2_) | copy-start | bytes 6291460
  57.1 3.0 %copy-start.7 = (s16[1024,128]{1,0:T(8,128)(2,1)}, s16[1024,128]{1,0:T(8,128)(2,1)S(1)}, u32[]{:S(2)}) copy-start(s16[1024,128]{1,0:T(8,128)(2,1)S(1)} %get-tuple-element.22.refs_2_.refs_5_) | copy-start | bytes 786436
  60.0 8.8 %copy-start.4 = (bf16[1024,256]{1,0:T(8,128)(2,1)S(1)}, bf16[1024,256]{1,0:T(8,128)(2,1)}, u32[]{:S(2)}) copy-start(bf16[1024,256]{1,0:T(8,128)(2,1)} %get-tuple-element.42.b0) | copy-start | bytes 1572868
  60.1 18.2 %collective-permute-start.12 = (s16[2048,128]{1,0:T(8,128)(2,1)S(1)}, s16[2048,128]{1,0:T(8,128)(2,1)S(1)}, u32[]{:S(2)}, u32[]{:S(2)}) collective-permute-start(s16[2048,128]{1,0:T(8,128)(2,1)S(1)} %join.12.refs_0_), channel_id=1, source_target_pairs={{0,16},{4,20},{8,24},{12,28},{16,0},{20,4},{24,8},{28,12},{32,48},... | collective-permute-start | bytes 1572872 | tf_op jit(solution)/shard_map/ppermute | solution.py:31
  63.2 9.3 %collective-permute-start.13 = (s16[1024,128]{1,0:T(8,128)(2,1)S(1)}, s16[1024,128]{1,0:T(8,128)(2,1)S(1)}, u32[]{:S(2)}, u32[]{:S(2)}) collective-permute-start(s16[1024,128]{1,0:T(8,128)(2,1)S(1)} %get-tuple-element.27), channel_id=1, source_target_pairs={{0,1},{1,2},{2,3},{3,0},{4,5},{5,6},{6,7},{7,4},{8,9},{9,10},{10,1... | collective-permute-start | bytes 786440 | tf_op jit(solution)/shard_map/ppermute | solution.py:35
  63.8 10.8 %collective-permute-start.14 = (s16[1024,128]{1,0:T(8,128)(2,1)S(1)}, s16[1024,128]{1,0:T(8,128)(2,1)S(1)}, u32[]{:S(2)}, u32[]{:S(2)}) collective-permute-start(s16[1024,128]{1,0:T(8,128)(2,1)S(1)} %get-tuple-element.28), channel_id=1, source_target_pairs={{0,2},{1,3},{2,0},{3,1},{4,6},{5,7},{6,4},{7,5},{8,10},{9,11},{10,... | collective-permute-start | bytes 786440 | tf_op jit(solution)/shard_map/ppermute | solution.py:35
  67.1 11.2 %collective-permute-start.15 = (s16[1024,128]{1,0:T(8,128)(2,1)S(1)}, s16[1024,128]{1,0:T(8,128)(2,1)S(1)}, u32[]{:S(2)}, u32[]{:S(2)}) collective-permute-start(s16[1024,128]{1,0:T(8,128)(2,1)S(1)} %get-tuple-element.29), channel_id=1, source_target_pairs={{0,3},{1,0},{2,1},{3,2},{4,7},{5,4},{6,5},{7,6},{8,11},{9,8},{10,9... | collective-permute-start | bytes 786440 | tf_op jit(solution)/shard_map/ppermute | solution.py:35
  72.5 5.8 %copy-start.18 = (s16[1024,128]{1,0:T(8,128)(2,1)}, s16[1024,128]{1,0:T(8,128)(2,1)S(1)}, u32[]{:S(2)}) copy-start(s16[1024,128]{1,0:T(8,128)(2,1)S(1)} %get-tuple-element.34) | copy-start | bytes 786436
  72.5 5.8 %copy-start.19 = (s16[1024,128]{1,0:T(8,128)(2,1)}, s16[1024,128]{1,0:T(8,128)(2,1)S(1)}, u32[]{:S(2)}) copy-start(s16[1024,128]{1,0:T(8,128)(2,1)S(1)} %get-tuple-element.33) | copy-start | bytes 786436
  72.5 11.9 %copy-start.1 = (f32[4096,128]{1,0:T(8,128)S(1)}, f32[4096,128]{1,0:T(8,128)}, u32[]{:S(2)}) copy-start(f32[4096,128]{1,0:T(8,128)} %copy-done) | copy-start | bytes 6291460
  72.5 5.8 %copy-start.9 = (s16[1024,128]{1,0:T(8,128)(2,1)}, s16[1024,128]{1,0:T(8,128)(2,1)S(1)}, u32[]{:S(2)}) copy-start(s16[1024,128]{1,0:T(8,128)(2,1)S(1)} %collective-permute-done.13.refs_3_.refs_6_) | copy-start | bytes 786436
  74.6 3.8 %copy-start.11 = (s16[1024,128]{1,0:T(8,128)(2,1)}, s16[1024,128]{1,0:T(8,128)(2,1)S(1)}, u32[]{:S(2)}) copy-start(s16[1024,128]{1,0:T(8,128)(2,1)S(1)} %collective-permute-done.14.refs_4_.refs_7_) | copy-start | bytes 786436
  79.0 5.5 %collective-permute-start.16 = (s16[4096,128]{1,0:T(8,128)(2,1)S(1)}, s16[4096,128]{1,0:T(8,128)(2,1)}, u32[]{:S(2)}, u32[]{:S(2)}) collective-permute-start(s16[4096,128]{1,0:T(8,128)(2,1)S(1)} %join.13.refs_3_), channel_id=1, source_target_pairs={{0,4},{4,0},{8,12},{12,8},{16,20},{20,16},{24,28},{28,24},{32,36},... | collective-permute-start | bytes 3145736 | tf_op jit(solution)/shard_map/ppermute | solution.py:31
  79.1 20.1 %collective-permute-start.17 = (s16[1024,128]{1,0:T(8,128)(2,1)}, s16[1024,128]{1,0:T(8,128)(2,1)S(1)}, u32[]{:S(2)}, u32[]{:S(2)}) collective-permute-start(s16[1024,128]{1,0:T(8,128)(2,1)} %copy-done.20), channel_id=1, source_target_pairs={{0,1},{1,2},{2,3},{3,0},{4,5},{5,6},{6,7},{7,4},{8,9},{9,10},{10,1... | collective-permute-start | bytes 786440 | tf_op jit(solution)/shard_map/ppermute | solution.py:35
  79.7 19.5 %collective-permute-start.18 = (s16[1024,128]{1,0:T(8,128)(2,1)}, s16[1024,128]{1,0:T(8,128)(2,1)S(1)}, u32[]{:S(2)}, u32[]{:S(2)}) collective-permute-start(s16[1024,128]{1,0:T(8,128)(2,1)} %copy-done.19), channel_id=1, source_target_pairs={{0,2},{1,3},{2,0},{3,1},{4,6},{5,7},{6,4},{7,5},{8,10},{9,11},{10,... | collective-permute-start | bytes 786440 | tf_op jit(solution)/shard_map/ppermute | solution.py:35
  83.0 16.2 %collective-permute-start.19 = (s16[1024,128]{1,0:T(8,128)(2,1)}, s16[1024,128]{1,0:T(8,128)(2,1)S(1)}, u32[]{:S(2)}, u32[]{:S(2)}) collective-permute-start(s16[1024,128]{1,0:T(8,128)(2,1)} %copy-done.18), channel_id=1, source_target_pairs={{0,3},{1,0},{2,1},{3,2},{4,7},{5,4},{6,5},{7,6},{8,11},{9,8},{10,9... | collective-permute-start | bytes 786440 | tf_op jit(solution)/shard_map/ppermute | solution.py:35
  84.4 1.0 copy-start.8
  85.4 0.9 copy-start.10
  88.2 10.9 %copy-start.3 = (f32[4096,128]{1,0:T(8,128)S(1)}, f32[4096,128]{1,0:T(8,128)}, u32[]{:S(2)}) copy-start(f32[4096,128]{1,0:T(8,128)} %copy-done.2) | copy-start | bytes 6291460
  110.0 4.2 %collective-permute-start.22 = (f32[4096,128]{1,0:T(8,128)S(1)}, f32[4096,128]{1,0:T(8,128)S(1)}, u32[]{:S(2)}, u32[]{:S(2)}) collective-permute-start(f32[4096,128]{1,0:T(8,128)S(1)} %get-tuple-element.39), channel_id=1, source_target_pairs={{0,4},{4,0},{8,12},{12,8},{16,20},{20,16},{24,28},{28,24},{32,36},... | collective-permute-start | bytes 6291464 | tf_op jit(solution)/shard_map/ppermute | solution.py:31
  114.7 10.8 %collective-permute-start.25 = (f16[2,4,128,128]{3,2,1,0:T(8,128)(2,1)S(1)}, f16[2,4,128,128]{3,2,1,0:T(8,128)(2,1)S(1)}, u32[]{:S(2)}, u32[]{:S(2)}) collective-permute-start(f16[2,4,128,128]{3,2,1,0:T(8,128)(2,1)S(1)} %bitcast.66), channel_id=1, source_target_pairs={{0,16},{4,20},{8,24},{12,28},{16,0},{20,4},{24,8},{28,12},{32,48},... | collective-permute-start | bytes 786440 | tf_op jit(solution)/shard_map/ppermute | solution.py:31
  115.1 13.7 %collective-permute-start.23 = (f16[2,4,128,128]{3,2,1,0:T(8,128)(2,1)S(1)}, f16[2,4,128,128]{3,2,1,0:T(8,128)(2,1)S(1)}, u32[]{:S(2)}, u32[]{:S(2)}) collective-permute-start(f16[2,4,128,128]{3,2,1,0:T(8,128)(2,1)S(1)} %bitcast.65), channel_id=1, source_target_pairs={{0,8},{4,12},{8,0},{12,4},{16,24},{20,28},{24,16},{28,20},{32,40},... | collective-permute-start | bytes 786440 | tf_op jit(solution)/shard_map/ppermute | solution.py:31
  116.9 13.4 %collective-permute-start.24 = (f16[2,4,128,128]{3,2,1,0:T(8,128)(2,1)S(1)}, f16[2,4,128,128]{3,2,1,0:T(8,128)(2,1)S(1)}, u32[]{:S(2)}, u32[]{:S(2)}) collective-permute-start(f16[2,4,128,128]{3,2,1,0:T(8,128)(2,1)S(1)} %bitcast.64), channel_id=1, source_target_pairs={{0,24},{4,28},{8,16},{12,20},{16,8},{20,12},{24,0},{28,4},{32,56},... | collective-permute-start | bytes 786440 | tf_op jit(solution)/shard_map/ppermute | solution.py:31
  120.7 12.4 %collective-permute-start.20 = (f32[128,128]{1,0:T(8,128)S(1)}, f32[128,128]{1,0:T(8,128)S(1)}, u32[]{:S(2)}, u32[]{:S(2)}) collective-permute-start(f32[128,128]{1,0:T(8,128)S(1)} %get-tuple-element.55), channel_id=1, source_target_pairs={{0,4},{4,8},{8,12},{12,16},{16,20},{20,24},{24,28},{28,32},{32,36}... | collective-permute-start | bytes 196616 | tf_op jit(solution)/shard_map/ppermute | solution.py:265
  122.1 11.1 %collective-permute-start.21 = (f32[128,128]{1,0:T(8,128)S(1)}, f32[128,128]{1,0:T(8,128)S(1)}, u32[]{:S(2)}, u32[]{:S(2)}) collective-permute-start(f32[128,128]{1,0:T(8,128)S(1)} %get-tuple-element.56), channel_id=1, source_target_pairs={{4,0},{8,4},{12,8},{16,12},{20,16},{24,20},{28,24},{32,28},{36,32}... | collective-permute-start | bytes 196616 | tf_op jit(solution)/shard_map/ppermute | solution.py:265
  130.5 6.4 %collective-permute-start.26 = (f16[4,128,128]{2,1,0:T(8,128)(2,1)S(1)}, f16[4,128,128]{2,1,0:T(8,128)(2,1)S(1)}, u32[]{:S(2)}, u32[]{:S(2)}) collective-permute-start(f16[4,128,128]{2,1,0:T(8,128)(2,1)S(1)} %get-tuple-element.53), channel_id=1, source_target_pairs={{0,32},{4,36},{8,40},{12,44},{16,48},{20,52},{24,56},{28,60},{32,0... | collective-permute-start | bytes 393224 | tf_op jit(solution)/shard_map/ppermute | solution.py:31
  133.2 19.1 %copy-start.15 = (f32[128,128]{1,0:T(8,128)}, f32[128,128]{1,0:T(8,128)S(1)}, u32[]{:S(2)}) copy-start(f32[128,128]{1,0:T(8,128)S(1)} %fusion.7.refs_1_) | copy-start | bytes 196612
  136.9 6.7 %collective-permute-start.27 = (f16[2,128,128]{2,1,0:T(8,128)(2,1)S(1)}, f16[2,128,128]{2,1,0:T(8,128)(2,1)S(1)}, u32[]{:S(2)}, u32[]{:S(2)}) collective-permute-start(f16[2,128,128]{2,1,0:T(8,128)(2,1)S(1)} %fusion.4), channel_id=1, source_target_pairs={{0,64},{4,68},{8,72},{12,76},{16,80},{20,84},{24,88},{28,92},{32,9... | collective-permute-start | bytes 196616 | tf_op jit(solution)/shard_map/ppermute | solution.py:31
  143.6 8.0 %collective-permute-start.28 = (f16[128,128]{1,0:T(8,128)(2,1)S(1)}, f16[128,128]{1,0:T(8,128)(2,1)S(1)}, u32[]{:S(2)}, u32[]{:S(2)}) collective-permute-start(f16[128,128]{1,0:T(8,128)(2,1)S(1)} %fusion.23), channel_id=1, source_target_pairs={{0,128},{4,132},{8,136},{12,140},{16,144},{20,148},{24,152},{28,15... | collective-permute-start | bytes 98312 | tf_op jit(solution)/shard_map/ppermute | solution.py:31
  (4 other events, 3.3 us)

commit v11 on v10

--- a/solution.py
+++ b/solution.py
@@ -14,7 +14,7 @@
 REC_SCALE = 65535.0 / (REC_HIGH - REC_LOW)
 SUM_SCALE = 1.0 / 32.0
 PIECES = (1024, 1024)
-SUMS = pltpu.CompilerParams(vmem_limit_bytes=32 * 2**20)
+SUMS = pltpu.CompilerParams(vmem_limit_bytes=24 * 2**20)
 SMALL = pltpu.CompilerParams(vmem_limit_bytes=12 * 2**20)
 COST = pl.CostEstimate(flops=1000, bytes_accessed=1000, transcendentals=0)
 
@@ -308,8 +308,8 @@
     terms = join([terms, swap(terms, 4, 0, 0)], got[0][1:] + [shot_near])
     terms = join([terms, swap(terms, 1, 0, 0)])
     shots = gather_shots(shot_near, shot_at, [size * NY for size in PIECES])
-    terms = join([terms, swap(terms, 0, 1, 0)], [coded[0][0], shots[0], rec_at] + got[1][1:])
-    terms = join([terms, swap(terms, 0, 2, 0)], [coded[1][0]] + codes[1:NY])
+    terms = join([terms, swap(terms, 0, 1, 0)], [codes[1], shots[0], rec_at] + got[1][1:])
+    terms = join([terms, swap(terms, 0, 2, 0)], [coded[1][0]] + codes[2:NY])
     far_terms = swap(terms, 0, 0, 1)
 
     sums, residuals, done = (), [], 0

time: 153 us -> 156 us (1.020)
  waiting for transfers between devices: 33.9 us -> 37 us
    ppermute x12, waiting for transfers between devices: 10.9 us -> 18.1 us  [send_y(): return lax.ppermute(value, 'fq', [(i, (i + k) % NY) for i in range(NY)])]
    ppermute x13, waiting for transfers between devices: 23 us -> 18.8 us  [swap(): lax.ppermute(value, 'tr', [(tr_of(z, x, c), tr_of(z ^ dz, x ^ dx, c ^ dc)...]
    ppermute x12, starting transfers between devices: 20.8 us -> 18.5 us  [send_y(): return lax.ppermute(value, 'fq', [(i, (i + k) % NY) for i in range(NY)])]
  transfers between devices with their start and end apart: 29 -> 29, of which waited for: 13 -> 12; matrix products, arithmetic and copies ran while one was open for 0% -> 0% of each run, Pallas kernels for 22% -> 21%
where the time goes in v11:
time: 156 us; the launch traced here: 155 us
  starting transfers between devices  58.9 us (38%)
  Pallas kernels  44.3 us (28%)
  waiting for transfers between devices  37 us (24%)
  local copies, waits for them, and re-layouts  11.6 us (7%)
  between operations  2.03 us (1%)
    ppermute x13, starting transfers between devices, swap(): lax.ppermute(value, 'tr', [(tr_of(z, x, c), tr_of(z ^ dz, x ^ dx, c ^ dc)...  33.4 us
    pallas_call x2, Pallas kernels, sum_receivers(): pl.pallas_call(body, in_specs=[sm, sm] + [vm] * (3 + parts + held), out_s...  21.9 us
    ppermute x13, waiting for transfers between devices, swap(): lax.ppermute(value, 'tr', [(tr_of(z, x, c), tr_of(z ^ dz, x ^ dx, c ^ dc)...  18.8 us
    ppermute x12, starting transfers between devices, send_y(): return lax.ppermute(value, 'fq', [(i, (i + k) % NY) for i in range(NY)])  18.5 us
    ppermute x12, waiting for transfers between devices, send_y(): return lax.ppermute(value, 'fq', [(i, (i + k) % NY) for i in range(NY)])  18.1 us
    pallas_call x1, Pallas kernels, gather_shots(): pl.pallas_call(body, in_specs=[sm, vm], out_specs=[vm] * len(sizes), out_...  8.11 us
    unnamed x51, local copies, waits for them, and re-layouts  7.1 us
    pallas_call x2, Pallas kernels, spectra(): pl.pallas_call(body, grid=(rows // tile,), in_specs=[pl.BlockSpec((tile,...  6.97 us
  transfers between devices with their start and end apart: 29, of which 12 were waited for; matrix products, arithmetic and copies ran while one was open for 0% of the time, Pallas kernels for 21%

profile of v11, /device:TPU:8, one launch (start us, length us, event | category | flops | bytes accessed | tf_op | source)
XLA Modules:
  0.0 155.2 jit_solution(13860721497236080111)
XLA Ops:
  0.7 4.0 %constant_dynamic-slice_fusion = (bf16[1024,256]{1,0:T(8,128)(2,1)}, bf16[1024,256]{1,0:T(8,128)(2,1)}, bf16[1024,256]{1,0:T(8,128)(2,1)}, bf16[1024,256]{1,0:T(...) fusion(bf16[8192,256]{1,0:T(8,128)(2,1)} %param.6, ...), kind=kLoop, calls=%fused_computation.74 | loop fusion | bytes 8388640 | tf_op jit(solution)/shard_map/dynamic_slice | solution.py:278
  4.7 2.3 %collective-permute-start.6 = (bf16[1024,256]{1,0:T(8,128)(2,1)}, bf16[1024,256]{1,0:T(8,128)(2,1)S(1)}, u32[]{:S(2)}, u32[]{:S(2)}) collective-permute-start(bf16[1024,256]{1,0:T(8,128)(2,1)} %get-tuple-element.45), channel_id=1, source_target_pairs={{0,3},{1,0},{2,1},{3,2},{4,7},{5,4},{6,5},{7,6},{8,11},{9,8},{10,9... | collective-permute-start | bytes 1572872 | tf_op jit(solution)/shard_map/ppermute | solution.py:35
  7.0 0.9 collective-permute-start.5
  7.8 1.9 %collective-permute-start.4 = (bf16[1024,256]{1,0:T(8,128)(2,1)}, bf16[1024,256]{1,0:T(8,128)(2,1)}, u32[]{:S(2)}, u32[]{:S(2)}) collective-permute-start(bf16[1024,256]{1,0:T(8,128)(2,1)} %get-tuple-element.47), channel_id=1, source_target_pairs={{0,1},{1,2},{2,3},{3,0},{4,5},{5,6},{6,7},{7,4},{8,9},{9,10},{10,1... | collective-permute-start | bytes 1572872 | tf_op jit(solution)/shard_map/ppermute | solution.py:35
  9.7 5.3 %make_table.1.refs_1_.refs_0_.t = bf16[1024,1024]{1,0:T(8,128)(2,1)S(1)} custom-call(s32[1]{0:T(128)} %bitcast.10.y_ref, bf16[1024,256]{1,0:T(8,128)(2,1)S(1)} %get-tuple-element.48.refs_0_.b0), custom_call_target="tpu_custom_call" | custom-call | flops 1073741824 | bytes 33554432 | tf_op jit(solution)/shard_map/make_table/pallas_call | solution.py:62
  15.1 3.4 %collective-permute-start.2 = (s16[128,128]{1,0:T(8,128)(2,1)S(1)}, s16[128,128]{1,0:T(8,128)(2,1)S(1)}, u32[]{:S(2)}, u32[]{:S(2)}) collective-permute-start(s16[128,128]{1,0:T(8,128)(2,1)S(1)} %encode_terms.1.refs_0_), channel_id=1, source_target_pairs={{0,64},{4,68},{8,72},{12,76},{16,80},{20,84},{24,88},{28,92},{32,9... | collective-permute-start | bytes 98312 | tf_op jit(solution)/shard_map/ppermute | solution.py:31
  18.5 1.3 collective-permute-start.1
  21.0 3.0 %collective-permute-start = (f32[128,128]{1,0:T(8,128)S(1)}, f32[128,128]{1,0:T(8,128)S(1)}, u32[]{:S(2)}, u32[]{:S(2)}) collective-permute-start(f32[128,128]{1,0:T(8,128)S(1)} %join.8), channel_id=1, source_target_pairs={{0,4},{4,8},{8,12},{12,16},{16,20},{20,24},{24,28},{28,32},{32,36}... | collective-permute-start | bytes 196616 | tf_op jit(solution)/shard_map/ppermute | solution.py:265
  24.1 5.5 %collective-permute-start.3 = (s16[256,128]{1,0:T(8,128)(2,1)S(1)}, s16[256,128]{1,0:T(8,128)(2,1)S(1)}, u32[]{:S(2)}, u32[]{:S(2)}) collective-permute-start(s16[256,128]{1,0:T(8,128)(2,1)S(1)} %join.9.refs_0_), channel_id=1, source_target_pairs={{0,128},{4,132},{8,136},{12,140},{16,144},{20,148},{24,152},{28,15... | collective-permute-start | bytes 196616 | tf_op jit(solution)/shard_map/ppermute | solution.py:31
  29.6 1.3 collective-permute-done.5.refs_3_.b2.refs_4_
  30.9 0.9 collective-permute-done.4.refs_2_.b1.refs_3_
  31.8 1.4 collective-permute-start.10
  33.3 3.5 %collective-permute-start.11 = (bf16[1024,256]{1,0:T(8,128)(2,1)}, bf16[1024,256]{1,0:T(8,128)(2,1)S(1)}, u32[]{:S(2)}, u32[]{:S(2)}) collective-permute-start(bf16[1024,256]{1,0:T(8,128)(2,1)} %get-tuple-element.24), channel_id=1, source_target_pairs={{0,2},{1,3},{2,0},{3,1},{4,6},{5,7},{6,4},{7,5},{8,10},{9,11},{10,... | collective-permute-start | bytes 1572872 | tf_op jit(solution)/shard_map/ppermute | solution.py:35
  36.8 2.0 %collective-permute-start.7 = (s16[512,128]{1,0:T(8,128)(2,1)S(1)}, s16[512,128]{1,0:T(8,128)(2,1)S(1)}, u32[]{:S(2)}, u32[]{:S(2)}) collective-permute-start(s16[512,128]{1,0:T(8,128)(2,1)S(1)} %join.10.refs_0_), channel_id=1, source_target_pairs={{0,32},{4,36},{8,40},{12,44},{16,48},{20,52},{24,56},{28,60},{32,0... | collective-permute-start | bytes 393224 | tf_op jit(solution)/shard_map/ppermute | solution.py:31
  38.8 4.0 %spectra.2 = (s16[1024,128]{1,0:T(8,128)(2,1)S(1)}, s16[1024,128]{1,0:T(8,128)(2,1)S(1)}, s16[1024,128]{1,0:T(8,128)(2,1)S(1)}, s16[1024,128]{1,0:T(8,128)(2,1)S(1)}) custom-call(bf16[1024,256]{1,0:T(8,128)(2,1)S(1)} %copy-done.6, bf16[1024,256]{1,0:T(8,128)(2,1)} %collective-permute-done.4.refs_2_.b1.refs_3_, ...), custom_call_target="tpu_custom_call" | custom-call | flops 1000 | bytes 1000 | tf_op jit(solution)/shard_map/spectra/pallas_call | solution.py:142
  42.8 2.1 %collective-permute-start.9 = (s16[1024,128]{1,0:T(8,128)(2,1)S(1)}, s16[1024,128]{1,0:T(8,128)(2,1)S(1)}, u32[]{:S(2)}, u32[]{:S(2)}) collective-permute-start(s16[1024,128]{1,0:T(8,128)(2,1)S(1)} %get-tuple-element.22), channel_id=1, source_target_pairs={{0,1},{1,2},{2,3},{3,0},{4,5},{5,6},{6,7},{7,4},{8,9},{9,10},{10,1... | collective-permute-start | bytes 786440 | tf_op jit(solution)/shard_map/ppermute | solution.py:35
  44.9 1.6 %collective-permute-start.8 = (s16[1024,128]{1,0:T(8,128)(2,1)S(1)}, s16[1024,128]{1,0:T(8,128)(2,1)S(1)}, u32[]{:S(2)}, u32[]{:S(2)}) collective-permute-start(s16[1024,128]{1,0:T(8,128)(2,1)S(1)} %join.11.refs_0_), channel_id=1, source_target_pairs={{0,8},{4,12},{8,0},{12,4},{16,24},{20,28},{24,16},{28,20},{32,40},... | collective-permute-start | bytes 786440 | tf_op jit(solution)/shard_map/ppermute | solution.py:31
  46.5 8.1 %gather_shots.1 = (f32[4096,128]{1,0:T(8,128)S(1)}, f32[4096,128]{1,0:T(8,128)S(1)}) custom-call(s32[8192]{0:T(1024)S(1)} %bitcast_dynamic-update-slice_fusion.shot_at, f32[384,128]{1,0:T(8,128)S(1)} %pad_maximum_fusion.shot.refs_5_), custom_call_target="tpu_custom_call" | custom-call | flops 1000 | bytes 1000 | tf_op jit(solution)/shard_map/gather_shots/pallas_call | solution.py:171
  54.6 1.3 copy-done.2
  56.0 8.0 %collective-permute-done.9.refs_2_.refs_6_ = s16[1024,128]{1,0:T(8,128)(2,1)S(1)} collective-permute-done((s16[1024,128]{1,0:T(8,128)(2,1)S(1)}, s16[1024,128]{1,0:T(8,128)(2,1)S(1)}, u32[]{:S(2)}, u32[]{:S(2)}) %collective-permute-start.9) | collective-permute-done | bytes 262176 | tf_op jit(solution)/shard_map/ppermute | solution.py:35
  64.6 3.0 %collective-permute-start.13 = (s16[2048,128]{1,0:T(8,128)(2,1)S(1)}, s16[2048,128]{1,0:T(8,128)(2,1)S(1)}, u32[]{:S(2)}, u32[]{:S(2)}) collective-permute-start(s16[2048,128]{1,0:T(8,128)(2,1)S(1)} %join.12.refs_0_), channel_id=1, source_target_pairs={{0,16},{4,20},{8,24},{12,28},{16,0},{20,4},{24,8},{28,12},{32,48},... | collective-permute-start | bytes 1572872 | tf_op jit(solution)/shard_map/ppermute | solution.py:31
  67.6 1.3 collective-permute-start.14
  68.9 1.6 %collective-permute-start.15 = (s16[1024,128]{1,0:T(8,128)(2,1)S(1)}, s16[1024,128]{1,0:T(8,128)(2,1)S(1)}, u32[]{:S(2)}, u32[]{:S(2)}) collective-permute-start(s16[1024,128]{1,0:T(8,128)(2,1)S(1)} %get-tuple-element.28), channel_id=1, source_target_pairs={{0,3},{1,0},{2,1},{3,2},{4,7},{5,4},{6,5},{7,6},{8,11},{9,8},{10,9... | collective-permute-start | bytes 786440 | tf_op jit(solution)/shard_map/ppermute | solution.py:35
  70.5 3.0 %spectra.3 = (s16[1024,128]{1,0:T(8,128)(2,1)S(1)}, s16[1024,128]{1,0:T(8,128)(2,1)S(1)}, s16[1024,128]{1,0:T(8,128)(2,1)S(1)}, s16[1024,128]{1,0:T(8,128)(2,1)S(1)}) custom-call(bf16[1024,256]{1,0:T(8,128)(2,1)S(1)} %copy-done.4, bf16[1024,256]{1,0:T(8,128)(2,1)S(1)} %collective-permute-done.10.refs_5_.b1, ...), custom_call_target="tpu_custom_call" | custom-call | flops 1000 | bytes 1000 | tf_op jit(solution)/shard_map/spectra/pallas_call | solution.py:142
  74.3 4.1 %collective-permute-done.14.refs_3_.refs_7_ = s16[1024,128]{1,0:T(8,128)(2,1)S(1)} collective-permute-done((s16[1024,128]{1,0:T(8,128)(2,1)S(1)}, s16[1024,128]{1,0:T(8,128)(2,1)S(1)}, u32[]{:S(2)}, u32[]{:S(2)}) %collective-permute-start.14) | collective-permute-done | bytes 262176 | tf_op jit(solution)/shard_map/ppermute | solution.py:35
  78.4 3.8 %collective-permute-done.15.refs_4_.refs_8_ = s16[1024,128]{1,0:T(8,128)(2,1)S(1)} collective-permute-done((s16[1024,128]{1,0:T(8,128)(2,1)S(1)}, s16[1024,128]{1,0:T(8,128)(2,1)S(1)}, u32[]{:S(2)}, u32[]{:S(2)}) %collective-permute-start.15) | collective-permute-done | bytes 262176 | tf_op jit(solution)/shard_map/ppermute | solution.py:35
  83.6 0.9 collective-permute-start.18
  84.5 2.1 %collective-permute-start.19 = (s16[1024,128]{1,0:T(8,128)(2,1)}, s16[1024,128]{1,0:T(8,128)(2,1)S(1)}, u32[]{:S(2)}, u32[]{:S(2)}) collective-permute-start(s16[1024,128]{1,0:T(8,128)(2,1)} %copy-done.18), channel_id=1, source_target_pairs={{0,3},{1,0},{2,1},{3,2},{4,7},{5,4},{6,5},{7,6},{8,11},{9,8},{10,9... | collective-permute-start | bytes 786440 | tf_op jit(solution)/shard_map/ppermute | solution.py:35
  86.7 0.9 copy-done.8
  87.6 0.9 copy-done.10
  88.6 0.9 copy-done.12
  89.5 0.9 copy-done.15
  90.5 10.9 %sum_receivers.2 = (f32[4096,128]{1,0:T(8,128)S(1)}, f32[4096,128]{1,0:T(8,128)S(1)}, f32[4096,128]{1,0:T(8,128)S(1)}) custom-call(s32[4096]{0:T(1024)S(1)} %bitcast.61, s32[4]{0:T(128)S(1)} %get-tuple-element.70.refs_1_, f32[4096,128]{1,0:T(8,128)S(1)} %copy-done.1, s16[4096,128]{1,0:T(8,128)(2,1)S(1)} %join.13.refs_3_, ...), custom_call_target="tpu_custom_call" | custom-call | flops 1000 | bytes 1000 | tf_op jit(solution)/shard_map/sum_receivers/pallas_call | solution.py:222
  101.4 11.0 %sum_receivers.3 = (f32[4096,128]{1,0:T(8,128)S(1)}, f32[4096,128]{1,0:T(8,128)S(1)}, f32[4096,128]{1,0:T(8,128)S(1)}) custom-call(s32[4096]{0:T(1024)S(1)} %bitcast.59, s32[4]{0:T(128)S(1)} %get-tuple-element.69.refs_1_, f32[4096,128]{1,0:T(8,128)S(1)} %copy-done.3, s16[4096,128]{1,0:T(8,128)(2,1)S(1)} %join.13.refs_3_, ...), custom_call_target="tpu_custom_call" | custom-call | flops 1000 | bytes 1000 | tf_op jit(solution)/shard_map/sum_receivers/pallas_call | solution.py:222
  112.5 4.1 %collective-permute-done.22 = f32[4096,128]{1,0:T(8,128)S(1)} collective-permute-done((f32[4096,128]{1,0:T(8,128)S(1)}, f32[4096,128]{1,0:T(8,128)S(1)}, u32[]{:S(2)}, u32[]{:S(2)}) %collective-permute-start.22) | collective-permute-done | bytes 2097184 | tf_op jit(solution)/shard_map/ppermute | solution.py:31
  118.5 2.8 %collective-permute-start.24 = (f16[2,4,128,128]{3,2,1,0:T(8,128)(2,1)S(1)}, f16[2,4,128,128]{3,2,1,0:T(8,128)(2,1)S(1)}, u32[]{:S(2)}, u32[]{:S(2)}) collective-permute-start(f16[2,4,128,128]{3,2,1,0:T(8,128)(2,1)S(1)} %bitcast.64), channel_id=1, source_target_pairs={{0,24},{4,28},{8,16},{12,20},{16,8},{20,12},{24,0},{28,4},{32,56},... | collective-permute-start | bytes 786440 | tf_op jit(solution)/shard_map/ppermute | solution.py:31
  121.3 1.8 %sum_shots.1.refs_1_ = f32[384,128]{1,0:T(8,128)S(1)} custom-call(s32[1,8192]{1,0:T(1,128)S(1)} %bitcast.57, f32[4096,128]{1,0:T(8,128)S(1)} %get-tuple-element.30.refs_0_, f32[4096,128]{1,0:T(8,128)S(1)} %get-tuple-element.37.refs_1_), custom_call_target="tpu_custom_call" | custom-call | flops 1000 | bytes 1000 | tf_op jit(solution)/shard_map/sum_shots/pallas_call | solution.py:252
  123.1 1.3 collective-permute-start.20
  124.4 1.3 collective-permute-start.21
  125.8 2.1 %collective-permute-done.25 = f16[2,4,128,128]{3,2,1,0:T(8,128)(2,1)S(1)} collective-permute-done((f16[2,4,128,128]{3,2,1,0:T(8,128)(2,1)S(1)}, f16[2,4,128,128]{3,2,1,0:T(8,128)(2,1)S(1)}, u32[]{:S(2)}, u32[]{:S(2)}) %collective-permute-start.25) | collective-permute-done | bytes 262176 | tf_op jit(solution)/shard_map/ppermute | solution.py:31
  127.9 2.6 %collective-permute-done.23 = f16[2,4,128,128]{3,2,1,0:T(8,128)(2,1)S(1)} collective-permute-done((f16[2,4,128,128]{3,2,1,0:T(8,128)(2,1)S(1)}, f16[2,4,128,128]{3,2,1,0:T(8,128)(2,1)S(1)}, u32[]{:S(2)}, u32[]{:S(2)}) %collective-permute-start.23) | collective-permute-done | bytes 262176 | tf_op jit(solution)/shard_map/ppermute | solution.py:31
  130.5 2.2 %collective-permute-done.24 = f16[2,4,128,128]{3,2,1,0:T(8,128)(2,1)S(1)} collective-permute-done((f16[2,4,128,128]{3,2,1,0:T(8,128)(2,1)S(1)}, f16[2,4,128,128]{3,2,1,0:T(8,128)(2,1)S(1)}, u32[]{:S(2)}, u32[]{:S(2)}) %collective-permute-start.24) | collective-permute-done | bytes 262176 | tf_op jit(solution)/shard_map/ppermute | solution.py:31
  132.9 2.7 %collective-permute-start.26 = (f16[4,128,128]{2,1,0:T(8,128)(2,1)S(1)}, f16[4,128,128]{2,1,0:T(8,128)(2,1)S(1)}, u32[]{:S(2)}, u32[]{:S(2)}) collective-permute-start(f16[4,128,128]{2,1,0:T(8,128)(2,1)S(1)} %get-tuple-element.53), channel_id=1, source_target_pairs={{0,32},{4,36},{8,40},{12,44},{16,48},{20,52},{24,56},{28,60},{32,0... | collective-permute-start | bytes 393224 | tf_op jit(solution)/shard_map/ppermute | solution.py:31
  135.6 3.6 %collective-permute-done.26 = f16[4,128,128]{2,1,0:T(8,128)(2,1)S(1)} collective-permute-done((f16[4,128,128]{2,1,0:T(8,128)(2,1)S(1)}, f16[4,128,128]{2,1,0:T(8,128)(2,1)S(1)}, u32[]{:S(2)}, u32[]{:S(2)}) %collective-permute-start.26) | collective-permute-done | bytes 131104 | tf_op jit(solution)/shard_map/ppermute | solution.py:31
  139.3 3.2 %collective-permute-start.27 = (f16[2,128,128]{2,1,0:T(8,128)(2,1)S(1)}, f16[2,128,128]{2,1,0:T(8,128)(2,1)S(1)}, u32[]{:S(2)}, u32[]{:S(2)}) collective-permute-start(f16[2,128,128]{2,1,0:T(8,128)(2,1)S(1)} %fusion.4), channel_id=1, source_target_pairs={{0,64},{4,68},{8,72},{12,76},{16,80},{20,84},{24,88},{28,92},{32,9... | collective-permute-start | bytes 196616 | tf_op jit(solution)/shard_map/ppermute | solution.py:31
  142.6 2.3 %collective-permute-done.27 = f16[2,128,128]{2,1,0:T(8,128)(2,1)S(1)} collective-permute-done((f16[2,128,128]{2,1,0:T(8,128)(2,1)S(1)}, f16[2,128,128]{2,1,0:T(8,128)(2,1)S(1)}, u32[]{:S(2)}, u32[]{:S(2)}) %collective-permute-start.27) | collective-permute-done | bytes 65568 | tf_op jit(solution)/shard_map/ppermute | solution.py:31
  144.9 7.7 %collective-permute-start.28 = (f16[128,128]{1,0:T(8,128)(2,1)S(1)}, f16[128,128]{1,0:T(8,128)(2,1)S(1)}, u32[]{:S(2)}, u32[]{:S(2)}) collective-permute-start(f16[128,128]{1,0:T(8,128)(2,1)S(1)} %fusion.23), channel_id=1, source_target_pairs={{0,128},{4,132},{8,136},{12,140},{16,144},{20,148},{24,152},{28,15... | collective-permute-start | bytes 98312 | tf_op jit(solution)/shard_map/ppermute | solution.py:31
  152.6 1.9 %collective-permute-done.28 = f16[128,128]{1,0:T(8,128)(2,1)S(1)} collective-permute-done((f16[128,128]{1,0:T(8,128)(2,1)S(1)}, f16[128,128]{1,0:T(8,128)(2,1)S(1)}, u32[]{:S(2)}, u32[]{:S(2)}) %collective-permute-start.28) | collective-permute-done | bytes 32800 | tf_op jit(solution)/shard_map/ppermute | solution.py:31
  (104 shorter events, 6.3 us)
Async XLA Ops:
  4.7 10.4 %copy-start.5 = (bf16[1024,256]{1,0:T(8,128)(2,1)}, bf16[1024,256]{1,0:T(8,128)(2,1)S(1)}, u32[]{:S(2)}) copy-start(bf16[1024,256]{1,0:T(8,128)(2,1)S(1)} %get-tuple-element.48.refs_0_.b0) | copy-start | bytes 1572868
  4.7 10.3 %copy-start.16 = (f32[128,128]{1,0:T(8,128)S(1)}, f32[128,128]{1,0:T(8,128)}, u32[]{:S(2)}) copy-start(f32[128,128]{1,0:T(8,128)} %a.1) | copy-start | bytes 196612
  4.7 24.8 %collective-permute-start.6 = (bf16[1024,256]{1,0:T(8,128)(2,1)}, bf16[1024,256]{1,0:T(8,128)(2,1)S(1)}, u32[]{:S(2)}, u32[]{:S(2)}) collective-permute-start(bf16[1024,256]{1,0:T(8,128)(2,1)} %get-tuple-element.45), channel_id=1, source_target_pairs={{0,3},{1,0},{2,1},{3,2},{4,7},{5,4},{6,5},{7,6},{8,11},{9,8},{10,9... | collective-permute-start | bytes 1572872 | tf_op jit(solution)/shard_map/ppermute | solution.py:35
  7.0 23.9 %collective-permute-start.5 = (bf16[1024,256]{1,0:T(8,128)(2,1)}, bf16[1024,256]{1,0:T(8,128)(2,1)S(1)}, u32[]{:S(2)}, u32[]{:S(2)}) collective-permute-start(bf16[1024,256]{1,0:T(8,128)(2,1)} %get-tuple-element.46), channel_id=1, source_target_pairs={{0,2},{1,3},{2,0},{3,1},{4,6},{5,7},{6,4},{7,5},{8,10},{9,11},{10,... | collective-permute-start | bytes 1572872 | tf_op jit(solution)/shard_map/ppermute | solution.py:35
  7.8 24.0 %collective-permute-start.4 = (bf16[1024,256]{1,0:T(8,128)(2,1)}, bf16[1024,256]{1,0:T(8,128)(2,1)}, u32[]{:S(2)}, u32[]{:S(2)}) collective-permute-start(bf16[1024,256]{1,0:T(8,128)(2,1)} %get-tuple-element.47), channel_id=1, source_target_pairs={{0,1},{1,2},{2,3},{3,0},{4,5},{5,6},{6,7},{7,4},{8,9},{9,10},{10,1... | collective-permute-start | bytes 1572872 | tf_op jit(solution)/shard_map/ppermute | solution.py:35
  9.7 8.7 %copy-start.17 = (f32[128,128]{1,0:T(8,128)S(1)}, f32[128,128]{1,0:T(8,128)}, u32[]{:S(2)}) copy-start(f32[128,128]{1,0:T(8,128)} %refs_0_.1) | copy-start | bytes 196612
  15.0 5.5 %copy-start.21 = (s32[8192]{0:T(1024)S(1)}, s32[8192]{0:T(1024)}, u32[]{:S(2)}) copy-start(s32[8192]{0:T(1024)} %param.8) | copy-start | bytes 98308
  15.1 5.7 %copy-start.22 = (s32[8192]{0:T(1024)S(1)}, s32[8192]{0:T(1024)}, u32[]{:S(2)}) copy-start(s32[8192]{0:T(1024)} %param.7) | copy-start | bytes 98308
  15.1 5.8 %collective-permute-start.2 = (s16[128,128]{1,0:T(8,128)(2,1)S(1)}, s16[128,128]{1,0:T(8,128)(2,1)S(1)}, u32[]{:S(2)}, u32[]{:S(2)}) collective-permute-start(s16[128,128]{1,0:T(8,128)(2,1)S(1)} %encode_terms.1.refs_0_), channel_id=1, source_target_pairs={{0,64},{4,68},{8,72},{12,76},{16,80},{20,84},{24,88},{28,92},{32,9... | collective-permute-start | bytes 98312 | tf_op jit(solution)/shard_map/ppermute | solution.py:31
  18.5 5.6 %collective-permute-start.1 = (f32[128,128]{1,0:T(8,128)S(1)}, f32[128,128]{1,0:T(8,128)S(1)}, u32[]{:S(2)}, u32[]{:S(2)}) collective-permute-start(f32[128,128]{1,0:T(8,128)S(1)} %join.8), channel_id=1, source_target_pairs={{4,0},{8,4},{12,8},{16,12},{20,16},{24,20},{28,24},{32,28},{36,32}... | collective-permute-start | bytes 196616 | tf_op jit(solution)/shard_map/ppermute | solution.py:265
  21.0 8.6 %collective-permute-start = (f32[128,128]{1,0:T(8,128)S(1)}, f32[128,128]{1,0:T(8,128)S(1)}, u32[]{:S(2)}, u32[]{:S(2)}) collective-permute-start(f32[128,128]{1,0:T(8,128)S(1)} %join.8), channel_id=1, source_target_pairs={{0,4},{4,8},{8,12},{12,16},{16,20},{20,24},{24,28},{28,32},{32,36}... | collective-permute-start | bytes 196616 | tf_op jit(solution)/shard_map/ppermute | solution.py:265
  24.1 12.7 %collective-permute-start.3 = (s16[256,128]{1,0:T(8,128)(2,1)S(1)}, s16[256,128]{1,0:T(8,128)(2,1)S(1)}, u32[]{:S(2)}, u32[]{:S(2)}) collective-permute-start(s16[256,128]{1,0:T(8,128)(2,1)S(1)} %join.9.refs_0_), channel_id=1, source_target_pairs={{0,128},{4,132},{8,136},{12,140},{16,144},{20,148},{24,152},{28,15... | collective-permute-start | bytes 196616 | tf_op jit(solution)/shard_map/ppermute | solution.py:31
  31.8 7.0 %copy-start.6 = (bf16[1024,256]{1,0:T(8,128)(2,1)S(1)}, bf16[1024,256]{1,0:T(8,128)(2,1)}, u32[]{:S(2)}) copy-start(bf16[1024,256]{1,0:T(8,128)(2,1)} %copy-done.5) | copy-start | bytes 1572868
  31.8 32.1 %collective-permute-start.10 = (bf16[1024,256]{1,0:T(8,128)(2,1)}, bf16[1024,256]{1,0:T(8,128)(2,1)S(1)}, u32[]{:S(2)}, u32[]{:S(2)}) collective-permute-start(bf16[1024,256]{1,0:T(8,128)(2,1)} %get-tuple-element.23), channel_id=1, source_target_pairs={{0,1},{1,2},{2,3},{3,0},{4,5},{5,6},{6,7},{7,4},{8,9},{9,10},{10,1... | collective-permute-start | bytes 1572872 | tf_op jit(solution)/shard_map/ppermute | solution.py:35
  33.3 30.7 %collective-permute-start.11 = (bf16[1024,256]{1,0:T(8,128)(2,1)}, bf16[1024,256]{1,0:T(8,128)(2,1)S(1)}, u32[]{:S(2)}, u32[]{:S(2)}) collective-permute-start(bf16[1024,256]{1,0:T(8,128)(2,1)} %get-tuple-element.24), channel_id=1, source_target_pairs={{0,2},{1,3},{2,0},{3,1},{4,6},{5,7},{6,4},{7,5},{8,10},{9,11},{10,... | collective-permute-start | bytes 1572872 | tf_op jit(solution)/shard_map/ppermute | solution.py:35
  36.8 27.2 %collective-permute-start.12 = (bf16[1024,256]{1,0:T(8,128)(2,1)}, bf16[1024,256]{1,0:T(8,128)(2,1)S(1)}, u32[]{:S(2)}, u32[]{:S(2)}) collective-permute-start(bf16[1024,256]{1,0:T(8,128)(2,1)} %get-tuple-element.25), channel_id=1, source_target_pairs={{0,3},{1,0},{2,1},{3,2},{4,7},{5,4},{6,5},{7,6},{8,11},{9,8},{10,9... | collective-permute-start | bytes 1572872 | tf_op jit(solution)/shard_map/ppermute | solution.py:35
  36.8 8.1 %collective-permute-start.7 = (s16[512,128]{1,0:T(8,128)(2,1)S(1)}, s16[512,128]{1,0:T(8,128)(2,1)S(1)}, u32[]{:S(2)}, u32[]{:S(2)}) collective-permute-start(s16[512,128]{1,0:T(8,128)(2,1)S(1)} %join.10.refs_0_), channel_id=1, source_target_pairs={{0,32},{4,36},{8,40},{12,44},{16,48},{20,52},{24,56},{28,60},{32,0... | collective-permute-start | bytes 393224 | tf_op jit(solution)/shard_map/ppermute | solution.py:31
  42.8 21.2 %copy-start.14 = (s16[1024,128]{1,0:T(8,128)(2,1)}, s16[1024,128]{1,0:T(8,128)(2,1)S(1)}, u32[]{:S(2)}) copy-start(s16[1024,128]{1,0:T(8,128)(2,1)S(1)} %get-tuple-element.29.refs_5_) | copy-start | bytes 786436
  42.8 21.1 %collective-permute-start.9 = (s16[1024,128]{1,0:T(8,128)(2,1)S(1)}, s16[1024,128]{1,0:T(8,128)(2,1)S(1)}, u32[]{:S(2)}, u32[]{:S(2)}) collective-permute-start(s16[1024,128]{1,0:T(8,128)(2,1)S(1)} %get-tuple-element.22), channel_id=1, source_target_pairs={{0,1},{1,2},{2,3},{3,0},{4,5},{5,6},{6,7},{7,4},{8,9},{9,10},{10,1... | collective-permute-start | bytes 786440 | tf_op jit(solution)/shard_map/ppermute | solution.py:35
  44.9 19.0 %collective-permute-start.8 = (s16[1024,128]{1,0:T(8,128)(2,1)S(1)}, s16[1024,128]{1,0:T(8,128)(2,1)S(1)}, u32[]{:S(2)}, u32[]{:S(2)}) collective-permute-start(s16[1024,128]{1,0:T(8,128)(2,1)S(1)} %join.11.refs_0_), channel_id=1, source_target_pairs={{0,8},{4,12},{8,0},{12,4},{16,24},{20,28},{24,16},{28,20},{32,40},... | collective-permute-start | bytes 786440 | tf_op jit(solution)/shard_map/ppermute | solution.py:31
  54.6 1.3 copy-start.2
  56.0 8.1 %copy-start = (f32[4096,128]{1,0:T(8,128)}, f32[4096,128]{1,0:T(8,128)S(1)}, u32[]{:S(2)}) copy-start(f32[4096,128]{1,0:T(8,128)S(1)} %get-tuple-element.21.refs_3_.refs_2_) | copy-start | bytes 6291460
  64.0 6.6 %copy-start.4 = (bf16[1024,256]{1,0:T(8,128)(2,1)S(1)}, bf16[1024,256]{1,0:T(8,128)(2,1)}, u32[]{:S(2)}) copy-start(bf16[1024,256]{1,0:T(8,128)(2,1)} %get-tuple-element.42.b0) | copy-start | bytes 1572868
  64.6 17.6 %collective-permute-start.13 = (s16[2048,128]{1,0:T(8,128)(2,1)S(1)}, s16[2048,128]{1,0:T(8,128)(2,1)S(1)}, u32[]{:S(2)}, u32[]{:S(2)}) collective-permute-start(s16[2048,128]{1,0:T(8,128)(2,1)S(1)} %join.12.refs_0_), channel_id=1, source_target_pairs={{0,16},{4,20},{8,24},{12,28},{16,0},{20,4},{24,8},{28,12},{32,48},... | collective-permute-start | bytes 1572872 | tf_op jit(solution)/shard_map/ppermute | solution.py:31
  67.6 10.8 %collective-permute-start.14 = (s16[1024,128]{1,0:T(8,128)(2,1)S(1)}, s16[1024,128]{1,0:T(8,128)(2,1)S(1)}, u32[]{:S(2)}, u32[]{:S(2)}) collective-permute-start(s16[1024,128]{1,0:T(8,128)(2,1)S(1)} %get-tuple-element.27), channel_id=1, source_target_pairs={{0,2},{1,3},{2,0},{3,1},{4,6},{5,7},{6,4},{7,5},{8,10},{9,11},{10,... | collective-permute-start | bytes 786440 | tf_op jit(solution)/shard_map/ppermute | solution.py:35
  68.9 13.3 %collective-permute-start.15 = (s16[1024,128]{1,0:T(8,128)(2,1)S(1)}, s16[1024,128]{1,0:T(8,128)(2,1)S(1)}, u32[]{:S(2)}, u32[]{:S(2)}) collective-permute-start(s16[1024,128]{1,0:T(8,128)(2,1)S(1)} %get-tuple-element.28), channel_id=1, source_target_pairs={{0,3},{1,0},{2,1},{3,2},{4,7},{5,4},{6,5},{7,6},{8,11},{9,8},{10,9... | collective-permute-start | bytes 786440 | tf_op jit(solution)/shard_map/ppermute | solution.py:35
  74.3 8.0 %copy-start.18 = (s16[1024,128]{1,0:T(8,128)(2,1)}, s16[1024,128]{1,0:T(8,128)(2,1)S(1)}, u32[]{:S(2)}) copy-start(s16[1024,128]{1,0:T(8,128)(2,1)S(1)} %get-tuple-element.34) | copy-start | bytes 786436
  74.3 8.0 %copy-start.19 = (s16[1024,128]{1,0:T(8,128)(2,1)}, s16[1024,128]{1,0:T(8,128)(2,1)S(1)}, u32[]{:S(2)}) copy-start(s16[1024,128]{1,0:T(8,128)(2,1)S(1)} %get-tuple-element.33) | copy-start | bytes 786436
  74.3 12.4 %copy-start.1 = (f32[4096,128]{1,0:T(8,128)S(1)}, f32[4096,128]{1,0:T(8,128)}, u32[]{:S(2)}) copy-start(f32[4096,128]{1,0:T(8,128)} %copy-done) | copy-start | bytes 6291460
  78.4 3.9 %copy-start.9 = (s16[1024,128]{1,0:T(8,128)(2,1)}, s16[1024,128]{1,0:T(8,128)(2,1)S(1)}, u32[]{:S(2)}) copy-start(s16[1024,128]{1,0:T(8,128)(2,1)S(1)} %collective-permute-done.14.refs_3_.refs_7_) | copy-start | bytes 786436
  82.9 3.8 %collective-permute-start.16 = (s16[4096,128]{1,0:T(8,128)(2,1)S(1)}, s16[4096,128]{1,0:T(8,128)(2,1)}, u32[]{:S(2)}, u32[]{:S(2)}) collective-permute-start(s16[4096,128]{1,0:T(8,128)(2,1)S(1)} %join.13.refs_3_), channel_id=1, source_target_pairs={{0,4},{4,0},{8,12},{12,8},{16,20},{20,16},{24,28},{28,24},{32,36},... | collective-permute-start | bytes 3145736 | tf_op jit(solution)/shard_map/ppermute | solution.py:31
  83.0 18.4 %collective-permute-start.17 = (s16[1024,128]{1,0:T(8,128)(2,1)}, s16[1024,128]{1,0:T(8,128)(2,1)S(1)}, u32[]{:S(2)}, u32[]{:S(2)}) collective-permute-start(s16[1024,128]{1,0:T(8,128)(2,1)} %copy-done.20), channel_id=1, source_target_pairs={{0,1},{1,2},{2,3},{3,0},{4,5},{5,6},{6,7},{7,4},{8,9},{9,10},{10,1... | collective-permute-start | bytes 786440 | tf_op jit(solution)/shard_map/ppermute | solution.py:35
  83.6 17.8 %collective-permute-start.18 = (s16[1024,128]{1,0:T(8,128)(2,1)}, s16[1024,128]{1,0:T(8,128)(2,1)S(1)}, u32[]{:S(2)}, u32[]{:S(2)}) collective-permute-start(s16[1024,128]{1,0:T(8,128)(2,1)} %copy-done.19), channel_id=1, source_target_pairs={{0,2},{1,3},{2,0},{3,1},{4,6},{5,7},{6,4},{7,5},{8,10},{9,11},{10,... | collective-permute-start | bytes 786440 | tf_op jit(solution)/shard_map/ppermute | solution.py:35
  84.5 16.9 %collective-permute-start.19 = (s16[1024,128]{1,0:T(8,128)(2,1)}, s16[1024,128]{1,0:T(8,128)(2,1)S(1)}, u32[]{:S(2)}, u32[]{:S(2)}) collective-permute-start(s16[1024,128]{1,0:T(8,128)(2,1)} %copy-done.18), channel_id=1, source_target_pairs={{0,3},{1,0},{2,1},{3,2},{4,7},{5,4},{6,5},{7,6},{8,11},{9,8},{10,9... | collective-permute-start | bytes 786440 | tf_op jit(solution)/shard_map/ppermute | solution.py:35
  86.7 1.0 copy-start.8
  87.6 0.9 copy-start.10
  88.6 0.9 copy-start.12
  90.5 10.9 %copy-start.3 = (f32[4096,128]{1,0:T(8,128)S(1)}, f32[4096,128]{1,0:T(8,128)}, u32[]{:S(2)}) copy-start(f32[4096,128]{1,0:T(8,128)} %copy-done.2) | copy-start | bytes 6291460
  112.4 4.2 %collective-permute-start.22 = (f32[4096,128]{1,0:T(8,128)S(1)}, f32[4096,128]{1,0:T(8,128)S(1)}, u32[]{:S(2)}, u32[]{:S(2)}) collective-permute-start(f32[4096,128]{1,0:T(8,128)S(1)} %get-tuple-element.39), channel_id=1, source_target_pairs={{0,4},{4,0},{8,12},{12,8},{16,20},{20,16},{24,28},{28,24},{32,36},... | collective-permute-start | bytes 6291464 | tf_op jit(solution)/shard_map/ppermute | solution.py:31
  117.1 10.8 %collective-permute-start.25 = (f16[2,4,128,128]{3,2,1,0:T(8,128)(2,1)S(1)}, f16[2,4,128,128]{3,2,1,0:T(8,128)(2,1)S(1)}, u32[]{:S(2)}, u32[]{:S(2)}) collective-permute-start(f16[2,4,128,128]{3,2,1,0:T(8,128)(2,1)S(1)} %bitcast.66), channel_id=1, source_target_pairs={{0,16},{4,20},{8,24},{12,28},{16,0},{20,4},{24,8},{28,12},{32,48},... | collective-permute-start | bytes 786440 | tf_op jit(solution)/shard_map/ppermute | solution.py:31
  117.9 12.5 %collective-permute-start.23 = (f16[2,4,128,128]{3,2,1,0:T(8,128)(2,1)S(1)}, f16[2,4,128,128]{3,2,1,0:T(8,128)(2,1)S(1)}, u32[]{:S(2)}, u32[]{:S(2)}) collective-permute-start(f16[2,4,128,128]{3,2,1,0:T(8,128)(2,1)S(1)} %bitcast.65), channel_id=1, source_target_pairs={{0,8},{4,12},{8,0},{12,4},{16,24},{20,28},{24,16},{28,20},{32,40},... | collective-permute-start | bytes 786440 | tf_op jit(solution)/shard_map/ppermute | solution.py:31
  118.5 14.2 %collective-permute-start.24 = (f16[2,4,128,128]{3,2,1,0:T(8,128)(2,1)S(1)}, f16[2,4,128,128]{3,2,1,0:T(8,128)(2,1)S(1)}, u32[]{:S(2)}, u32[]{:S(2)}) collective-permute-start(f16[2,4,128,128]{3,2,1,0:T(8,128)(2,1)S(1)} %bitcast.64), channel_id=1, source_target_pairs={{0,24},{4,28},{8,16},{12,20},{16,8},{20,12},{24,0},{28,4},{32,56},... | collective-permute-start | bytes 786440 | tf_op jit(solution)/shard_map/ppermute | solution.py:31
  123.1 12.5 %collective-permute-start.20 = (f32[128,128]{1,0:T(8,128)S(1)}, f32[128,128]{1,0:T(8,128)S(1)}, u32[]{:S(2)}, u32[]{:S(2)}) collective-permute-start(f32[128,128]{1,0:T(8,128)S(1)} %get-tuple-element.55), channel_id=1, source_target_pairs={{0,4},{4,8},{8,12},{12,16},{16,20},{20,24},{24,28},{28,32},{32,36}... | collective-permute-start | bytes 196616 | tf_op jit(solution)/shard_map/ppermute | solution.py:265
  124.4 11.1 %collective-permute-start.21 = (f32[128,128]{1,0:T(8,128)S(1)}, f32[128,128]{1,0:T(8,128)S(1)}, u32[]{:S(2)}, u32[]{:S(2)}) collective-permute-start(f32[128,128]{1,0:T(8,128)S(1)} %get-tuple-element.56), channel_id=1, source_target_pairs={{4,0},{8,4},{12,8},{16,12},{20,16},{24,20},{28,24},{32,28},{36,32}... | collective-permute-start | bytes 196616 | tf_op jit(solution)/shard_map/ppermute | solution.py:265
  132.9 6.4 %collective-permute-start.26 = (f16[4,128,128]{2,1,0:T(8,128)(2,1)S(1)}, f16[4,128,128]{2,1,0:T(8,128)(2,1)S(1)}, u32[]{:S(2)}, u32[]{:S(2)}) collective-permute-start(f16[4,128,128]{2,1,0:T(8,128)(2,1)S(1)} %get-tuple-element.53), channel_id=1, source_target_pairs={{0,32},{4,36},{8,40},{12,44},{16,48},{20,52},{24,56},{28,60},{32,0... | collective-permute-start | bytes 393224 | tf_op jit(solution)/shard_map/ppermute | solution.py:31
  135.6 19.6 %copy-start.13 = (f32[128,128]{1,0:T(8,128)}, f32[128,128]{1,0:T(8,128)S(1)}, u32[]{:S(2)}) copy-start(f32[128,128]{1,0:T(8,128)S(1)} %fusion.7.refs_1_) | copy-start | bytes 196612
  139.3 5.5 %collective-permute-start.27 = (f16[2,128,128]{2,1,0:T(8,128)(2,1)S(1)}, f16[2,128,128]{2,1,0:T(8,128)(2,1)S(1)}, u32[]{:S(2)}, u32[]{:S(2)}) collective-permute-start(f16[2,128,128]{2,1,0:T(8,128)(2,1)S(1)} %fusion.4), channel_id=1, source_target_pairs={{0,64},{4,68},{8,72},{12,76},{16,80},{20,84},{24,88},{28,92},{32,9... | collective-permute-start | bytes 196616 | tf_op jit(solution)/shard_map/ppermute | solution.py:31
  144.9 9.6 %collective-permute-start.28 = (f16[128,128]{1,0:T(8,128)(2,1)S(1)}, f16[128,128]{1,0:T(8,128)(2,1)S(1)}, u32[]{:S(2)}, u32[]{:S(2)}) collective-permute-start(f16[128,128]{1,0:T(8,128)(2,1)S(1)} %fusion.23), channel_id=1, source_target_pairs={{0,128},{4,132},{8,136},{12,140},{16,144},{20,148},{24,152},{28,15... | collective-permute-start | bytes 98312 | tf_op jit(solution)/shard_map/ppermute | solution.py:31
  (4 other events, 3.1 us)

commit v12 on v10

--- a/solution.py
+++ b/solution.py
@@ -308,8 +308,8 @@
     terms = join([terms, swap(terms, 4, 0, 0)], got[0][1:] + [shot_near])
     terms = join([terms, swap(terms, 1, 0, 0)])
     shots = gather_shots(shot_near, shot_at, [size * NY for size in PIECES])
-    terms = join([terms, swap(terms, 0, 1, 0)], [coded[0][0], shots[0], rec_at] + got[1][1:])
-    terms = join([terms, swap(terms, 0, 2, 0)], [coded[1][0]] + codes[1:NY])
+    terms = join([terms, swap(terms, 0, 1, 0)], [coded[0][0], got[1][1], got[1][3]])
+    terms = join([terms, swap(terms, 0, 2, 0)], [shots[0], rec_at, got[1][2], coded[1][0], codes[1]])
     far_terms = swap(terms, 0, 0, 1)
 
     sums, residuals, done = (), [], 0

time: 153 us -> 159 us (1.039)
  starting transfers between devices: 59.7 us -> 69.7 us
  local copies, waits for them, and re-layouts: 11 us -> 7.49 us
    ppermute x12, starting transfers between devices: 20.8 us -> 29 us  [send_y(): return lax.ppermute(value, 'fq', [(i, (i + k) % NY) for i in range(NY)])]
    unnamed x51 -> x37, local copies, waits for them, and re-layouts: 6.5 us -> 3.02 us
    ppermute x13, starting transfers between devices: 32 us -> 33.8 us  [swap(): lax.ppermute(value, 'tr', [(tr_of(z, x, c), tr_of(z ^ dz, x ^ dx, c ^ dc)...]
  transfers between devices with their start and end apart: 29 -> 29, of which waited for: 13 -> 13; matrix products, arithmetic and copies ran while one was open for 0% -> 0% of each run, Pallas kernels for 22% -> 21%
where the time goes in v12:
time: 159 us
  starting transfers between devices  69.7 us (44%)
  Pallas kernels  43.7 us (27%)
  waiting for transfers between devices  34.5 us (22%)
  local copies, waits for them, and re-layouts  7.49 us (5%)
  between operations  1.99 us (1%)
    ppermute x13, starting transfers between devices, swap(): lax.ppermute(value, 'tr', [(tr_of(z, x, c), tr_of(z ^ dz, x ^ dx, c ^ dc)...  33.8 us
    ppermute x12, starting transfers between devices, send_y(): return lax.ppermute(value, 'fq', [(i, (i + k) % NY) for i in range(NY)])  29 us
    ppermute x13, waiting for transfers between devices, swap(): lax.ppermute(value, 'tr', [(tr_of(z, x, c), tr_of(z ^ dz, x ^ dx, c ^ dc)...  22.7 us
    pallas_call x2, Pallas kernels, sum_receivers(): pl.pallas_call(body, in_specs=[sm, sm] + [vm] * (3 + parts + held), out_s...  20.6 us
    ppermute x12, waiting for transfers between devices, send_y(): return lax.ppermute(value, 'fq', [(i, (i + k) % NY) for i in range(NY)])  11.8 us
    pallas_call x1, Pallas kernels, gather_shots(): pl.pallas_call(body, in_specs=[sm, vm], out_specs=[vm] * len(sizes), out_...  8.11 us
    pallas_call x2, Pallas kernels, spectra(): pl.pallas_call(body, grid=(rows // tile,), in_specs=[pl.BlockSpec((tile,...  7.62 us
    ppermute x4, starting transfers between devices, neighbour(): lax.ppermute(value, 'tr', [(i, i + by) for i in range(size) if 0 <= i + b...  6.91 us
  transfers between devices with their start and end apart: 29, of which 13 were waited for; matrix products, arithmetic and copies ran while one was open for 0% of the time, Pallas kernels for 21%

profile of v12, /device:TPU:8, one launch (start us, length us, event | category | flops | bytes accessed | tf_op | source)
XLA Modules:
  0.0 158.7 jit_solution(13496073443940111082)
XLA Ops:
  0.7 4.0 %constant_dynamic-slice_fusion = (bf16[1024,256]{1,0:T(8,128)(2,1)}, bf16[1024,256]{1,0:T(8,128)(2,1)}, bf16[1024,256]{1,0:T(8,128)(2,1)}, bf16[1024,256]{1,0:T(...) fusion(bf16[8192,256]{1,0:T(8,128)(2,1)} %param.6, ...), kind=kLoop, calls=%fused_computation.74 | loop fusion | bytes 8388640 | tf_op jit(solution)/shard_map/dynamic_slice | solution.py:278
  4.7 2.3 %collective-permute-start.6 = (bf16[1024,256]{1,0:T(8,128)(2,1)}, bf16[1024,256]{1,0:T(8,128)(2,1)S(1)}, u32[]{:S(2)}, u32[]{:S(2)}) collective-permute-start(bf16[1024,256]{1,0:T(8,128)(2,1)} %get-tuple-element.45), channel_id=1, source_target_pairs={{0,3},{1,0},{2,1},{3,2},{4,7},{5,4},{6,5},{7,6},{8,11},{9,8},{10,9... | collective-permute-start | bytes 1572872 | tf_op jit(solution)/shard_map/ppermute | solution.py:35
  7.0 0.9 collective-permute-start.5
  7.8 1.9 %collective-permute-start.4 = (bf16[1024,256]{1,0:T(8,128)(2,1)}, bf16[1024,256]{1,0:T(8,128)(2,1)}, u32[]{:S(2)}, u32[]{:S(2)}) collective-permute-start(bf16[1024,256]{1,0:T(8,128)(2,1)} %get-tuple-element.47), channel_id=1, source_target_pairs={{0,1},{1,2},{2,3},{3,0},{4,5},{5,6},{6,7},{7,4},{8,9},{9,10},{10,1... | collective-permute-start | bytes 1572872 | tf_op jit(solution)/shard_map/ppermute | solution.py:35
  9.7 5.3 %make_table.1.refs_1_.refs_0_.t = bf16[1024,1024]{1,0:T(8,128)(2,1)S(1)} custom-call(s32[1]{0:T(128)} %bitcast.10.y_ref, bf16[1024,256]{1,0:T(8,128)(2,1)S(1)} %get-tuple-element.48.refs_0_.b0), custom_call_target="tpu_custom_call" | custom-call | flops 1073741824 | bytes 33554432 | tf_op jit(solution)/shard_map/make_table/pallas_call | solution.py:62
  15.1 3.4 %collective-permute-start.2 = (s16[128,128]{1,0:T(8,128)(2,1)S(1)}, s16[128,128]{1,0:T(8,128)(2,1)S(1)}, u32[]{:S(2)}, u32[]{:S(2)}) collective-permute-start(s16[128,128]{1,0:T(8,128)(2,1)S(1)} %encode_terms.1.refs_0_), channel_id=1, source_target_pairs={{0,64},{4,68},{8,72},{12,76},{16,80},{20,84},{24,88},{28,92},{32,9... | collective-permute-start | bytes 98312 | tf_op jit(solution)/shard_map/ppermute | solution.py:31
  18.5 1.3 collective-permute-start.1
  20.9 3.0 %collective-permute-start = (f32[128,128]{1,0:T(8,128)S(1)}, f32[128,128]{1,0:T(8,128)S(1)}, u32[]{:S(2)}, u32[]{:S(2)}) collective-permute-start(f32[128,128]{1,0:T(8,128)S(1)} %join.8), channel_id=1, source_target_pairs={{0,4},{4,8},{8,12},{12,16},{16,20},{20,24},{24,28},{28,32},{32,36}... | collective-permute-start | bytes 196616 | tf_op jit(solution)/shard_map/ppermute | solution.py:265
  24.0 5.5 %collective-permute-start.3 = (s16[256,128]{1,0:T(8,128)(2,1)S(1)}, s16[256,128]{1,0:T(8,128)(2,1)S(1)}, u32[]{:S(2)}, u32[]{:S(2)}) collective-permute-start(s16[256,128]{1,0:T(8,128)(2,1)S(1)} %join.9.refs_0_), channel_id=1, source_target_pairs={{0,128},{4,132},{8,136},{12,140},{16,144},{20,148},{24,152},{28,15... | collective-permute-start | bytes 196616 | tf_op jit(solution)/shard_map/ppermute | solution.py:31
  29.5 1.4 collective-permute-done.5.refs_3_.b2.refs_4_
  30.9 0.9 collective-permute-done.4.refs_2_.b1.refs_3_
  31.8 1.4 collective-permute-start.9
  33.3 1.4 collective-permute-start.10
  34.7 2.0 %collective-permute-start.7 = (s16[512,128]{1,0:T(8,128)(2,1)S(1)}, s16[512,128]{1,0:T(8,128)(2,1)S(1)}, u32[]{:S(2)}, u32[]{:S(2)}) collective-permute-start(s16[512,128]{1,0:T(8,128)(2,1)S(1)} %join.10.refs_0_), channel_id=1, source_target_pairs={{0,32},{4,36},{8,40},{12,44},{16,48},{20,52},{24,56},{28,60},{32,0... | collective-permute-start | bytes 393224 | tf_op jit(solution)/shard_map/ppermute | solution.py:31
  36.7 3.5 %collective-permute-done.7.refs_1_ = s16[512,128]{1,0:T(8,128)(2,1)S(1)} collective-permute-done((s16[512,128]{1,0:T(8,128)(2,1)S(1)}, s16[512,128]{1,0:T(8,128)(2,1)S(1)}, u32[]{:S(2)}, u32[]{:S(2)}) %collective-permute-start.7) | collective-permute-done | bytes 131104 | tf_op jit(solution)/shard_map/ppermute | solution.py:31
  40.3 1.5 collective-permute-start.8
  41.8 2.2 %collective-permute-start.12 = (bf16[1024,256]{1,0:T(8,128)(2,1)}, bf16[1024,256]{1,0:T(8,128)(2,1)S(1)}, u32[]{:S(2)}, u32[]{:S(2)}) collective-permute-start(bf16[1024,256]{1,0:T(8,128)(2,1)} %get-tuple-element.25), channel_id=1, source_target_pairs={{0,2},{1,3},{2,0},{3,1},{4,6},{5,7},{6,4},{7,5},{8,10},{9,11},{10,... | collective-permute-start | bytes 1572872 | tf_op jit(solution)/shard_map/ppermute | solution.py:35
  44.0 4.6 %spectra.2 = (s16[1024,128]{1,0:T(8,128)(2,1)S(1)}, s16[1024,128]{1,0:T(8,128)(2,1)S(1)}, s16[1024,128]{1,0:T(8,128)(2,1)}, s16[1024,128]{1,0:T(8,128)(2,1)S(1)}) custom-call(bf16[1024,256]{1,0:T(8,128)(2,1)S(1)} %copy-done.6, bf16[1024,256]{1,0:T(8,128)(2,1)} %collective-permute-done.4.refs_2_.b1.refs_3_, ...), custom_call_target="tpu_custom_call" | custom-call | flops 1000 | bytes 1000 | tf_op jit(solution)/shard_map/spectra/pallas_call | solution.py:142
  48.6 2.8 %collective-permute-start.11 = (s16[2048,128]{1,0:T(8,128)(2,1)S(1)}, s16[2048,128]{1,0:T(8,128)(2,1)S(1)}, u32[]{:S(2)}, u32[]{:S(2)}) collective-permute-start(s16[2048,128]{1,0:T(8,128)(2,1)S(1)} %join.12.refs_0_), channel_id=1, source_target_pairs={{0,16},{4,20},{8,24},{12,28},{16,0},{20,4},{24,8},{28,12},{32,48},... | collective-permute-start | bytes 1572872 | tf_op jit(solution)/shard_map/ppermute | solution.py:31
  51.5 2.3 %collective-permute-start.13 = (s16[1024,128]{1,0:T(8,128)(2,1)S(1)}, s16[1024,128]{1,0:T(8,128)(2,1)S(1)}, u32[]{:S(2)}, u32[]{:S(2)}) collective-permute-start(s16[1024,128]{1,0:T(8,128)(2,1)S(1)} %get-tuple-element.27), channel_id=1, source_target_pairs={{0,1},{1,2},{2,3},{3,0},{4,5},{5,6},{6,7},{7,4},{8,9},{9,10},{10,1... | collective-permute-start | bytes 786440 | tf_op jit(solution)/shard_map/ppermute | solution.py:35
  53.8 8.1 %gather_shots.1 = (f32[4096,128]{1,0:T(8,128)S(1)}, f32[4096,128]{1,0:T(8,128)S(1)}) custom-call(s32[8192]{0:T(1024)S(1)} %bitcast_dynamic-update-slice_fusion.shot_at, f32[384,128]{1,0:T(8,128)S(1)} %pad_maximum_fusion.shot.refs_5_), custom_call_target="tpu_custom_call" | custom-call | flops 1000 | bytes 1000 | tf_op jit(solution)/shard_map/gather_shots/pallas_call | solution.py:171
  62.0 1.3 copy-done.2
  63.3 3.0 %spectra.3 = (s16[1024,128]{1,0:T(8,128)(2,1)S(1)}, s16[1024,128]{1,0:T(8,128)(2,1)S(1)}, s16[1024,128]{1,0:T(8,128)(2,1)S(1)}, s16[1024,128]{1,0:T(8,128)(2,1)S(1)}) custom-call(bf16[1024,256]{1,0:T(8,128)(2,1)S(1)} %copy-done.4, bf16[1024,256]{1,0:T(8,128)(2,1)S(1)} %collective-permute-done.9.refs_3_.b1, ...), custom_call_target="tpu_custom_call" | custom-call | flops 1000 | bytes 1000 | tf_op jit(solution)/shard_map/spectra/pallas_call | solution.py:142
  66.4 3.4 %collective-permute-done.13.refs_6_ = s16[1024,128]{1,0:T(8,128)(2,1)S(1)} collective-permute-done((s16[1024,128]{1,0:T(8,128)(2,1)S(1)}, s16[1024,128]{1,0:T(8,128)(2,1)S(1)}, u32[]{:S(2)}, u32[]{:S(2)}) %collective-permute-start.13) | collective-permute-done | bytes 262176 | tf_op jit(solution)/shard_map/ppermute | solution.py:35
  70.1 9.8 %collective-permute-start.15 = (s16[1024,128]{1,0:T(8,128)(2,1)}, s16[1024,128]{1,0:T(8,128)(2,1)S(1)}, u32[]{:S(2)}, u32[]{:S(2)}) collective-permute-start(s16[1024,128]{1,0:T(8,128)(2,1)} %get-tuple-element.28), channel_id=1, source_target_pairs={{0,2},{1,3},{2,0},{3,1},{4,6},{5,7},{6,4},{7,5},{8,10},{9,11},{10,... | collective-permute-start | bytes 786440 | tf_op jit(solution)/shard_map/ppermute | solution.py:35
  80.0 2.4 %collective-permute-start.16 = (s16[1024,128]{1,0:T(8,128)(2,1)}, s16[1024,128]{1,0:T(8,128)(2,1)S(1)}, u32[]{:S(2)}, u32[]{:S(2)}) collective-permute-start(s16[1024,128]{1,0:T(8,128)(2,1)} %copy-done.10), channel_id=1, source_target_pairs={{0,3},{1,0},{2,1},{3,2},{4,7},{5,4},{6,5},{7,6},{8,11},{9,8},{10,9... | collective-permute-start | bytes 786440 | tf_op jit(solution)/shard_map/ppermute | solution.py:35
  82.3 2.2 %collective-permute-start.18 = (s16[1024,128]{1,0:T(8,128)(2,1)}, s16[1024,128]{1,0:T(8,128)(2,1)S(1)}, u32[]{:S(2)}, u32[]{:S(2)}) collective-permute-start(s16[1024,128]{1,0:T(8,128)(2,1)} %copy-done.12), channel_id=1, source_target_pairs={{0,2},{1,3},{2,0},{3,1},{4,6},{5,7},{6,4},{7,5},{8,10},{9,11},{10,... | collective-permute-start | bytes 786440 | tf_op jit(solution)/shard_map/ppermute | solution.py:35
  84.5 2.8 %collective-permute-done.15.refs_7_ = s16[1024,128]{1,0:T(8,128)(2,1)S(1)} collective-permute-done((s16[1024,128]{1,0:T(8,128)(2,1)}, s16[1024,128]{1,0:T(8,128)(2,1)S(1)}, u32[]{:S(2)}, u32[]{:S(2)}) %collective-permute-start.15) | collective-permute-done | bytes 262176 | tf_op jit(solution)/shard_map/ppermute | solution.py:35
  87.3 2.3 %collective-permute-start.19 = (s16[1024,128]{1,0:T(8,128)(2,1)}, s16[1024,128]{1,0:T(8,128)(2,1)S(1)}, u32[]{:S(2)}, u32[]{:S(2)}) collective-permute-start(s16[1024,128]{1,0:T(8,128)(2,1)} %copy-done.11), channel_id=1, source_target_pairs={{0,3},{1,0},{2,1},{3,2},{4,7},{5,4},{6,5},{7,6},{8,11},{9,8},{10,9... | collective-permute-start | bytes 786440 | tf_op jit(solution)/shard_map/ppermute | solution.py:35
  89.7 3.2 %collective-permute-done.16.refs_8_ = s16[1024,128]{1,0:T(8,128)(2,1)S(1)} collective-permute-done((s16[1024,128]{1,0:T(8,128)(2,1)}, s16[1024,128]{1,0:T(8,128)(2,1)S(1)}, u32[]{:S(2)}, u32[]{:S(2)}) %collective-permute-start.16) | collective-permute-done | bytes 262176 | tf_op jit(solution)/shard_map/ppermute | solution.py:35
  92.9 1.6 %copy-done.1 = f32[4096,128]{1,0:T(8,128)S(1)} copy-done((f32[4096,128]{1,0:T(8,128)S(1)}, f32[4096,128]{1,0:T(8,128)}, u32[]{:S(2)}) %copy-start.1) | copy-done | bytes 2097176
  94.5 10.3 %sum_receivers.2 = (f32[4096,128]{1,0:T(8,128)S(1)}, f32[4096,128]{1,0:T(8,128)S(1)}, f32[4096,128]{1,0:T(8,128)S(1)}) custom-call(s32[4096]{0:T(1024)S(1)} %bitcast.61, s32[4]{0:T(128)S(1)} %get-tuple-element.70.refs_1_, f32[4096,128]{1,0:T(8,128)S(1)} %copy-done.1, s16[4096,128]{1,0:T(8,128)(2,1)S(1)} %join.13.refs_3_, ...), custom_call_target="tpu_custom_call" | custom-call | flops 1000 | bytes 1000 | tf_op jit(solution)/shard_map/sum_receivers/pallas_call | solution.py:222
  104.9 10.3 %sum_receivers.3 = (f32[4096,128]{1,0:T(8,128)S(1)}, f32[4096,128]{1,0:T(8,128)S(1)}, f32[4096,128]{1,0:T(8,128)S(1)}) custom-call(s32[4096]{0:T(1024)S(1)} %bitcast.59, s32[4]{0:T(128)S(1)} %get-tuple-element.69.refs_1_, f32[4096,128]{1,0:T(8,128)S(1)} %copy-done.3, s16[4096,128]{1,0:T(8,128)(2,1)S(1)} %join.13.refs_3_, ...), custom_call_target="tpu_custom_call" | custom-call | flops 1000 | bytes 1000 | tf_op jit(solution)/shard_map/sum_receivers/pallas_call | solution.py:222
  115.5 3.9 %collective-permute-done.22 = f32[4096,128]{1,0:T(8,128)S(1)} collective-permute-done((f32[4096,128]{1,0:T(8,128)S(1)}, f32[4096,128]{1,0:T(8,128)S(1)}, u32[]{:S(2)}, u32[]{:S(2)}) %collective-permute-start.22) | collective-permute-done | bytes 2097184 | tf_op jit(solution)/shard_map/ppermute | solution.py:31
  119.9 1.5 collective-permute-start.25
  121.8 2.3 %collective-permute-start.24 = (f16[2,4,128,128]{3,2,1,0:T(8,128)(2,1)S(1)}, f16[2,4,128,128]{3,2,1,0:T(8,128)(2,1)S(1)}, u32[]{:S(2)}, u32[]{:S(2)}) collective-permute-start(f16[2,4,128,128]{3,2,1,0:T(8,128)(2,1)S(1)} %bitcast.64), channel_id=1, source_target_pairs={{0,24},{4,28},{8,16},{12,20},{16,8},{20,12},{24,0},{28,4},{32,56},... | collective-permute-start | bytes 786440 | tf_op jit(solution)/shard_map/ppermute | solution.py:31
  124.1 1.8 %sum_shots.1.refs_1_ = f32[384,128]{1,0:T(8,128)S(1)} custom-call(s32[1,8192]{1,0:T(1,128)S(1)} %bitcast.57, f32[4096,128]{1,0:T(8,128)S(1)} %get-tuple-element.30.refs_0_, f32[4096,128]{1,0:T(8,128)S(1)} %get-tuple-element.37.refs_1_), custom_call_target="tpu_custom_call" | custom-call | flops 1000 | bytes 1000 | tf_op jit(solution)/shard_map/sum_shots/pallas_call | solution.py:252
  125.9 1.3 collective-permute-start.20
  127.3 1.3 collective-permute-start.21
  128.6 2.1 %collective-permute-done.25 = f16[2,4,128,128]{3,2,1,0:T(8,128)(2,1)S(1)} collective-permute-done((f16[2,4,128,128]{3,2,1,0:T(8,128)(2,1)S(1)}, f16[2,4,128,128]{3,2,1,0:T(8,128)(2,1)S(1)}, u32[]{:S(2)}, u32[]{:S(2)}) %collective-permute-start.25) | collective-permute-done | bytes 262176 | tf_op jit(solution)/shard_map/ppermute | solution.py:31
  130.7 3.3 %collective-permute-done.23 = f16[2,4,128,128]{3,2,1,0:T(8,128)(2,1)S(1)} collective-permute-done((f16[2,4,128,128]{3,2,1,0:T(8,128)(2,1)S(1)}, f16[2,4,128,128]{3,2,1,0:T(8,128)(2,1)S(1)}, u32[]{:S(2)}, u32[]{:S(2)}) %collective-permute-start.23) | collective-permute-done | bytes 262176 | tf_op jit(solution)/shard_map/ppermute | solution.py:31
  134.0 1.5 collective-permute-done.24
  135.7 2.8 %collective-permute-start.26 = (f16[4,128,128]{2,1,0:T(8,128)(2,1)S(1)}, f16[4,128,128]{2,1,0:T(8,128)(2,1)S(1)}, u32[]{:S(2)}, u32[]{:S(2)}) collective-permute-start(f16[4,128,128]{2,1,0:T(8,128)(2,1)S(1)} %get-tuple-element.53), channel_id=1, source_target_pairs={{0,32},{4,36},{8,40},{12,44},{16,48},{20,52},{24,56},{28,60},{32,0... | collective-permute-start | bytes 393224 | tf_op jit(solution)/shard_map/ppermute | solution.py:31
  138.5 3.6 %collective-permute-done.26 = f16[4,128,128]{2,1,0:T(8,128)(2,1)S(1)} collective-permute-done((f16[4,128,128]{2,1,0:T(8,128)(2,1)S(1)}, f16[4,128,128]{2,1,0:T(8,128)(2,1)S(1)}, u32[]{:S(2)}, u32[]{:S(2)}) %collective-permute-start.26) | collective-permute-done | bytes 131104 | tf_op jit(solution)/shard_map/ppermute | solution.py:31
  142.2 3.4 %collective-permute-start.27 = (f16[2,128,128]{2,1,0:T(8,128)(2,1)S(1)}, f16[2,128,128]{2,1,0:T(8,128)(2,1)S(1)}, u32[]{:S(2)}, u32[]{:S(2)}) collective-permute-start(f16[2,128,128]{2,1,0:T(8,128)(2,1)S(1)} %fusion.4), channel_id=1, source_target_pairs={{0,64},{4,68},{8,72},{12,76},{16,80},{20,84},{24,88},{28,92},{32,9... | collective-permute-start | bytes 196616 | tf_op jit(solution)/shard_map/ppermute | solution.py:31
  145.6 2.4 %collective-permute-done.27 = f16[2,128,128]{2,1,0:T(8,128)(2,1)S(1)} collective-permute-done((f16[2,128,128]{2,1,0:T(8,128)(2,1)S(1)}, f16[2,128,128]{2,1,0:T(8,128)(2,1)S(1)}, u32[]{:S(2)}, u32[]{:S(2)}) %collective-permute-start.27) | collective-permute-done | bytes 65568 | tf_op jit(solution)/shard_map/ppermute | solution.py:31
  148.0 7.8 %collective-permute-start.28 = (f16[128,128]{1,0:T(8,128)(2,1)S(1)}, f16[128,128]{1,0:T(8,128)(2,1)S(1)}, u32[]{:S(2)}, u32[]{:S(2)}) collective-permute-start(f16[128,128]{1,0:T(8,128)(2,1)S(1)} %fusion.23), channel_id=1, source_target_pairs={{0,128},{4,132},{8,136},{12,140},{16,144},{20,148},{24,152},{28,15... | collective-permute-start | bytes 98312 | tf_op jit(solution)/shard_map/ppermute | solution.py:31
  155.8 2.2 %collective-permute-done.28 = f16[128,128]{1,0:T(8,128)(2,1)S(1)} collective-permute-done((f16[128,128]{1,0:T(8,128)(2,1)S(1)}, f16[128,128]{1,0:T(8,128)(2,1)S(1)}, u32[]{:S(2)}, u32[]{:S(2)}) %collective-permute-start.28) | collective-permute-done | bytes 32800 | tf_op jit(solution)/shard_map/ppermute | solution.py:31
  (90 shorter events, 3.2 us)
Async XLA Ops:
  4.7 10.4 %copy-start.5 = (bf16[1024,256]{1,0:T(8,128)(2,1)}, bf16[1024,256]{1,0:T(8,128)(2,1)S(1)}, u32[]{:S(2)}) copy-start(bf16[1024,256]{1,0:T(8,128)(2,1)S(1)} %get-tuple-element.48.refs_0_.b0) | copy-start | bytes 1572868
  4.7 10.3 %copy-start.8 = (f32[128,128]{1,0:T(8,128)S(1)}, f32[128,128]{1,0:T(8,128)}, u32[]{:S(2)}) copy-start(f32[128,128]{1,0:T(8,128)} %a.1) | copy-start | bytes 196612
  4.7 24.8 %collective-permute-start.6 = (bf16[1024,256]{1,0:T(8,128)(2,1)}, bf16[1024,256]{1,0:T(8,128)(2,1)S(1)}, u32[]{:S(2)}, u32[]{:S(2)}) collective-permute-start(bf16[1024,256]{1,0:T(8,128)(2,1)} %get-tuple-element.45), channel_id=1, source_target_pairs={{0,3},{1,0},{2,1},{3,2},{4,7},{5,4},{6,5},{7,6},{8,11},{9,8},{10,9... | collective-permute-start | bytes 1572872 | tf_op jit(solution)/shard_map/ppermute | solution.py:35
  7.0 23.9 %collective-permute-start.5 = (bf16[1024,256]{1,0:T(8,128)(2,1)}, bf16[1024,256]{1,0:T(8,128)(2,1)S(1)}, u32[]{:S(2)}, u32[]{:S(2)}) collective-permute-start(bf16[1024,256]{1,0:T(8,128)(2,1)} %get-tuple-element.46), channel_id=1, source_target_pairs={{0,2},{1,3},{2,0},{3,1},{4,6},{5,7},{6,4},{7,5},{8,10},{9,11},{10,... | collective-permute-start | bytes 1572872 | tf_op jit(solution)/shard_map/ppermute | solution.py:35
  7.8 24.0 %collective-permute-start.4 = (bf16[1024,256]{1,0:T(8,128)(2,1)}, bf16[1024,256]{1,0:T(8,128)(2,1)}, u32[]{:S(2)}, u32[]{:S(2)}) collective-permute-start(bf16[1024,256]{1,0:T(8,128)(2,1)} %get-tuple-element.47), channel_id=1, source_target_pairs={{0,1},{1,2},{2,3},{3,0},{4,5},{5,6},{6,7},{7,4},{8,9},{9,10},{10,1... | collective-permute-start | bytes 1572872 | tf_op jit(solution)/shard_map/ppermute | solution.py:35
  9.7 8.7 %copy-start.9 = (f32[128,128]{1,0:T(8,128)S(1)}, f32[128,128]{1,0:T(8,128)}, u32[]{:S(2)}) copy-start(f32[128,128]{1,0:T(8,128)} %refs_0_.1) | copy-start | bytes 196612
  15.0 5.5 %copy-start.14 = (s32[8192]{0:T(1024)S(1)}, s32[8192]{0:T(1024)}, u32[]{:S(2)}) copy-start(s32[8192]{0:T(1024)} %param.8) | copy-start | bytes 98308
  15.1 5.7 %copy-start.15 = (s32[8192]{0:T(1024)S(1)}, s32[8192]{0:T(1024)}, u32[]{:S(2)}) copy-start(s32[8192]{0:T(1024)} %param.7) | copy-start | bytes 98308
  15.1 5.7 %collective-permute-start.2 = (s16[128,128]{1,0:T(8,128)(2,1)S(1)}, s16[128,128]{1,0:T(8,128)(2,1)S(1)}, u32[]{:S(2)}, u32[]{:S(2)}) collective-permute-start(s16[128,128]{1,0:T(8,128)(2,1)S(1)} %encode_terms.1.refs_0_), channel_id=1, source_target_pairs={{0,64},{4,68},{8,72},{12,76},{16,80},{20,84},{24,88},{28,92},{32,9... | collective-permute-start | bytes 98312 | tf_op jit(solution)/shard_map/ppermute | solution.py:31
  18.5 5.5 %collective-permute-start.1 = (f32[128,128]{1,0:T(8,128)S(1)}, f32[128,128]{1,0:T(8,128)S(1)}, u32[]{:S(2)}, u32[]{:S(2)}) collective-permute-start(f32[128,128]{1,0:T(8,128)S(1)} %join.8), channel_id=1, source_target_pairs={{4,0},{8,4},{12,8},{16,12},{20,16},{24,20},{28,24},{32,28},{36,32}... | collective-permute-start | bytes 196616 | tf_op jit(solution)/shard_map/ppermute | solution.py:265
  20.9 8.6 %collective-permute-start = (f32[128,128]{1,0:T(8,128)S(1)}, f32[128,128]{1,0:T(8,128)S(1)}, u32[]{:S(2)}, u32[]{:S(2)}) collective-permute-start(f32[128,128]{1,0:T(8,128)S(1)} %join.8), channel_id=1, source_target_pairs={{0,4},{4,8},{8,12},{12,16},{16,20},{20,24},{24,28},{28,32},{32,36}... | collective-permute-start | bytes 196616 | tf_op jit(solution)/shard_map/ppermute | solution.py:265
  24.0 10.7 %collective-permute-start.3 = (s16[256,128]{1,0:T(8,128)(2,1)S(1)}, s16[256,128]{1,0:T(8,128)(2,1)S(1)}, u32[]{:S(2)}, u32[]{:S(2)}) collective-permute-start(s16[256,128]{1,0:T(8,128)(2,1)S(1)} %join.9.refs_0_), channel_id=1, source_target_pairs={{0,128},{4,132},{8,136},{12,140},{16,144},{20,148},{24,152},{28,15... | collective-permute-start | bytes 196616 | tf_op jit(solution)/shard_map/ppermute | solution.py:31
  31.8 12.1 %copy-start.6 = (bf16[1024,256]{1,0:T(8,128)(2,1)S(1)}, bf16[1024,256]{1,0:T(8,128)(2,1)}, u32[]{:S(2)}) copy-start(bf16[1024,256]{1,0:T(8,128)(2,1)} %copy-done.5) | copy-start | bytes 1572868
  31.8 16.7 %collective-permute-start.9 = (bf16[1024,256]{1,0:T(8,128)(2,1)}, bf16[1024,256]{1,0:T(8,128)(2,1)S(1)}, u32[]{:S(2)}, u32[]{:S(2)}) collective-permute-start(bf16[1024,256]{1,0:T(8,128)(2,1)} %get-tuple-element.23), channel_id=1, source_target_pairs={{0,1},{1,2},{2,3},{3,0},{4,5},{5,6},{6,7},{7,4},{8,9},{9,10},{10,1... | collective-permute-start | bytes 1572872 | tf_op jit(solution)/shard_map/ppermute | solution.py:35
  33.3 15.3 %collective-permute-start.10 = (bf16[1024,256]{1,0:T(8,128)(2,1)}, bf16[1024,256]{1,0:T(8,128)(2,1)S(1)}, u32[]{:S(2)}, u32[]{:S(2)}) collective-permute-start(bf16[1024,256]{1,0:T(8,128)(2,1)} %get-tuple-element.24), channel_id=1, source_target_pairs={{0,3},{1,0},{2,1},{3,2},{4,7},{5,4},{6,5},{7,6},{8,11},{9,8},{10,9... | collective-permute-start | bytes 1572872 | tf_op jit(solution)/shard_map/ppermute | solution.py:35
  34.7 5.5 %collective-permute-start.7 = (s16[512,128]{1,0:T(8,128)(2,1)S(1)}, s16[512,128]{1,0:T(8,128)(2,1)S(1)}, u32[]{:S(2)}, u32[]{:S(2)}) collective-permute-start(s16[512,128]{1,0:T(8,128)(2,1)S(1)} %join.10.refs_0_), channel_id=1, source_target_pairs={{0,32},{4,36},{8,40},{12,44},{16,48},{20,52},{24,56},{28,60},{32,0... | collective-permute-start | bytes 393224 | tf_op jit(solution)/shard_map/ppermute | solution.py:31
  40.3 8.3 %collective-permute-start.8 = (s16[1024,128]{1,0:T(8,128)(2,1)S(1)}, s16[1024,128]{1,0:T(8,128)(2,1)S(1)}, u32[]{:S(2)}, u32[]{:S(2)}) collective-permute-start(s16[1024,128]{1,0:T(8,128)(2,1)S(1)} %join.11.refs_0_), channel_id=1, source_target_pairs={{0,8},{4,12},{8,0},{12,4},{16,24},{20,28},{24,16},{28,20},{32,40},... | collective-permute-start | bytes 786440 | tf_op jit(solution)/shard_map/ppermute | solution.py:31
  41.8 21.5 %collective-permute-start.12 = (bf16[1024,256]{1,0:T(8,128)(2,1)}, bf16[1024,256]{1,0:T(8,128)(2,1)S(1)}, u32[]{:S(2)}, u32[]{:S(2)}) collective-permute-start(bf16[1024,256]{1,0:T(8,128)(2,1)} %get-tuple-element.25), channel_id=1, source_target_pairs={{0,2},{1,3},{2,0},{3,1},{4,6},{5,7},{6,4},{7,5},{8,10},{9,11},{10,... | collective-permute-start | bytes 1572872 | tf_op jit(solution)/shard_map/ppermute | solution.py:35
  48.6 5.3 %copy-start.10 = (s16[1024,128]{1,0:T(8,128)(2,1)}, s16[1024,128]{1,0:T(8,128)(2,1)S(1)}, u32[]{:S(2)}) copy-start(s16[1024,128]{1,0:T(8,128)(2,1)S(1)} %get-tuple-element.29) | copy-start | bytes 786436
  48.6 14.7 %copy-start.4 = (bf16[1024,256]{1,0:T(8,128)(2,1)S(1)}, bf16[1024,256]{1,0:T(8,128)(2,1)}, u32[]{:S(2)}) copy-start(bf16[1024,256]{1,0:T(8,128)(2,1)} %get-tuple-element.42.b0) | copy-start | bytes 1572868
  48.6 21.1 %collective-permute-start.11 = (s16[2048,128]{1,0:T(8,128)(2,1)S(1)}, s16[2048,128]{1,0:T(8,128)(2,1)S(1)}, u32[]{:S(2)}, u32[]{:S(2)}) collective-permute-start(s16[2048,128]{1,0:T(8,128)(2,1)S(1)} %join.12.refs_0_), channel_id=1, source_target_pairs={{0,16},{4,20},{8,24},{12,28},{16,0},{20,4},{24,8},{28,12},{32,48},... | collective-permute-start | bytes 1572872 | tf_op jit(solution)/shard_map/ppermute | solution.py:31
  51.5 18.3 %collective-permute-start.13 = (s16[1024,128]{1,0:T(8,128)(2,1)S(1)}, s16[1024,128]{1,0:T(8,128)(2,1)S(1)}, u32[]{:S(2)}, u32[]{:S(2)}) collective-permute-start(s16[1024,128]{1,0:T(8,128)(2,1)S(1)} %get-tuple-element.27), channel_id=1, source_target_pairs={{0,1},{1,2},{2,3},{3,0},{4,5},{5,6},{6,7},{7,4},{8,9},{9,10},{10,1... | collective-permute-start | bytes 786440 | tf_op jit(solution)/shard_map/ppermute | solution.py:35
  61.9 1.4 copy-start.2
  63.3 6.4 %copy-start = (f32[4096,128]{1,0:T(8,128)}, f32[4096,128]{1,0:T(8,128)S(1)}, u32[]{:S(2)}) copy-start(f32[4096,128]{1,0:T(8,128)S(1)} %get-tuple-element.21.refs_2_) | copy-start | bytes 6291460
  66.3 3.5 %copy-start.11 = (s16[1024,128]{1,0:T(8,128)(2,1)}, s16[1024,128]{1,0:T(8,128)(2,1)S(1)}, u32[]{:S(2)}) copy-start(s16[1024,128]{1,0:T(8,128)(2,1)S(1)} %get-tuple-element.34) | copy-start | bytes 786436
  66.3 3.5 %copy-start.12 = (s16[1024,128]{1,0:T(8,128)(2,1)}, s16[1024,128]{1,0:T(8,128)(2,1)S(1)}, u32[]{:S(2)}) copy-start(s16[1024,128]{1,0:T(8,128)(2,1)S(1)} %get-tuple-element.33) | copy-start | bytes 786436
  66.4 3.5 %copy-start.13 = (s16[1024,128]{1,0:T(8,128)(2,1)}, s16[1024,128]{1,0:T(8,128)(2,1)S(1)}, u32[]{:S(2)}) copy-start(s16[1024,128]{1,0:T(8,128)(2,1)S(1)} %get-tuple-element.32) | copy-start | bytes 786436
  69.8 23.1 %collective-permute-start.14 = (s16[4096,128]{1,0:T(8,128)(2,1)S(1)}, s16[4096,128]{1,0:T(8,128)(2,1)S(1)}, u32[]{:S(2)}, u32[]{:S(2)}) collective-permute-start(s16[4096,128]{1,0:T(8,128)(2,1)S(1)} %join.13.refs_3_), channel_id=1, source_target_pairs={{0,4},{4,0},{8,12},{12,8},{16,20},{20,16},{24,28},{28,24},{32,36},... | collective-permute-start | bytes 3145736 | tf_op jit(solution)/shard_map/ppermute | solution.py:31
  70.1 17.2 %collective-permute-start.15 = (s16[1024,128]{1,0:T(8,128)(2,1)}, s16[1024,128]{1,0:T(8,128)(2,1)S(1)}, u32[]{:S(2)}, u32[]{:S(2)}) collective-permute-start(s16[1024,128]{1,0:T(8,128)(2,1)} %get-tuple-element.28), channel_id=1, source_target_pairs={{0,2},{1,3},{2,0},{3,1},{4,6},{5,7},{6,4},{7,5},{8,10},{9,11},{10,... | collective-permute-start | bytes 786440 | tf_op jit(solution)/shard_map/ppermute | solution.py:35
  80.0 13.0 %collective-permute-start.16 = (s16[1024,128]{1,0:T(8,128)(2,1)}, s16[1024,128]{1,0:T(8,128)(2,1)S(1)}, u32[]{:S(2)}, u32[]{:S(2)}) collective-permute-start(s16[1024,128]{1,0:T(8,128)(2,1)} %copy-done.10), channel_id=1, source_target_pairs={{0,3},{1,0},{2,1},{3,2},{4,7},{5,4},{6,5},{7,6},{8,11},{9,8},{10,9... | collective-permute-start | bytes 786440 | tf_op jit(solution)/shard_map/ppermute | solution.py:35
  82.3 22.5 %collective-permute-start.17 = (s16[1024,128]{1,0:T(8,128)(2,1)}, s16[1024,128]{1,0:T(8,128)(2,1)S(1)}, u32[]{:S(2)}, u32[]{:S(2)}) collective-permute-start(s16[1024,128]{1,0:T(8,128)(2,1)} %copy-done.13), channel_id=1, source_target_pairs={{0,1},{1,2},{2,3},{3,0},{4,5},{5,6},{6,7},{7,4},{8,9},{9,10},{10,1... | collective-permute-start | bytes 786440 | tf_op jit(solution)/shard_map/ppermute | solution.py:35
  82.3 22.6 %collective-permute-start.18 = (s16[1024,128]{1,0:T(8,128)(2,1)}, s16[1024,128]{1,0:T(8,128)(2,1)S(1)}, u32[]{:S(2)}, u32[]{:S(2)}) collective-permute-start(s16[1024,128]{1,0:T(8,128)(2,1)} %copy-done.12), channel_id=1, source_target_pairs={{0,2},{1,3},{2,0},{3,1},{4,6},{5,7},{6,4},{7,5},{8,10},{9,11},{10,... | collective-permute-start | bytes 786440 | tf_op jit(solution)/shard_map/ppermute | solution.py:35
  87.3 17.6 %collective-permute-start.19 = (s16[1024,128]{1,0:T(8,128)(2,1)}, s16[1024,128]{1,0:T(8,128)(2,1)S(1)}, u32[]{:S(2)}, u32[]{:S(2)}) collective-permute-start(s16[1024,128]{1,0:T(8,128)(2,1)} %copy-done.11), channel_id=1, source_target_pairs={{0,3},{1,0},{2,1},{3,2},{4,7},{5,4},{6,5},{7,6},{8,11},{9,8},{10,9... | collective-permute-start | bytes 786440 | tf_op jit(solution)/shard_map/ppermute | solution.py:35
  92.9 1.6 %copy-start.1 = (f32[4096,128]{1,0:T(8,128)S(1)}, f32[4096,128]{1,0:T(8,128)}, u32[]{:S(2)}) copy-start(f32[4096,128]{1,0:T(8,128)} %copy-done) | copy-start | bytes 6291460
  94.5 10.4 %copy-start.3 = (f32[4096,128]{1,0:T(8,128)S(1)}, f32[4096,128]{1,0:T(8,128)}, u32[]{:S(2)}) copy-start(f32[4096,128]{1,0:T(8,128)} %copy-done.2) | copy-start | bytes 6291460
  115.2 4.2 %collective-permute-start.22 = (f32[4096,128]{1,0:T(8,128)S(1)}, f32[4096,128]{1,0:T(8,128)S(1)}, u32[]{:S(2)}, u32[]{:S(2)}) collective-permute-start(f32[4096,128]{1,0:T(8,128)S(1)} %get-tuple-element.39), channel_id=1, source_target_pairs={{0,4},{4,0},{8,12},{12,8},{16,20},{20,16},{24,28},{28,24},{32,36},... | collective-permute-start | bytes 6291464 | tf_op jit(solution)/shard_map/ppermute | solution.py:31
  119.9 10.8 %collective-permute-start.25 = (f16[2,4,128,128]{3,2,1,0:T(8,128)(2,1)S(1)}, f16[2,4,128,128]{3,2,1,0:T(8,128)(2,1)S(1)}, u32[]{:S(2)}, u32[]{:S(2)}) collective-permute-start(f16[2,4,128,128]{3,2,1,0:T(8,128)(2,1)S(1)} %bitcast.66), channel_id=1, source_target_pairs={{0,16},{4,20},{8,24},{12,28},{16,0},{20,4},{24,8},{28,12},{32,48},... | collective-permute-start | bytes 786440 | tf_op jit(solution)/shard_map/ppermute | solution.py:31
  121.4 12.6 %collective-permute-start.23 = (f16[2,4,128,128]{3,2,1,0:T(8,128)(2,1)S(1)}, f16[2,4,128,128]{3,2,1,0:T(8,128)(2,1)S(1)}, u32[]{:S(2)}, u32[]{:S(2)}) collective-permute-start(f16[2,4,128,128]{3,2,1,0:T(8,128)(2,1)S(1)} %bitcast.65), channel_id=1, source_target_pairs={{0,8},{4,12},{8,0},{12,4},{16,24},{20,28},{24,16},{28,20},{32,40},... | collective-permute-start | bytes 786440 | tf_op jit(solution)/shard_map/ppermute | solution.py:31
  121.8 13.7 %collective-permute-start.24 = (f16[2,4,128,128]{3,2,1,0:T(8,128)(2,1)S(1)}, f16[2,4,128,128]{3,2,1,0:T(8,128)(2,1)S(1)}, u32[]{:S(2)}, u32[]{:S(2)}) collective-permute-start(f16[2,4,128,128]{3,2,1,0:T(8,128)(2,1)S(1)} %bitcast.64), channel_id=1, source_target_pairs={{0,24},{4,28},{8,16},{12,20},{16,8},{20,12},{24,0},{28,4},{32,56},... | collective-permute-start | bytes 786440 | tf_op jit(solution)/shard_map/ppermute | solution.py:31
  125.9 12.6 %collective-permute-start.20 = (f32[128,128]{1,0:T(8,128)S(1)}, f32[128,128]{1,0:T(8,128)S(1)}, u32[]{:S(2)}, u32[]{:S(2)}) collective-permute-start(f32[128,128]{1,0:T(8,128)S(1)} %get-tuple-element.55), channel_id=1, source_target_pairs={{0,4},{4,8},{8,12},{12,16},{16,20},{20,24},{24,28},{28,32},{32,36}... | collective-permute-start | bytes 196616 | tf_op jit(solution)/shard_map/ppermute | solution.py:265
  127.3 11.2 %collective-permute-start.21 = (f32[128,128]{1,0:T(8,128)S(1)}, f32[128,128]{1,0:T(8,128)S(1)}, u32[]{:S(2)}, u32[]{:S(2)}) collective-permute-start(f32[128,128]{1,0:T(8,128)S(1)} %get-tuple-element.56), channel_id=1, source_target_pairs={{4,0},{8,4},{12,8},{16,12},{20,16},{24,20},{28,24},{32,28},{36,32}... | collective-permute-start | bytes 196616 | tf_op jit(solution)/shard_map/ppermute | solution.py:265
  135.7 6.4 %collective-permute-start.26 = (f16[4,128,128]{2,1,0:T(8,128)(2,1)S(1)}, f16[4,128,128]{2,1,0:T(8,128)(2,1)S(1)}, u32[]{:S(2)}, u32[]{:S(2)}) collective-permute-start(f16[4,128,128]{2,1,0:T(8,128)(2,1)S(1)} %get-tuple-element.53), channel_id=1, source_target_pairs={{0,32},{4,36},{8,40},{12,44},{16,48},{20,52},{24,56},{28,60},{32,0... | collective-permute-start | bytes 393224 | tf_op jit(solution)/shard_map/ppermute | solution.py:31
  138.5 20.2 %copy-start.7 = (f32[128,128]{1,0:T(8,128)}, f32[128,128]{1,0:T(8,128)S(1)}, u32[]{:S(2)}) copy-start(f32[128,128]{1,0:T(8,128)S(1)} %fusion.7.refs_1_) | copy-start | bytes 196612
  142.2 5.8 %collective-permute-start.27 = (f16[2,128,128]{2,1,0:T(8,128)(2,1)S(1)}, f16[2,128,128]{2,1,0:T(8,128)(2,1)S(1)}, u32[]{:S(2)}, u32[]{:S(2)}) collective-permute-start(f16[2,128,128]{2,1,0:T(8,128)(2,1)S(1)} %fusion.4), channel_id=1, source_target_pairs={{0,64},{4,68},{8,72},{12,76},{16,80},{20,84},{24,88},{28,92},{32,9... | collective-permute-start | bytes 196616 | tf_op jit(solution)/shard_map/ppermute | solution.py:31
  148.0 10.0 %collective-permute-start.28 = (f16[128,128]{1,0:T(8,128)(2,1)S(1)}, f16[128,128]{1,0:T(8,128)(2,1)S(1)}, u32[]{:S(2)}, u32[]{:S(2)}) collective-permute-start(f16[128,128]{1,0:T(8,128)(2,1)S(1)} %fusion.23), channel_id=1, source_target_pairs={{0,128},{4,132},{8,136},{12,140},{16,144},{20,148},{24,152},{28,15... | collective-permute-start | bytes 98312 | tf_op jit(solution)/shard_map/ppermute | solution.py:31

commit v13 on v8

--- a/solution.py
+++ b/solution.py
@@ -15,7 +15,7 @@
 SUM_SCALE = 1.0 / 32.0
 PIECES = (1024, 1024)
 LARGE = pltpu.CompilerParams(vmem_limit_bytes=60 * 2**20)
-SUMS = pltpu.CompilerParams(vmem_limit_bytes=32 * 2**20)
+SUMS = pltpu.CompilerParams(vmem_limit_bytes=20 * 2**20)
 SMALL = pltpu.CompilerParams(vmem_limit_bytes=12 * 2**20)
 COST = pl.CostEstimate(flops=1000, bytes_accessed=1000, transcendentals=0)
 MEDIUM = pltpu.CompilerParams(vmem_limit_bytes=18 * 2**20)
@@ -194,26 +194,25 @@
     )(shot_at, shot_near)
 
 
-def sum_receivers(codes, shots, coded, live, rec_at, before):
+def sum_receivers(codes, shots, coded, live, rec_at, held, last):
     rows, width = shots.shape
     size, half = codes[0].shape[0], coded[0].shape[0]
     banks, unroll = 4, 32
-    parts, held = len(codes), len(before)
+    parts, first = len(codes), not held
+    given = list(coded) if first else list(held)
 
     def body(*refs):
-        rec_at, live, shots, own, other = refs[:5]
-        codes, before = refs[5 : 5 + parts], refs[5 + parts : 5 + parts + held]
-        near, far, res, rec = refs[5 + parts + held : 9 + parts + held]
-        sums = refs[9 + parts + held :]
+        rec_at, live, shots = refs[:3]
+        codes, given = refs[3 : 3 + parts], refs[3 + parts :]
+        res, outs = given[2 if first else banks + 1], given[3 if first else banks + 2 :]
+        rec, sums = outs[0], outs[1 : 1 + banks]
         halves = (pl.ds(0, half), pl.ds(half, half))
-        for code, at in zip((own, other), halves):
-            rec[at, :] = (code[...].astype(jnp.float32) + 32768.0) * (1.0 / REC_SCALE) + REC_LOW
-        rec[pl.ds(2 * half, 8), :] = jnp.zeros((8, width), jnp.float32)
-        for k, s in enumerate(sums):
-            if k or not held:
+        if first:
+            for code, at in zip(given[:2], halves):
+                rec[at, :] = (code[...].astype(jnp.float32) + 32768.0) * (1.0 / REC_SCALE) + REC_LOW
+            rec[pl.ds(2 * half, 8), :] = jnp.zeros((8, width), jnp.float32)
+            for s in sums:
                 s[...] = jnp.zeros_like(s)
-        for s, at in zip(before, halves):
-            sums[0][at, :] = s[...]
         for k, code in enumerate(codes):
             at = pl.ds(k * size, size)
             logamp = (code[...].astype(jnp.float32) + 32768.0) * (1.0 / LA_SCALE)
@@ -229,21 +228,22 @@
             return 0
 
         lax.fori_loop(0, rows // unroll, step, 0)
-        for out, at in zip((near, far), halves):
-            out[...] = (sums[0][at, :] + sums[1][at, :]) + (sums[2][at, :] + sums[3][at, :])
+        if last:
+            for out, at in zip(outs[1 + banks :], halves):
+                out[...] = (sums[0][at, :] + sums[1][at, :]) + (sums[2][at, :] + sums[3][at, :])
 
     vm, sm = pl.BlockSpec(memory_space=pltpu.VMEM), pl.BlockSpec(memory_space=pltpu.SMEM)
-    sums = pltpu.VMEM((2 * half + 8, width), jnp.float32)
-    return pl.pallas_call(
-        body,
-        in_specs=[sm, sm] + [vm] * (3 + parts + held),
-        out_specs=[vm] * 3,
-        out_shape=[jax.ShapeDtypeStruct((n, width), jnp.float32) for n in (half, half, rows)],
-        scratch_shapes=[sums] * (1 + banks),
+    shapes = [(rows, width)] + [(2 * half + 8, width)] * (1 + banks) + [(half, width)] * (2 if last else 0)
+    return pl.pallas_call(
+        body,
+        in_specs=[sm, sm] + [vm] * (1 + parts + len(given)),
+        out_specs=[vm] * len(shapes),
+        out_shape=[jax.ShapeDtypeStruct(shape, jnp.float32) for shape in shapes],
+        input_output_aliases={} if first else {3 + parts + k: 1 + k for k in range(1 + banks)},
         compiler_params=SUMS,
         cost_estimate=COST,
         name="sum_receivers",
-    )(rec_at, live, shots, *coded, *codes, *before)
+    )(rec_at, live, shots, *codes, *given)
 
 
 def sum_shots(residuals, shot_at, count):
@@ -329,14 +329,14 @@
     terms = join([terms, swap(terms, 0, 2, 0)], [shots[0], rec_at] + got[1][1:])
     far_terms = swap(terms, 0, 0, 1)
 
-    sums, residuals, done = (), [], 0
+    held, residuals, done = [], [], 0
     for h, part_shots in enumerate(shots):
-        some = slice(h * NY, (h + 1) * NY)
+        some, last = slice(h * NY, (h + 1) * NY), h == len(shots) - 1
         at = rec_at[done : done + part_shots.shape[0]]
         done += part_shots.shape[0]
-        *sums, resid = sum_receivers(codes[some], part_shots, [terms, far_terms], live[some], at, sums)
+        resid, *held = sum_receivers(codes[some], part_shots, [terms, far_terms], live[some], at, held, last)
         residuals.append(resid)
-    sums, far_sums = sums
+    sums, far_sums = held[-2:]
     sums = (sums + swap(far_sums, 0, 0, 1)).reshape(NX, 2, NZ // 2, block, width)
     shots = sum_shots(residuals, shot_at, 3 * block)
     sent = (sums * SUM_SCALE).astype(jnp.float16)

time: 150 us -> 147 us (0.980)
  Pallas kernels: 44.4 us -> 41.6 us
    pallas_call x2, Pallas kernels: 21.1 us -> 18.3 us  [sum_receivers(): pl.pallas_call(body, in_specs=[sm, sm] + [vm] * (1 + parts + len(given)),...]
  transfers between devices with their start and end apart: 29 -> 29, of which waited for: 9 -> 10; matrix products, arithmetic and copies ran while one was open for 0% -> 1% of each run, Pallas kernels for 23% -> 22%
where the time goes in v13:
time: 147 us
  starting transfers between devices  59.8 us (41%)
  Pallas kernels  41.6 us (28%)
  waiting for transfers between devices  30.8 us (21%)
  local copies, waits for them, and re-layouts  11.1 us (8%)
  between operations  1.99 us (1%)
    ppermute x13, starting transfers between devices, swap(): lax.ppermute(value, 'tr', [(tr_of(z, x, c), tr_of(z ^ dz, x ^ dx, c ^ dc)...  33.6 us
    ppermute x13, waiting for transfers between devices, swap(): lax.ppermute(value, 'tr', [(tr_of(z, x, c), tr_of(z ^ dz, x ^ dx, c ^ dc)...  23.2 us
    ppermute x12, starting transfers between devices, send_y(): return lax.ppermute(value, 'fq', [(i, (i + k) % NY) for i in range(NY)])  19 us
    pallas_call x2, Pallas kernels, sum_receivers(): pl.pallas_call(body, in_specs=[sm, sm] + [vm] * (1 + parts + len(given)),...  18.3 us
    pallas_call x1, Pallas kernels, gather_shots(): pl.pallas_call(body, in_specs=[sm, vm], out_specs=[vm] * len(sizes), out_...  8.11 us
    unnamed x47, local copies, waits for them, and re-layouts  7.93 us
    pallas_call x2, Pallas kernels, spectra(): pl.pallas_call(body, grid=(rows // tile,), in_specs=[pl.BlockSpec((tile,...  7.63 us
    ppermute x12, waiting for transfers between devices, send_y(): return lax.ppermute(value, 'fq', [(i, (i + k) % NY) for i in range(NY)])  7.52 us
  transfers between devices with their start and end apart: 29, of which 10 were waited for; matrix products, arithmetic and copies ran while one was open for 1% of the time, Pallas kernels for 22%

profile of v13, /device:TPU:8, one launch (start us, length us, event | category | flops | bytes accessed | tf_op | source)
XLA Modules:
  0.0 146.7 jit_solution(54727252830000283)
XLA Ops:
  0.7 2.7 %constant_dynamic-slice_fusion = (bf16[1024,256]{1,0:T(8,128)(2,1)}, bf16[1024,256]{1,0:T(8,128)(2,1)}, bf16[1024,256]{1,0:T(8,128)(2,1)}, bf16[1024,256]{1,0:T(8,128)(2,1)S(1)}) fusion(bf16[8192,256]{1,0:T(8,128)(2,1)} %traces.1, s32[]{:T(128)S(6)} %select_n.159, s32[]{:T(128)S(6)} %select_n.157, s32[]{:T(128)S(6)} %select_n.155, s32[]{:T(128)S(6)} %select_n.153), kind=kLoop, calls=%fused_computation.74 | loop fusion | bytes 4194320 | tf_op jit(solution)/shard_map/dynamic_slice | solution.py:296
  3.4 2.2 %collective-permute-start.4 = (bf16[1024,256]{1,0:T(8,128)(2,1)}, bf16[1024,256]{1,0:T(8,128)(2,1)S(1)}, u32[]{:S(2)}, u32[]{:S(2)}) collective-permute-start(bf16[1024,256]{1,0:T(8,128)(2,1)} %get-tuple-element.50), channel_id=1, source_target_pairs={{0,3},{1,0},{2,1},{3,2},{4,7},{5,4},{6,5},{7,6},{8,11},{9,8},{10,9... | collective-permute-start | bytes 1572872 | tf_op jit(solution)/shard_map/ppermute | solution.py:37
  5.6 0.9 collective-permute-start.3
  6.5 1.9 %collective-permute-start.2 = (bf16[1024,256]{1,0:T(8,128)(2,1)}, bf16[1024,256]{1,0:T(8,128)(2,1)}, u32[]{:S(2)}, u32[]{:S(2)}) collective-permute-start(bf16[1024,256]{1,0:T(8,128)(2,1)} %get-tuple-element.52), channel_id=1, source_target_pairs={{0,1},{1,2},{2,3},{3,0},{4,5},{5,6},{6,7},{7,4},{8,9},{9,10},{10,1... | collective-permute-start | bytes 1572872 | tf_op jit(solution)/shard_map/ppermute | solution.py:37
  8.4 5.3 %make_table.1.refs_1_.t.refs_0_ = bf16[1024,1024]{1,0:T(8,128)(2,1)S(1)} custom-call(s32[1]{0:T(128)} %bitcast.10.y_ref, bf16[1024,256]{1,0:T(8,128)(2,1)S(1)} %get-tuple-element.53.refs_0_.b0), custom_call_target="tpu_custom_call" | custom-call | flops 1073741824 | bytes 33554432 | tf_op jit(solution)/shard_map/make_table/pallas_call | solution.py:64
  13.7 3.4 %collective-permute-start.8 = (s16[128,128]{1,0:T(8,128)(2,1)S(1)}, s16[128,128]{1,0:T(8,128)(2,1)S(1)}, u32[]{:S(2)}, u32[]{:S(2)}) collective-permute-start(s16[128,128]{1,0:T(8,128)(2,1)S(1)} %encode_terms.1.refs_0_), channel_id=1, source_target_pairs={{0,64},{4,68},{8,72},{12,76},{16,80},{20,84},{24,88},{28,92},{32,9... | collective-permute-start | bytes 98312 | tf_op jit(solution)/shard_map/ppermute | solution.py:33
  17.1 1.3 collective-permute-start.1
  19.5 3.0 %collective-permute-start = (f32[128,128]{1,0:T(8,128)S(1)}, f32[128,128]{1,0:T(8,128)S(1)}, u32[]{:S(2)}, u32[]{:S(2)}) collective-permute-start(f32[128,128]{1,0:T(8,128)S(1)} %join.8), channel_id=1, source_target_pairs={{0,4},{4,8},{8,12},{12,16},{16,20},{20,24},{24,28},{28,32},{32,36}... | collective-permute-start | bytes 196616 | tf_op jit(solution)/shard_map/ppermute | solution.py:280
  22.6 5.5 %collective-permute-start.9 = (s16[256,128]{1,0:T(8,128)(2,1)S(1)}, s16[256,128]{1,0:T(8,128)(2,1)S(1)}, u32[]{:S(2)}, u32[]{:S(2)}) collective-permute-start(s16[256,128]{1,0:T(8,128)(2,1)S(1)} %join.9.refs_0_), channel_id=1, source_target_pairs={{0,128},{4,132},{8,136},{12,140},{16,144},{20,148},{24,152},{28,15... | collective-permute-start | bytes 196616 | tf_op jit(solution)/shard_map/ppermute | solution.py:33
  28.1 3.4 %collective-permute-done.9.refs_1_ = s16[256,128]{1,0:T(8,128)(2,1)S(1)} collective-permute-done((s16[256,128]{1,0:T(8,128)(2,1)S(1)}, s16[256,128]{1,0:T(8,128)(2,1)S(1)}, u32[]{:S(2)}, u32[]{:S(2)}) %collective-permute-start.9) | collective-permute-done | bytes 65568 | tf_op jit(solution)/shard_map/ppermute | solution.py:33
  31.5 3.7 %collective-permute-start.10 = (s16[512,128]{1,0:T(8,128)(2,1)S(1)}, s16[512,128]{1,0:T(8,128)(2,1)S(1)}, u32[]{:S(2)}, u32[]{:S(2)}) collective-permute-start(s16[512,128]{1,0:T(8,128)(2,1)S(1)} %join.10.refs_0_), channel_id=1, source_target_pairs={{0,32},{4,36},{8,40},{12,44},{16,48},{20,52},{24,56},{28,60},{32,0... | collective-permute-start | bytes 393224 | tf_op jit(solution)/shard_map/ppermute | solution.py:33
  35.2 2.2 %copy-done = bf16[8192,256]{1,0:T(8,128)(2,1)S(1)} copy-done((bf16[8192,256]{1,0:T(8,128)(2,1)S(1)}, bf16[8192,256]{1,0:T(8,128)(2,1)}, u32[]{:S(2)}) %copy-start) | copy-done | bytes 4194328
  37.5 1.3 collective-permute-done.10.refs_1_
  38.9 0.8 copy-done.5
  39.7 1.2 collective-permute-start.11
  41.1 2.4 %collective-permute-start.14 = (bf16[1024,256]{1,0:T(8,128)(2,1)S(1)}, bf16[1024,256]{1,0:T(8,128)(2,1)S(1)}, u32[]{:S(2)}, u32[]{:S(2)}) collective-permute-start(bf16[1024,256]{1,0:T(8,128)(2,1)S(1)} %get-tuple-element.32), channel_id=1, source_target_pairs={{0,2},{1,3},{2,0},{3,1},{4,6},{5,7},{6,4},{7,5},{8,10},{9,11},{10,... | collective-permute-start | bytes 1572872 | tf_op jit(solution)/shard_map/ppermute | solution.py:37
  43.6 1.4 collective-permute-start.15
  45.0 4.6 %spectra.2 = (s16[1024,128]{1,0:T(8,128)(2,1)S(1)}, s16[1024,128]{1,0:T(8,128)(2,1)}, s16[1024,128]{1,0:T(8,128)(2,1)}, s16[1024,128]{1,0:T(8,128)(2,1)S(1)}) custom-call(bf16[1024,256]{1,0:T(8,128)(2,1)S(1)} %copy-done.8, bf16[1024,256]{1,0:T(8,128)(2,1)} %collective-permute-done.2.b1.refs_2_.refs_0_, ...), custom_call_target="tpu_custom_call" | custom-call | flops 1000 | bytes 1000 | tf_op jit(solution)/shard_map/spectra/pallas_call | solution.py:157
  49.6 2.0 %collective-permute-start.12 = (s16[2048,128]{1,0:T(8,128)(2,1)S(1)}, s16[2048,128]{1,0:T(8,128)(2,1)S(1)}, u32[]{:S(2)}, u32[]{:S(2)}) collective-permute-start(s16[2048,128]{1,0:T(8,128)(2,1)S(1)} %join.12.refs_0_), channel_id=1, source_target_pairs={{0,16},{4,20},{8,24},{12,28},{16,0},{20,4},{24,8},{28,12},{32,48},... | collective-permute-start | bytes 1572872 | tf_op jit(solution)/shard_map/ppermute | solution.py:33
  51.7 8.1 %gather_shots.1 = (f32[4096,128]{1,0:T(8,128)S(1)}, f32[4096,128]{1,0:T(8,128)S(1)}) custom-call(s32[8192]{0:T(1024)S(1)} %bitcast_dynamic-update-slice_fusion.shot_at, f32[384,128]{1,0:T(8,128)S(1)} %pad_maximum_fusion.shot.refs_5_), custom_call_target="tpu_custom_call" | custom-call | flops 1000 | bytes 1000 | tf_op jit(solution)/shard_map/gather_shots/pallas_call | solution.py:186
  59.8 7.3 %collective-permute-done.15.refs_6_.b3 = bf16[1024,256]{1,0:T(8,128)(2,1)S(1)} collective-permute-done((bf16[1024,256]{1,0:T(8,128)(2,1)S(1)}, bf16[1024,256]{1,0:T(8,128)(2,1)S(1)}, u32[]{:S(2)}, u32[]{:S(2)}) %collective-permute-start.15) | collective-permute-done | bytes 524320 | tf_op jit(solution)/shard_map/ppermute | solution.py:37
  67.2 0.7 copy-done.13
  68.5 1.9 %collective-permute-start.6 = (s16[1024,128]{1,0:T(8,128)(2,1)}, s16[1024,128]{1,0:T(8,128)(2,1)}, u32[]{:S(2)}, u32[]{:S(2)}) collective-permute-start(s16[1024,128]{1,0:T(8,128)(2,1)} %get-tuple-element.28), channel_id=1, source_target_pairs={{0,2},{1,3},{2,0},{3,1},{4,6},{5,7},{6,4},{7,5},{8,10},{9,11},{10,... | collective-permute-start | bytes 786440 | tf_op jit(solution)/shard_map/ppermute | solution.py:37
  70.5 2.3 %collective-permute-start.7 = (s16[1024,128]{1,0:T(8,128)(2,1)}, s16[1024,128]{1,0:T(8,128)(2,1)S(1)}, u32[]{:S(2)}, u32[]{:S(2)}) collective-permute-start(s16[1024,128]{1,0:T(8,128)(2,1)} %copy-done.18), channel_id=1, source_target_pairs={{0,3},{1,0},{2,1},{3,2},{4,7},{5,4},{6,5},{7,6},{8,11},{9,8},{10,9... | collective-permute-start | bytes 786440 | tf_op jit(solution)/shard_map/ppermute | solution.py:37
  72.7 1.0 copy-done.6
  73.8 1.0 copy-done.10
  74.8 1.0 copy-done.12
  75.9 1.0 copy-done.14
  76.9 3.0 %spectra.3 = (s16[1024,128]{1,0:T(8,128)(2,1)S(1)}, s16[1024,128]{1,0:T(8,128)(2,1)S(1)}, s16[1024,128]{1,0:T(8,128)(2,1)S(1)}, s16[1024,128]{1,0:T(8,128)(2,1)S(1)}) custom-call(bf16[1024,256]{1,0:T(8,128)(2,1)S(1)} %copy-done.6, bf16[1024,256]{1,0:T(8,128)(2,1)S(1)} %copy-done.10, bf16[1024,256]{1,0:T(8,128)(2,1)S(1)} %copy-done.12, ...), custom_call_target="tpu_custom_call" | custom-call | flops 1000 | bytes 1000 | tf_op jit(solution)/shard_map/spectra/pallas_call | solution.py:157
  80.0 2.9 %collective-permute-start.18 = (s16[1024,128]{1,0:T(8,128)(2,1)S(1)}, s16[1024,128]{1,0:T(8,128)(2,1)S(1)}, u32[]{:S(2)}, u32[]{:S(2)}) collective-permute-start(s16[1024,128]{1,0:T(8,128)(2,1)S(1)} %get-tuple-element.38), channel_id=1, source_target_pairs={{0,2},{1,3},{2,0},{3,1},{4,6},{5,7},{6,4},{7,5},{8,10},{9,11},{10,... | collective-permute-start | bytes 786440 | tf_op jit(solution)/shard_map/ppermute | solution.py:37
  82.9 2.5 %collective-permute-start.19 = (s16[1024,128]{1,0:T(8,128)(2,1)S(1)}, s16[1024,128]{1,0:T(8,128)(2,1)S(1)}, u32[]{:S(2)}, u32[]{:S(2)}) collective-permute-start(s16[1024,128]{1,0:T(8,128)(2,1)S(1)} %get-tuple-element.39), channel_id=1, source_target_pairs={{0,3},{1,0},{2,1},{3,2},{4,7},{5,4},{6,5},{7,6},{8,11},{9,8},{10,9... | collective-permute-start | bytes 786440 | tf_op jit(solution)/shard_map/ppermute | solution.py:37
  85.5 9.8 %sum_receivers.2 = (f32[4096,128]{1,0:T(8,128)S(1)}, f32[8200,128]{1,0:T(8,128)S(1)}, f32[8200,128]{1,0:T(8,128)S(1)}, f32[8200,128]{1,0:T(8,128)S(1)}, f32[8200...) custom-call(s32[4096]{0:T(1024)S(1)} %bitcast.59, s32[4]{0:T(128)S(1)} %get-tuple-element.74.refs_1_, f32[4096,128]{1,0:T(8,128)S(1)} %copy-done.2, ...), custom_call_target="tpu_custom_call" | custom-call | flops 1000 | bytes 1000 | tf_op jit(solution)/shard_map/sum_receivers/pallas_call | solution.py:237
  95.5 8.6 %sum_receivers.3 = (f32[4096,128]{1,0:T(8,128)S(1)}, f32[8200,128]{1,0:T(8,128)S(1)}, f32[8200,128]{1,0:T(8,128)S(1)}, f32[8200,128]{1,0:T(8,128)S(1)}, f32[8200...) custom-call(s32[4096]{0:T(1024)S(1)} %bitcast.61, ...), custom_call_target="tpu_custom_call", output_to_operand_aliasing={{1}: (7, {}), {2}: (8, {}), {3}: (9, {}), {4}: (10, {}), {5... | custom-call | flops 1000 | bytes 1000 | tf_op jit(solution)/shard_map/sum_receivers/pallas_call | solution.py:237
  104.1 0.8 collective-permute-start.22
  104.9 3.8 %collective-permute-done.22 = f32[4096,128]{1,0:T(8,128)S(1)} collective-permute-done((f32[4096,128]{1,0:T(8,128)S(1)}, f32[4096,128]{1,0:T(8,128)S(1)}, u32[]{:S(2)}, u32[]{:S(2)}) %collective-permute-start.22) | collective-permute-done | bytes 2097184 | tf_op jit(solution)/shard_map/ppermute | solution.py:33
  109.1 3.6 %collective-permute-start.25 = (f16[2,4,128,128]{3,2,1,0:T(8,128)(2,1)S(1)}, f16[2,4,128,128]{3,2,1,0:T(8,128)(2,1)S(1)}, u32[]{:S(2)}, u32[]{:S(2)}) collective-permute-start(f16[2,4,128,128]{3,2,1,0:T(8,128)(2,1)S(1)} %bitcast.66), channel_id=1, source_target_pairs={{0,16},{4,20},{8,24},{12,28},{16,0},{20,4},{24,8},{28,12},{32,48},... | collective-permute-start | bytes 786440 | tf_op jit(solution)/shard_map/ppermute | solution.py:33
  112.7 0.7 collective-permute-start.24
  113.4 1.8 %sum_shots.1.refs_1_ = f32[384,128]{1,0:T(8,128)S(1)} custom-call(s32[1,8192]{1,0:T(1,128)S(1)} %bitcast.57, f32[4096,128]{1,0:T(8,128)S(1)} %get-tuple-element.34.refs_0_, f32[4096,128]{1,0:T(8,128)S(1)} %get-tuple-element.45.refs_1_), custom_call_target="tpu_custom_call" | custom-call | flops 1000 | bytes 1000 | tf_op jit(solution)/shard_map/sum_shots/pallas_call | solution.py:267
  115.2 1.5 %collective-permute-start.20 = (f32[128,128]{1,0:T(8,128)S(1)}, f32[128,128]{1,0:T(8,128)S(1)}, u32[]{:S(2)}, u32[]{:S(2)}) collective-permute-start(f32[128,128]{1,0:T(8,128)S(1)} %get-tuple-element.59), channel_id=1, source_target_pairs={{0,4},{4,8},{8,12},{12,16},{16,20},{20,24},{24,28},{28,32},{32,36}... | collective-permute-start | bytes 196616 | tf_op jit(solution)/shard_map/ppermute | solution.py:280
  116.8 1.3 collective-permute-start.21
  118.1 1.8 %collective-permute-done.25 = f16[2,4,128,128]{3,2,1,0:T(8,128)(2,1)S(1)} collective-permute-done((f16[2,4,128,128]{3,2,1,0:T(8,128)(2,1)S(1)}, f16[2,4,128,128]{3,2,1,0:T(8,128)(2,1)S(1)}, u32[]{:S(2)}, u32[]{:S(2)}) %collective-permute-start.25) | collective-permute-done | bytes 262176 | tf_op jit(solution)/shard_map/ppermute | solution.py:33
  119.9 5.1 %collective-permute-done.23 = f16[2,4,128,128]{3,2,1,0:T(8,128)(2,1)S(1)} collective-permute-done((f16[2,4,128,128]{3,2,1,0:T(8,128)(2,1)S(1)}, f16[2,4,128,128]{3,2,1,0:T(8,128)(2,1)S(1)}, u32[]{:S(2)}, u32[]{:S(2)}) %collective-permute-start.23) | collective-permute-done | bytes 262176 | tf_op jit(solution)/shard_map/ppermute | solution.py:33
  125.2 2.1 %collective-permute-start.26 = (f16[4,128,128]{2,1,0:T(8,128)(2,1)S(1)}, f16[4,128,128]{2,1,0:T(8,128)(2,1)S(1)}, u32[]{:S(2)}, u32[]{:S(2)}) collective-permute-start(f16[4,128,128]{2,1,0:T(8,128)(2,1)S(1)} %get-tuple-element.57), channel_id=1, source_target_pairs={{0,32},{4,36},{8,40},{12,44},{16,48},{20,52},{24,56},{28,60},{32,0... | collective-permute-start | bytes 393224 | tf_op jit(solution)/shard_map/ppermute | solution.py:33
  127.3 3.6 %collective-permute-done.26 = f16[4,128,128]{2,1,0:T(8,128)(2,1)S(1)} collective-permute-done((f16[4,128,128]{2,1,0:T(8,128)(2,1)S(1)}, f16[4,128,128]{2,1,0:T(8,128)(2,1)S(1)}, u32[]{:S(2)}, u32[]{:S(2)}) %collective-permute-start.26) | collective-permute-done | bytes 131104 | tf_op jit(solution)/shard_map/ppermute | solution.py:33
  131.0 3.4 %collective-permute-start.27 = (f16[2,128,128]{2,1,0:T(8,128)(2,1)S(1)}, f16[2,128,128]{2,1,0:T(8,128)(2,1)S(1)}, u32[]{:S(2)}, u32[]{:S(2)}) collective-permute-start(f16[2,128,128]{2,1,0:T(8,128)(2,1)S(1)} %fusion.4), channel_id=1, source_target_pairs={{0,64},{4,68},{8,72},{12,76},{16,80},{20,84},{24,88},{28,92},{32,9... | collective-permute-start | bytes 196616 | tf_op jit(solution)/shard_map/ppermute | solution.py:33
  134.4 2.4 %collective-permute-done.27 = f16[2,128,128]{2,1,0:T(8,128)(2,1)S(1)} collective-permute-done((f16[2,128,128]{2,1,0:T(8,128)(2,1)S(1)}, f16[2,128,128]{2,1,0:T(8,128)(2,1)S(1)}, u32[]{:S(2)}, u32[]{:S(2)}) %collective-permute-start.27) | collective-permute-done | bytes 65568 | tf_op jit(solution)/shard_map/ppermute | solution.py:33
  136.8 7.3 %collective-permute-start.28 = (f16[128,128]{1,0:T(8,128)(2,1)S(1)}, f16[128,128]{1,0:T(8,128)(2,1)S(1)}, u32[]{:S(2)}, u32[]{:S(2)}) collective-permute-start(f16[128,128]{1,0:T(8,128)(2,1)S(1)} %fusion.23), channel_id=1, source_target_pairs={{0,128},{4,132},{8,136},{12,140},{16,144},{20,148},{24,152},{28,15... | collective-permute-start | bytes 98312 | tf_op jit(solution)/shard_map/ppermute | solution.py:33
  144.1 1.9 %collective-permute-done.28 = f16[128,128]{1,0:T(8,128)(2,1)S(1)} collective-permute-done((f16[128,128]{1,0:T(8,128)(2,1)S(1)}, f16[128,128]{1,0:T(8,128)(2,1)S(1)}, u32[]{:S(2)}, u32[]{:S(2)}) %collective-permute-start.28) | collective-permute-done | bytes 32800 | tf_op jit(solution)/shard_map/ppermute | solution.py:33
  (100 shorter events, 3.5 us)
Async XLA Ops:
  3.4 10.3 %copy-start.7 = (bf16[1024,256]{1,0:T(8,128)(2,1)}, bf16[1024,256]{1,0:T(8,128)(2,1)S(1)}, u32[]{:S(2)}) copy-start(bf16[1024,256]{1,0:T(8,128)(2,1)S(1)} %get-tuple-element.53.refs_0_.b0) | copy-start | bytes 1572868
  3.4 10.2 %copy-start.16 = (f32[128,128]{1,0:T(8,128)S(1)}, f32[128,128]{1,0:T(8,128)}, u32[]{:S(2)}) copy-start(f32[128,128]{1,0:T(8,128)} %a.1) | copy-start | bytes 196612
  3.4 28.0 %collective-permute-start.4 = (bf16[1024,256]{1,0:T(8,128)(2,1)}, bf16[1024,256]{1,0:T(8,128)(2,1)S(1)}, u32[]{:S(2)}, u32[]{:S(2)}) collective-permute-start(bf16[1024,256]{1,0:T(8,128)(2,1)} %get-tuple-element.50), channel_id=1, source_target_pairs={{0,3},{1,0},{2,1},{3,2},{4,7},{5,4},{6,5},{7,6},{8,11},{9,8},{10,9... | collective-permute-start | bytes 1572872 | tf_op jit(solution)/shard_map/ppermute | solution.py:37
  5.6 25.9 %collective-permute-start.3 = (bf16[1024,256]{1,0:T(8,128)(2,1)}, bf16[1024,256]{1,0:T(8,128)(2,1)S(1)}, u32[]{:S(2)}, u32[]{:S(2)}) collective-permute-start(bf16[1024,256]{1,0:T(8,128)(2,1)} %get-tuple-element.51), channel_id=1, source_target_pairs={{0,2},{1,3},{2,0},{3,1},{4,6},{5,7},{6,4},{7,5},{8,10},{9,11},{10,... | collective-permute-start | bytes 1572872 | tf_op jit(solution)/shard_map/ppermute | solution.py:37
  6.5 25.0 %collective-permute-start.2 = (bf16[1024,256]{1,0:T(8,128)(2,1)}, bf16[1024,256]{1,0:T(8,128)(2,1)}, u32[]{:S(2)}, u32[]{:S(2)}) collective-permute-start(bf16[1024,256]{1,0:T(8,128)(2,1)} %get-tuple-element.52), channel_id=1, source_target_pairs={{0,1},{1,2},{2,3},{3,0},{4,5},{5,6},{6,7},{7,4},{8,9},{9,10},{10,1... | collective-permute-start | bytes 1572872 | tf_op jit(solution)/shard_map/ppermute | solution.py:37
  8.4 8.8 %copy-start.17 = (f32[128,128]{1,0:T(8,128)S(1)}, f32[128,128]{1,0:T(8,128)}, u32[]{:S(2)}) copy-start(f32[128,128]{1,0:T(8,128)} %refs_0_.1) | copy-start | bytes 196612
  13.7 5.5 %copy-start.19 = (s32[8192]{0:T(1024)S(1)}, s32[8192]{0:T(1024)}, u32[]{:S(2)}) copy-start(s32[8192]{0:T(1024)} %param.8) | copy-start | bytes 98308
  13.7 5.7 %copy-start.20 = (s32[8192]{0:T(1024)S(1)}, s32[8192]{0:T(1024)}, u32[]{:S(2)}) copy-start(s32[8192]{0:T(1024)} %param.7) | copy-start | bytes 98308
  13.7 5.7 %collective-permute-start.8 = (s16[128,128]{1,0:T(8,128)(2,1)S(1)}, s16[128,128]{1,0:T(8,128)(2,1)S(1)}, u32[]{:S(2)}, u32[]{:S(2)}) collective-permute-start(s16[128,128]{1,0:T(8,128)(2,1)S(1)} %encode_terms.1.refs_0_), channel_id=1, source_target_pairs={{0,64},{4,68},{8,72},{12,76},{16,80},{20,84},{24,88},{28,92},{32,9... | collective-permute-start | bytes 98312 | tf_op jit(solution)/shard_map/ppermute | solution.py:33
  17.1 5.5 %collective-permute-start.1 = (f32[128,128]{1,0:T(8,128)S(1)}, f32[128,128]{1,0:T(8,128)S(1)}, u32[]{:S(2)}, u32[]{:S(2)}) collective-permute-start(f32[128,128]{1,0:T(8,128)S(1)} %join.8), channel_id=1, source_target_pairs={{4,0},{8,4},{12,8},{16,12},{20,16},{24,20},{28,24},{32,28},{36,32}... | collective-permute-start | bytes 196616 | tf_op jit(solution)/shard_map/ppermute | solution.py:280
  19.5 8.6 %collective-permute-start = (f32[128,128]{1,0:T(8,128)S(1)}, f32[128,128]{1,0:T(8,128)S(1)}, u32[]{:S(2)}, u32[]{:S(2)}) collective-permute-start(f32[128,128]{1,0:T(8,128)S(1)} %join.8), channel_id=1, source_target_pairs={{0,4},{4,8},{8,12},{12,16},{16,20},{20,24},{24,28},{28,32},{32,36}... | collective-permute-start | bytes 196616 | tf_op jit(solution)/shard_map/ppermute | solution.py:280
  22.6 8.9 %collective-permute-start.9 = (s16[256,128]{1,0:T(8,128)(2,1)S(1)}, s16[256,128]{1,0:T(8,128)(2,1)S(1)}, u32[]{:S(2)}, u32[]{:S(2)}) collective-permute-start(s16[256,128]{1,0:T(8,128)(2,1)S(1)} %join.9.refs_0_), channel_id=1, source_target_pairs={{0,128},{4,132},{8,136},{12,140},{16,144},{20,148},{24,152},{28,15... | collective-permute-start | bytes 196616 | tf_op jit(solution)/shard_map/ppermute | solution.py:33
  31.5 7.4 %collective-permute-start.10 = (s16[512,128]{1,0:T(8,128)(2,1)S(1)}, s16[512,128]{1,0:T(8,128)(2,1)S(1)}, u32[]{:S(2)}, u32[]{:S(2)}) collective-permute-start(s16[512,128]{1,0:T(8,128)(2,1)S(1)} %join.10.refs_0_), channel_id=1, source_target_pairs={{0,32},{4,36},{8,40},{12,44},{16,48},{20,52},{24,56},{28,60},{32,0... | collective-permute-start | bytes 393224 | tf_op jit(solution)/shard_map/ppermute | solution.py:33
  35.2 2.2 %copy-start = (bf16[8192,256]{1,0:T(8,128)(2,1)S(1)}, bf16[8192,256]{1,0:T(8,128)(2,1)}, u32[]{:S(2)}) copy-start(bf16[8192,256]{1,0:T(8,128)(2,1)} %traces.1) | copy-start | bytes 12582916
  37.4 7.6 %copy-start.8 = (bf16[1024,256]{1,0:T(8,128)(2,1)S(1)}, bf16[1024,256]{1,0:T(8,128)(2,1)}, u32[]{:S(2)}) copy-start(bf16[1024,256]{1,0:T(8,128)(2,1)} %copy-done.7) | copy-start | bytes 1572868
  39.7 9.9 %collective-permute-start.11 = (s16[1024,128]{1,0:T(8,128)(2,1)S(1)}, s16[1024,128]{1,0:T(8,128)(2,1)S(1)}, u32[]{:S(2)}, u32[]{:S(2)}) collective-permute-start(s16[1024,128]{1,0:T(8,128)(2,1)S(1)} %join.11.refs_0_), channel_id=1, source_target_pairs={{0,8},{4,12},{8,0},{12,4},{16,24},{20,28},{24,16},{28,20},{32,40},... | collective-permute-start | bytes 786440 | tf_op jit(solution)/shard_map/ppermute | solution.py:33
  41.0 18.8 %collective-permute-start.13 = (bf16[1024,256]{1,0:T(8,128)(2,1)S(1)}, bf16[1024,256]{1,0:T(8,128)(2,1)S(1)}, u32[]{:S(2)}, u32[]{:S(2)}) collective-permute-start(bf16[1024,256]{1,0:T(8,128)(2,1)S(1)} %get-tuple-element.31), channel_id=1, source_target_pairs={{0,1},{1,2},{2,3},{3,0},{4,5},{5,6},{6,7},{7,4},{8,9},{9,10},{10,1... | collective-permute-start | bytes 1572872 | tf_op jit(solution)/shard_map/ppermute | solution.py:37
  41.1 18.7 %collective-permute-start.14 = (bf16[1024,256]{1,0:T(8,128)(2,1)S(1)}, bf16[1024,256]{1,0:T(8,128)(2,1)S(1)}, u32[]{:S(2)}, u32[]{:S(2)}) collective-permute-start(bf16[1024,256]{1,0:T(8,128)(2,1)S(1)} %get-tuple-element.32), channel_id=1, source_target_pairs={{0,2},{1,3},{2,0},{3,1},{4,6},{5,7},{6,4},{7,5},{8,10},{9,11},{10,... | collective-permute-start | bytes 1572872 | tf_op jit(solution)/shard_map/ppermute | solution.py:37
  43.6 23.5 %collective-permute-start.15 = (bf16[1024,256]{1,0:T(8,128)(2,1)S(1)}, bf16[1024,256]{1,0:T(8,128)(2,1)S(1)}, u32[]{:S(2)}, u32[]{:S(2)}) collective-permute-start(bf16[1024,256]{1,0:T(8,128)(2,1)S(1)} %get-tuple-element.33), channel_id=1, source_target_pairs={{0,3},{1,0},{2,1},{3,2},{4,7},{5,4},{6,5},{7,6},{8,11},{9,8},{10,9... | collective-permute-start | bytes 1572872 | tf_op jit(solution)/shard_map/ppermute | solution.py:37
  49.6 2.0 %copy-start.18 = (s16[1024,128]{1,0:T(8,128)(2,1)}, s16[1024,128]{1,0:T(8,128)(2,1)S(1)}, u32[]{:S(2)}) copy-start(s16[1024,128]{1,0:T(8,128)(2,1)S(1)} %get-tuple-element.29) | copy-start | bytes 786436
  49.6 17.5 %collective-permute-start.12 = (s16[2048,128]{1,0:T(8,128)(2,1)S(1)}, s16[2048,128]{1,0:T(8,128)(2,1)S(1)}, u32[]{:S(2)}, u32[]{:S(2)}) collective-permute-start(s16[2048,128]{1,0:T(8,128)(2,1)S(1)} %join.12.refs_0_), channel_id=1, source_target_pairs={{0,16},{4,20},{8,24},{12,28},{16,0},{20,4},{24,8},{28,12},{32,48},... | collective-permute-start | bytes 1572872 | tf_op jit(solution)/shard_map/ppermute | solution.py:33
  59.8 7.4 %copy-start.1 = (f32[4096,128]{1,0:T(8,128)}, f32[4096,128]{1,0:T(8,128)S(1)}, u32[]{:S(2)}) copy-start(f32[4096,128]{1,0:T(8,128)S(1)} %get-tuple-element.25.refs_2_) | copy-start | bytes 6291460
  59.8 7.4 %copy-start.3 = (f32[4096,128]{1,0:T(8,128)}, f32[4096,128]{1,0:T(8,128)S(1)}, u32[]{:S(2)}) copy-start(f32[4096,128]{1,0:T(8,128)S(1)} %get-tuple-element.35.refs_2_) | copy-start | bytes 6291460
  59.8 7.4 %copy-start.9 = (bf16[1024,256]{1,0:T(8,128)(2,1)}, bf16[1024,256]{1,0:T(8,128)(2,1)S(1)}, u32[]{:S(2)}) copy-start(bf16[1024,256]{1,0:T(8,128)(2,1)S(1)} %collective-permute-done.13.refs_4_.b1) | copy-start | bytes 1572868
  59.8 7.4 %copy-start.11 = (bf16[1024,256]{1,0:T(8,128)(2,1)}, bf16[1024,256]{1,0:T(8,128)(2,1)S(1)}, u32[]{:S(2)}) copy-start(bf16[1024,256]{1,0:T(8,128)(2,1)S(1)} %collective-permute-done.14.refs_5_.b2) | copy-start | bytes 1572868
  67.9 17.6 %collective-permute-start.16 = (s16[4096,128]{1,0:T(8,128)(2,1)S(1)}, s16[4096,128]{1,0:T(8,128)(2,1)}, u32[]{:S(2)}, u32[]{:S(2)}) collective-permute-start(s16[4096,128]{1,0:T(8,128)(2,1)S(1)} %join.13.refs_7_), channel_id=1, source_target_pairs={{0,4},{4,0},{8,12},{12,8},{16,20},{20,16},{24,28},{28,24},{32,36},... | collective-permute-start | bytes 3145736 | tf_op jit(solution)/shard_map/ppermute | solution.py:33
  67.9 12.1 %collective-permute-start.5 = (s16[1024,128]{1,0:T(8,128)(2,1)}, s16[1024,128]{1,0:T(8,128)(2,1)}, u32[]{:S(2)}, u32[]{:S(2)}) collective-permute-start(s16[1024,128]{1,0:T(8,128)(2,1)} %get-tuple-element.27), channel_id=1, source_target_pairs={{0,1},{1,2},{2,3},{3,0},{4,5},{5,6},{6,7},{7,4},{8,9},{9,10},{10,1... | collective-permute-start | bytes 786440 | tf_op jit(solution)/shard_map/ppermute | solution.py:37
  68.5 14.4 %collective-permute-start.6 = (s16[1024,128]{1,0:T(8,128)(2,1)}, s16[1024,128]{1,0:T(8,128)(2,1)}, u32[]{:S(2)}, u32[]{:S(2)}) collective-permute-start(s16[1024,128]{1,0:T(8,128)(2,1)} %get-tuple-element.28), channel_id=1, source_target_pairs={{0,2},{1,3},{2,0},{3,1},{4,6},{5,7},{6,4},{7,5},{8,10},{9,11},{10,... | collective-permute-start | bytes 786440 | tf_op jit(solution)/shard_map/ppermute | solution.py:37
  70.5 15.0 %copy-start.2 = (f32[4096,128]{1,0:T(8,128)S(1)}, f32[4096,128]{1,0:T(8,128)}, u32[]{:S(2)}) copy-start(f32[4096,128]{1,0:T(8,128)} %copy-done.1) | copy-start | bytes 6291460
  70.5 15.0 %collective-permute-start.7 = (s16[1024,128]{1,0:T(8,128)(2,1)}, s16[1024,128]{1,0:T(8,128)(2,1)S(1)}, u32[]{:S(2)}, u32[]{:S(2)}) collective-permute-start(s16[1024,128]{1,0:T(8,128)(2,1)} %copy-done.18), channel_id=1, source_target_pairs={{0,3},{1,0},{2,1},{3,2},{4,7},{5,4},{6,5},{7,6},{8,11},{9,8},{10,9... | collective-permute-start | bytes 786440 | tf_op jit(solution)/shard_map/ppermute | solution.py:37
  72.7 1.0 copy-start.6
  73.8 1.0 copy-start.10
  74.8 1.0 copy-start.12
  75.9 1.0 copy-start.14
  79.9 15.4 %collective-permute-start.17 = (s16[1024,128]{1,0:T(8,128)(2,1)S(1)}, s16[1024,128]{1,0:T(8,128)(2,1)S(1)}, u32[]{:S(2)}, u32[]{:S(2)}) collective-permute-start(s16[1024,128]{1,0:T(8,128)(2,1)S(1)} %get-tuple-element.37), channel_id=1, source_target_pairs={{0,1},{1,2},{2,3},{3,0},{4,5},{5,6},{6,7},{7,4},{8,9},{9,10},{10,1... | collective-permute-start | bytes 786440 | tf_op jit(solution)/shard_map/ppermute | solution.py:37
  80.0 15.3 %collective-permute-start.18 = (s16[1024,128]{1,0:T(8,128)(2,1)S(1)}, s16[1024,128]{1,0:T(8,128)(2,1)S(1)}, u32[]{:S(2)}, u32[]{:S(2)}) collective-permute-start(s16[1024,128]{1,0:T(8,128)(2,1)S(1)} %get-tuple-element.38), channel_id=1, source_target_pairs={{0,2},{1,3},{2,0},{3,1},{4,6},{5,7},{6,4},{7,5},{8,10},{9,11},{10,... | collective-permute-start | bytes 786440 | tf_op jit(solution)/shard_map/ppermute | solution.py:37
  82.9 12.6 %collective-permute-start.19 = (s16[1024,128]{1,0:T(8,128)(2,1)S(1)}, s16[1024,128]{1,0:T(8,128)(2,1)S(1)}, u32[]{:S(2)}, u32[]{:S(2)}) collective-permute-start(s16[1024,128]{1,0:T(8,128)(2,1)S(1)} %get-tuple-element.39), channel_id=1, source_target_pairs={{0,3},{1,0},{2,1},{3,2},{4,7},{5,4},{6,5},{7,6},{8,11},{9,8},{10,9... | collective-permute-start | bytes 786440 | tf_op jit(solution)/shard_map/ppermute | solution.py:37
  85.5 10.0 %copy-start.4 = (f32[4096,128]{1,0:T(8,128)S(1)}, f32[4096,128]{1,0:T(8,128)}, u32[]{:S(2)}) copy-start(f32[4096,128]{1,0:T(8,128)} %copy-done.3) | copy-start | bytes 6291460
  104.1 4.6 %collective-permute-start.22 = (f32[4096,128]{1,0:T(8,128)S(1)}, f32[4096,128]{1,0:T(8,128)S(1)}, u32[]{:S(2)}, u32[]{:S(2)}) collective-permute-start(f32[4096,128]{1,0:T(8,128)S(1)} %get-tuple-element.47), channel_id=1, source_target_pairs={{0,4},{4,0},{8,12},{12,8},{16,20},{20,16},{24,28},{28,24},{32,36},... | collective-permute-start | bytes 6291464 | tf_op jit(solution)/shard_map/ppermute | solution.py:33
  109.1 10.8 %collective-permute-start.25 = (f16[2,4,128,128]{3,2,1,0:T(8,128)(2,1)S(1)}, f16[2,4,128,128]{3,2,1,0:T(8,128)(2,1)S(1)}, u32[]{:S(2)}, u32[]{:S(2)}) collective-permute-start(f16[2,4,128,128]{3,2,1,0:T(8,128)(2,1)S(1)} %bitcast.66), channel_id=1, source_target_pairs={{0,16},{4,20},{8,24},{12,28},{16,0},{20,4},{24,8},{28,12},{32,48},... | collective-permute-start | bytes 786440 | tf_op jit(solution)/shard_map/ppermute | solution.py:33
  112.7 12.2 %collective-permute-start.23 = (f16[2,4,128,128]{3,2,1,0:T(8,128)(2,1)S(1)}, f16[2,4,128,128]{3,2,1,0:T(8,128)(2,1)S(1)}, u32[]{:S(2)}, u32[]{:S(2)}) collective-permute-start(f16[2,4,128,128]{3,2,1,0:T(8,128)(2,1)S(1)} %bitcast.65), channel_id=1, source_target_pairs={{0,8},{4,12},{8,0},{12,4},{16,24},{20,28},{24,16},{28,20},{32,40},... | collective-permute-start | bytes 786440 | tf_op jit(solution)/shard_map/ppermute | solution.py:33
  112.7 12.2 %collective-permute-start.24 = (f16[2,4,128,128]{3,2,1,0:T(8,128)(2,1)S(1)}, f16[2,4,128,128]{3,2,1,0:T(8,128)(2,1)S(1)}, u32[]{:S(2)}, u32[]{:S(2)}) collective-permute-start(f16[2,4,128,128]{3,2,1,0:T(8,128)(2,1)S(1)} %bitcast.64), channel_id=1, source_target_pairs={{0,24},{4,28},{8,16},{12,20},{16,8},{20,12},{24,0},{28,4},{32,56},... | collective-permute-start | bytes 786440 | tf_op jit(solution)/shard_map/ppermute | solution.py:33
  115.2 12.0 %collective-permute-start.20 = (f32[128,128]{1,0:T(8,128)S(1)}, f32[128,128]{1,0:T(8,128)S(1)}, u32[]{:S(2)}, u32[]{:S(2)}) collective-permute-start(f32[128,128]{1,0:T(8,128)S(1)} %get-tuple-element.59), channel_id=1, source_target_pairs={{0,4},{4,8},{8,12},{12,16},{16,20},{20,24},{24,28},{28,32},{32,36}... | collective-permute-start | bytes 196616 | tf_op jit(solution)/shard_map/ppermute | solution.py:280
  116.8 10.5 %collective-permute-start.21 = (f32[128,128]{1,0:T(8,128)S(1)}, f32[128,128]{1,0:T(8,128)S(1)}, u32[]{:S(2)}, u32[]{:S(2)}) collective-permute-start(f32[128,128]{1,0:T(8,128)S(1)} %get-tuple-element.60), channel_id=1, source_target_pairs={{4,0},{8,4},{12,8},{16,12},{20,16},{24,20},{28,24},{32,28},{36,32}... | collective-permute-start | bytes 196616 | tf_op jit(solution)/shard_map/ppermute | solution.py:280
  125.2 5.8 %collective-permute-start.26 = (f16[4,128,128]{2,1,0:T(8,128)(2,1)S(1)}, f16[4,128,128]{2,1,0:T(8,128)(2,1)S(1)}, u32[]{:S(2)}, u32[]{:S(2)}) collective-permute-start(f16[4,128,128]{2,1,0:T(8,128)(2,1)S(1)} %get-tuple-element.57), channel_id=1, source_target_pairs={{0,32},{4,36},{8,40},{12,44},{16,48},{20,52},{24,56},{28,60},{32,0... | collective-permute-start | bytes 393224 | tf_op jit(solution)/shard_map/ppermute | solution.py:33
  127.3 19.4 %copy-start.15 = (f32[128,128]{1,0:T(8,128)}, f32[128,128]{1,0:T(8,128)S(1)}, u32[]{:S(2)}) copy-start(f32[128,128]{1,0:T(8,128)S(1)} %fusion.7.refs_1_) | copy-start | bytes 196612
  131.0 5.8 %collective-permute-start.27 = (f16[2,128,128]{2,1,0:T(8,128)(2,1)S(1)}, f16[2,128,128]{2,1,0:T(8,128)(2,1)S(1)}, u32[]{:S(2)}, u32[]{:S(2)}) collective-permute-start(f16[2,128,128]{2,1,0:T(8,128)(2,1)S(1)} %fusion.4), channel_id=1, source_target_pairs={{0,64},{4,68},{8,72},{12,76},{16,80},{20,84},{24,88},{28,92},{32,9... | collective-permute-start | bytes 196616 | tf_op jit(solution)/shard_map/ppermute | solution.py:33
  136.8 9.2 %collective-permute-start.28 = (f16[128,128]{1,0:T(8,128)(2,1)S(1)}, f16[128,128]{1,0:T(8,128)(2,1)S(1)}, u32[]{:S(2)}, u32[]{:S(2)}) collective-permute-start(f16[128,128]{1,0:T(8,128)(2,1)S(1)} %fusion.23), channel_id=1, source_target_pairs={{0,128},{4,132},{8,136},{12,140},{16,144},{20,148},{24,152},{28,15... | collective-permute-start | bytes 98312 | tf_op jit(solution)/shard_map/ppermute | solution.py:33
  (2 other events, 1.6 us)

commit v14 on v13

--- a/solution.py
+++ b/solution.py
@@ -337,16 +337,17 @@
         resid, *held = sum_receivers(codes[some], part_shots, [terms, far_terms], live[some], at, held, last)
         residuals.append(resid)
     sums, far_sums = held[-2:]
-    sums = (sums + swap(far_sums, 0, 0, 1)).reshape(NX, 2, NZ // 2, block, width)
+    sums = (sums + swap(far_sums, 0, 0, 1)).reshape(NX, 2, NZ // 2 * block, width)
     shots = sum_shots(residuals, shot_at, 3 * block)
     sent = (sums * SUM_SCALE).astype(jnp.float16)
-    come = [swap(sent[k], 0, k, 0).astype(jnp.float32) for k in (1, 3, 2)]
-    mine = join([sums[0].reshape(-1, width)], (shots,)).reshape(sums.shape[1:])
-    sums = mine + (come[0] + come[1] + come[2]) * (1.0 / SUM_SCALE)
+    halves = [None, None]
+    for h in (1, 0):
+        come = [swap(sent[k, h], 0, k, 0).astype(jnp.float32) for k in (1, 3, 2)]
+        mine = join([sums[0, h]], (shots,)) if h else sums[0, h]
+        halves[h] = mine + (come[0] + come[1] + come[2]) * (1.0 / SUM_SCALE)
     shot_sums = shots[block : 2 * block] + neighbour(shots[2 * block :], 1) + neighbour(shots[:block], -1)
-    sent = (sums[1] * SUM_SCALE).astype(jnp.float16)
-    mine = join([sums[0].reshape(-1, width)], (shot_sums,)).reshape(sums.shape[1:])
-    sums = mine + swap(sent, 1, 0, 0).astype(jnp.float32) * (1.0 / SUM_SCALE)
+    sent = (halves[1] * SUM_SCALE).astype(jnp.float16)
+    sums = halves[0] + swap(sent, 1, 0, 0).astype(jnp.float32) * (1.0 / SUM_SCALE)
     sums = sums.reshape(2, 2, block, width)
     sent = (sums[:, 1] * SUM_SCALE).astype(jnp.float16)
     sums = sums[:, 0] + swap(sent, 2, 0, 0).astype(jnp.float32) * (1.0 / SUM_SCALE)

time: 147 us -> 148 us (level)
  waiting for transfers between devices: 30.8 us -> 22.5 us
  starting transfers between devices: 59.8 us -> 67 us
    ppermute x13 -> x16, waiting for transfers between devices: 23.2 us -> 15.2 us  [swap(): lax.ppermute(value, 'tr', [(tr_of(z, x, c), tr_of(z ^ dz, x ^ dx, c ^ dc)...]
    ppermute x13 -> x16, starting transfers between devices: 33.6 us -> 41.1 us  [swap(): lax.ppermute(value, 'tr', [(tr_of(z, x, c), tr_of(z ^ dz, x ^ dx, c ^ dc)...]
    unnamed x47 -> x45, local copies, waits for them, and re-layouts: 7.93 us -> 7.92 us
  transfers between devices with their start and end apart: 29 -> 32, of which waited for: 10 -> 10; matrix products, arithmetic and copies ran while one was open for 1% -> 1% of each run, Pallas kernels for 22% -> 23%
where the time goes in v14:
time: 148 us
  starting transfers between devices  67 us (45%)
  Pallas kernels  42.8 us (29%)
  waiting for transfers between devices  22.5 us (15%)
  local copies, waits for them, and re-layouts  11.1 us (8%)
  other arithmetic  2.27 us (2%)
  between operations  1.97 us (1%)
    ppermute x16, starting transfers between devices, swap(): lax.ppermute(value, 'tr', [(tr_of(z, x, c), tr_of(z ^ dz, x ^ dx, c ^ dc)...  41.1 us
    pallas_call x2, Pallas kernels, sum_receivers(): pl.pallas_call(body, in_specs=[sm, sm] + [vm] * (1 + parts + len(given)),...  19.5 us
    ppermute x12, starting transfers between devices, send_y(): return lax.ppermute(value, 'fq', [(i, (i + k) % NY) for i in range(NY)])  19.1 us
    ppermute x16, waiting for transfers between devices, swap(): lax.ppermute(value, 'tr', [(tr_of(z, x, c), tr_of(z ^ dz, x ^ dx, c ^ dc)...  15.2 us
    pallas_call x1, Pallas kernels, gather_shots(): pl.pallas_call(body, in_specs=[sm, vm], out_specs=[vm] * len(sizes), out_...  8.11 us
    unnamed x45, local copies, waits for them, and re-layouts  7.92 us
    pallas_call x2, Pallas kernels, spectra(): pl.pallas_call(body, grid=(rows // tile,), in_specs=[pl.BlockSpec((tile,...  7.63 us
    ppermute x12, waiting for transfers between devices, send_y(): return lax.ppermute(value, 'fq', [(i, (i + k) % NY) for i in range(NY)])  7.29 us
  transfers between devices with their start and end apart: 32, of which 10 were waited for; matrix products, arithmetic and copies ran while one was open for 1% of the time, Pallas kernels for 23%

profile of v14, /device:TPU:8, one launch (start us, length us, event | category | flops | bytes accessed | tf_op | source)
XLA Modules:
  0.0 147.7 jit_solution(15655294200176711664)
XLA Ops:
  0.7 2.7 %constant_dynamic-slice_fusion = (bf16[1024,256]{1,0:T(8,128)(2,1)}, bf16[1024,256]{1,0:T(8,128)(2,1)}, bf16[1024,256]{1,0:T(8,128)(2,1)}, bf16[1024,256]{1,0:T(8,128)(2,1)S(1)}) fusion(bf16[8192,256]{1,0:T(8,128)(2,1)} %traces.1, s32[]{:T(128)S(6)} %select_n.159, s32[]{:T(128)S(6)} %select_n.157, s32[]{:T(128)S(6)} %select_n.155, s32[]{:T(128)S(6)} %select_n.153), kind=kLoop, calls=%fused_computation.81 | loop fusion | bytes 4194320 | tf_op jit(solution)/shard_map/dynamic_slice | solution.py:296
  3.4 2.2 %collective-permute-start.4 = (bf16[1024,256]{1,0:T(8,128)(2,1)}, bf16[1024,256]{1,0:T(8,128)(2,1)S(1)}, u32[]{:S(2)}, u32[]{:S(2)}) collective-permute-start(bf16[1024,256]{1,0:T(8,128)(2,1)} %get-tuple-element.48), channel_id=1, source_target_pairs={{0,3},{1,0},{2,1},{3,2},{4,7},{5,4},{6,5},{7,6},{8,11},{9,8},{10,9... | collective-permute-start | bytes 1572872 | tf_op jit(solution)/shard_map/ppermute | solution.py:37
  5.6 0.9 collective-permute-start.3
  6.5 1.9 %collective-permute-start.2 = (bf16[1024,256]{1,0:T(8,128)(2,1)}, bf16[1024,256]{1,0:T(8,128)(2,1)}, u32[]{:S(2)}, u32[]{:S(2)}) collective-permute-start(bf16[1024,256]{1,0:T(8,128)(2,1)} %get-tuple-element.50), channel_id=1, source_target_pairs={{0,1},{1,2},{2,3},{3,0},{4,5},{5,6},{6,7},{7,4},{8,9},{9,10},{10,1... | collective-permute-start | bytes 1572872 | tf_op jit(solution)/shard_map/ppermute | solution.py:37
  8.4 5.3 %make_table.1.refs_1_.t.refs_0_ = bf16[1024,1024]{1,0:T(8,128)(2,1)S(1)} custom-call(s32[1]{0:T(128)} %bitcast.10.y_ref, bf16[1024,256]{1,0:T(8,128)(2,1)S(1)} %get-tuple-element.51.refs_0_.b0), custom_call_target="tpu_custom_call" | custom-call | flops 1073741824 | bytes 33554432 | tf_op jit(solution)/shard_map/make_table/pallas_call | solution.py:64
  13.7 3.4 %collective-permute-start.8 = (s16[128,128]{1,0:T(8,128)(2,1)S(1)}, s16[128,128]{1,0:T(8,128)(2,1)S(1)}, u32[]{:S(2)}, u32[]{:S(2)}) collective-permute-start(s16[128,128]{1,0:T(8,128)(2,1)S(1)} %encode_terms.1.refs_0_), channel_id=1, source_target_pairs={{0,64},{4,68},{8,72},{12,76},{16,80},{20,84},{24,88},{28,92},{32,9... | collective-permute-start | bytes 98312 | tf_op jit(solution)/shard_map/ppermute | solution.py:33
  17.1 1.3 collective-permute-start.1
  19.5 3.0 %collective-permute-start = (f32[128,128]{1,0:T(8,128)S(1)}, f32[128,128]{1,0:T(8,128)S(1)}, u32[]{:S(2)}, u32[]{:S(2)}) collective-permute-start(f32[128,128]{1,0:T(8,128)S(1)} %join.7), channel_id=1, source_target_pairs={{0,4},{4,8},{8,12},{12,16},{16,20},{20,24},{24,28},{28,32},{32,36}... | collective-permute-start | bytes 196616 | tf_op jit(solution)/shard_map/ppermute | solution.py:280
  22.6 5.5 %collective-permute-start.9 = (s16[256,128]{1,0:T(8,128)(2,1)S(1)}, s16[256,128]{1,0:T(8,128)(2,1)S(1)}, u32[]{:S(2)}, u32[]{:S(2)}) collective-permute-start(s16[256,128]{1,0:T(8,128)(2,1)S(1)} %join.8.refs_0_), channel_id=1, source_target_pairs={{0,128},{4,132},{8,136},{12,140},{16,144},{20,148},{24,152},{28,15... | collective-permute-start | bytes 196616 | tf_op jit(solution)/shard_map/ppermute | solution.py:33
  28.1 3.4 %collective-permute-done.9.refs_1_ = s16[256,128]{1,0:T(8,128)(2,1)S(1)} collective-permute-done((s16[256,128]{1,0:T(8,128)(2,1)S(1)}, s16[256,128]{1,0:T(8,128)(2,1)S(1)}, u32[]{:S(2)}, u32[]{:S(2)}) %collective-permute-start.9) | collective-permute-done | bytes 65568 | tf_op jit(solution)/shard_map/ppermute | solution.py:33
  31.5 3.7 %collective-permute-start.10 = (s16[512,128]{1,0:T(8,128)(2,1)S(1)}, s16[512,128]{1,0:T(8,128)(2,1)S(1)}, u32[]{:S(2)}, u32[]{:S(2)}) collective-permute-start(s16[512,128]{1,0:T(8,128)(2,1)S(1)} %join.9.refs_0_), channel_id=1, source_target_pairs={{0,32},{4,36},{8,40},{12,44},{16,48},{20,52},{24,56},{28,60},{32,0... | collective-permute-start | bytes 393224 | tf_op jit(solution)/shard_map/ppermute | solution.py:33
  35.2 2.2 %copy-done = bf16[8192,256]{1,0:T(8,128)(2,1)S(1)} copy-done((bf16[8192,256]{1,0:T(8,128)(2,1)S(1)}, bf16[8192,256]{1,0:T(8,128)(2,1)}, u32[]{:S(2)}) %copy-start) | copy-done | bytes 4194328
  37.5 1.3 collective-permute-done.10.refs_1_
  38.9 0.8 copy-done.5
  39.7 1.2 collective-permute-start.11
  41.1 2.4 %collective-permute-start.14 = (bf16[1024,256]{1,0:T(8,128)(2,1)S(1)}, bf16[1024,256]{1,0:T(8,128)(2,1)S(1)}, u32[]{:S(2)}, u32[]{:S(2)}) collective-permute-start(bf16[1024,256]{1,0:T(8,128)(2,1)S(1)} %get-tuple-element.32), channel_id=1, source_target_pairs={{0,2},{1,3},{2,0},{3,1},{4,6},{5,7},{6,4},{7,5},{8,10},{9,11},{10,... | collective-permute-start | bytes 1572872 | tf_op jit(solution)/shard_map/ppermute | solution.py:37
  43.6 1.4 collective-permute-start.15
  45.0 4.6 %spectra.2 = (s16[1024,128]{1,0:T(8,128)(2,1)S(1)}, s16[1024,128]{1,0:T(8,128)(2,1)}, s16[1024,128]{1,0:T(8,128)(2,1)}, s16[1024,128]{1,0:T(8,128)(2,1)S(1)}) custom-call(bf16[1024,256]{1,0:T(8,128)(2,1)S(1)} %copy-done.8, bf16[1024,256]{1,0:T(8,128)(2,1)} %collective-permute-done.2.b1.refs_2_.refs_0_, ...), custom_call_target="tpu_custom_call" | custom-call | flops 1000 | bytes 1000 | tf_op jit(solution)/shard_map/spectra/pallas_call | solution.py:157
  49.6 2.0 %collective-permute-start.12 = (s16[2048,128]{1,0:T(8,128)(2,1)S(1)}, s16[2048,128]{1,0:T(8,128)(2,1)S(1)}, u32[]{:S(2)}, u32[]{:S(2)}) collective-permute-start(s16[2048,128]{1,0:T(8,128)(2,1)S(1)} %join.11.refs_0_), channel_id=1, source_target_pairs={{0,16},{4,20},{8,24},{12,28},{16,0},{20,4},{24,8},{28,12},{32,48},... | collective-permute-start | bytes 1572872 | tf_op jit(solution)/shard_map/ppermute | solution.py:33
  51.7 8.1 %gather_shots.1 = (f32[4096,128]{1,0:T(8,128)S(1)}, f32[4096,128]{1,0:T(8,128)S(1)}) custom-call(s32[8192]{0:T(1024)S(1)} %bitcast_dynamic-update-slice_fusion.shot_at, f32[384,128]{1,0:T(8,128)S(1)} %pad_maximum_fusion.shot.refs_5_), custom_call_target="tpu_custom_call" | custom-call | flops 1000 | bytes 1000 | tf_op jit(solution)/shard_map/gather_shots/pallas_call | solution.py:186
  59.8 7.3 %collective-permute-done.15.refs_6_.b3 = bf16[1024,256]{1,0:T(8,128)(2,1)S(1)} collective-permute-done((bf16[1024,256]{1,0:T(8,128)(2,1)S(1)}, bf16[1024,256]{1,0:T(8,128)(2,1)S(1)}, u32[]{:S(2)}, u32[]{:S(2)}) %collective-permute-start.15) | collective-permute-done | bytes 524320 | tf_op jit(solution)/shard_map/ppermute | solution.py:37
  68.5 1.9 %collective-permute-start.6 = (s16[1024,128]{1,0:T(8,128)(2,1)}, s16[1024,128]{1,0:T(8,128)(2,1)}, u32[]{:S(2)}, u32[]{:S(2)}) collective-permute-start(s16[1024,128]{1,0:T(8,128)(2,1)} %get-tuple-element.28), channel_id=1, source_target_pairs={{0,2},{1,3},{2,0},{3,1},{4,6},{5,7},{6,4},{7,5},{8,10},{9,11},{10,... | collective-permute-start | bytes 786440 | tf_op jit(solution)/shard_map/ppermute | solution.py:37
  70.5 2.3 %collective-permute-start.7 = (s16[1024,128]{1,0:T(8,128)(2,1)}, s16[1024,128]{1,0:T(8,128)(2,1)S(1)}, u32[]{:S(2)}, u32[]{:S(2)}) collective-permute-start(s16[1024,128]{1,0:T(8,128)(2,1)} %copy-done.17), channel_id=1, source_target_pairs={{0,3},{1,0},{2,1},{3,2},{4,7},{5,4},{6,5},{7,6},{8,11},{9,8},{10,9... | collective-permute-start | bytes 786440 | tf_op jit(solution)/shard_map/ppermute | solution.py:37
  72.7 1.0 copy-done.6
  73.8 1.0 copy-done.10
  74.8 1.0 copy-done.12
  75.9 1.0 copy-done.14
  76.9 3.0 %spectra.3 = (s16[1024,128]{1,0:T(8,128)(2,1)S(1)}, s16[1024,128]{1,0:T(8,128)(2,1)S(1)}, s16[1024,128]{1,0:T(8,128)(2,1)S(1)}, s16[1024,128]{1,0:T(8,128)(2,1)S(1)}) custom-call(bf16[1024,256]{1,0:T(8,128)(2,1)S(1)} %copy-done.6, bf16[1024,256]{1,0:T(8,128)(2,1)S(1)} %copy-done.10, bf16[1024,256]{1,0:T(8,128)(2,1)S(1)} %copy-done.12, ...), custom_call_target="tpu_custom_call" | custom-call | flops 1000 | bytes 1000 | tf_op jit(solution)/shard_map/spectra/pallas_call | solution.py:157
  80.0 2.9 %collective-permute-start.18 = (s16[1024,128]{1,0:T(8,128)(2,1)S(1)}, s16[1024,128]{1,0:T(8,128)(2,1)S(1)}, u32[]{:S(2)}, u32[]{:S(2)}) collective-permute-start(s16[1024,128]{1,0:T(8,128)(2,1)S(1)} %get-tuple-element.38), channel_id=1, source_target_pairs={{0,2},{1,3},{2,0},{3,1},{4,6},{5,7},{6,4},{7,5},{8,10},{9,11},{10,... | collective-permute-start | bytes 786440 | tf_op jit(solution)/shard_map/ppermute | solution.py:37
  82.9 2.5 %collective-permute-start.19 = (s16[1024,128]{1,0:T(8,128)(2,1)S(1)}, s16[1024,128]{1,0:T(8,128)(2,1)S(1)}, u32[]{:S(2)}, u32[]{:S(2)}) collective-permute-start(s16[1024,128]{1,0:T(8,128)(2,1)S(1)} %get-tuple-element.39), channel_id=1, source_target_pairs={{0,3},{1,0},{2,1},{3,2},{4,7},{5,4},{6,5},{7,6},{8,11},{9,8},{10,9... | collective-permute-start | bytes 786440 | tf_op jit(solution)/shard_map/ppermute | solution.py:37
  85.5 10.2 %sum_receivers.2 = (f32[4096,128]{1,0:T(8,128)S(1)}, f32[8200,128]{1,0:T(8,128)S(1)}, f32[8200,128]{1,0:T(8,128)S(1)}, f32[8200,128]{1,0:T(8,128)S(1)}, f32[8200...) custom-call(s32[4096]{0:T(1024)S(1)} %bitcast.77, s32[4]{0:T(128)S(1)} %get-tuple-element.73.refs_1_, f32[4096,128]{1,0:T(8,128)S(1)} %copy-done.2, ...), custom_call_target="tpu_custom_call" | custom-call | flops 1000 | bytes 1000 | tf_op jit(solution)/shard_map/sum_receivers/pallas_call | solution.py:237
  95.8 9.3 %sum_receivers.3 = (f32[4096,128]{1,0:T(8,128)S(1)}, f32[8200,128]{1,0:T(8,128)S(1)}, f32[8200,128]{1,0:T(8,128)S(1)}, f32[8200,128]{1,0:T(8,128)S(1)}, f32[8200...) custom-call(s32[4096]{0:T(1024)S(1)} %bitcast.79, ...), custom_call_target="tpu_custom_call", output_to_operand_aliasing={{1}: (7, {}), {2}: (8, {}), {3}: (9, {}), {4}: (10, {}), {5... | custom-call | flops 1000 | bytes 1000 | tf_op jit(solution)/shard_map/sum_receivers/pallas_call | solution.py:237
  105.2 1.8 %sum_shots.1.refs_1_ = f32[384,128]{1,0:T(8,128)S(1)} custom-call(s32[1,8192]{1,0:T(1,128)S(1)} %bitcast.75, f32[4096,128]{1,0:T(8,128)S(1)} %get-tuple-element.34.refs_0_, f32[4096,128]{1,0:T(8,128)S(1)} %get-tuple-element.45.refs_1_), custom_call_target="tpu_custom_call" | custom-call | flops 1000 | bytes 1000 | tf_op jit(solution)/shard_map/sum_shots/pallas_call | solution.py:267
  107.0 2.3 %collective-permute-done.22 = f32[4096,128]{1,0:T(8,128)S(1)} collective-permute-done((f32[4096,128]{1,0:T(8,128)S(1)}, f32[4096,128]{1,0:T(8,128)S(1)}, u32[]{:S(2)}, u32[]{:S(2)}) %collective-permute-start.22) | collective-permute-done | bytes 2097184 | tf_op jit(solution)/shard_map/ppermute | solution.py:33
  110.5 2.4 %collective-permute-start.28 = (f16[512,128]{1,0:T(8,128)(2,1)S(1)}, f16[512,128]{1,0:T(8,128)(2,1)S(1)}, u32[]{:S(2)}, u32[]{:S(2)}) collective-permute-start(f16[512,128]{1,0:T(8,128)(2,1)S(1)} %get-tuple-element.53), channel_id=1, source_target_pairs={{0,16},{4,20},{8,24},{12,28},{16,0},{20,4},{24,8},{28,12},{32,48},... | collective-permute-start | bytes 393224 | tf_op jit(solution)/shard_map/ppermute | solution.py:33
  112.9 1.9 %collective-permute-start.27 = (f16[512,128]{1,0:T(8,128)(2,1)S(1)}, f16[512,128]{1,0:T(8,128)(2,1)S(1)}, u32[]{:S(2)}, u32[]{:S(2)}) collective-permute-start(f16[512,128]{1,0:T(8,128)(2,1)S(1)} %get-tuple-element.54), channel_id=1, source_target_pairs={{0,24},{4,28},{8,16},{12,20},{16,8},{20,12},{24,0},{28,4},{32,56},... | collective-permute-start | bytes 393224 | tf_op jit(solution)/shard_map/ppermute | solution.py:33
  114.8 2.9 %collective-permute-start.25 = (f16[512,128]{1,0:T(8,128)(2,1)S(1)}, f16[512,128]{1,0:T(8,128)(2,1)S(1)}, u32[]{:S(2)}, u32[]{:S(2)}) collective-permute-start(f16[512,128]{1,0:T(8,128)(2,1)S(1)} %get-tuple-element.56), channel_id=1, source_target_pairs={{0,16},{4,20},{8,24},{12,28},{16,0},{20,4},{24,8},{28,12},{32,48},... | collective-permute-start | bytes 393224 | tf_op jit(solution)/shard_map/ppermute | solution.py:33
  117.8 2.3 %collective-permute-done.28 = f16[512,128]{1,0:T(8,128)(2,1)S(1)} collective-permute-done((f16[512,128]{1,0:T(8,128)(2,1)S(1)}, f16[512,128]{1,0:T(8,128)(2,1)S(1)}, u32[]{:S(2)}, u32[]{:S(2)}) %collective-permute-start.28) | collective-permute-done | bytes 131104 | tf_op jit(solution)/shard_map/ppermute | solution.py:33
  120.1 1.9 %collective-permute-start.24 = (f16[512,128]{1,0:T(8,128)(2,1)S(1)}, f16[512,128]{1,0:T(8,128)(2,1)S(1)}, u32[]{:S(2)}, u32[]{:S(2)}) collective-permute-start(f16[512,128]{1,0:T(8,128)(2,1)S(1)} %get-tuple-element.57), channel_id=1, source_target_pairs={{0,24},{4,28},{8,16},{12,20},{16,8},{20,12},{24,0},{28,4},{32,56},... | collective-permute-start | bytes 393224 | tf_op jit(solution)/shard_map/ppermute | solution.py:33
  122.3 1.9 %collective-permute-start.29 = (f16[512,128]{1,0:T(8,128)(2,1)S(1)}, f16[512,128]{1,0:T(8,128)(2,1)S(1)}, u32[]{:S(2)}, u32[]{:S(2)}) collective-permute-start(f16[512,128]{1,0:T(8,128)(2,1)S(1)} %multiply_convert_fusion.1), channel_id=1, source_target_pairs={{0,32},{4,36},{8,40},{12,44},{16,48},{20,52},{24,56},{28,60},{32,0... | collective-permute-start | bytes 393224 | tf_op jit(solution)/shard_map/ppermute | solution.py:33
  124.2 1.0 collective-permute-done.25
  125.2 2.7 %collective-permute-done.24 = f16[512,128]{1,0:T(8,128)(2,1)S(1)} collective-permute-done((f16[512,128]{1,0:T(8,128)(2,1)S(1)}, f16[512,128]{1,0:T(8,128)(2,1)S(1)}, u32[]{:S(2)}, u32[]{:S(2)}) %collective-permute-start.24) | collective-permute-done | bytes 131104 | tf_op jit(solution)/shard_map/ppermute | solution.py:33
  128.0 3.3 %collective-permute-start.30 = (f16[2,128,128]{2,1,0:T(8,128)(2,1)S(1)}, f16[2,128,128]{2,1,0:T(8,128)(2,1)S(1)}, u32[]{:S(2)}, u32[]{:S(2)}) collective-permute-start(f16[2,128,128]{2,1,0:T(8,128)(2,1)S(1)} %fusion.5), channel_id=1, source_target_pairs={{0,64},{4,68},{8,72},{12,76},{16,80},{20,84},{24,88},{28,92},{32,9... | collective-permute-start | bytes 196616 | tf_op jit(solution)/shard_map/ppermute | solution.py:33
  131.3 1.3 collective-permute-start.20
  132.6 1.3 collective-permute-start.21
  133.9 0.7 collective-permute-done.30
  134.7 10.4 %collective-permute-start.31 = (f16[128,128]{1,0:T(8,128)(2,1)S(1)}, f16[128,128]{1,0:T(8,128)(2,1)S(1)}, u32[]{:S(2)}, u32[]{:S(2)}) collective-permute-start(f16[128,128]{1,0:T(8,128)(2,1)S(1)} %fusion.24), channel_id=1, source_target_pairs={{0,128},{4,132},{8,136},{12,140},{16,144},{20,148},{24,152},{28,15... | collective-permute-start | bytes 98312 | tf_op jit(solution)/shard_map/ppermute | solution.py:33
  145.8 1.2 collective-permute-done.31
  (103 shorter events, 5.5 us)
Async XLA Ops:
  3.4 10.3 %copy-start.7 = (bf16[1024,256]{1,0:T(8,128)(2,1)}, bf16[1024,256]{1,0:T(8,128)(2,1)S(1)}, u32[]{:S(2)}) copy-start(bf16[1024,256]{1,0:T(8,128)(2,1)S(1)} %get-tuple-element.51.refs_0_.b0) | copy-start | bytes 1572868
  3.4 10.2 %copy-start.15 = (f32[128,128]{1,0:T(8,128)S(1)}, f32[128,128]{1,0:T(8,128)}, u32[]{:S(2)}) copy-start(f32[128,128]{1,0:T(8,128)} %a.1) | copy-start | bytes 196612
  3.4 28.0 %collective-permute-start.4 = (bf16[1024,256]{1,0:T(8,128)(2,1)}, bf16[1024,256]{1,0:T(8,128)(2,1)S(1)}, u32[]{:S(2)}, u32[]{:S(2)}) collective-permute-start(bf16[1024,256]{1,0:T(8,128)(2,1)} %get-tuple-element.48), channel_id=1, source_target_pairs={{0,3},{1,0},{2,1},{3,2},{4,7},{5,4},{6,5},{7,6},{8,11},{9,8},{10,9... | collective-permute-start | bytes 1572872 | tf_op jit(solution)/shard_map/ppermute | solution.py:37
  5.6 25.9 %collective-permute-start.3 = (bf16[1024,256]{1,0:T(8,128)(2,1)}, bf16[1024,256]{1,0:T(8,128)(2,1)S(1)}, u32[]{:S(2)}, u32[]{:S(2)}) collective-permute-start(bf16[1024,256]{1,0:T(8,128)(2,1)} %get-tuple-element.49), channel_id=1, source_target_pairs={{0,2},{1,3},{2,0},{3,1},{4,6},{5,7},{6,4},{7,5},{8,10},{9,11},{10,... | collective-permute-start | bytes 1572872 | tf_op jit(solution)/shard_map/ppermute | solution.py:37
  6.5 25.0 %collective-permute-start.2 = (bf16[1024,256]{1,0:T(8,128)(2,1)}, bf16[1024,256]{1,0:T(8,128)(2,1)}, u32[]{:S(2)}, u32[]{:S(2)}) collective-permute-start(bf16[1024,256]{1,0:T(8,128)(2,1)} %get-tuple-element.50), channel_id=1, source_target_pairs={{0,1},{1,2},{2,3},{3,0},{4,5},{5,6},{6,7},{7,4},{8,9},{9,10},{10,1... | collective-permute-start | bytes 1572872 | tf_op jit(solution)/shard_map/ppermute | solution.py:37
  8.4 8.8 %copy-start.16 = (f32[128,128]{1,0:T(8,128)S(1)}, f32[128,128]{1,0:T(8,128)}, u32[]{:S(2)}) copy-start(f32[128,128]{1,0:T(8,128)} %refs_0_.1) | copy-start | bytes 196612
  13.7 5.5 %copy-start.18 = (s32[8192]{0:T(1024)S(1)}, s32[8192]{0:T(1024)}, u32[]{:S(2)}) copy-start(s32[8192]{0:T(1024)} %param.8) | copy-start | bytes 98308
  13.7 5.7 %copy-start.19 = (s32[8192]{0:T(1024)S(1)}, s32[8192]{0:T(1024)}, u32[]{:S(2)}) copy-start(s32[8192]{0:T(1024)} %param.7) | copy-start | bytes 98308
  13.7 5.7 %collective-permute-start.8 = (s16[128,128]{1,0:T(8,128)(2,1)S(1)}, s16[128,128]{1,0:T(8,128)(2,1)S(1)}, u32[]{:S(2)}, u32[]{:S(2)}) collective-permute-start(s16[128,128]{1,0:T(8,128)(2,1)S(1)} %encode_terms.1.refs_0_), channel_id=1, source_target_pairs={{0,64},{4,68},{8,72},{12,76},{16,80},{20,84},{24,88},{28,92},{32,9... | collective-permute-start | bytes 98312 | tf_op jit(solution)/shard_map/ppermute | solution.py:33
  17.1 5.5 %collective-permute-start.1 = (f32[128,128]{1,0:T(8,128)S(1)}, f32[128,128]{1,0:T(8,128)S(1)}, u32[]{:S(2)}, u32[]{:S(2)}) collective-permute-start(f32[128,128]{1,0:T(8,128)S(1)} %join.7), channel_id=1, source_target_pairs={{4,0},{8,4},{12,8},{16,12},{20,16},{24,20},{28,24},{32,28},{36,32}... | collective-permute-start | bytes 196616 | tf_op jit(solution)/shard_map/ppermute | solution.py:280
  19.5 8.6 %collective-permute-start = (f32[128,128]{1,0:T(8,128)S(1)}, f32[128,128]{1,0:T(8,128)S(1)}, u32[]{:S(2)}, u32[]{:S(2)}) collective-permute-start(f32[128,128]{1,0:T(8,128)S(1)} %join.7), channel_id=1, source_target_pairs={{0,4},{4,8},{8,12},{12,16},{16,20},{20,24},{24,28},{28,32},{32,36}... | collective-permute-start | bytes 196616 | tf_op jit(solution)/shard_map/ppermute | solution.py:280
  22.6 8.9 %collective-permute-start.9 = (s16[256,128]{1,0:T(8,128)(2,1)S(1)}, s16[256,128]{1,0:T(8,128)(2,1)S(1)}, u32[]{:S(2)}, u32[]{:S(2)}) collective-permute-start(s16[256,128]{1,0:T(8,128)(2,1)S(1)} %join.8.refs_0_), channel_id=1, source_target_pairs={{0,128},{4,132},{8,136},{12,140},{16,144},{20,148},{24,152},{28,15... | collective-permute-start | bytes 196616 | tf_op jit(solution)/shard_map/ppermute | solution.py:33
  31.5 7.4 %collective-permute-start.10 = (s16[512,128]{1,0:T(8,128)(2,1)S(1)}, s16[512,128]{1,0:T(8,128)(2,1)S(1)}, u32[]{:S(2)}, u32[]{:S(2)}) collective-permute-start(s16[512,128]{1,0:T(8,128)(2,1)S(1)} %join.9.refs_0_), channel_id=1, source_target_pairs={{0,32},{4,36},{8,40},{12,44},{16,48},{20,52},{24,56},{28,60},{32,0... | collective-permute-start | bytes 393224 | tf_op jit(solution)/shard_map/ppermute | solution.py:33
  35.2 2.2 %copy-start = (bf16[8192,256]{1,0:T(8,128)(2,1)S(1)}, bf16[8192,256]{1,0:T(8,128)(2,1)}, u32[]{:S(2)}) copy-start(bf16[8192,256]{1,0:T(8,128)(2,1)} %traces.1) | copy-start | bytes 12582916
  37.4 7.6 %copy-start.8 = (bf16[1024,256]{1,0:T(8,128)(2,1)S(1)}, bf16[1024,256]{1,0:T(8,128)(2,1)}, u32[]{:S(2)}) copy-start(bf16[1024,256]{1,0:T(8,128)(2,1)} %copy-done.7) | copy-start | bytes 1572868
  39.7 9.9 %collective-permute-start.11 = (s16[1024,128]{1,0:T(8,128)(2,1)S(1)}, s16[1024,128]{1,0:T(8,128)(2,1)S(1)}, u32[]{:S(2)}, u32[]{:S(2)}) collective-permute-start(s16[1024,128]{1,0:T(8,128)(2,1)S(1)} %join.10.refs_0_), channel_id=1, source_target_pairs={{0,8},{4,12},{8,0},{12,4},{16,24},{20,28},{24,16},{28,20},{32,40},... | collective-permute-start | bytes 786440 | tf_op jit(solution)/shard_map/ppermute | solution.py:33
  41.0 18.8 %collective-permute-start.13 = (bf16[1024,256]{1,0:T(8,128)(2,1)S(1)}, bf16[1024,256]{1,0:T(8,128)(2,1)S(1)}, u32[]{:S(2)}, u32[]{:S(2)}) collective-permute-start(bf16[1024,256]{1,0:T(8,128)(2,1)S(1)} %get-tuple-element.31), channel_id=1, source_target_pairs={{0,1},{1,2},{2,3},{3,0},{4,5},{5,6},{6,7},{7,4},{8,9},{9,10},{10,1... | collective-permute-start | bytes 1572872 | tf_op jit(solution)/shard_map/ppermute | solution.py:37
  41.1 18.7 %collective-permute-start.14 = (bf16[1024,256]{1,0:T(8,128)(2,1)S(1)}, bf16[1024,256]{1,0:T(8,128)(2,1)S(1)}, u32[]{:S(2)}, u32[]{:S(2)}) collective-permute-start(bf16[1024,256]{1,0:T(8,128)(2,1)S(1)} %get-tuple-element.32), channel_id=1, source_target_pairs={{0,2},{1,3},{2,0},{3,1},{4,6},{5,7},{6,4},{7,5},{8,10},{9,11},{10,... | collective-permute-start | bytes 1572872 | tf_op jit(solution)/shard_map/ppermute | solution.py:37
  43.6 23.5 %collective-permute-start.15 = (bf16[1024,256]{1,0:T(8,128)(2,1)S(1)}, bf16[1024,256]{1,0:T(8,128)(2,1)S(1)}, u32[]{:S(2)}, u32[]{:S(2)}) collective-permute-start(bf16[1024,256]{1,0:T(8,128)(2,1)S(1)} %get-tuple-element.33), channel_id=1, source_target_pairs={{0,3},{1,0},{2,1},{3,2},{4,7},{5,4},{6,5},{7,6},{8,11},{9,8},{10,9... | collective-permute-start | bytes 1572872 | tf_op jit(solution)/shard_map/ppermute | solution.py:37
  49.6 2.0 %copy-start.17 = (s16[1024,128]{1,0:T(8,128)(2,1)}, s16[1024,128]{1,0:T(8,128)(2,1)S(1)}, u32[]{:S(2)}) copy-start(s16[1024,128]{1,0:T(8,128)(2,1)S(1)} %get-tuple-element.29) | copy-start | bytes 786436
  49.6 17.5 %collective-permute-start.12 = (s16[2048,128]{1,0:T(8,128)(2,1)S(1)}, s16[2048,128]{1,0:T(8,128)(2,1)S(1)}, u32[]{:S(2)}, u32[]{:S(2)}) collective-permute-start(s16[2048,128]{1,0:T(8,128)(2,1)S(1)} %join.11.refs_0_), channel_id=1, source_target_pairs={{0,16},{4,20},{8,24},{12,28},{16,0},{20,4},{24,8},{28,12},{32,48},... | collective-permute-start | bytes 1572872 | tf_op jit(solution)/shard_map/ppermute | solution.py:33
  59.8 7.4 %copy-start.1 = (f32[4096,128]{1,0:T(8,128)}, f32[4096,128]{1,0:T(8,128)S(1)}, u32[]{:S(2)}) copy-start(f32[4096,128]{1,0:T(8,128)S(1)} %get-tuple-element.25.refs_2_) | copy-start | bytes 6291460
  59.8 7.4 %copy-start.3 = (f32[4096,128]{1,0:T(8,128)}, f32[4096,128]{1,0:T(8,128)S(1)}, u32[]{:S(2)}) copy-start(f32[4096,128]{1,0:T(8,128)S(1)} %get-tuple-element.35.refs_2_) | copy-start | bytes 6291460
  59.8 7.4 %copy-start.9 = (bf16[1024,256]{1,0:T(8,128)(2,1)}, bf16[1024,256]{1,0:T(8,128)(2,1)S(1)}, u32[]{:S(2)}) copy-start(bf16[1024,256]{1,0:T(8,128)(2,1)S(1)} %collective-permute-done.13.refs_4_.b1) | copy-start | bytes 1572868
  59.8 7.4 %copy-start.11 = (bf16[1024,256]{1,0:T(8,128)(2,1)}, bf16[1024,256]{1,0:T(8,128)(2,1)S(1)}, u32[]{:S(2)}) copy-start(bf16[1024,256]{1,0:T(8,128)(2,1)S(1)} %collective-permute-done.14.refs_5_.b2) | copy-start | bytes 1572868
  67.9 17.6 %collective-permute-start.16 = (s16[4096,128]{1,0:T(8,128)(2,1)S(1)}, s16[4096,128]{1,0:T(8,128)(2,1)}, u32[]{:S(2)}, u32[]{:S(2)}) collective-permute-start(s16[4096,128]{1,0:T(8,128)(2,1)S(1)} %join.12.refs_7_), channel_id=1, source_target_pairs={{0,4},{4,0},{8,12},{12,8},{16,20},{20,16},{24,28},{28,24},{32,36},... | collective-permute-start | bytes 3145736 | tf_op jit(solution)/shard_map/ppermute | solution.py:33
  67.9 12.1 %collective-permute-start.5 = (s16[1024,128]{1,0:T(8,128)(2,1)}, s16[1024,128]{1,0:T(8,128)(2,1)}, u32[]{:S(2)}, u32[]{:S(2)}) collective-permute-start(s16[1024,128]{1,0:T(8,128)(2,1)} %get-tuple-element.27), channel_id=1, source_target_pairs={{0,1},{1,2},{2,3},{3,0},{4,5},{5,6},{6,7},{7,4},{8,9},{9,10},{10,1... | collective-permute-start | bytes 786440 | tf_op jit(solution)/shard_map/ppermute | solution.py:37
  68.5 14.4 %collective-permute-start.6 = (s16[1024,128]{1,0:T(8,128)(2,1)}, s16[1024,128]{1,0:T(8,128)(2,1)}, u32[]{:S(2)}, u32[]{:S(2)}) collective-permute-start(s16[1024,128]{1,0:T(8,128)(2,1)} %get-tuple-element.28), channel_id=1, source_target_pairs={{0,2},{1,3},{2,0},{3,1},{4,6},{5,7},{6,4},{7,5},{8,10},{9,11},{10,... | collective-permute-start | bytes 786440 | tf_op jit(solution)/shard_map/ppermute | solution.py:37
  70.5 15.0 %copy-start.2 = (f32[4096,128]{1,0:T(8,128)S(1)}, f32[4096,128]{1,0:T(8,128)}, u32[]{:S(2)}) copy-start(f32[4096,128]{1,0:T(8,128)} %copy-done.1) | copy-start | bytes 6291460
  70.5 15.0 %collective-permute-start.7 = (s16[1024,128]{1,0:T(8,128)(2,1)}, s16[1024,128]{1,0:T(8,128)(2,1)S(1)}, u32[]{:S(2)}, u32[]{:S(2)}) collective-permute-start(s16[1024,128]{1,0:T(8,128)(2,1)} %copy-done.17), channel_id=1, source_target_pairs={{0,3},{1,0},{2,1},{3,2},{4,7},{5,4},{6,5},{7,6},{8,11},{9,8},{10,9... | collective-permute-start | bytes 786440 | tf_op jit(solution)/shard_map/ppermute | solution.py:37
  72.7 1.0 copy-start.6
  73.8 1.0 copy-start.10
  79.9 15.8 %collective-permute-start.17 = (s16[1024,128]{1,0:T(8,128)(2,1)S(1)}, s16[1024,128]{1,0:T(8,128)(2,1)S(1)}, u32[]{:S(2)}, u32[]{:S(2)}) collective-permute-start(s16[1024,128]{1,0:T(8,128)(2,1)S(1)} %get-tuple-element.37), channel_id=1, source_target_pairs={{0,1},{1,2},{2,3},{3,0},{4,5},{5,6},{6,7},{7,4},{8,9},{9,10},{10,1... | collective-permute-start | bytes 786440 | tf_op jit(solution)/shard_map/ppermute | solution.py:37
  80.0 15.7 %collective-permute-start.18 = (s16[1024,128]{1,0:T(8,128)(2,1)S(1)}, s16[1024,128]{1,0:T(8,128)(2,1)S(1)}, u32[]{:S(2)}, u32[]{:S(2)}) collective-permute-start(s16[1024,128]{1,0:T(8,128)(2,1)S(1)} %get-tuple-element.38), channel_id=1, source_target_pairs={{0,2},{1,3},{2,0},{3,1},{4,6},{5,7},{6,4},{7,5},{8,10},{9,11},{10,... | collective-permute-start | bytes 786440 | tf_op jit(solution)/shard_map/ppermute | solution.py:37
  82.9 12.9 %collective-permute-start.19 = (s16[1024,128]{1,0:T(8,128)(2,1)S(1)}, s16[1024,128]{1,0:T(8,128)(2,1)S(1)}, u32[]{:S(2)}, u32[]{:S(2)}) collective-permute-start(s16[1024,128]{1,0:T(8,128)(2,1)S(1)} %get-tuple-element.39), channel_id=1, source_target_pairs={{0,3},{1,0},{2,1},{3,2},{4,7},{5,4},{6,5},{7,6},{8,11},{9,8},{10,9... | collective-permute-start | bytes 786440 | tf_op jit(solution)/shard_map/ppermute | solution.py:37
  85.5 10.3 %copy-start.4 = (f32[4096,128]{1,0:T(8,128)S(1)}, f32[4096,128]{1,0:T(8,128)}, u32[]{:S(2)}) copy-start(f32[4096,128]{1,0:T(8,128)} %copy-done.3) | copy-start | bytes 6291460
  105.1 4.2 %collective-permute-start.22 = (f32[4096,128]{1,0:T(8,128)S(1)}, f32[4096,128]{1,0:T(8,128)S(1)}, u32[]{:S(2)}, u32[]{:S(2)}) collective-permute-start(f32[4096,128]{1,0:T(8,128)S(1)} %get-tuple-element.47), channel_id=1, source_target_pairs={{0,4},{4,0},{8,12},{12,8},{16,20},{20,16},{24,28},{28,24},{32,36},... | collective-permute-start | bytes 6291464 | tf_op jit(solution)/shard_map/ppermute | solution.py:33
  110.0 14.1 %collective-permute-start.23 = (f16[512,128]{1,0:T(8,128)(2,1)S(1)}, f16[512,128]{1,0:T(8,128)(2,1)S(1)}, u32[]{:S(2)}, u32[]{:S(2)}) collective-permute-start(f16[512,128]{1,0:T(8,128)(2,1)S(1)} %get-tuple-element.52), channel_id=1, source_target_pairs={{0,8},{4,12},{8,0},{12,4},{16,24},{20,28},{24,16},{28,20},{32,40},... | collective-permute-start | bytes 393224 | tf_op jit(solution)/shard_map/ppermute | solution.py:33
  110.5 9.5 %collective-permute-start.28 = (f16[512,128]{1,0:T(8,128)(2,1)S(1)}, f16[512,128]{1,0:T(8,128)(2,1)S(1)}, u32[]{:S(2)}, u32[]{:S(2)}) collective-permute-start(f16[512,128]{1,0:T(8,128)(2,1)S(1)} %get-tuple-element.53), channel_id=1, source_target_pairs={{0,16},{4,20},{8,24},{12,28},{16,0},{20,4},{24,8},{28,12},{32,48},... | collective-permute-start | bytes 393224 | tf_op jit(solution)/shard_map/ppermute | solution.py:33
  112.9 9.2 %collective-permute-start.27 = (f16[512,128]{1,0:T(8,128)(2,1)S(1)}, f16[512,128]{1,0:T(8,128)(2,1)S(1)}, u32[]{:S(2)}, u32[]{:S(2)}) collective-permute-start(f16[512,128]{1,0:T(8,128)(2,1)S(1)} %get-tuple-element.54), channel_id=1, source_target_pairs={{0,24},{4,28},{8,16},{12,20},{16,8},{20,12},{24,0},{28,4},{32,56},... | collective-permute-start | bytes 393224 | tf_op jit(solution)/shard_map/ppermute | solution.py:33
  114.8 7.3 %collective-permute-start.26 = (f16[512,128]{1,0:T(8,128)(2,1)S(1)}, f16[512,128]{1,0:T(8,128)(2,1)S(1)}, u32[]{:S(2)}, u32[]{:S(2)}) collective-permute-start(f16[512,128]{1,0:T(8,128)(2,1)S(1)} %get-tuple-element.55), channel_id=1, source_target_pairs={{0,8},{4,12},{8,0},{12,4},{16,24},{20,28},{24,16},{28,20},{32,40},... | collective-permute-start | bytes 393224 | tf_op jit(solution)/shard_map/ppermute | solution.py:33
  114.8 10.4 %collective-permute-start.25 = (f16[512,128]{1,0:T(8,128)(2,1)S(1)}, f16[512,128]{1,0:T(8,128)(2,1)S(1)}, u32[]{:S(2)}, u32[]{:S(2)}) collective-permute-start(f16[512,128]{1,0:T(8,128)(2,1)S(1)} %get-tuple-element.56), channel_id=1, source_target_pairs={{0,16},{4,20},{8,24},{12,28},{16,0},{20,4},{24,8},{28,12},{32,48},... | collective-permute-start | bytes 393224 | tf_op jit(solution)/shard_map/ppermute | solution.py:33
  120.1 7.8 %collective-permute-start.24 = (f16[512,128]{1,0:T(8,128)(2,1)S(1)}, f16[512,128]{1,0:T(8,128)(2,1)S(1)}, u32[]{:S(2)}, u32[]{:S(2)}) collective-permute-start(f16[512,128]{1,0:T(8,128)(2,1)S(1)} %get-tuple-element.57), channel_id=1, source_target_pairs={{0,24},{4,28},{8,16},{12,20},{16,8},{20,12},{24,0},{28,4},{32,56},... | collective-permute-start | bytes 393224 | tf_op jit(solution)/shard_map/ppermute | solution.py:33
  122.3 5.6 %collective-permute-start.29 = (f16[512,128]{1,0:T(8,128)(2,1)S(1)}, f16[512,128]{1,0:T(8,128)(2,1)S(1)}, u32[]{:S(2)}, u32[]{:S(2)}) collective-permute-start(f16[512,128]{1,0:T(8,128)(2,1)S(1)} %multiply_convert_fusion.1), channel_id=1, source_target_pairs={{0,32},{4,36},{8,40},{12,44},{16,48},{20,52},{24,56},{28,60},{32,0... | collective-permute-start | bytes 393224 | tf_op jit(solution)/shard_map/ppermute | solution.py:33
  128.0 6.6 %collective-permute-start.30 = (f16[2,128,128]{2,1,0:T(8,128)(2,1)S(1)}, f16[2,128,128]{2,1,0:T(8,128)(2,1)S(1)}, u32[]{:S(2)}, u32[]{:S(2)}) collective-permute-start(f16[2,128,128]{2,1,0:T(8,128)(2,1)S(1)} %fusion.5), channel_id=1, source_target_pairs={{0,64},{4,68},{8,72},{12,76},{16,80},{20,84},{24,88},{28,92},{32,9... | collective-permute-start | bytes 196616 | tf_op jit(solution)/shard_map/ppermute | solution.py:33
  131.3 13.8 %collective-permute-start.20 = (f32[128,128]{1,0:T(8,128)S(1)}, f32[128,128]{1,0:T(8,128)S(1)}, u32[]{:S(2)}, u32[]{:S(2)}) collective-permute-start(f32[128,128]{1,0:T(8,128)S(1)} %get-tuple-element.58), channel_id=1, source_target_pairs={{0,4},{4,8},{8,12},{12,16},{16,20},{20,24},{24,28},{28,32},{32,36}... | collective-permute-start | bytes 196616 | tf_op jit(solution)/shard_map/ppermute | solution.py:280
  132.6 12.5 %collective-permute-start.21 = (f32[128,128]{1,0:T(8,128)S(1)}, f32[128,128]{1,0:T(8,128)S(1)}, u32[]{:S(2)}, u32[]{:S(2)}) collective-permute-start(f32[128,128]{1,0:T(8,128)S(1)} %get-tuple-element.59), channel_id=1, source_target_pairs={{4,0},{8,4},{12,8},{16,12},{20,16},{24,20},{28,24},{32,28},{36,32}... | collective-permute-start | bytes 196616 | tf_op jit(solution)/shard_map/ppermute | solution.py:280
  134.7 12.3 %collective-permute-start.31 = (f16[128,128]{1,0:T(8,128)(2,1)S(1)}, f16[128,128]{1,0:T(8,128)(2,1)S(1)}, u32[]{:S(2)}, u32[]{:S(2)}) collective-permute-start(f16[128,128]{1,0:T(8,128)(2,1)S(1)} %fusion.24), channel_id=1, source_target_pairs={{0,128},{4,132},{8,136},{12,140},{16,144},{20,148},{24,152},{28,15... | collective-permute-start | bytes 98312 | tf_op jit(solution)/shard_map/ppermute | solution.py:33
  (4 other events, 3.7 us)

commit v15 on v14

--- a/solution.py
+++ b/solution.py
@@ -345,9 +345,10 @@
         come = [swap(sent[k, h], 0, k, 0).astype(jnp.float32) for k in (1, 3, 2)]
         mine = join([sums[0, h]], (shots,)) if h else sums[0, h]
         halves[h] = mine + (come[0] + come[1] + come[2]) * (1.0 / SUM_SCALE)
+    shots = join([shots], (halves[1],))
     shot_sums = shots[block : 2 * block] + neighbour(shots[2 * block :], 1) + neighbour(shots[:block], -1)
     sent = (halves[1] * SUM_SCALE).astype(jnp.float16)
-    sums = halves[0] + swap(sent, 1, 0, 0).astype(jnp.float32) * (1.0 / SUM_SCALE)
+    sums = join(halves[:1], (shot_sums,)) + swap(sent, 1, 0, 0).astype(jnp.float32) * (1.0 / SUM_SCALE)
     sums = sums.reshape(2, 2, block, width)
     sent = (sums[:, 1] * SUM_SCALE).astype(jnp.float16)
     sums = sums[:, 0] + swap(sent, 2, 0, 0).astype(jnp.float32) * (1.0 / SUM_SCALE)

time: 148 us -> 152 us (1.027)
  waiting for transfers between devices: 22.5 us -> 24.8 us
  starting transfers between devices: 67 us -> 69 us
    ppermute x16, waiting for transfers between devices: 15.2 us -> 17.5 us  [swap(): lax.ppermute(value, 'tr', [(tr_of(z, x, c), tr_of(z ^ dz, x ^ dx, c ^ dc)...]
    ppermute x16, starting transfers between devices: 41.1 us -> 43.1 us  [swap(): lax.ppermute(value, 'tr', [(tr_of(z, x, c), tr_of(z ^ dz, x ^ dx, c ^ dc)...]
    unnamed x45 -> x47, local copies, waits for them, and re-layouts: 7.92 us -> 7.94 us
  transfers between devices with their start and end apart: 32 -> 32, of which waited for: 10 -> 9; matrix products, arithmetic and copies ran while one was open for 1% -> 0% of each run, Pallas kernels for 23% -> 22%
where the time goes in v15:
time: 152 us; the launch traced here: 151 us
  starting transfers between devices  69 us (45%)
  Pallas kernels  42.6 us (28%)
  waiting for transfers between devices  24.8 us (16%)
  local copies, waits for them, and re-layouts  11.1 us (7%)
  between operations  2.04 us (1%)
  other arithmetic  1.65 us (1%)
    ppermute x16, starting transfers between devices, swap(): lax.ppermute(value, 'tr', [(tr_of(z, x, c), tr_of(z ^ dz, x ^ dx, c ^ dc)...  43.1 us
    pallas_call x2, Pallas kernels, sum_receivers(): pl.pallas_call(body, in_specs=[sm, sm] + [vm] * (1 + parts + len(given)),...  19.4 us
    ppermute x12, starting transfers between devices, send_y(): return lax.ppermute(value, 'fq', [(i, (i + k) % NY) for i in range(NY)])  19 us
    ppermute x16, waiting for transfers between devices, swap(): lax.ppermute(value, 'tr', [(tr_of(z, x, c), tr_of(z ^ dz, x ^ dx, c ^ dc)...  17.5 us
    pallas_call x1, Pallas kernels, gather_shots(): pl.pallas_call(body, in_specs=[sm, vm], out_specs=[vm] * len(sizes), out_...  8.11 us
    unnamed x47, local copies, waits for them, and re-layouts  7.94 us
    pallas_call x2, Pallas kernels, spectra(): pl.pallas_call(body, grid=(rows // tile,), in_specs=[pl.BlockSpec((tile,...  7.63 us
    ppermute x12, waiting for transfers between devices, send_y(): return lax.ppermute(value, 'fq', [(i, (i + k) % NY) for i in range(NY)])  7.29 us
  transfers between devices with their start and end apart: 32, of which 9 were waited for; matrix products, arithmetic and copies ran while one was open for 0% of the time, Pallas kernels for 22%

profile of v15, /device:TPU:8, one launch (start us, length us, event | category | flops | bytes accessed | tf_op | source)
XLA Modules:
  0.0 151.2 jit_solution(3823287734259744220)
XLA Ops:
  0.7 2.7 %constant_dynamic-slice_fusion = (bf16[1024,256]{1,0:T(8,128)(2,1)}, bf16[1024,256]{1,0:T(8,128)(2,1)}, bf16[1024,256]{1,0:T(8,128)(2,1)}, bf16[1024,256]{1,0:T(8,128)(2,1)S(1)}) fusion(bf16[8192,256]{1,0:T(8,128)(2,1)} %traces.1, s32[]{:T(128)S(6)} %select_n.159, s32[]{:T(128)S(6)} %select_n.157, s32[]{:T(128)S(6)} %select_n.155, s32[]{:T(128)S(6)} %select_n.153), kind=kLoop, calls=%fused_computation.82 | loop fusion | bytes 4194320 | tf_op jit(solution)/shard_map/dynamic_slice | solution.py:296
  3.4 2.2 %collective-permute-start.4 = (bf16[1024,256]{1,0:T(8,128)(2,1)}, bf16[1024,256]{1,0:T(8,128)(2,1)S(1)}, u32[]{:S(2)}, u32[]{:S(2)}) collective-permute-start(bf16[1024,256]{1,0:T(8,128)(2,1)} %get-tuple-element.50), channel_id=1, source_target_pairs={{0,3},{1,0},{2,1},{3,2},{4,7},{5,4},{6,5},{7,6},{8,11},{9,8},{10,9... | collective-permute-start | bytes 1572872 | tf_op jit(solution)/shard_map/ppermute | solution.py:37
  5.6 0.9 collective-permute-start.3
  6.4 1.9 %collective-permute-start.2 = (bf16[1024,256]{1,0:T(8,128)(2,1)}, bf16[1024,256]{1,0:T(8,128)(2,1)}, u32[]{:S(2)}, u32[]{:S(2)}) collective-permute-start(bf16[1024,256]{1,0:T(8,128)(2,1)} %get-tuple-element.52), channel_id=1, source_target_pairs={{0,1},{1,2},{2,3},{3,0},{4,5},{5,6},{6,7},{7,4},{8,9},{9,10},{10,1... | collective-permute-start | bytes 1572872 | tf_op jit(solution)/shard_map/ppermute | solution.py:37
  8.3 5.3 %make_table.1.refs_1_.t.refs_0_ = bf16[1024,1024]{1,0:T(8,128)(2,1)S(1)} custom-call(s32[1]{0:T(128)} %bitcast.10.y_ref, bf16[1024,256]{1,0:T(8,128)(2,1)S(1)} %get-tuple-element.53.refs_0_.b0), custom_call_target="tpu_custom_call" | custom-call | flops 1073741824 | bytes 33554432 | tf_op jit(solution)/shard_map/make_table/pallas_call | solution.py:64
  13.7 3.4 %collective-permute-start.8 = (s16[128,128]{1,0:T(8,128)(2,1)S(1)}, s16[128,128]{1,0:T(8,128)(2,1)S(1)}, u32[]{:S(2)}, u32[]{:S(2)}) collective-permute-start(s16[128,128]{1,0:T(8,128)(2,1)S(1)} %encode_terms.1.refs_0_), channel_id=1, source_target_pairs={{0,64},{4,68},{8,72},{12,76},{16,80},{20,84},{24,88},{28,92},{32,9... | collective-permute-start | bytes 98312 | tf_op jit(solution)/shard_map/ppermute | solution.py:33
  17.1 1.3 collective-permute-start.1
  19.5 3.0 %collective-permute-start = (f32[128,128]{1,0:T(8,128)S(1)}, f32[128,128]{1,0:T(8,128)S(1)}, u32[]{:S(2)}, u32[]{:S(2)}) collective-permute-start(f32[128,128]{1,0:T(8,128)S(1)} %join.9), channel_id=1, source_target_pairs={{0,4},{4,8},{8,12},{12,16},{16,20},{20,24},{24,28},{28,32},{32,36}... | collective-permute-start | bytes 196616 | tf_op jit(solution)/shard_map/ppermute | solution.py:280
  22.6 5.5 %collective-permute-start.9 = (s16[256,128]{1,0:T(8,128)(2,1)S(1)}, s16[256,128]{1,0:T(8,128)(2,1)S(1)}, u32[]{:S(2)}, u32[]{:S(2)}) collective-permute-start(s16[256,128]{1,0:T(8,128)(2,1)S(1)} %join.10.refs_0_), channel_id=1, source_target_pairs={{0,128},{4,132},{8,136},{12,140},{16,144},{20,148},{24,152},{28,15... | collective-permute-start | bytes 196616 | tf_op jit(solution)/shard_map/ppermute | solution.py:33
  28.1 3.4 %collective-permute-done.9.refs_1_ = s16[256,128]{1,0:T(8,128)(2,1)S(1)} collective-permute-done((s16[256,128]{1,0:T(8,128)(2,1)S(1)}, s16[256,128]{1,0:T(8,128)(2,1)S(1)}, u32[]{:S(2)}, u32[]{:S(2)}) %collective-permute-start.9) | collective-permute-done | bytes 65568 | tf_op jit(solution)/shard_map/ppermute | solution.py:33
  31.5 3.7 %collective-permute-start.10 = (s16[512,128]{1,0:T(8,128)(2,1)S(1)}, s16[512,128]{1,0:T(8,128)(2,1)S(1)}, u32[]{:S(2)}, u32[]{:S(2)}) collective-permute-start(s16[512,128]{1,0:T(8,128)(2,1)S(1)} %join.11.refs_0_), channel_id=1, source_target_pairs={{0,32},{4,36},{8,40},{12,44},{16,48},{20,52},{24,56},{28,60},{32,0... | collective-permute-start | bytes 393224 | tf_op jit(solution)/shard_map/ppermute | solution.py:33
  35.1 2.2 %copy-done = bf16[8192,256]{1,0:T(8,128)(2,1)S(1)} copy-done((bf16[8192,256]{1,0:T(8,128)(2,1)S(1)}, bf16[8192,256]{1,0:T(8,128)(2,1)}, u32[]{:S(2)}) %copy-start) | copy-done | bytes 4194328
  37.5 1.3 collective-permute-done.10.refs_1_
  38.9 0.8 copy-done.5
  39.7 1.2 collective-permute-start.11
  41.1 2.4 %collective-permute-start.14 = (bf16[1024,256]{1,0:T(8,128)(2,1)S(1)}, bf16[1024,256]{1,0:T(8,128)(2,1)S(1)}, u32[]{:S(2)}, u32[]{:S(2)}) collective-permute-start(bf16[1024,256]{1,0:T(8,128)(2,1)S(1)} %get-tuple-element.32), channel_id=1, source_target_pairs={{0,2},{1,3},{2,0},{3,1},{4,6},{5,7},{6,4},{7,5},{8,10},{9,11},{10,... | collective-permute-start | bytes 1572872 | tf_op jit(solution)/shard_map/ppermute | solution.py:37
  43.5 1.4 collective-permute-start.15
  44.9 4.6 %spectra.2 = (s16[1024,128]{1,0:T(8,128)(2,1)S(1)}, s16[1024,128]{1,0:T(8,128)(2,1)}, s16[1024,128]{1,0:T(8,128)(2,1)}, s16[1024,128]{1,0:T(8,128)(2,1)S(1)}) custom-call(bf16[1024,256]{1,0:T(8,128)(2,1)S(1)} %copy-done.8, bf16[1024,256]{1,0:T(8,128)(2,1)} %collective-permute-done.2.b1.refs_2_.refs_0_, ...), custom_call_target="tpu_custom_call" | custom-call | flops 1000 | bytes 1000 | tf_op jit(solution)/shard_map/spectra/pallas_call | solution.py:157
  49.6 2.0 %collective-permute-start.12 = (s16[2048,128]{1,0:T(8,128)(2,1)S(1)}, s16[2048,128]{1,0:T(8,128)(2,1)S(1)}, u32[]{:S(2)}, u32[]{:S(2)}) collective-permute-start(s16[2048,128]{1,0:T(8,128)(2,1)S(1)} %join.13.refs_0_), channel_id=1, source_target_pairs={{0,16},{4,20},{8,24},{12,28},{16,0},{20,4},{24,8},{28,12},{32,48},... | collective-permute-start | bytes 1572872 | tf_op jit(solution)/shard_map/ppermute | solution.py:33
  51.6 8.1 %gather_shots.1 = (f32[4096,128]{1,0:T(8,128)S(1)}, f32[4096,128]{1,0:T(8,128)S(1)}) custom-call(s32[8192]{0:T(1024)S(1)} %bitcast_dynamic-update-slice_fusion.shot_at, f32[384,128]{1,0:T(8,128)S(1)} %pad_maximum_fusion.shot.refs_5_), custom_call_target="tpu_custom_call" | custom-call | flops 1000 | bytes 1000 | tf_op jit(solution)/shard_map/gather_shots/pallas_call | solution.py:186
  59.8 7.3 %collective-permute-done.15.refs_6_.b3 = bf16[1024,256]{1,0:T(8,128)(2,1)S(1)} collective-permute-done((bf16[1024,256]{1,0:T(8,128)(2,1)S(1)}, bf16[1024,256]{1,0:T(8,128)(2,1)S(1)}, u32[]{:S(2)}, u32[]{:S(2)}) %collective-permute-start.15) | collective-permute-done | bytes 524320 | tf_op jit(solution)/shard_map/ppermute | solution.py:37
  67.2 0.7 copy-done.13
  68.5 1.9 %collective-permute-start.6 = (s16[1024,128]{1,0:T(8,128)(2,1)}, s16[1024,128]{1,0:T(8,128)(2,1)}, u32[]{:S(2)}, u32[]{:S(2)}) collective-permute-start(s16[1024,128]{1,0:T(8,128)(2,1)} %get-tuple-element.28), channel_id=1, source_target_pairs={{0,2},{1,3},{2,0},{3,1},{4,6},{5,7},{6,4},{7,5},{8,10},{9,11},{10,... | collective-permute-start | bytes 786440 | tf_op jit(solution)/shard_map/ppermute | solution.py:37
  70.5 2.3 %collective-permute-start.7 = (s16[1024,128]{1,0:T(8,128)(2,1)}, s16[1024,128]{1,0:T(8,128)(2,1)S(1)}, u32[]{:S(2)}, u32[]{:S(2)}) collective-permute-start(s16[1024,128]{1,0:T(8,128)(2,1)} %copy-done.18), channel_id=1, source_target_pairs={{0,3},{1,0},{2,1},{3,2},{4,7},{5,4},{6,5},{7,6},{8,11},{9,8},{10,9... | collective-permute-start | bytes 786440 | tf_op jit(solution)/shard_map/ppermute | solution.py:37
  72.7 1.0 copy-done.6
  73.8 1.0 copy-done.10
  74.8 1.0 copy-done.12
  75.8 1.0 copy-done.14
  76.9 3.0 %spectra.3 = (s16[1024,128]{1,0:T(8,128)(2,1)S(1)}, s16[1024,128]{1,0:T(8,128)(2,1)S(1)}, s16[1024,128]{1,0:T(8,128)(2,1)S(1)}, s16[1024,128]{1,0:T(8,128)(2,1)S(1)}) custom-call(bf16[1024,256]{1,0:T(8,128)(2,1)S(1)} %copy-done.6, bf16[1024,256]{1,0:T(8,128)(2,1)S(1)} %copy-done.10, bf16[1024,256]{1,0:T(8,128)(2,1)S(1)} %copy-done.12, ...), custom_call_target="tpu_custom_call" | custom-call | flops 1000 | bytes 1000 | tf_op jit(solution)/shard_map/spectra/pallas_call | solution.py:157
  80.0 2.9 %collective-permute-start.18 = (s16[1024,128]{1,0:T(8,128)(2,1)S(1)}, s16[1024,128]{1,0:T(8,128)(2,1)S(1)}, u32[]{:S(2)}, u32[]{:S(2)}) collective-permute-start(s16[1024,128]{1,0:T(8,128)(2,1)S(1)} %get-tuple-element.38), channel_id=1, source_target_pairs={{0,2},{1,3},{2,0},{3,1},{4,6},{5,7},{6,4},{7,5},{8,10},{9,11},{10,... | collective-permute-start | bytes 786440 | tf_op jit(solution)/shard_map/ppermute | solution.py:37
  82.9 2.5 %collective-permute-start.19 = (s16[1024,128]{1,0:T(8,128)(2,1)S(1)}, s16[1024,128]{1,0:T(8,128)(2,1)S(1)}, u32[]{:S(2)}, u32[]{:S(2)}) collective-permute-start(s16[1024,128]{1,0:T(8,128)(2,1)S(1)} %get-tuple-element.39), channel_id=1, source_target_pairs={{0,3},{1,0},{2,1},{3,2},{4,7},{5,4},{6,5},{7,6},{8,11},{9,8},{10,9... | collective-permute-start | bytes 786440 | tf_op jit(solution)/shard_map/ppermute | solution.py:37
  85.5 10.1 %sum_receivers.2 = (f32[4096,128]{1,0:T(8,128)S(1)}, f32[8200,128]{1,0:T(8,128)S(1)}, f32[8200,128]{1,0:T(8,128)S(1)}, f32[8200,128]{1,0:T(8,128)S(1)}, f32[8200...) custom-call(s32[4096]{0:T(1024)S(1)} %bitcast.75, s32[4]{0:T(128)S(1)} %get-tuple-element.75.refs_1_, f32[4096,128]{1,0:T(8,128)S(1)} %copy-done.2, ...), custom_call_target="tpu_custom_call" | custom-call | flops 1000 | bytes 1000 | tf_op jit(solution)/shard_map/sum_receivers/pallas_call | solution.py:237
  95.6 9.3 %sum_receivers.3 = (f32[4096,128]{1,0:T(8,128)S(1)}, f32[8200,128]{1,0:T(8,128)S(1)}, f32[8200,128]{1,0:T(8,128)S(1)}, f32[8200,128]{1,0:T(8,128)S(1)}, f32[8200...) custom-call(s32[4096]{0:T(1024)S(1)} %bitcast.77, ...), custom_call_target="tpu_custom_call", output_to_operand_aliasing={{1}: (7, {}), {2}: (8, {}), {3}: (9, {}), {4}: (10, {}), {5... | custom-call | flops 1000 | bytes 1000 | tf_op jit(solution)/shard_map/sum_receivers/pallas_call | solution.py:237
  105.0 1.8 %sum_shots.1.refs_1_.refs_0_ = f32[384,128]{1,0:T(8,128)S(1)} custom-call(s32[1,8192]{1,0:T(1,128)S(1)} %bitcast.73, f32[4096,128]{1,0:T(8,128)S(1)} %get-tuple-element.34.refs_0_, f32[4096,128]{1,0:T(8,128)S(1)} %get-tuple-element.45.refs_1_), custom_call_target="tpu_custom_call" | custom-call | flops 1000 | bytes 1000 | tf_op jit(solution)/shard_map/sum_shots/pallas_call | solution.py:267
  106.8 2.3 %collective-permute-done.20 = f32[4096,128]{1,0:T(8,128)S(1)} collective-permute-done((f32[4096,128]{1,0:T(8,128)S(1)}, f32[4096,128]{1,0:T(8,128)S(1)}, u32[]{:S(2)}, u32[]{:S(2)}) %collective-permute-start.20) | collective-permute-done | bytes 2097184 | tf_op jit(solution)/shard_map/ppermute | solution.py:33
  110.2 2.8 %collective-permute-start.23 = (f16[512,128]{1,0:T(8,128)(2,1)S(1)}, f16[512,128]{1,0:T(8,128)(2,1)S(1)}, u32[]{:S(2)}, u32[]{:S(2)}) collective-permute-start(f16[512,128]{1,0:T(8,128)(2,1)S(1)} %get-tuple-element.57), channel_id=1, source_target_pairs={{0,16},{4,20},{8,24},{12,28},{16,0},{20,4},{24,8},{28,12},{32,48},... | collective-permute-start | bytes 393224 | tf_op jit(solution)/shard_map/ppermute | solution.py:33
  113.0 1.7 %collective-permute-start.22 = (f16[512,128]{1,0:T(8,128)(2,1)S(1)}, f16[512,128]{1,0:T(8,128)(2,1)S(1)}, u32[]{:S(2)}, u32[]{:S(2)}) collective-permute-start(f16[512,128]{1,0:T(8,128)(2,1)S(1)} %get-tuple-element.58), channel_id=1, source_target_pairs={{0,24},{4,28},{8,16},{12,20},{16,8},{20,12},{24,0},{28,4},{32,56},... | collective-permute-start | bytes 393224 | tf_op jit(solution)/shard_map/ppermute | solution.py:33
  114.7 3.1 %collective-permute-start.28 = (f16[512,128]{1,0:T(8,128)(2,1)S(1)}, f16[512,128]{1,0:T(8,128)(2,1)S(1)}, u32[]{:S(2)}, u32[]{:S(2)}) collective-permute-start(f16[512,128]{1,0:T(8,128)(2,1)S(1)} %get-tuple-element.55), channel_id=1, source_target_pairs={{0,16},{4,20},{8,24},{12,28},{16,0},{20,4},{24,8},{28,12},{32,48},... | collective-permute-start | bytes 393224 | tf_op jit(solution)/shard_map/ppermute | solution.py:33
  117.8 2.3 %collective-permute-done.23 = f16[512,128]{1,0:T(8,128)(2,1)S(1)} collective-permute-done((f16[512,128]{1,0:T(8,128)(2,1)S(1)}, f16[512,128]{1,0:T(8,128)(2,1)S(1)}, u32[]{:S(2)}, u32[]{:S(2)}) %collective-permute-start.23) | collective-permute-done | bytes 131104 | tf_op jit(solution)/shard_map/ppermute | solution.py:33
  120.1 1.7 %collective-permute-start.27 = (f16[512,128]{1,0:T(8,128)(2,1)S(1)}, f16[512,128]{1,0:T(8,128)(2,1)S(1)}, u32[]{:S(2)}, u32[]{:S(2)}) collective-permute-start(f16[512,128]{1,0:T(8,128)(2,1)S(1)} %get-tuple-element.56), channel_id=1, source_target_pairs={{0,24},{4,28},{8,16},{12,20},{16,8},{20,12},{24,0},{28,4},{32,56},... | collective-permute-start | bytes 393224 | tf_op jit(solution)/shard_map/ppermute | solution.py:33
  122.1 1.3 collective-permute-start.24
  123.4 1.3 collective-permute-start.25
  124.7 6.9 %collective-permute-start.29 = (f16[512,128]{1,0:T(8,128)(2,1)S(1)}, f16[512,128]{1,0:T(8,128)(2,1)S(1)}, u32[]{:S(2)}, u32[]{:S(2)}) collective-permute-start(f16[512,128]{1,0:T(8,128)(2,1)S(1)} %get-tuple-element.48), channel_id=1, source_target_pairs={{0,32},{4,36},{8,40},{12,44},{16,48},{20,52},{24,56},{28,60},{32,0... | collective-permute-start | bytes 393224 | tf_op jit(solution)/shard_map/ppermute | solution.py:33
  131.7 3.8 %collective-permute-done.29 = f16[512,128]{1,0:T(8,128)(2,1)S(1)} collective-permute-done((f16[512,128]{1,0:T(8,128)(2,1)S(1)}, f16[512,128]{1,0:T(8,128)(2,1)S(1)}, u32[]{:S(2)}, u32[]{:S(2)}) %collective-permute-start.29) | collective-permute-done | bytes 131104 | tf_op jit(solution)/shard_map/ppermute | solution.py:33
  135.6 3.5 %collective-permute-start.30 = (f16[2,128,128]{2,1,0:T(8,128)(2,1)S(1)}, f16[2,128,128]{2,1,0:T(8,128)(2,1)S(1)}, u32[]{:S(2)}, u32[]{:S(2)}) collective-permute-start(f16[2,128,128]{2,1,0:T(8,128)(2,1)S(1)} %fusion.4), channel_id=1, source_target_pairs={{0,64},{4,68},{8,72},{12,76},{16,80},{20,84},{24,88},{28,92},{32,9... | collective-permute-start | bytes 196616 | tf_op jit(solution)/shard_map/ppermute | solution.py:33
  139.1 2.2 %collective-permute-done.30 = f16[2,128,128]{2,1,0:T(8,128)(2,1)S(1)} collective-permute-done((f16[2,128,128]{2,1,0:T(8,128)(2,1)S(1)}, f16[2,128,128]{2,1,0:T(8,128)(2,1)S(1)}, u32[]{:S(2)}, u32[]{:S(2)}) %collective-permute-start.30) | collective-permute-done | bytes 65568 | tf_op jit(solution)/shard_map/ppermute | solution.py:33
  141.4 7.3 %collective-permute-start.31 = (f16[128,128]{1,0:T(8,128)(2,1)S(1)}, f16[128,128]{1,0:T(8,128)(2,1)S(1)}, u32[]{:S(2)}, u32[]{:S(2)}) collective-permute-start(f16[128,128]{1,0:T(8,128)(2,1)S(1)} %fusion.23), channel_id=1, source_target_pairs={{0,128},{4,132},{8,136},{12,140},{16,144},{20,148},{24,152},{28,15... | collective-permute-start | bytes 98312 | tf_op jit(solution)/shard_map/ppermute | solution.py:33
  148.7 1.9 %collective-permute-done.31 = f16[128,128]{1,0:T(8,128)(2,1)S(1)} collective-permute-done((f16[128,128]{1,0:T(8,128)(2,1)S(1)}, f16[128,128]{1,0:T(8,128)(2,1)S(1)}, u32[]{:S(2)}, u32[]{:S(2)}) %collective-permute-start.31) | collective-permute-done | bytes 32800 | tf_op jit(solution)/shard_map/ppermute | solution.py:33
  (108 shorter events, 4.0 us)
Async XLA Ops:
  3.4 10.3 %copy-start.7 = (bf16[1024,256]{1,0:T(8,128)(2,1)}, bf16[1024,256]{1,0:T(8,128)(2,1)S(1)}, u32[]{:S(2)}) copy-start(bf16[1024,256]{1,0:T(8,128)(2,1)S(1)} %get-tuple-element.53.refs_0_.b0) | copy-start | bytes 1572868
  3.4 10.2 %copy-start.16 = (f32[128,128]{1,0:T(8,128)S(1)}, f32[128,128]{1,0:T(8,128)}, u32[]{:S(2)}) copy-start(f32[128,128]{1,0:T(8,128)} %a.1) | copy-start | bytes 196612
  3.4 28.0 %collective-permute-start.4 = (bf16[1024,256]{1,0:T(8,128)(2,1)}, bf16[1024,256]{1,0:T(8,128)(2,1)S(1)}, u32[]{:S(2)}, u32[]{:S(2)}) collective-permute-start(bf16[1024,256]{1,0:T(8,128)(2,1)} %get-tuple-element.50), channel_id=1, source_target_pairs={{0,3},{1,0},{2,1},{3,2},{4,7},{5,4},{6,5},{7,6},{8,11},{9,8},{10,9... | collective-permute-start | bytes 1572872 | tf_op jit(solution)/shard_map/ppermute | solution.py:37
  5.6 25.9 %collective-permute-start.3 = (bf16[1024,256]{1,0:T(8,128)(2,1)}, bf16[1024,256]{1,0:T(8,128)(2,1)S(1)}, u32[]{:S(2)}, u32[]{:S(2)}) collective-permute-start(bf16[1024,256]{1,0:T(8,128)(2,1)} %get-tuple-element.51), channel_id=1, source_target_pairs={{0,2},{1,3},{2,0},{3,1},{4,6},{5,7},{6,4},{7,5},{8,10},{9,11},{10,... | collective-permute-start | bytes 1572872 | tf_op jit(solution)/shard_map/ppermute | solution.py:37
  6.4 25.0 %collective-permute-start.2 = (bf16[1024,256]{1,0:T(8,128)(2,1)}, bf16[1024,256]{1,0:T(8,128)(2,1)}, u32[]{:S(2)}, u32[]{:S(2)}) collective-permute-start(bf16[1024,256]{1,0:T(8,128)(2,1)} %get-tuple-element.52), channel_id=1, source_target_pairs={{0,1},{1,2},{2,3},{3,0},{4,5},{5,6},{6,7},{7,4},{8,9},{9,10},{10,1... | collective-permute-start | bytes 1572872 | tf_op jit(solution)/shard_map/ppermute | solution.py:37
  8.3 8.8 %copy-start.17 = (f32[128,128]{1,0:T(8,128)S(1)}, f32[128,128]{1,0:T(8,128)}, u32[]{:S(2)}) copy-start(f32[128,128]{1,0:T(8,128)} %refs_0_.1) | copy-start | bytes 196612
  13.6 5.5 %copy-start.19 = (s32[8192]{0:T(1024)S(1)}, s32[8192]{0:T(1024)}, u32[]{:S(2)}) copy-start(s32[8192]{0:T(1024)} %param.8) | copy-start | bytes 98308
  13.7 5.7 %copy-start.20 = (s32[8192]{0:T(1024)S(1)}, s32[8192]{0:T(1024)}, u32[]{:S(2)}) copy-start(s32[8192]{0:T(1024)} %param.7) | copy-start | bytes 98308
  13.7 5.7 %collective-permute-start.8 = (s16[128,128]{1,0:T(8,128)(2,1)S(1)}, s16[128,128]{1,0:T(8,128)(2,1)S(1)}, u32[]{:S(2)}, u32[]{:S(2)}) collective-permute-start(s16[128,128]{1,0:T(8,128)(2,1)S(1)} %encode_terms.1.refs_0_), channel_id=1, source_target_pairs={{0,64},{4,68},{8,72},{12,76},{16,80},{20,84},{24,88},{28,92},{32,9... | collective-permute-start | bytes 98312 | tf_op jit(solution)/shard_map/ppermute | solution.py:33
  17.1 5.5 %collective-permute-start.1 = (f32[128,128]{1,0:T(8,128)S(1)}, f32[128,128]{1,0:T(8,128)S(1)}, u32[]{:S(2)}, u32[]{:S(2)}) collective-permute-start(f32[128,128]{1,0:T(8,128)S(1)} %join.9), channel_id=1, source_target_pairs={{4,0},{8,4},{12,8},{16,12},{20,16},{24,20},{28,24},{32,28},{36,32}... | collective-permute-start | bytes 196616 | tf_op jit(solution)/shard_map/ppermute | solution.py:280
  19.5 8.6 %collective-permute-start = (f32[128,128]{1,0:T(8,128)S(1)}, f32[128,128]{1,0:T(8,128)S(1)}, u32[]{:S(2)}, u32[]{:S(2)}) collective-permute-start(f32[128,128]{1,0:T(8,128)S(1)} %join.9), channel_id=1, source_target_pairs={{0,4},{4,8},{8,12},{12,16},{16,20},{20,24},{24,28},{28,32},{32,36}... | collective-permute-start | bytes 196616 | tf_op jit(solution)/shard_map/ppermute | solution.py:280
  22.6 8.9 %collective-permute-start.9 = (s16[256,128]{1,0:T(8,128)(2,1)S(1)}, s16[256,128]{1,0:T(8,128)(2,1)S(1)}, u32[]{:S(2)}, u32[]{:S(2)}) collective-permute-start(s16[256,128]{1,0:T(8,128)(2,1)S(1)} %join.10.refs_0_), channel_id=1, source_target_pairs={{0,128},{4,132},{8,136},{12,140},{16,144},{20,148},{24,152},{28,15... | collective-permute-start | bytes 196616 | tf_op jit(solution)/shard_map/ppermute | solution.py:33
  31.5 7.4 %collective-permute-start.10 = (s16[512,128]{1,0:T(8,128)(2,1)S(1)}, s16[512,128]{1,0:T(8,128)(2,1)S(1)}, u32[]{:S(2)}, u32[]{:S(2)}) collective-permute-start(s16[512,128]{1,0:T(8,128)(2,1)S(1)} %join.11.refs_0_), channel_id=1, source_target_pairs={{0,32},{4,36},{8,40},{12,44},{16,48},{20,52},{24,56},{28,60},{32,0... | collective-permute-start | bytes 393224 | tf_op jit(solution)/shard_map/ppermute | solution.py:33
  35.1 2.2 %copy-start = (bf16[8192,256]{1,0:T(8,128)(2,1)S(1)}, bf16[8192,256]{1,0:T(8,128)(2,1)}, u32[]{:S(2)}) copy-start(bf16[8192,256]{1,0:T(8,128)(2,1)} %traces.1) | copy-start | bytes 12582916
  37.3 7.6 %copy-start.8 = (bf16[1024,256]{1,0:T(8,128)(2,1)S(1)}, bf16[1024,256]{1,0:T(8,128)(2,1)}, u32[]{:S(2)}) copy-start(bf16[1024,256]{1,0:T(8,128)(2,1)} %copy-done.7) | copy-start | bytes 1572868
  39.7 9.9 %collective-permute-start.11 = (s16[1024,128]{1,0:T(8,128)(2,1)S(1)}, s16[1024,128]{1,0:T(8,128)(2,1)S(1)}, u32[]{:S(2)}, u32[]{:S(2)}) collective-permute-start(s16[1024,128]{1,0:T(8,128)(2,1)S(1)} %join.12.refs_0_), channel_id=1, source_target_pairs={{0,8},{4,12},{8,0},{12,4},{16,24},{20,28},{24,16},{28,20},{32,40},... | collective-permute-start | bytes 786440 | tf_op jit(solution)/shard_map/ppermute | solution.py:33
  41.0 18.8 %collective-permute-start.13 = (bf16[1024,256]{1,0:T(8,128)(2,1)S(1)}, bf16[1024,256]{1,0:T(8,128)(2,1)S(1)}, u32[]{:S(2)}, u32[]{:S(2)}) collective-permute-start(bf16[1024,256]{1,0:T(8,128)(2,1)S(1)} %get-tuple-element.31), channel_id=1, source_target_pairs={{0,1},{1,2},{2,3},{3,0},{4,5},{5,6},{6,7},{7,4},{8,9},{9,10},{10,1... | collective-permute-start | bytes 1572872 | tf_op jit(solution)/shard_map/ppermute | solution.py:37
  41.1 18.7 %collective-permute-start.14 = (bf16[1024,256]{1,0:T(8,128)(2,1)S(1)}, bf16[1024,256]{1,0:T(8,128)(2,1)S(1)}, u32[]{:S(2)}, u32[]{:S(2)}) collective-permute-start(bf16[1024,256]{1,0:T(8,128)(2,1)S(1)} %get-tuple-element.32), channel_id=1, source_target_pairs={{0,2},{1,3},{2,0},{3,1},{4,6},{5,7},{6,4},{7,5},{8,10},{9,11},{10,... | collective-permute-start | bytes 1572872 | tf_op jit(solution)/shard_map/ppermute | solution.py:37
  43.5 23.5 %collective-permute-start.15 = (bf16[1024,256]{1,0:T(8,128)(2,1)S(1)}, bf16[1024,256]{1,0:T(8,128)(2,1)S(1)}, u32[]{:S(2)}, u32[]{:S(2)}) collective-permute-start(bf16[1024,256]{1,0:T(8,128)(2,1)S(1)} %get-tuple-element.33), channel_id=1, source_target_pairs={{0,3},{1,0},{2,1},{3,2},{4,7},{5,4},{6,5},{7,6},{8,11},{9,8},{10,9... | collective-permute-start | bytes 1572872 | tf_op jit(solution)/shard_map/ppermute | solution.py:37
  49.6 2.0 %copy-start.18 = (s16[1024,128]{1,0:T(8,128)(2,1)}, s16[1024,128]{1,0:T(8,128)(2,1)S(1)}, u32[]{:S(2)}) copy-start(s16[1024,128]{1,0:T(8,128)(2,1)S(1)} %get-tuple-element.29) | copy-start | bytes 786436
  49.6 17.5 %collective-permute-start.12 = (s16[2048,128]{1,0:T(8,128)(2,1)S(1)}, s16[2048,128]{1,0:T(8,128)(2,1)S(1)}, u32[]{:S(2)}, u32[]{:S(2)}) collective-permute-start(s16[2048,128]{1,0:T(8,128)(2,1)S(1)} %join.13.refs_0_), channel_id=1, source_target_pairs={{0,16},{4,20},{8,24},{12,28},{16,0},{20,4},{24,8},{28,12},{32,48},... | collective-permute-start | bytes 1572872 | tf_op jit(solution)/shard_map/ppermute | solution.py:33
  59.7 7.4 %copy-start.1 = (f32[4096,128]{1,0:T(8,128)}, f32[4096,128]{1,0:T(8,128)S(1)}, u32[]{:S(2)}) copy-start(f32[4096,128]{1,0:T(8,128)S(1)} %get-tuple-element.25.refs_2_) | copy-start | bytes 6291460
  59.8 7.4 %copy-start.3 = (f32[4096,128]{1,0:T(8,128)}, f32[4096,128]{1,0:T(8,128)S(1)}, u32[]{:S(2)}) copy-start(f32[4096,128]{1,0:T(8,128)S(1)} %get-tuple-element.35.refs_2_) | copy-start | bytes 6291460
  59.8 7.4 %copy-start.9 = (bf16[1024,256]{1,0:T(8,128)(2,1)}, bf16[1024,256]{1,0:T(8,128)(2,1)S(1)}, u32[]{:S(2)}) copy-start(bf16[1024,256]{1,0:T(8,128)(2,1)S(1)} %collective-permute-done.13.refs_4_.b1) | copy-start | bytes 1572868
  59.8 7.4 %copy-start.11 = (bf16[1024,256]{1,0:T(8,128)(2,1)}, bf16[1024,256]{1,0:T(8,128)(2,1)S(1)}, u32[]{:S(2)}) copy-start(bf16[1024,256]{1,0:T(8,128)(2,1)S(1)} %collective-permute-done.14.refs_5_.b2) | copy-start | bytes 1572868
  67.9 17.6 %collective-permute-start.16 = (s16[4096,128]{1,0:T(8,128)(2,1)S(1)}, s16[4096,128]{1,0:T(8,128)(2,1)}, u32[]{:S(2)}, u32[]{:S(2)}) collective-permute-start(s16[4096,128]{1,0:T(8,128)(2,1)S(1)} %join.14.refs_7_), channel_id=1, source_target_pairs={{0,4},{4,0},{8,12},{12,8},{16,20},{20,16},{24,28},{28,24},{32,36},... | collective-permute-start | bytes 3145736 | tf_op jit(solution)/shard_map/ppermute | solution.py:33
  67.9 12.1 %collective-permute-start.5 = (s16[1024,128]{1,0:T(8,128)(2,1)}, s16[1024,128]{1,0:T(8,128)(2,1)}, u32[]{:S(2)}, u32[]{:S(2)}) collective-permute-start(s16[1024,128]{1,0:T(8,128)(2,1)} %get-tuple-element.27), channel_id=1, source_target_pairs={{0,1},{1,2},{2,3},{3,0},{4,5},{5,6},{6,7},{7,4},{8,9},{9,10},{10,1... | collective-permute-start | bytes 786440 | tf_op jit(solution)/shard_map/ppermute | solution.py:37
  68.5 14.4 %collective-permute-start.6 = (s16[1024,128]{1,0:T(8,128)(2,1)}, s16[1024,128]{1,0:T(8,128)(2,1)}, u32[]{:S(2)}, u32[]{:S(2)}) collective-permute-start(s16[1024,128]{1,0:T(8,128)(2,1)} %get-tuple-element.28), channel_id=1, source_target_pairs={{0,2},{1,3},{2,0},{3,1},{4,6},{5,7},{6,4},{7,5},{8,10},{9,11},{10,... | collective-permute-start | bytes 786440 | tf_op jit(solution)/shard_map/ppermute | solution.py:37
  70.5 15.0 %copy-start.2 = (f32[4096,128]{1,0:T(8,128)S(1)}, f32[4096,128]{1,0:T(8,128)}, u32[]{:S(2)}) copy-start(f32[4096,128]{1,0:T(8,128)} %copy-done.1) | copy-start | bytes 6291460
  70.5 15.0 %collective-permute-start.7 = (s16[1024,128]{1,0:T(8,128)(2,1)}, s16[1024,128]{1,0:T(8,128)(2,1)S(1)}, u32[]{:S(2)}, u32[]{:S(2)}) collective-permute-start(s16[1024,128]{1,0:T(8,128)(2,1)} %copy-done.18), channel_id=1, source_target_pairs={{0,3},{1,0},{2,1},{3,2},{4,7},{5,4},{6,5},{7,6},{8,11},{9,8},{10,9... | collective-permute-start | bytes 786440 | tf_op jit(solution)/shard_map/ppermute | solution.py:37
  72.7 1.0 copy-start.6
  79.9 15.7 %collective-permute-start.17 = (s16[1024,128]{1,0:T(8,128)(2,1)S(1)}, s16[1024,128]{1,0:T(8,128)(2,1)S(1)}, u32[]{:S(2)}, u32[]{:S(2)}) collective-permute-start(s16[1024,128]{1,0:T(8,128)(2,1)S(1)} %get-tuple-element.37), channel_id=1, source_target_pairs={{0,1},{1,2},{2,3},{3,0},{4,5},{5,6},{6,7},{7,4},{8,9},{9,10},{10,1... | collective-permute-start | bytes 786440 | tf_op jit(solution)/shard_map/ppermute | solution.py:37
  80.0 15.6 %collective-permute-start.18 = (s16[1024,128]{1,0:T(8,128)(2,1)S(1)}, s16[1024,128]{1,0:T(8,128)(2,1)S(1)}, u32[]{:S(2)}, u32[]{:S(2)}) collective-permute-start(s16[1024,128]{1,0:T(8,128)(2,1)S(1)} %get-tuple-element.38), channel_id=1, source_target_pairs={{0,2},{1,3},{2,0},{3,1},{4,6},{5,7},{6,4},{7,5},{8,10},{9,11},{10,... | collective-permute-start | bytes 786440 | tf_op jit(solution)/shard_map/ppermute | solution.py:37
  82.9 12.7 %collective-permute-start.19 = (s16[1024,128]{1,0:T(8,128)(2,1)S(1)}, s16[1024,128]{1,0:T(8,128)(2,1)S(1)}, u32[]{:S(2)}, u32[]{:S(2)}) collective-permute-start(s16[1024,128]{1,0:T(8,128)(2,1)S(1)} %get-tuple-element.39), channel_id=1, source_target_pairs={{0,3},{1,0},{2,1},{3,2},{4,7},{5,4},{6,5},{7,6},{8,11},{9,8},{10,9... | collective-permute-start | bytes 786440 | tf_op jit(solution)/shard_map/ppermute | solution.py:37
  85.5 10.1 %copy-start.4 = (f32[4096,128]{1,0:T(8,128)S(1)}, f32[4096,128]{1,0:T(8,128)}, u32[]{:S(2)}) copy-start(f32[4096,128]{1,0:T(8,128)} %copy-done.3) | copy-start | bytes 6291460
  104.9 4.2 %collective-permute-start.20 = (f32[4096,128]{1,0:T(8,128)S(1)}, f32[4096,128]{1,0:T(8,128)S(1)}, u32[]{:S(2)}, u32[]{:S(2)}) collective-permute-start(f32[4096,128]{1,0:T(8,128)S(1)} %get-tuple-element.47), channel_id=1, source_target_pairs={{0,4},{4,0},{8,12},{12,8},{16,20},{20,16},{24,28},{28,24},{32,36},... | collective-permute-start | bytes 6291464 | tf_op jit(solution)/shard_map/ppermute | solution.py:33
  109.8 14.8 %collective-permute-start.26 = (f16[512,128]{1,0:T(8,128)(2,1)S(1)}, f16[512,128]{1,0:T(8,128)(2,1)S(1)}, u32[]{:S(2)}, u32[]{:S(2)}) collective-permute-start(f16[512,128]{1,0:T(8,128)(2,1)S(1)} %get-tuple-element.54), channel_id=1, source_target_pairs={{0,8},{4,12},{8,0},{12,4},{16,24},{20,28},{24,16},{28,20},{32,40},... | collective-permute-start | bytes 393224 | tf_op jit(solution)/shard_map/ppermute | solution.py:33
  110.2 9.9 %collective-permute-start.23 = (f16[512,128]{1,0:T(8,128)(2,1)S(1)}, f16[512,128]{1,0:T(8,128)(2,1)S(1)}, u32[]{:S(2)}, u32[]{:S(2)}) collective-permute-start(f16[512,128]{1,0:T(8,128)(2,1)S(1)} %get-tuple-element.57), channel_id=1, source_target_pairs={{0,16},{4,20},{8,24},{12,28},{16,0},{20,4},{24,8},{28,12},{32,48},... | collective-permute-start | bytes 393224 | tf_op jit(solution)/shard_map/ppermute | solution.py:33
  113.0 9.0 %collective-permute-start.22 = (f16[512,128]{1,0:T(8,128)(2,1)S(1)}, f16[512,128]{1,0:T(8,128)(2,1)S(1)}, u32[]{:S(2)}, u32[]{:S(2)}) collective-permute-start(f16[512,128]{1,0:T(8,128)(2,1)S(1)} %get-tuple-element.58), channel_id=1, source_target_pairs={{0,24},{4,28},{8,16},{12,20},{16,8},{20,12},{24,0},{28,4},{32,56},... | collective-permute-start | bytes 393224 | tf_op jit(solution)/shard_map/ppermute | solution.py:33
  114.6 7.3 %collective-permute-start.21 = (f16[512,128]{1,0:T(8,128)(2,1)S(1)}, f16[512,128]{1,0:T(8,128)(2,1)S(1)}, u32[]{:S(2)}, u32[]{:S(2)}) collective-permute-start(f16[512,128]{1,0:T(8,128)(2,1)S(1)} %get-tuple-element.59), channel_id=1, source_target_pairs={{0,8},{4,12},{8,0},{12,4},{16,24},{20,28},{24,16},{28,20},{32,40},... | collective-permute-start | bytes 393224 | tf_op jit(solution)/shard_map/ppermute | solution.py:33
  114.7 16.9 %collective-permute-start.28 = (f16[512,128]{1,0:T(8,128)(2,1)S(1)}, f16[512,128]{1,0:T(8,128)(2,1)S(1)}, u32[]{:S(2)}, u32[]{:S(2)}) collective-permute-start(f16[512,128]{1,0:T(8,128)(2,1)S(1)} %get-tuple-element.55), channel_id=1, source_target_pairs={{0,16},{4,20},{8,24},{12,28},{16,0},{20,4},{24,8},{28,12},{32,48},... | collective-permute-start | bytes 393224 | tf_op jit(solution)/shard_map/ppermute | solution.py:33
  120.1 11.4 %collective-permute-start.27 = (f16[512,128]{1,0:T(8,128)(2,1)S(1)}, f16[512,128]{1,0:T(8,128)(2,1)S(1)}, u32[]{:S(2)}, u32[]{:S(2)}) collective-permute-start(f16[512,128]{1,0:T(8,128)(2,1)S(1)} %get-tuple-element.56), channel_id=1, source_target_pairs={{0,24},{4,28},{8,16},{12,20},{16,8},{20,12},{24,0},{28,4},{32,56},... | collective-permute-start | bytes 393224 | tf_op jit(solution)/shard_map/ppermute | solution.py:33
  122.1 9.6 %collective-permute-start.24 = (f32[128,128]{1,0:T(8,128)S(1)}, f32[128,128]{1,0:T(8,128)S(1)}, u32[]{:S(2)}, u32[]{:S(2)}) collective-permute-start(f32[128,128]{1,0:T(8,128)S(1)} %get-tuple-element.60), channel_id=1, source_target_pairs={{0,4},{4,8},{8,12},{12,16},{16,20},{20,24},{24,28},{28,32},{32,36}... | collective-permute-start | bytes 196616 | tf_op jit(solution)/shard_map/ppermute | solution.py:280
  123.4 8.3 %collective-permute-start.25 = (f32[128,128]{1,0:T(8,128)S(1)}, f32[128,128]{1,0:T(8,128)S(1)}, u32[]{:S(2)}, u32[]{:S(2)}) collective-permute-start(f32[128,128]{1,0:T(8,128)S(1)} %get-tuple-element.61), channel_id=1, source_target_pairs={{4,0},{8,4},{12,8},{16,12},{20,16},{24,20},{28,24},{32,28},{36,32}... | collective-permute-start | bytes 196616 | tf_op jit(solution)/shard_map/ppermute | solution.py:280
  124.7 10.9 %collective-permute-start.29 = (f16[512,128]{1,0:T(8,128)(2,1)S(1)}, f16[512,128]{1,0:T(8,128)(2,1)S(1)}, u32[]{:S(2)}, u32[]{:S(2)}) collective-permute-start(f16[512,128]{1,0:T(8,128)(2,1)S(1)} %get-tuple-element.48), channel_id=1, source_target_pairs={{0,32},{4,36},{8,40},{12,44},{16,48},{20,52},{24,56},{28,60},{32,0... | collective-permute-start | bytes 393224 | tf_op jit(solution)/shard_map/ppermute | solution.py:33
  131.7 19.5 %copy-start.15 = (f32[128,128]{1,0:T(8,128)}, f32[128,128]{1,0:T(8,128)S(1)}, u32[]{:S(2)}) copy-start(f32[128,128]{1,0:T(8,128)S(1)} %fusion.7.refs_1_) | copy-start | bytes 196612
  135.6 5.7 %collective-permute-start.30 = (f16[2,128,128]{2,1,0:T(8,128)(2,1)S(1)}, f16[2,128,128]{2,1,0:T(8,128)(2,1)S(1)}, u32[]{:S(2)}, u32[]{:S(2)}) collective-permute-start(f16[2,128,128]{2,1,0:T(8,128)(2,1)S(1)} %fusion.4), channel_id=1, source_target_pairs={{0,64},{4,68},{8,72},{12,76},{16,80},{20,84},{24,88},{28,92},{32,9... | collective-permute-start | bytes 196616 | tf_op jit(solution)/shard_map/ppermute | solution.py:33
  141.4 9.2 %collective-permute-start.31 = (f16[128,128]{1,0:T(8,128)(2,1)S(1)}, f16[128,128]{1,0:T(8,128)(2,1)S(1)}, u32[]{:S(2)}, u32[]{:S(2)}) collective-permute-start(f16[128,128]{1,0:T(8,128)(2,1)S(1)} %fusion.23), channel_id=1, source_target_pairs={{0,128},{4,132},{8,136},{12,140},{16,144},{20,148},{24,152},{28,15... | collective-permute-start | bytes 98312 | tf_op jit(solution)/shard_map/ppermute | solution.py:33
  (5 other events, 4.8 us)

commit v16 on v13

--- a/solution.py
+++ b/solution.py
@@ -93,31 +93,18 @@
     )(*parts, *after)
 
 
-def take_rows(traces, y, first, size, after=()):
-    rows, part = traces.shape
-
-    def body(y_ref, traces, *refs):
-        outs, sems = refs[len(after) : len(after) + NY], refs[len(after) + NY :]
-        copies = []
-        for k in range(NY):
-            at = pl.multiple_of((y_ref[0] + k) % NY * (rows // NY) + first, 16)
-            copies.append(pltpu.make_async_copy(traces.at[pl.ds(at, size), :], outs[k], sems[k]))
-        for copy in copies:
-            copy.start()
-        for copy in copies:
-            copy.wait()
-
-    hbm, vm = pl.BlockSpec(memory_space=pl.ANY), pl.BlockSpec(memory_space=pltpu.VMEM)
-    return pl.pallas_call(
-        body,
-        in_specs=[pl.BlockSpec(memory_space=pltpu.SMEM), hbm] + [hbm] * len(after),
-        out_specs=[vm] * NY,
-        out_shape=[jax.ShapeDtypeStruct((size, part), traces.dtype)] * NY,
-        scratch_shapes=[pltpu.SemaphoreType.DMA] * NY,
+def tie(values, after):
+    hbm = pl.BlockSpec(memory_space=pl.ANY)
+    return pl.pallas_call(
+        lambda *refs: None,
+        in_specs=[hbm] * (len(values) + len(after)),
+        out_specs=[hbm] * len(values),
+        out_shape=[jax.ShapeDtypeStruct(value.shape, value.dtype) for value in values],
+        input_output_aliases={k: k for k in range(len(values))},
         compiler_params=SMALL,
         cost_estimate=COST,
-        name="take_rows",
-    )(y[None], traces, *after)
+        name="tie",
+    )(*values, *after)
 
 
 def encode_terms(terms, after):
@@ -288,15 +275,13 @@
     owner, y = lax.axis_index("tr"), lax.axis_index("fq")
     z, x, c = owner // (NX * NC), owner // NC % NX, owner % NC
 
-    got, after = [], ()
+    got = []
     for at, size in zip(first, PIECES):
-        if after:
-            mine = take_rows(traces, y, at, size, after)
-        else:
-            mine = [lax.dynamic_slice_in_dim(traces, (y + k) % NY * share + at, size, 0) for k in range(NY)]
+        mine = [lax.dynamic_slice_in_dim(traces, (y + k) % NY * share + at, size, 0) for k in range(NY)]
+        if got:
+            mine[1:] = tie(mine[1:], got[0][1:])
         come = {k: send_y(mine[k], k) for k in (1, 3, 2)}
-        after = [come[k] for k in range(1, NY)]
-        got.append([mine[0]] + after)
+        got.append([mine[0]] + [come[k] for k in range(1, NY)])
     table = make_table(part * NY, y, width, got[0][:1])
     codes, coded = [], []
     for blocks in got:
@@ -323,7 +308,7 @@
     terms = encode_terms(receiver_terms, (table,))
     terms = join([terms, swap(terms, 2, 0, 0)])
     terms = join([terms, swap(terms, 4, 0, 0)], got[0][1:] + [shot_near])
-    terms = join([terms, swap(terms, 1, 0, 0)], got[1][:1])
+    terms = join([terms, swap(terms, 1, 0, 0)])
     shots = gather_shots(shot_near, shot_at, [size * NY for size in PIECES])
     terms = join([terms, swap(terms, 0, 1, 0)], [coded[0][0]])
     terms = join([terms, swap(terms, 0, 2, 0)], [shots[0], rec_at] + got[1][1:])

time: 147 us -> 147 us (level)
  starting transfers between devices: 59.8 us -> 57.8 us
  waiting for transfers between devices: 30.8 us -> 32.6 us
    ppermute x13, waiting for transfers between devices: 23.2 us -> 25.9 us  [swap(): lax.ppermute(value, 'tr', [(tr_of(z, x, c), tr_of(z ^ dz, x ^ dx, c ^ dc)...]
    unnamed x47 -> x49, local copies, waits for them, and re-layouts: 7.93 us -> 5.67 us
    ppermute x13, starting transfers between devices: 33.6 us -> 31.5 us  [swap(): lax.ppermute(value, 'tr', [(tr_of(z, x, c), tr_of(z ^ dz, x ^ dx, c ^ dc)...]
  transfers between devices with their start and end apart: 29 -> 29, of which waited for: 10 -> 11; matrix products, arithmetic and copies ran while one was open for 1% -> 1% of each run, Pallas kernels for 22% -> 23%
where the time goes in v16:
time: 147 us; the launch traced here: 146 us
  starting transfers between devices  57.8 us (39%)
  Pallas kernels  41.9 us (29%)
  waiting for transfers between devices  32.6 us (22%)
  local copies, waits for them, and re-layouts  10.1 us (7%)
  between operations  2.05 us (1%)
    ppermute x13, starting transfers between devices, swap(): lax.ppermute(value, 'tr', [(tr_of(z, x, c), tr_of(z ^ dz, x ^ dx, c ^ dc)...  31.5 us
    ppermute x13, waiting for transfers between devices, swap(): lax.ppermute(value, 'tr', [(tr_of(z, x, c), tr_of(z ^ dz, x ^ dx, c ^ dc)...  25.9 us
    ppermute x12, starting transfers between devices, send_y(): return lax.ppermute(value, 'fq', [(i, (i + k) % NY) for i in range(NY)])  19.1 us
    pallas_call x2, Pallas kernels, sum_receivers(): pl.pallas_call(body, in_specs=[sm, sm] + [vm] * (1 + parts + len(given)),...  18.8 us
    pallas_call x1, Pallas kernels, gather_shots(): pl.pallas_call(body, in_specs=[sm, vm], out_specs=[vm] * len(sizes), out_...  8.11 us
    pallas_call x2, Pallas kernels, spectra(): pl.pallas_call(body, grid=(rows // tile,), in_specs=[pl.BlockSpec((tile,...  7.61 us
    ppermute x4, starting transfers between devices, neighbour(): lax.ppermute(value, 'tr', [(i, i + by) for i in range(size) if 0 <= i + b...  7.15 us
    ppermute x12, waiting for transfers between devices, send_y(): return lax.ppermute(value, 'fq', [(i, (i + k) % NY) for i in range(NY)])  6.69 us
  transfers between devices with their start and end apart: 29, of which 11 were waited for; matrix products, arithmetic and copies ran while one was open for 1% of the time, Pallas kernels for 23%

profile of v16, /device:TPU:8, one launch (start us, length us, event | category | flops | bytes accessed | tf_op | source)
XLA Modules:
  0.0 145.9 jit_solution(1165162228137128802)
XLA Ops:
  0.7 4.0 %constant_dynamic-slice_fusion = (bf16[1024,256]{1,0:T(8,128)(2,1)}, bf16[1024,256]{1,0:T(8,128)(2,1)}, bf16[1024,256]{1,0:T(8,128)(2,1)}, bf16[1024,256]{1,0:T(...) fusion(bf16[8192,256]{1,0:T(8,128)(2,1)} %param.6, ...), kind=kLoop, calls=%fused_computation.74 | loop fusion | bytes 8388640 | tf_op jit(solution)/shard_map/dynamic_slice | solution.py:280
  4.7 2.3 %collective-permute-start.4 = (bf16[1024,256]{1,0:T(8,128)(2,1)}, bf16[1024,256]{1,0:T(8,128)(2,1)S(1)}, u32[]{:S(2)}, u32[]{:S(2)}) collective-permute-start(bf16[1024,256]{1,0:T(8,128)(2,1)} %get-tuple-element.51), channel_id=1, source_target_pairs={{0,3},{1,0},{2,1},{3,2},{4,7},{5,4},{6,5},{7,6},{8,11},{9,8},{10,9... | collective-permute-start | bytes 1572872 | tf_op jit(solution)/shard_map/ppermute | solution.py:37
  7.0 0.9 collective-permute-start.3
  7.8 1.9 %collective-permute-start.2 = (bf16[1024,256]{1,0:T(8,128)(2,1)}, bf16[1024,256]{1,0:T(8,128)(2,1)}, u32[]{:S(2)}, u32[]{:S(2)}) collective-permute-start(bf16[1024,256]{1,0:T(8,128)(2,1)} %get-tuple-element.53), channel_id=1, source_target_pairs={{0,1},{1,2},{2,3},{3,0},{4,5},{5,6},{6,7},{7,4},{8,9},{9,10},{10,1... | collective-permute-start | bytes 1572872 | tf_op jit(solution)/shard_map/ppermute | solution.py:37
  9.7 5.3 %make_table.1.refs_1_.t.refs_0_ = bf16[1024,1024]{1,0:T(8,128)(2,1)S(1)} custom-call(s32[1]{0:T(128)} %bitcast.10.y_ref, bf16[1024,256]{1,0:T(8,128)(2,1)S(1)} %get-tuple-element.54.refs_0_.b0), custom_call_target="tpu_custom_call" | custom-call | flops 1073741824 | bytes 33554432 | tf_op jit(solution)/shard_map/make_table/pallas_call | solution.py:64
  15.1 3.4 %collective-permute-start.8 = (s16[128,128]{1,0:T(8,128)(2,1)S(1)}, s16[128,128]{1,0:T(8,128)(2,1)S(1)}, u32[]{:S(2)}, u32[]{:S(2)}) collective-permute-start(s16[128,128]{1,0:T(8,128)(2,1)S(1)} %encode_terms.1.refs_0_), channel_id=1, source_target_pairs={{0,64},{4,68},{8,72},{12,76},{16,80},{20,84},{24,88},{28,92},{32,9... | collective-permute-start | bytes 98312 | tf_op jit(solution)/shard_map/ppermute | solution.py:33
  18.5 1.3 collective-permute-start.1
  20.9 3.2 %collective-permute-start = (f32[128,128]{1,0:T(8,128)S(1)}, f32[128,128]{1,0:T(8,128)S(1)}, u32[]{:S(2)}, u32[]{:S(2)}) collective-permute-start(f32[128,128]{1,0:T(8,128)S(1)} %join.8), channel_id=1, source_target_pairs={{0,4},{4,8},{8,12},{12,16},{16,20},{20,24},{24,28},{28,32},{32,36}... | collective-permute-start | bytes 196616 | tf_op jit(solution)/shard_map/ppermute | solution.py:267
  24.1 5.5 %collective-permute-start.9 = (s16[256,128]{1,0:T(8,128)(2,1)S(1)}, s16[256,128]{1,0:T(8,128)(2,1)S(1)}, u32[]{:S(2)}, u32[]{:S(2)}) collective-permute-start(s16[256,128]{1,0:T(8,128)(2,1)S(1)} %join.9.refs_0_), channel_id=1, source_target_pairs={{0,128},{4,132},{8,136},{12,140},{16,144},{20,148},{24,152},{28,15... | collective-permute-start | bytes 196616 | tf_op jit(solution)/shard_map/ppermute | solution.py:33
  29.6 3.4 %collective-permute-done.9.refs_1_ = s16[256,128]{1,0:T(8,128)(2,1)S(1)} collective-permute-done((s16[256,128]{1,0:T(8,128)(2,1)S(1)}, s16[256,128]{1,0:T(8,128)(2,1)S(1)}, u32[]{:S(2)}, u32[]{:S(2)}) %collective-permute-start.9) | collective-permute-done | bytes 65568 | tf_op jit(solution)/shard_map/ppermute | solution.py:33
  33.1 3.6 %collective-permute-start.10 = (s16[512,128]{1,0:T(8,128)(2,1)S(1)}, s16[512,128]{1,0:T(8,128)(2,1)S(1)}, u32[]{:S(2)}, u32[]{:S(2)}) collective-permute-start(s16[512,128]{1,0:T(8,128)(2,1)S(1)} %join.10.refs_0_), channel_id=1, source_target_pairs={{0,32},{4,36},{8,40},{12,44},{16,48},{20,52},{24,56},{28,60},{32,0... | collective-permute-start | bytes 393224 | tf_op jit(solution)/shard_map/ppermute | solution.py:33
  36.7 3.7 %collective-permute-done.10.refs_1_ = s16[512,128]{1,0:T(8,128)(2,1)S(1)} collective-permute-done((s16[512,128]{1,0:T(8,128)(2,1)S(1)}, s16[512,128]{1,0:T(8,128)(2,1)S(1)}, u32[]{:S(2)}, u32[]{:S(2)}) %collective-permute-start.10) | collective-permute-done | bytes 131104 | tf_op jit(solution)/shard_map/ppermute | solution.py:33
  40.5 1.3 collective-permute-start.11
  42.0 2.3 %collective-permute-start.14 = (bf16[1024,256]{1,0:T(8,128)(2,1)S(1)}, bf16[1024,256]{1,0:T(8,128)(2,1)S(1)}, u32[]{:S(2)}, u32[]{:S(2)}) collective-permute-start(bf16[1024,256]{1,0:T(8,128)(2,1)S(1)} %get-tuple-element.30), channel_id=1, source_target_pairs={{0,2},{1,3},{2,0},{3,1},{4,6},{5,7},{6,4},{7,5},{8,10},{9,11},{10,... | collective-permute-start | bytes 1572872 | tf_op jit(solution)/shard_map/ppermute | solution.py:37
  44.3 1.6 %collective-permute-start.15 = (bf16[1024,256]{1,0:T(8,128)(2,1)S(1)}, bf16[1024,256]{1,0:T(8,128)(2,1)S(1)}, u32[]{:S(2)}, u32[]{:S(2)}) collective-permute-start(bf16[1024,256]{1,0:T(8,128)(2,1)S(1)} %get-tuple-element.31), channel_id=1, source_target_pairs={{0,3},{1,0},{2,1},{3,2},{4,7},{5,4},{6,5},{7,6},{8,11},{9,8},{10,9... | collective-permute-start | bytes 1572872 | tf_op jit(solution)/shard_map/ppermute | solution.py:37
  45.9 4.6 %spectra.2 = (s16[1024,128]{1,0:T(8,128)(2,1)S(1)}, s16[1024,128]{1,0:T(8,128)(2,1)}, s16[1024,128]{1,0:T(8,128)(2,1)}, s16[1024,128]{1,0:T(8,128)(2,1)S(1)}) custom-call(bf16[1024,256]{1,0:T(8,128)(2,1)S(1)} %copy-done.15, bf16[1024,256]{1,0:T(8,128)(2,1)} %collective-permute-done.2.b1.refs_2_.refs_3_, ...), custom_call_target="tpu_custom_call" | custom-call | flops 1000 | bytes 1000 | tf_op jit(solution)/shard_map/spectra/pallas_call | solution.py:144
  50.5 0.7 copy-done.19
  51.2 2.0 %collective-permute-start.12 = (s16[2048,128]{1,0:T(8,128)(2,1)S(1)}, s16[2048,128]{1,0:T(8,128)(2,1)S(1)}, u32[]{:S(2)}, u32[]{:S(2)}) collective-permute-start(s16[2048,128]{1,0:T(8,128)(2,1)S(1)} %join.12.refs_0_), channel_id=1, source_target_pairs={{0,16},{4,20},{8,24},{12,28},{16,0},{20,4},{24,8},{28,12},{32,48},... | collective-permute-start | bytes 1572872 | tf_op jit(solution)/shard_map/ppermute | solution.py:33
  53.2 8.1 %gather_shots.1 = (f32[4096,128]{1,0:T(8,128)S(1)}, f32[4096,128]{1,0:T(8,128)S(1)}) custom-call(s32[8192]{0:T(1024)S(1)} %bitcast_dynamic-update-slice_fusion.shot_at, f32[384,128]{1,0:T(8,128)S(1)} %pad_maximum_fusion.shot.refs_5_), custom_call_target="tpu_custom_call" | custom-call | flops 1000 | bytes 1000 | tf_op jit(solution)/shard_map/gather_shots/pallas_call | solution.py:173
  61.4 6.5 %collective-permute-done.15.refs_6_.b3 = bf16[1024,256]{1,0:T(8,128)(2,1)S(1)} collective-permute-done((bf16[1024,256]{1,0:T(8,128)(2,1)S(1)}, bf16[1024,256]{1,0:T(8,128)(2,1)S(1)}, u32[]{:S(2)}, u32[]{:S(2)}) %collective-permute-start.15) | collective-permute-done | bytes 524320 | tf_op jit(solution)/shard_map/ppermute | solution.py:37
  68.0 0.7 copy-done.8
  68.7 0.7 collective-permute-start.5
  69.4 1.9 %collective-permute-start.6 = (s16[1024,128]{1,0:T(8,128)(2,1)}, s16[1024,128]{1,0:T(8,128)(2,1)}, u32[]{:S(2)}, u32[]{:S(2)}) collective-permute-start(s16[1024,128]{1,0:T(8,128)(2,1)} %get-tuple-element.27), channel_id=1, source_target_pairs={{0,2},{1,3},{2,0},{3,1},{4,6},{5,7},{6,4},{7,5},{8,10},{9,11},{10,... | collective-permute-start | bytes 786440 | tf_op jit(solution)/shard_map/ppermute | solution.py:37
  71.3 1.9 %collective-permute-start.7 = (s16[1024,128]{1,0:T(8,128)(2,1)}, s16[1024,128]{1,0:T(8,128)(2,1)S(1)}, u32[]{:S(2)}, u32[]{:S(2)}) collective-permute-start(s16[1024,128]{1,0:T(8,128)(2,1)} %copy-done.19), channel_id=1, source_target_pairs={{0,3},{1,0},{2,1},{3,2},{4,7},{5,4},{6,5},{7,6},{8,11},{9,8},{10,9... | collective-permute-start | bytes 786440 | tf_op jit(solution)/shard_map/ppermute | solution.py:37
  73.2 1.0 copy-done.5
  74.3 1.0 copy-done.7
  75.3 1.0 copy-done.9
  76.3 1.0 copy-done.13
  77.4 3.0 %spectra.3 = (s16[1024,128]{1,0:T(8,128)(2,1)S(1)}, s16[1024,128]{1,0:T(8,128)(2,1)S(1)}, s16[1024,128]{1,0:T(8,128)(2,1)S(1)}, s16[1024,128]{1,0:T(8,128)(2,1)S(1)}) custom-call(bf16[1024,256]{1,0:T(8,128)(2,1)S(1)} %copy-done.13, bf16[1024,256]{1,0:T(8,128)(2,1)S(1)} %copy-done.5, bf16[1024,256]{1,0:T(8,128)(2,1)S(1)} %copy-done.7, ...), custom_call_target="tpu_custom_call" | custom-call | flops 1000 | bytes 1000 | tf_op jit(solution)/shard_map/spectra/pallas_call | solution.py:144
  80.7 2.9 %collective-permute-start.18 = (s16[1024,128]{1,0:T(8,128)(2,1)S(1)}, s16[1024,128]{1,0:T(8,128)(2,1)S(1)}, u32[]{:S(2)}, u32[]{:S(2)}) collective-permute-start(s16[1024,128]{1,0:T(8,128)(2,1)S(1)} %get-tuple-element.36), channel_id=1, source_target_pairs={{0,2},{1,3},{2,0},{3,1},{4,6},{5,7},{6,4},{7,5},{8,10},{9,11},{10,... | collective-permute-start | bytes 786440 | tf_op jit(solution)/shard_map/ppermute | solution.py:37
  83.5 2.6 %collective-permute-start.19 = (s16[1024,128]{1,0:T(8,128)(2,1)S(1)}, s16[1024,128]{1,0:T(8,128)(2,1)S(1)}, u32[]{:S(2)}, u32[]{:S(2)}) collective-permute-start(s16[1024,128]{1,0:T(8,128)(2,1)S(1)} %get-tuple-element.37), channel_id=1, source_target_pairs={{0,3},{1,0},{2,1},{3,2},{4,7},{5,4},{6,5},{7,6},{8,11},{9,8},{10,9... | collective-permute-start | bytes 786440 | tf_op jit(solution)/shard_map/ppermute | solution.py:37
  86.2 10.0 %sum_receivers.2 = (f32[4096,128]{1,0:T(8,128)S(1)}, f32[8200,128]{1,0:T(8,128)S(1)}, f32[8200,128]{1,0:T(8,128)S(1)}, f32[8200,128]{1,0:T(8,128)S(1)}, f32[8200...) custom-call(s32[4096]{0:T(1024)S(1)} %bitcast.59, s32[4]{0:T(128)S(1)} %get-tuple-element.76.refs_1_, f32[4096,128]{1,0:T(8,128)S(1)} %copy-done.1, ...), custom_call_target="tpu_custom_call" | custom-call | flops 1000 | bytes 1000 | tf_op jit(solution)/shard_map/sum_receivers/pallas_call | solution.py:224
  96.4 8.9 %sum_receivers.3 = (f32[4096,128]{1,0:T(8,128)S(1)}, f32[8200,128]{1,0:T(8,128)S(1)}, f32[8200,128]{1,0:T(8,128)S(1)}, f32[8200,128]{1,0:T(8,128)S(1)}, f32[8200...) custom-call(s32[4096]{0:T(1024)S(1)} %bitcast.61, ...), custom_call_target="tpu_custom_call", output_to_operand_aliasing={{1}: (7, {}), {2}: (8, {}), {3}: (9, {}), {4}: (10, {}), {5... | custom-call | flops 1000 | bytes 1000 | tf_op jit(solution)/shard_map/sum_receivers/pallas_call | solution.py:224
  105.6 3.9 %collective-permute-done.22 = f32[4096,128]{1,0:T(8,128)S(1)} collective-permute-done((f32[4096,128]{1,0:T(8,128)S(1)}, f32[4096,128]{1,0:T(8,128)S(1)}, u32[]{:S(2)}, u32[]{:S(2)}) %collective-permute-start.22) | collective-permute-done | bytes 2097184 | tf_op jit(solution)/shard_map/ppermute | solution.py:33
  110.0 3.0 %collective-permute-start.25 = (f16[2,4,128,128]{3,2,1,0:T(8,128)(2,1)S(1)}, f16[2,4,128,128]{3,2,1,0:T(8,128)(2,1)S(1)}, u32[]{:S(2)}, u32[]{:S(2)}) collective-permute-start(f16[2,4,128,128]{3,2,1,0:T(8,128)(2,1)S(1)} %bitcast.66), channel_id=1, source_target_pairs={{0,16},{4,20},{8,24},{12,28},{16,0},{20,4},{24,8},{28,12},{32,48},... | collective-permute-start | bytes 786440 | tf_op jit(solution)/shard_map/ppermute | solution.py:33
  113.4 0.8 collective-permute-start.24
  114.2 1.8 %sum_shots.1.refs_1_ = f32[384,128]{1,0:T(8,128)S(1)} custom-call(s32[1,8192]{1,0:T(1,128)S(1)} %bitcast.57, f32[4096,128]{1,0:T(8,128)S(1)} %get-tuple-element.32.refs_0_, f32[4096,128]{1,0:T(8,128)S(1)} %get-tuple-element.43.refs_1_), custom_call_target="tpu_custom_call" | custom-call | flops 1000 | bytes 1000 | tf_op jit(solution)/shard_map/sum_shots/pallas_call | solution.py:254
  116.0 1.4 collective-permute-start.20
  117.5 1.3 collective-permute-start.21
  118.8 1.9 %collective-permute-done.25 = f16[2,4,128,128]{3,2,1,0:T(8,128)(2,1)S(1)} collective-permute-done((f16[2,4,128,128]{3,2,1,0:T(8,128)(2,1)S(1)}, f16[2,4,128,128]{3,2,1,0:T(8,128)(2,1)S(1)}, u32[]{:S(2)}, u32[]{:S(2)}) %collective-permute-start.25) | collective-permute-done | bytes 262176 | tf_op jit(solution)/shard_map/ppermute | solution.py:33
  120.8 4.6 %collective-permute-done.23 = f16[2,4,128,128]{3,2,1,0:T(8,128)(2,1)S(1)} collective-permute-done((f16[2,4,128,128]{3,2,1,0:T(8,128)(2,1)S(1)}, f16[2,4,128,128]{3,2,1,0:T(8,128)(2,1)S(1)}, u32[]{:S(2)}, u32[]{:S(2)}) %collective-permute-start.23) | collective-permute-done | bytes 262176 | tf_op jit(solution)/shard_map/ppermute | solution.py:33
  125.8 2.3 %collective-permute-start.26 = (f16[4,128,128]{2,1,0:T(8,128)(2,1)S(1)}, f16[4,128,128]{2,1,0:T(8,128)(2,1)S(1)}, u32[]{:S(2)}, u32[]{:S(2)}) collective-permute-start(f16[4,128,128]{2,1,0:T(8,128)(2,1)S(1)} %get-tuple-element.59), channel_id=1, source_target_pairs={{0,32},{4,36},{8,40},{12,44},{16,48},{20,52},{24,56},{28,60},{32,0... | collective-permute-start | bytes 393224 | tf_op jit(solution)/shard_map/ppermute | solution.py:33
  128.2 3.6 %collective-permute-done.26 = f16[4,128,128]{2,1,0:T(8,128)(2,1)S(1)} collective-permute-done((f16[4,128,128]{2,1,0:T(8,128)(2,1)S(1)}, f16[4,128,128]{2,1,0:T(8,128)(2,1)S(1)}, u32[]{:S(2)}, u32[]{:S(2)}) %collective-permute-start.26) | collective-permute-done | bytes 131104 | tf_op jit(solution)/shard_map/ppermute | solution.py:33
  131.9 2.9 %collective-permute-start.27 = (f16[2,128,128]{2,1,0:T(8,128)(2,1)S(1)}, f16[2,128,128]{2,1,0:T(8,128)(2,1)S(1)}, u32[]{:S(2)}, u32[]{:S(2)}) collective-permute-start(f16[2,128,128]{2,1,0:T(8,128)(2,1)S(1)} %fusion.4), channel_id=1, source_target_pairs={{0,64},{4,68},{8,72},{12,76},{16,80},{20,84},{24,88},{28,92},{32,9... | collective-permute-start | bytes 196616 | tf_op jit(solution)/shard_map/ppermute | solution.py:33
  134.9 2.5 %collective-permute-done.27 = f16[2,128,128]{2,1,0:T(8,128)(2,1)S(1)} collective-permute-done((f16[2,128,128]{2,1,0:T(8,128)(2,1)S(1)}, f16[2,128,128]{2,1,0:T(8,128)(2,1)S(1)}, u32[]{:S(2)}, u32[]{:S(2)}) %collective-permute-start.27) | collective-permute-done | bytes 65568 | tf_op jit(solution)/shard_map/ppermute | solution.py:33
  137.4 6.0 %collective-permute-start.28 = (f16[128,128]{1,0:T(8,128)(2,1)S(1)}, f16[128,128]{1,0:T(8,128)(2,1)S(1)}, u32[]{:S(2)}, u32[]{:S(2)}) collective-permute-start(f16[128,128]{1,0:T(8,128)(2,1)S(1)} %fusion.23), channel_id=1, source_target_pairs={{0,128},{4,132},{8,136},{12,140},{16,144},{20,148},{24,152},{28,15... | collective-permute-start | bytes 98312 | tf_op jit(solution)/shard_map/ppermute | solution.py:33
  143.3 2.0 %collective-permute-done.28 = f16[128,128]{1,0:T(8,128)(2,1)S(1)} collective-permute-done((f16[128,128]{1,0:T(8,128)(2,1)S(1)}, f16[128,128]{1,0:T(8,128)(2,1)S(1)}, u32[]{:S(2)}, u32[]{:S(2)}) %collective-permute-start.28) | collective-permute-done | bytes 32800 | tf_op jit(solution)/shard_map/ppermute | solution.py:33
  145.3 0.6 fusion.6
  (102 shorter events, 3.2 us)
Async XLA Ops:
  4.7 10.4 %copy-start.14 = (bf16[1024,256]{1,0:T(8,128)(2,1)}, bf16[1024,256]{1,0:T(8,128)(2,1)S(1)}, u32[]{:S(2)}) copy-start(bf16[1024,256]{1,0:T(8,128)(2,1)S(1)} %get-tuple-element.54.refs_0_.b0) | copy-start | bytes 1572868
  4.7 10.3 %copy-start.17 = (f32[128,128]{1,0:T(8,128)S(1)}, f32[128,128]{1,0:T(8,128)}, u32[]{:S(2)}) copy-start(f32[128,128]{1,0:T(8,128)} %a.1) | copy-start | bytes 196612
  4.7 28.3 %collective-permute-start.4 = (bf16[1024,256]{1,0:T(8,128)(2,1)}, bf16[1024,256]{1,0:T(8,128)(2,1)S(1)}, u32[]{:S(2)}, u32[]{:S(2)}) collective-permute-start(bf16[1024,256]{1,0:T(8,128)(2,1)} %get-tuple-element.51), channel_id=1, source_target_pairs={{0,3},{1,0},{2,1},{3,2},{4,7},{5,4},{6,5},{7,6},{8,11},{9,8},{10,9... | collective-permute-start | bytes 1572872 | tf_op jit(solution)/shard_map/ppermute | solution.py:37
  7.0 26.1 %collective-permute-start.3 = (bf16[1024,256]{1,0:T(8,128)(2,1)}, bf16[1024,256]{1,0:T(8,128)(2,1)S(1)}, u32[]{:S(2)}, u32[]{:S(2)}) collective-permute-start(bf16[1024,256]{1,0:T(8,128)(2,1)} %get-tuple-element.52), channel_id=1, source_target_pairs={{0,2},{1,3},{2,0},{3,1},{4,6},{5,7},{6,4},{7,5},{8,10},{9,11},{10,... | collective-permute-start | bytes 1572872 | tf_op jit(solution)/shard_map/ppermute | solution.py:37
  7.8 25.2 %collective-permute-start.2 = (bf16[1024,256]{1,0:T(8,128)(2,1)}, bf16[1024,256]{1,0:T(8,128)(2,1)}, u32[]{:S(2)}, u32[]{:S(2)}) collective-permute-start(bf16[1024,256]{1,0:T(8,128)(2,1)} %get-tuple-element.53), channel_id=1, source_target_pairs={{0,1},{1,2},{2,3},{3,0},{4,5},{5,6},{6,7},{7,4},{8,9},{9,10},{10,1... | collective-permute-start | bytes 1572872 | tf_op jit(solution)/shard_map/ppermute | solution.py:37
  9.7 8.7 %copy-start.18 = (f32[128,128]{1,0:T(8,128)S(1)}, f32[128,128]{1,0:T(8,128)}, u32[]{:S(2)}) copy-start(f32[128,128]{1,0:T(8,128)} %refs_0_.1) | copy-start | bytes 196612
  15.1 5.5 %copy-start.20 = (s32[8192]{0:T(1024)S(1)}, s32[8192]{0:T(1024)}, u32[]{:S(2)}) copy-start(s32[8192]{0:T(1024)} %param.8) | copy-start | bytes 98308
  15.1 5.7 %copy-start.21 = (s32[8192]{0:T(1024)S(1)}, s32[8192]{0:T(1024)}, u32[]{:S(2)}) copy-start(s32[8192]{0:T(1024)} %param.7) | copy-start | bytes 98308
  15.1 5.8 %collective-permute-start.8 = (s16[128,128]{1,0:T(8,128)(2,1)S(1)}, s16[128,128]{1,0:T(8,128)(2,1)S(1)}, u32[]{:S(2)}, u32[]{:S(2)}) collective-permute-start(s16[128,128]{1,0:T(8,128)(2,1)S(1)} %encode_terms.1.refs_0_), channel_id=1, source_target_pairs={{0,64},{4,68},{8,72},{12,76},{16,80},{20,84},{24,88},{28,92},{32,9... | collective-permute-start | bytes 98312 | tf_op jit(solution)/shard_map/ppermute | solution.py:33
  18.5 5.6 %collective-permute-start.1 = (f32[128,128]{1,0:T(8,128)S(1)}, f32[128,128]{1,0:T(8,128)S(1)}, u32[]{:S(2)}, u32[]{:S(2)}) collective-permute-start(f32[128,128]{1,0:T(8,128)S(1)} %join.8), channel_id=1, source_target_pairs={{4,0},{8,4},{12,8},{16,12},{20,16},{24,20},{28,24},{32,28},{36,32}... | collective-permute-start | bytes 196616 | tf_op jit(solution)/shard_map/ppermute | solution.py:267
  20.8 21.1 %copy-start.10 = (bf16[1024,256]{1,0:T(8,128)(2,1)S(1)}, bf16[1024,256]{1,0:T(8,128)(2,1)}, u32[]{:S(2)}) copy-start(bf16[1024,256]{1,0:T(8,128)(2,1)} %get-tuple-element.49.refs_1_) | copy-start | bytes 1572868
  20.8 21.1 %copy-start.11 = (bf16[1024,256]{1,0:T(8,128)(2,1)S(1)}, bf16[1024,256]{1,0:T(8,128)(2,1)}, u32[]{:S(2)}) copy-start(bf16[1024,256]{1,0:T(8,128)(2,1)} %get-tuple-element.50.refs_0_) | copy-start | bytes 1572868
  20.8 21.1 %copy-start.12 = (bf16[1024,256]{1,0:T(8,128)(2,1)S(1)}, bf16[1024,256]{1,0:T(8,128)(2,1)}, u32[]{:S(2)}) copy-start(bf16[1024,256]{1,0:T(8,128)(2,1)} %get-tuple-element.55.refs_2_) | copy-start | bytes 1572868
  20.9 8.7 %collective-permute-start = (f32[128,128]{1,0:T(8,128)S(1)}, f32[128,128]{1,0:T(8,128)S(1)}, u32[]{:S(2)}, u32[]{:S(2)}) collective-permute-start(f32[128,128]{1,0:T(8,128)S(1)} %join.8), channel_id=1, source_target_pairs={{0,4},{4,8},{8,12},{12,16},{16,20},{20,24},{24,28},{28,32},{32,36}... | collective-permute-start | bytes 196616 | tf_op jit(solution)/shard_map/ppermute | solution.py:267
  24.1 8.9 %collective-permute-start.9 = (s16[256,128]{1,0:T(8,128)(2,1)S(1)}, s16[256,128]{1,0:T(8,128)(2,1)S(1)}, u32[]{:S(2)}, u32[]{:S(2)}) collective-permute-start(s16[256,128]{1,0:T(8,128)(2,1)S(1)} %join.9.refs_0_), channel_id=1, source_target_pairs={{0,128},{4,132},{8,136},{12,140},{16,144},{20,148},{24,152},{28,15... | collective-permute-start | bytes 196616 | tf_op jit(solution)/shard_map/ppermute | solution.py:33
  33.1 12.8 %copy-start.15 = (bf16[1024,256]{1,0:T(8,128)(2,1)S(1)}, bf16[1024,256]{1,0:T(8,128)(2,1)}, u32[]{:S(2)}) copy-start(bf16[1024,256]{1,0:T(8,128)(2,1)} %copy-done.14) | copy-start | bytes 1572868
  33.1 7.4 %collective-permute-start.10 = (s16[512,128]{1,0:T(8,128)(2,1)S(1)}, s16[512,128]{1,0:T(8,128)(2,1)S(1)}, u32[]{:S(2)}, u32[]{:S(2)}) collective-permute-start(s16[512,128]{1,0:T(8,128)(2,1)S(1)} %join.10.refs_0_), channel_id=1, source_target_pairs={{0,32},{4,36},{8,40},{12,44},{16,48},{20,52},{24,56},{28,60},{32,0... | collective-permute-start | bytes 393224 | tf_op jit(solution)/shard_map/ppermute | solution.py:33
  40.5 10.0 %collective-permute-start.11 = (s16[1024,128]{1,0:T(8,128)(2,1)S(1)}, s16[1024,128]{1,0:T(8,128)(2,1)S(1)}, u32[]{:S(2)}, u32[]{:S(2)}) collective-permute-start(s16[1024,128]{1,0:T(8,128)(2,1)S(1)} %join.11.refs_0_), channel_id=1, source_target_pairs={{0,8},{4,12},{8,0},{12,4},{16,24},{20,28},{24,16},{28,20},{32,40},... | collective-permute-start | bytes 786440 | tf_op jit(solution)/shard_map/ppermute | solution.py:33
  41.9 19.4 %collective-permute-start.13 = (bf16[1024,256]{1,0:T(8,128)(2,1)S(1)}, bf16[1024,256]{1,0:T(8,128)(2,1)S(1)}, u32[]{:S(2)}, u32[]{:S(2)}) collective-permute-start(bf16[1024,256]{1,0:T(8,128)(2,1)S(1)} %get-tuple-element.29), channel_id=1, source_target_pairs={{0,1},{1,2},{2,3},{3,0},{4,5},{5,6},{6,7},{7,4},{8,9},{9,10},{10,1... | collective-permute-start | bytes 1572872 | tf_op jit(solution)/shard_map/ppermute | solution.py:37
  42.0 19.4 %collective-permute-start.14 = (bf16[1024,256]{1,0:T(8,128)(2,1)S(1)}, bf16[1024,256]{1,0:T(8,128)(2,1)S(1)}, u32[]{:S(2)}, u32[]{:S(2)}) collective-permute-start(bf16[1024,256]{1,0:T(8,128)(2,1)S(1)} %get-tuple-element.30), channel_id=1, source_target_pairs={{0,2},{1,3},{2,0},{3,1},{4,6},{5,7},{6,4},{7,5},{8,10},{9,11},{10,... | collective-permute-start | bytes 1572872 | tf_op jit(solution)/shard_map/ppermute | solution.py:37
  44.3 23.6 %collective-permute-start.15 = (bf16[1024,256]{1,0:T(8,128)(2,1)S(1)}, bf16[1024,256]{1,0:T(8,128)(2,1)S(1)}, u32[]{:S(2)}, u32[]{:S(2)}) collective-permute-start(bf16[1024,256]{1,0:T(8,128)(2,1)S(1)} %get-tuple-element.31), channel_id=1, source_target_pairs={{0,3},{1,0},{2,1},{3,2},{4,7},{5,4},{6,5},{7,6},{8,11},{9,8},{10,9... | collective-permute-start | bytes 1572872 | tf_op jit(solution)/shard_map/ppermute | solution.py:37
  51.2 16.7 %collective-permute-start.12 = (s16[2048,128]{1,0:T(8,128)(2,1)S(1)}, s16[2048,128]{1,0:T(8,128)(2,1)S(1)}, u32[]{:S(2)}, u32[]{:S(2)}) collective-permute-start(s16[2048,128]{1,0:T(8,128)(2,1)S(1)} %join.12.refs_0_), channel_id=1, source_target_pairs={{0,16},{4,20},{8,24},{12,28},{16,0},{20,4},{24,8},{28,12},{32,48},... | collective-permute-start | bytes 1572872 | tf_op jit(solution)/shard_map/ppermute | solution.py:33
  61.3 6.6 %copy-start = (f32[4096,128]{1,0:T(8,128)}, f32[4096,128]{1,0:T(8,128)S(1)}, u32[]{:S(2)}) copy-start(f32[4096,128]{1,0:T(8,128)S(1)} %get-tuple-element.24.refs_2_) | copy-start | bytes 6291460
  61.3 6.6 %copy-start.2 = (f32[4096,128]{1,0:T(8,128)}, f32[4096,128]{1,0:T(8,128)S(1)}, u32[]{:S(2)}) copy-start(f32[4096,128]{1,0:T(8,128)S(1)} %get-tuple-element.33.refs_2_) | copy-start | bytes 6291460
  61.4 6.6 %copy-start.4 = (bf16[1024,256]{1,0:T(8,128)(2,1)}, bf16[1024,256]{1,0:T(8,128)(2,1)S(1)}, u32[]{:S(2)}) copy-start(bf16[1024,256]{1,0:T(8,128)(2,1)S(1)} %collective-permute-done.13.refs_4_.b1) | copy-start | bytes 1572868
  61.4 6.6 %copy-start.6 = (bf16[1024,256]{1,0:T(8,128)(2,1)}, bf16[1024,256]{1,0:T(8,128)(2,1)S(1)}, u32[]{:S(2)}) copy-start(bf16[1024,256]{1,0:T(8,128)(2,1)S(1)} %collective-permute-done.14.refs_5_.b2) | copy-start | bytes 1572868
  68.7 17.5 %collective-permute-start.16 = (s16[4096,128]{1,0:T(8,128)(2,1)S(1)}, s16[4096,128]{1,0:T(8,128)(2,1)}, u32[]{:S(2)}, u32[]{:S(2)}) collective-permute-start(s16[4096,128]{1,0:T(8,128)(2,1)S(1)} %join.13.refs_7_), channel_id=1, source_target_pairs={{0,4},{4,0},{8,12},{12,8},{16,20},{20,16},{24,28},{28,24},{32,36},... | collective-permute-start | bytes 3145736 | tf_op jit(solution)/shard_map/ppermute | solution.py:33
  68.7 12.0 %collective-permute-start.5 = (s16[1024,128]{1,0:T(8,128)(2,1)}, s16[1024,128]{1,0:T(8,128)(2,1)}, u32[]{:S(2)}, u32[]{:S(2)}) collective-permute-start(s16[1024,128]{1,0:T(8,128)(2,1)} %get-tuple-element.26), channel_id=1, source_target_pairs={{0,1},{1,2},{2,3},{3,0},{4,5},{5,6},{6,7},{7,4},{8,9},{9,10},{10,1... | collective-permute-start | bytes 786440 | tf_op jit(solution)/shard_map/ppermute | solution.py:37
  69.4 14.1 %collective-permute-start.6 = (s16[1024,128]{1,0:T(8,128)(2,1)}, s16[1024,128]{1,0:T(8,128)(2,1)}, u32[]{:S(2)}, u32[]{:S(2)}) collective-permute-start(s16[1024,128]{1,0:T(8,128)(2,1)} %get-tuple-element.27), channel_id=1, source_target_pairs={{0,2},{1,3},{2,0},{3,1},{4,6},{5,7},{6,4},{7,5},{8,10},{9,11},{10,... | collective-permute-start | bytes 786440 | tf_op jit(solution)/shard_map/ppermute | solution.py:37
  71.3 14.9 %collective-permute-start.7 = (s16[1024,128]{1,0:T(8,128)(2,1)}, s16[1024,128]{1,0:T(8,128)(2,1)S(1)}, u32[]{:S(2)}, u32[]{:S(2)}) collective-permute-start(s16[1024,128]{1,0:T(8,128)(2,1)} %copy-done.19), channel_id=1, source_target_pairs={{0,3},{1,0},{2,1},{3,2},{4,7},{5,4},{6,5},{7,6},{8,11},{9,8},{10,9... | collective-permute-start | bytes 786440 | tf_op jit(solution)/shard_map/ppermute | solution.py:37
  73.2 1.0 copy-start.5
  74.3 1.0 copy-start.7
  75.3 1.0 copy-start.9
  77.4 8.8 %copy-start.1 = (f32[4096,128]{1,0:T(8,128)S(1)}, f32[4096,128]{1,0:T(8,128)}, u32[]{:S(2)}) copy-start(f32[4096,128]{1,0:T(8,128)} %copy-done) | copy-start | bytes 6291460
  80.4 15.8 %collective-permute-start.17 = (s16[1024,128]{1,0:T(8,128)(2,1)S(1)}, s16[1024,128]{1,0:T(8,128)(2,1)S(1)}, u32[]{:S(2)}, u32[]{:S(2)}) collective-permute-start(s16[1024,128]{1,0:T(8,128)(2,1)S(1)} %get-tuple-element.35), channel_id=1, source_target_pairs={{0,1},{1,2},{2,3},{3,0},{4,5},{5,6},{6,7},{7,4},{8,9},{9,10},{10,1... | collective-permute-start | bytes 786440 | tf_op jit(solution)/shard_map/ppermute | solution.py:37
  80.7 15.6 %collective-permute-start.18 = (s16[1024,128]{1,0:T(8,128)(2,1)S(1)}, s16[1024,128]{1,0:T(8,128)(2,1)S(1)}, u32[]{:S(2)}, u32[]{:S(2)}) collective-permute-start(s16[1024,128]{1,0:T(8,128)(2,1)S(1)} %get-tuple-element.36), channel_id=1, source_target_pairs={{0,2},{1,3},{2,0},{3,1},{4,6},{5,7},{6,4},{7,5},{8,10},{9,11},{10,... | collective-permute-start | bytes 786440 | tf_op jit(solution)/shard_map/ppermute | solution.py:37
  83.5 12.9 %collective-permute-start.19 = (s16[1024,128]{1,0:T(8,128)(2,1)S(1)}, s16[1024,128]{1,0:T(8,128)(2,1)S(1)}, u32[]{:S(2)}, u32[]{:S(2)}) collective-permute-start(s16[1024,128]{1,0:T(8,128)(2,1)S(1)} %get-tuple-element.37), channel_id=1, source_target_pairs={{0,3},{1,0},{2,1},{3,2},{4,7},{5,4},{6,5},{7,6},{8,11},{9,8},{10,9... | collective-permute-start | bytes 786440 | tf_op jit(solution)/shard_map/ppermute | solution.py:37
  86.2 10.2 %copy-start.3 = (f32[4096,128]{1,0:T(8,128)S(1)}, f32[4096,128]{1,0:T(8,128)}, u32[]{:S(2)}) copy-start(f32[4096,128]{1,0:T(8,128)} %copy-done.2) | copy-start | bytes 6291460
  105.3 4.2 %collective-permute-start.22 = (f32[4096,128]{1,0:T(8,128)S(1)}, f32[4096,128]{1,0:T(8,128)S(1)}, u32[]{:S(2)}, u32[]{:S(2)}) collective-permute-start(f32[4096,128]{1,0:T(8,128)S(1)} %get-tuple-element.45), channel_id=1, source_target_pairs={{0,4},{4,0},{8,12},{12,8},{16,20},{20,16},{24,28},{28,24},{32,36},... | collective-permute-start | bytes 6291464 | tf_op jit(solution)/shard_map/ppermute | solution.py:33
  110.0 10.8 %collective-permute-start.25 = (f16[2,4,128,128]{3,2,1,0:T(8,128)(2,1)S(1)}, f16[2,4,128,128]{3,2,1,0:T(8,128)(2,1)S(1)}, u32[]{:S(2)}, u32[]{:S(2)}) collective-permute-start(f16[2,4,128,128]{3,2,1,0:T(8,128)(2,1)S(1)} %bitcast.66), channel_id=1, source_target_pairs={{0,16},{4,20},{8,24},{12,28},{16,0},{20,4},{24,8},{28,12},{32,48},... | collective-permute-start | bytes 786440 | tf_op jit(solution)/shard_map/ppermute | solution.py:33
  113.0 12.4 %collective-permute-start.23 = (f16[2,4,128,128]{3,2,1,0:T(8,128)(2,1)S(1)}, f16[2,4,128,128]{3,2,1,0:T(8,128)(2,1)S(1)}, u32[]{:S(2)}, u32[]{:S(2)}) collective-permute-start(f16[2,4,128,128]{3,2,1,0:T(8,128)(2,1)S(1)} %bitcast.65), channel_id=1, source_target_pairs={{0,8},{4,12},{8,0},{12,4},{16,24},{20,28},{24,16},{28,20},{32,40},... | collective-permute-start | bytes 786440 | tf_op jit(solution)/shard_map/ppermute | solution.py:33
  113.4 12.3 %collective-permute-start.24 = (f16[2,4,128,128]{3,2,1,0:T(8,128)(2,1)S(1)}, f16[2,4,128,128]{3,2,1,0:T(8,128)(2,1)S(1)}, u32[]{:S(2)}, u32[]{:S(2)}) collective-permute-start(f16[2,4,128,128]{3,2,1,0:T(8,128)(2,1)S(1)} %bitcast.64), channel_id=1, source_target_pairs={{0,24},{4,28},{8,16},{12,20},{16,8},{20,12},{24,0},{28,4},{32,56},... | collective-permute-start | bytes 786440 | tf_op jit(solution)/shard_map/ppermute | solution.py:33
  116.0 12.1 %collective-permute-start.20 = (f32[128,128]{1,0:T(8,128)S(1)}, f32[128,128]{1,0:T(8,128)S(1)}, u32[]{:S(2)}, u32[]{:S(2)}) collective-permute-start(f32[128,128]{1,0:T(8,128)S(1)} %get-tuple-element.61), channel_id=1, source_target_pairs={{0,4},{4,8},{8,12},{12,16},{16,20},{20,24},{24,28},{28,32},{32,36}... | collective-permute-start | bytes 196616 | tf_op jit(solution)/shard_map/ppermute | solution.py:267
  117.5 10.7 %collective-permute-start.21 = (f32[128,128]{1,0:T(8,128)S(1)}, f32[128,128]{1,0:T(8,128)S(1)}, u32[]{:S(2)}, u32[]{:S(2)}) collective-permute-start(f32[128,128]{1,0:T(8,128)S(1)} %get-tuple-element.62), channel_id=1, source_target_pairs={{4,0},{8,4},{12,8},{16,12},{20,16},{24,20},{28,24},{32,28},{36,32}... | collective-permute-start | bytes 196616 | tf_op jit(solution)/shard_map/ppermute | solution.py:267
  125.8 6.0 %collective-permute-start.26 = (f16[4,128,128]{2,1,0:T(8,128)(2,1)S(1)}, f16[4,128,128]{2,1,0:T(8,128)(2,1)S(1)}, u32[]{:S(2)}, u32[]{:S(2)}) collective-permute-start(f16[4,128,128]{2,1,0:T(8,128)(2,1)S(1)} %get-tuple-element.59), channel_id=1, source_target_pairs={{0,32},{4,36},{8,40},{12,44},{16,48},{20,52},{24,56},{28,60},{32,0... | collective-permute-start | bytes 393224 | tf_op jit(solution)/shard_map/ppermute | solution.py:33
  128.2 17.7 %copy-start.16 = (f32[128,128]{1,0:T(8,128)}, f32[128,128]{1,0:T(8,128)S(1)}, u32[]{:S(2)}) copy-start(f32[128,128]{1,0:T(8,128)S(1)} %fusion.7.refs_1_) | copy-start | bytes 196612
  131.9 5.4 %collective-permute-start.27 = (f16[2,128,128]{2,1,0:T(8,128)(2,1)S(1)}, f16[2,128,128]{2,1,0:T(8,128)(2,1)S(1)}, u32[]{:S(2)}, u32[]{:S(2)}) collective-permute-start(f16[2,128,128]{2,1,0:T(8,128)(2,1)S(1)} %fusion.4), channel_id=1, source_target_pairs={{0,64},{4,68},{8,72},{12,76},{16,80},{20,84},{24,88},{28,92},{32,9... | collective-permute-start | bytes 196616 | tf_op jit(solution)/shard_map/ppermute | solution.py:33
  137.4 7.9 %collective-permute-start.28 = (f16[128,128]{1,0:T(8,128)(2,1)S(1)}, f16[128,128]{1,0:T(8,128)(2,1)S(1)}, u32[]{:S(2)}, u32[]{:S(2)}) collective-permute-start(f16[128,128]{1,0:T(8,128)(2,1)S(1)} %fusion.23), channel_id=1, source_target_pairs={{0,128},{4,132},{8,136},{12,140},{16,144},{20,148},{24,152},{28,15... | collective-permute-start | bytes 98312 | tf_op jit(solution)/shard_map/ppermute | solution.py:33
  (3 other events, 2.6 us)
